TPU v7x, 32 devices: a whole 2x2x4 slice. The times are simulated.
32 devices in a mesh: patch: 16 (over z, x, core), head: 2 (over y).
Axes of the slice: x: 2, y: 2, z: 4, core: 2. Of those that a mesh axis runs over, the one named last changes fastest.
Arguments:
- queries: bfloat16 [768, 3072], P('patch', 'head'), as said below
- stale_kv: bfloat16 [2, 768, 3072], P(None, None, 'head'), may hold values from -6 to 6, as said below
- codes: int32 [2, 768, 3072], P(None, 'patch', 'head'), may hold values from -127 to 127
- exponents: int32 [2, 768, 24], P(None, 'patch', 'head'), may hold values from -9 to -6
- text_kv: bfloat16 [2, 512, 3072], P(None, None, 'head'), may hold values from -6 to 6, as said below
- out_weight: bfloat16 [3072, 3072], P('head', 'patch'), may hold values from -0.109375 to 0.109375
- out_bias: float32 [3072], P('head'), may hold values from -0.6 to 0.6
- out_gate: float32 [3072], P('head'), may hold values from 2 to 8
Outputs:
- gated_out: bfloat16 [768, 3072], P('patch', 'head')
Inputs may be any that keep to these rules, and one draw needn't show every extreme that they name: queries are real-valued. `stale_kv`: last step's keys and values are real-valued. `text_kv`: text keys and values are real-valued.
All inputs are finite; a program needn't handle non-finite values.
Results may differ from a plain program's by a relative error of at most 0.0075.
Values may be sent and summed in bfloat16 or wider, within the bound.
No kernel may reach another device: no remote copies, remote signals or barrier semaphores. Data moves between devices by JAX's collectives and lax.ppermute only.
A program may use at most 64 MiB of HBM per device.

v0:
```python
import jax
import jax.numpy as jnp
from jax import lax
from jax.sharding import PartitionSpec as P

HD = 128


def body(queries, stale_kv, codes, exponents, text_kv, out_weight, out_bias, out_gate):
    tok_rows = queries.shape[0]
    row_width = queries.shape[1]
    head_count = row_width // HD
    text_count = text_kv.shape[1]
    scale_factor = HD ** (-0.5)
    blocks = jnp.exp2(exponents.astype(jnp.float32))
    decoded = codes.astype(jnp.float32).reshape(2, tok_rows, head_count, HD) * blocks[..., None]
    decoded = decoded.astype(jnp.bfloat16).reshape(2, tok_rows, row_width)
    arrived = lax.all_gather(decoded, "patch", axis=1, tiled=True)
    all_rows = arrived.shape[1]
    query_heads = queries.reshape(tok_rows, head_count, HD)
    text_heads = text_kv.reshape(2, text_count, head_count, HD)
    stale_heads = stale_kv.reshape(2, all_rows, head_count, HD)
    arrived_heads = arrived.reshape(2, all_rows, head_count, HD)
    text_scores = jnp.einsum(
        "thd,khd->htk", query_heads, text_heads[0], preferred_element_type=jnp.float32
    )
    rebuilt = stale_heads.astype(jnp.float32) + arrived_heads.astype(jnp.float32)
    image_scores = jnp.einsum(
        "thd,khd->htk", query_heads.astype(jnp.float32), rebuilt[0], precision=lax.Precision.HIGHEST
    )
    scores = jnp.concatenate([text_scores, image_scores], axis=2) * scale_factor
    row_peak = jnp.max(scores, axis=2, keepdims=True)
    weights = jnp.exp(scores - row_peak).astype(jnp.bfloat16)
    row_total = jnp.sum(weights.astype(jnp.float32), axis=2)
    text_part = jnp.einsum(
        "htk,khd->thd",
        weights[:, :, :text_count],
        text_heads[1],
        preferred_element_type=jnp.float32,
    )
    image_weights = weights[:, :, text_count:]
    image_part = jnp.einsum(
        "htk,khd->thd",
        image_weights.astype(jnp.float32),
        rebuilt[1],
        precision=lax.Precision.HIGHEST,
    )
    attended = (
        ((text_part + image_part) / row_total.T[:, :, None])
        .astype(jnp.bfloat16)
        .reshape(tok_rows, row_width)
    )
    partial_terms = jnp.dot(
        attended,
        lax.all_gather(out_weight, "patch", axis=1, tiled=True),
        preferred_element_type=jnp.float32,
    )
    column_share = lax.psum_scatter(partial_terms, "head", scatter_dimension=1, tiled=True)
    return (out_gate * (column_share + out_bias)).astype(jnp.bfloat16)


def solution(mesh):
    placed = (
        P("patch", "head"),
        P(None, None, "head"),
        P(None, "patch", "head"),
        P(None, "patch", "head"),
        P(None, None, "head"),
        P("head", "patch"),
        P("head"),
        P("head"),
    )
    return jax.shard_map(
        body, mesh=mesh, in_specs=placed, out_specs=P("patch", "head"), check_vma=False
    )
```

profile of v0, /device:TPU:0, one launch (start us, length us, event | category | flops | bytes accessed | tf_op | source)
XLA Modules:
  0.0 177.2 jit_solution(10978136096835227180)
XLA Ops:
  6.5 0.8 multiply_exponential_fusion
  7.3 0.1 copy.15
  7.4 0.3 mul.26
  7.7 0.1 mul.27
  7.8 1.8 %multiply_convert_fusion = bf16[2,48,1536]{2,1,0:T(8,128)(2,1)} fusion(f32[2,48,1536]{2,1,0:T(8,128)S(1)} %mul.27, s32[2,48,1536]{2,1,0:T(8,128)} %param.10), kind=kLoop, calls=%fused_computation.18 | loop fusion | flops 442368 | bytes 1474560 | tf_op jit(solution)/shard_map/convert_element_type | solution.py:17
  9.6 0.0 all-gather.3.cloned.1.call-update
  9.6 0.0 all-gather.5.cloned.1.call-start
  9.7 0.7 all-gather.5.cloned.1.call-update
  10.4 0.0 reduce-scatter.2.cloned.1.call-start
  10.4 3.2 %fusion.23 = (bf16[1,512,1536]{2,1,0:T(8,128)(2,1)S(1)}, bf16[1,512,1536]{2,1,0:T(8,128)(2,1)}) fusion(bf16[2,512,1536]{2,1,0:T(8,128)(2,1)} %param.12), kind=kLoop, calls=%fused_computation.32 | loop fusion | bytes 6291456 | tf_op jit(solution)/shard_map/slice | solution.py:25
  13.6 0.7 copy.28
  14.3 1.7 copy.29
  16.1 1.4 fusion.16
  17.5 48.3 %all-gather.3.cloned.1.call-done = bf16[2,768,1536]{2,1,0:T(8,128)(2,1)} async-done(((bf16[2,48,1536]{2,1,0:T(8,128)(2,1)}), bf16[2,768,1536]{2,1,0:T(8,128)(2,1)}) %all-gather.3.cloned.1.call-update) | async-done | bytes 4718608 | tf_op jit(solution)/shard_map/all_gather | solution.py:18
  65.7 5.2 %convert_add_fusion = f32[2,768,1536]{2,1,0:T(8,128)S(1)} fusion(bf16[2,768,1536]{2,1,0:T(8,128)(2,1)} %all-gather.3.cloned.1.call-done, bf16[2,768,1536]{2,1,0:T(8,128)(2,1)} %param.9), kind=kLoop, calls=%fused_computation.1 | loop fusion | flops 7077888 | bytes 18874368 | tf_op jit(solution)/shard_map/add | solution.py:27
  71.0 4.6 %fusion.22 = (f32[1,768,1536]{2,1,0:T(8,128)}, f32[1,768,1536]{2,1,0:T(8,128)}) fusion(f32[2,768,1536]{2,1,0:T(8,128)S(1)} %convert_add_fusion), kind=kLoop, calls=%fused_computation.31 | loop fusion | bytes 18874368 | tf_op jit(solution)/shard_map/slice | solution.py:45
  75.6 6.1 %copy.16 = f32[1,768,1536]{1,2,0:T(8,128)} copy(f32[1,768,1536]{2,1,0:T(8,128)} %get-tuple-element.6) | data formatting | bytes 9437184 | tf_op jit(solution)/shard_map/slice | solution.py:29
  81.7 6.1 %copy.21 = f32[1,768,1536]{1,2,0:T(8,128)} copy(f32[1,768,1536]{2,1,0:T(8,128)} %get-tuple-element.5) | data formatting | bytes 9437184 | tf_op jit(solution)/shard_map/slice | solution.py:45
  87.8 4.2 %convolution_bitcast_fusion = f32[12,48,768]{2,1,0:T(8,128)S(1)} fusion(f32[768,12,128]{0,2,1:T(8,128)} %bitcast.44, bf16[48,1536]{1,0:T(8,128)(2,1)S(1)} %copy-done), kind=kOutput, calls=%fused_computation.8 | convolution fusion | flops 679477248 | bytes 6635520 | tf_op jit(solution)/shard_map/thd,khd->htk/dot_general | solution.py:28
  92.0 0.0 copy-done.1
  92.0 0.0 slice-start.1
  92.0 1.1 convert_reduce_fusion
  93.1 0.6 convolution_bitcast_fusion.2
  93.7 0.0 slice-done
  93.8 2.9 %fusion.9 = bf16[12,6,8,128]{3,2,1,0:T(8,128)(2,1)S(1)} fusion(f32[48,12,128]{2,0,1:T(8,128)S(1)} %convolution_bitcast_fusion.2, f32[768,12,128]{0,2,1:T(8,128)S(1)} %bitcast.43, bf16[12,48,1280]{2,1,0:T(8,128)(2,1)S(1)} %get-tuple-element.10, f32[48,12]{0,1:T(8,128)S(1)} %bitcast.47), kind=kOutput, calls=%fused_computation.15 | convolution fusion | flops 679698432 | bytes 6053888 | tf_op jit(solution)/shard_map/htk,khd->thd/dot_general | solution.py:42
  96.6 0.0 copy-start.2
  96.6 0.0 copy-start.3
  96.7 51.4 %all-gather.5.cloned.1.call-done = bf16[1536,3072]{0,1:T(8,128)(2,1)} async-done(((bf16[1536,192]{0,1:T(8,128)(2,1)}), bf16[1536,3072]{0,1:T(8,128)(2,1)}) %all-gather.5.cloned.1.call-update) | async-done | bytes 9437200 | tf_op jit(solution)/shard_map/all_gather | solution.py:55
  148.0 7.3 %fusion.12 = f32[48,3072]{1,0:T(8,128)} fusion(bf16[1536,3072]{0,1:T(8,128)(2,1)} %all-gather.5.cloned.1.call-done, bf16[12,6,8,128]{3,2,1,0:T(8,128)(2,1)S(1)} %fusion.9), kind=kOutput, calls=%fused_computation.20 | convolution fusion | flops 452984832 | bytes 10174464 | tf_op jit(solution)/shard_map/dot_general | solution.py:53
  155.4 0.0 reduce-scatter.2.cloned.1.call-update
  155.4 13.6 %reduce-scatter.2.cloned.1.call-done = f32[48,1536]{1,0:T(8,128)} async-done(((f32[48,3072]{1,0:T(8,128)}), f32[48,1536]{1,0:T(8,128)}) %reduce-scatter.2.cloned.1.call-update) | async-done | bytes 294928 | tf_op jit(solution)/shard_map/reduce_scatter | solution.py:58
  169.0 1.7 multiply_convert_fusion.1
  (9 shorter events, 0.0 us)
Async XLA Ops:
  6.5 9.5 %copy-start = (bf16[48,1536]{1,0:T(8,128)(2,1)S(1)}, bf16[48,1536]{1,0:T(8,128)(2,1)}, u32[]{:S(2)}) copy-start(bf16[48,1536]{1,0:T(8,128)(2,1)} %param.8) | copy-start | bytes 442372
  6.5 59.2 %all-gather.3.cloned.1.call-start = ((), (), s32[]{:S(2)}) async-start(), calls=%async_computation.1 | async-start | bytes 5013504 | tf_op jit(solution)/shard_map/all_gather | solution.py:18
  9.6 138.4 %all-gather.5.cloned.1.call-start = ((), (), s32[]{:S(2)}) async-start(), calls=%async_computation.2 | async-start | bytes 10027008 | tf_op jit(solution)/shard_map/all_gather | solution.py:55
  10.4 158.6 %reduce-scatter.2.cloned.1.call-start = ((), (), s32[]{:S(2)}) async-start(), calls=%async_computation.3 | async-start | bytes 884736 | tf_op jit(solution)/shard_map/reduce_scatter | solution.py:58
  87.8 4.2 %copy-start.1 = (f32[12,48,512]{2,1,0:T(8,128)S(1)}, f32[12,48,512]{2,1,0:T(8,128)}, u32[]{:S(2)}) copy-start(f32[12,48,512]{2,1,0:T(8,128)} %fusion.16) | copy-start | bytes 3538948
  87.8 6.0 %slice-start = ((s8[4718592]{0:T(1024)(128)(4,1)}), s8[4194304]{0:T(1024)(128)(4,1)S(1)}, s32[]{:S(2)}) async-start(s8[4718592]{0:T(1024)(128)(4,1)} %bitcast.41), calls=%async_computation.4 | async-start | bytes 8388608
  92.0 1.8 slice-start.1
  96.6 72.3 %copy-start.2 = (f32[1536]{0:T(1024)S(1)}, f32[1536]{0:T(1024)}, u32[]{:S(2)}) copy-start(f32[1536]{0:T(1024)} %param.14) | copy-start | bytes 18436
  96.6 72.3 %copy-start.3 = (f32[1536]{0:T(1024)S(1)}, f32[1536]{0:T(1024)}, u32[]{:S(2)}) copy-start(f32[1536]{0:T(1024)} %param.15) | copy-start | bytes 18436
Sparse Core Ops, SparseCore 0:
  9.7 55.9 all-gather.2
  68.0 79.9 all-gather.4
  155.5 13.4 reduce-scatter.1
where the time goes:
time: 178 us; the launch traced here: 177 us
  waiting for transfers between devices  114 us (64%)
  local copies, waits for them, and re-layouts  22.9 us (13%)
  matrix products  16.4 us (9%)
  between operations  13.2 us (7%)
  other arithmetic  10.6 us (6%)
    all_gather x1, waiting for transfers between devices, body(): lax.all_gather(out_weight, 'patch', axis=1, tiled=True)  51.4 us
    all_gather x1, waiting for transfers between devices, body(): arrived = lax.all_gather(decoded, 'patch', axis=1, tiled=True)  48.3 us
    reduce_scatter x1, waiting for transfers between devices, body(): lax.psum_scatter(partial_terms, 'head', scatter_dimension=1, tiled=True)  13.6 us
    slice x2, local copies, waits for them, and re-layouts, body(): rebuilt[1]  10.7 us
    dot_general x1, matrix products, body(): jnp.dot(attended, lax.all_gather(out_weight, 'patch', axis=1, tiled=True)...  7.35 us
    slice x1, local copies, waits for them, and re-layouts, body(): rebuilt[0]  6.07 us
    add x1, other arithmetic, body(): stale_heads.astype(jnp.float32) + arrived_heads.astype(jnp.float32)  5.25 us
    dot_general x1, matrix products, body(): jnp.einsum('thd,khd->htk', query_heads.astype(jnp.float32), rebuilt[0], p...  4.21 us
  transfers between devices with their start and end apart: 3, of which 3 were waited for; matrix products, arithmetic and copies ran while one was open for 21% of the time, Pallas kernels for 0%

commit v1 on v0

v1 whole, which is shorter than its diff:
```python
import functools

import jax
import jax.numpy as jnp
from jax import lax
from jax.experimental import pallas as pl
from jax.experimental.pallas import tpu as pltpu
from jax.sharding import PartitionSpec as P

HD = 128
SPREAD = 4
VMEM = pl.BlockSpec(memory_space=pltpu.VMEM)
ANY = pl.BlockSpec(memory_space=pl.ANY)
NT = (((1,), (1,)), ((), ()))


def plain_body(queries, stale_kv, codes, exponents, text_kv, out_weight, out_bias, out_gate):
    tok_rows = queries.shape[0]
    row_width = queries.shape[1]
    head_count = row_width // HD
    text_count = text_kv.shape[1]
    scale_factor = HD ** (-0.5)
    blocks = jnp.exp2(exponents.astype(jnp.float32))
    decoded = codes.astype(jnp.float32).reshape(2, tok_rows, head_count, HD) * blocks[..., None]
    decoded = decoded.astype(jnp.bfloat16).reshape(2, tok_rows, row_width)
    arrived = lax.all_gather(decoded, "patch", axis=1, tiled=True)
    all_rows = arrived.shape[1]
    query_heads = queries.reshape(tok_rows, head_count, HD)
    text_heads = text_kv.reshape(2, text_count, head_count, HD)
    stale_heads = stale_kv.reshape(2, all_rows, head_count, HD)
    arrived_heads = arrived.reshape(2, all_rows, head_count, HD)
    text_scores = jnp.einsum("thd,khd->htk", query_heads, text_heads[0], preferred_element_type=jnp.float32)
    rebuilt = stale_heads.astype(jnp.float32) + arrived_heads.astype(jnp.float32)
    image_scores = jnp.einsum(
        "thd,khd->htk", query_heads.astype(jnp.float32), rebuilt[0], precision=lax.Precision.HIGHEST
    )
    scores = jnp.concatenate([text_scores, image_scores], axis=2) * scale_factor
    row_peak = jnp.max(scores, axis=2, keepdims=True)
    weights = jnp.exp(scores - row_peak).astype(jnp.bfloat16)
    row_total = jnp.sum(weights.astype(jnp.float32), axis=2)
    text_part = jnp.einsum(
        "htk,khd->thd", weights[:, :, :text_count], text_heads[1], preferred_element_type=jnp.float32
    )
    image_part = jnp.einsum(
        "htk,khd->thd",
        weights[:, :, text_count:].astype(jnp.float32),
        rebuilt[1],
        precision=lax.Precision.HIGHEST,
    )
    attended = ((text_part + image_part) / row_total.T[:, :, None]).astype(jnp.bfloat16).reshape(tok_rows, row_width)
    partial_terms = jnp.dot(
        attended, lax.all_gather(out_weight, "patch", axis=1, tiled=True), preferred_element_type=jnp.float32
    )
    column_share = lax.psum_scatter(partial_terms, "head", scatter_dimension=1, tiled=True)
    return (out_gate * (column_share + out_bias)).astype(jnp.bfloat16)


def aligned(value, step):
    return pl.multiple_of(value * step, step)


def place(groups):
    me = lax.axis_index("patch")
    return me // SPREAD, lax.rem(me, SPREAD)


def pack_kernel(groups, queries, codes, exponents, *rest):
    outs, (held,) = rest[: 2 * groups], rest[2 * groups :]
    group, _ = place(groups)
    heads = queries.shape[1] // HD
    per = heads // groups
    for kind in range(2):
        scales = jnp.left_shift(1, exponents[kind] + 16).astype(jnp.float32) * (2.0**-16)
        for head in range(heads):
            slot = lax.rem(head // per - group + groups, groups)
            inside = slice((head % per) * HD, (head % per + 1) * HD)
            whole = slice(head * HD, (head + 1) * HD)
            decoded = codes[kind, :, whole].astype(jnp.float32) * scales[:, head : head + 1]
            held[slot, kind, :, inside] = decoded.astype(jnp.bfloat16)
    for target in range(groups):
        slot = lax.rem(target - group + groups, groups)
        held[slot, 2] = queries[:, target * per * HD : (target + 1) * per * HD]
    for slot in range(groups):
        outs[2 * slot][...] = held[slot, 0:2]
        outs[2 * slot + 1][...] = held[slot, 2]


def pack(groups, queries, codes, exponents):
    rows, width = queries.shape
    share = width // groups
    shapes = []
    for _ in range(groups):
        shapes += [
            jax.ShapeDtypeStruct((2, rows, share), jnp.bfloat16),
            jax.ShapeDtypeStruct((rows, share), jnp.bfloat16),
        ]
    outs = pl.pallas_call(
        functools.partial(pack_kernel, groups),
        out_shape=shapes,
        in_specs=[VMEM] * 3,
        out_specs=[VMEM] * len(shapes),
        scratch_shapes=[pltpu.VMEM((groups, 3, rows, share), jnp.bfloat16)],
        compiler_params=pltpu.CompilerParams(vmem_limit_bytes=16 << 20),
        cost_estimate=pl.CostEstimate(flops=2 * codes.size, bytes_accessed=6 * codes.size, transcendentals=0),
    )(queries, codes, exponents)
    return outs[0::2], outs[1::2]


def attend_kernel(groups, *refs):
    parts, refs = refs[: groups * SPREAD], refs[groups * SPREAD :]
    query_parts, refs = refs[:groups], refs[groups:]
    text_hbm, stale_hbm, out, query, residual, text, stale, sems = refs
    group, spot = place(groups)
    rows, width = query_parts[0].shape
    columns = pl.ds(aligned(group, width), width)
    text_copy = pltpu.make_async_copy(text_hbm.at[:, :, columns], text, sems.at[0])
    stale_copy = pltpu.make_async_copy(stale_hbm.at[:, :, columns], stale, sems.at[1])
    text_copy.start()
    stale_copy.start()
    for slot in range(groups):
        origin = lax.rem(group - slot + groups, groups)
        query[pl.ds(aligned(origin, rows), rows), :] = query_parts[slot][...]
        for twist in range(SPREAD):
            token = origin * SPREAD + jnp.bitwise_xor(spot, twist)
            residual[:, pl.ds(aligned(token, rows), rows), :] = parts[slot * SPREAD + twist][...]
    text_copy.wait()
    stale_copy.wait()
    for head in range(width // HD):
        cols = slice(head * HD, (head + 1) * HD)
        asked = query[:, cols]
        text_scores = lax.dot_general(asked, text[0, :, cols], NT, preferred_element_type=jnp.float32)
        image_scores = lax.dot_general(asked, stale[0, :, cols], NT, preferred_element_type=jnp.float32)
        image_scores += lax.dot_general(asked, residual[0, :, cols], NT, preferred_element_type=jnp.float32)
        text_scores *= HD**-0.5
        image_scores *= HD**-0.5
        peak = jnp.maximum(
            jnp.max(text_scores, axis=1, keepdims=True), jnp.max(image_scores, axis=1, keepdims=True)
        )
        text_weights = jnp.exp(text_scores - peak).astype(jnp.bfloat16)
        image_weights = jnp.exp(image_scores - peak).astype(jnp.bfloat16)
        total = jnp.sum(text_weights.astype(jnp.float32), axis=1, keepdims=True)
        total += jnp.sum(image_weights.astype(jnp.float32), axis=1, keepdims=True)
        mixed = jnp.dot(text_weights, text[1, :, cols], preferred_element_type=jnp.float32)
        mixed += jnp.dot(image_weights, stale[1, :, cols], preferred_element_type=jnp.float32)
        mixed += jnp.dot(image_weights, residual[1, :, cols], preferred_element_type=jnp.float32)
        out[:, cols] = (mixed / total).astype(jnp.bfloat16)


def attend(groups, parts, query_parts, text_kv, stale_kv):
    rows, width = query_parts[0].shape
    keys = stale_kv.shape[1]
    texts = text_kv.shape[1]
    bf16 = jnp.bfloat16
    return pl.pallas_call(
        functools.partial(attend_kernel, groups),
        out_shape=jax.ShapeDtypeStruct((groups * rows, width), bf16),
        in_specs=[VMEM] * (len(parts) + len(query_parts)) + [ANY] * 2,
        out_specs=VMEM,
        scratch_shapes=[
            pltpu.VMEM((groups * rows, width), bf16),
            pltpu.VMEM((2, keys, width), bf16),
            pltpu.VMEM((2, texts, width), bf16),
            pltpu.VMEM((2, keys, width), bf16),
            pltpu.SemaphoreType.DMA((2,)),
        ],
        compiler_params=pltpu.CompilerParams(vmem_limit_bytes=40 << 20),
        cost_estimate=pl.CostEstimate(
            flops=4 * groups * rows * width * (texts + 2 * keys),
            bytes_accessed=4 * width * (texts + 2 * keys),
            transcendentals=groups * rows * (texts + keys) * (width // HD),
        ),
    )(*parts, *query_parts, text_kv, stale_kv)


def order_kernel(groups, *refs):
    parts, out = refs[:SPREAD], refs[SPREAD]
    _, spot = place(groups)
    rows = parts[0].shape[0]
    for twist in range(SPREAD):
        out[pl.ds(aligned(jnp.bitwise_xor(spot, twist), rows), rows), :] = parts[twist][...]


def order(groups, parts):
    rows, width = parts[0].shape
    return pl.pallas_call(
        functools.partial(order_kernel, groups),
        out_shape=jax.ShapeDtypeStruct((SPREAD * rows, width), jnp.bfloat16),
        in_specs=[VMEM] * SPREAD,
        out_specs=VMEM,
        compiler_params=pltpu.CompilerParams(vmem_limit_bytes=16 << 20),
        cost_estimate=pl.CostEstimate(flops=0, bytes_accessed=4 * SPREAD * rows * width, transcendentals=0),
    )(*parts)


def project_kernel(groups, halves, *refs):
    parts, weight, refs = refs[:groups], refs[groups], refs[groups + 1 :]
    outs, (total,) = refs[:groups], refs[groups:]
    group, _ = place(groups)
    half = lax.axis_index("head")
    width = parts[0].shape[1]
    rows = outs[0].shape[0]
    for slot in range(groups):
        origin = lax.rem(group - slot + groups, groups)
        term = lax.dot_general(
            parts[slot][...],
            weight[:, pl.ds(aligned(origin, width), width)],
            NT,
            preferred_element_type=jnp.float32,
        )
        if slot == 0:
            total[...] = term
        else:
            total[...] += term
    first = lax.rem(group, groups // halves) * halves + half
    for turn in range(groups):
        target = lax.rem(first + turn, groups)
        outs[turn][...] = total[pl.ds(aligned(target, rows), rows), :].astype(jnp.bfloat16)


def project(groups, halves, parts, weight):
    tokens, width = parts[0].shape
    columns = weight.shape[0]
    shape = jax.ShapeDtypeStruct((tokens // groups, columns), jnp.bfloat16)
    return pl.pallas_call(
        functools.partial(project_kernel, groups, halves),
        out_shape=[shape] * groups,
        in_specs=[VMEM] * (groups + 1),
        out_specs=[VMEM] * groups,
        scratch_shapes=[pltpu.VMEM((tokens, columns), jnp.float32)],
        compiler_params=pltpu.CompilerParams(vmem_limit_bytes=24 << 20),
        cost_estimate=pl.CostEstimate(
            flops=2 * tokens * columns * width * groups,
            bytes_accessed=2 * columns * width * groups,
            transcendentals=0,
        ),
    )(*parts, weight)


def finish_kernel(groups, halves, *refs):
    parts, (bias, gate, out, held) = refs[:groups], refs[groups:]
    group, _ = place(groups)
    columns = parts[0].shape[1]
    for turn in range(groups):
        held[lax.rem(group - turn + groups, groups)] = parts[turn][...]
    for block in range(groups // halves):
        cols = slice(block * columns, (block + 1) * columns)
        total = bias[:, cols]
        for half in range(halves):
            total = total + held[block * halves + half].astype(jnp.float32)
        out[:, cols] = (gate[:, cols] * total).astype(jnp.bfloat16)


def finish(groups, halves, parts, bias, gate):
    rows, columns = parts[0].shape
    width = columns * groups // halves
    return pl.pallas_call(
        functools.partial(finish_kernel, groups, halves),
        out_shape=jax.ShapeDtypeStruct((rows, width), jnp.bfloat16),
        in_specs=[VMEM] * (groups + 2),
        out_specs=VMEM,
        scratch_shapes=[pltpu.VMEM((groups, rows, columns), jnp.bfloat16)],
        compiler_params=pltpu.CompilerParams(vmem_limit_bytes=16 << 20),
        cost_estimate=pl.CostEstimate(flops=3 * rows * width, bytes_accessed=4 * rows * width, transcendentals=0),
    )(*parts, bias.reshape(1, width), gate.reshape(1, width))


def grouped_body(groups, halves, queries, stale_kv, codes, exponents, text_kv, out_weight, out_bias, out_gate):
    size = groups * SPREAD

    def to_group(value, turn):
        pairs = [(p, (p // SPREAD + turn) % groups * SPREAD + p % SPREAD) for p in range(size)]
        return lax.ppermute(value, "patch", pairs)

    def swap(value, twist):
        return lax.ppermute(value, "patch", [(p, p ^ twist) for p in range(size)])

    def spread(value):
        far = swap(value, 2)
        return [value, swap(value, 1), far, swap(far, 1)]

    residuals, query_parts = pack(groups, queries, codes, exponents)
    parts = []
    for turn in range(groups):
        parts += spread(residuals[turn] if turn == 0 else to_group(residuals[turn], turn))
    query_parts = [q if turn == 0 else to_group(q, turn) for turn, q in enumerate(query_parts)]
    weight = order(groups, spread(out_weight.T))
    attended = attend(groups, parts, query_parts, text_kv, stale_kv)
    attended_parts = [attended] + [to_group(attended, turn) for turn in range(1, groups)]
    terms = project(groups, halves, attended_parts, weight)
    per = groups // halves
    arrived = []
    for turn, term in enumerate(terms):
        pairs = []
        for p in range(size):
            for half in range(halves):
                group, spot = divmod(p, SPREAD)
                target = (group % per * halves + half + turn) % groups
                pairs.append((p * halves + half, (target * SPREAD + spot) * halves + group // per))
        arrived.append(lax.ppermute(term, ("patch", "head"), pairs))
    return finish(groups, halves, arrived, out_bias, out_gate)


def solution(mesh):
    patches, halves = mesh.shape["patch"], mesh.shape["head"]
    placed = (
        P("patch", "head"),
        P(None, None, "head"),
        P(None, "patch", "head"),
        P(None, "patch", "head"),
        P(None, None, "head"),
        P("head", "patch"),
        P("head"),
        P("head"),
    )

    def body(*args):
        heads = args[0].shape[1] // HD
        groups = patches // SPREAD
        if patches % SPREAD or heads % groups or groups % halves:
            return plain_body(*args)
        return grouped_body(groups, halves, *args)

    return jax.shard_map(body, mesh=mesh, in_specs=placed, out_specs=P("patch", "head"), check_vma=False)
```

time: 178 us -> 78.8 us (0.44)
  waiting for transfers between devices: 114 us -> 26.6 us
  starting transfers between devices: 0.08 us -> 39.8 us
  matrix products: 16.4 us -> 0 us
  local copies, waits for them, and re-layouts: 22.9 us -> 7.02 us
  between operations: 13.2 us -> 0.16 us
  other arithmetic: 10.6 us -> 0 us
  Pallas kernels: 0 us -> 4.79 us
    all_gather x2 -> x0, waiting for transfers between devices: 99.6 us -> none  [the longest x1 51.4 us: body(): lax.all_gather(out_weight, 'patch', axis=1, tiled=True)]
    ppermute x0 -> x28, starting transfers between devices: none -> 39.8 us  [the longest x9 16.2 us: to_group(): return lax.ppermute(value, 'patch', pairs)]
    ppermute x0 -> x28, waiting for transfers between devices: none -> 26.6 us  [the longest x9 13.8 us: to_group(): return lax.ppermute(value, 'patch', pairs)]
    slice x4 -> x0, local copies, waits for them, and re-layouts: 20 us -> none  [the longest x2 10.7 us: body(): rebuilt[1]]
    dot_general x5 -> x0, matrix products: 16.4 us -> none  [the longest x1 7.35 us: body(): jnp.dot(attended, lax.all_gather(out_weight, 'patch', axis=1, tiled=True)...]
    reduce_scatter x1 -> x0, waiting for transfers between devices: 13.6 us -> none  [body(): lax.psum_scatter(partial_terms, 'head', scatter_dimension=1, tiled=True)]
    add x1 -> x0, other arithmetic: 5.25 us -> none  [body(): stale_heads.astype(jnp.float32) + arrived_heads.astype(jnp.float32)]
    pallas_call x0 -> x5, Pallas kernels: none -> 4.79 us  [the longest x1 2.58 us: attend(): pl.pallas_call(functools.partial(attend_kernel, groups), out_shape=jax.Sh...]
  transfers between devices with their start and end apart: 3 -> 28, of which waited for: 3 -> 13; matrix products, arithmetic and copies ran while one was open for 21% -> 1% of each run, Pallas kernels for 0% -> 4%
where the time goes in v1:
time: 78.8 us; the launch traced here: 78.4 us
  starting transfers between devices  39.8 us (51%)
  waiting for transfers between devices  26.6 us (34%)
  local copies, waits for them, and re-layouts  7.02 us (9%)
  Pallas kernels  4.79 us (6%)
    ppermute x9, starting transfers between devices, to_group(): return lax.ppermute(value, 'patch', pairs)  16.2 us
    ppermute x4, starting transfers between devices, grouped_body(): arrived.append(lax.ppermute(term, ('patch', 'head'), pairs))  14.4 us
    ppermute x9, waiting for transfers between devices, to_group(): return lax.ppermute(value, 'patch', pairs)  13.8 us
    ppermute x15, waiting for transfers between devices, swap(): return lax.ppermute(value, 'patch', [(p, p ^ twist) for p in range(size)])  10.9 us
    ppermute x15, starting transfers between devices, swap(): return lax.ppermute(value, 'patch', [(p, p ^ twist) for p in range(size)])  9.25 us
    unnamed x15, local copies, waits for them, and re-layouts  7.01 us
    pallas_call x1, Pallas kernels, attend(): pl.pallas_call(functools.partial(attend_kernel, groups), out_shape=jax.Sh...  2.58 us
    ppermute x4, waiting for transfers between devices, grouped_body(): arrived.append(lax.ppermute(term, ('patch', 'head'), pairs))  1.89 us
  transfers between devices with their start and end apart: 28, of which 13 were waited for; matrix products, arithmetic and copies ran while one was open for 1% of the time, Pallas kernels for 4%

profile of v1, /device:TPU:0, one launch (start us, length us, event | category | flops | bytes accessed | tf_op | source)
XLA Modules:
  0.0 78.4 jit_solution(2247903912303339017)
XLA Ops:
  0.0 2.9 %collective-permute-start.22 = (bf16[192,1536]{1,0:T(8,128)(2,1)}, bf16[192,1536]{1,0:T(8,128)(2,1)S(1)}, u32[]{:S(2)}, u32[]{:S(2)}) collective-permute-start(bf16[192,1536]{1,0:T(8,128)(2,1)} %bitcast.1), channel_id=1, source_target_pairs={{0,4},{2,6},{4,0},{6,2},{8,12},{10,14},{12,8},{14,10},{16,20},{18,... | collective-permute-start | bytes 1769480 | tf_op jit(solution)/shard_map/ppermute | solution.py:275
  2.9 0.8 %copy.9.exponents = s32[2,48,12]{2,1,0:T(8,128)S(1)} copy(s32[2,48,12]{1,0,2:T(2,128)} %param.11) | data formatting | bytes 9216 | tf_op args[3]
  3.7 1.1 %copy-done.3 = s32[2,48,1536]{2,1,0:T(8,128)S(1)} copy-done((s32[2,48,1536]{2,1,0:T(8,128)S(1)}, s32[2,48,1536]{2,1,0:T(8,128)}, u32[]{:S(2)}) %copy-start.3) | copy-done | bytes 589848
  4.8 0.9 %copy-done.4 = bf16[48,1536]{1,0:T(8,128)(2,1)S(1)} copy-done((bf16[48,1536]{1,0:T(8,128)(2,1)S(1)}, bf16[48,1536]{1,0:T(8,128)(2,1)}, u32[]{:S(2)}) %copy-start.4) | copy-done | bytes 147480
  6.0 1.6 %collective-permute-start.15 = (bf16[48,384]{1,0:T(8,128)(2,1)S(1)}, bf16[48,384]{1,0:T(8,128)(2,1)S(1)}, u32[]{:S(2)}, u32[]{:S(2)}) collective-permute-start(bf16[48,384]{1,0:T(8,128)(2,1)S(1)} %get-tuple-element.22), channel_id=1, source_target_pairs={{0,8},{2,10},{4,12},{6,14},{8,16},{10,18},{12,20},{14,22},{16,24},... | collective-permute-start | bytes 110600 | tf_op jit(solution)/shard_map/ppermute | solution.py:272
  7.7 2.6 %collective-permute-start.16 = (bf16[48,384]{1,0:T(8,128)(2,1)S(1)}, bf16[48,384]{1,0:T(8,128)(2,1)S(1)}, u32[]{:S(2)}, u32[]{:S(2)}) collective-permute-start(bf16[48,384]{1,0:T(8,128)(2,1)S(1)} %get-tuple-element.23), channel_id=1, source_target_pairs={{0,16},{2,18},{4,20},{6,22},{8,24},{10,26},{12,28},{14,30},{16,0},... | collective-permute-start | bytes 110600 | tf_op jit(solution)/shard_map/ppermute | solution.py:272
  10.3 1.3 %collective-permute-start.17 = (bf16[48,384]{1,0:T(8,128)(2,1)S(1)}, bf16[48,384]{1,0:T(8,128)(2,1)S(1)}, u32[]{:S(2)}, u32[]{:S(2)}) collective-permute-start(bf16[48,384]{1,0:T(8,128)(2,1)S(1)} %get-tuple-element.24), channel_id=1, source_target_pairs={{0,24},{2,26},{4,28},{6,30},{8,0},{10,2},{12,4},{14,6},{16,8},{18,... | collective-permute-start | bytes 110600 | tf_op jit(solution)/shard_map/ppermute | solution.py:272
  11.6 4.9 %collective-permute-done.22.refs_2_ = bf16[192,1536]{1,0:T(8,128)(2,1)S(1)} collective-permute-done((bf16[192,1536]{1,0:T(8,128)(2,1)}, bf16[192,1536]{1,0:T(8,128)(2,1)S(1)}, u32[]{:S(2)}, u32[]{:S(2)}) %collective-permute-start.22) | collective-permute-done | bytes 589856 | tf_op jit(solution)/shard_map/ppermute | solution.py:275
  16.5 2.8 %collective-permute-start.7 = (bf16[2,48,384]{2,1,0:T(8,128)(2,1)S(1)}, bf16[2,48,384]{2,1,0:T(8,128)(2,1)S(1)}, u32[]{:S(2)}, u32[]{:S(2)}) collective-permute-start(bf16[2,48,384]{2,1,0:T(8,128)(2,1)S(1)} %get-tuple-element.19), channel_id=1, source_target_pairs={{0,16},{2,18},{4,20},{6,22},{8,24},{10,26},{12,28},{14,30},{16,0},... | collective-permute-start | bytes 221192 | tf_op jit(solution)/shard_map/ppermute | solution.py:272
  19.3 1.3 %collective-permute-start.11 = (bf16[2,48,384]{2,1,0:T(8,128)(2,1)S(1)}, bf16[2,48,384]{2,1,0:T(8,128)(2,1)S(1)}, u32[]{:S(2)}, u32[]{:S(2)}) collective-permute-start(bf16[2,48,384]{2,1,0:T(8,128)(2,1)S(1)} %get-tuple-element.20), channel_id=1, source_target_pairs={{0,24},{2,26},{4,28},{6,30},{8,0},{10,2},{12,4},{14,6},{16,8},{18,... | collective-permute-start | bytes 221192 | tf_op jit(solution)/shard_map/ppermute | solution.py:272
  21.4 2.7 %collective-permute-done.7.refs_8_ = bf16[2,48,384]{2,1,0:T(8,128)(2,1)S(1)} collective-permute-done((bf16[2,48,384]{2,1,0:T(8,128)(2,1)S(1)}, bf16[2,48,384]{2,1,0:T(8,128)(2,1)S(1)}, u32[]{:S(2)}, u32[]{:S(2)}) %collective-permute-start.7) | collective-permute-done | bytes 73760 | tf_op jit(solution)/shard_map/ppermute | solution.py:272
  24.1 1.7 %collective-permute-start.1 = (bf16[2,48,384]{2,1,0:T(8,128)(2,1)S(1)}, bf16[2,48,384]{2,1,0:T(8,128)(2,1)S(1)}, u32[]{:S(2)}, u32[]{:S(2)}) collective-permute-start(bf16[2,48,384]{2,1,0:T(8,128)(2,1)S(1)} %get-tuple-element.17.refs_0_), channel_id=1, source_target_pairs={{0,4},{2,6},{4,0},{6,2},{8,12},{10,14},{12,8},{14,10},{16,20},{18,... | collective-permute-start | bytes 221192 | tf_op jit(solution)/shard_map/ppermute | solution.py:275
  25.8 1.1 %collective-permute-done.3.refs_4_ = bf16[2,48,384]{2,1,0:T(8,128)(2,1)S(1)} collective-permute-done((bf16[2,48,384]{2,1,0:T(8,128)(2,1)S(1)}, bf16[2,48,384]{2,1,0:T(8,128)(2,1)S(1)}, u32[]{:S(2)}, u32[]{:S(2)}) %collective-permute-start.3) | collective-permute-done | bytes 73760 | tf_op jit(solution)/shard_map/ppermute | solution.py:272
  26.9 1.5 %collective-permute-start.9 = (bf16[2,48,384]{2,1,0:T(8,128)(2,1)S(1)}, bf16[2,48,384]{2,1,0:T(8,128)(2,1)S(1)}, u32[]{:S(2)}, u32[]{:S(2)}) collective-permute-start(bf16[2,48,384]{2,1,0:T(8,128)(2,1)S(1)} %collective-permute-done.7.refs_8_), channel_id=1, source_target_pairs={{0,4},{2,6},{4,0},{6,2},{8,12},{10,14},{12,8},{14,10},{16,20},{18,... | collective-permute-start | bytes 221192 | tf_op jit(solution)/shard_map/ppermute | solution.py:275
  28.5 2.0 %collective-permute-start.13 = (bf16[2,48,384]{2,1,0:T(8,128)(2,1)S(1)}, bf16[2,48,384]{2,1,0:T(8,128)(2,1)S(1)}, u32[]{:S(2)}, u32[]{:S(2)}) collective-permute-start(bf16[2,48,384]{2,1,0:T(8,128)(2,1)S(1)} %collective-permute-done.11.refs_12_), channel_id=1, source_target_pairs={{0,4},{2,6},{4,0},{6,2},{8,12},{10,14},{12,8},{14,10},{16,20},{18,... | collective-permute-start | bytes 221192 | tf_op jit(solution)/shard_map/ppermute | solution.py:275
  30.5 1.3 %collective-permute-done.9.refs_10_ = bf16[2,48,384]{2,1,0:T(8,128)(2,1)S(1)} collective-permute-done((bf16[2,48,384]{2,1,0:T(8,128)(2,1)S(1)}, bf16[2,48,384]{2,1,0:T(8,128)(2,1)S(1)}, u32[]{:S(2)}, u32[]{:S(2)}) %collective-permute-start.9) | collective-permute-done | bytes 73760 | tf_op jit(solution)/shard_map/ppermute | solution.py:275
  31.8 1.0 %collective-permute-done.13.refs_14_ = bf16[2,48,384]{2,1,0:T(8,128)(2,1)S(1)} collective-permute-done((bf16[2,48,384]{2,1,0:T(8,128)(2,1)S(1)}, bf16[2,48,384]{2,1,0:T(8,128)(2,1)S(1)}, u32[]{:S(2)}, u32[]{:S(2)}) %collective-permute-start.13) | collective-permute-done | bytes 73760 | tf_op jit(solution)/shard_map/ppermute | solution.py:275
  32.8 2.0 %collective-permute-done.5.refs_6_ = bf16[2,48,384]{2,1,0:T(8,128)(2,1)S(1)} collective-permute-done((bf16[2,48,384]{2,1,0:T(8,128)(2,1)S(1)}, bf16[2,48,384]{2,1,0:T(8,128)(2,1)S(1)}, u32[]{:S(2)}, u32[]{:S(2)}) %collective-permute-start.5) | collective-permute-done | bytes 73760 | tf_op jit(solution)/shard_map/ppermute | solution.py:275
  36.6 0.7 collective-permute-done.14.refs_15_
  37.5 2.3 %copy-done = bf16[2,768,1536]{2,1,0:T(8,128)(2,1)S(1)} copy-done((bf16[2,768,1536]{2,1,0:T(8,128)(2,1)S(1)}, bf16[2,768,1536]{2,1,0:T(8,128)(2,1)}, u32[]{:S(2)}) %copy-start) | copy-done | bytes 4718616
  39.9 1.9 %copy-done.1 = bf16[2,512,1536]{2,1,0:T(8,128)(2,1)S(1)} copy-done((bf16[2,512,1536]{2,1,0:T(8,128)(2,1)S(1)}, bf16[2,512,1536]{2,1,0:T(8,128)(2,1)}, u32[]{:S(2)}) %copy-start.1) | copy-done | bytes 3145752
  41.8 2.6 %shard_map.83.refs_0_ = bf16[192,384]{1,0:T(8,128)(2,1)S(1)} custom-call(bf16[2,48,384]{2,1,0:T(8,128)(2,1)S(1)} %get-tuple-element.17.refs_0_, bf16[2,48,384]{2,1,0:T(8,128)(2,1)S(1)} %collective-permute-done.refs_1_, bf16[2,48,384]{2,1,0:T(8,128)(2,1)S(1)} %collective-permute-done.1.refs_2_, bf16[2,48,384]{2,1,0:T(8,128)(2,1)S(1)} %collective-permute-done.2.refs_3_, ...), custom_call_target="tpu_custom_call" | custom-call | flops 603979776 | bytes 3145728 | tf_op jit(solution)/shard_map/pallas_call | solution.py:154
  44.4 1.6 %collective-permute-start.18 = (bf16[192,384]{1,0:T(8,128)(2,1)S(1)}, bf16[192,384]{1,0:T(8,128)(2,1)S(1)}, u32[]{:S(2)}, u32[]{:S(2)}) collective-permute-start(bf16[192,384]{1,0:T(8,128)(2,1)S(1)} %shard_map.83.refs_0_), channel_id=1, source_target_pairs={{0,8},{2,10},{4,12},{6,14},{8,16},{10,18},{12,20},{14,22},{16,24},... | collective-permute-start | bytes 442376 | tf_op jit(solution)/shard_map/ppermute | solution.py:272
  46.0 4.1 %collective-permute-start.19 = (bf16[192,384]{1,0:T(8,128)(2,1)S(1)}, bf16[192,384]{1,0:T(8,128)(2,1)S(1)}, u32[]{:S(2)}, u32[]{:S(2)}) collective-permute-start(bf16[192,384]{1,0:T(8,128)(2,1)S(1)} %shard_map.83.refs_0_), channel_id=1, source_target_pairs={{0,16},{2,18},{4,20},{6,22},{8,24},{10,26},{12,28},{14,30},{16,0},... | collective-permute-start | bytes 442376 | tf_op jit(solution)/shard_map/ppermute | solution.py:272
  50.3 4.0 %collective-permute-done.18.refs_1_ = bf16[192,384]{1,0:T(8,128)(2,1)S(1)} collective-permute-done((bf16[192,384]{1,0:T(8,128)(2,1)S(1)}, bf16[192,384]{1,0:T(8,128)(2,1)S(1)}, u32[]{:S(2)}, u32[]{:S(2)}) %collective-permute-start.18) | collective-permute-done | bytes 147488 | tf_op jit(solution)/shard_map/ppermute | solution.py:272
  54.4 5.9 %collective-permute-done.19.refs_2_ = bf16[192,384]{1,0:T(8,128)(2,1)S(1)} collective-permute-done((bf16[192,384]{1,0:T(8,128)(2,1)S(1)}, bf16[192,384]{1,0:T(8,128)(2,1)S(1)}, u32[]{:S(2)}, u32[]{:S(2)}) %collective-permute-start.19) | collective-permute-done | bytes 147488 | tf_op jit(solution)/shard_map/ppermute | solution.py:272
  60.3 1.0 %shard_map.85 = (bf16[48,768]{1,0:T(8,128)(2,1)S(1)}, bf16[48,768]{1,0:T(8,128)(2,1)S(1)}, bf16[48,768]{1,0:T(8,128)(2,1)S(1)}, bf16[48,768]{1,0:T(8,128)(2,1)S(1)}) custom-call(bf16[192,384]{1,0:T(8,128)(2,1)S(1)} %shard_map.83.refs_0_, bf16[192,384]{1,0:T(8,128)(2,1)S(1)} %collective-permute-done.18.refs_1_, ...), custom_call_target="tpu_custom_call" | custom-call | flops 452984832 | bytes 2359296 | tf_op jit(solution)/shard_map/pallas_call | solution.py:224
  62.0 6.8 %collective-permute-start.25 = (bf16[48,768]{1,0:T(8,128)(2,1)S(1)}, bf16[48,768]{1,0:T(8,128)(2,1)S(1)}, u32[]{:S(2)}, u32[]{:S(2)}) collective-permute-start(bf16[48,768]{1,0:T(8,128)(2,1)S(1)} %get-tuple-element.26), channel_id=1, source_target_pairs={{0,8},{1,16},{2,10},{3,18},{4,12},{5,20},{6,14},{7,22},{8,24},{9,0... | collective-permute-start | bytes 221192 | tf_op jit(solution)/shard_map/ppermute | solution.py:299
  68.8 2.5 %collective-permute-start.26 = (bf16[48,768]{1,0:T(8,128)(2,1)S(1)}, bf16[48,768]{1,0:T(8,128)(2,1)S(1)}, u32[]{:S(2)}, u32[]{:S(2)}) collective-permute-start(bf16[48,768]{1,0:T(8,128)(2,1)S(1)} %get-tuple-element.27), channel_id=1, source_target_pairs={{0,16},{1,24},{2,18},{3,26},{4,20},{5,28},{6,22},{7,30},{8,0},{9,8... | collective-permute-start | bytes 221192 | tf_op jit(solution)/shard_map/ppermute | solution.py:299
  71.3 4.4 %collective-permute-start.27 = (bf16[48,768]{1,0:T(8,128)(2,1)S(1)}, bf16[48,768]{1,0:T(8,128)(2,1)S(1)}, u32[]{:S(2)}, u32[]{:S(2)}) collective-permute-start(bf16[48,768]{1,0:T(8,128)(2,1)S(1)} %get-tuple-element.28), channel_id=1, source_target_pairs={{0,24},{1,0},{2,26},{3,2},{4,28},{5,4},{6,30},{7,6},{8,8},{9,16},{... | collective-permute-start | bytes 221192 | tf_op jit(solution)/shard_map/ppermute | solution.py:299
  75.8 1.9 %collective-permute-done.27.refs_3_ = bf16[48,768]{1,0:T(8,128)(2,1)S(1)} collective-permute-done((bf16[48,768]{1,0:T(8,128)(2,1)S(1)}, bf16[48,768]{1,0:T(8,128)(2,1)S(1)}, u32[]{:S(2)}, u32[]{:S(2)}) %collective-permute-start.27) | collective-permute-done | bytes 73760 | tf_op jit(solution)/shard_map/ppermute | solution.py:299
  77.6 0.8 shard_map.86
  (46 shorter events, 4.0 us)
Async XLA Ops:
  0.0 16.5 %collective-permute-start.22 = (bf16[192,1536]{1,0:T(8,128)(2,1)}, bf16[192,1536]{1,0:T(8,128)(2,1)S(1)}, u32[]{:S(2)}, u32[]{:S(2)}) collective-permute-start(bf16[192,1536]{1,0:T(8,128)(2,1)} %bitcast.1), channel_id=1, source_target_pairs={{0,4},{2,6},{4,0},{6,2},{8,12},{10,14},{12,8},{14,10},{16,20},{18,... | collective-permute-start | bytes 1769480 | tf_op jit(solution)/shard_map/ppermute | solution.py:275
  6.0 10.5 %collective-permute-start.15 = (bf16[48,384]{1,0:T(8,128)(2,1)S(1)}, bf16[48,384]{1,0:T(8,128)(2,1)S(1)}, u32[]{:S(2)}, u32[]{:S(2)}) collective-permute-start(bf16[48,384]{1,0:T(8,128)(2,1)S(1)} %get-tuple-element.22), channel_id=1, source_target_pairs={{0,8},{2,10},{4,12},{6,14},{8,16},{10,18},{12,20},{14,22},{16,24},... | collective-permute-start | bytes 110600 | tf_op jit(solution)/shard_map/ppermute | solution.py:272
  7.7 11.7 %collective-permute-start.16 = (bf16[48,384]{1,0:T(8,128)(2,1)S(1)}, bf16[48,384]{1,0:T(8,128)(2,1)S(1)}, u32[]{:S(2)}, u32[]{:S(2)}) collective-permute-start(bf16[48,384]{1,0:T(8,128)(2,1)S(1)} %get-tuple-element.23), channel_id=1, source_target_pairs={{0,16},{2,18},{4,20},{6,22},{8,24},{10,26},{12,28},{14,30},{16,0},... | collective-permute-start | bytes 110600 | tf_op jit(solution)/shard_map/ppermute | solution.py:272
  10.3 10.4 %collective-permute-start.17 = (bf16[48,384]{1,0:T(8,128)(2,1)S(1)}, bf16[48,384]{1,0:T(8,128)(2,1)S(1)}, u32[]{:S(2)}, u32[]{:S(2)}) collective-permute-start(bf16[48,384]{1,0:T(8,128)(2,1)S(1)} %get-tuple-element.24), channel_id=1, source_target_pairs={{0,24},{2,26},{4,28},{6,30},{8,0},{10,2},{12,4},{14,6},{16,8},{18,... | collective-permute-start | bytes 110600 | tf_op jit(solution)/shard_map/ppermute | solution.py:272
  11.6 38.5 %collective-permute-start.21 = (bf16[192,1536]{1,0:T(8,128)(2,1)}, bf16[192,1536]{1,0:T(8,128)(2,1)S(1)}, u32[]{:S(2)}, u32[]{:S(2)}) collective-permute-start(bf16[192,1536]{1,0:T(8,128)(2,1)} %bitcast.2), channel_id=1, source_target_pairs={{0,2},{2,0},{4,6},{6,4},{8,10},{10,8},{12,14},{14,12},{16,18},{18,... | collective-permute-start | bytes 1769480 | tf_op jit(solution)/shard_map/ppermute | solution.py:275
  16.5 33.7 %collective-permute-start.23 = (bf16[192,1536]{1,0:T(8,128)(2,1)S(1)}, bf16[192,1536]{1,0:T(8,128)(2,1)S(1)}, u32[]{:S(2)}, u32[]{:S(2)}) collective-permute-start(bf16[192,1536]{1,0:T(8,128)(2,1)S(1)} %collective-permute-done.22.refs_2_), channel_id=1, source_target_pairs={{0,2},{2,0},{4,6},{6,4},{8,10},{10,8},{12,14},{14,12},{16,18},{18,... | collective-permute-start | bytes 1769480 | tf_op jit(solution)/shard_map/ppermute | solution.py:275
  16.5 7.6 %collective-permute-start.7 = (bf16[2,48,384]{2,1,0:T(8,128)(2,1)S(1)}, bf16[2,48,384]{2,1,0:T(8,128)(2,1)S(1)}, u32[]{:S(2)}, u32[]{:S(2)}) collective-permute-start(bf16[2,48,384]{2,1,0:T(8,128)(2,1)S(1)} %get-tuple-element.19), channel_id=1, source_target_pairs={{0,16},{2,18},{4,20},{6,22},{8,24},{10,26},{12,28},{14,30},{16,0},... | collective-permute-start | bytes 221192 | tf_op jit(solution)/shard_map/ppermute | solution.py:272
  19.3 6.4 %collective-permute-start.11 = (bf16[2,48,384]{2,1,0:T(8,128)(2,1)S(1)}, bf16[2,48,384]{2,1,0:T(8,128)(2,1)S(1)}, u32[]{:S(2)}, u32[]{:S(2)}) collective-permute-start(bf16[2,48,384]{2,1,0:T(8,128)(2,1)S(1)} %get-tuple-element.20), channel_id=1, source_target_pairs={{0,24},{2,26},{4,28},{6,30},{8,0},{10,2},{12,4},{14,6},{16,8},{18,... | collective-permute-start | bytes 221192 | tf_op jit(solution)/shard_map/ppermute | solution.py:272
  20.7 6.2 %collective-permute-start.3 = (bf16[2,48,384]{2,1,0:T(8,128)(2,1)S(1)}, bf16[2,48,384]{2,1,0:T(8,128)(2,1)S(1)}, u32[]{:S(2)}, u32[]{:S(2)}) collective-permute-start(bf16[2,48,384]{2,1,0:T(8,128)(2,1)S(1)} %get-tuple-element.18), channel_id=1, source_target_pairs={{0,8},{2,10},{4,12},{6,14},{8,16},{10,18},{12,20},{14,22},{16,24},... | collective-permute-start | bytes 221192 | tf_op jit(solution)/shard_map/ppermute | solution.py:272
  24.1 4.4 %collective-permute-start.1 = (bf16[2,48,384]{2,1,0:T(8,128)(2,1)S(1)}, bf16[2,48,384]{2,1,0:T(8,128)(2,1)S(1)}, u32[]{:S(2)}, u32[]{:S(2)}) collective-permute-start(bf16[2,48,384]{2,1,0:T(8,128)(2,1)S(1)} %get-tuple-element.17.refs_0_), channel_id=1, source_target_pairs={{0,4},{2,6},{4,0},{6,2},{8,12},{10,14},{12,8},{14,10},{16,20},{18,... | collective-permute-start | bytes 221192 | tf_op jit(solution)/shard_map/ppermute | solution.py:275
  25.8 4.7 %collective-permute-start = (bf16[2,48,384]{2,1,0:T(8,128)(2,1)S(1)}, bf16[2,48,384]{2,1,0:T(8,128)(2,1)S(1)}, u32[]{:S(2)}, u32[]{:S(2)}) collective-permute-start(bf16[2,48,384]{2,1,0:T(8,128)(2,1)S(1)} %get-tuple-element.17.refs_0_), channel_id=1, source_target_pairs={{0,2},{2,0},{4,6},{6,4},{8,10},{10,8},{12,14},{14,12},{16,18},{18,... | collective-permute-start | bytes 221192 | tf_op jit(solution)/shard_map/ppermute | solution.py:275
  26.9 4.9 %collective-permute-start.9 = (bf16[2,48,384]{2,1,0:T(8,128)(2,1)S(1)}, bf16[2,48,384]{2,1,0:T(8,128)(2,1)S(1)}, u32[]{:S(2)}, u32[]{:S(2)}) collective-permute-start(bf16[2,48,384]{2,1,0:T(8,128)(2,1)S(1)} %collective-permute-done.7.refs_8_), channel_id=1, source_target_pairs={{0,4},{2,6},{4,0},{6,2},{8,12},{10,14},{12,8},{14,10},{16,20},{18,... | collective-permute-start | bytes 221192 | tf_op jit(solution)/shard_map/ppermute | solution.py:275
  28.5 4.4 %collective-permute-start.13 = (bf16[2,48,384]{2,1,0:T(8,128)(2,1)S(1)}, bf16[2,48,384]{2,1,0:T(8,128)(2,1)S(1)}, u32[]{:S(2)}, u32[]{:S(2)}) collective-permute-start(bf16[2,48,384]{2,1,0:T(8,128)(2,1)S(1)} %collective-permute-done.11.refs_12_), channel_id=1, source_target_pairs={{0,4},{2,6},{4,0},{6,2},{8,12},{10,14},{12,8},{14,10},{16,20},{18,... | collective-permute-start | bytes 221192 | tf_op jit(solution)/shard_map/ppermute | solution.py:275
  30.5 4.4 %collective-permute-start.5 = (bf16[2,48,384]{2,1,0:T(8,128)(2,1)S(1)}, bf16[2,48,384]{2,1,0:T(8,128)(2,1)S(1)}, u32[]{:S(2)}, u32[]{:S(2)}) collective-permute-start(bf16[2,48,384]{2,1,0:T(8,128)(2,1)S(1)} %collective-permute-done.3.refs_4_), channel_id=1, source_target_pairs={{0,4},{2,6},{4,0},{6,2},{8,12},{10,14},{12,8},{14,10},{16,20},{18,... | collective-permute-start | bytes 221192 | tf_op jit(solution)/shard_map/ppermute | solution.py:275
  31.8 3.0 %collective-permute-start.2 = (bf16[2,48,384]{2,1,0:T(8,128)(2,1)S(1)}, bf16[2,48,384]{2,1,0:T(8,128)(2,1)S(1)}, u32[]{:S(2)}, u32[]{:S(2)}) collective-permute-start(bf16[2,48,384]{2,1,0:T(8,128)(2,1)S(1)} %collective-permute-done.1.refs_2_), channel_id=1, source_target_pairs={{0,2},{2,0},{4,6},{6,4},{8,10},{10,8},{12,14},{14,12},{16,18},{18,... | collective-permute-start | bytes 221192 | tf_op jit(solution)/shard_map/ppermute | solution.py:275
  32.8 2.5 %collective-permute-start.12 = (bf16[2,48,384]{2,1,0:T(8,128)(2,1)S(1)}, bf16[2,48,384]{2,1,0:T(8,128)(2,1)S(1)}, u32[]{:S(2)}, u32[]{:S(2)}) collective-permute-start(bf16[2,48,384]{2,1,0:T(8,128)(2,1)S(1)} %collective-permute-done.11.refs_12_), channel_id=1, source_target_pairs={{0,2},{2,0},{4,6},{6,4},{8,10},{10,8},{12,14},{14,12},{16,18},{18,... | collective-permute-start | bytes 221192 | tf_op jit(solution)/shard_map/ppermute | solution.py:275
  34.8 1.3 %collective-permute-start.4 = (bf16[2,48,384]{2,1,0:T(8,128)(2,1)S(1)}, bf16[2,48,384]{2,1,0:T(8,128)(2,1)S(1)}, u32[]{:S(2)}, u32[]{:S(2)}) collective-permute-start(bf16[2,48,384]{2,1,0:T(8,128)(2,1)S(1)} %collective-permute-done.3.refs_4_), channel_id=1, source_target_pairs={{0,2},{2,0},{4,6},{6,4},{8,10},{10,8},{12,14},{14,12},{16,18},{18,... | collective-permute-start | bytes 221192 | tf_op jit(solution)/shard_map/ppermute | solution.py:275
  34.9 1.4 %collective-permute-start.8 = (bf16[2,48,384]{2,1,0:T(8,128)(2,1)S(1)}, bf16[2,48,384]{2,1,0:T(8,128)(2,1)S(1)}, u32[]{:S(2)}, u32[]{:S(2)}) collective-permute-start(bf16[2,48,384]{2,1,0:T(8,128)(2,1)S(1)} %collective-permute-done.7.refs_8_), channel_id=1, source_target_pairs={{0,2},{2,0},{4,6},{6,4},{8,10},{10,8},{12,14},{14,12},{16,18},{18,... | collective-permute-start | bytes 221192 | tf_op jit(solution)/shard_map/ppermute | solution.py:275
  35.4 1.3 %collective-permute-start.10 = (bf16[2,48,384]{2,1,0:T(8,128)(2,1)S(1)}, bf16[2,48,384]{2,1,0:T(8,128)(2,1)S(1)}, u32[]{:S(2)}, u32[]{:S(2)}) collective-permute-start(bf16[2,48,384]{2,1,0:T(8,128)(2,1)S(1)} %collective-permute-done.9.refs_10_), channel_id=1, source_target_pairs={{0,2},{2,0},{4,6},{6,4},{8,10},{10,8},{12,14},{14,12},{16,18},{18,... | collective-permute-start | bytes 221192 | tf_op jit(solution)/shard_map/ppermute | solution.py:275
  36.1 1.3 %collective-permute-start.14 = (bf16[2,48,384]{2,1,0:T(8,128)(2,1)S(1)}, bf16[2,48,384]{2,1,0:T(8,128)(2,1)S(1)}, u32[]{:S(2)}, u32[]{:S(2)}) collective-permute-start(bf16[2,48,384]{2,1,0:T(8,128)(2,1)S(1)} %collective-permute-done.13.refs_14_), channel_id=1, source_target_pairs={{0,2},{2,0},{4,6},{6,4},{8,10},{10,8},{12,14},{14,12},{16,18},{18,... | collective-permute-start | bytes 221192 | tf_op jit(solution)/shard_map/ppermute | solution.py:275
  36.3 1.3 %collective-permute-start.6 = (bf16[2,48,384]{2,1,0:T(8,128)(2,1)S(1)}, bf16[2,48,384]{2,1,0:T(8,128)(2,1)S(1)}, u32[]{:S(2)}, u32[]{:S(2)}) collective-permute-start(bf16[2,48,384]{2,1,0:T(8,128)(2,1)S(1)} %collective-permute-done.5.refs_6_), channel_id=1, source_target_pairs={{0,2},{2,0},{4,6},{6,4},{8,10},{10,8},{12,14},{14,12},{16,18},{18,... | collective-permute-start | bytes 221192 | tf_op jit(solution)/shard_map/ppermute | solution.py:275
  37.5 2.3 %copy-start = (bf16[2,768,1536]{2,1,0:T(8,128)(2,1)S(1)}, bf16[2,768,1536]{2,1,0:T(8,128)(2,1)}, u32[]{:S(2)}) copy-start(bf16[2,768,1536]{2,1,0:T(8,128)(2,1)} %refs_21_.1) | copy-start | bytes 14155780
  41.8 8.4 %copy-start.2 = (bf16[1536,192]{0,1:T(8,128)(2,1)S(1)}, bf16[1536,192]{0,1:T(8,128)(2,1)}, u32[]{:S(2)}) copy-start(bf16[1536,192]{0,1:T(8,128)(2,1)} %param.13) | copy-start | bytes 1769476
  44.4 31.3 %copy-start.5 = (f32[1536]{0:T(1024)S(1)}, f32[1536]{0:T(1024)}, u32[]{:S(2)}) copy-start(f32[1536]{0:T(1024)} %param.14) | copy-start | bytes 18436
  44.4 31.3 %copy-start.6 = (f32[1536]{0:T(1024)S(1)}, f32[1536]{0:T(1024)}, u32[]{:S(2)}) copy-start(f32[1536]{0:T(1024)} %param.15) | copy-start | bytes 18436
  44.4 10.0 %collective-permute-start.18 = (bf16[192,384]{1,0:T(8,128)(2,1)S(1)}, bf16[192,384]{1,0:T(8,128)(2,1)S(1)}, u32[]{:S(2)}, u32[]{:S(2)}) collective-permute-start(bf16[192,384]{1,0:T(8,128)(2,1)S(1)} %shard_map.83.refs_0_), channel_id=1, source_target_pairs={{0,8},{2,10},{4,12},{6,14},{8,16},{10,18},{12,20},{14,22},{16,24},... | collective-permute-start | bytes 442376 | tf_op jit(solution)/shard_map/ppermute | solution.py:272
  46.0 14.3 %collective-permute-start.19 = (bf16[192,384]{1,0:T(8,128)(2,1)S(1)}, bf16[192,384]{1,0:T(8,128)(2,1)S(1)}, u32[]{:S(2)}, u32[]{:S(2)}) collective-permute-start(bf16[192,384]{1,0:T(8,128)(2,1)S(1)} %shard_map.83.refs_0_), channel_id=1, source_target_pairs={{0,16},{2,18},{4,20},{6,22},{8,24},{10,26},{12,28},{14,30},{16,0},... | collective-permute-start | bytes 442376 | tf_op jit(solution)/shard_map/ppermute | solution.py:272
  50.1 10.2 %collective-permute-start.20 = (bf16[192,384]{1,0:T(8,128)(2,1)S(1)}, bf16[192,384]{1,0:T(8,128)(2,1)S(1)}, u32[]{:S(2)}, u32[]{:S(2)}) collective-permute-start(bf16[192,384]{1,0:T(8,128)(2,1)S(1)} %shard_map.83.refs_0_), channel_id=1, source_target_pairs={{0,24},{2,26},{4,28},{6,30},{8,0},{10,2},{12,4},{14,6},{16,8},{18,... | collective-permute-start | bytes 442376 | tf_op jit(solution)/shard_map/ppermute | solution.py:272
  61.3 14.4 %collective-permute-start.24 = (bf16[48,768]{1,0:T(8,128)(2,1)S(1)}, bf16[48,768]{1,0:T(8,128)(2,1)S(1)}, u32[]{:S(2)}, u32[]{:S(2)}) collective-permute-start(bf16[48,768]{1,0:T(8,128)(2,1)S(1)} %get-tuple-element.25), channel_id=1, source_target_pairs={{0,0},{1,8},{2,2},{3,10},{4,4},{5,12},{6,6},{7,14},{8,16},{9,24},{... | collective-permute-start | bytes 221192 | tf_op jit(solution)/shard_map/ppermute | solution.py:299
  62.0 13.8 %collective-permute-start.25 = (bf16[48,768]{1,0:T(8,128)(2,1)S(1)}, bf16[48,768]{1,0:T(8,128)(2,1)S(1)}, u32[]{:S(2)}, u32[]{:S(2)}) collective-permute-start(bf16[48,768]{1,0:T(8,128)(2,1)S(1)} %get-tuple-element.26), channel_id=1, source_target_pairs={{0,8},{1,16},{2,10},{3,18},{4,12},{5,20},{6,14},{7,22},{8,24},{9,0... | collective-permute-start | bytes 221192 | tf_op jit(solution)/shard_map/ppermute | solution.py:299
  68.8 7.0 %collective-permute-start.26 = (bf16[48,768]{1,0:T(8,128)(2,1)S(1)}, bf16[48,768]{1,0:T(8,128)(2,1)S(1)}, u32[]{:S(2)}, u32[]{:S(2)}) collective-permute-start(bf16[48,768]{1,0:T(8,128)(2,1)S(1)} %get-tuple-element.27), channel_id=1, source_target_pairs={{0,16},{1,24},{2,18},{3,26},{4,20},{5,28},{6,22},{7,30},{8,0},{9,8... | collective-permute-start | bytes 221192 | tf_op jit(solution)/shard_map/ppermute | solution.py:299
  71.3 6.4 %collective-permute-start.27 = (bf16[48,768]{1,0:T(8,128)(2,1)S(1)}, bf16[48,768]{1,0:T(8,128)(2,1)S(1)}, u32[]{:S(2)}, u32[]{:S(2)}) collective-permute-start(bf16[48,768]{1,0:T(8,128)(2,1)S(1)} %get-tuple-element.28), channel_id=1, source_target_pairs={{0,24},{1,0},{2,26},{3,2},{4,28},{5,4},{6,30},{7,6},{8,8},{9,16},{... | collective-permute-start | bytes 221192 | tf_op jit(solution)/shard_map/ppermute | solution.py:299
  (3 other events, 3.9 us)

commit v2 on v0

v2 whole, which is shorter than its diff:
```python
import jax
import jax.numpy as jnp
from jax import lax
from jax.experimental import pallas as pl
from jax.experimental.pallas import tpu as pltpu
from jax.sharding import PartitionSpec as P

HD = 128
SPREAD = 4
VMEM = pl.BlockSpec(memory_space=pltpu.VMEM)
HBM = pl.BlockSpec(memory_space=pltpu.HBM)
NT = (((1,), (1,)), ((), ()))


def plain_body(queries, stale_kv, codes, exponents, text_kv, out_weight, out_bias, out_gate):
    tok_rows = queries.shape[0]
    row_width = queries.shape[1]
    head_count = row_width // HD
    text_count = text_kv.shape[1]
    scale_factor = HD ** (-0.5)
    blocks = jnp.exp2(exponents.astype(jnp.float32))
    decoded = codes.astype(jnp.float32).reshape(2, tok_rows, head_count, HD) * blocks[..., None]
    decoded = decoded.astype(jnp.bfloat16).reshape(2, tok_rows, row_width)
    arrived = lax.all_gather(decoded, "patch", axis=1, tiled=True)
    all_rows = arrived.shape[1]
    query_heads = queries.reshape(tok_rows, head_count, HD)
    text_heads = text_kv.reshape(2, text_count, head_count, HD)
    stale_heads = stale_kv.reshape(2, all_rows, head_count, HD)
    arrived_heads = arrived.reshape(2, all_rows, head_count, HD)
    text_scores = jnp.einsum("thd,khd->htk", query_heads, text_heads[0], preferred_element_type=jnp.float32)
    rebuilt = stale_heads.astype(jnp.float32) + arrived_heads.astype(jnp.float32)
    image_scores = jnp.einsum(
        "thd,khd->htk", query_heads.astype(jnp.float32), rebuilt[0], precision=lax.Precision.HIGHEST
    )
    scores = jnp.concatenate([text_scores, image_scores], axis=2) * scale_factor
    row_peak = jnp.max(scores, axis=2, keepdims=True)
    weights = jnp.exp(scores - row_peak).astype(jnp.bfloat16)
    row_total = jnp.sum(weights.astype(jnp.float32), axis=2)
    text_part = jnp.einsum(
        "htk,khd->thd", weights[:, :, :text_count], text_heads[1], preferred_element_type=jnp.float32
    )
    image_part = jnp.einsum(
        "htk,khd->thd",
        weights[:, :, text_count:].astype(jnp.float32),
        rebuilt[1],
        precision=lax.Precision.HIGHEST,
    )
    attended = ((text_part + image_part) / row_total.T[:, :, None]).astype(jnp.bfloat16).reshape(tok_rows, row_width)
    partial_terms = jnp.dot(
        attended, lax.all_gather(out_weight, "patch", axis=1, tiled=True), preferred_element_type=jnp.float32
    )
    column_share = lax.psum_scatter(partial_terms, "head", scatter_dimension=1, tiled=True)
    return (out_gate * (column_share + out_bias)).astype(jnp.bfloat16)


def aligned(value, step):
    return pl.multiple_of(value * step, step)


def place():
    me = lax.axis_index("patch")
    return me // SPREAD, lax.rem(me, SPREAD)


def pack_kernel(queries_hbm, codes_hbm, exponents, residual, query, codes, queries, sems):
    groups, rows, width = query.shape
    codes_copy = pltpu.make_async_copy(codes_hbm, codes, sems.at[0])
    queries_copy = pltpu.make_async_copy(queries_hbm, queries, sems.at[1])
    codes_copy.start()
    queries_copy.start()
    codes_copy.wait()
    per = width // HD
    for kind in range(2):
        scales = jnp.left_shift(1, exponents[kind] + 16).astype(jnp.float32) * (2.0**-16)
        for head in range(groups * per):
            inside = slice((head % per) * HD, (head % per + 1) * HD)
            whole = slice(head * HD, (head + 1) * HD)
            decoded = codes[kind, :, whole].astype(jnp.float32) * scales[:, head : head + 1]
            residual[head // per, kind, :, inside] = decoded.astype(jnp.bfloat16)
    queries_copy.wait()
    for group in range(groups):
        query[group] = queries[:, group * width : (group + 1) * width]


def pack(groups, queries, codes, exponents):
    rows, width = queries.shape
    share = width // groups
    bf16 = jnp.bfloat16
    return pl.pallas_call(
        pack_kernel,
        out_shape=[
            jax.ShapeDtypeStruct((groups, 2, rows, share), bf16),
            jax.ShapeDtypeStruct((groups, rows, share), bf16),
        ],
        in_specs=[HBM, HBM, VMEM],
        out_specs=[VMEM] * 2,
        scratch_shapes=[
            pltpu.VMEM(codes.shape, jnp.int32),
            pltpu.VMEM(queries.shape, bf16),
            pltpu.SemaphoreType.DMA((2,)),
        ],
        compiler_params=pltpu.CompilerParams(vmem_limit_bytes=56 << 20),
        cost_estimate=pl.CostEstimate(flops=2 * codes.size, bytes_accessed=6 * codes.size, transcendentals=0),
    )(queries, codes, exponents)


def attend_kernel(*refs):
    parts, (asked, text_hbm, stale_hbm, out, query, residual, text, stale, sems) = refs[:SPREAD], refs[SPREAD:]
    group, spot = place()
    groups, rows, width = asked.shape
    columns = pl.ds(aligned(group, width), width)
    text_copy = pltpu.make_async_copy(text_hbm.at[:, :, columns], text, sems.at[0])
    stale_copy = pltpu.make_async_copy(stale_hbm.at[:, :, columns], stale, sems.at[1])
    text_copy.start()
    stale_copy.start()
    for origin in range(groups):
        query[origin * rows : (origin + 1) * rows, :] = asked[origin]
        for twist in range(SPREAD):
            token = origin * SPREAD + jnp.bitwise_xor(spot, twist)
            residual[:, pl.ds(aligned(token, rows), rows), :] = parts[twist][origin]
    text_copy.wait()
    stale_copy.wait()
    for head in range(width // HD):
        cols = slice(head * HD, (head + 1) * HD)
        heads_query = query[:, cols]
        text_scores = lax.dot_general(heads_query, text[0, :, cols], NT, preferred_element_type=jnp.float32)
        image_scores = lax.dot_general(heads_query, stale[0, :, cols], NT, preferred_element_type=jnp.float32)
        image_scores += lax.dot_general(heads_query, residual[0, :, cols], NT, preferred_element_type=jnp.float32)
        text_scores *= HD**-0.5
        image_scores *= HD**-0.5
        peak = jnp.maximum(
            jnp.max(text_scores, axis=1, keepdims=True), jnp.max(image_scores, axis=1, keepdims=True)
        )
        text_weights = jnp.exp(text_scores - peak).astype(jnp.bfloat16)
        image_weights = jnp.exp(image_scores - peak).astype(jnp.bfloat16)
        total = jnp.sum(text_weights.astype(jnp.float32), axis=1, keepdims=True)
        total += jnp.sum(image_weights.astype(jnp.float32), axis=1, keepdims=True)
        mixed = jnp.dot(text_weights, text[1, :, cols], preferred_element_type=jnp.float32)
        mixed += jnp.dot(image_weights, stale[1, :, cols], preferred_element_type=jnp.float32)
        mixed += jnp.dot(image_weights, residual[1, :, cols], preferred_element_type=jnp.float32)
        out[:, cols] = (mixed / total).astype(jnp.bfloat16)


def attend(parts, query, text_kv, stale_kv):
    groups, rows, width = query.shape
    keys = stale_kv.shape[1]
    texts = text_kv.shape[1]
    bf16 = jnp.bfloat16
    return pl.pallas_call(
        attend_kernel,
        out_shape=jax.ShapeDtypeStruct((groups * rows, width), bf16),
        in_specs=[VMEM] * (SPREAD + 1) + [HBM] * 2,
        out_specs=VMEM,
        scratch_shapes=[
            pltpu.VMEM((groups * rows, width), bf16),
            pltpu.VMEM((2, keys, width), bf16),
            pltpu.VMEM((2, texts, width), bf16),
            pltpu.VMEM((2, keys, width), bf16),
            pltpu.SemaphoreType.DMA((2,)),
        ],
        compiler_params=pltpu.CompilerParams(vmem_limit_bytes=50 << 20),
        cost_estimate=pl.CostEstimate(
            flops=4 * groups * rows * width * (texts + 2 * keys),
            bytes_accessed=4 * width * (texts + 2 * keys),
            transcendentals=groups * rows * (texts + keys) * (width // HD),
        ),
    )(*parts, query, text_kv, stale_kv)


def project_kernel(parts, weights, out, weight):
    group, spot = place()
    width = parts[0].shape[1]
    rows = weight.shape[0] // SPREAD
    for twist in range(SPREAD):
        start = jnp.bitwise_xor(spot, twist) * rows
        for piece in weights[twist]:
            height = piece.shape[0]
            weight[pl.ds(pl.multiple_of(start, height), height), :] = piece[...]
            start += height
    total = None
    for twist, part in enumerate(parts):
        origin = jnp.bitwise_xor(group, twist)
        term = lax.dot_general(
            part[...], weight[:, pl.ds(aligned(origin, width), width)], NT, preferred_element_type=jnp.float32
        )
        total = term if total is None else total + term
    out[...] = total.astype(jnp.bfloat16).reshape(out.shape)


def project(parts, weights):
    groups = len(parts)
    tokens, width = parts[0].shape
    rows, depth = weights[0][0].shape
    flat, tree = jax.tree.flatten(weights)

    def kernel(*refs):
        project_kernel(refs[:groups], jax.tree.unflatten(tree, refs[groups:-2]), *refs[-2:])

    return pl.pallas_call(
        kernel,
        out_shape=jax.ShapeDtypeStruct((groups, tokens // groups, SPREAD * rows), jnp.bfloat16),
        in_specs=[VMEM] * (groups + len(flat)),
        out_specs=VMEM,
        scratch_shapes=[pltpu.VMEM((SPREAD * rows, depth), jnp.bfloat16)],
        compiler_params=pltpu.CompilerParams(vmem_limit_bytes=24 << 20),
        cost_estimate=pl.CostEstimate(
            flops=2 * tokens * SPREAD * rows * depth,
            bytes_accessed=2 * SPREAD * rows * depth,
            transcendentals=0,
        ),
    )(*parts, *flat)


def finish_kernel(terms, bias, gate, out):
    halves, blocks, _, columns = terms.shape
    for block in range(blocks):
        cols = slice(block * columns, (block + 1) * columns)
        total = terms[0, block].astype(jnp.float32)
        for half in range(1, halves):
            total = total + terms[half, block].astype(jnp.float32)
        out[:, cols] = (gate[:, cols] * (total + bias[:, cols])).astype(jnp.bfloat16)


def finish(terms, bias, gate):
    _, blocks, rows, columns = terms.shape
    width = blocks * columns
    return pl.pallas_call(
        finish_kernel,
        out_shape=jax.ShapeDtypeStruct((rows, width), jnp.bfloat16),
        in_specs=[VMEM] * 3,
        out_specs=VMEM,
        compiler_params=pltpu.CompilerParams(vmem_limit_bytes=16 << 20),
        cost_estimate=pl.CostEstimate(flops=3 * rows * width, bytes_accessed=4 * rows * width, transcendentals=0),
    )(terms, bias.reshape(1, width), gate.reshape(1, width))


def grouped_body(groups, halves, queries, stale_kv, codes, exponents, text_kv, out_weight, out_bias, out_gate):
    size = groups * SPREAD
    columns = [[group * SPREAD + spot for group in range(groups)] for spot in range(SPREAD)]

    def exchange(value):
        return lax.all_to_all(value, "patch", 0, 0, axis_index_groups=columns, tiled=True)

    def swap(value, twist):
        return lax.ppermute(value, "patch", [(p, p ^ twist) for p in range(size)])

    def after(value, *others):
        return lax.optimization_barrier((value, *others))[0]

    residual, query = pack(groups, queries, codes, exponents)
    weight = out_weight.T
    half = weight.shape[0] // 2
    early = swap(weight[:half], 2)
    own = exchange(residual)
    far = swap(own, 2)
    near = swap(own, 1)
    query = exchange(after(query, own))
    corner = swap(after(far, query), 1)
    late = swap(after(weight[half:], corner), 2)
    beside = swap(after(weight, near), 1)
    attended = attend([own, near, far, corner], after(query, beside), text_kv, stale_kv)
    across = swap(attended, 2 * SPREAD)
    next_to = swap(attended, SPREAD)
    last = swap(across, SPREAD)
    early, late = after(early, across), after(late, across)
    weights = [(weight,), (beside,), (early, late), (swap(early, 1), swap(late, 1))]
    attended_parts = [attended, next_to, across, last]
    terms = exchange(project(attended_parts, weights))
    terms = lax.all_to_all(terms, "head", 0, 0, tiled=True)
    return finish(terms.reshape(halves, groups // halves, *terms.shape[1:]), out_bias, out_gate)


def solution(mesh):
    patches, halves = mesh.shape["patch"], mesh.shape["head"]
    placed = (
        P("patch", "head"),
        P(None, None, "head"),
        P(None, "patch", "head"),
        P(None, "patch", "head"),
        P(None, None, "head"),
        P("head", "patch"),
        P("head"),
        P("head"),
    )

    def body(*args):
        heads = args[0].shape[1] // HD
        groups = patches // SPREAD
        if patches != 4 * SPREAD or heads % groups or groups % halves:
            return plain_body(*args)
        return grouped_body(groups, halves, *args)

    return jax.shard_map(body, mesh=mesh, in_specs=placed, out_specs=P("patch", "head"), check_vma=False)
```

time: 178 us -> 81.5 us (0.46)
  waiting for transfers between devices: 114 us -> 27.7 us
  blocking collectives: 0 us -> 28.1 us
  local copies, waits for them, and re-layouts: 22.9 us -> 2.53 us
  matrix products: 16.4 us -> 0 us
  starting transfers between devices: 0.08 us -> 13.9 us
  between operations: 13.2 us -> 0.11 us
  other arithmetic: 10.6 us -> 0 us
  Pallas kernels: 0 us -> 8.6 us
    all_gather x2 -> x0, waiting for transfers between devices: 99.6 us -> none  [the longest x1 51.4 us: body(): lax.all_gather(out_weight, 'patch', axis=1, tiled=True)]
    all_to_all x0 -> x2, blocking collectives: none -> 28.1 us  [exchange(): lax.all_to_all(value, 'patch', 0, 0, axis_index_groups=columns, tiled=True)]
    slice x4 -> x1, local copies, waits for them, and re-layouts: 20 us -> 1.09 us  [grouped_body(): late = swap(after(weight[half:], corner), 2)]
    dot_general x5 -> x0, matrix products: 16.4 us -> none  [the longest x1 7.35 us: body(): jnp.dot(attended, lax.all_gather(out_weight, 'patch', axis=1, tiled=True)...]
    ppermute x0 -> x11, waiting for transfers between devices: none -> 16.1 us  [swap(): return lax.ppermute(value, 'patch', [(p, p ^ twist) for p in range(size)])]
    reduce_scatter x1 -> x0, waiting for transfers between devices: 13.6 us -> none  [body(): lax.psum_scatter(partial_terms, 'head', scatter_dimension=1, tiled=True)]
    all_to_all x0 -> x2, waiting for transfers between devices: none -> 11.6 us  [the longest x1 6.35 us: exchange(): lax.all_to_all(value, 'patch', 0, 0, axis_index_groups=columns, tiled=True)]
    pallas_call x0 -> x4, Pallas kernels: none -> 8.6 us  [the longest x1 3.89 us: attend(): pl.pallas_call(attend_kernel, out_shape=jax.ShapeDtypeStruct((groups * ro...]
  transfers between devices with their start and end apart: 3 -> 13, of which waited for: 3 -> 7; matrix products, arithmetic and copies ran while one was open for 21% -> 1% of each run, Pallas kernels for 0% -> 5%
where the time goes in v2:
time: 81.5 us; the launch traced here: 81 us
  blocking collectives  28.1 us (34%)
  waiting for transfers between devices  27.7 us (34%)
  starting transfers between devices  13.9 us (17%)
  Pallas kernels  8.6 us (11%)
  local copies, waits for them, and re-layouts  2.53 us (3%)
    all_to_all x2, blocking collectives, exchange(): lax.all_to_all(value, 'patch', 0, 0, axis_index_groups=columns, tiled=True)  28.1 us
    ppermute x11, waiting for transfers between devices, swap(): return lax.ppermute(value, 'patch', [(p, p ^ twist) for p in range(size)])  16.1 us
    ppermute x11, starting transfers between devices, swap(): return lax.ppermute(value, 'patch', [(p, p ^ twist) for p in range(size)])  7.09 us
    all_to_all x1, waiting for transfers between devices, exchange(): lax.all_to_all(value, 'patch', 0, 0, axis_index_groups=columns, tiled=True)  6.35 us
    all_to_all x1, waiting for transfers between devices, grouped_body(): terms = lax.all_to_all(terms, 'head', 0, 0, tiled=True)  5.29 us
    pallas_call x1, Pallas kernels, attend(): pl.pallas_call(attend_kernel, out_shape=jax.ShapeDtypeStruct((groups * ro...  3.89 us
    all_to_all x1, starting transfers between devices, grouped_body(): terms = lax.all_to_all(terms, 'head', 0, 0, tiled=True)  3.45 us
    all_to_all x1, starting transfers between devices, exchange(): lax.all_to_all(value, 'patch', 0, 0, axis_index_groups=columns, tiled=True)  3.34 us
  transfers between devices with their start and end apart: 13, of which 7 were waited for; matrix products, arithmetic and copies ran while one was open for 1% of the time, Pallas kernels for 5%

profile of v2, /device:TPU:0, one launch (start us, length us, event | category | flops | bytes accessed | tf_op | source)
XLA Modules:
  0.0 81.0 jit_solution(8008440686367186784)
XLA Ops:
  0.0 1.4 %copy.9.exponents = s32[2,48,12]{2,1,0:T(8,128)} copy(s32[2,48,12]{1,0,2:T(2,128)} %param.11) | data formatting | bytes 9216 | tf_op args[3]
  1.4 2.9 %shard_map.82 = (bf16[4,2,48,384]{3,2,1,0:T(8,128)(2,1)}, bf16[4,48,384]{2,1,0:T(8,128)(2,1)}) custom-call(bf16[48,1536]{1,0:T(8,128)(2,1)} %queries_hbm.1, s32[2,48,1536]{2,1,0:T(8,128)} %codes_hbm.1, s32[2,48,12]{2,1,0:T(8,128)} %copy.9.exponents), custom_call_target="tpu_custom_call" | custom-call | flops 294912 | bytes 884736 | tf_op jit(solution)/shard_map/pallas_call | solution.py:89
  4.3 15.9 %all_to_all.20.refs_0_ = bf16[4,2,48,384]{3,2,1,0:T(8,128)(2,1)S(1)} all-to-all(bf16[4,2,48,384]{3,2,1,0:T(8,128)(2,1)} %get-tuple-element.14), channel_id=1, replica_groups={{0,8,16,24},{2,10,18,26},{4,12,20,28},{6,14,22,30},{1,9,17,25},{3,11,19..., dimensions={0} | all-to-all | bytes 589824 | tf_op jit(solution)/shard_map/all_to_all | solution.py:242
  20.2 0.0 collective-permute-start
  20.2 1.5 %collective-permute-start.1 = (bf16[4,2,48,384]{3,2,1,0:T(8,128)(2,1)S(1)}, bf16[4,2,48,384]{3,2,1,0:T(8,128)(2,1)S(1)}, u32[]{:S(2)}, u32[]{:S(2)}) collective-permute-start(bf16[4,2,48,384]{3,2,1,0:T(8,128)(2,1)S(1)} %all_to_all.20.refs_0_), channel_id=1, source_target_pairs={{0,4},{2,6},{4,0},{6,2},{8,12},{10,14},{12,8},{14,10},{16,20},{18,... | collective-permute-start | bytes 884744 | tf_op jit(solution)/shard_map/ppermute | solution.py:245
  21.7 3.3 %all-to-all-start.1 = ((bf16[4,48,384]{2,1,0:T(8,128)(2,1)}), bf16[4,48,384]{2,1,0:T(8,128)(2,1)S(1)}, u32[]{:S(2)}, u32[]{:S(2)}) async-start(bf16[4,48,384]{2,1,0:T(8,128)(2,1)} %get-tuple-element.16), calls=%async_computation.1 | async-start | bytes 294912 | tf_op jit(solution)/shard_map/all_to_all | solution.py:242
  25.1 0.0 collective-permute-done.refs_1_
  25.1 0.3 collective-permute-start.3
  25.4 6.4 %all-to-all-done.1.refs_4_ = bf16[4,48,384]{2,1,0:T(8,128)(2,1)S(1)} async-done(((bf16[4,48,384]{2,1,0:T(8,128)(2,1)}), bf16[4,48,384]{2,1,0:T(8,128)(2,1)S(1)}, u32[]{:S(2)}, u32[]{:S(2)}) %all-to-all-start.1) | async-done | bytes 147488 | tf_op jit(solution)/shard_map/all_to_all | solution.py:242
  31.7 0.0 collective-permute-done.1.refs_2_
  31.7 0.0 collective-permute-start.2
  31.7 1.1 %fusion = (bf16[96,1536]{1,0:T(8,128)(2,1)S(1)}, bf16[96,1536]{1,0:T(8,128)(2,1)S(1)}) fusion(bf16[192,1536]{1,0:T(8,128)(2,1)} %bitcast.3), kind=kLoop, calls=%fused_computation | loop fusion | bytes 1179648 | tf_op jit(solution)/shard_map/slice | solution.py:259
  32.8 0.0 copy-start
  32.8 0.5 collective-permute-done.2.refs_3_
  33.3 0.5 collective-permute-start.8
  33.8 1.5 %collective-permute-start.7 = (bf16[96,1536]{1,0:T(8,128)(2,1)S(1)}, bf16[96,1536]{1,0:T(8,128)(2,1)S(1)}, u32[]{:S(2)}, u32[]{:S(2)}) collective-permute-start(bf16[96,1536]{1,0:T(8,128)(2,1)S(1)} %get-tuple-element.24), channel_id=1, source_target_pairs={{0,4},{2,6},{4,0},{6,2},{8,12},{10,14},{12,8},{14,10},{16,20},{18,... | collective-permute-start | bytes 884744 | tf_op jit(solution)/shard_map/ppermute | solution.py:245
  35.3 0.0 collective-permute-done.3.refs_5_
  35.3 3.9 %shard_map.83.refs_0_ = bf16[192,384]{1,0:T(8,128)(2,1)S(1)} custom-call(bf16[4,2,48,384]{3,2,1,0:T(8,128)(2,1)S(1)} %all_to_all.20.refs_0_, bf16[4,2,48,384]{3,2,1,0:T(8,128)(2,1)S(1)} %collective-permute-done.refs_1_, bf16[4,2,48,384]{3,2,1,0:T(8,128)(2,1)S(1)} %collective-permute-done.1.refs_2_, ...), custom_call_target="tpu_custom_call" | custom-call | flops 603979776 | bytes 3145728 | tf_op jit(solution)/shard_map/pallas_call | solution.py:149
  39.2 0.7 collective-permute-start.5
  40.0 3.2 %collective-permute-done.8.refs_7_ = bf16[96,1536]{1,0:T(8,128)(2,1)S(1)} collective-permute-done((bf16[96,1536]{1,0:T(8,128)(2,1)S(1)}, bf16[96,1536]{1,0:T(8,128)(2,1)S(1)}, u32[]{:S(2)}, u32[]{:S(2)}) %collective-permute-start.8) | collective-permute-done | bytes 294944 | tf_op jit(solution)/shard_map/ppermute | solution.py:245
  43.2 5.5 %collective-permute-done.5.refs_2_ = bf16[192,384]{1,0:T(8,128)(2,1)S(1)} collective-permute-done((bf16[192,384]{1,0:T(8,128)(2,1)S(1)}, bf16[192,384]{1,0:T(8,128)(2,1)S(1)}, u32[]{:S(2)}, u32[]{:S(2)}) %collective-permute-start.5) | collective-permute-done | bytes 147488 | tf_op jit(solution)/shard_map/ppermute | solution.py:245
  48.7 0.5 collective-permute-start.9
  49.2 0.5 collective-permute-start.4
  49.7 1.5 %collective-permute-start.6 = (bf16[192,384]{1,0:T(8,128)(2,1)S(1)}, bf16[192,384]{1,0:T(8,128)(2,1)S(1)}, u32[]{:S(2)}, u32[]{:S(2)}) collective-permute-start(bf16[192,384]{1,0:T(8,128)(2,1)S(1)} %collective-permute-done.5.refs_2_), channel_id=1, source_target_pairs={{0,8},{2,10},{4,12},{6,14},{8,0},{10,2},{12,4},{14,6},{16,24},{18,... | collective-permute-start | bytes 442376 | tf_op jit(solution)/shard_map/ppermute | solution.py:245
  51.2 4.7 %collective-permute-done.4.refs_1_ = bf16[192,384]{1,0:T(8,128)(2,1)S(1)} collective-permute-done((bf16[192,384]{1,0:T(8,128)(2,1)S(1)}, bf16[192,384]{1,0:T(8,128)(2,1)S(1)}, u32[]{:S(2)}, u32[]{:S(2)}) %collective-permute-start.4) | collective-permute-done | bytes 147488 | tf_op jit(solution)/shard_map/ppermute | solution.py:245
  55.9 2.2 %collective-permute-done.6.refs_3_ = bf16[192,384]{1,0:T(8,128)(2,1)S(1)} collective-permute-done((bf16[192,384]{1,0:T(8,128)(2,1)S(1)}, bf16[192,384]{1,0:T(8,128)(2,1)S(1)}, u32[]{:S(2)}, u32[]{:S(2)}) %collective-permute-start.6) | collective-permute-done | bytes 147488 | tf_op jit(solution)/shard_map/ppermute | solution.py:245
  58.1 0.0 collective-permute-done.10.refs_9_
  58.1 1.1 %shard_map.84 = bf16[4,48,768]{2,1,0:T(8,128)(2,1)S(1)} custom-call(bf16[192,384]{1,0:T(8,128)(2,1)S(1)} %shard_map.83.refs_0_, bf16[192,384]{1,0:T(8,128)(2,1)S(1)} %collective-permute-done.4.refs_1_, bf16[192,384]{1,0:T(8,128)(2,1)S(1)} %collective-permute-done.5.refs_2_, bf16[192,384]{1,0:T(8,128)(2,1)S(1)} %collective-permute-done.6.refs_3_, ...), custom_call_target="tpu_custom_call" | custom-call | flops 452984832 | bytes 2359296 | tf_op jit(solution)/shard_map/pallas_call | solution.py:199
  59.2 12.2 %all_to_all.21 = bf16[4,48,768]{2,1,0:T(8,128)(2,1)} all-to-all(bf16[4,48,768]{2,1,0:T(8,128)(2,1)S(1)} %shard_map.84), channel_id=1, replica_groups={{0,8,16,24},{2,10,18,26},{4,12,20,28},{6,14,22,30},{1,9,17,25},{3,11,19..., dimensions={0} | all-to-all | bytes 589824 | tf_op jit(solution)/shard_map/all_to_all | solution.py:242
  71.5 3.4 %all-to-all-start.3 = ((bf16[4,48,768]{2,1,0:T(8,128)(2,1)}), bf16[4,48,768]{2,1,0:T(8,128)(2,1)S(1)}, u32[]{:S(2)}, u32[]{:S(2)}) async-start(bf16[4,48,768]{2,1,0:T(8,128)(2,1)} %all_to_all.21), calls=%async_computation.3 | async-start | bytes 589824 | tf_op jit(solution)/shard_map/all_to_all | solution.py:269
  75.0 5.3 %all-to-all-done.3 = bf16[4,48,768]{2,1,0:T(8,128)(2,1)S(1)} async-done(((bf16[4,48,768]{2,1,0:T(8,128)(2,1)}), bf16[4,48,768]{2,1,0:T(8,128)(2,1)S(1)}, u32[]{:S(2)}, u32[]{:S(2)}) %all-to-all-start.3) | async-done | bytes 294944 | tf_op jit(solution)/shard_map/all_to_all | solution.py:269
  80.3 0.7 shard_map.85
  (10 shorter events, 0.0 us)
Async XLA Ops:
  20.2 4.8 %collective-permute-start = (bf16[4,2,48,384]{3,2,1,0:T(8,128)(2,1)S(1)}, bf16[4,2,48,384]{3,2,1,0:T(8,128)(2,1)S(1)}, u32[]{:S(2)}, u32[]{:S(2)}) collective-permute-start(bf16[4,2,48,384]{3,2,1,0:T(8,128)(2,1)S(1)} %all_to_all.20.refs_0_), channel_id=1, source_target_pairs={{0,2},{2,0},{4,6},{6,4},{8,10},{10,8},{12,14},{14,12},{16,18},{18,... | collective-permute-start | bytes 884744 | tf_op jit(solution)/shard_map/ppermute | solution.py:245
  20.2 11.5 %collective-permute-start.1 = (bf16[4,2,48,384]{3,2,1,0:T(8,128)(2,1)S(1)}, bf16[4,2,48,384]{3,2,1,0:T(8,128)(2,1)S(1)}, u32[]{:S(2)}, u32[]{:S(2)}) collective-permute-start(bf16[4,2,48,384]{3,2,1,0:T(8,128)(2,1)S(1)} %all_to_all.20.refs_0_), channel_id=1, source_target_pairs={{0,4},{2,6},{4,0},{6,2},{8,12},{10,14},{12,8},{14,10},{16,20},{18,... | collective-permute-start | bytes 884744 | tf_op jit(solution)/shard_map/ppermute | solution.py:245
  21.7 10.0 %all-to-all-start.1 = ((bf16[4,48,384]{2,1,0:T(8,128)(2,1)}), bf16[4,48,384]{2,1,0:T(8,128)(2,1)S(1)}, u32[]{:S(2)}, u32[]{:S(2)}) async-start(bf16[4,48,384]{2,1,0:T(8,128)(2,1)} %get-tuple-element.16), calls=%async_computation.1 | async-start | bytes 294912 | tf_op jit(solution)/shard_map/all_to_all | solution.py:242
  25.1 10.3 %collective-permute-start.3 = (bf16[192,1536]{1,0:T(8,128)(2,1)}, bf16[192,1536]{1,0:T(8,128)(2,1)S(1)}, u32[]{:S(2)}, u32[]{:S(2)}) collective-permute-start(bf16[192,1536]{1,0:T(8,128)(2,1)} %bitcast.2), channel_id=1, source_target_pairs={{0,2},{2,0},{4,6},{6,4},{8,10},{10,8},{12,14},{14,12},{16,18},{18,... | collective-permute-start | bytes 1769480 | tf_op jit(solution)/shard_map/ppermute | solution.py:245
  31.7 1.6 %collective-permute-start.2 = (bf16[4,2,48,384]{3,2,1,0:T(8,128)(2,1)S(1)}, bf16[4,2,48,384]{3,2,1,0:T(8,128)(2,1)S(1)}, u32[]{:S(2)}, u32[]{:S(2)}) collective-permute-start(bf16[4,2,48,384]{3,2,1,0:T(8,128)(2,1)S(1)} %collective-permute-done.1.refs_2_), channel_id=1, source_target_pairs={{0,2},{2,0},{4,6},{6,4},{8,10},{10,8},{12,14},{14,12},{16,18},{18,... | collective-permute-start | bytes 884744 | tf_op jit(solution)/shard_map/ppermute | solution.py:245
  32.8 25.3 %copy-start = (bf16[1536,192]{0,1:T(8,128)(2,1)S(1)}, bf16[1536,192]{0,1:T(8,128)(2,1)}, u32[]{:S(2)}) copy-start(bf16[1536,192]{0,1:T(8,128)(2,1)} %param.13) | copy-start | bytes 1769476
  33.3 9.9 %collective-permute-start.8 = (bf16[96,1536]{1,0:T(8,128)(2,1)S(1)}, bf16[96,1536]{1,0:T(8,128)(2,1)S(1)}, u32[]{:S(2)}, u32[]{:S(2)}) collective-permute-start(bf16[96,1536]{1,0:T(8,128)(2,1)S(1)} %get-tuple-element.21), channel_id=1, source_target_pairs={{0,4},{2,6},{4,0},{6,2},{8,12},{10,14},{12,8},{14,10},{16,20},{18,... | collective-permute-start | bytes 884744 | tf_op jit(solution)/shard_map/ppermute | solution.py:245
  33.8 41.1 %copy-start.1 = (f32[1536]{0:T(1024)S(1)}, f32[1536]{0:T(1024)}, u32[]{:S(2)}) copy-start(f32[1536]{0:T(1024)} %param.14) | copy-start | bytes 18436
  33.8 41.1 %copy-start.2 = (f32[1536]{0:T(1024)S(1)}, f32[1536]{0:T(1024)}, u32[]{:S(2)}) copy-start(f32[1536]{0:T(1024)} %param.15) | copy-start | bytes 18436
  33.8 14.9 %collective-permute-start.7 = (bf16[96,1536]{1,0:T(8,128)(2,1)S(1)}, bf16[96,1536]{1,0:T(8,128)(2,1)S(1)}, u32[]{:S(2)}, u32[]{:S(2)}) collective-permute-start(bf16[96,1536]{1,0:T(8,128)(2,1)S(1)} %get-tuple-element.24), channel_id=1, source_target_pairs={{0,4},{2,6},{4,0},{6,2},{8,12},{10,14},{12,8},{14,10},{16,20},{18,... | collective-permute-start | bytes 884744 | tf_op jit(solution)/shard_map/ppermute | solution.py:245
  39.2 9.5 %collective-permute-start.5 = (bf16[192,384]{1,0:T(8,128)(2,1)S(1)}, bf16[192,384]{1,0:T(8,128)(2,1)S(1)}, u32[]{:S(2)}, u32[]{:S(2)}) collective-permute-start(bf16[192,384]{1,0:T(8,128)(2,1)S(1)} %shard_map.83.refs_0_), channel_id=1, source_target_pairs={{0,16},{2,18},{4,20},{6,22},{8,24},{10,26},{12,28},{14,30},{16,0},... | collective-permute-start | bytes 442376 | tf_op jit(solution)/shard_map/ppermute | solution.py:245
  48.7 9.4 %collective-permute-start.10 = (bf16[96,1536]{1,0:T(8,128)(2,1)S(1)}, bf16[96,1536]{1,0:T(8,128)(2,1)S(1)}, u32[]{:S(2)}, u32[]{:S(2)}) collective-permute-start(bf16[96,1536]{1,0:T(8,128)(2,1)S(1)} %collective-permute-done.8.refs_7_), channel_id=1, source_target_pairs={{0,2},{2,0},{4,6},{6,4},{8,10},{10,8},{12,14},{14,12},{16,18},{18,... | collective-permute-start | bytes 884744 | tf_op jit(solution)/shard_map/ppermute | solution.py:245
  48.7 9.4 %collective-permute-start.9 = (bf16[96,1536]{1,0:T(8,128)(2,1)S(1)}, bf16[96,1536]{1,0:T(8,128)(2,1)S(1)}, u32[]{:S(2)}, u32[]{:S(2)}) collective-permute-start(bf16[96,1536]{1,0:T(8,128)(2,1)S(1)} %collective-permute-done.7.refs_6_), channel_id=1, source_target_pairs={{0,2},{2,0},{4,6},{6,4},{8,10},{10,8},{12,14},{14,12},{16,18},{18,... | collective-permute-start | bytes 884744 | tf_op jit(solution)/shard_map/ppermute | solution.py:245
  49.2 6.7 %collective-permute-start.4 = (bf16[192,384]{1,0:T(8,128)(2,1)S(1)}, bf16[192,384]{1,0:T(8,128)(2,1)S(1)}, u32[]{:S(2)}, u32[]{:S(2)}) collective-permute-start(bf16[192,384]{1,0:T(8,128)(2,1)S(1)} %shard_map.83.refs_0_), channel_id=1, source_target_pairs={{0,8},{2,10},{4,12},{6,14},{8,0},{10,2},{12,4},{14,6},{16,24},{18,... | collective-permute-start | bytes 442376 | tf_op jit(solution)/shard_map/ppermute | solution.py:245
  49.7 8.4 %collective-permute-start.6 = (bf16[192,384]{1,0:T(8,128)(2,1)S(1)}, bf16[192,384]{1,0:T(8,128)(2,1)S(1)}, u32[]{:S(2)}, u32[]{:S(2)}) collective-permute-start(bf16[192,384]{1,0:T(8,128)(2,1)S(1)} %collective-permute-done.5.refs_2_), channel_id=1, source_target_pairs={{0,8},{2,10},{4,12},{6,14},{8,0},{10,2},{12,4},{14,6},{16,24},{18,... | collective-permute-start | bytes 442376 | tf_op jit(solution)/shard_map/ppermute | solution.py:245
  71.5 8.8 %all-to-all-start.3 = ((bf16[4,48,768]{2,1,0:T(8,128)(2,1)}), bf16[4,48,768]{2,1,0:T(8,128)(2,1)S(1)}, u32[]{:S(2)}, u32[]{:S(2)}) async-start(bf16[4,48,768]{2,1,0:T(8,128)(2,1)} %all_to_all.21), calls=%async_computation.3 | async-start | bytes 589824 | tf_op jit(solution)/shard_map/all_to_all | solution.py:269

commit v3 on v2

v3 whole, which is shorter than its diff:
```python
import functools

import jax
import jax.numpy as jnp
from jax import lax
from jax.experimental import pallas as pl
from jax.experimental.pallas import tpu as pltpu
from jax.sharding import PartitionSpec as P

HD = 128
SPREAD = 4
PACK_LIMIT = 56 << 20
PICK_LIMIT = 50 << 20
VMEM = pl.BlockSpec(memory_space=pltpu.VMEM)
HBM = pl.BlockSpec(memory_space=pltpu.HBM)
NT = (((1,), (1,)), ((), ()))


def plain_body(queries, stale_kv, codes, exponents, text_kv, out_weight, out_bias, out_gate):
    tok_rows = queries.shape[0]
    row_width = queries.shape[1]
    head_count = row_width // HD
    text_count = text_kv.shape[1]
    scale_factor = HD ** (-0.5)
    blocks = jnp.exp2(exponents.astype(jnp.float32))
    decoded = codes.astype(jnp.float32).reshape(2, tok_rows, head_count, HD) * blocks[..., None]
    decoded = decoded.astype(jnp.bfloat16).reshape(2, tok_rows, row_width)
    arrived = lax.all_gather(decoded, "patch", axis=1, tiled=True)
    all_rows = arrived.shape[1]
    query_heads = queries.reshape(tok_rows, head_count, HD)
    text_heads = text_kv.reshape(2, text_count, head_count, HD)
    stale_heads = stale_kv.reshape(2, all_rows, head_count, HD)
    arrived_heads = arrived.reshape(2, all_rows, head_count, HD)
    text_scores = jnp.einsum("thd,khd->htk", query_heads, text_heads[0], preferred_element_type=jnp.float32)
    rebuilt = stale_heads.astype(jnp.float32) + arrived_heads.astype(jnp.float32)
    image_scores = jnp.einsum(
        "thd,khd->htk", query_heads.astype(jnp.float32), rebuilt[0], precision=lax.Precision.HIGHEST
    )
    scores = jnp.concatenate([text_scores, image_scores], axis=2) * scale_factor
    row_peak = jnp.max(scores, axis=2, keepdims=True)
    weights = jnp.exp(scores - row_peak).astype(jnp.bfloat16)
    row_total = jnp.sum(weights.astype(jnp.float32), axis=2)
    text_part = jnp.einsum(
        "htk,khd->thd", weights[:, :, :text_count], text_heads[1], preferred_element_type=jnp.float32
    )
    image_part = jnp.einsum(
        "htk,khd->thd",
        weights[:, :, text_count:].astype(jnp.float32),
        rebuilt[1],
        precision=lax.Precision.HIGHEST,
    )
    attended = ((text_part + image_part) / row_total.T[:, :, None]).astype(jnp.bfloat16).reshape(tok_rows, row_width)
    partial_terms = jnp.dot(
        attended, lax.all_gather(out_weight, "patch", axis=1, tiled=True), preferred_element_type=jnp.float32
    )
    column_share = lax.psum_scatter(partial_terms, "head", scatter_dimension=1, tiled=True)
    return (out_gate * (column_share + out_bias)).astype(jnp.bfloat16)


def aligned(value, step):
    return pl.multiple_of(value * step, step)


def place():
    me = lax.axis_index("patch")
    return me // SPREAD, lax.rem(me, SPREAD)


def pack_kernel(queries_hbm, codes_hbm, exponents_hbm, *rest):
    outs, (codes, queries, exponents, held, sems) = rest[:-5], rest[-5:]
    groups, kinds, rows, width = held.shape
    group, _ = place()
    per = width // HD
    copies = [
        pltpu.make_async_copy(exponents_hbm, exponents, sems.at[0]),
        pltpu.make_async_copy(codes_hbm, codes, sems.at[1]),
        pltpu.make_async_copy(queries_hbm, queries, sems.at[2]),
    ]
    for copy in copies:
        copy.start()
    copies[0].wait()
    copies[1].wait()
    eye = lax.broadcasted_iota(jnp.int32, (rows, rows), 0) == lax.broadcasted_iota(jnp.int32, (rows, rows), 1)
    eye = eye.astype(jnp.float32).astype(jnp.bfloat16)
    for kind in range(kinds - 1):
        scales = jnp.left_shift(1, exponents[:, kind, :] + 16).astype(jnp.float32) * (2.0**-16)
        scales = lax.dot_general(eye, scales.astype(jnp.bfloat16), NT, preferred_element_type=jnp.float32)
        for head in range(groups * per):
            inside = slice((head % per) * HD, (head % per + 1) * HD)
            whole = slice(head * HD, (head + 1) * HD)
            decoded = codes[kind, :, whole].astype(jnp.float32) * scales[:, head : head + 1]
            held[head // per, kind, :, inside] = decoded.astype(jnp.bfloat16)
    copies[2].wait()
    for target in range(groups):
        held[target, kinds - 1] = queries[:, target * width : (target + 1) * width]
    for turn in range(groups):
        target = jnp.bitwise_xor(group, turn)
        outs[turn][...] = held[target, 0 : kinds - 1]
        outs[groups + turn][...] = held[target, kinds - 1]


def pack(groups, queries, codes, exponents):
    rows, width = queries.shape
    kinds = codes.shape[0]
    share = width // groups
    bf16 = jnp.bfloat16
    exponents = exponents.transpose(2, 0, 1)
    outs = pl.pallas_call(
        pack_kernel,
        out_shape=[jax.ShapeDtypeStruct((kinds, rows, share), bf16)] * groups
        + [jax.ShapeDtypeStruct((rows, share), bf16)] * groups,
        in_specs=[HBM] * 3,
        out_specs=[VMEM] * (2 * groups),
        scratch_shapes=[
            pltpu.VMEM(codes.shape, jnp.int32),
            pltpu.VMEM(queries.shape, bf16),
            pltpu.VMEM(exponents.shape, jnp.int32),
            pltpu.VMEM((groups, kinds + 1, rows, share), bf16),
            pltpu.SemaphoreType.DMA((3,)),
        ],
        compiler_params=pltpu.CompilerParams(vmem_limit_bytes=PACK_LIMIT),
        cost_estimate=pl.CostEstimate(flops=2 * codes.size, bytes_accessed=6 * codes.size, transcendentals=0),
    )(queries, codes, exponents)
    return outs[:groups], outs[groups:]


def pick_kernel(text_hbm, stale_hbm, text, stale, sems):
    group, _ = place()
    width = text.shape[2]
    columns = pl.ds(aligned(group, width), width)
    text_copy = pltpu.make_async_copy(text_hbm.at[:, :, columns], text, sems.at[0])
    stale_copy = pltpu.make_async_copy(stale_hbm.at[:, :, columns], stale, sems.at[1])
    text_copy.start()
    stale_copy.start()
    text_copy.wait()
    stale_copy.wait()


def pick(groups, text_kv, stale_kv):
    shapes = [(2, value.shape[1], value.shape[2] // groups) for value in (text_kv, stale_kv)]
    return pl.pallas_call(
        pick_kernel,
        out_shape=[jax.ShapeDtypeStruct(shape, jnp.bfloat16) for shape in shapes],
        in_specs=[HBM] * 2,
        out_specs=[VMEM] * 2,
        scratch_shapes=[pltpu.SemaphoreType.DMA((2,))],
        compiler_params=pltpu.CompilerParams(vmem_limit_bytes=PICK_LIMIT),
        cost_estimate=pl.CostEstimate(flops=0, bytes_accessed=8 << 20, transcendentals=0),
    )(text_kv, stale_kv)


def merge_kernel(*refs):
    for index, ref in enumerate(refs[:-1]):
        refs[-1][index] = ref[...]


def merge(parts):
    return pl.pallas_call(
        merge_kernel,
        out_shape=jax.ShapeDtypeStruct((len(parts), *parts[0].shape), parts[0].dtype),
        in_specs=[VMEM] * len(parts),
        out_specs=VMEM,
        cost_estimate=pl.CostEstimate(flops=0, bytes_accessed=4 * len(parts) * parts[0].size, transcendentals=0),
    )(*parts)


def attend_kernel(groups, *refs):
    owns, merged, asked, refs = refs[:SPREAD], refs[SPREAD : 2 * SPREAD], refs[2 * SPREAD : 2 * SPREAD + groups], refs[2 * SPREAD + groups :]
    text, stale, out, query, residual = refs
    group, spot = place()
    rows, width = asked[0].shape
    for turn in range(groups):
        origin = jnp.bitwise_xor(group, turn)
        query[pl.ds(aligned(origin, rows), rows), :] = asked[turn][...]
        for twist in range(SPREAD):
            token = origin * SPREAD + jnp.bitwise_xor(spot, twist)
            part = owns[twist][...] if turn == 0 else merged[twist][turn - 1]
            residual[:, pl.ds(aligned(token, rows), rows), :] = part
    for head in range(width // HD):
        cols = slice(head * HD, (head + 1) * HD)
        heads_query = query[:, cols]
        text_scores = lax.dot_general(heads_query, text[0, :, cols], NT, preferred_element_type=jnp.float32)
        image_scores = lax.dot_general(heads_query, stale[0, :, cols], NT, preferred_element_type=jnp.float32)
        image_scores += lax.dot_general(heads_query, residual[0, :, cols], NT, preferred_element_type=jnp.float32)
        text_scores *= HD**-0.5
        image_scores *= HD**-0.5
        peak = jnp.maximum(
            jnp.max(text_scores, axis=1, keepdims=True), jnp.max(image_scores, axis=1, keepdims=True)
        )
        text_weights = jnp.exp(text_scores - peak).astype(jnp.bfloat16)
        image_weights = jnp.exp(image_scores - peak).astype(jnp.bfloat16)
        total = jnp.sum(text_weights.astype(jnp.float32), axis=1, keepdims=True)
        total += jnp.sum(image_weights.astype(jnp.float32), axis=1, keepdims=True)
        mixed = jnp.dot(text_weights, text[1, :, cols], preferred_element_type=jnp.float32)
        mixed += jnp.dot(image_weights, stale[1, :, cols], preferred_element_type=jnp.float32)
        mixed += jnp.dot(image_weights, residual[1, :, cols], preferred_element_type=jnp.float32)
        out[:, cols] = (mixed / total).astype(jnp.bfloat16)


def attend(owns, merged, query_parts, text, stale):
    groups = len(query_parts)
    rows, width = query_parts[0].shape
    keys = stale.shape[1]
    texts = text.shape[1]
    bf16 = jnp.bfloat16
    return pl.pallas_call(
        functools.partial(attend_kernel, groups),
        out_shape=jax.ShapeDtypeStruct((groups * rows, width), bf16),
        in_specs=[VMEM] * (2 * SPREAD + groups + 2),
        out_specs=VMEM,
        scratch_shapes=[pltpu.VMEM((groups * rows, width), bf16), pltpu.VMEM((2, keys, width), bf16)],
        compiler_params=pltpu.CompilerParams(vmem_limit_bytes=24 << 20),
        cost_estimate=pl.CostEstimate(
            flops=4 * groups * rows * width * (texts + 2 * keys),
            bytes_accessed=4 * width * (texts + 2 * keys),
            transcendentals=groups * rows * (texts + keys) * (width // HD),
        ),
    )(*owns, *merged, *query_parts, text, stale)


def project_kernel(parts, weights, outs, weight, total):
    group, spot = place()
    width = parts[0].shape[1]
    span = weight.shape[0] // SPREAD
    rows = outs[0].shape[0]
    for twist in range(SPREAD):
        start = jnp.bitwise_xor(spot, twist) * span
        for piece in weights[twist]:
            height = piece.shape[0]
            weight[pl.ds(pl.multiple_of(start, height), height), :] = piece[...]
            start += height
    added = None
    for turn, part in enumerate(parts):
        origin = jnp.bitwise_xor(group, turn)
        term = lax.dot_general(
            part[...], weight[:, pl.ds(aligned(origin, width), width)], NT, preferred_element_type=jnp.float32
        )
        added = term if added is None else added + term
    total[...] = added.astype(jnp.bfloat16)
    for turn, out in enumerate(outs):
        out[...] = total[pl.ds(aligned(jnp.bitwise_xor(group, turn), rows), rows), :]


def project(parts, weights):
    groups = len(parts)
    tokens, width = parts[0].shape
    depth = weights[0][0].shape[1]
    columns = SPREAD * sum(piece.shape[0] for piece in weights[0])
    flat, tree = jax.tree.flatten(weights)

    def kernel(*refs):
        ins, outs, scratch = refs[: groups + len(flat)], refs[groups + len(flat) : -2], refs[-2:]
        project_kernel(ins[:groups], jax.tree.unflatten(tree, ins[groups:]), outs, *scratch)

    return pl.pallas_call(
        kernel,
        out_shape=[jax.ShapeDtypeStruct((tokens // groups, columns), jnp.bfloat16)] * groups,
        in_specs=[VMEM] * (groups + len(flat)),
        out_specs=[VMEM] * groups,
        scratch_shapes=[pltpu.VMEM((columns, depth), jnp.bfloat16), pltpu.VMEM((tokens, columns), jnp.bfloat16)],
        compiler_params=pltpu.CompilerParams(vmem_limit_bytes=24 << 20),
        cost_estimate=pl.CostEstimate(
            flops=2 * tokens * columns * depth, bytes_accessed=2 * columns * depth, transcendentals=0
        ),
    )(*parts, *flat)


def divide_kernel(*refs):
    parts, (keep, send, held) = refs[:-3], refs[-3:]
    group, _ = place()
    half = lax.axis_index("head")
    blocks = keep.shape[0]
    for turn, part in enumerate(parts):
        held[jnp.bitwise_xor(group, turn)] = part[...]
    for block in range(blocks):
        keep[block] = held[half * blocks + block]
        send[block] = held[(1 - half) * blocks + block]


def divide(parts):
    groups = len(parts)
    shape = jax.ShapeDtypeStruct((groups // 2, *parts[0].shape), jnp.bfloat16)
    return pl.pallas_call(
        divide_kernel,
        out_shape=[shape] * 2,
        in_specs=[VMEM] * groups,
        out_specs=[VMEM] * 2,
        scratch_shapes=[pltpu.VMEM((groups, *parts[0].shape), jnp.bfloat16)],
        cost_estimate=pl.CostEstimate(flops=0, bytes_accessed=4 * groups * parts[0].size, transcendentals=0),
    )(*parts)


def finish_kernel(kept, arrived, bias, gate, out):
    blocks, _, columns = kept.shape
    for block in range(blocks):
        cols = slice(block * columns, (block + 1) * columns)
        total = kept[block].astype(jnp.float32) + arrived[block].astype(jnp.float32)
        out[:, cols] = (gate[:, cols] * (total + bias[:, cols])).astype(jnp.bfloat16)


def finish(kept, arrived, bias, gate):
    blocks, rows, columns = kept.shape
    width = blocks * columns
    return pl.pallas_call(
        finish_kernel,
        out_shape=jax.ShapeDtypeStruct((rows, width), jnp.bfloat16),
        in_specs=[VMEM] * 4,
        out_specs=VMEM,
        cost_estimate=pl.CostEstimate(flops=3 * rows * width, bytes_accessed=4 * rows * width, transcendentals=0),
    )(kept, arrived, bias.reshape(1, width), gate.reshape(1, width))


def after(value, *others):
    return lax.optimization_barrier((value, *others))[0]


def grouped_body(queries, stale_kv, codes, exponents, text_kv, out_weight, out_bias, out_gate):
    groups = lax.axis_size("patch") // SPREAD
    size = groups * SPREAD

    def swap(value, twist):
        return lax.ppermute(value, "patch", [(p, p ^ twist) for p in range(size)])

    def along(values):
        return [swap(values[turn], turn * SPREAD) for turn in range(1, groups)]

    residuals, queries = pack(groups, queries, codes, exponents)
    weight = out_weight.T
    half = weight.shape[0] // 2
    text, stale = pick(groups, text_kv, stale_kv)

    own = residuals[0]
    arrived = along(residuals)
    own_far, own_near = swap(own, 2), swap(own, 1)
    early = swap(weight[:half], 2)

    merged = merge(arrived)
    merged = after(merged, own_far, own_near, text, stale)
    queries = lax.optimization_barrier((*queries, merged))[:groups]
    merged_far, merged_near = swap(merged, 2), swap(merged, 1)
    own_corner = swap(after(own_far, merged), 1)
    asked = [queries[0], *along(queries)]

    merged_corner = swap(after(merged_far, merged_near, own_corner, *asked), 1)
    owns = [own, own_near, own_far, own_corner]
    attended = attend(owns, [merged, merged_near, merged_far, merged_corner], asked, text, stale)

    weight, late, early = lax.optimization_barrier((weight, weight[half:], early, merged_corner))[:3]
    across, beside = swap(attended, 2 * SPREAD), swap(attended, SPREAD)
    late = swap(late, 2)
    early_near = swap(early, 1)
    weight_near = swap(weight, 1)

    across, late = lax.optimization_barrier((across, late, beside, weight_near, early_near))[:2]
    last = swap(across, SPREAD)
    late_near = swap(late, 1)
    weights = [(weight,), (weight_near,), (early, late), (early_near, late_near)]
    terms = project([attended, beside, across, last], weights)

    kept, sent = divide([terms[0], *along(terms)])
    received = lax.ppermute(sent, "head", [(0, 1), (1, 0)])
    return finish(kept, received, out_bias, out_gate)


def solution(mesh):
    patches, halves = mesh.shape["patch"], mesh.shape["head"]
    placed = (
        P("patch", "head"),
        P(None, None, "head"),
        P(None, "patch", "head"),
        P(None, "patch", "head"),
        P(None, None, "head"),
        P("head", "patch"),
        P("head"),
        P("head"),
    )

    def body(*args):
        heads = args[0].shape[1] // HD
        groups = patches // SPREAD
        if groups != 4 or patches % SPREAD or heads % groups or halves != 2:
            return plain_body(*args)
        return grouped_body(*args)

    return jax.shard_map(body, mesh=mesh, in_specs=placed, out_specs=P("patch", "head"), check_vma=False)
```

time: 81.5 us -> 75 us (0.920)
  blocking collectives: 28.1 us -> 0 us
  starting transfers between devices: 13.9 us -> 26 us
  Pallas kernels: 8.6 us -> 12.4 us
  waiting for transfers between devices: 27.7 us -> 31.3 us
  local copies, waits for them, and re-layouts: 2.53 us -> 4.74 us
    all_to_all x2 -> x0, blocking collectives: 28.1 us -> none  [exchange(): lax.all_to_all(value, 'patch', 0, 0, axis_index_groups=columns, tiled=True)]
    ppermute x11 -> x23, starting transfers between devices: 7.09 us -> 24.5 us  [swap(): return lax.ppermute(value, 'patch', [(p, p ^ twist) for p in range(size)])]
    ppermute x11 -> x23, waiting for transfers between devices: 16.1 us -> 28.7 us  [swap(): return lax.ppermute(value, 'patch', [(p, p ^ twist) for p in range(size)])]
    all_to_all x2 -> x0, waiting for transfers between devices: 11.6 us -> none  [the longest x1 6.35 us: exchange(): lax.all_to_all(value, 'patch', 0, 0, axis_index_groups=columns, tiled=True)]
    all_to_all x2 -> x0, starting transfers between devices: 6.78 us -> none  [the longest x1 3.45 us: grouped_body(): terms = lax.all_to_all(terms, 'head', 0, 0, tiled=True)]
    pallas_call x3 -> x6, Pallas kernels: 7.88 us -> 10.7 us  [the longest x1 2.33 us: attend(): pl.pallas_call(functools.partial(attend_kernel, groups), out_shape=jax.Sh...]
    ppermute x0 -> x1, waiting for transfers between devices: none -> 2.63 us  [grouped_body(): received = lax.ppermute(sent, 'head', [(0, 1), (1, 0)])]
    unnamed x7 -> x34, local copies, waits for them, and re-layouts: 1.42 us -> 3.51 us
  transfers between devices with their start and end apart: 13 -> 24, of which waited for: 7 -> 14; matrix products, arithmetic and copies ran while one was open for 1% -> 2% of each run, Pallas kernels for 5% -> 7%
where the time goes in v3:
time: 75 us; the launch traced here: 74.7 us
  waiting for transfers between devices  31.3 us (42%)
  starting transfers between devices  26 us (35%)
  Pallas kernels  12.4 us (17%)
  local copies, waits for them, and re-layouts  4.74 us (6%)
    ppermute x23, waiting for transfers between devices, swap(): return lax.ppermute(value, 'patch', [(p, p ^ twist) for p in range(size)])  28.7 us
    ppermute x23, starting transfers between devices, swap(): return lax.ppermute(value, 'patch', [(p, p ^ twist) for p in range(size)])  24.5 us
    unnamed x34, local copies, waits for them, and re-layouts  3.51 us
    ppermute x1, waiting for transfers between devices, grouped_body(): received = lax.ppermute(sent, 'head', [(0, 1), (1, 0)])  2.63 us
    pallas_call x1, Pallas kernels, attend(): pl.pallas_call(functools.partial(attend_kernel, groups), out_shape=jax.Sh...  2.33 us
    pallas_call x1, Pallas kernels, pack(): pl.pallas_call(pack_kernel, out_shape=[jax.ShapeDtypeStruct((kinds, rows,...  2.3 us
    pallas_call x1, Pallas kernels, divide(): pl.pallas_call(divide_kernel, out_shape=[shape] * 2, in_specs=[VMEM] * gr...  1.75 us
    pallas_call x1, Pallas kernels, finish(): pl.pallas_call(finish_kernel, out_shape=jax.ShapeDtypeStruct((rows, width...  1.7 us
  transfers between devices with their start and end apart: 24, of which 14 were waited for; matrix products, arithmetic and copies ran while one was open for 2% of the time, Pallas kernels for 7%

profile of v3, /device:TPU:0, one launch (start us, length us, event | category | flops | bytes accessed | tf_op | source)
XLA Modules:
  0.0 74.7 jit_solution(470083966665049754)
XLA Ops:
  0.0 2.3 %shard_map.82 = (bf16[2,48,384]{2,1,0:T(8,128)(2,1)}, bf16[2,48,384]{2,1,0:T(8,128)(2,1)}, bf16[2,48,384]{2,1,0:T(8,128)(2,1)}, bf16[2,48,384]{2,1,0:T(8,128)(2,...) custom-call(bf16[48,1536]{1,0:T(8,128)(2,1)} %queries_hbm.1, ...), custom_call_target="tpu_custom_call" | custom-call | flops 294912 | bytes 884736 | tf_op jit(solution)/shard_map/pallas_call | solution.py:108
  2.3 3.1 %collective-permute-start.2 = (bf16[2,48,384]{2,1,0:T(8,128)(2,1)}, bf16[2,48,384]{2,1,0:T(8,128)(2,1)S(1)}, u32[]{:S(2)}, u32[]{:S(2)}) collective-permute-start(bf16[2,48,384]{2,1,0:T(8,128)(2,1)} %get-tuple-element.34), channel_id=1, source_target_pairs={{0,8},{2,10},{4,12},{6,14},{8,0},{10,2},{12,4},{14,6},{16,24},{18,... | collective-permute-start | bytes 221192 | tf_op jit(solution)/shard_map/ppermute | solution.py:322
  5.4 2.6 %collective-permute-start.3 = (bf16[2,48,384]{2,1,0:T(8,128)(2,1)}, bf16[2,48,384]{2,1,0:T(8,128)(2,1)S(1)}, u32[]{:S(2)}, u32[]{:S(2)}) collective-permute-start(bf16[2,48,384]{2,1,0:T(8,128)(2,1)} %get-tuple-element.35), channel_id=1, source_target_pairs={{0,16},{2,18},{4,20},{6,22},{8,24},{10,26},{12,28},{14,30},{16,0},... | collective-permute-start | bytes 221192 | tf_op jit(solution)/shard_map/ppermute | solution.py:322
  8.1 1.8 %collective-permute-start.1 = (bf16[2,48,384]{2,1,0:T(8,128)(2,1)}, bf16[2,48,384]{2,1,0:T(8,128)(2,1)S(1)}, u32[]{:S(2)}, u32[]{:S(2)}) collective-permute-start(bf16[2,48,384]{2,1,0:T(8,128)(2,1)} %get-tuple-element.33.refs_0_), channel_id=1, source_target_pairs={{0,4},{2,6},{4,0},{6,2},{8,12},{10,14},{12,8},{14,10},{16,20},{18,... | collective-permute-start | bytes 221192 | tf_op jit(solution)/shard_map/ppermute | solution.py:322
  9.9 1.5 %shard_map.84 = (bf16[2,512,384]{2,1,0:T(8,128)(2,1)S(1)}, bf16[2,768,384]{2,1,0:T(8,128)(2,1)S(1)}) custom-call(bf16[2,512,1536]{2,1,0:T(8,128)(2,1)} %text_hbm.1, bf16[2,768,1536]{2,1,0:T(8,128)(2,1)} %stale_hbm.1), custom_call_target="tpu_custom_call" | custom-call | bytes 8388608 | tf_op jit(solution)/shard_map/pallas_call | solution.py:141
  11.4 2.0 %collective-permute-done.3.refs_1_ = bf16[2,48,384]{2,1,0:T(8,128)(2,1)S(1)} collective-permute-done((bf16[2,48,384]{2,1,0:T(8,128)(2,1)}, bf16[2,48,384]{2,1,0:T(8,128)(2,1)S(1)}, u32[]{:S(2)}, u32[]{:S(2)}) %collective-permute-start.3) | collective-permute-done | bytes 73760 | tf_op jit(solution)/shard_map/ppermute | solution.py:322
  13.4 1.1 %collective-permute-done.4.refs_2_ = bf16[2,48,384]{2,1,0:T(8,128)(2,1)S(1)} collective-permute-done((bf16[2,48,384]{2,1,0:T(8,128)(2,1)}, bf16[2,48,384]{2,1,0:T(8,128)(2,1)S(1)}, u32[]{:S(2)}, u32[]{:S(2)}) %collective-permute-start.4) | collective-permute-done | bytes 73760 | tf_op jit(solution)/shard_map/ppermute | solution.py:322
  15.1 1.7 %shard_map.83.refs_4_ = bf16[3,2,48,384]{3,2,1,0:T(8,128)(2,1)} custom-call(bf16[2,48,384]{2,1,0:T(8,128)(2,1)} %copy-done.6, bf16[2,48,384]{2,1,0:T(8,128)(2,1)} %copy-done.7, bf16[2,48,384]{2,1,0:T(8,128)(2,1)} %copy-done.8), custom_call_target="tpu_custom_call" | custom-call | bytes 442368 | tf_op jit(solution)/shard_map/pallas_call | solution.py:158
  16.8 1.6 %collective-permute-start.7 = (bf16[3,2,48,384]{3,2,1,0:T(8,128)(2,1)}, bf16[3,2,48,384]{3,2,1,0:T(8,128)(2,1)S(1)}, u32[]{:S(2)}, u32[]{:S(2)}) collective-permute-start(bf16[3,2,48,384]{3,2,1,0:T(8,128)(2,1)} %shard_map.83.refs_4_), channel_id=1, source_target_pairs={{0,4},{2,6},{4,0},{6,2},{8,12},{10,14},{12,8},{14,10},{16,20},{18,... | collective-permute-start | bytes 663560 | tf_op jit(solution)/shard_map/ppermute | solution.py:322
  18.5 1.1 %collective-permute-start.8 = (bf16[48,384]{1,0:T(8,128)(2,1)S(1)}, bf16[48,384]{1,0:T(8,128)(2,1)S(1)}, u32[]{:S(2)}, u32[]{:S(2)}) collective-permute-start(bf16[48,384]{1,0:T(8,128)(2,1)S(1)} %copy-done.16), channel_id=1, source_target_pairs={{0,8},{2,10},{4,12},{6,14},{8,0},{10,2},{12,4},{14,6},{16,24},{18,... | collective-permute-start | bytes 110600 | tf_op jit(solution)/shard_map/ppermute | solution.py:322
  19.6 2.3 %collective-permute-start.9 = (bf16[48,384]{1,0:T(8,128)(2,1)S(1)}, bf16[48,384]{1,0:T(8,128)(2,1)S(1)}, u32[]{:S(2)}, u32[]{:S(2)}) collective-permute-start(bf16[48,384]{1,0:T(8,128)(2,1)S(1)} %copy-done.15), channel_id=1, source_target_pairs={{0,16},{2,18},{4,20},{6,22},{8,24},{10,26},{12,28},{14,30},{16,0},... | collective-permute-start | bytes 110600 | tf_op jit(solution)/shard_map/ppermute | solution.py:322
  23.0 1.9 %collective-permute-done.9.refs_10_ = bf16[48,384]{1,0:T(8,128)(2,1)S(1)} collective-permute-done((bf16[48,384]{1,0:T(8,128)(2,1)S(1)}, bf16[48,384]{1,0:T(8,128)(2,1)S(1)}, u32[]{:S(2)}, u32[]{:S(2)}) %collective-permute-start.9) | collective-permute-done | bytes 36896 | tf_op jit(solution)/shard_map/ppermute | solution.py:322
  24.9 2.2 %collective-permute-start.10 = (bf16[48,384]{1,0:T(8,128)(2,1)S(1)}, bf16[48,384]{1,0:T(8,128)(2,1)S(1)}, u32[]{:S(2)}, u32[]{:S(2)}) collective-permute-start(bf16[48,384]{1,0:T(8,128)(2,1)S(1)} %copy-done.14), channel_id=1, source_target_pairs={{0,24},{2,26},{4,28},{6,30},{8,16},{10,18},{12,20},{14,22},{16,8},... | collective-permute-start | bytes 110600 | tf_op jit(solution)/shard_map/ppermute | solution.py:322
  27.1 3.5 %collective-permute-done.10.refs_11_ = bf16[48,384]{1,0:T(8,128)(2,1)S(1)} collective-permute-done((bf16[48,384]{1,0:T(8,128)(2,1)S(1)}, bf16[48,384]{1,0:T(8,128)(2,1)S(1)}, u32[]{:S(2)}, u32[]{:S(2)}) %collective-permute-start.10) | collective-permute-done | bytes 36896 | tf_op jit(solution)/shard_map/ppermute | solution.py:322
  31.1 1.1 %collective-permute-done.11.refs_7_ = bf16[3,2,48,384]{3,2,1,0:T(8,128)(2,1)S(1)} collective-permute-done((bf16[3,2,48,384]{3,2,1,0:T(8,128)(2,1)S(1)}, bf16[3,2,48,384]{3,2,1,0:T(8,128)(2,1)S(1)}, u32[]{:S(2)}, u32[]{:S(2)}) %collective-permute-start.11) | collective-permute-done | bytes 221216 | tf_op jit(solution)/shard_map/ppermute | solution.py:322
  33.0 0.9 %copy-done.1 = bf16[3,2,48,384]{3,2,1,0:T(8,128)(2,1)S(1)} copy-done((bf16[3,2,48,384]{3,2,1,0:T(8,128)(2,1)S(1)}, bf16[3,2,48,384]{3,2,1,0:T(8,128)(2,1)}, u32[]{:S(2)}) %copy-start.1) | copy-done | bytes 221208
  33.9 2.3 %shard_map.85.refs_0_ = bf16[192,384]{1,0:T(8,128)(2,1)S(1)} custom-call(bf16[2,48,384]{2,1,0:T(8,128)(2,1)S(1)} %copy-done.3, bf16[2,48,384]{2,1,0:T(8,128)(2,1)S(1)} %collective-permute-done.refs_1_, bf16[2,48,384]{2,1,0:T(8,128)(2,1)S(1)} %collective-permute-done.1.refs_2_, bf16[2,48,384]{2,1,0:T(8,128)(2,1)S(1)} %collective-permute-done.5.refs_3_, ...), custom_call_target="tpu_custom_call" | custom-call | flops 603979776 | bytes 3145728 | tf_op jit(solution)/shard_map/pallas_call | solution.py:206
  36.3 1.0 %collective-permute-start.12 = (bf16[192,384]{1,0:T(8,128)(2,1)S(1)}, bf16[192,384]{1,0:T(8,128)(2,1)S(1)}, u32[]{:S(2)}, u32[]{:S(2)}) collective-permute-start(bf16[192,384]{1,0:T(8,128)(2,1)S(1)} %shard_map.85.refs_0_), channel_id=1, source_target_pairs={{0,8},{2,10},{4,12},{6,14},{8,0},{10,2},{12,4},{14,6},{16,24},{18,... | collective-permute-start | bytes 442376 | tf_op jit(solution)/shard_map/ppermute | solution.py:322
  37.3 2.3 %collective-permute-start.13 = (bf16[192,384]{1,0:T(8,128)(2,1)S(1)}, bf16[192,384]{1,0:T(8,128)(2,1)S(1)}, u32[]{:S(2)}, u32[]{:S(2)}) collective-permute-start(bf16[192,384]{1,0:T(8,128)(2,1)S(1)} %shard_map.85.refs_0_), channel_id=1, source_target_pairs={{0,16},{2,18},{4,20},{6,22},{8,24},{10,26},{12,28},{14,30},{16,0},... | collective-permute-start | bytes 442376 | tf_op jit(solution)/shard_map/ppermute | solution.py:322
  39.6 6.0 %collective-permute-done.12.refs_1_ = bf16[192,384]{1,0:T(8,128)(2,1)S(1)} collective-permute-done((bf16[192,384]{1,0:T(8,128)(2,1)S(1)}, bf16[192,384]{1,0:T(8,128)(2,1)S(1)}, u32[]{:S(2)}, u32[]{:S(2)}) %collective-permute-start.12) | collective-permute-done | bytes 147488 | tf_op jit(solution)/shard_map/ppermute | solution.py:322
  45.6 1.6 %collective-permute-done.13.refs_2_ = bf16[192,384]{1,0:T(8,128)(2,1)S(1)} collective-permute-done((bf16[192,384]{1,0:T(8,128)(2,1)S(1)}, bf16[192,384]{1,0:T(8,128)(2,1)S(1)}, u32[]{:S(2)}, u32[]{:S(2)}) %collective-permute-start.13) | collective-permute-done | bytes 147488 | tf_op jit(solution)/shard_map/ppermute | solution.py:322
  47.8 5.7 %collective-permute-done.18.refs_3_ = bf16[192,384]{1,0:T(8,128)(2,1)S(1)} collective-permute-done((bf16[192,384]{1,0:T(8,128)(2,1)S(1)}, bf16[192,384]{1,0:T(8,128)(2,1)S(1)}, u32[]{:S(2)}, u32[]{:S(2)}) %collective-permute-start.18) | collective-permute-done | bytes 147488 | tf_op jit(solution)/shard_map/ppermute | solution.py:322
  53.5 1.1 %shard_map.86 = (bf16[48,768]{1,0:T(8,128)(2,1)S(1)}, bf16[48,768]{1,0:T(8,128)(2,1)S(1)}, bf16[48,768]{1,0:T(8,128)(2,1)S(1)}, bf16[48,768]{1,0:T(8,128)(2,1)S(1)}) custom-call(bf16[192,384]{1,0:T(8,128)(2,1)S(1)} %shard_map.85.refs_0_, bf16[192,384]{1,0:T(8,128)(2,1)S(1)} %collective-permute-done.12.refs_1_, ...), custom_call_target="tpu_custom_call" | custom-call | flops 452984832 | bytes 2359296 | tf_op jit(solution)/shard_map/pallas_call | solution.py:255
  55.7 2.6 %collective-permute-start.21 = (bf16[48,768]{1,0:T(8,128)(2,1)S(1)}, bf16[48,768]{1,0:T(8,128)(2,1)S(1)}, u32[]{:S(2)}, u32[]{:S(2)}) collective-permute-start(bf16[48,768]{1,0:T(8,128)(2,1)S(1)} %get-tuple-element.57), channel_id=1, source_target_pairs={{0,16},{2,18},{4,20},{6,22},{8,24},{10,26},{12,28},{14,30},{16,0},... | collective-permute-start | bytes 221192 | tf_op jit(solution)/shard_map/ppermute | solution.py:322
  58.3 1.3 %collective-permute-start.22 = (bf16[48,768]{1,0:T(8,128)(2,1)S(1)}, bf16[48,768]{1,0:T(8,128)(2,1)S(1)}, u32[]{:S(2)}, u32[]{:S(2)}) collective-permute-start(bf16[48,768]{1,0:T(8,128)(2,1)S(1)} %get-tuple-element.58), channel_id=1, source_target_pairs={{0,24},{2,26},{4,28},{6,30},{8,16},{10,18},{12,20},{14,22},{16,8},... | collective-permute-start | bytes 221192 | tf_op jit(solution)/shard_map/ppermute | solution.py:322
  60.2 3.5 %collective-permute-done.21.refs_2_ = bf16[48,768]{1,0:T(8,128)(2,1)S(1)} collective-permute-done((bf16[48,768]{1,0:T(8,128)(2,1)S(1)}, bf16[48,768]{1,0:T(8,128)(2,1)S(1)}, u32[]{:S(2)}, u32[]{:S(2)}) %collective-permute-start.21) | collective-permute-done | bytes 73760 | tf_op jit(solution)/shard_map/ppermute | solution.py:322
  63.7 0.9 %collective-permute-done.22.refs_3_ = bf16[48,768]{1,0:T(8,128)(2,1)S(1)} collective-permute-done((bf16[48,768]{1,0:T(8,128)(2,1)S(1)}, bf16[48,768]{1,0:T(8,128)(2,1)S(1)}, u32[]{:S(2)}, u32[]{:S(2)}) %collective-permute-start.22) | collective-permute-done | bytes 73760 | tf_op jit(solution)/shard_map/ppermute | solution.py:322
  65.2 1.8 %shard_map.87 = (bf16[2,48,768]{2,1,0:T(8,128)(2,1)}, bf16[2,48,768]{2,1,0:T(8,128)(2,1)}) custom-call(bf16[48,768]{1,0:T(8,128)(2,1)} %copy-done.2, bf16[48,768]{1,0:T(8,128)(2,1)} %copy-done.9, bf16[48,768]{1,0:T(8,128)(2,1)} %copy-done.10, bf16[48,768]{1,0:T(8,128)(2,1)} %copy-done.11), custom_call_target="tpu_custom_call" | custom-call | bytes 589824 | tf_op jit(solution)/shard_map/pallas_call | solution.py:283
  66.9 1.5 %collective-permute-start.23 = (bf16[2,48,768]{2,1,0:T(8,128)(2,1)}, bf16[2,48,768]{2,1,0:T(8,128)(2,1)S(1)}, u32[]{:S(2)}, u32[]{:S(2)}) collective-permute-start(bf16[2,48,768]{2,1,0:T(8,128)(2,1)} %get-tuple-element.60), channel_id=1, source_target_pairs={{0,1},{1,0},{2,3},{3,2},{4,5},{5,4},{6,7},{7,6},{8,9},{9,8},{10,11... | collective-permute-start | bytes 442376 | tf_op jit(solution)/shard_map/ppermute | solution.py:361
  69.7 2.6 %collective-permute-done.23.arrived = bf16[2,48,768]{2,1,0:T(8,128)(2,1)S(1)} collective-permute-done((bf16[2,48,768]{2,1,0:T(8,128)(2,1)}, bf16[2,48,768]{2,1,0:T(8,128)(2,1)S(1)}, u32[]{:S(2)}, u32[]{:S(2)}) %collective-permute-start.23) | collective-permute-done | bytes 147488 | tf_op jit(solution)/shard_map/ppermute | solution.py:361
  72.3 0.7 copy-done.5
  73.0 1.7 %shard_map.88 = bf16[48,1536]{1,0:T(8,128)(2,1)} custom-call(bf16[2,48,768]{2,1,0:T(8,128)(2,1)} %get-tuple-element.59.kept, bf16[2,48,768]{2,1,0:T(8,128)(2,1)} %copy-done.5, f32[1,1536]{1,0:T(1,128)} %reshape.6.bias, f32[1,1536]{1,0:T(1,128)} %reshape.7.gate), custom_call_target="tpu_custom_call" | custom-call | flops 221184 | bytes 294912 | tf_op jit(solution)/shard_map/pallas_call | solution.py:304
  (60 shorter events, 7.2 us)
Async XLA Ops:
  2.3 9.1 %collective-permute-start.2 = (bf16[2,48,384]{2,1,0:T(8,128)(2,1)}, bf16[2,48,384]{2,1,0:T(8,128)(2,1)S(1)}, u32[]{:S(2)}, u32[]{:S(2)}) collective-permute-start(bf16[2,48,384]{2,1,0:T(8,128)(2,1)} %get-tuple-element.34), channel_id=1, source_target_pairs={{0,8},{2,10},{4,12},{6,14},{8,0},{10,2},{12,4},{14,6},{16,24},{18,... | collective-permute-start | bytes 221192 | tf_op jit(solution)/shard_map/ppermute | solution.py:322
  5.4 8.0 %collective-permute-start.3 = (bf16[2,48,384]{2,1,0:T(8,128)(2,1)}, bf16[2,48,384]{2,1,0:T(8,128)(2,1)S(1)}, u32[]{:S(2)}, u32[]{:S(2)}) collective-permute-start(bf16[2,48,384]{2,1,0:T(8,128)(2,1)} %get-tuple-element.35), channel_id=1, source_target_pairs={{0,16},{2,18},{4,20},{6,22},{8,24},{10,26},{12,28},{14,30},{16,0},... | collective-permute-start | bytes 221192 | tf_op jit(solution)/shard_map/ppermute | solution.py:322
  8.0 6.5 %collective-permute-start.4 = (bf16[2,48,384]{2,1,0:T(8,128)(2,1)}, bf16[2,48,384]{2,1,0:T(8,128)(2,1)S(1)}, u32[]{:S(2)}, u32[]{:S(2)}) collective-permute-start(bf16[2,48,384]{2,1,0:T(8,128)(2,1)} %get-tuple-element.36), channel_id=1, source_target_pairs={{0,24},{2,26},{4,28},{6,30},{8,16},{10,18},{12,20},{14,22},{16,8},... | collective-permute-start | bytes 221192 | tf_op jit(solution)/shard_map/ppermute | solution.py:322
  8.0 10.5 %copy-start.16 = (bf16[48,384]{1,0:T(8,128)(2,1)S(1)}, bf16[48,384]{1,0:T(8,128)(2,1)}, u32[]{:S(2)}) copy-start(bf16[48,384]{1,0:T(8,128)(2,1)} %get-tuple-element.46) | copy-start | bytes 110596
  8.0 11.6 %copy-start.15 = (bf16[48,384]{1,0:T(8,128)(2,1)S(1)}, bf16[48,384]{1,0:T(8,128)(2,1)}, u32[]{:S(2)}) copy-start(bf16[48,384]{1,0:T(8,128)(2,1)} %get-tuple-element.47) | copy-start | bytes 110596
  8.0 13.9 %copy-start = (bf16[1536,192]{0,1:T(8,128)(2,1)S(1)}, bf16[1536,192]{0,1:T(8,128)(2,1)}, u32[]{:S(2)}) copy-start(bf16[1536,192]{0,1:T(8,128)(2,1)} %param.13) | copy-start | bytes 1769476
  8.0 16.9 %copy-start.14 = (bf16[48,384]{1,0:T(8,128)(2,1)S(1)}, bf16[48,384]{1,0:T(8,128)(2,1)}, u32[]{:S(2)}) copy-start(bf16[48,384]{1,0:T(8,128)(2,1)} %get-tuple-element.48) | copy-start | bytes 110596
  8.0 25.0 %copy-start.3 = (bf16[2,48,384]{2,1,0:T(8,128)(2,1)S(1)}, bf16[2,48,384]{2,1,0:T(8,128)(2,1)}, u32[]{:S(2)}) copy-start(bf16[2,48,384]{2,1,0:T(8,128)(2,1)} %get-tuple-element.33.refs_0_) | copy-start | bytes 221188
  8.0 25.0 %copy-start.4 = (bf16[48,384]{1,0:T(8,128)(2,1)S(1)}, bf16[48,384]{1,0:T(8,128)(2,1)}, u32[]{:S(2)}) copy-start(bf16[48,384]{1,0:T(8,128)(2,1)} %get-tuple-element.45.refs_8_) | copy-start | bytes 110596
  8.0 8.7 %collective-permute-start = (bf16[2,48,384]{2,1,0:T(8,128)(2,1)}, bf16[2,48,384]{2,1,0:T(8,128)(2,1)S(1)}, u32[]{:S(2)}, u32[]{:S(2)}) collective-permute-start(bf16[2,48,384]{2,1,0:T(8,128)(2,1)} %get-tuple-element.33.refs_0_), channel_id=1, source_target_pairs={{0,2},{2,0},{4,6},{6,4},{8,10},{10,8},{12,14},{14,12},{16,18},{18,... | collective-permute-start | bytes 221192 | tf_op jit(solution)/shard_map/ppermute | solution.py:322
  8.1 8.6 %collective-permute-start.1 = (bf16[2,48,384]{2,1,0:T(8,128)(2,1)}, bf16[2,48,384]{2,1,0:T(8,128)(2,1)S(1)}, u32[]{:S(2)}, u32[]{:S(2)}) collective-permute-start(bf16[2,48,384]{2,1,0:T(8,128)(2,1)} %get-tuple-element.33.refs_0_), channel_id=1, source_target_pairs={{0,4},{2,6},{4,0},{6,2},{8,12},{10,14},{12,8},{14,10},{16,20},{18,... | collective-permute-start | bytes 221192 | tf_op jit(solution)/shard_map/ppermute | solution.py:322
  16.7 13.9 %collective-permute-start.6 = (bf16[3,2,48,384]{3,2,1,0:T(8,128)(2,1)}, bf16[3,2,48,384]{3,2,1,0:T(8,128)(2,1)S(1)}, u32[]{:S(2)}, u32[]{:S(2)}) collective-permute-start(bf16[3,2,48,384]{3,2,1,0:T(8,128)(2,1)} %shard_map.83.refs_4_), channel_id=1, source_target_pairs={{0,2},{2,0},{4,6},{6,4},{8,10},{10,8},{12,14},{14,12},{16,18},{18,... | collective-permute-start | bytes 663560 | tf_op jit(solution)/shard_map/ppermute | solution.py:322
  16.8 13.9 %collective-permute-start.7 = (bf16[3,2,48,384]{3,2,1,0:T(8,128)(2,1)}, bf16[3,2,48,384]{3,2,1,0:T(8,128)(2,1)S(1)}, u32[]{:S(2)}, u32[]{:S(2)}) collective-permute-start(bf16[3,2,48,384]{3,2,1,0:T(8,128)(2,1)} %shard_map.83.refs_4_), channel_id=1, source_target_pairs={{0,4},{2,6},{4,0},{6,2},{8,12},{10,14},{12,8},{14,10},{16,20},{18,... | collective-permute-start | bytes 663560 | tf_op jit(solution)/shard_map/ppermute | solution.py:322
  18.3 12.4 %collective-permute-start.5 = (bf16[2,48,384]{2,1,0:T(8,128)(2,1)S(1)}, bf16[2,48,384]{2,1,0:T(8,128)(2,1)S(1)}, u32[]{:S(2)}, u32[]{:S(2)}) collective-permute-start(bf16[2,48,384]{2,1,0:T(8,128)(2,1)S(1)} %collective-permute-done.1.refs_2_), channel_id=1, source_target_pairs={{0,2},{2,0},{4,6},{6,4},{8,10},{10,8},{12,14},{14,12},{16,18},{18,... | collective-permute-start | bytes 221192 | tf_op jit(solution)/shard_map/ppermute | solution.py:322
  18.5 4.0 %collective-permute-start.8 = (bf16[48,384]{1,0:T(8,128)(2,1)S(1)}, bf16[48,384]{1,0:T(8,128)(2,1)S(1)}, u32[]{:S(2)}, u32[]{:S(2)}) collective-permute-start(bf16[48,384]{1,0:T(8,128)(2,1)S(1)} %copy-done.16), channel_id=1, source_target_pairs={{0,8},{2,10},{4,12},{6,14},{8,0},{10,2},{12,4},{14,6},{16,24},{18,... | collective-permute-start | bytes 110600 | tf_op jit(solution)/shard_map/ppermute | solution.py:322
  19.6 5.4 %collective-permute-start.9 = (bf16[48,384]{1,0:T(8,128)(2,1)S(1)}, bf16[48,384]{1,0:T(8,128)(2,1)S(1)}, u32[]{:S(2)}, u32[]{:S(2)}) collective-permute-start(bf16[48,384]{1,0:T(8,128)(2,1)S(1)} %copy-done.15), channel_id=1, source_target_pairs={{0,16},{2,18},{4,20},{6,22},{8,24},{10,26},{12,28},{14,30},{16,0},... | collective-permute-start | bytes 110600 | tf_op jit(solution)/shard_map/ppermute | solution.py:322
  22.4 8.7 %collective-permute-start.14 = (bf16[96,1536]{1,0:T(8,128)(2,1)S(1)}, bf16[96,1536]{1,0:T(8,128)(2,1)S(1)}, u32[]{:S(2)}, u32[]{:S(2)}) collective-permute-start(bf16[96,1536]{1,0:T(8,128)(2,1)S(1)} %get-tuple-element.61), channel_id=1, source_target_pairs={{0,4},{2,6},{4,0},{6,2},{8,12},{10,14},{12,8},{14,10},{16,20},{18,... | collective-permute-start | bytes 884744 | tf_op jit(solution)/shard_map/ppermute | solution.py:322
  24.9 5.8 %collective-permute-start.10 = (bf16[48,384]{1,0:T(8,128)(2,1)S(1)}, bf16[48,384]{1,0:T(8,128)(2,1)S(1)}, u32[]{:S(2)}, u32[]{:S(2)}) collective-permute-start(bf16[48,384]{1,0:T(8,128)(2,1)S(1)} %copy-done.14), channel_id=1, source_target_pairs={{0,24},{2,26},{4,28},{6,30},{8,16},{10,18},{12,20},{14,22},{16,8},... | collective-permute-start | bytes 110600 | tf_op jit(solution)/shard_map/ppermute | solution.py:322
  30.7 1.5 %collective-permute-start.11 = (bf16[3,2,48,384]{3,2,1,0:T(8,128)(2,1)S(1)}, bf16[3,2,48,384]{3,2,1,0:T(8,128)(2,1)S(1)}, u32[]{:S(2)}, u32[]{:S(2)}) collective-permute-start(bf16[3,2,48,384]{3,2,1,0:T(8,128)(2,1)S(1)} %collective-permute-done.7.refs_6_), channel_id=1, source_target_pairs={{0,2},{2,0},{4,6},{6,4},{8,10},{10,8},{12,14},{14,12},{16,18},{18,... | collective-permute-start | bytes 663560 | tf_op jit(solution)/shard_map/ppermute | solution.py:322
  32.2 14.9 %collective-permute-start.16 = (bf16[192,1536]{1,0:T(8,128)(2,1)S(1)}, bf16[192,1536]{1,0:T(8,128)(2,1)S(1)}, u32[]{:S(2)}, u32[]{:S(2)}) collective-permute-start(bf16[192,1536]{1,0:T(8,128)(2,1)S(1)} %bitcast.3), channel_id=1, source_target_pairs={{0,2},{2,0},{4,6},{6,4},{8,10},{10,8},{12,14},{14,12},{16,18},{18,... | collective-permute-start | bytes 1769480 | tf_op jit(solution)/shard_map/ppermute | solution.py:322
  32.4 14.8 %collective-permute-start.15 = (bf16[96,1536]{1,0:T(8,128)(2,1)S(1)}, bf16[96,1536]{1,0:T(8,128)(2,1)S(1)}, u32[]{:S(2)}, u32[]{:S(2)}) collective-permute-start(bf16[96,1536]{1,0:T(8,128)(2,1)S(1)} %get-tuple-element.50), channel_id=1, source_target_pairs={{0,4},{2,6},{4,0},{6,2},{8,12},{10,14},{12,8},{14,10},{16,20},{18,... | collective-permute-start | bytes 884744 | tf_op jit(solution)/shard_map/ppermute | solution.py:322
  32.9 14.2 %collective-permute-start.17 = (bf16[96,1536]{1,0:T(8,128)(2,1)S(1)}, bf16[96,1536]{1,0:T(8,128)(2,1)S(1)}, u32[]{:S(2)}, u32[]{:S(2)}) collective-permute-start(bf16[96,1536]{1,0:T(8,128)(2,1)S(1)} %collective-permute-done.14.refs_6_), channel_id=1, source_target_pairs={{0,2},{2,0},{4,6},{6,4},{8,10},{10,8},{12,14},{14,12},{16,18},{18,... | collective-permute-start | bytes 884744 | tf_op jit(solution)/shard_map/ppermute | solution.py:322
  33.9 34.5 %copy-start.12 = (f32[1536]{0:T(1024)S(1)}, f32[1536]{0:T(1024)}, u32[]{:S(2)}) copy-start(f32[1536]{0:T(1024)} %param.14) | copy-start | bytes 18436
  33.9 35.1 %copy-start.13 = (f32[1536]{0:T(1024)S(1)}, f32[1536]{0:T(1024)}, u32[]{:S(2)}) copy-start(f32[1536]{0:T(1024)} %param.15) | copy-start | bytes 18436
  36.3 9.3 %collective-permute-start.12 = (bf16[192,384]{1,0:T(8,128)(2,1)S(1)}, bf16[192,384]{1,0:T(8,128)(2,1)S(1)}, u32[]{:S(2)}, u32[]{:S(2)}) collective-permute-start(bf16[192,384]{1,0:T(8,128)(2,1)S(1)} %shard_map.85.refs_0_), channel_id=1, source_target_pairs={{0,8},{2,10},{4,12},{6,14},{8,0},{10,2},{12,4},{14,6},{16,24},{18,... | collective-permute-start | bytes 442376 | tf_op jit(solution)/shard_map/ppermute | solution.py:322
  37.3 9.9 %collective-permute-start.13 = (bf16[192,384]{1,0:T(8,128)(2,1)S(1)}, bf16[192,384]{1,0:T(8,128)(2,1)S(1)}, u32[]{:S(2)}, u32[]{:S(2)}) collective-permute-start(bf16[192,384]{1,0:T(8,128)(2,1)S(1)} %shard_map.85.refs_0_), channel_id=1, source_target_pairs={{0,16},{2,18},{4,20},{6,22},{8,24},{10,26},{12,28},{14,30},{16,0},... | collective-permute-start | bytes 442376 | tf_op jit(solution)/shard_map/ppermute | solution.py:322
  47.2 6.3 %collective-permute-start.19 = (bf16[96,1536]{1,0:T(8,128)(2,1)S(1)}, bf16[96,1536]{1,0:T(8,128)(2,1)S(1)}, u32[]{:S(2)}, u32[]{:S(2)}) collective-permute-start(bf16[96,1536]{1,0:T(8,128)(2,1)S(1)} %collective-permute-done.15.refs_7_), channel_id=1, source_target_pairs={{0,2},{2,0},{4,6},{6,4},{8,10},{10,8},{12,14},{14,12},{16,18},{18,... | collective-permute-start | bytes 884744 | tf_op jit(solution)/shard_map/ppermute | solution.py:322
  47.2 6.3 %collective-permute-start.18 = (bf16[192,384]{1,0:T(8,128)(2,1)S(1)}, bf16[192,384]{1,0:T(8,128)(2,1)S(1)}, u32[]{:S(2)}, u32[]{:S(2)}) collective-permute-start(bf16[192,384]{1,0:T(8,128)(2,1)S(1)} %collective-permute-done.13.refs_2_), channel_id=1, source_target_pairs={{0,8},{2,10},{4,12},{6,14},{8,0},{10,2},{12,4},{14,6},{16,24},{18,... | collective-permute-start | bytes 442376 | tf_op jit(solution)/shard_map/ppermute | solution.py:322
  55.2 4.9 %collective-permute-start.20 = (bf16[48,768]{1,0:T(8,128)(2,1)S(1)}, bf16[48,768]{1,0:T(8,128)(2,1)S(1)}, u32[]{:S(2)}, u32[]{:S(2)}) collective-permute-start(bf16[48,768]{1,0:T(8,128)(2,1)S(1)} %get-tuple-element.56), channel_id=1, source_target_pairs={{0,8},{2,10},{4,12},{6,14},{8,0},{10,2},{12,4},{14,6},{16,24},{18,... | collective-permute-start | bytes 221192 | tf_op jit(solution)/shard_map/ppermute | solution.py:322
  55.7 8.0 %collective-permute-start.21 = (bf16[48,768]{1,0:T(8,128)(2,1)S(1)}, bf16[48,768]{1,0:T(8,128)(2,1)S(1)}, u32[]{:S(2)}, u32[]{:S(2)}) collective-permute-start(bf16[48,768]{1,0:T(8,128)(2,1)S(1)} %get-tuple-element.57), channel_id=1, source_target_pairs={{0,16},{2,18},{4,20},{6,22},{8,24},{10,26},{12,28},{14,30},{16,0},... | collective-permute-start | bytes 221192 | tf_op jit(solution)/shard_map/ppermute | solution.py:322
  58.3 6.3 %collective-permute-start.22 = (bf16[48,768]{1,0:T(8,128)(2,1)S(1)}, bf16[48,768]{1,0:T(8,128)(2,1)S(1)}, u32[]{:S(2)}, u32[]{:S(2)}) collective-permute-start(bf16[48,768]{1,0:T(8,128)(2,1)S(1)} %get-tuple-element.58), channel_id=1, source_target_pairs={{0,24},{2,26},{4,28},{6,30},{8,16},{10,18},{12,20},{14,22},{16,8},... | collective-permute-start | bytes 221192 | tf_op jit(solution)/shard_map/ppermute | solution.py:322
  66.9 5.4 %collective-permute-start.23 = (bf16[2,48,768]{2,1,0:T(8,128)(2,1)}, bf16[2,48,768]{2,1,0:T(8,128)(2,1)S(1)}, u32[]{:S(2)}, u32[]{:S(2)}) collective-permute-start(bf16[2,48,768]{2,1,0:T(8,128)(2,1)} %get-tuple-element.60), channel_id=1, source_target_pairs={{0,1},{1,0},{2,3},{3,2},{4,5},{5,4},{6,7},{7,6},{8,9},{9,8},{10,11... | collective-permute-start | bytes 442376 | tf_op jit(solution)/shard_map/ppermute | solution.py:361
  (9 other events, 12.8 us)

commit v4 on v3

--- a/solution.py
+++ b/solution.py
@@ -10,6 +10,7 @@
 HD = 128
 SPREAD = 4
 PACK_LIMIT = 56 << 20
+SMALL = 16 << 20
 PICK_LIMIT = 50 << 20
 VMEM = pl.BlockSpec(memory_space=pltpu.VMEM)
 HBM = pl.BlockSpec(memory_space=pltpu.HBM)
@@ -150,23 +151,28 @@
 
 
 def merge_kernel(*refs):
-    for index, ref in enumerate(refs[:-1]):
-        refs[-1][index] = ref[...]
+    parts, (some, every) = refs[:-2], refs[-2:]
+    for index, part in enumerate(parts):
+        every[index] = part[...]
+        if index:
+            some[index - 1] = part[...]
 
 
 def merge(parts):
+    shapes = [(count, *parts[0].shape) for count in (len(parts) - 1, len(parts))]
     return pl.pallas_call(
         merge_kernel,
-        out_shape=jax.ShapeDtypeStruct((len(parts), *parts[0].shape), parts[0].dtype),
+        out_shape=[jax.ShapeDtypeStruct(shape, parts[0].dtype) for shape in shapes],
         in_specs=[VMEM] * len(parts),
-        out_specs=VMEM,
+        out_specs=[VMEM] * 2,
+        compiler_params=pltpu.CompilerParams(vmem_limit_bytes=SMALL),
         cost_estimate=pl.CostEstimate(flops=0, bytes_accessed=4 * len(parts) * parts[0].size, transcendentals=0),
     )(*parts)
 
 
 def attend_kernel(groups, *refs):
-    owns, merged, asked, refs = refs[:SPREAD], refs[SPREAD : 2 * SPREAD], refs[2 * SPREAD : 2 * SPREAD + groups], refs[2 * SPREAD + groups :]
-    text, stale, out, query, residual = refs
+    (every, near, own_far, some_far, own_corner, some_corner), refs = refs[:6], refs[6:]
+    asked, (text, stale, out, query, residual) = refs[:groups], refs[groups:]
     group, spot = place()
     rows, width = asked[0].shape
     for turn in range(groups):
@@ -174,7 +180,12 @@
         query[pl.ds(aligned(origin, rows), rows), :] = asked[turn][...]
         for twist in range(SPREAD):
             token = origin * SPREAD + jnp.bitwise_xor(spot, twist)
-            part = owns[twist][...] if turn == 0 else merged[twist][turn - 1]
+            if twist < 2:
+                part = (every, near)[twist][turn]
+            elif turn == 0:
+                part = (own_far, own_corner)[twist - 2][...]
+            else:
+                part = (some_far, some_corner)[twist - 2][turn - 1]
             residual[:, pl.ds(aligned(token, rows), rows), :] = part
     for head in range(width // HD):
         cols = slice(head * HD, (head + 1) * HD)
@@ -197,7 +208,7 @@
         out[:, cols] = (mixed / total).astype(jnp.bfloat16)
 
 
-def attend(owns, merged, query_parts, text, stale):
+def attend(pieces, query_parts, text, stale):
     groups = len(query_parts)
     rows, width = query_parts[0].shape
     keys = stale.shape[1]
@@ -206,7 +217,7 @@
     return pl.pallas_call(
         functools.partial(attend_kernel, groups),
         out_shape=jax.ShapeDtypeStruct((groups * rows, width), bf16),
-        in_specs=[VMEM] * (2 * SPREAD + groups + 2),
+        in_specs=[VMEM] * (len(pieces) + groups + 2),
         out_specs=VMEM,
         scratch_shapes=[pltpu.VMEM((groups * rows, width), bf16), pltpu.VMEM((2, keys, width), bf16)],
         compiler_params=pltpu.CompilerParams(vmem_limit_bytes=24 << 20),
@@ -215,7 +226,7 @@
             bytes_accessed=4 * width * (texts + 2 * keys),
             transcendentals=groups * rows * (texts + keys) * (width // HD),
         ),
-    )(*owns, *merged, *query_parts, text, stale)
+    )(*pieces, *query_parts, text, stale)
 
 
 def project_kernel(parts, weights, outs, weight, total):
@@ -227,7 +238,7 @@
         start = jnp.bitwise_xor(spot, twist) * span
         for piece in weights[twist]:
             height = piece.shape[0]
-            weight[pl.ds(pl.multiple_of(start, height), height), :] = piece[...]
+            weight[pl.ds(pl.multiple_of(start, 16), height), :] = piece[...]
             start += height
     added = None
     for turn, part in enumerate(parts):
@@ -286,6 +297,7 @@
         in_specs=[VMEM] * groups,
         out_specs=[VMEM] * 2,
         scratch_shapes=[pltpu.VMEM((groups, *parts[0].shape), jnp.bfloat16)],
+        compiler_params=pltpu.CompilerParams(vmem_limit_bytes=SMALL),
         cost_estimate=pl.CostEstimate(flops=0, bytes_accessed=4 * groups * parts[0].size, transcendentals=0),
     )(*parts)
 
@@ -306,6 +318,7 @@
         out_shape=jax.ShapeDtypeStruct((rows, width), jnp.bfloat16),
         in_specs=[VMEM] * 4,
         out_specs=VMEM,
+        compiler_params=pltpu.CompilerParams(vmem_limit_bytes=SMALL),
         cost_estimate=pl.CostEstimate(flops=3 * rows * width, bytes_accessed=4 * rows * width, transcendentals=0),
     )(kept, arrived, bias.reshape(1, width), gate.reshape(1, width))
 
@@ -322,32 +335,33 @@
         return lax.ppermute(value, "patch", [(p, p ^ twist) for p in range(size)])
 
     def along(values):
-        return [swap(values[turn], turn * SPREAD) for turn in range(1, groups)]
+        moved = {turn: swap(values[turn], turn * SPREAD) for turn in (2, 1, 3)}
+        return [moved[turn] for turn in range(1, groups)]
 
     residuals, queries = pack(groups, queries, codes, exponents)
     weight = out_weight.T
-    half = weight.shape[0] // 2
+    cut = weight.shape[0] // SPREAD
+    early, late = weight[:cut], weight[cut:]
     text, stale = pick(groups, text_kv, stale_kv)
 
     own = residuals[0]
     arrived = along(residuals)
-    own_far, own_near = swap(own, 2), swap(own, 1)
-    early = swap(weight[:half], 2)
-
-    merged = merge(arrived)
-    merged = after(merged, own_far, own_near, text, stale)
-    queries = lax.optimization_barrier((*queries, merged))[:groups]
-    merged_far, merged_near = swap(merged, 2), swap(merged, 1)
-    own_corner = swap(after(own_far, merged), 1)
+    own_far = swap(own, 2)
+    early = swap(early, 2)
+
+    some, every = merge([own, *arrived])
+    some, every = lax.optimization_barrier((some, every, own_far, early, text, stale))[:2]
+    queries = lax.optimization_barrier((*queries, some))[:groups]
+    some_far, near = swap(some, 2), swap(every, 1)
     asked = [queries[0], *along(queries)]
 
-    merged_corner = swap(after(merged_far, merged_near, own_corner, *asked), 1)
-    owns = [own, own_near, own_far, own_corner]
-    attended = attend(owns, [merged, merged_near, merged_far, merged_corner], asked, text, stale)
-
-    weight, late, early = lax.optimization_barrier((weight, weight[half:], early, merged_corner))[:3]
+    own_far, some_far = lax.optimization_barrier((own_far, some_far, near, *asked))[:2]
+    own_corner, some_corner = swap(own_far, 1), swap(some_far, 1)
+    attended = attend([every, near, own_far, some_far, own_corner, some_corner], asked, text, stale)
+
+    late = swap(after(late, some_far), 2)
+    weight, early = lax.optimization_barrier((weight, early, own_corner, some_corner))[:2]
     across, beside = swap(attended, 2 * SPREAD), swap(attended, SPREAD)
-    late = swap(late, 2)
     early_near = swap(early, 1)
     weight_near = swap(weight, 1)
 
@@ -356,7 +370,6 @@
     late_near = swap(late, 1)
     weights = [(weight,), (weight_near,), (early, late), (early_near, late_near)]
     terms = project([attended, beside, across, last], weights)
-
     kept, sent = divide([terms[0], *along(terms)])
     received = lax.ppermute(sent, "head", [(0, 1), (1, 0)])
     return finish(kept, received, out_bias, out_gate)

time: 75 us -> 64.3 us (0.86)
  Pallas kernels: 12.4 us -> 8.09 us
  local copies, waits for them, and re-layouts: 4.74 us -> 1 us
  starting transfers between devices: 26 us -> 23.9 us
    unnamed x34 -> x16, local copies, waits for them, and re-layouts: 3.51 us -> 0.04 us
    ppermute x23 -> x22, starting transfers between devices: 24.5 us -> 22.3 us  [swap(): return lax.ppermute(value, 'patch', [(p, p ^ twist) for p in range(size)])]
    pallas_call x1, Pallas kernels: 1.75 us -> 0.05 us  [divide(): pl.pallas_call(divide_kernel, out_shape=[shape] * 2, in_specs=[VMEM] * gr...]
    pallas_call x1, Pallas kernels: 1.66 us -> 0.05 us  [merge(): pl.pallas_call(merge_kernel, out_shape=[jax.ShapeDtypeStruct(shape, parts...]
    ppermute x23 -> x22, waiting for transfers between devices: 28.7 us -> 27.4 us  [swap(): return lax.ppermute(value, 'patch', [(p, p ^ twist) for p in range(size)])]
    pallas_call x1, Pallas kernels: 1.7 us -> 0.72 us  [finish(): pl.pallas_call(finish_kernel, out_shape=jax.ShapeDtypeStruct((rows, width...]
    ppermute x1, waiting for transfers between devices: 2.63 us -> 3.58 us  [grouped_body(): received = lax.ppermute(sent, 'head', [(0, 1), (1, 0)])]
    slice x1 -> x2, local copies, waits for them, and re-layouts: 0.04 us -> 0.95 us  [grouped_body(): early, late = (weight[:cut], weight[cut:])]
  transfers between devices with their start and end apart: 24 -> 23, of which waited for: 14 -> 11; matrix products, arithmetic and copies ran while one was open for 2% -> 0% of each run, Pallas kernels for 7% -> 10%
where the time goes in v4:
time: 64.3 us; the launch traced here: 64.1 us
  waiting for transfers between devices  31 us (48%)
  starting transfers between devices  23.9 us (37%)
  Pallas kernels  8.09 us (13%)
  local copies, waits for them, and re-layouts  1 us (2%)
    ppermute x22, waiting for transfers between devices, swap(): return lax.ppermute(value, 'patch', [(p, p ^ twist) for p in range(size)])  27.4 us
    ppermute x22, starting transfers between devices, swap(): return lax.ppermute(value, 'patch', [(p, p ^ twist) for p in range(size)])  22.3 us
    ppermute x1, waiting for transfers between devices, grouped_body(): received = lax.ppermute(sent, 'head', [(0, 1), (1, 0)])  3.58 us
    pallas_call x1, Pallas kernels, attend(): pl.pallas_call(functools.partial(attend_kernel, groups), out_shape=jax.Sh...  2.33 us
    pallas_call x1, Pallas kernels, pack(): pl.pallas_call(pack_kernel, out_shape=[jax.ShapeDtypeStruct((kinds, rows,...  2.3 us
    ppermute x1, starting transfers between devices, grouped_body(): received = lax.ppermute(sent, 'head', [(0, 1), (1, 0)])  1.59 us
    pallas_call x1, Pallas kernels, pick(): pl.pallas_call(pick_kernel, out_shape=[jax.ShapeDtypeStruct(shape, jnp.bf...  1.53 us
  transfers between devices with their start and end apart: 23, of which 11 were waited for; matrix products, arithmetic and copies ran while one was open for 0% of the time, Pallas kernels for 10%

profile of v4, /device:TPU:0, one launch (start us, length us, event | category | flops | bytes accessed | tf_op | source)
XLA Modules:
  0.0 64.1 jit_solution(16005584577483547167)
XLA Ops:
  0.0 0.9 %slice.8 = bf16[48,1536]{1,0:T(8,128)(2,1)S(1)} slice(bf16[192,1536]{1,0:T(8,128)(2,1)} %bitcast.2), slice={[0:48], [0:1536]} | slice | bytes 294912 | tf_op jit(solution)/shard_map/slice | solution.py:344
  0.9 3.0 %collective-permute-start.4 = (bf16[48,1536]{1,0:T(8,128)(2,1)S(1)}, bf16[48,1536]{1,0:T(8,128)(2,1)S(1)}, u32[]{:S(2)}, u32[]{:S(2)}) collective-permute-start(bf16[48,1536]{1,0:T(8,128)(2,1)S(1)} %slice.8), channel_id=1, source_target_pairs={{0,4},{2,6},{4,0},{6,2},{8,12},{10,14},{12,8},{14,10},{16,20},{18,... | collective-permute-start | bytes 442376 | tf_op jit(solution)/shard_map/ppermute | solution.py:335
  3.9 2.3 %shard_map.82 = (bf16[2,48,384]{2,1,0:T(8,128)(2,1)}, bf16[2,48,384]{2,1,0:T(8,128)(2,1)}, bf16[2,48,384]{2,1,0:T(8,128)(2,1)}, bf16[2,48,384]{2,1,0:T(8,128)(2,...) custom-call(bf16[48,1536]{1,0:T(8,128)(2,1)} %queries_hbm.1, ...), custom_call_target="tpu_custom_call" | custom-call | flops 294912 | bytes 884736 | tf_op jit(solution)/shard_map/pallas_call | solution.py:109
  6.2 1.6 %collective-permute-start = (bf16[2,48,384]{2,1,0:T(8,128)(2,1)}, bf16[2,48,384]{2,1,0:T(8,128)(2,1)S(1)}, u32[]{:S(2)}, u32[]{:S(2)}) collective-permute-start(bf16[2,48,384]{2,1,0:T(8,128)(2,1)} %get-tuple-element.37), channel_id=1, source_target_pairs={{0,8},{2,10},{4,12},{6,14},{8,0},{10,2},{12,4},{14,6},{16,24},{18,... | collective-permute-start | bytes 221192 | tf_op jit(solution)/shard_map/ppermute | solution.py:335
  7.9 2.6 %collective-permute-start.1 = (bf16[2,48,384]{2,1,0:T(8,128)(2,1)}, bf16[2,48,384]{2,1,0:T(8,128)(2,1)S(1)}, u32[]{:S(2)}, u32[]{:S(2)}) collective-permute-start(bf16[2,48,384]{2,1,0:T(8,128)(2,1)} %get-tuple-element.38), channel_id=1, source_target_pairs={{0,16},{2,18},{4,20},{6,22},{8,24},{10,26},{12,28},{14,30},{16,0},... | collective-permute-start | bytes 221192 | tf_op jit(solution)/shard_map/ppermute | solution.py:335
  10.7 0.4 collective-permute-start.3
  11.1 1.5 %shard_map.84 = (bf16[2,512,384]{2,1,0:T(8,128)(2,1)S(1)}, bf16[2,768,384]{2,1,0:T(8,128)(2,1)S(1)}) custom-call(bf16[2,512,1536]{2,1,0:T(8,128)(2,1)} %text_hbm.1, bf16[2,768,1536]{2,1,0:T(8,128)(2,1)} %stale_hbm.1), custom_call_target="tpu_custom_call" | custom-call | bytes 8388608 | tf_op jit(solution)/shard_map/pallas_call | solution.py:142
  12.7 2.9 %collective-permute-done.1.refs_2_ = bf16[2,48,384]{2,1,0:T(8,128)(2,1)S(1)} collective-permute-done((bf16[2,48,384]{2,1,0:T(8,128)(2,1)}, bf16[2,48,384]{2,1,0:T(8,128)(2,1)S(1)}, u32[]{:S(2)}, u32[]{:S(2)}) %collective-permute-start.1) | collective-permute-done | bytes 73760 | tf_op jit(solution)/shard_map/ppermute | solution.py:335
  15.6 1.3 %collective-permute-done.2.refs_3_ = bf16[2,48,384]{2,1,0:T(8,128)(2,1)S(1)} collective-permute-done((bf16[2,48,384]{2,1,0:T(8,128)(2,1)}, bf16[2,48,384]{2,1,0:T(8,128)(2,1)S(1)}, u32[]{:S(2)}, u32[]{:S(2)}) %collective-permute-start.2) | collective-permute-done | bytes 73760 | tf_op jit(solution)/shard_map/ppermute | solution.py:335
  17.1 0.6 collective-permute-start.6
  17.7 0.8 %collective-permute-start.7 = (bf16[48,384]{1,0:T(8,128)(2,1)S(1)}, bf16[48,384]{1,0:T(8,128)(2,1)S(1)}, u32[]{:S(2)}, u32[]{:S(2)}) collective-permute-start(bf16[48,384]{1,0:T(8,128)(2,1)S(1)} %copy-done.7), channel_id=1, source_target_pairs={{0,8},{2,10},{4,12},{6,14},{8,0},{10,2},{12,4},{14,6},{16,24},{18,... | collective-permute-start | bytes 110600 | tf_op jit(solution)/shard_map/ppermute | solution.py:335
  18.5 1.7 %collective-permute-start.8 = (bf16[48,384]{1,0:T(8,128)(2,1)S(1)}, bf16[48,384]{1,0:T(8,128)(2,1)S(1)}, u32[]{:S(2)}, u32[]{:S(2)}) collective-permute-start(bf16[48,384]{1,0:T(8,128)(2,1)S(1)} %copy-done.6), channel_id=1, source_target_pairs={{0,16},{2,18},{4,20},{6,22},{8,24},{10,26},{12,28},{14,30},{16,0},... | collective-permute-start | bytes 110600 | tf_op jit(solution)/shard_map/ppermute | solution.py:335
  20.2 1.9 %collective-permute-start.9 = (bf16[48,384]{1,0:T(8,128)(2,1)S(1)}, bf16[48,384]{1,0:T(8,128)(2,1)S(1)}, u32[]{:S(2)}, u32[]{:S(2)}) collective-permute-start(bf16[48,384]{1,0:T(8,128)(2,1)S(1)} %copy-done.5), channel_id=1, source_target_pairs={{0,24},{2,26},{4,28},{6,30},{8,16},{10,18},{12,20},{14,22},{16,8},... | collective-permute-start | bytes 110600 | tf_op jit(solution)/shard_map/ppermute | solution.py:335
  22.1 2.5 %collective-permute-done.8.refs_8_ = bf16[48,384]{1,0:T(8,128)(2,1)S(1)} collective-permute-done((bf16[48,384]{1,0:T(8,128)(2,1)S(1)}, bf16[48,384]{1,0:T(8,128)(2,1)S(1)}, u32[]{:S(2)}, u32[]{:S(2)}) %collective-permute-start.8) | collective-permute-done | bytes 36896 | tf_op jit(solution)/shard_map/ppermute | solution.py:335
  24.6 1.3 %collective-permute-done.9.refs_9_ = bf16[48,384]{1,0:T(8,128)(2,1)S(1)} collective-permute-done((bf16[48,384]{1,0:T(8,128)(2,1)S(1)}, bf16[48,384]{1,0:T(8,128)(2,1)S(1)}, u32[]{:S(2)}, u32[]{:S(2)}) %collective-permute-start.9) | collective-permute-done | bytes 36896 | tf_op jit(solution)/shard_map/ppermute | solution.py:335
  26.0 0.5 collective-permute-start.10
  26.5 1.1 %collective-permute-done.10.refs_4_ = bf16[2,48,384]{2,1,0:T(8,128)(2,1)S(1)} collective-permute-done((bf16[2,48,384]{2,1,0:T(8,128)(2,1)S(1)}, bf16[2,48,384]{2,1,0:T(8,128)(2,1)S(1)}, u32[]{:S(2)}, u32[]{:S(2)}) %collective-permute-start.10) | collective-permute-done | bytes 73760 | tf_op jit(solution)/shard_map/ppermute | solution.py:335
  27.8 1.6 %collective-permute-start.14 = (bf16[144,1536]{1,0:T(8,128)(2,1)S(1)}, bf16[144,1536]{1,0:T(8,128)(2,1)S(1)}, u32[]{:S(2)}, u32[]{:S(2)}) collective-permute-start(bf16[144,1536]{1,0:T(8,128)(2,1)S(1)} %slice.9), channel_id=1, source_target_pairs={{0,4},{2,6},{4,0},{6,2},{8,12},{10,14},{12,8},{14,10},{16,20},{18,... | collective-permute-start | bytes 1327112 | tf_op jit(solution)/shard_map/ppermute | solution.py:335
  29.4 2.3 %shard_map.85.refs_0_ = bf16[192,384]{1,0:T(8,128)(2,1)S(1)} custom-call(bf16[4,2,48,384]{3,2,1,0:T(8,128)(2,1)S(1)} %get-tuple-element.44.refs_0_, bf16[4,2,48,384]{3,2,1,0:T(8,128)(2,1)S(1)} %collective-permute-done.5.refs_1_, bf16[2,48,384]{2,1,0:T(8,128)(2,1)S(1)} %collective-permute-done.3.refs_2_, ...), custom_call_target="tpu_custom_call" | custom-call | flops 603979776 | bytes 3145728 | tf_op jit(solution)/shard_map/pallas_call | solution.py:217
  31.8 2.4 %collective-permute-start.13 = (bf16[192,384]{1,0:T(8,128)(2,1)S(1)}, bf16[192,384]{1,0:T(8,128)(2,1)S(1)}, u32[]{:S(2)}, u32[]{:S(2)}) collective-permute-start(bf16[192,384]{1,0:T(8,128)(2,1)S(1)} %shard_map.85.refs_0_), channel_id=1, source_target_pairs={{0,16},{2,18},{4,20},{6,22},{8,24},{10,26},{12,28},{14,30},{16,0},... | collective-permute-start | bytes 442376 | tf_op jit(solution)/shard_map/ppermute | solution.py:335
  34.2 5.7 %collective-permute-done.12.refs_1_ = bf16[192,384]{1,0:T(8,128)(2,1)S(1)} collective-permute-done((bf16[192,384]{1,0:T(8,128)(2,1)S(1)}, bf16[192,384]{1,0:T(8,128)(2,1)S(1)}, u32[]{:S(2)}, u32[]{:S(2)}) %collective-permute-start.12) | collective-permute-done | bytes 147488 | tf_op jit(solution)/shard_map/ppermute | solution.py:335
  39.9 1.8 %collective-permute-done.13.refs_2_ = bf16[192,384]{1,0:T(8,128)(2,1)S(1)} collective-permute-done((bf16[192,384]{1,0:T(8,128)(2,1)S(1)}, bf16[192,384]{1,0:T(8,128)(2,1)S(1)}, u32[]{:S(2)}, u32[]{:S(2)}) %collective-permute-start.13) | collective-permute-done | bytes 147488 | tf_op jit(solution)/shard_map/ppermute | solution.py:335
  41.9 6.2 %collective-permute-done.17.refs_3_ = bf16[192,384]{1,0:T(8,128)(2,1)S(1)} collective-permute-done((bf16[192,384]{1,0:T(8,128)(2,1)S(1)}, bf16[192,384]{1,0:T(8,128)(2,1)S(1)}, u32[]{:S(2)}, u32[]{:S(2)}) %collective-permute-start.17) | collective-permute-done | bytes 147488 | tf_op jit(solution)/shard_map/ppermute | solution.py:335
  48.1 1.1 %shard_map.86 = (bf16[48,768]{1,0:T(8,128)(2,1)S(1)}, bf16[48,768]{1,0:T(8,128)(2,1)S(1)}, bf16[48,768]{1,0:T(8,128)(2,1)S(1)}, bf16[48,768]{1,0:T(8,128)(2,1)S(1)}) custom-call(bf16[192,384]{1,0:T(8,128)(2,1)S(1)} %shard_map.85.refs_0_, bf16[192,384]{1,0:T(8,128)(2,1)S(1)} %collective-permute-done.12.refs_1_, ...), custom_call_target="tpu_custom_call" | custom-call | flops 452984832 | bytes 2359296 | tf_op jit(solution)/shard_map/pallas_call | solution.py:266
  49.2 0.3 collective-permute-start.19
  49.5 2.2 %collective-permute-start.20 = (bf16[48,768]{1,0:T(8,128)(2,1)S(1)}, bf16[48,768]{1,0:T(8,128)(2,1)S(1)}, u32[]{:S(2)}, u32[]{:S(2)}) collective-permute-start(bf16[48,768]{1,0:T(8,128)(2,1)S(1)} %get-tuple-element.63), channel_id=1, source_target_pairs={{0,16},{2,18},{4,20},{6,22},{8,24},{10,26},{12,28},{14,30},{16,0},... | collective-permute-start | bytes 221192 | tf_op jit(solution)/shard_map/ppermute | solution.py:335
  51.7 1.9 %collective-permute-start.21 = (bf16[48,768]{1,0:T(8,128)(2,1)S(1)}, bf16[48,768]{1,0:T(8,128)(2,1)S(1)}, u32[]{:S(2)}, u32[]{:S(2)}) collective-permute-start(bf16[48,768]{1,0:T(8,128)(2,1)S(1)} %get-tuple-element.64), channel_id=1, source_target_pairs={{0,24},{2,26},{4,28},{6,30},{8,16},{10,18},{12,20},{14,22},{16,8},... | collective-permute-start | bytes 221192 | tf_op jit(solution)/shard_map/ppermute | solution.py:335
  53.7 0.5 collective-permute-done.19.refs_1_
  54.2 3.9 %collective-permute-done.20.refs_2_ = bf16[48,768]{1,0:T(8,128)(2,1)S(1)} collective-permute-done((bf16[48,768]{1,0:T(8,128)(2,1)S(1)}, bf16[48,768]{1,0:T(8,128)(2,1)S(1)}, u32[]{:S(2)}, u32[]{:S(2)}) %collective-permute-start.20) | collective-permute-done | bytes 73760 | tf_op jit(solution)/shard_map/ppermute | solution.py:335
  58.2 1.6 %collective-permute-start.22 = (bf16[2,48,768]{2,1,0:T(8,128)(2,1)S(1)}, bf16[2,48,768]{2,1,0:T(8,128)(2,1)S(1)}, u32[]{:S(2)}, u32[]{:S(2)}) collective-permute-start(bf16[2,48,768]{2,1,0:T(8,128)(2,1)S(1)} %get-tuple-element.66), channel_id=1, source_target_pairs={{0,1},{1,0},{2,3},{3,2},{4,5},{5,4},{6,7},{7,6},{8,9},{9,8},{10,11... | collective-permute-start | bytes 442376 | tf_op jit(solution)/shard_map/ppermute | solution.py:374
  59.8 3.6 %collective-permute-done.22.arrived = bf16[2,48,768]{2,1,0:T(8,128)(2,1)S(1)} collective-permute-done((bf16[2,48,768]{2,1,0:T(8,128)(2,1)S(1)}, bf16[2,48,768]{2,1,0:T(8,128)(2,1)S(1)}, u32[]{:S(2)}, u32[]{:S(2)}) %collective-permute-start.22) | collective-permute-done | bytes 147488 | tf_op jit(solution)/shard_map/ppermute | solution.py:374
  63.4 0.7 %shard_map.88 = bf16[48,1536]{1,0:T(8,128)(2,1)} custom-call(bf16[2,48,768]{2,1,0:T(8,128)(2,1)S(1)} %get-tuple-element.65.kept, bf16[2,48,768]{2,1,0:T(8,128)(2,1)S(1)} %collective-permute-done.22.arrived, f32[1,1536]{1,0:T(1,128)S(1)} %reshape.6.bias, f32[1,1536]{1,0:T(1,128)S(1)} %reshape.7.gate), custom_call_target="tpu_custom_call" | custom-call | flops 221184 | bytes 294912 | tf_op jit(solution)/shard_map/pallas_call | solution.py:316
  (41 shorter events, 0.9 us)
Async XLA Ops:
  0.9 16.1 %collective-permute-start.4 = (bf16[48,1536]{1,0:T(8,128)(2,1)S(1)}, bf16[48,1536]{1,0:T(8,128)(2,1)S(1)}, u32[]{:S(2)}, u32[]{:S(2)}) collective-permute-start(bf16[48,1536]{1,0:T(8,128)(2,1)S(1)} %slice.8), channel_id=1, source_target_pairs={{0,4},{2,6},{4,0},{6,2},{8,12},{10,14},{12,8},{14,10},{16,20},{18,... | collective-permute-start | bytes 442376 | tf_op jit(solution)/shard_map/ppermute | solution.py:335
  6.2 6.4 %collective-permute-start = (bf16[2,48,384]{2,1,0:T(8,128)(2,1)}, bf16[2,48,384]{2,1,0:T(8,128)(2,1)S(1)}, u32[]{:S(2)}, u32[]{:S(2)}) collective-permute-start(bf16[2,48,384]{2,1,0:T(8,128)(2,1)} %get-tuple-element.37), channel_id=1, source_target_pairs={{0,8},{2,10},{4,12},{6,14},{8,0},{10,2},{12,4},{14,6},{16,24},{18,... | collective-permute-start | bytes 221192 | tf_op jit(solution)/shard_map/ppermute | solution.py:335
  7.9 7.7 %collective-permute-start.1 = (bf16[2,48,384]{2,1,0:T(8,128)(2,1)}, bf16[2,48,384]{2,1,0:T(8,128)(2,1)S(1)}, u32[]{:S(2)}, u32[]{:S(2)}) collective-permute-start(bf16[2,48,384]{2,1,0:T(8,128)(2,1)} %get-tuple-element.38), channel_id=1, source_target_pairs={{0,16},{2,18},{4,20},{6,22},{8,24},{10,26},{12,28},{14,30},{16,0},... | collective-permute-start | bytes 221192 | tf_op jit(solution)/shard_map/ppermute | solution.py:335
  10.5 6.5 %collective-permute-start.2 = (bf16[2,48,384]{2,1,0:T(8,128)(2,1)}, bf16[2,48,384]{2,1,0:T(8,128)(2,1)S(1)}, u32[]{:S(2)}, u32[]{:S(2)}) collective-permute-start(bf16[2,48,384]{2,1,0:T(8,128)(2,1)} %get-tuple-element.39), channel_id=1, source_target_pairs={{0,24},{2,26},{4,28},{6,30},{8,16},{10,18},{12,20},{14,22},{16,8},... | collective-permute-start | bytes 221192 | tf_op jit(solution)/shard_map/ppermute | solution.py:335
  10.7 6.2 %copy-start.1 = (bf16[2,48,384]{2,1,0:T(8,128)(2,1)S(1)}, bf16[2,48,384]{2,1,0:T(8,128)(2,1)}, u32[]{:S(2)}) copy-start(bf16[2,48,384]{2,1,0:T(8,128)(2,1)} %get-tuple-element.36.refs_0_) | copy-start | bytes 221188
  10.7 7.0 %copy-start.7 = (bf16[48,384]{1,0:T(8,128)(2,1)S(1)}, bf16[48,384]{1,0:T(8,128)(2,1)}, u32[]{:S(2)}) copy-start(bf16[48,384]{1,0:T(8,128)(2,1)} %get-tuple-element.51) | copy-start | bytes 110596
  10.7 7.8 %copy-start.6 = (bf16[48,384]{1,0:T(8,128)(2,1)S(1)}, bf16[48,384]{1,0:T(8,128)(2,1)}, u32[]{:S(2)}) copy-start(bf16[48,384]{1,0:T(8,128)(2,1)} %get-tuple-element.52) | copy-start | bytes 110596
  10.7 9.5 %copy-start.5 = (bf16[48,384]{1,0:T(8,128)(2,1)S(1)}, bf16[48,384]{1,0:T(8,128)(2,1)}, u32[]{:S(2)}) copy-start(bf16[48,384]{1,0:T(8,128)(2,1)} %get-tuple-element.53) | copy-start | bytes 110596
  10.7 16.8 %copy-start = (bf16[1536,192]{0,1:T(8,128)(2,1)S(1)}, bf16[1536,192]{0,1:T(8,128)(2,1)}, u32[]{:S(2)}) copy-start(bf16[1536,192]{0,1:T(8,128)(2,1)} %param.13) | copy-start | bytes 1769476
  10.7 18.6 %copy-start.2 = (bf16[48,384]{1,0:T(8,128)(2,1)S(1)}, bf16[48,384]{1,0:T(8,128)(2,1)}, u32[]{:S(2)}) copy-start(bf16[48,384]{1,0:T(8,128)(2,1)} %get-tuple-element.50.refs_6_) | copy-start | bytes 110596
  10.7 6.3 %collective-permute-start.3 = (bf16[2,48,384]{2,1,0:T(8,128)(2,1)}, bf16[2,48,384]{2,1,0:T(8,128)(2,1)S(1)}, u32[]{:S(2)}, u32[]{:S(2)}) collective-permute-start(bf16[2,48,384]{2,1,0:T(8,128)(2,1)} %get-tuple-element.36.refs_0_), channel_id=1, source_target_pairs={{0,4},{2,6},{4,0},{6,2},{8,12},{10,14},{12,8},{14,10},{16,20},{18,... | collective-permute-start | bytes 221192 | tf_op jit(solution)/shard_map/ppermute | solution.py:335
  17.0 8.9 %collective-permute-start.5 = (bf16[4,2,48,384]{3,2,1,0:T(8,128)(2,1)S(1)}, bf16[4,2,48,384]{3,2,1,0:T(8,128)(2,1)S(1)}, u32[]{:S(2)}, u32[]{:S(2)}) collective-permute-start(bf16[4,2,48,384]{3,2,1,0:T(8,128)(2,1)S(1)} %get-tuple-element.44.refs_0_), channel_id=1, source_target_pairs={{0,2},{2,0},{4,6},{6,4},{8,10},{10,8},{12,14},{14,12},{16,18},{18,... | collective-permute-start | bytes 884744 | tf_op jit(solution)/shard_map/ppermute | solution.py:335
  17.1 8.9 %collective-permute-start.6 = (bf16[3,2,48,384]{3,2,1,0:T(8,128)(2,1)S(1)}, bf16[3,2,48,384]{3,2,1,0:T(8,128)(2,1)S(1)}, u32[]{:S(2)}, u32[]{:S(2)}) collective-permute-start(bf16[3,2,48,384]{3,2,1,0:T(8,128)(2,1)S(1)} %get-tuple-element.45), channel_id=1, source_target_pairs={{0,4},{2,6},{4,0},{6,2},{8,12},{10,14},{12,8},{14,10},{16,20},{18,... | collective-permute-start | bytes 663560 | tf_op jit(solution)/shard_map/ppermute | solution.py:335
  17.7 4.4 %collective-permute-start.7 = (bf16[48,384]{1,0:T(8,128)(2,1)S(1)}, bf16[48,384]{1,0:T(8,128)(2,1)S(1)}, u32[]{:S(2)}, u32[]{:S(2)}) collective-permute-start(bf16[48,384]{1,0:T(8,128)(2,1)S(1)} %copy-done.7), channel_id=1, source_target_pairs={{0,8},{2,10},{4,12},{6,14},{8,0},{10,2},{12,4},{14,6},{16,24},{18,... | collective-permute-start | bytes 110600 | tf_op jit(solution)/shard_map/ppermute | solution.py:335
  18.5 6.1 %collective-permute-start.8 = (bf16[48,384]{1,0:T(8,128)(2,1)S(1)}, bf16[48,384]{1,0:T(8,128)(2,1)S(1)}, u32[]{:S(2)}, u32[]{:S(2)}) collective-permute-start(bf16[48,384]{1,0:T(8,128)(2,1)S(1)} %copy-done.6), channel_id=1, source_target_pairs={{0,16},{2,18},{4,20},{6,22},{8,24},{10,26},{12,28},{14,30},{16,0},... | collective-permute-start | bytes 110600 | tf_op jit(solution)/shard_map/ppermute | solution.py:335
  20.2 5.8 %collective-permute-start.9 = (bf16[48,384]{1,0:T(8,128)(2,1)S(1)}, bf16[48,384]{1,0:T(8,128)(2,1)S(1)}, u32[]{:S(2)}, u32[]{:S(2)}) collective-permute-start(bf16[48,384]{1,0:T(8,128)(2,1)S(1)} %copy-done.5), channel_id=1, source_target_pairs={{0,24},{2,26},{4,28},{6,30},{8,16},{10,18},{12,20},{14,22},{16,8},... | collective-permute-start | bytes 110600 | tf_op jit(solution)/shard_map/ppermute | solution.py:335
  26.0 1.6 %collective-permute-start.11 = (bf16[3,2,48,384]{3,2,1,0:T(8,128)(2,1)S(1)}, bf16[3,2,48,384]{3,2,1,0:T(8,128)(2,1)S(1)}, u32[]{:S(2)}, u32[]{:S(2)}) collective-permute-start(bf16[3,2,48,384]{3,2,1,0:T(8,128)(2,1)S(1)} %collective-permute-done.6.refs_3_), channel_id=1, source_target_pairs={{0,2},{2,0},{4,6},{6,4},{8,10},{10,8},{12,14},{14,12},{16,18},{18,... | collective-permute-start | bytes 663560 | tf_op jit(solution)/shard_map/ppermute | solution.py:335
  26.0 1.6 %collective-permute-start.10 = (bf16[2,48,384]{2,1,0:T(8,128)(2,1)S(1)}, bf16[2,48,384]{2,1,0:T(8,128)(2,1)S(1)}, u32[]{:S(2)}, u32[]{:S(2)}) collective-permute-start(bf16[2,48,384]{2,1,0:T(8,128)(2,1)S(1)} %collective-permute-done.3.refs_2_), channel_id=1, source_target_pairs={{0,2},{2,0},{4,6},{6,4},{8,10},{10,8},{12,14},{14,12},{16,18},{18,... | collective-permute-start | bytes 221192 | tf_op jit(solution)/shard_map/ppermute | solution.py:335
  27.5 14.2 %collective-permute-start.15 = (bf16[192,1536]{1,0:T(8,128)(2,1)S(1)}, bf16[192,1536]{1,0:T(8,128)(2,1)S(1)}, u32[]{:S(2)}, u32[]{:S(2)}) collective-permute-start(bf16[192,1536]{1,0:T(8,128)(2,1)S(1)} %bitcast.3), channel_id=1, source_target_pairs={{0,2},{2,0},{4,6},{6,4},{8,10},{10,8},{12,14},{14,12},{16,18},{18,... | collective-permute-start | bytes 1769480 | tf_op jit(solution)/shard_map/ppermute | solution.py:335
  27.8 32.0 %copy-start.3 = (f32[1536]{0:T(1024)S(1)}, f32[1536]{0:T(1024)}, u32[]{:S(2)}) copy-start(f32[1536]{0:T(1024)} %param.14) | copy-start | bytes 18436
  27.8 32.0 %copy-start.4 = (f32[1536]{0:T(1024)S(1)}, f32[1536]{0:T(1024)}, u32[]{:S(2)}) copy-start(f32[1536]{0:T(1024)} %param.15) | copy-start | bytes 18436
  27.8 13.9 %collective-permute-start.14 = (bf16[144,1536]{1,0:T(8,128)(2,1)S(1)}, bf16[144,1536]{1,0:T(8,128)(2,1)S(1)}, u32[]{:S(2)}, u32[]{:S(2)}) collective-permute-start(bf16[144,1536]{1,0:T(8,128)(2,1)S(1)} %slice.9), channel_id=1, source_target_pairs={{0,4},{2,6},{4,0},{6,2},{8,12},{10,14},{12,8},{14,10},{16,20},{18,... | collective-permute-start | bytes 1327112 | tf_op jit(solution)/shard_map/ppermute | solution.py:335
  31.7 8.2 %collective-permute-start.12 = (bf16[192,384]{1,0:T(8,128)(2,1)S(1)}, bf16[192,384]{1,0:T(8,128)(2,1)S(1)}, u32[]{:S(2)}, u32[]{:S(2)}) collective-permute-start(bf16[192,384]{1,0:T(8,128)(2,1)S(1)} %shard_map.85.refs_0_), channel_id=1, source_target_pairs={{0,8},{2,10},{4,12},{6,14},{8,0},{10,2},{12,4},{14,6},{16,24},{18,... | collective-permute-start | bytes 442376 | tf_op jit(solution)/shard_map/ppermute | solution.py:335
  31.8 10.0 %collective-permute-start.13 = (bf16[192,384]{1,0:T(8,128)(2,1)S(1)}, bf16[192,384]{1,0:T(8,128)(2,1)S(1)}, u32[]{:S(2)}, u32[]{:S(2)}) collective-permute-start(bf16[192,384]{1,0:T(8,128)(2,1)S(1)} %shard_map.85.refs_0_), channel_id=1, source_target_pairs={{0,16},{2,18},{4,20},{6,22},{8,24},{10,26},{12,28},{14,30},{16,0},... | collective-permute-start | bytes 442376 | tf_op jit(solution)/shard_map/ppermute | solution.py:335
  34.2 7.5 %collective-permute-start.16 = (bf16[48,1536]{1,0:T(8,128)(2,1)S(1)}, bf16[48,1536]{1,0:T(8,128)(2,1)S(1)}, u32[]{:S(2)}, u32[]{:S(2)}) collective-permute-start(bf16[48,1536]{1,0:T(8,128)(2,1)S(1)} %collective-permute-done.4.refs_6_), channel_id=1, source_target_pairs={{0,2},{2,0},{4,6},{6,4},{8,10},{10,8},{12,14},{14,12},{16,18},{18,... | collective-permute-start | bytes 442376 | tf_op jit(solution)/shard_map/ppermute | solution.py:335
  41.7 6.3 %collective-permute-start.18 = (bf16[144,1536]{1,0:T(8,128)(2,1)S(1)}, bf16[144,1536]{1,0:T(8,128)(2,1)S(1)}, u32[]{:S(2)}, u32[]{:S(2)}) collective-permute-start(bf16[144,1536]{1,0:T(8,128)(2,1)S(1)} %collective-permute-done.14.refs_7_), channel_id=1, source_target_pairs={{0,2},{2,0},{4,6},{6,4},{8,10},{10,8},{12,14},{14,12},{16,18},{18,... | collective-permute-start | bytes 1327112 | tf_op jit(solution)/shard_map/ppermute | solution.py:335
  41.8 6.3 %collective-permute-start.17 = (bf16[192,384]{1,0:T(8,128)(2,1)S(1)}, bf16[192,384]{1,0:T(8,128)(2,1)S(1)}, u32[]{:S(2)}, u32[]{:S(2)}) collective-permute-start(bf16[192,384]{1,0:T(8,128)(2,1)S(1)} %collective-permute-done.13.refs_2_), channel_id=1, source_target_pairs={{0,8},{2,10},{4,12},{6,14},{8,0},{10,2},{12,4},{14,6},{16,24},{18,... | collective-permute-start | bytes 442376 | tf_op jit(solution)/shard_map/ppermute | solution.py:335
  49.2 5.0 %collective-permute-start.19 = (bf16[48,768]{1,0:T(8,128)(2,1)S(1)}, bf16[48,768]{1,0:T(8,128)(2,1)S(1)}, u32[]{:S(2)}, u32[]{:S(2)}) collective-permute-start(bf16[48,768]{1,0:T(8,128)(2,1)S(1)} %get-tuple-element.62), channel_id=1, source_target_pairs={{0,8},{2,10},{4,12},{6,14},{8,0},{10,2},{12,4},{14,6},{16,24},{18,... | collective-permute-start | bytes 221192 | tf_op jit(solution)/shard_map/ppermute | solution.py:335
  49.5 8.6 %collective-permute-start.20 = (bf16[48,768]{1,0:T(8,128)(2,1)S(1)}, bf16[48,768]{1,0:T(8,128)(2,1)S(1)}, u32[]{:S(2)}, u32[]{:S(2)}) collective-permute-start(bf16[48,768]{1,0:T(8,128)(2,1)S(1)} %get-tuple-element.63), channel_id=1, source_target_pairs={{0,16},{2,18},{4,20},{6,22},{8,24},{10,26},{12,28},{14,30},{16,0},... | collective-permute-start | bytes 221192 | tf_op jit(solution)/shard_map/ppermute | solution.py:335
  51.7 6.4 %collective-permute-start.21 = (bf16[48,768]{1,0:T(8,128)(2,1)S(1)}, bf16[48,768]{1,0:T(8,128)(2,1)S(1)}, u32[]{:S(2)}, u32[]{:S(2)}) collective-permute-start(bf16[48,768]{1,0:T(8,128)(2,1)S(1)} %get-tuple-element.64), channel_id=1, source_target_pairs={{0,24},{2,26},{4,28},{6,30},{8,16},{10,18},{12,20},{14,22},{16,8},... | collective-permute-start | bytes 221192 | tf_op jit(solution)/shard_map/ppermute | solution.py:335
  58.2 5.2 %collective-permute-start.22 = (bf16[2,48,768]{2,1,0:T(8,128)(2,1)S(1)}, bf16[2,48,768]{2,1,0:T(8,128)(2,1)S(1)}, u32[]{:S(2)}, u32[]{:S(2)}) collective-permute-start(bf16[2,48,768]{2,1,0:T(8,128)(2,1)S(1)} %get-tuple-element.66), channel_id=1, source_target_pairs={{0,1},{1,0},{2,3},{3,2},{4,5},{5,4},{6,7},{7,6},{8,9},{9,8},{10,11... | collective-permute-start | bytes 442376 | tf_op jit(solution)/shard_map/ppermute | solution.py:374

commit v5 on v4

--- a/solution.py
+++ b/solution.py
@@ -67,8 +67,8 @@
     return me // SPREAD, lax.rem(me, SPREAD)
 
 
-def pack_kernel(queries_hbm, codes_hbm, exponents_hbm, *rest):
-    outs, (codes, queries, exponents, held, sems) = rest[:-5], rest[-5:]
+def pack_kernel(queries_hbm, codes_hbm, exponents_hbm, weight_hbm, *rest):
+    outs, early, (codes, queries, exponents, held, sems) = rest[:-6], rest[-6], rest[-5:]
     groups, kinds, rows, width = held.shape
     group, _ = place()
     per = width // HD
@@ -76,6 +76,7 @@
         pltpu.make_async_copy(exponents_hbm, exponents, sems.at[0]),
         pltpu.make_async_copy(codes_hbm, codes, sems.at[1]),
         pltpu.make_async_copy(queries_hbm, queries, sems.at[2]),
+        pltpu.make_async_copy(weight_hbm.at[0 : early.shape[0]], early, sems.at[3]),
     ]
     for copy in copies:
         copy.start()
@@ -98,9 +99,10 @@
         target = jnp.bitwise_xor(group, turn)
         outs[turn][...] = held[target, 0 : kinds - 1]
         outs[groups + turn][...] = held[target, kinds - 1]
-
-
-def pack(groups, queries, codes, exponents):
+    copies[3].wait()
+
+
+def pack(groups, queries, codes, exponents, weight):
     rows, width = queries.shape
     kinds = codes.shape[0]
     share = width // groups
@@ -109,20 +111,21 @@
     outs = pl.pallas_call(
         pack_kernel,
         out_shape=[jax.ShapeDtypeStruct((kinds, rows, share), bf16)] * groups
-        + [jax.ShapeDtypeStruct((rows, share), bf16)] * groups,
-        in_specs=[HBM] * 3,
-        out_specs=[VMEM] * (2 * groups),
+        + [jax.ShapeDtypeStruct((rows, share), bf16)] * groups
+        + [jax.ShapeDtypeStruct((weight.shape[0] // 2, weight.shape[1]), bf16)],
+        in_specs=[HBM] * 4,
+        out_specs=[VMEM] * (2 * groups) + [HBM],
         scratch_shapes=[
             pltpu.VMEM(codes.shape, jnp.int32),
             pltpu.VMEM(queries.shape, bf16),
             pltpu.VMEM(exponents.shape, jnp.int32),
             pltpu.VMEM((groups, kinds + 1, rows, share), bf16),
-            pltpu.SemaphoreType.DMA((3,)),
+            pltpu.SemaphoreType.DMA((4,)),
         ],
         compiler_params=pltpu.CompilerParams(vmem_limit_bytes=PACK_LIMIT),
         cost_estimate=pl.CostEstimate(flops=2 * codes.size, bytes_accessed=6 * codes.size, transcendentals=0),
-    )(queries, codes, exponents)
-    return outs[:groups], outs[groups:]
+    )(queries, codes, exponents, weight)
+    return outs[:groups], outs[groups : 2 * groups], outs[-1]
 
 
 def pick_kernel(text_hbm, stale_hbm, text, stale, sems):
@@ -168,6 +171,23 @@
         compiler_params=pltpu.CompilerParams(vmem_limit_bytes=SMALL),
         cost_estimate=pl.CostEstimate(flops=0, bytes_accessed=4 * len(parts) * parts[0].size, transcendentals=0),
     )(*parts)
+
+
+def head_output(query, text, stale, residual, cols):
+    text_scores = lax.dot_general(query, text[0, :, cols], NT, preferred_element_type=jnp.float32)
+    image_scores = lax.dot_general(query, stale[0, :, cols], NT, preferred_element_type=jnp.float32)
+    image_scores += lax.dot_general(query, residual[0, :, cols], NT, preferred_element_type=jnp.float32)
+    text_scores *= HD**-0.5
+    image_scores *= HD**-0.5
+    peak = jnp.maximum(jnp.max(text_scores, axis=1, keepdims=True), jnp.max(image_scores, axis=1, keepdims=True))
+    text_weights = jnp.exp(text_scores - peak).astype(jnp.bfloat16)
+    image_weights = jnp.exp(image_scores - peak).astype(jnp.bfloat16)
+    total = jnp.sum(text_weights.astype(jnp.float32), axis=1, keepdims=True)
+    total += jnp.sum(image_weights.astype(jnp.float32), axis=1, keepdims=True)
+    mixed = jnp.dot(text_weights, text[1, :, cols], preferred_element_type=jnp.float32)
+    mixed += jnp.dot(image_weights, stale[1, :, cols], preferred_element_type=jnp.float32)
+    mixed += jnp.dot(image_weights, residual[1, :, cols], preferred_element_type=jnp.float32)
+    return (mixed / total).astype(jnp.bfloat16)
 
 
 def attend_kernel(groups, *refs):
@@ -189,138 +209,143 @@
             residual[:, pl.ds(aligned(token, rows), rows), :] = part
     for head in range(width // HD):
         cols = slice(head * HD, (head + 1) * HD)
-        heads_query = query[:, cols]
-        text_scores = lax.dot_general(heads_query, text[0, :, cols], NT, preferred_element_type=jnp.float32)
-        image_scores = lax.dot_general(heads_query, stale[0, :, cols], NT, preferred_element_type=jnp.float32)
-        image_scores += lax.dot_general(heads_query, residual[0, :, cols], NT, preferred_element_type=jnp.float32)
-        text_scores *= HD**-0.5
-        image_scores *= HD**-0.5
-        peak = jnp.maximum(
-            jnp.max(text_scores, axis=1, keepdims=True), jnp.max(image_scores, axis=1, keepdims=True)
-        )
-        text_weights = jnp.exp(text_scores - peak).astype(jnp.bfloat16)
-        image_weights = jnp.exp(image_scores - peak).astype(jnp.bfloat16)
-        total = jnp.sum(text_weights.astype(jnp.float32), axis=1, keepdims=True)
-        total += jnp.sum(image_weights.astype(jnp.float32), axis=1, keepdims=True)
-        mixed = jnp.dot(text_weights, text[1, :, cols], preferred_element_type=jnp.float32)
-        mixed += jnp.dot(image_weights, stale[1, :, cols], preferred_element_type=jnp.float32)
-        mixed += jnp.dot(image_weights, residual[1, :, cols], preferred_element_type=jnp.float32)
-        out[:, cols] = (mixed / total).astype(jnp.bfloat16)
+        out[:, cols] = head_output(query[:, cols], text, stale, residual, cols)
+
+
+def attend_cost(heads, tokens, texts, keys):
+    return pl.CostEstimate(
+        flops=4 * heads * tokens * HD * (texts + 2 * keys),
+        bytes_accessed=4 * heads * HD * (texts + 2 * keys),
+        transcendentals=heads * tokens * (texts + keys),
+    )
 
 
 def attend(pieces, query_parts, text, stale):
     groups = len(query_parts)
     rows, width = query_parts[0].shape
+    tokens = groups * rows
     keys = stale.shape[1]
     texts = text.shape[1]
-    bf16 = jnp.bfloat16
+    heads = width // HD
+
     return pl.pallas_call(
         functools.partial(attend_kernel, groups),
-        out_shape=jax.ShapeDtypeStruct((groups * rows, width), bf16),
+        out_shape=jax.ShapeDtypeStruct((tokens, width), jnp.bfloat16),
         in_specs=[VMEM] * (len(pieces) + groups + 2),
         out_specs=VMEM,
-        scratch_shapes=[pltpu.VMEM((groups * rows, width), bf16), pltpu.VMEM((2, keys, width), bf16)],
-        compiler_params=pltpu.CompilerParams(vmem_limit_bytes=24 << 20),
+        scratch_shapes=[pltpu.VMEM((tokens, width), jnp.bfloat16), pltpu.VMEM((2, keys, width), jnp.bfloat16)],
+        compiler_params=pltpu.CompilerParams(vmem_limit_bytes=SMALL),
+        cost_estimate=attend_cost(heads, tokens, texts, keys),
+    )(*pieces, *query_parts, text, stale)
+
+
+def order_kernel(*refs):
+    wholes, halves, out = refs[:2], refs[2:-1], refs[-1]
+    _, spot = place()
+    span = out.shape[0] // SPREAD
+    for twist, whole in enumerate(wholes):
+        start = jnp.bitwise_xor(spot, twist) * span
+        out[pl.ds(pl.multiple_of(start, 16), span), :] = whole[...]
+    for index, piece in enumerate(halves):
+        start = jnp.bitwise_xor(spot, 2 + index // 2) * span + index % 2 * (span // 2)
+        out[pl.ds(pl.multiple_of(start, 16), span // 2), :] = piece[...]
+
+
+def order(weight, near, halves):
+    pieces = [weight, near, *halves]
+    span, depth = weight.shape
+    shape = (SPREAD * span, depth)
+    return pl.pallas_call(
+        order_kernel,
+        out_shape=jax.ShapeDtypeStruct(shape, jnp.bfloat16),
+        in_specs=[VMEM] * len(pieces),
+        out_specs=VMEM,
+        compiler_params=pltpu.CompilerParams(vmem_limit_bytes=SMALL),
+        cost_estimate=pl.CostEstimate(flops=0, bytes_accessed=4 * shape[0] * depth, transcendentals=0),
+    )(*pieces)
+
+
+def term_of(part, weight, turn):
+    group, _ = place()
+    width = part.shape[1]
+    columns = pl.ds(aligned(jnp.bitwise_xor(group, turn), width), width)
+    return lax.dot_general(part[...], weight[:, columns], NT, preferred_element_type=jnp.float32)
+
+
+def begin_kernel(*refs):
+    parts, (weight, out) = refs[:-2], refs[-2:]
+    total = term_of(parts[0], weight, 0)
+    for turn in range(1, len(parts)):
+        total += term_of(parts[turn], weight, turn)
+    out[...] = total
+
+
+def begin(parts, weight):
+    tokens, width = parts[0].shape
+    columns = weight.shape[0]
+    return pl.pallas_call(
+        begin_kernel,
+        out_shape=jax.ShapeDtypeStruct((tokens, columns), jnp.float32),
+        in_specs=[VMEM] * (len(parts) + 1),
+        out_specs=VMEM,
+        compiler_params=pltpu.CompilerParams(vmem_limit_bytes=SMALL),
         cost_estimate=pl.CostEstimate(
-            flops=4 * groups * rows * width * (texts + 2 * keys),
-            bytes_accessed=4 * width * (texts + 2 * keys),
-            transcendentals=groups * rows * (texts + keys) * (width // HD),
+            flops=2 * tokens * columns * width * len(parts), bytes_accessed=4 * tokens * columns, transcendentals=0
         ),
-    )(*pieces, *query_parts, text, stale)
-
-
-def project_kernel(parts, weights, outs, weight, total):
-    group, spot = place()
-    width = parts[0].shape[1]
-    span = weight.shape[0] // SPREAD
+    )(*parts, weight)
+
+
+def close_kernel(partial, part, weight, *rest):
+    outs, total = rest[:-1], rest[-1]
+    group, _ = place()
     rows = outs[0].shape[0]
-    for twist in range(SPREAD):
-        start = jnp.bitwise_xor(spot, twist) * span
-        for piece in weights[twist]:
-            height = piece.shape[0]
-            weight[pl.ds(pl.multiple_of(start, 16), height), :] = piece[...]
-            start += height
-    added = None
-    for turn, part in enumerate(parts):
-        origin = jnp.bitwise_xor(group, turn)
-        term = lax.dot_general(
-            part[...], weight[:, pl.ds(aligned(origin, width), width)], NT, preferred_element_type=jnp.float32
-        )
-        added = term if added is None else added + term
-    total[...] = added.astype(jnp.bfloat16)
+    total[...] = (partial[...] + term_of(part, weight, len(outs) - 1)).astype(jnp.bfloat16)
     for turn, out in enumerate(outs):
         out[...] = total[pl.ds(aligned(jnp.bitwise_xor(group, turn), rows), rows), :]
 
 
-def project(parts, weights):
-    groups = len(parts)
-    tokens, width = parts[0].shape
-    depth = weights[0][0].shape[1]
-    columns = SPREAD * sum(piece.shape[0] for piece in weights[0])
-    flat, tree = jax.tree.flatten(weights)
-
-    def kernel(*refs):
-        ins, outs, scratch = refs[: groups + len(flat)], refs[groups + len(flat) : -2], refs[-2:]
-        project_kernel(ins[:groups], jax.tree.unflatten(tree, ins[groups:]), outs, *scratch)
-
-    return pl.pallas_call(
-        kernel,
+def close(groups, partial, part, weight):
+    tokens, columns = partial.shape
+    return pl.pallas_call(
+        close_kernel,
         out_shape=[jax.ShapeDtypeStruct((tokens // groups, columns), jnp.bfloat16)] * groups,
-        in_specs=[VMEM] * (groups + len(flat)),
+        in_specs=[VMEM] * 3,
         out_specs=[VMEM] * groups,
-        scratch_shapes=[pltpu.VMEM((columns, depth), jnp.bfloat16), pltpu.VMEM((tokens, columns), jnp.bfloat16)],
-        compiler_params=pltpu.CompilerParams(vmem_limit_bytes=24 << 20),
+        scratch_shapes=[pltpu.VMEM((tokens, columns), jnp.bfloat16)],
+        compiler_params=pltpu.CompilerParams(vmem_limit_bytes=SMALL),
         cost_estimate=pl.CostEstimate(
-            flops=2 * tokens * columns * depth, bytes_accessed=2 * columns * depth, transcendentals=0
+            flops=2 * tokens * columns * part.shape[1], bytes_accessed=8 * tokens * columns, transcendentals=0
         ),
-    )(*parts, *flat)
-
-
-def divide_kernel(*refs):
-    parts, (keep, send, held) = refs[:-3], refs[-3:]
+    )(partial, part, weight)
+
+
+def finish_kernel(groups, *refs):
+    mine, other, (bias, gate, out, held) = refs[:groups], refs[groups : 2 * groups], refs[2 * groups :]
     group, _ = place()
-    half = lax.axis_index("head")
-    blocks = keep.shape[0]
-    for turn, part in enumerate(parts):
-        held[jnp.bitwise_xor(group, turn)] = part[...]
-    for block in range(blocks):
-        keep[block] = held[half * blocks + block]
-        send[block] = held[(1 - half) * blocks + block]
-
-
-def divide(parts):
-    groups = len(parts)
-    shape = jax.ShapeDtypeStruct((groups // 2, *parts[0].shape), jnp.bfloat16)
-    return pl.pallas_call(
-        divide_kernel,
-        out_shape=[shape] * 2,
-        in_specs=[VMEM] * groups,
-        out_specs=[VMEM] * 2,
-        scratch_shapes=[pltpu.VMEM((groups, *parts[0].shape), jnp.bfloat16)],
-        compiler_params=pltpu.CompilerParams(vmem_limit_bytes=SMALL),
-        cost_estimate=pl.CostEstimate(flops=0, bytes_accessed=4 * groups * parts[0].size, transcendentals=0),
-    )(*parts)
-
-
-def finish_kernel(kept, arrived, bias, gate, out):
-    blocks, _, columns = kept.shape
+    columns = mine[0].shape[1]
+    blocks = groups // 2
+    first = lax.axis_index("head") * blocks
+    for turn in range(groups):
+        origin = jnp.bitwise_xor(group, turn)
+        held[origin] = mine[turn][...].astype(jnp.float32) + other[turn][...].astype(jnp.float32)
     for block in range(blocks):
         cols = slice(block * columns, (block + 1) * columns)
-        total = kept[block].astype(jnp.float32) + arrived[block].astype(jnp.float32)
-        out[:, cols] = (gate[:, cols] * (total + bias[:, cols])).astype(jnp.bfloat16)
-
-
-def finish(kept, arrived, bias, gate):
-    blocks, rows, columns = kept.shape
-    width = blocks * columns
-    return pl.pallas_call(
-        finish_kernel,
+        out[:, cols] = (gate[:, cols] * (held[first + block] + bias[:, cols])).astype(jnp.bfloat16)
+
+
+def finish(mine, other, bias, gate):
+    groups = len(mine)
+    rows, columns = mine[0].shape
+    width = columns * groups // 2
+    return pl.pallas_call(
+        functools.partial(finish_kernel, groups),
         out_shape=jax.ShapeDtypeStruct((rows, width), jnp.bfloat16),
-        in_specs=[VMEM] * 4,
+        in_specs=[VMEM] * (2 * groups + 2),
         out_specs=VMEM,
+        scratch_shapes=[pltpu.VMEM((groups, rows, columns), jnp.float32)],
         compiler_params=pltpu.CompilerParams(vmem_limit_bytes=SMALL),
         cost_estimate=pl.CostEstimate(flops=3 * rows * width, bytes_accessed=4 * rows * width, transcendentals=0),
-    )(kept, arrived, bias.reshape(1, width), gate.reshape(1, width))
+    )(*mine, *other, bias.reshape(1, width), gate.reshape(1, width))
 
 
 def after(value, *others):
@@ -338,16 +363,14 @@
         moved = {turn: swap(values[turn], turn * SPREAD) for turn in (2, 1, 3)}
         return [moved[turn] for turn in range(1, groups)]
 
-    residuals, queries = pack(groups, queries, codes, exponents)
     weight = out_weight.T
-    cut = weight.shape[0] // SPREAD
-    early, late = weight[:cut], weight[cut:]
+    half = weight.shape[0] // 2
+    residuals, queries, early = pack(groups, queries, codes, exponents, weight)
     text, stale = pick(groups, text_kv, stale_kv)
 
     own = residuals[0]
     arrived = along(residuals)
-    own_far = swap(own, 2)
-    early = swap(early, 2)
+    own_far, early = swap(own, 2), swap(early, 2)
 
     some, every = merge([own, *arrived])
     some, every = lax.optimization_barrier((some, every, own_far, early, text, stale))[:2]
@@ -355,24 +378,21 @@
     some_far, near = swap(some, 2), swap(every, 1)
     asked = [queries[0], *along(queries)]
 
-    own_far, some_far = lax.optimization_barrier((own_far, some_far, near, *asked))[:2]
+    own_far, some_far = lax.optimization_barrier((own_far, some_far, near, *asked[2:]))[:2]
     own_corner, some_corner = swap(own_far, 1), swap(some_far, 1)
+    weight, early = lax.optimization_barrier((weight, early, own_corner, some_corner))[:2]
+    weight_near, early_near, late = swap(weight, 1), swap(early, 1), swap(weight[half:], 2)
     attended = attend([every, near, own_far, some_far, own_corner, some_corner], asked, text, stale)
 
-    late = swap(after(late, some_far), 2)
-    weight, early = lax.optimization_barrier((weight, early, own_corner, some_corner))[:2]
     across, beside = swap(attended, 2 * SPREAD), swap(attended, SPREAD)
-    early_near = swap(early, 1)
-    weight_near = swap(weight, 1)
-
-    across, late = lax.optimization_barrier((across, late, beside, weight_near, early_near))[:2]
+    across, beside, late = lax.optimization_barrier((across, beside, late, weight_near, early_near))[:3]
     last = swap(across, SPREAD)
-    late_near = swap(late, 1)
-    weights = [(weight,), (weight_near,), (early, late), (early_near, late_near)]
-    terms = project([attended, beside, across, last], weights)
-    kept, sent = divide([terms[0], *along(terms)])
-    received = lax.ppermute(sent, "head", [(0, 1), (1, 0)])
-    return finish(kept, received, out_bias, out_gate)
+    weight = order(weight, weight_near, [early, late, early_near, swap(late, 1)])
+    terms = close(groups, begin([attended, beside, across], weight), last, weight)
+
+    terms = [terms[0], *along(terms)]
+    received = [lax.ppermute(term, "head", [(0, 1), (1, 0)]) for term in terms]
+    return finish(terms, received, out_bias, out_gate)
 
 
 def solution(mesh):

time: 64.3 us -> 74.4 us (1.16)
  Pallas kernels: 8.09 us -> 16.8 us
  waiting for transfers between devices: 31 us -> 32.4 us
  local copies, waits for them, and re-layouts: 1 us -> 0.07 us
  starting transfers between devices: 23.9 us -> 24.7 us
    pallas_call x1, Pallas kernels: 2.3 us -> 10.8 us  [pack(): pl.pallas_call(pack_kernel, out_shape=[jax.ShapeDtypeStruct((kinds, rows,...]
    ppermute x1 -> x4, starting transfers between devices: 1.59 us -> 4.07 us  [grouped_body(): received = [lax.ppermute(term, 'head', [(0, 1), (1, 0)]) for term in terms]]
    ppermute x22, starting transfers between devices: 22.3 us -> 20.7 us  [swap(): return lax.ppermute(value, 'patch', [(p, p ^ twist) for p in range(size)])]
    ppermute x22, waiting for transfers between devices: 27.4 us -> 28.6 us  [swap(): return lax.ppermute(value, 'patch', [(p, p ^ twist) for p in range(size)])]
    slice x2 -> x1, local copies, waits for them, and re-layouts: 0.95 us -> 0.02 us  [grouped_body(): weight[half:]]
    ppermute x1 -> x4, waiting for transfers between devices: 3.58 us -> 3.8 us  [grouped_body(): received = [lax.ppermute(term, 'head', [(0, 1), (1, 0)]) for term in terms]]
    pallas_call x3 -> x4, Pallas kernels: 1.89 us -> 2.05 us  [the longest x1 0.76 us: finish(): pl.pallas_call(functools.partial(finish_kernel, groups), out_shape=jax.Sh...]
  transfers between devices with their start and end apart: 23 -> 26, of which waited for: 11 -> 12; matrix products, arithmetic and copies ran while one was open for 0% -> 0% of each run, Pallas kernels for 10% -> 6%
where the time goes in v5:
time: 74.4 us; the launch traced here: 74.2 us
  waiting for transfers between devices  32.4 us (44%)
  starting transfers between devices  24.7 us (33%)
  Pallas kernels  16.8 us (23%)
    ppermute x22, waiting for transfers between devices, swap(): return lax.ppermute(value, 'patch', [(p, p ^ twist) for p in range(size)])  28.6 us
    ppermute x22, starting transfers between devices, swap(): return lax.ppermute(value, 'patch', [(p, p ^ twist) for p in range(size)])  20.7 us
    pallas_call x1, Pallas kernels, pack(): pl.pallas_call(pack_kernel, out_shape=[jax.ShapeDtypeStruct((kinds, rows,...  10.8 us
    ppermute x4, starting transfers between devices, grouped_body(): received = [lax.ppermute(term, 'head', [(0, 1), (1, 0)]) for term in terms]  4.07 us
    ppermute x4, waiting for transfers between devices, grouped_body(): received = [lax.ppermute(term, 'head', [(0, 1), (1, 0)]) for term in terms]  3.8 us
    pallas_call x1, Pallas kernels, attend(): pl.pallas_call(functools.partial(attend_kernel, groups), out_shape=jax.Sh...  2.33 us
    pallas_call x1, Pallas kernels, pick(): pl.pallas_call(pick_kernel, out_shape=[jax.ShapeDtypeStruct(shape, jnp.bf...  1.53 us
  transfers between devices with their start and end apart: 26, of which 12 were waited for; matrix products, arithmetic and copies ran while one was open for 0% of the time, Pallas kernels for 6%

profile of v5, /device:TPU:0, one launch (start us, length us, event | category | flops | bytes accessed | tf_op | source)
XLA Modules:
  0.0 74.2 jit_solution(3890981883154705377)
XLA Ops:
  0.0 10.8 %shard_map.82 = (bf16[2,48,384]{2,1,0:T(8,128)(2,1)}, bf16[2,48,384]{2,1,0:T(8,128)(2,1)}, bf16[2,48,384]{2,1,0:T(8,128)(2,1)}, bf16[2,48,384]{2,1,0:T(8,128)(2,...) custom-call(bf16[48,1536]{1,0:T(8,128)(2,1)} %queries_hbm.1, ...), custom_call_target="tpu_custom_call" | custom-call | flops 294912 | bytes 884736 | tf_op jit(solution)/shard_map/pallas_call | solution.py:111
  10.8 3.0 %collective-permute-start.4 = (bf16[96,1536]{1,0:T(8,128)(2,1)}, bf16[96,1536]{1,0:T(8,128)(2,1)S(1)}, u32[]{:S(2)}, u32[]{:S(2)}) collective-permute-start(bf16[96,1536]{1,0:T(8,128)(2,1)} %get-tuple-element.41), channel_id=1, source_target_pairs={{0,4},{2,6},{4,0},{6,2},{8,12},{10,14},{12,8},{14,10},{16,20},{18,... | collective-permute-start | bytes 884744 | tf_op jit(solution)/shard_map/ppermute | solution.py:360
  13.8 1.6 %collective-permute-start = (bf16[2,48,384]{2,1,0:T(8,128)(2,1)}, bf16[2,48,384]{2,1,0:T(8,128)(2,1)S(1)}, u32[]{:S(2)}, u32[]{:S(2)}) collective-permute-start(bf16[2,48,384]{2,1,0:T(8,128)(2,1)} %get-tuple-element.36), channel_id=1, source_target_pairs={{0,8},{2,10},{4,12},{6,14},{8,0},{10,2},{12,4},{14,6},{16,24},{18,... | collective-permute-start | bytes 221192 | tf_op jit(solution)/shard_map/ppermute | solution.py:360
  15.4 2.6 %collective-permute-start.1 = (bf16[2,48,384]{2,1,0:T(8,128)(2,1)}, bf16[2,48,384]{2,1,0:T(8,128)(2,1)S(1)}, u32[]{:S(2)}, u32[]{:S(2)}) collective-permute-start(bf16[2,48,384]{2,1,0:T(8,128)(2,1)} %get-tuple-element.37), channel_id=1, source_target_pairs={{0,16},{2,18},{4,20},{6,22},{8,24},{10,26},{12,28},{14,30},{16,0},... | collective-permute-start | bytes 221192 | tf_op jit(solution)/shard_map/ppermute | solution.py:360
  18.6 1.5 %shard_map.84 = (bf16[2,512,384]{2,1,0:T(8,128)(2,1)S(1)}, bf16[2,768,384]{2,1,0:T(8,128)(2,1)S(1)}) custom-call(bf16[2,512,1536]{2,1,0:T(8,128)(2,1)} %text_hbm.1, bf16[2,768,1536]{2,1,0:T(8,128)(2,1)} %stale_hbm.1), custom_call_target="tpu_custom_call" | custom-call | bytes 8388608 | tf_op jit(solution)/shard_map/pallas_call | solution.py:145
  20.2 2.9 %collective-permute-done.1.refs_2_ = bf16[2,48,384]{2,1,0:T(8,128)(2,1)S(1)} collective-permute-done((bf16[2,48,384]{2,1,0:T(8,128)(2,1)}, bf16[2,48,384]{2,1,0:T(8,128)(2,1)S(1)}, u32[]{:S(2)}, u32[]{:S(2)}) %collective-permute-start.1) | collective-permute-done | bytes 73760 | tf_op jit(solution)/shard_map/ppermute | solution.py:360
  23.1 1.3 %collective-permute-done.2.refs_3_ = bf16[2,48,384]{2,1,0:T(8,128)(2,1)S(1)} collective-permute-done((bf16[2,48,384]{2,1,0:T(8,128)(2,1)}, bf16[2,48,384]{2,1,0:T(8,128)(2,1)S(1)}, u32[]{:S(2)}, u32[]{:S(2)}) %collective-permute-start.2) | collective-permute-done | bytes 73760 | tf_op jit(solution)/shard_map/ppermute | solution.py:360
  24.6 0.6 collective-permute-start.6
  25.2 1.8 %collective-permute-start.7 = (bf16[48,384]{1,0:T(8,128)(2,1)S(1)}, bf16[48,384]{1,0:T(8,128)(2,1)S(1)}, u32[]{:S(2)}, u32[]{:S(2)}) collective-permute-start(bf16[48,384]{1,0:T(8,128)(2,1)S(1)} %copy-done.7), channel_id=1, source_target_pairs={{0,16},{2,18},{4,20},{6,22},{8,24},{10,26},{12,28},{14,30},{16,0},... | collective-permute-start | bytes 110600 | tf_op jit(solution)/shard_map/ppermute | solution.py:360
  27.0 1.3 %collective-permute-start.8 = (bf16[48,384]{1,0:T(8,128)(2,1)S(1)}, bf16[48,384]{1,0:T(8,128)(2,1)S(1)}, u32[]{:S(2)}, u32[]{:S(2)}) collective-permute-start(bf16[48,384]{1,0:T(8,128)(2,1)S(1)} %copy-done.6), channel_id=1, source_target_pairs={{0,24},{2,26},{4,28},{6,30},{8,16},{10,18},{12,20},{14,22},{16,8},... | collective-permute-start | bytes 110600 | tf_op jit(solution)/shard_map/ppermute | solution.py:360
  28.4 2.1 %collective-permute-done.7.refs_8_ = bf16[48,384]{1,0:T(8,128)(2,1)S(1)} collective-permute-done((bf16[48,384]{1,0:T(8,128)(2,1)S(1)}, bf16[48,384]{1,0:T(8,128)(2,1)S(1)}, u32[]{:S(2)}, u32[]{:S(2)}) %collective-permute-start.7) | collective-permute-done | bytes 36896 | tf_op jit(solution)/shard_map/ppermute | solution.py:360
  30.5 2.3 %collective-permute-done.8.refs_9_ = bf16[48,384]{1,0:T(8,128)(2,1)S(1)} collective-permute-done((bf16[48,384]{1,0:T(8,128)(2,1)S(1)}, bf16[48,384]{1,0:T(8,128)(2,1)S(1)}, u32[]{:S(2)}, u32[]{:S(2)}) %collective-permute-start.8) | collective-permute-done | bytes 36896 | tf_op jit(solution)/shard_map/ppermute | solution.py:360
  33.3 1.1 %collective-permute-done.9.refs_4_ = bf16[2,48,384]{2,1,0:T(8,128)(2,1)S(1)} collective-permute-done((bf16[2,48,384]{2,1,0:T(8,128)(2,1)S(1)}, bf16[2,48,384]{2,1,0:T(8,128)(2,1)S(1)}, u32[]{:S(2)}, u32[]{:S(2)}) %collective-permute-start.9) | collective-permute-done | bytes 73760 | tf_op jit(solution)/shard_map/ppermute | solution.py:360
  34.6 1.6 %collective-permute-start.14 = (bf16[96,1536]{1,0:T(8,128)(2,1)S(1)}, bf16[96,1536]{1,0:T(8,128)(2,1)S(1)}, u32[]{:S(2)}, u32[]{:S(2)}) collective-permute-start(bf16[96,1536]{1,0:T(8,128)(2,1)S(1)} %slice.3), channel_id=1, source_target_pairs={{0,4},{2,6},{4,0},{6,2},{8,12},{10,14},{12,8},{14,10},{16,20},{18,... | collective-permute-start | bytes 884744 | tf_op jit(solution)/shard_map/ppermute | solution.py:360
  36.2 4.0 %collective-permute-done.11.refs_7_ = bf16[48,384]{1,0:T(8,128)(2,1)S(1)} collective-permute-done((bf16[48,384]{1,0:T(8,128)(2,1)S(1)}, bf16[48,384]{1,0:T(8,128)(2,1)S(1)}, u32[]{:S(2)}, u32[]{:S(2)}) %collective-permute-start.11) | collective-permute-done | bytes 36896 | tf_op jit(solution)/shard_map/ppermute | solution.py:360
  40.2 2.3 %shard_map.85.refs_0_ = bf16[192,384]{1,0:T(8,128)(2,1)S(1)} custom-call(bf16[4,2,48,384]{3,2,1,0:T(8,128)(2,1)S(1)} %get-tuple-element.44.refs_0_, bf16[4,2,48,384]{3,2,1,0:T(8,128)(2,1)S(1)} %collective-permute-done.5.refs_1_, bf16[2,48,384]{2,1,0:T(8,128)(2,1)S(1)} %collective-permute-done.3.refs_2_, ...), custom_call_target="tpu_custom_call" | custom-call | flops 603979776 | bytes 3145728 | tf_op jit(solution)/shard_map/pallas_call | solution.py:231
  42.5 0.7 collective-permute-start.12
  43.2 1.5 %collective-permute-start.13 = (bf16[192,384]{1,0:T(8,128)(2,1)S(1)}, bf16[192,384]{1,0:T(8,128)(2,1)S(1)}, u32[]{:S(2)}, u32[]{:S(2)}) collective-permute-start(bf16[192,384]{1,0:T(8,128)(2,1)S(1)} %shard_map.85.refs_0_), channel_id=1, source_target_pairs={{0,8},{2,10},{4,12},{6,14},{8,0},{10,2},{12,4},{14,6},{16,24},{18,... | collective-permute-start | bytes 442376 | tf_op jit(solution)/shard_map/ppermute | solution.py:360
  44.6 7.2 %collective-permute-done.12.refs_2_ = bf16[192,384]{1,0:T(8,128)(2,1)S(1)} collective-permute-done((bf16[192,384]{1,0:T(8,128)(2,1)S(1)}, bf16[192,384]{1,0:T(8,128)(2,1)S(1)}, u32[]{:S(2)}, u32[]{:S(2)}) %collective-permute-start.12) | collective-permute-done | bytes 147488 | tf_op jit(solution)/shard_map/ppermute | solution.py:360
  52.1 1.5 %collective-permute-done.17.refs_5_ = bf16[96,1536]{1,0:T(8,128)(2,1)S(1)} collective-permute-done((bf16[96,1536]{1,0:T(8,128)(2,1)S(1)}, bf16[96,1536]{1,0:T(8,128)(2,1)S(1)}, u32[]{:S(2)}, u32[]{:S(2)}) %collective-permute-start.17) | collective-permute-done | bytes 294944 | tf_op jit(solution)/shard_map/ppermute | solution.py:360
  53.8 0.7 shard_map.87.partial
  54.5 3.8 %collective-permute-done.18.part = bf16[192,384]{1,0:T(8,128)(2,1)S(1)} collective-permute-done((bf16[192,384]{1,0:T(8,128)(2,1)S(1)}, bf16[192,384]{1,0:T(8,128)(2,1)S(1)}, u32[]{:S(2)}, u32[]{:S(2)}) %collective-permute-start.18) | collective-permute-done | bytes 147488 | tf_op jit(solution)/shard_map/ppermute | solution.py:360
  59.0 2.0 %collective-permute-start.20 = (bf16[48,768]{1,0:T(8,128)(2,1)S(1)}, bf16[48,768]{1,0:T(8,128)(2,1)S(1)}, u32[]{:S(2)}, u32[]{:S(2)}) collective-permute-start(bf16[48,768]{1,0:T(8,128)(2,1)S(1)} %get-tuple-element.63), channel_id=1, source_target_pairs={{0,16},{2,18},{4,20},{6,22},{8,24},{10,26},{12,28},{14,30},{16,0},... | collective-permute-start | bytes 221192 | tf_op jit(solution)/shard_map/ppermute | solution.py:360
  61.0 2.1 %collective-permute-start.21 = (bf16[48,768]{1,0:T(8,128)(2,1)S(1)}, bf16[48,768]{1,0:T(8,128)(2,1)S(1)}, u32[]{:S(2)}, u32[]{:S(2)}) collective-permute-start(bf16[48,768]{1,0:T(8,128)(2,1)S(1)} %get-tuple-element.64), channel_id=1, source_target_pairs={{0,24},{2,26},{4,28},{6,30},{8,16},{10,18},{12,20},{14,22},{16,8},... | collective-permute-start | bytes 221192 | tf_op jit(solution)/shard_map/ppermute | solution.py:360
  63.1 1.5 %collective-permute-start.22 = (bf16[48,768]{1,0:T(8,128)(2,1)S(1)}, bf16[48,768]{1,0:T(8,128)(2,1)S(1)}, u32[]{:S(2)}, u32[]{:S(2)}) collective-permute-start(bf16[48,768]{1,0:T(8,128)(2,1)S(1)} %get-tuple-element.61.refs_0_), channel_id=1, source_target_pairs={{0,1},{1,0},{2,3},{3,2},{4,5},{5,4},{6,7},{7,6},{8,9},{9,8},{10,11... | collective-permute-start | bytes 221192 | tf_op jit(solution)/shard_map/ppermute | solution.py:394
  64.6 0.5 collective-permute-start.23
  65.1 2.4 %collective-permute-done.20.refs_2_ = bf16[48,768]{1,0:T(8,128)(2,1)S(1)} collective-permute-done((bf16[48,768]{1,0:T(8,128)(2,1)S(1)}, bf16[48,768]{1,0:T(8,128)(2,1)S(1)}, u32[]{:S(2)}, u32[]{:S(2)}) %collective-permute-start.20) | collective-permute-done | bytes 73760 | tf_op jit(solution)/shard_map/ppermute | solution.py:360
  67.6 1.5 %collective-permute-start.24 = (bf16[48,768]{1,0:T(8,128)(2,1)S(1)}, bf16[48,768]{1,0:T(8,128)(2,1)S(1)}, u32[]{:S(2)}, u32[]{:S(2)}) collective-permute-start(bf16[48,768]{1,0:T(8,128)(2,1)S(1)} %collective-permute-done.20.refs_2_), channel_id=1, source_target_pairs={{0,1},{1,0},{2,3},{3,2},{4,5},{5,4},{6,7},{7,6},{8,9},{9,8},{10,11... | collective-permute-start | bytes 221192 | tf_op jit(solution)/shard_map/ppermute | solution.py:394
  69.1 0.5 collective-permute-start.25
  69.7 2.3 %collective-permute-done.24.refs_6_ = bf16[48,768]{1,0:T(8,128)(2,1)S(1)} collective-permute-done((bf16[48,768]{1,0:T(8,128)(2,1)S(1)}, bf16[48,768]{1,0:T(8,128)(2,1)S(1)}, u32[]{:S(2)}, u32[]{:S(2)}) %collective-permute-start.24) | collective-permute-done | bytes 73760 | tf_op jit(solution)/shard_map/ppermute | solution.py:394
  71.9 1.5 %collective-permute-done.25.refs_7_ = bf16[48,768]{1,0:T(8,128)(2,1)S(1)} collective-permute-done((bf16[48,768]{1,0:T(8,128)(2,1)S(1)}, bf16[48,768]{1,0:T(8,128)(2,1)S(1)}, u32[]{:S(2)}, u32[]{:S(2)}) %collective-permute-start.25) | collective-permute-done | bytes 73760 | tf_op jit(solution)/shard_map/ppermute | solution.py:394
  73.5 0.8 %shard_map.89 = bf16[48,1536]{1,0:T(8,128)(2,1)} custom-call(bf16[48,768]{1,0:T(8,128)(2,1)S(1)} %get-tuple-element.61.refs_0_, bf16[48,768]{1,0:T(8,128)(2,1)S(1)} %collective-permute-done.19.refs_1_, bf16[48,768]{1,0:T(8,128)(2,1)S(1)} %collective-permute-done.20.refs_2_, bf16[48,768]{1,0:T(8,128)(2,1)S(1)} %collective-permute-done.21.refs_3_, ...), custom_call_target="tpu_custom_call" | custom-call | flops 221184 | bytes 294912 | tf_op jit(solution)/shard_map/pallas_call | solution.py:340
  (47 shorter events, 2.6 us)
Async XLA Ops:
  10.8 13.7 %collective-permute-start.4 = (bf16[96,1536]{1,0:T(8,128)(2,1)}, bf16[96,1536]{1,0:T(8,128)(2,1)S(1)}, u32[]{:S(2)}, u32[]{:S(2)}) collective-permute-start(bf16[96,1536]{1,0:T(8,128)(2,1)} %get-tuple-element.41), channel_id=1, source_target_pairs={{0,4},{2,6},{4,0},{6,2},{8,12},{10,14},{12,8},{14,10},{16,20},{18,... | collective-permute-start | bytes 884744 | tf_op jit(solution)/shard_map/ppermute | solution.py:360
  13.8 6.4 %collective-permute-start = (bf16[2,48,384]{2,1,0:T(8,128)(2,1)}, bf16[2,48,384]{2,1,0:T(8,128)(2,1)S(1)}, u32[]{:S(2)}, u32[]{:S(2)}) collective-permute-start(bf16[2,48,384]{2,1,0:T(8,128)(2,1)} %get-tuple-element.36), channel_id=1, source_target_pairs={{0,8},{2,10},{4,12},{6,14},{8,0},{10,2},{12,4},{14,6},{16,24},{18,... | collective-permute-start | bytes 221192 | tf_op jit(solution)/shard_map/ppermute | solution.py:360
  15.4 7.7 %collective-permute-start.1 = (bf16[2,48,384]{2,1,0:T(8,128)(2,1)}, bf16[2,48,384]{2,1,0:T(8,128)(2,1)S(1)}, u32[]{:S(2)}, u32[]{:S(2)}) collective-permute-start(bf16[2,48,384]{2,1,0:T(8,128)(2,1)} %get-tuple-element.37), channel_id=1, source_target_pairs={{0,16},{2,18},{4,20},{6,22},{8,24},{10,26},{12,28},{14,30},{16,0},... | collective-permute-start | bytes 221192 | tf_op jit(solution)/shard_map/ppermute | solution.py:360
  18.0 6.5 %collective-permute-start.2 = (bf16[2,48,384]{2,1,0:T(8,128)(2,1)}, bf16[2,48,384]{2,1,0:T(8,128)(2,1)S(1)}, u32[]{:S(2)}, u32[]{:S(2)}) collective-permute-start(bf16[2,48,384]{2,1,0:T(8,128)(2,1)} %get-tuple-element.38), channel_id=1, source_target_pairs={{0,24},{2,26},{4,28},{6,30},{8,16},{10,18},{12,20},{14,22},{16,8},... | collective-permute-start | bytes 221192 | tf_op jit(solution)/shard_map/ppermute | solution.py:360
  18.2 8.8 %copy-start.6 = (bf16[48,384]{1,0:T(8,128)(2,1)S(1)}, bf16[48,384]{1,0:T(8,128)(2,1)}, u32[]{:S(2)}) copy-start(bf16[48,384]{1,0:T(8,128)(2,1)} %get-tuple-element.51) | copy-start | bytes 110596
  18.2 16.2 %copy-start = (bf16[1536,192]{0,1:T(8,128)(2,1)S(1)}, bf16[1536,192]{0,1:T(8,128)(2,1)}, u32[]{:S(2)}) copy-start(bf16[1536,192]{0,1:T(8,128)(2,1)} %param.13) | copy-start | bytes 1769476
  18.2 18.0 %copy-start.5 = (bf16[48,384]{1,0:T(8,128)(2,1)S(1)}, bf16[48,384]{1,0:T(8,128)(2,1)}, u32[]{:S(2)}) copy-start(bf16[48,384]{1,0:T(8,128)(2,1)} %get-tuple-element.55) | copy-start | bytes 110596
  18.2 21.9 %copy-start.2 = (bf16[48,384]{1,0:T(8,128)(2,1)S(1)}, bf16[48,384]{1,0:T(8,128)(2,1)}, u32[]{:S(2)}) copy-start(bf16[48,384]{1,0:T(8,128)(2,1)} %get-tuple-element.54.refs_6_) | copy-start | bytes 110596
  18.2 6.3 %collective-permute-start.3 = (bf16[2,48,384]{2,1,0:T(8,128)(2,1)}, bf16[2,48,384]{2,1,0:T(8,128)(2,1)S(1)}, u32[]{:S(2)}, u32[]{:S(2)}) collective-permute-start(bf16[2,48,384]{2,1,0:T(8,128)(2,1)} %get-tuple-element.35.refs_0_), channel_id=1, source_target_pairs={{0,4},{2,6},{4,0},{6,2},{8,12},{10,14},{12,8},{14,10},{16,20},{18,... | collective-permute-start | bytes 221192 | tf_op jit(solution)/shard_map/ppermute | solution.py:360
  24.5 8.3 %collective-permute-start.5 = (bf16[4,2,48,384]{3,2,1,0:T(8,128)(2,1)S(1)}, bf16[4,2,48,384]{3,2,1,0:T(8,128)(2,1)S(1)}, u32[]{:S(2)}, u32[]{:S(2)}) collective-permute-start(bf16[4,2,48,384]{3,2,1,0:T(8,128)(2,1)S(1)} %get-tuple-element.44.refs_0_), channel_id=1, source_target_pairs={{0,2},{2,0},{4,6},{6,4},{8,10},{10,8},{12,14},{14,12},{16,18},{18,... | collective-permute-start | bytes 884744 | tf_op jit(solution)/shard_map/ppermute | solution.py:360
  24.6 8.2 %collective-permute-start.6 = (bf16[3,2,48,384]{3,2,1,0:T(8,128)(2,1)S(1)}, bf16[3,2,48,384]{3,2,1,0:T(8,128)(2,1)S(1)}, u32[]{:S(2)}, u32[]{:S(2)}) collective-permute-start(bf16[3,2,48,384]{3,2,1,0:T(8,128)(2,1)S(1)} %get-tuple-element.45), channel_id=1, source_target_pairs={{0,4},{2,6},{4,0},{6,2},{8,12},{10,14},{12,8},{14,10},{16,20},{18,... | collective-permute-start | bytes 663560 | tf_op jit(solution)/shard_map/ppermute | solution.py:360
  25.2 5.3 %collective-permute-start.7 = (bf16[48,384]{1,0:T(8,128)(2,1)S(1)}, bf16[48,384]{1,0:T(8,128)(2,1)S(1)}, u32[]{:S(2)}, u32[]{:S(2)}) collective-permute-start(bf16[48,384]{1,0:T(8,128)(2,1)S(1)} %copy-done.7), channel_id=1, source_target_pairs={{0,16},{2,18},{4,20},{6,22},{8,24},{10,26},{12,28},{14,30},{16,0},... | collective-permute-start | bytes 110600 | tf_op jit(solution)/shard_map/ppermute | solution.py:360
  27.0 5.8 %collective-permute-start.8 = (bf16[48,384]{1,0:T(8,128)(2,1)S(1)}, bf16[48,384]{1,0:T(8,128)(2,1)S(1)}, u32[]{:S(2)}, u32[]{:S(2)}) collective-permute-start(bf16[48,384]{1,0:T(8,128)(2,1)S(1)} %copy-done.6), channel_id=1, source_target_pairs={{0,24},{2,26},{4,28},{6,30},{8,16},{10,18},{12,20},{14,22},{16,8},... | collective-permute-start | bytes 110600 | tf_op jit(solution)/shard_map/ppermute | solution.py:360
  32.8 1.6 %collective-permute-start.10 = (bf16[3,2,48,384]{3,2,1,0:T(8,128)(2,1)S(1)}, bf16[3,2,48,384]{3,2,1,0:T(8,128)(2,1)S(1)}, u32[]{:S(2)}, u32[]{:S(2)}) collective-permute-start(bf16[3,2,48,384]{3,2,1,0:T(8,128)(2,1)S(1)} %collective-permute-done.6.refs_3_), channel_id=1, source_target_pairs={{0,2},{2,0},{4,6},{6,4},{8,10},{10,8},{12,14},{14,12},{16,18},{18,... | collective-permute-start | bytes 663560 | tf_op jit(solution)/shard_map/ppermute | solution.py:360
  32.8 1.6 %collective-permute-start.9 = (bf16[2,48,384]{2,1,0:T(8,128)(2,1)S(1)}, bf16[2,48,384]{2,1,0:T(8,128)(2,1)S(1)}, u32[]{:S(2)}, u32[]{:S(2)}) collective-permute-start(bf16[2,48,384]{2,1,0:T(8,128)(2,1)S(1)} %collective-permute-done.3.refs_2_), channel_id=1, source_target_pairs={{0,2},{2,0},{4,6},{6,4},{8,10},{10,8},{12,14},{14,12},{16,18},{18,... | collective-permute-start | bytes 221192 | tf_op jit(solution)/shard_map/ppermute | solution.py:360
  34.4 17.5 %collective-permute-start.15 = (bf16[192,1536]{1,0:T(8,128)(2,1)S(1)}, bf16[192,1536]{1,0:T(8,128)(2,1)S(1)}, u32[]{:S(2)}, u32[]{:S(2)}) collective-permute-start(bf16[192,1536]{1,0:T(8,128)(2,1)S(1)} %bitcast.3), channel_id=1, source_target_pairs={{0,2},{2,0},{4,6},{6,4},{8,10},{10,8},{12,14},{14,12},{16,18},{18,... | collective-permute-start | bytes 1769480 | tf_op jit(solution)/shard_map/ppermute | solution.py:360
  34.6 17.3 %collective-permute-start.14 = (bf16[96,1536]{1,0:T(8,128)(2,1)S(1)}, bf16[96,1536]{1,0:T(8,128)(2,1)S(1)}, u32[]{:S(2)}, u32[]{:S(2)}) collective-permute-start(bf16[96,1536]{1,0:T(8,128)(2,1)S(1)} %slice.3), channel_id=1, source_target_pairs={{0,4},{2,6},{4,0},{6,2},{8,12},{10,14},{12,8},{14,10},{16,20},{18,... | collective-permute-start | bytes 884744 | tf_op jit(solution)/shard_map/ppermute | solution.py:360
  36.2 15.7 %collective-permute-start.16 = (bf16[96,1536]{1,0:T(8,128)(2,1)S(1)}, bf16[96,1536]{1,0:T(8,128)(2,1)S(1)}, u32[]{:S(2)}, u32[]{:S(2)}) collective-permute-start(bf16[96,1536]{1,0:T(8,128)(2,1)S(1)} %collective-permute-done.4.refs_2_), channel_id=1, source_target_pairs={{0,2},{2,0},{4,6},{6,4},{8,10},{10,8},{12,14},{14,12},{16,18},{18,... | collective-permute-start | bytes 884744 | tf_op jit(solution)/shard_map/ppermute | solution.py:360
  36.2 4.0 %collective-permute-start.11 = (bf16[48,384]{1,0:T(8,128)(2,1)S(1)}, bf16[48,384]{1,0:T(8,128)(2,1)S(1)}, u32[]{:S(2)}, u32[]{:S(2)}) collective-permute-start(bf16[48,384]{1,0:T(8,128)(2,1)S(1)} %copy-done.5), channel_id=1, source_target_pairs={{0,8},{2,10},{4,12},{6,14},{8,0},{10,2},{12,4},{14,6},{16,24},{18,... | collective-permute-start | bytes 110600 | tf_op jit(solution)/shard_map/ppermute | solution.py:360
  42.5 9.4 %collective-permute-start.12 = (bf16[192,384]{1,0:T(8,128)(2,1)S(1)}, bf16[192,384]{1,0:T(8,128)(2,1)S(1)}, u32[]{:S(2)}, u32[]{:S(2)}) collective-permute-start(bf16[192,384]{1,0:T(8,128)(2,1)S(1)} %shard_map.85.refs_0_), channel_id=1, source_target_pairs={{0,16},{2,18},{4,20},{6,22},{8,24},{10,26},{12,28},{14,30},{16,0},... | collective-permute-start | bytes 442376 | tf_op jit(solution)/shard_map/ppermute | solution.py:360
  43.2 8.7 %collective-permute-start.13 = (bf16[192,384]{1,0:T(8,128)(2,1)S(1)}, bf16[192,384]{1,0:T(8,128)(2,1)S(1)}, u32[]{:S(2)}, u32[]{:S(2)}) collective-permute-start(bf16[192,384]{1,0:T(8,128)(2,1)S(1)} %shard_map.85.refs_0_), channel_id=1, source_target_pairs={{0,8},{2,10},{4,12},{6,14},{8,0},{10,2},{12,4},{14,6},{16,24},{18,... | collective-permute-start | bytes 442376 | tf_op jit(solution)/shard_map/ppermute | solution.py:360
  51.9 1.6 %collective-permute-start.17 = (bf16[96,1536]{1,0:T(8,128)(2,1)S(1)}, bf16[96,1536]{1,0:T(8,128)(2,1)S(1)}, u32[]{:S(2)}, u32[]{:S(2)}) collective-permute-start(bf16[96,1536]{1,0:T(8,128)(2,1)S(1)} %collective-permute-done.14.refs_3_), channel_id=1, source_target_pairs={{0,2},{2,0},{4,6},{6,4},{8,10},{10,8},{12,14},{14,12},{16,18},{18,... | collective-permute-start | bytes 884744 | tf_op jit(solution)/shard_map/ppermute | solution.py:360
  52.0 6.3 %collective-permute-start.18 = (bf16[192,384]{1,0:T(8,128)(2,1)S(1)}, bf16[192,384]{1,0:T(8,128)(2,1)S(1)}, u32[]{:S(2)}, u32[]{:S(2)}) collective-permute-start(bf16[192,384]{1,0:T(8,128)(2,1)S(1)} %collective-permute-done.12.refs_2_), channel_id=1, source_target_pairs={{0,8},{2,10},{4,12},{6,14},{8,0},{10,2},{12,4},{14,6},{16,24},{18,... | collective-permute-start | bytes 442376 | tf_op jit(solution)/shard_map/ppermute | solution.py:360
  53.7 15.9 %copy-start.3 = (f32[1536]{0:T(1024)S(1)}, f32[1536]{0:T(1024)}, u32[]{:S(2)}) copy-start(f32[1536]{0:T(1024)} %param.14) | copy-start | bytes 18436
  53.7 15.9 %copy-start.4 = (f32[1536]{0:T(1024)S(1)}, f32[1536]{0:T(1024)}, u32[]{:S(2)}) copy-start(f32[1536]{0:T(1024)} %param.15) | copy-start | bytes 18436
  58.6 6.0 %collective-permute-start.19 = (bf16[48,768]{1,0:T(8,128)(2,1)S(1)}, bf16[48,768]{1,0:T(8,128)(2,1)S(1)}, u32[]{:S(2)}, u32[]{:S(2)}) collective-permute-start(bf16[48,768]{1,0:T(8,128)(2,1)S(1)} %get-tuple-element.62), channel_id=1, source_target_pairs={{0,8},{2,10},{4,12},{6,14},{8,0},{10,2},{12,4},{14,6},{16,24},{18,... | collective-permute-start | bytes 221192 | tf_op jit(solution)/shard_map/ppermute | solution.py:360
  59.0 8.6 %collective-permute-start.20 = (bf16[48,768]{1,0:T(8,128)(2,1)S(1)}, bf16[48,768]{1,0:T(8,128)(2,1)S(1)}, u32[]{:S(2)}, u32[]{:S(2)}) collective-permute-start(bf16[48,768]{1,0:T(8,128)(2,1)S(1)} %get-tuple-element.63), channel_id=1, source_target_pairs={{0,16},{2,18},{4,20},{6,22},{8,24},{10,26},{12,28},{14,30},{16,0},... | collective-permute-start | bytes 221192 | tf_op jit(solution)/shard_map/ppermute | solution.py:360
  61.0 8.1 %collective-permute-start.21 = (bf16[48,768]{1,0:T(8,128)(2,1)S(1)}, bf16[48,768]{1,0:T(8,128)(2,1)S(1)}, u32[]{:S(2)}, u32[]{:S(2)}) collective-permute-start(bf16[48,768]{1,0:T(8,128)(2,1)S(1)} %get-tuple-element.64), channel_id=1, source_target_pairs={{0,24},{2,26},{4,28},{6,30},{8,16},{10,18},{12,20},{14,22},{16,8},... | collective-permute-start | bytes 221192 | tf_op jit(solution)/shard_map/ppermute | solution.py:360
  63.1 6.5 %collective-permute-start.22 = (bf16[48,768]{1,0:T(8,128)(2,1)S(1)}, bf16[48,768]{1,0:T(8,128)(2,1)S(1)}, u32[]{:S(2)}, u32[]{:S(2)}) collective-permute-start(bf16[48,768]{1,0:T(8,128)(2,1)S(1)} %get-tuple-element.61.refs_0_), channel_id=1, source_target_pairs={{0,1},{1,0},{2,3},{3,2},{4,5},{5,4},{6,7},{7,6},{8,9},{9,8},{10,11... | collective-permute-start | bytes 221192 | tf_op jit(solution)/shard_map/ppermute | solution.py:394
  64.6 5.0 %collective-permute-start.23 = (bf16[48,768]{1,0:T(8,128)(2,1)S(1)}, bf16[48,768]{1,0:T(8,128)(2,1)S(1)}, u32[]{:S(2)}, u32[]{:S(2)}) collective-permute-start(bf16[48,768]{1,0:T(8,128)(2,1)S(1)} %collective-permute-done.19.refs_1_), channel_id=1, source_target_pairs={{0,1},{1,0},{2,3},{3,2},{4,5},{5,4},{6,7},{7,6},{8,9},{9,8},{10,11... | collective-permute-start | bytes 221192 | tf_op jit(solution)/shard_map/ppermute | solution.py:394
  67.6 4.4 %collective-permute-start.24 = (bf16[48,768]{1,0:T(8,128)(2,1)S(1)}, bf16[48,768]{1,0:T(8,128)(2,1)S(1)}, u32[]{:S(2)}, u32[]{:S(2)}) collective-permute-start(bf16[48,768]{1,0:T(8,128)(2,1)S(1)} %collective-permute-done.20.refs_2_), channel_id=1, source_target_pairs={{0,1},{1,0},{2,3},{3,2},{4,5},{5,4},{6,7},{7,6},{8,9},{9,8},{10,11... | collective-permute-start | bytes 221192 | tf_op jit(solution)/shard_map/ppermute | solution.py:394
  69.1 4.4 %collective-permute-start.25 = (bf16[48,768]{1,0:T(8,128)(2,1)S(1)}, bf16[48,768]{1,0:T(8,128)(2,1)S(1)}, u32[]{:S(2)}, u32[]{:S(2)}) collective-permute-start(bf16[48,768]{1,0:T(8,128)(2,1)S(1)} %collective-permute-done.21.refs_3_), channel_id=1, source_target_pairs={{0,1},{1,0},{2,3},{3,2},{4,5},{5,4},{6,7},{7,6},{8,9},{9,8},{10,11... | collective-permute-start | bytes 221192 | tf_op jit(solution)/shard_map/ppermute | solution.py:394
  (2 other events, 13.2 us)

commit v6 on v5

--- a/solution.py
+++ b/solution.py
@@ -67,8 +67,8 @@
     return me // SPREAD, lax.rem(me, SPREAD)
 
 
-def pack_kernel(queries_hbm, codes_hbm, exponents_hbm, weight_hbm, *rest):
-    outs, early, (codes, queries, exponents, held, sems) = rest[:-6], rest[-6], rest[-5:]
+def pack_kernel(queries_hbm, codes_hbm, exponents_hbm, *rest):
+    outs, (codes, queries, exponents, held, sems) = rest[:-5], rest[-5:]
     groups, kinds, rows, width = held.shape
     group, _ = place()
     per = width // HD
@@ -76,7 +76,6 @@
         pltpu.make_async_copy(exponents_hbm, exponents, sems.at[0]),
         pltpu.make_async_copy(codes_hbm, codes, sems.at[1]),
         pltpu.make_async_copy(queries_hbm, queries, sems.at[2]),
-        pltpu.make_async_copy(weight_hbm.at[0 : early.shape[0]], early, sems.at[3]),
     ]
     for copy in copies:
         copy.start()
@@ -99,10 +98,9 @@
         target = jnp.bitwise_xor(group, turn)
         outs[turn][...] = held[target, 0 : kinds - 1]
         outs[groups + turn][...] = held[target, kinds - 1]
-    copies[3].wait()
-
-
-def pack(groups, queries, codes, exponents, weight):
+
+
+def pack(groups, queries, codes, exponents):
     rows, width = queries.shape
     kinds = codes.shape[0]
     share = width // groups
@@ -111,21 +109,20 @@
     outs = pl.pallas_call(
         pack_kernel,
         out_shape=[jax.ShapeDtypeStruct((kinds, rows, share), bf16)] * groups
-        + [jax.ShapeDtypeStruct((rows, share), bf16)] * groups
-        + [jax.ShapeDtypeStruct((weight.shape[0] // 2, weight.shape[1]), bf16)],
-        in_specs=[HBM] * 4,
-        out_specs=[VMEM] * (2 * groups) + [HBM],
+        + [jax.ShapeDtypeStruct((rows, share), bf16)] * groups,
+        in_specs=[HBM] * 3,
+        out_specs=[VMEM] * (2 * groups),
         scratch_shapes=[
             pltpu.VMEM(codes.shape, jnp.int32),
             pltpu.VMEM(queries.shape, bf16),
             pltpu.VMEM(exponents.shape, jnp.int32),
             pltpu.VMEM((groups, kinds + 1, rows, share), bf16),
-            pltpu.SemaphoreType.DMA((4,)),
+            pltpu.SemaphoreType.DMA((3,)),
         ],
         compiler_params=pltpu.CompilerParams(vmem_limit_bytes=PACK_LIMIT),
         cost_estimate=pl.CostEstimate(flops=2 * codes.size, bytes_accessed=6 * codes.size, transcendentals=0),
-    )(queries, codes, exponents, weight)
-    return outs[:groups], outs[groups : 2 * groups], outs[-1]
+    )(queries, codes, exponents)
+    return outs[:groups], outs[groups:]
 
 
 def pick_kernel(text_hbm, stale_hbm, text, stale, sems):
@@ -192,7 +189,7 @@
 
 def attend_kernel(groups, *refs):
     (every, near, own_far, some_far, own_corner, some_corner), refs = refs[:6], refs[6:]
-    asked, (text, stale, out, query, residual) = refs[:groups], refs[groups:]
+    asked, (text, stale, out, most, last, query, residual) = refs[:groups], refs[groups:]
     group, spot = place()
     rows, width = asked[0].shape
     for turn in range(groups):
@@ -209,7 +206,12 @@
             residual[:, pl.ds(aligned(token, rows), rows), :] = part
     for head in range(width // HD):
         cols = slice(head * HD, (head + 1) * HD)
-        out[:, cols] = head_output(query[:, cols], text, stale, residual, cols)
+        value = head_output(query[:, cols], text, stale, residual, cols)
+        out[:, cols] = value
+        if head < width // HD - 1:
+            most[:, cols] = value
+        else:
+            last[...] = value
 
 
 def attend_cost(heads, tokens, texts, keys):
@@ -230,9 +232,9 @@
 
     return pl.pallas_call(
         functools.partial(attend_kernel, groups),
-        out_shape=jax.ShapeDtypeStruct((tokens, width), jnp.bfloat16),
+        out_shape=[jax.ShapeDtypeStruct((tokens, size), jnp.bfloat16) for size in (width, width - HD, HD)],
         in_specs=[VMEM] * (len(pieces) + groups + 2),
-        out_specs=VMEM,
+        out_specs=[VMEM] * 3,
         scratch_shapes=[pltpu.VMEM((tokens, width), jnp.bfloat16), pltpu.VMEM((2, keys, width), jnp.bfloat16)],
         compiler_params=pltpu.CompilerParams(vmem_limit_bytes=SMALL),
         cost_estimate=attend_cost(heads, tokens, texts, keys),
@@ -240,20 +242,15 @@
 
 
 def order_kernel(*refs):
-    wholes, halves, out = refs[:2], refs[2:-1], refs[-1]
+    pieces, out = refs[:-1], refs[-1]
     _, spot = place()
     span = out.shape[0] // SPREAD
-    for twist, whole in enumerate(wholes):
-        start = jnp.bitwise_xor(spot, twist) * span
-        out[pl.ds(pl.multiple_of(start, 16), span), :] = whole[...]
-    for index, piece in enumerate(halves):
-        start = jnp.bitwise_xor(spot, 2 + index // 2) * span + index % 2 * (span // 2)
-        out[pl.ds(pl.multiple_of(start, 16), span // 2), :] = piece[...]
-
-
-def order(weight, near, halves):
-    pieces = [weight, near, *halves]
-    span, depth = weight.shape
+    for twist, piece in enumerate(pieces):
+        out[pl.ds(aligned(jnp.bitwise_xor(spot, twist), span), span), :] = piece[...]
+
+
+def order(pieces):
+    span, depth = pieces[0].shape
     shape = (SPREAD * span, depth)
     return pl.pallas_call(
         order_kernel,
@@ -265,24 +262,23 @@
     )(*pieces)
 
 
-def term_of(part, weight, turn):
+def term_of(part, weight, turn, skip, width):
     group, _ = place()
-    width = part.shape[1]
-    columns = pl.ds(aligned(jnp.bitwise_xor(group, turn), width), width)
+    start = jnp.bitwise_xor(group, turn) * width + skip
+    columns = pl.ds(pl.multiple_of(start, HD), part.shape[1])
     return lax.dot_general(part[...], weight[:, columns], NT, preferred_element_type=jnp.float32)
 
 
-def begin_kernel(*refs):
-    parts, (weight, out) = refs[:-2], refs[-2:]
-    total = term_of(parts[0], weight, 0)
-    for turn in range(1, len(parts)):
-        total += term_of(parts[turn], weight, turn)
-    out[...] = total
+def begin_kernel(full, beside, across_most, across_last, weight, out):
+    width = full.shape[1]
+    total = term_of(full, weight, 0, 0, width) + term_of(beside, weight, 1, 0, width)
+    total += term_of(across_most, weight, 2, 0, width)
+    out[...] = total + term_of(across_last, weight, 2, width - HD, width)
 
 
 def begin(parts, weight):
-    tokens, width = parts[0].shape
-    columns = weight.shape[0]
+    tokens = parts[0].shape[0]
+    columns, depth = weight.shape
     return pl.pallas_call(
         begin_kernel,
         out_shape=jax.ShapeDtypeStruct((tokens, columns), jnp.float32),
@@ -290,62 +286,82 @@
         out_specs=VMEM,
         compiler_params=pltpu.CompilerParams(vmem_limit_bytes=SMALL),
         cost_estimate=pl.CostEstimate(
-            flops=2 * tokens * columns * width * len(parts), bytes_accessed=4 * tokens * columns, transcendentals=0
+            flops=2 * tokens * columns * depth, bytes_accessed=4 * tokens * columns, transcendentals=0
         ),
     )(*parts, weight)
 
 
-def close_kernel(partial, part, weight, *rest):
+def close_kernel(partial, most, last, weight, *rest):
     outs, total = rest[:-1], rest[-1]
     group, _ = place()
     rows = outs[0].shape[0]
-    total[...] = (partial[...] + term_of(part, weight, len(outs) - 1)).astype(jnp.bfloat16)
+    width = most.shape[1] + last.shape[1]
+    added = partial[...] + term_of(most, weight, 3, 0, width) + term_of(last, weight, 3, width - HD, width)
+    total[...] = added.astype(jnp.bfloat16)
     for turn, out in enumerate(outs):
         out[...] = total[pl.ds(aligned(jnp.bitwise_xor(group, turn), rows), rows), :]
 
 
-def close(groups, partial, part, weight):
+def close(groups, partial, parts, weight):
     tokens, columns = partial.shape
     return pl.pallas_call(
         close_kernel,
         out_shape=[jax.ShapeDtypeStruct((tokens // groups, columns), jnp.bfloat16)] * groups,
-        in_specs=[VMEM] * 3,
+        in_specs=[VMEM] * 4,
         out_specs=[VMEM] * groups,
         scratch_shapes=[pltpu.VMEM((tokens, columns), jnp.bfloat16)],
         compiler_params=pltpu.CompilerParams(vmem_limit_bytes=SMALL),
         cost_estimate=pl.CostEstimate(
-            flops=2 * tokens * columns * part.shape[1], bytes_accessed=8 * tokens * columns, transcendentals=0
+            flops=tokens * weight.size, bytes_accessed=8 * tokens * columns, transcendentals=0
         ),
-    )(partial, part, weight)
-
-
-def finish_kernel(groups, *refs):
-    mine, other, (bias, gate, out, held) = refs[:groups], refs[groups : 2 * groups], refs[2 * groups :]
+    )(partial, *parts, weight)
+
+
+def divide_kernel(*refs):
+    parts, (keep, send, held) = refs[:-3], refs[-3:]
     group, _ = place()
-    columns = mine[0].shape[1]
-    blocks = groups // 2
-    first = lax.axis_index("head") * blocks
-    for turn in range(groups):
-        origin = jnp.bitwise_xor(group, turn)
-        held[origin] = mine[turn][...].astype(jnp.float32) + other[turn][...].astype(jnp.float32)
+    half = lax.axis_index("head")
+    blocks = keep.shape[0]
+    for turn, part in enumerate(parts):
+        held[jnp.bitwise_xor(group, turn)] = part[...]
+    for block in range(blocks):
+        keep[block] = held[half * blocks + block]
+        send[block] = held[(1 - half) * blocks + block]
+
+
+def divide(parts):
+    groups = len(parts)
+    shape = jax.ShapeDtypeStruct((groups // 2, *parts[0].shape), jnp.bfloat16)
+    return pl.pallas_call(
+        divide_kernel,
+        out_shape=[shape] * 2,
+        in_specs=[VMEM] * groups,
+        out_specs=[VMEM] * 2,
+        scratch_shapes=[pltpu.VMEM((groups, *parts[0].shape), jnp.bfloat16)],
+        compiler_params=pltpu.CompilerParams(vmem_limit_bytes=SMALL),
+        cost_estimate=pl.CostEstimate(flops=0, bytes_accessed=4 * groups * parts[0].size, transcendentals=0),
+    )(*parts)
+
+
+def finish_kernel(kept, arrived, bias, gate, out):
+    blocks, _, columns = kept.shape
     for block in range(blocks):
         cols = slice(block * columns, (block + 1) * columns)
-        out[:, cols] = (gate[:, cols] * (held[first + block] + bias[:, cols])).astype(jnp.bfloat16)
-
-
-def finish(mine, other, bias, gate):
-    groups = len(mine)
-    rows, columns = mine[0].shape
-    width = columns * groups // 2
-    return pl.pallas_call(
-        functools.partial(finish_kernel, groups),
+        total = kept[block].astype(jnp.float32) + arrived[block].astype(jnp.float32)
+        out[:, cols] = (gate[:, cols] * (total + bias[:, cols])).astype(jnp.bfloat16)
+
+
+def finish(kept, arrived, bias, gate):
+    blocks, rows, columns = kept.shape
+    width = blocks * columns
+    return pl.pallas_call(
+        finish_kernel,
         out_shape=jax.ShapeDtypeStruct((rows, width), jnp.bfloat16),
-        in_specs=[VMEM] * (2 * groups + 2),
+        in_specs=[VMEM] * 4,
         out_specs=VMEM,
-        scratch_shapes=[pltpu.VMEM((groups, rows, columns), jnp.float32)],
         compiler_params=pltpu.CompilerParams(vmem_limit_bytes=SMALL),
         cost_estimate=pl.CostEstimate(flops=3 * rows * width, bytes_accessed=4 * rows * width, transcendentals=0),
-    )(*mine, *other, bias.reshape(1, width), gate.reshape(1, width))
+    )(kept, arrived, bias.reshape(1, width), gate.reshape(1, width))
 
 
 def after(value, *others):
@@ -360,39 +376,41 @@
         return lax.ppermute(value, "patch", [(p, p ^ twist) for p in range(size)])
 
     def along(values):
-        moved = {turn: swap(values[turn], turn * SPREAD) for turn in (2, 1, 3)}
+        moved = {turn: swap(values[turn], turn * SPREAD) for turn in (3, 2, 1)}
         return [moved[turn] for turn in range(1, groups)]
 
     weight = out_weight.T
-    half = weight.shape[0] // 2
-    residuals, queries, early = pack(groups, queries, codes, exponents, weight)
+    weight_far = swap(weight, 2)
+    residuals, queries = pack(groups, queries, codes, exponents)
     text, stale = pick(groups, text_kv, stale_kv)
 
     own = residuals[0]
     arrived = along(residuals)
-    own_far, early = swap(own, 2), swap(early, 2)
+    own_far = swap(own, 2)
 
     some, every = merge([own, *arrived])
-    some, every = lax.optimization_barrier((some, every, own_far, early, text, stale))[:2]
+    some, every = lax.optimization_barrier((some, every, own_far, weight_far, text, stale))[:2]
     queries = lax.optimization_barrier((*queries, some))[:groups]
     some_far, near = swap(some, 2), swap(every, 1)
     asked = [queries[0], *along(queries)]
 
-    own_far, some_far = lax.optimization_barrier((own_far, some_far, near, *asked[2:]))[:2]
+    own_far, some_far = lax.optimization_barrier((own_far, some_far, near, *asked))[:2]
     own_corner, some_corner = swap(own_far, 1), swap(some_far, 1)
-    weight, early = lax.optimization_barrier((weight, early, own_corner, some_corner))[:2]
-    weight_near, early_near, late = swap(weight, 1), swap(early, 1), swap(weight[half:], 2)
-    attended = attend([every, near, own_far, some_far, own_corner, some_corner], asked, text, stale)
-
-    across, beside = swap(attended, 2 * SPREAD), swap(attended, SPREAD)
-    across, beside, late = lax.optimization_barrier((across, beside, late, weight_near, early_near))[:3]
-    last = swap(across, SPREAD)
-    weight = order(weight, weight_near, [early, late, early_near, swap(late, 1)])
-    terms = close(groups, begin([attended, beside, across], weight), last, weight)
-
-    terms = [terms[0], *along(terms)]
-    received = [lax.ppermute(term, "head", [(0, 1), (1, 0)]) for term in terms]
-    return finish(terms, received, out_bias, out_gate)
+    weight, weight_far = lax.optimization_barrier((weight, weight_far, own_corner, some_corner))[:2]
+    weight_near, weight_corner = swap(weight, 1), swap(weight_far, 1)
+    full, most, last = attend([every, near, own_far, some_far, own_corner, some_corner], asked, text, stale)
+
+    across_most, across_last = swap(most, 2 * SPREAD), swap(last, 2 * SPREAD)
+    beside = swap(full, SPREAD)
+    final_most = swap(across_most, SPREAD)
+    final_last = swap(after(across_last, beside, weight_near, weight_corner), SPREAD)
+    weight = order([weight, weight_near, weight_far, weight_corner])
+    partial = begin([full, beside, across_most, across_last], weight)
+    terms = close(groups, partial, [final_most, final_last], weight)
+
+    kept, sent = divide([terms[0], *along(terms)])
+    received = lax.ppermute(sent, "head", [(0, 1), (1, 0)])
+    return finish(kept, received, out_bias, out_gate)
 
 
 def solution(mesh):

time: 74.4 us -> 63.8 us (0.86)
  Pallas kernels: 16.8 us -> 8.28 us
  waiting for transfers between devices: 32.4 us -> 29.5 us
  starting transfers between devices: 24.7 us -> 25.6 us
    pallas_call x1, Pallas kernels: 10.8 us -> 2.3 us  [pack(): pl.pallas_call(pack_kernel, out_shape=[jax.ShapeDtypeStruct((kinds, rows,...]
    ppermute x22, starting transfers between devices: 20.7 us -> 24 us  [swap(): return lax.ppermute(value, 'patch', [(p, p ^ twist) for p in range(size)])]
    ppermute x22, waiting for transfers between devices: 28.6 us -> 25.9 us  [swap(): return lax.ppermute(value, 'patch', [(p, p ^ twist) for p in range(size)])]
    ppermute x4 -> x1, starting transfers between devices: 4.07 us -> 1.56 us  [grouped_body(): received = lax.ppermute(sent, 'head', [(0, 1), (1, 0)])]
    ppermute x4 -> x1, waiting for transfers between devices: 3.8 us -> 3.61 us  [grouped_body(): received = lax.ppermute(sent, 'head', [(0, 1), (1, 0)])]
    pallas_call x2 -> x3, Pallas kernels: 3.09 us -> 3.11 us  [the longest x1 2.34 us: attend(): pl.pallas_call(functools.partial(attend_kernel, groups), out_shape=[jax.S...]
  transfers between devices with their start and end apart: 26 -> 23, of which waited for: 12 -> 13; matrix products, arithmetic and copies ran while one was open for 0% -> 0% of each run, Pallas kernels for 6% -> 11%
where the time goes in v6:
time: 63.8 us; the launch traced here: 63.6 us
  waiting for transfers between devices  29.5 us (46%)
  starting transfers between devices  25.6 us (40%)
  Pallas kernels  8.28 us (13%)
    ppermute x22, waiting for transfers between devices, swap(): return lax.ppermute(value, 'patch', [(p, p ^ twist) for p in range(size)])  25.9 us
    ppermute x22, starting transfers between devices, swap(): return lax.ppermute(value, 'patch', [(p, p ^ twist) for p in range(size)])  24 us
    ppermute x1, waiting for transfers between devices, grouped_body(): received = lax.ppermute(sent, 'head', [(0, 1), (1, 0)])  3.61 us
    pallas_call x1, Pallas kernels, attend(): pl.pallas_call(functools.partial(attend_kernel, groups), out_shape=[jax.S...  2.34 us
    pallas_call x1, Pallas kernels, pack(): pl.pallas_call(pack_kernel, out_shape=[jax.ShapeDtypeStruct((kinds, rows,...  2.3 us
    ppermute x1, starting transfers between devices, grouped_body(): received = lax.ppermute(sent, 'head', [(0, 1), (1, 0)])  1.56 us
    pallas_call x1, Pallas kernels, pick(): pl.pallas_call(pick_kernel, out_shape=[jax.ShapeDtypeStruct(shape, jnp.bf...  1.53 us
  transfers between devices with their start and end apart: 23, of which 13 were waited for; matrix products, arithmetic and copies ran while one was open for 0% of the time, Pallas kernels for 11%

profile of v6, /device:TPU:0, one launch (start us, length us, event | category | flops | bytes accessed | tf_op | source)
XLA Modules:
  0.0 63.6 jit_solution(6372260887646107482)
XLA Ops:
  0.0 2.9 %collective-permute-start.4 = (bf16[192,1536]{1,0:T(8,128)(2,1)}, bf16[192,1536]{1,0:T(8,128)(2,1)S(1)}, u32[]{:S(2)}, u32[]{:S(2)}) collective-permute-start(bf16[192,1536]{1,0:T(8,128)(2,1)} %bitcast.2), channel_id=1, source_target_pairs={{0,4},{2,6},{4,0},{6,2},{8,12},{10,14},{12,8},{14,10},{16,20},{18,... | collective-permute-start | bytes 1769480 | tf_op jit(solution)/shard_map/ppermute | solution.py:376
  2.9 2.3 %shard_map.82 = (bf16[2,48,384]{2,1,0:T(8,128)(2,1)}, bf16[2,48,384]{2,1,0:T(8,128)(2,1)}, bf16[2,48,384]{2,1,0:T(8,128)(2,1)}, bf16[2,48,384]{2,1,0:T(8,128)(2,...) custom-call(bf16[48,1536]{1,0:T(8,128)(2,1)} %queries_hbm.1, ...), custom_call_target="tpu_custom_call" | custom-call | flops 294912 | bytes 884736 | tf_op jit(solution)/shard_map/pallas_call | solution.py:109
  5.2 1.6 %collective-permute-start = (bf16[2,48,384]{2,1,0:T(8,128)(2,1)}, bf16[2,48,384]{2,1,0:T(8,128)(2,1)S(1)}, u32[]{:S(2)}, u32[]{:S(2)}) collective-permute-start(bf16[2,48,384]{2,1,0:T(8,128)(2,1)} %get-tuple-element.38), channel_id=1, source_target_pairs={{0,8},{2,10},{4,12},{6,14},{8,0},{10,2},{12,4},{14,6},{16,24},{18,... | collective-permute-start | bytes 221192 | tf_op jit(solution)/shard_map/ppermute | solution.py:376
  6.9 2.6 %collective-permute-start.1 = (bf16[2,48,384]{2,1,0:T(8,128)(2,1)}, bf16[2,48,384]{2,1,0:T(8,128)(2,1)S(1)}, u32[]{:S(2)}, u32[]{:S(2)}) collective-permute-start(bf16[2,48,384]{2,1,0:T(8,128)(2,1)} %get-tuple-element.39), channel_id=1, source_target_pairs={{0,16},{2,18},{4,20},{6,22},{8,24},{10,26},{12,28},{14,30},{16,0},... | collective-permute-start | bytes 221192 | tf_op jit(solution)/shard_map/ppermute | solution.py:376
  10.1 1.5 %shard_map.84 = (bf16[2,512,384]{2,1,0:T(8,128)(2,1)S(1)}, bf16[2,768,384]{2,1,0:T(8,128)(2,1)S(1)}) custom-call(bf16[2,512,1536]{2,1,0:T(8,128)(2,1)} %text_hbm.1, bf16[2,768,1536]{2,1,0:T(8,128)(2,1)} %stale_hbm.1), custom_call_target="tpu_custom_call" | custom-call | bytes 8388608 | tf_op jit(solution)/shard_map/pallas_call | solution.py:142
  11.7 2.9 %collective-permute-done.1.refs_2_ = bf16[2,48,384]{2,1,0:T(8,128)(2,1)S(1)} collective-permute-done((bf16[2,48,384]{2,1,0:T(8,128)(2,1)}, bf16[2,48,384]{2,1,0:T(8,128)(2,1)S(1)}, u32[]{:S(2)}, u32[]{:S(2)}) %collective-permute-start.1) | collective-permute-done | bytes 73760 | tf_op jit(solution)/shard_map/ppermute | solution.py:376
  14.6 1.3 %collective-permute-done.2.refs_3_ = bf16[2,48,384]{2,1,0:T(8,128)(2,1)S(1)} collective-permute-done((bf16[2,48,384]{2,1,0:T(8,128)(2,1)}, bf16[2,48,384]{2,1,0:T(8,128)(2,1)S(1)}, u32[]{:S(2)}, u32[]{:S(2)}) %collective-permute-start.2) | collective-permute-done | bytes 73760 | tf_op jit(solution)/shard_map/ppermute | solution.py:376
  16.0 2.1 %collective-permute-done.3.refs_2_ = bf16[2,48,384]{2,1,0:T(8,128)(2,1)S(1)} collective-permute-done((bf16[2,48,384]{2,1,0:T(8,128)(2,1)}, bf16[2,48,384]{2,1,0:T(8,128)(2,1)S(1)}, u32[]{:S(2)}, u32[]{:S(2)}) %collective-permute-start.3) | collective-permute-done | bytes 73760 | tf_op jit(solution)/shard_map/ppermute | solution.py:376
  18.1 1.7 %collective-permute-start.6 = (bf16[3,2,48,384]{3,2,1,0:T(8,128)(2,1)S(1)}, bf16[3,2,48,384]{3,2,1,0:T(8,128)(2,1)S(1)}, u32[]{:S(2)}, u32[]{:S(2)}) collective-permute-start(bf16[3,2,48,384]{3,2,1,0:T(8,128)(2,1)S(1)} %get-tuple-element.46), channel_id=1, source_target_pairs={{0,4},{2,6},{4,0},{6,2},{8,12},{10,14},{12,8},{14,10},{16,20},{18,... | collective-permute-start | bytes 663560 | tf_op jit(solution)/shard_map/ppermute | solution.py:376
  19.8 1.6 %collective-permute-start.7 = (bf16[48,384]{1,0:T(8,128)(2,1)S(1)}, bf16[48,384]{1,0:T(8,128)(2,1)S(1)}, u32[]{:S(2)}, u32[]{:S(2)}) collective-permute-start(bf16[48,384]{1,0:T(8,128)(2,1)S(1)} %copy-done.7), channel_id=1, source_target_pairs={{0,8},{2,10},{4,12},{6,14},{8,0},{10,2},{12,4},{14,6},{16,24},{18,... | collective-permute-start | bytes 110600 | tf_op jit(solution)/shard_map/ppermute | solution.py:376
  21.4 2.6 %collective-permute-start.8 = (bf16[48,384]{1,0:T(8,128)(2,1)S(1)}, bf16[48,384]{1,0:T(8,128)(2,1)S(1)}, u32[]{:S(2)}, u32[]{:S(2)}) collective-permute-start(bf16[48,384]{1,0:T(8,128)(2,1)S(1)} %copy-done.6), channel_id=1, source_target_pairs={{0,16},{2,18},{4,20},{6,22},{8,24},{10,26},{12,28},{14,30},{16,0},... | collective-permute-start | bytes 110600 | tf_op jit(solution)/shard_map/ppermute | solution.py:376
  24.2 2.8 %collective-permute-done.8.refs_8_ = bf16[48,384]{1,0:T(8,128)(2,1)S(1)} collective-permute-done((bf16[48,384]{1,0:T(8,128)(2,1)S(1)}, bf16[48,384]{1,0:T(8,128)(2,1)S(1)}, u32[]{:S(2)}, u32[]{:S(2)}) %collective-permute-start.8) | collective-permute-done | bytes 36896 | tf_op jit(solution)/shard_map/ppermute | solution.py:376
  27.0 2.7 %collective-permute-done.9.refs_9_ = bf16[48,384]{1,0:T(8,128)(2,1)S(1)} collective-permute-done((bf16[48,384]{1,0:T(8,128)(2,1)S(1)}, bf16[48,384]{1,0:T(8,128)(2,1)S(1)}, u32[]{:S(2)}, u32[]{:S(2)}) %collective-permute-start.9) | collective-permute-done | bytes 36896 | tf_op jit(solution)/shard_map/ppermute | solution.py:376
  29.8 0.5 collective-permute-start.10
  30.3 1.1 %collective-permute-done.10.refs_4_ = bf16[2,48,384]{2,1,0:T(8,128)(2,1)S(1)} collective-permute-done((bf16[2,48,384]{2,1,0:T(8,128)(2,1)S(1)}, bf16[2,48,384]{2,1,0:T(8,128)(2,1)S(1)}, u32[]{:S(2)}, u32[]{:S(2)}) %collective-permute-start.10) | collective-permute-done | bytes 73760 | tf_op jit(solution)/shard_map/ppermute | solution.py:376
  31.9 2.3 %shard_map.85 = (bf16[192,384]{1,0:T(8,128)(2,1)S(1)}, bf16[192,256]{1,0:T(8,128)(2,1)S(1)}, bf16[192,128]{1,0:T(8,128)(2,1)S(1)}) custom-call(bf16[4,2,48,384]{3,2,1,0:T(8,128)(2,1)S(1)} %get-tuple-element.45.refs_0_, bf16[4,2,48,384]{3,2,1,0:T(8,128)(2,1)S(1)} %collective-permute-done.5.refs_1_, bf16[2,48,384]{2,1,0:T(8,128)(2,1)S(1)} %collective-permute-done.3.refs_2_, ...), custom_call_target="tpu_custom_call" | custom-call | flops 603979776 | bytes 3145728 | tf_op jit(solution)/shard_map/pallas_call | solution.py:233
  34.3 1.2 %collective-permute-start.13 = (bf16[192,256]{1,0:T(8,128)(2,1)S(1)}, bf16[192,256]{1,0:T(8,128)(2,1)S(1)}, u32[]{:S(2)}, u32[]{:S(2)}) collective-permute-start(bf16[192,256]{1,0:T(8,128)(2,1)S(1)} %get-tuple-element.58), channel_id=1, source_target_pairs={{0,16},{2,18},{4,20},{6,22},{8,24},{10,26},{12,28},{14,30},{16,0},... | collective-permute-start | bytes 294920 | tf_op jit(solution)/shard_map/ppermute | solution.py:376
  35.4 1.8 %collective-permute-start.14 = (bf16[192,128]{1,0:T(8,128)(2,1)S(1)}, bf16[192,128]{1,0:T(8,128)(2,1)S(1)}, u32[]{:S(2)}, u32[]{:S(2)}) collective-permute-start(bf16[192,128]{1,0:T(8,128)(2,1)S(1)} %get-tuple-element.59), channel_id=1, source_target_pairs={{0,16},{2,18},{4,20},{6,22},{8,24},{10,26},{12,28},{14,30},{16,0},... | collective-permute-start | bytes 147464 | tf_op jit(solution)/shard_map/ppermute | solution.py:376
  37.3 6.7 %collective-permute-done.13.across_most = bf16[192,256]{1,0:T(8,128)(2,1)S(1)} collective-permute-done((bf16[192,256]{1,0:T(8,128)(2,1)S(1)}, bf16[192,256]{1,0:T(8,128)(2,1)S(1)}, u32[]{:S(2)}, u32[]{:S(2)}) %collective-permute-start.13) | collective-permute-done | bytes 98336 | tf_op jit(solution)/shard_map/ppermute | solution.py:376
  44.0 0.5 collective-permute-done.14.across_last
  44.5 1.6 %collective-permute-start.18 = (bf16[192,128]{1,0:T(8,128)(2,1)S(1)}, bf16[192,128]{1,0:T(8,128)(2,1)S(1)}, u32[]{:S(2)}, u32[]{:S(2)}) collective-permute-start(bf16[192,128]{1,0:T(8,128)(2,1)S(1)} %collective-permute-done.14.across_last), channel_id=1, source_target_pairs={{0,8},{2,10},{4,12},{6,14},{8,0},{10,2},{12,4},{14,6},{16,24},{18,... | collective-permute-start | bytes 147464 | tf_op jit(solution)/shard_map/ppermute | solution.py:376
  46.3 0.7 %shard_map.87.partial = f32[192,768]{1,0:T(8,128)S(1)} custom-call(bf16[192,384]{1,0:T(8,128)(2,1)S(1)} %get-tuple-element.57.full, bf16[192,384]{1,0:T(8,128)(2,1)S(1)} %collective-permute-done.12.beside, bf16[192,256]{1,0:T(8,128)(2,1)S(1)} %collective-permute-done.13.across_most, bf16[192,128]{1,0:T(8,128)(2,1)S(1)} %collective-permute-done.14.across_last, ...), custom_call_target="tpu_custom_call" | custom-call | flops 452984832 | bytes 589824 | tf_op jit(solution)/shard_map/pallas_call | solution.py:282
  47.0 1.6 %collective-permute-done.17.most = bf16[192,256]{1,0:T(8,128)(2,1)S(1)} collective-permute-done((bf16[192,256]{1,0:T(8,128)(2,1)S(1)}, bf16[192,256]{1,0:T(8,128)(2,1)S(1)}, u32[]{:S(2)}, u32[]{:S(2)}) %collective-permute-start.17) | collective-permute-done | bytes 98336 | tf_op jit(solution)/shard_map/ppermute | solution.py:376
  48.6 0.5 collective-permute-done.18.last
  49.5 1.3 %collective-permute-start.19 = (bf16[48,768]{1,0:T(8,128)(2,1)S(1)}, bf16[48,768]{1,0:T(8,128)(2,1)S(1)}, u32[]{:S(2)}, u32[]{:S(2)}) collective-permute-start(bf16[48,768]{1,0:T(8,128)(2,1)S(1)} %get-tuple-element.64), channel_id=1, source_target_pairs={{0,8},{2,10},{4,12},{6,14},{8,0},{10,2},{12,4},{14,6},{16,24},{18,... | collective-permute-start | bytes 221192 | tf_op jit(solution)/shard_map/ppermute | solution.py:376
  50.8 0.5 collective-permute-start.20
  51.3 2.7 %collective-permute-start.21 = (bf16[48,768]{1,0:T(8,128)(2,1)S(1)}, bf16[48,768]{1,0:T(8,128)(2,1)S(1)}, u32[]{:S(2)}, u32[]{:S(2)}) collective-permute-start(bf16[48,768]{1,0:T(8,128)(2,1)S(1)} %get-tuple-element.66), channel_id=1, source_target_pairs={{0,24},{2,26},{4,28},{6,30},{8,16},{10,18},{12,20},{14,22},{16,8},... | collective-permute-start | bytes 221192 | tf_op jit(solution)/shard_map/ppermute | solution.py:376
  54.0 0.7 %collective-permute-done.19.refs_1_ = bf16[48,768]{1,0:T(8,128)(2,1)S(1)} collective-permute-done((bf16[48,768]{1,0:T(8,128)(2,1)S(1)}, bf16[48,768]{1,0:T(8,128)(2,1)S(1)}, u32[]{:S(2)}, u32[]{:S(2)}) %collective-permute-start.19) | collective-permute-done | bytes 73760 | tf_op jit(solution)/shard_map/ppermute | solution.py:376
  54.7 2.9 %collective-permute-done.20.refs_2_ = bf16[48,768]{1,0:T(8,128)(2,1)S(1)} collective-permute-done((bf16[48,768]{1,0:T(8,128)(2,1)S(1)}, bf16[48,768]{1,0:T(8,128)(2,1)S(1)}, u32[]{:S(2)}, u32[]{:S(2)}) %collective-permute-start.20) | collective-permute-done | bytes 73760 | tf_op jit(solution)/shard_map/ppermute | solution.py:376
  57.7 1.6 %collective-permute-start.22 = (bf16[2,48,768]{2,1,0:T(8,128)(2,1)S(1)}, bf16[2,48,768]{2,1,0:T(8,128)(2,1)S(1)}, u32[]{:S(2)}, u32[]{:S(2)}) collective-permute-start(bf16[2,48,768]{2,1,0:T(8,128)(2,1)S(1)} %get-tuple-element.68), channel_id=1, source_target_pairs={{0,1},{1,0},{2,3},{3,2},{4,5},{5,4},{6,7},{7,6},{8,9},{9,8},{10,11... | collective-permute-start | bytes 442376 | tf_op jit(solution)/shard_map/ppermute | solution.py:412
  59.3 3.6 %collective-permute-done.22.arrived = bf16[2,48,768]{2,1,0:T(8,128)(2,1)S(1)} collective-permute-done((bf16[2,48,768]{2,1,0:T(8,128)(2,1)S(1)}, bf16[2,48,768]{2,1,0:T(8,128)(2,1)S(1)}, u32[]{:S(2)}, u32[]{:S(2)}) %collective-permute-start.22) | collective-permute-done | bytes 147488 | tf_op jit(solution)/shard_map/ppermute | solution.py:412
  62.9 0.7 %shard_map.90 = bf16[48,1536]{1,0:T(8,128)(2,1)} custom-call(bf16[2,48,768]{2,1,0:T(8,128)(2,1)S(1)} %get-tuple-element.67.kept, bf16[2,48,768]{2,1,0:T(8,128)(2,1)S(1)} %collective-permute-done.22.arrived, f32[1,1536]{1,0:T(1,128)S(1)} %reshape.6.bias, f32[1,1536]{1,0:T(1,128)S(1)} %reshape.7.gate), custom_call_target="tpu_custom_call" | custom-call | flops 221184 | bytes 294912 | tf_op jit(solution)/shard_map/pallas_call | solution.py:357
  (41 shorter events, 2.2 us)
Async XLA Ops:
  0.0 18.1 %collective-permute-start.4 = (bf16[192,1536]{1,0:T(8,128)(2,1)}, bf16[192,1536]{1,0:T(8,128)(2,1)S(1)}, u32[]{:S(2)}, u32[]{:S(2)}) collective-permute-start(bf16[192,1536]{1,0:T(8,128)(2,1)} %bitcast.2), channel_id=1, source_target_pairs={{0,4},{2,6},{4,0},{6,2},{8,12},{10,14},{12,8},{14,10},{16,20},{18,... | collective-permute-start | bytes 1769480 | tf_op jit(solution)/shard_map/ppermute | solution.py:376
  5.2 6.4 %collective-permute-start = (bf16[2,48,384]{2,1,0:T(8,128)(2,1)}, bf16[2,48,384]{2,1,0:T(8,128)(2,1)S(1)}, u32[]{:S(2)}, u32[]{:S(2)}) collective-permute-start(bf16[2,48,384]{2,1,0:T(8,128)(2,1)} %get-tuple-element.38), channel_id=1, source_target_pairs={{0,8},{2,10},{4,12},{6,14},{8,0},{10,2},{12,4},{14,6},{16,24},{18,... | collective-permute-start | bytes 221192 | tf_op jit(solution)/shard_map/ppermute | solution.py:376
  6.9 7.7 %collective-permute-start.1 = (bf16[2,48,384]{2,1,0:T(8,128)(2,1)}, bf16[2,48,384]{2,1,0:T(8,128)(2,1)S(1)}, u32[]{:S(2)}, u32[]{:S(2)}) collective-permute-start(bf16[2,48,384]{2,1,0:T(8,128)(2,1)} %get-tuple-element.39), channel_id=1, source_target_pairs={{0,16},{2,18},{4,20},{6,22},{8,24},{10,26},{12,28},{14,30},{16,0},... | collective-permute-start | bytes 221192 | tf_op jit(solution)/shard_map/ppermute | solution.py:376
  9.5 6.5 %collective-permute-start.2 = (bf16[2,48,384]{2,1,0:T(8,128)(2,1)}, bf16[2,48,384]{2,1,0:T(8,128)(2,1)S(1)}, u32[]{:S(2)}, u32[]{:S(2)}) collective-permute-start(bf16[2,48,384]{2,1,0:T(8,128)(2,1)} %get-tuple-element.40), channel_id=1, source_target_pairs={{0,24},{2,26},{4,28},{6,30},{8,16},{10,18},{12,20},{14,22},{16,8},... | collective-permute-start | bytes 221192 | tf_op jit(solution)/shard_map/ppermute | solution.py:376
  9.7 6.3 %copy-start.1 = (bf16[2,48,384]{2,1,0:T(8,128)(2,1)S(1)}, bf16[2,48,384]{2,1,0:T(8,128)(2,1)}, u32[]{:S(2)}) copy-start(bf16[2,48,384]{2,1,0:T(8,128)(2,1)} %get-tuple-element.37.refs_0_) | copy-start | bytes 221188
  9.7 10.1 %copy-start.7 = (bf16[48,384]{1,0:T(8,128)(2,1)S(1)}, bf16[48,384]{1,0:T(8,128)(2,1)}, u32[]{:S(2)}) copy-start(bf16[48,384]{1,0:T(8,128)(2,1)} %get-tuple-element.52) | copy-start | bytes 110596
  9.7 11.7 %copy-start.6 = (bf16[48,384]{1,0:T(8,128)(2,1)S(1)}, bf16[48,384]{1,0:T(8,128)(2,1)}, u32[]{:S(2)}) copy-start(bf16[48,384]{1,0:T(8,128)(2,1)} %get-tuple-element.53) | copy-start | bytes 110596
  9.7 14.3 %copy-start.5 = (bf16[48,384]{1,0:T(8,128)(2,1)S(1)}, bf16[48,384]{1,0:T(8,128)(2,1)}, u32[]{:S(2)}) copy-start(bf16[48,384]{1,0:T(8,128)(2,1)} %get-tuple-element.54) | copy-start | bytes 110596
  9.7 21.6 %copy-start = (bf16[1536,192]{0,1:T(8,128)(2,1)S(1)}, bf16[1536,192]{0,1:T(8,128)(2,1)}, u32[]{:S(2)}) copy-start(bf16[1536,192]{0,1:T(8,128)(2,1)} %param.13) | copy-start | bytes 1769476
  9.7 22.1 %copy-start.2 = (bf16[48,384]{1,0:T(8,128)(2,1)S(1)}, bf16[48,384]{1,0:T(8,128)(2,1)}, u32[]{:S(2)}) copy-start(bf16[48,384]{1,0:T(8,128)(2,1)} %get-tuple-element.51.refs_6_) | copy-start | bytes 110596
  9.7 8.3 %collective-permute-start.3 = (bf16[2,48,384]{2,1,0:T(8,128)(2,1)}, bf16[2,48,384]{2,1,0:T(8,128)(2,1)S(1)}, u32[]{:S(2)}, u32[]{:S(2)}) collective-permute-start(bf16[2,48,384]{2,1,0:T(8,128)(2,1)} %get-tuple-element.37.refs_0_), channel_id=1, source_target_pairs={{0,4},{2,6},{4,0},{6,2},{8,12},{10,14},{12,8},{14,10},{16,20},{18,... | collective-permute-start | bytes 221192 | tf_op jit(solution)/shard_map/ppermute | solution.py:376
  18.1 11.7 %collective-permute-start.5 = (bf16[4,2,48,384]{3,2,1,0:T(8,128)(2,1)S(1)}, bf16[4,2,48,384]{3,2,1,0:T(8,128)(2,1)S(1)}, u32[]{:S(2)}, u32[]{:S(2)}) collective-permute-start(bf16[4,2,48,384]{3,2,1,0:T(8,128)(2,1)S(1)} %get-tuple-element.45.refs_0_), channel_id=1, source_target_pairs={{0,2},{2,0},{4,6},{6,4},{8,10},{10,8},{12,14},{14,12},{16,18},{18,... | collective-permute-start | bytes 884744 | tf_op jit(solution)/shard_map/ppermute | solution.py:376
  18.1 11.7 %collective-permute-start.6 = (bf16[3,2,48,384]{3,2,1,0:T(8,128)(2,1)S(1)}, bf16[3,2,48,384]{3,2,1,0:T(8,128)(2,1)S(1)}, u32[]{:S(2)}, u32[]{:S(2)}) collective-permute-start(bf16[3,2,48,384]{3,2,1,0:T(8,128)(2,1)S(1)} %get-tuple-element.46), channel_id=1, source_target_pairs={{0,4},{2,6},{4,0},{6,2},{8,12},{10,14},{12,8},{14,10},{16,20},{18,... | collective-permute-start | bytes 663560 | tf_op jit(solution)/shard_map/ppermute | solution.py:376
  19.8 4.4 %collective-permute-start.7 = (bf16[48,384]{1,0:T(8,128)(2,1)S(1)}, bf16[48,384]{1,0:T(8,128)(2,1)S(1)}, u32[]{:S(2)}, u32[]{:S(2)}) collective-permute-start(bf16[48,384]{1,0:T(8,128)(2,1)S(1)} %copy-done.7), channel_id=1, source_target_pairs={{0,8},{2,10},{4,12},{6,14},{8,0},{10,2},{12,4},{14,6},{16,24},{18,... | collective-permute-start | bytes 110600 | tf_op jit(solution)/shard_map/ppermute | solution.py:376
  21.4 5.6 %collective-permute-start.8 = (bf16[48,384]{1,0:T(8,128)(2,1)S(1)}, bf16[48,384]{1,0:T(8,128)(2,1)S(1)}, u32[]{:S(2)}, u32[]{:S(2)}) collective-permute-start(bf16[48,384]{1,0:T(8,128)(2,1)S(1)} %copy-done.6), channel_id=1, source_target_pairs={{0,16},{2,18},{4,20},{6,22},{8,24},{10,26},{12,28},{14,30},{16,0},... | collective-permute-start | bytes 110600 | tf_op jit(solution)/shard_map/ppermute | solution.py:376
  24.0 5.8 %collective-permute-start.9 = (bf16[48,384]{1,0:T(8,128)(2,1)S(1)}, bf16[48,384]{1,0:T(8,128)(2,1)S(1)}, u32[]{:S(2)}, u32[]{:S(2)}) collective-permute-start(bf16[48,384]{1,0:T(8,128)(2,1)S(1)} %copy-done.5), channel_id=1, source_target_pairs={{0,24},{2,26},{4,28},{6,30},{8,16},{10,18},{12,20},{14,22},{16,8},... | collective-permute-start | bytes 110600 | tf_op jit(solution)/shard_map/ppermute | solution.py:376
  29.7 1.6 %collective-permute-start.11 = (bf16[3,2,48,384]{3,2,1,0:T(8,128)(2,1)S(1)}, bf16[3,2,48,384]{3,2,1,0:T(8,128)(2,1)S(1)}, u32[]{:S(2)}, u32[]{:S(2)}) collective-permute-start(bf16[3,2,48,384]{3,2,1,0:T(8,128)(2,1)S(1)} %collective-permute-done.6.refs_3_), channel_id=1, source_target_pairs={{0,2},{2,0},{4,6},{6,4},{8,10},{10,8},{12,14},{14,12},{16,18},{18,... | collective-permute-start | bytes 663560 | tf_op jit(solution)/shard_map/ppermute | solution.py:376
  29.8 1.6 %collective-permute-start.10 = (bf16[2,48,384]{2,1,0:T(8,128)(2,1)S(1)}, bf16[2,48,384]{2,1,0:T(8,128)(2,1)S(1)}, u32[]{:S(2)}, u32[]{:S(2)}) collective-permute-start(bf16[2,48,384]{2,1,0:T(8,128)(2,1)S(1)} %collective-permute-done.3.refs_2_), channel_id=1, source_target_pairs={{0,2},{2,0},{4,6},{6,4},{8,10},{10,8},{12,14},{14,12},{16,18},{18,... | collective-permute-start | bytes 221192 | tf_op jit(solution)/shard_map/ppermute | solution.py:376
  31.3 13.2 %collective-permute-start.15 = (bf16[192,1536]{1,0:T(8,128)(2,1)S(1)}, bf16[192,1536]{1,0:T(8,128)(2,1)S(1)}, u32[]{:S(2)}, u32[]{:S(2)}) collective-permute-start(bf16[192,1536]{1,0:T(8,128)(2,1)S(1)} %bitcast.3), channel_id=1, source_target_pairs={{0,2},{2,0},{4,6},{6,4},{8,10},{10,8},{12,14},{14,12},{16,18},{18,... | collective-permute-start | bytes 1769480 | tf_op jit(solution)/shard_map/ppermute | solution.py:376
  31.5 13.0 %collective-permute-start.16 = (bf16[192,1536]{1,0:T(8,128)(2,1)S(1)}, bf16[192,1536]{1,0:T(8,128)(2,1)S(1)}, u32[]{:S(2)}, u32[]{:S(2)}) collective-permute-start(bf16[192,1536]{1,0:T(8,128)(2,1)S(1)} %collective-permute-done.4.refs_2_), channel_id=1, source_target_pairs={{0,2},{2,0},{4,6},{6,4},{8,10},{10,8},{12,14},{14,12},{16,18},{18,... | collective-permute-start | bytes 1769480 | tf_op jit(solution)/shard_map/ppermute | solution.py:376
  34.2 10.3 %collective-permute-start.12 = (bf16[192,384]{1,0:T(8,128)(2,1)S(1)}, bf16[192,384]{1,0:T(8,128)(2,1)S(1)}, u32[]{:S(2)}, u32[]{:S(2)}) collective-permute-start(bf16[192,384]{1,0:T(8,128)(2,1)S(1)} %get-tuple-element.57.full), channel_id=1, source_target_pairs={{0,8},{2,10},{4,12},{6,14},{8,0},{10,2},{12,4},{14,6},{16,24},{18,... | collective-permute-start | bytes 442376 | tf_op jit(solution)/shard_map/ppermute | solution.py:376
  34.3 9.7 %collective-permute-start.13 = (bf16[192,256]{1,0:T(8,128)(2,1)S(1)}, bf16[192,256]{1,0:T(8,128)(2,1)S(1)}, u32[]{:S(2)}, u32[]{:S(2)}) collective-permute-start(bf16[192,256]{1,0:T(8,128)(2,1)S(1)} %get-tuple-element.58), channel_id=1, source_target_pairs={{0,16},{2,18},{4,20},{6,22},{8,24},{10,26},{12,28},{14,30},{16,0},... | collective-permute-start | bytes 294920 | tf_op jit(solution)/shard_map/ppermute | solution.py:376
  35.4 9.0 %collective-permute-start.14 = (bf16[192,128]{1,0:T(8,128)(2,1)S(1)}, bf16[192,128]{1,0:T(8,128)(2,1)S(1)}, u32[]{:S(2)}, u32[]{:S(2)}) collective-permute-start(bf16[192,128]{1,0:T(8,128)(2,1)S(1)} %get-tuple-element.59), channel_id=1, source_target_pairs={{0,16},{2,18},{4,20},{6,22},{8,24},{10,26},{12,28},{14,30},{16,0},... | collective-permute-start | bytes 147464 | tf_op jit(solution)/shard_map/ppermute | solution.py:376
  44.0 4.6 %collective-permute-start.17 = (bf16[192,256]{1,0:T(8,128)(2,1)S(1)}, bf16[192,256]{1,0:T(8,128)(2,1)S(1)}, u32[]{:S(2)}, u32[]{:S(2)}) collective-permute-start(bf16[192,256]{1,0:T(8,128)(2,1)S(1)} %collective-permute-done.13.across_most), channel_id=1, source_target_pairs={{0,8},{2,10},{4,12},{6,14},{8,0},{10,2},{12,4},{14,6},{16,24},{18,... | collective-permute-start | bytes 294920 | tf_op jit(solution)/shard_map/ppermute | solution.py:376
  44.5 4.6 %collective-permute-start.18 = (bf16[192,128]{1,0:T(8,128)(2,1)S(1)}, bf16[192,128]{1,0:T(8,128)(2,1)S(1)}, u32[]{:S(2)}, u32[]{:S(2)}) collective-permute-start(bf16[192,128]{1,0:T(8,128)(2,1)S(1)} %collective-permute-done.14.across_last), channel_id=1, source_target_pairs={{0,8},{2,10},{4,12},{6,14},{8,0},{10,2},{12,4},{14,6},{16,24},{18,... | collective-permute-start | bytes 147464 | tf_op jit(solution)/shard_map/ppermute | solution.py:376
  46.3 13.0 %copy-start.3 = (f32[1536]{0:T(1024)S(1)}, f32[1536]{0:T(1024)}, u32[]{:S(2)}) copy-start(f32[1536]{0:T(1024)} %param.14) | copy-start | bytes 18436
  46.3 13.0 %copy-start.4 = (f32[1536]{0:T(1024)S(1)}, f32[1536]{0:T(1024)}, u32[]{:S(2)}) copy-start(f32[1536]{0:T(1024)} %param.15) | copy-start | bytes 18436
  49.5 5.2 %collective-permute-start.19 = (bf16[48,768]{1,0:T(8,128)(2,1)S(1)}, bf16[48,768]{1,0:T(8,128)(2,1)S(1)}, u32[]{:S(2)}, u32[]{:S(2)}) collective-permute-start(bf16[48,768]{1,0:T(8,128)(2,1)S(1)} %get-tuple-element.64), channel_id=1, source_target_pairs={{0,8},{2,10},{4,12},{6,14},{8,0},{10,2},{12,4},{14,6},{16,24},{18,... | collective-permute-start | bytes 221192 | tf_op jit(solution)/shard_map/ppermute | solution.py:376
  50.8 6.8 %collective-permute-start.20 = (bf16[48,768]{1,0:T(8,128)(2,1)S(1)}, bf16[48,768]{1,0:T(8,128)(2,1)S(1)}, u32[]{:S(2)}, u32[]{:S(2)}) collective-permute-start(bf16[48,768]{1,0:T(8,128)(2,1)S(1)} %get-tuple-element.65), channel_id=1, source_target_pairs={{0,16},{2,18},{4,20},{6,22},{8,24},{10,26},{12,28},{14,30},{16,0},... | collective-permute-start | bytes 221192 | tf_op jit(solution)/shard_map/ppermute | solution.py:376
  51.3 6.3 %collective-permute-start.21 = (bf16[48,768]{1,0:T(8,128)(2,1)S(1)}, bf16[48,768]{1,0:T(8,128)(2,1)S(1)}, u32[]{:S(2)}, u32[]{:S(2)}) collective-permute-start(bf16[48,768]{1,0:T(8,128)(2,1)S(1)} %get-tuple-element.66), channel_id=1, source_target_pairs={{0,24},{2,26},{4,28},{6,30},{8,16},{10,18},{12,20},{14,22},{16,8},... | collective-permute-start | bytes 221192 | tf_op jit(solution)/shard_map/ppermute | solution.py:376
  57.7 5.2 %collective-permute-start.22 = (bf16[2,48,768]{2,1,0:T(8,128)(2,1)S(1)}, bf16[2,48,768]{2,1,0:T(8,128)(2,1)S(1)}, u32[]{:S(2)}, u32[]{:S(2)}) collective-permute-start(bf16[2,48,768]{2,1,0:T(8,128)(2,1)S(1)} %get-tuple-element.68), channel_id=1, source_target_pairs={{0,1},{1,0},{2,3},{3,2},{4,5},{5,4},{6,7},{7,6},{8,9},{9,8},{10,11... | collective-permute-start | bytes 442376 | tf_op jit(solution)/shard_map/ppermute | solution.py:412

commit v7 on v6

--- a/solution.py
+++ b/solution.py
@@ -67,8 +67,8 @@
     return me // SPREAD, lax.rem(me, SPREAD)
 
 
-def pack_kernel(queries_hbm, codes_hbm, exponents_hbm, *rest):
-    outs, (codes, queries, exponents, held, sems) = rest[:-5], rest[-5:]
+def pack_kernel(queries_hbm, codes_hbm, exponents_hbm, weight_hbm, *rest):
+    outs, early, (codes, queries, exponents, held, sems) = rest[:-6], rest[-6], rest[-5:]
     groups, kinds, rows, width = held.shape
     group, _ = place()
     per = width // HD
@@ -76,6 +76,7 @@
         pltpu.make_async_copy(exponents_hbm, exponents, sems.at[0]),
         pltpu.make_async_copy(codes_hbm, codes, sems.at[1]),
         pltpu.make_async_copy(queries_hbm, queries, sems.at[2]),
+        pltpu.make_async_copy(weight_hbm.at[0 : early.shape[0]], early, sems.at[3]),
     ]
     for copy in copies:
         copy.start()
@@ -98,9 +99,10 @@
         target = jnp.bitwise_xor(group, turn)
         outs[turn][...] = held[target, 0 : kinds - 1]
         outs[groups + turn][...] = held[target, kinds - 1]
-
-
-def pack(groups, queries, codes, exponents):
+    copies[3].wait()
+
+
+def pack(groups, queries, codes, exponents, weight, cut):
     rows, width = queries.shape
     kinds = codes.shape[0]
     share = width // groups
@@ -109,20 +111,21 @@
     outs = pl.pallas_call(
         pack_kernel,
         out_shape=[jax.ShapeDtypeStruct((kinds, rows, share), bf16)] * groups
-        + [jax.ShapeDtypeStruct((rows, share), bf16)] * groups,
-        in_specs=[HBM] * 3,
-        out_specs=[VMEM] * (2 * groups),
+        + [jax.ShapeDtypeStruct((rows, share), bf16)] * groups
+        + [jax.ShapeDtypeStruct((cut, weight.shape[1]), bf16)],
+        in_specs=[HBM] * 4,
+        out_specs=[VMEM] * (2 * groups + 1),
         scratch_shapes=[
             pltpu.VMEM(codes.shape, jnp.int32),
             pltpu.VMEM(queries.shape, bf16),
             pltpu.VMEM(exponents.shape, jnp.int32),
             pltpu.VMEM((groups, kinds + 1, rows, share), bf16),
-            pltpu.SemaphoreType.DMA((3,)),
+            pltpu.SemaphoreType.DMA((4,)),
         ],
         compiler_params=pltpu.CompilerParams(vmem_limit_bytes=PACK_LIMIT),
         cost_estimate=pl.CostEstimate(flops=2 * codes.size, bytes_accessed=6 * codes.size, transcendentals=0),
-    )(queries, codes, exponents)
-    return outs[:groups], outs[groups:]
+    )(queries, codes, exponents, weight)
+    return outs[:groups], outs[groups : 2 * groups], outs[-1]
 
 
 def pick_kernel(text_hbm, stale_hbm, text, stale, sems):
@@ -151,20 +154,16 @@
 
 
 def merge_kernel(*refs):
-    parts, (some, every) = refs[:-2], refs[-2:]
-    for index, part in enumerate(parts):
-        every[index] = part[...]
-        if index:
-            some[index - 1] = part[...]
+    for index, ref in enumerate(refs[:-1]):
+        refs[-1][index] = ref[...]
 
 
 def merge(parts):
-    shapes = [(count, *parts[0].shape) for count in (len(parts) - 1, len(parts))]
     return pl.pallas_call(
         merge_kernel,
-        out_shape=[jax.ShapeDtypeStruct(shape, parts[0].dtype) for shape in shapes],
+        out_shape=jax.ShapeDtypeStruct((len(parts), *parts[0].shape), parts[0].dtype),
         in_specs=[VMEM] * len(parts),
-        out_specs=[VMEM] * 2,
+        out_specs=VMEM,
         compiler_params=pltpu.CompilerParams(vmem_limit_bytes=SMALL),
         cost_estimate=pl.CostEstimate(flops=0, bytes_accessed=4 * len(parts) * parts[0].size, transcendentals=0),
     )(*parts)
@@ -188,22 +187,17 @@
 
 
 def attend_kernel(groups, *refs):
-    (every, near, own_far, some_far, own_corner, some_corner), refs = refs[:6], refs[6:]
+    pieces, refs = refs[:SPREAD], refs[SPREAD:]
     asked, (text, stale, out, most, last, query, residual) = refs[:groups], refs[groups:]
     group, spot = place()
     rows, width = asked[0].shape
     for turn in range(groups):
         origin = jnp.bitwise_xor(group, turn)
-        query[pl.ds(aligned(origin, rows), rows), :] = asked[turn][...]
+        position = (groups - turn) % groups
+        query[pl.ds(aligned(origin, rows), rows), :] = asked[position][...]
         for twist in range(SPREAD):
             token = origin * SPREAD + jnp.bitwise_xor(spot, twist)
-            if twist < 2:
-                part = (every, near)[twist][turn]
-            elif turn == 0:
-                part = (own_far, own_corner)[twist - 2][...]
-            else:
-                part = (some_far, some_corner)[twist - 2][turn - 1]
-            residual[:, pl.ds(aligned(token, rows), rows), :] = part
+            residual[:, pl.ds(aligned(token, rows), rows), :] = pieces[twist][position]
     for head in range(width // HD):
         cols = slice(head * HD, (head + 1) * HD)
         value = head_output(query[:, cols], text, stale, residual, cols)
@@ -241,15 +235,16 @@
     )(*pieces, *query_parts, text, stale)
 
 
-def order_kernel(*refs):
-    pieces, out = refs[:-1], refs[-1]
+def order_kernel(weight, near, early, late, early_corner, late_corner, out):
     _, spot = place()
-    span = out.shape[0] // SPREAD
-    for twist, piece in enumerate(pieces):
-        out[pl.ds(aligned(jnp.bitwise_xor(spot, twist), span), span), :] = piece[...]
-
-
-def order(pieces):
+    span, cut = weight.shape[0], early.shape[0]
+    pieces = [(0, 0, weight), (1, 0, near), (2, 0, early), (2, cut, late), (3, 0, early_corner), (3, cut, late_corner)]
+    for twist, skip, piece in pieces:
+        start = jnp.bitwise_xor(spot, twist) * span + skip
+        out[pl.ds(pl.multiple_of(start, 16), piece.shape[0]), :] = piece[...]
+
+
+def order(*pieces):
     span, depth = pieces[0].shape
     shape = (SPREAD * span, depth)
     return pl.pallas_call(
@@ -322,8 +317,8 @@
     group, _ = place()
     half = lax.axis_index("head")
     blocks = keep.shape[0]
-    for turn, part in enumerate(parts):
-        held[jnp.bitwise_xor(group, turn)] = part[...]
+    for position, part in enumerate(parts):
+        held[jnp.bitwise_xor(group, (len(parts) - position) % len(parts))] = part[...]
     for block in range(blocks):
         keep[block] = held[half * blocks + block]
         send[block] = held[(1 - half) * blocks + block]
@@ -376,35 +371,32 @@
         return lax.ppermute(value, "patch", [(p, p ^ twist) for p in range(size)])
 
     def along(values):
-        moved = {turn: swap(values[turn], turn * SPREAD) for turn in (3, 2, 1)}
-        return [moved[turn] for turn in range(1, groups)]
+        return [swap(values[turn], turn * SPREAD) for turn in reversed(range(1, groups))]
 
     weight = out_weight.T
-    weight_far = swap(weight, 2)
-    residuals, queries = pack(groups, queries, codes, exponents)
+    cut = weight.shape[0] // 48 * 32
+    residuals, queries, early = pack(groups, queries, codes, exponents, weight, cut)
     text, stale = pick(groups, text_kv, stale_kv)
 
-    own = residuals[0]
-    arrived = along(residuals)
-    own_far = swap(own, 2)
-
-    some, every = merge([own, *arrived])
-    some, every = lax.optimization_barrier((some, every, own_far, weight_far, text, stale))[:2]
-    queries = lax.optimization_barrier((*queries, some))[:groups]
-    some_far, near = swap(some, 2), swap(every, 1)
+    own = merge([residuals[0], *along(residuals)])
+    early = swap(early, 2)
+
+    own = after(own, text, stale, early)
+    queries = lax.optimization_barrier((*queries, own))[:groups]
+    far, near = swap(own, 2), swap(own, 1)
     asked = [queries[0], *along(queries)]
 
-    own_far, some_far = lax.optimization_barrier((own_far, some_far, near, *asked))[:2]
-    own_corner, some_corner = swap(own_far, 1), swap(some_far, 1)
-    weight, weight_far = lax.optimization_barrier((weight, weight_far, own_corner, some_corner))[:2]
-    weight_near, weight_corner = swap(weight, 1), swap(weight_far, 1)
-    full, most, last = attend([every, near, own_far, some_far, own_corner, some_corner], asked, text, stale)
-
-    across_most, across_last = swap(most, 2 * SPREAD), swap(last, 2 * SPREAD)
+    far, early = lax.optimization_barrier((far, early, near, *asked))[:2]
+    corner, early_corner = swap(far, 1), swap(early, 1)
+    weight = after(weight, corner, early_corner)
+    weight_near, late, late_corner = swap(weight, 1), swap(weight[cut:], 2), swap(weight[cut:], 3)
+    full, most, last = attend([own, near, far, corner], asked, text, stale)
+
+    across_most, across_last = swap(most, 2 * SPREAD), swap(after(last, weight_near), 2 * SPREAD)
     beside = swap(full, SPREAD)
     final_most = swap(across_most, SPREAD)
-    final_last = swap(after(across_last, beside, weight_near, weight_corner), SPREAD)
-    weight = order([weight, weight_near, weight_far, weight_corner])
+    final_last = swap(after(across_last, beside, late, late_corner), SPREAD)
+    weight = order(weight, weight_near, early, late, early_corner, late_corner)
     partial = begin([full, beside, across_most, across_last], weight)
     terms = close(groups, partial, [final_most, final_last], weight)
 

time: 63.8 us -> 62.1 us (0.973)
  waiting for transfers between devices: 29.5 us -> 24.1 us
  starting transfers between devices: 25.6 us -> 29.1 us
    ppermute x22, waiting for transfers between devices: 25.9 us -> 20.5 us  [swap(): return lax.ppermute(value, 'patch', [(p, p ^ twist) for p in range(size)])]
    ppermute x22, starting transfers between devices: 24 us -> 27.5 us  [swap(): return lax.ppermute(value, 'patch', [(p, p ^ twist) for p in range(size)])]
  transfers between devices with their start and end apart: 23 -> 23, of which waited for: 13 -> 12; matrix products, arithmetic and copies ran while one was open for 0% -> 0% of each run, Pallas kernels for 11% -> 8%
where the time goes in v7:
time: 62.1 us; the launch traced here: 61.9 us
  starting transfers between devices  29.1 us (47%)
  waiting for transfers between devices  24.1 us (39%)
  Pallas kernels  8.44 us (14%)
    ppermute x22, starting transfers between devices, swap(): return lax.ppermute(value, 'patch', [(p, p ^ twist) for p in range(size)])  27.5 us
    ppermute x22, waiting for transfers between devices, swap(): return lax.ppermute(value, 'patch', [(p, p ^ twist) for p in range(size)])  20.5 us
    ppermute x1, waiting for transfers between devices, grouped_body(): received = lax.ppermute(sent, 'head', [(0, 1), (1, 0)])  3.58 us
    pallas_call x1, Pallas kernels, pack(): pl.pallas_call(pack_kernel, out_shape=[jax.ShapeDtypeStruct((kinds, rows,...  2.49 us
    pallas_call x1, Pallas kernels, attend(): pl.pallas_call(functools.partial(attend_kernel, groups), out_shape=[jax.S...  2.34 us
    ppermute x1, starting transfers between devices, grouped_body(): received = lax.ppermute(sent, 'head', [(0, 1), (1, 0)])  1.59 us
    pallas_call x1, Pallas kernels, pick(): pl.pallas_call(pick_kernel, out_shape=[jax.ShapeDtypeStruct(shape, jnp.bf...  1.53 us
  transfers between devices with their start and end apart: 23, of which 12 were waited for; matrix products, arithmetic and copies ran while one was open for 0% of the time, Pallas kernels for 8%

profile of v7, /device:TPU:0, one launch (start us, length us, event | category | flops | bytes accessed | tf_op | source)
XLA Modules:
  0.0 61.9 jit_solution(11199886356528848157)
XLA Ops:
  0.0 2.5 %shard_map.82 = (bf16[2,48,384]{2,1,0:T(8,128)(2,1)}, bf16[2,48,384]{2,1,0:T(8,128)(2,1)}, bf16[2,48,384]{2,1,0:T(8,128)(2,1)}, bf16[2,48,384]{2,1,0:T(8,128)(2,...) custom-call(bf16[48,1536]{1,0:T(8,128)(2,1)} %queries_hbm.1, ...), custom_call_target="tpu_custom_call" | custom-call | flops 294912 | bytes 884736 | tf_op jit(solution)/shard_map/pallas_call | solution.py:111
  2.5 3.0 %collective-permute-start.3 = (bf16[128,1536]{1,0:T(8,128)(2,1)}, bf16[128,1536]{1,0:T(8,128)(2,1)S(1)}, u32[]{:S(2)}, u32[]{:S(2)}) collective-permute-start(bf16[128,1536]{1,0:T(8,128)(2,1)} %get-tuple-element.41), channel_id=1, source_target_pairs={{0,4},{2,6},{4,0},{6,2},{8,12},{10,14},{12,8},{14,10},{16,20},{18,... | collective-permute-start | bytes 1179656 | tf_op jit(solution)/shard_map/ppermute | solution.py:371
  5.5 3.6 %collective-permute-start = (bf16[2,48,384]{2,1,0:T(8,128)(2,1)}, bf16[2,48,384]{2,1,0:T(8,128)(2,1)S(1)}, u32[]{:S(2)}, u32[]{:S(2)}) collective-permute-start(bf16[2,48,384]{2,1,0:T(8,128)(2,1)} %get-tuple-element.36), channel_id=1, source_target_pairs={{0,24},{2,26},{4,28},{6,30},{8,16},{10,18},{12,20},{14,22},{16,8},... | collective-permute-start | bytes 221192 | tf_op jit(solution)/shard_map/ppermute | solution.py:371
  9.1 0.8 %collective-permute-start.2 = (bf16[2,48,384]{2,1,0:T(8,128)(2,1)}, bf16[2,48,384]{2,1,0:T(8,128)(2,1)S(1)}, u32[]{:S(2)}, u32[]{:S(2)}) collective-permute-start(bf16[2,48,384]{2,1,0:T(8,128)(2,1)} %get-tuple-element.38), channel_id=1, source_target_pairs={{0,8},{2,10},{4,12},{6,14},{8,0},{10,2},{12,4},{14,6},{16,24},{18,... | collective-permute-start | bytes 221192 | tf_op jit(solution)/shard_map/ppermute | solution.py:371
  10.0 1.5 %shard_map.84 = (bf16[2,512,384]{2,1,0:T(8,128)(2,1)S(1)}, bf16[2,768,384]{2,1,0:T(8,128)(2,1)S(1)}) custom-call(bf16[2,512,1536]{2,1,0:T(8,128)(2,1)} %text_hbm.1, bf16[2,768,1536]{2,1,0:T(8,128)(2,1)} %stale_hbm.1), custom_call_target="tpu_custom_call" | custom-call | bytes 8388608 | tf_op jit(solution)/shard_map/pallas_call | solution.py:145
  11.5 1.2 %collective-permute-done.refs_1_ = bf16[2,48,384]{2,1,0:T(8,128)(2,1)S(1)} collective-permute-done((bf16[2,48,384]{2,1,0:T(8,128)(2,1)}, bf16[2,48,384]{2,1,0:T(8,128)(2,1)S(1)}, u32[]{:S(2)}, u32[]{:S(2)}) %collective-permute-start) | collective-permute-done | bytes 73760 | tf_op jit(solution)/shard_map/ppermute | solution.py:371
  12.7 2.6 %collective-permute-done.1.refs_2_ = bf16[2,48,384]{2,1,0:T(8,128)(2,1)S(1)} collective-permute-done((bf16[2,48,384]{2,1,0:T(8,128)(2,1)}, bf16[2,48,384]{2,1,0:T(8,128)(2,1)S(1)}, u32[]{:S(2)}, u32[]{:S(2)}) %collective-permute-start.1) | collective-permute-done | bytes 73760 | tf_op jit(solution)/shard_map/ppermute | solution.py:371
  15.5 1.1 %collective-permute-start.5 = (bf16[4,2,48,384]{3,2,1,0:T(8,128)(2,1)S(1)}, bf16[4,2,48,384]{3,2,1,0:T(8,128)(2,1)S(1)}, u32[]{:S(2)}, u32[]{:S(2)}) collective-permute-start(bf16[4,2,48,384]{3,2,1,0:T(8,128)(2,1)S(1)} %shard_map.83.refs_0_), channel_id=1, source_target_pairs={{0,4},{2,6},{4,0},{6,2},{8,12},{10,14},{12,8},{14,10},{16,20},{18,... | collective-permute-start | bytes 884744 | tf_op jit(solution)/shard_map/ppermute | solution.py:371
  16.6 3.6 %collective-permute-start.6 = (bf16[48,384]{1,0:T(8,128)(2,1)S(1)}, bf16[48,384]{1,0:T(8,128)(2,1)S(1)}, u32[]{:S(2)}, u32[]{:S(2)}) collective-permute-start(bf16[48,384]{1,0:T(8,128)(2,1)S(1)} %copy-done.7), channel_id=1, source_target_pairs={{0,24},{2,26},{4,28},{6,30},{8,16},{10,18},{12,20},{14,22},{16,8},... | collective-permute-start | bytes 110600 | tf_op jit(solution)/shard_map/ppermute | solution.py:371
  20.2 0.8 %collective-permute-start.8 = (bf16[48,384]{1,0:T(8,128)(2,1)S(1)}, bf16[48,384]{1,0:T(8,128)(2,1)S(1)}, u32[]{:S(2)}, u32[]{:S(2)}) collective-permute-start(bf16[48,384]{1,0:T(8,128)(2,1)S(1)} %copy-done.5), channel_id=1, source_target_pairs={{0,8},{2,10},{4,12},{6,14},{8,0},{10,2},{12,4},{14,6},{16,24},{18,... | collective-permute-start | bytes 110600 | tf_op jit(solution)/shard_map/ppermute | solution.py:371
  21.0 1.4 %collective-permute-done.6.refs_5_ = bf16[48,384]{1,0:T(8,128)(2,1)S(1)} collective-permute-done((bf16[48,384]{1,0:T(8,128)(2,1)S(1)}, bf16[48,384]{1,0:T(8,128)(2,1)S(1)}, u32[]{:S(2)}, u32[]{:S(2)}) %collective-permute-start.6) | collective-permute-done | bytes 36896 | tf_op jit(solution)/shard_map/ppermute | solution.py:371
  22.3 2.7 %collective-permute-done.7.refs_6_ = bf16[48,384]{1,0:T(8,128)(2,1)S(1)} collective-permute-done((bf16[48,384]{1,0:T(8,128)(2,1)S(1)}, bf16[48,384]{1,0:T(8,128)(2,1)S(1)}, u32[]{:S(2)}, u32[]{:S(2)}) %collective-permute-start.7) | collective-permute-done | bytes 36896 | tf_op jit(solution)/shard_map/ppermute | solution.py:371
  25.1 0.5 collective-permute-start.9
  25.6 1.6 %collective-permute-done.9.refs_3_ = bf16[4,2,48,384]{3,2,1,0:T(8,128)(2,1)S(1)} collective-permute-done((bf16[4,2,48,384]{3,2,1,0:T(8,128)(2,1)S(1)}, bf16[4,2,48,384]{3,2,1,0:T(8,128)(2,1)S(1)}, u32[]{:S(2)}, u32[]{:S(2)}) %collective-permute-start.9) | collective-permute-done | bytes 294944 | tf_op jit(solution)/shard_map/ppermute | solution.py:371
  27.4 1.0 %collective-permute-start.15 = (bf16[64,1536]{1,0:T(8,128)(2,1)S(1)}, bf16[64,1536]{1,0:T(8,128)(2,1)S(1)}, u32[]{:S(2)}, u32[]{:S(2)}) collective-permute-start(bf16[64,1536]{1,0:T(8,128)(2,1)S(1)} %slice.4), channel_id=1, source_target_pairs={{0,4},{2,6},{4,0},{6,2},{8,12},{10,14},{12,8},{14,10},{16,20},{18,... | collective-permute-start | bytes 589832 | tf_op jit(solution)/shard_map/ppermute | solution.py:371
  28.4 0.8 %collective-permute-start.16 = (bf16[64,1536]{1,0:T(8,128)(2,1)S(1)}, bf16[64,1536]{1,0:T(8,128)(2,1)S(1)}, u32[]{:S(2)}, u32[]{:S(2)}) collective-permute-start(bf16[64,1536]{1,0:T(8,128)(2,1)S(1)} %slice.4), channel_id=1, source_target_pairs={{0,6},{2,4},{4,2},{6,0},{8,14},{10,12},{12,10},{14,8},{16,22},{18,... | collective-permute-start | bytes 589832 | tf_op jit(solution)/shard_map/ppermute | solution.py:371
  29.2 2.3 %shard_map.85 = (bf16[192,384]{1,0:T(8,128)(2,1)S(1)}, bf16[192,256]{1,0:T(8,128)(2,1)S(1)}, bf16[192,128]{1,0:T(8,128)(2,1)S(1)}) custom-call(bf16[4,2,48,384]{3,2,1,0:T(8,128)(2,1)S(1)} %shard_map.83.refs_0_, bf16[4,2,48,384]{3,2,1,0:T(8,128)(2,1)S(1)} %collective-permute-done.4.refs_1_, bf16[4,2,48,384]{3,2,1,0:T(8,128)(2,1)S(1)} %collective-permute-done.5.refs_2_, ...), custom_call_target="tpu_custom_call" | custom-call | flops 603979776 | bytes 3145728 | tf_op jit(solution)/shard_map/pallas_call | solution.py:227
  31.6 1.0 %collective-permute-start.10 = (bf16[192,384]{1,0:T(8,128)(2,1)S(1)}, bf16[192,384]{1,0:T(8,128)(2,1)S(1)}, u32[]{:S(2)}, u32[]{:S(2)}) collective-permute-start(bf16[192,384]{1,0:T(8,128)(2,1)S(1)} %get-tuple-element.52.full), channel_id=1, source_target_pairs={{0,8},{2,10},{4,12},{6,14},{8,0},{10,2},{12,4},{14,6},{16,24},{18,... | collective-permute-start | bytes 442376 | tf_op jit(solution)/shard_map/ppermute | solution.py:371
  32.6 2.6 %collective-permute-start.11 = (bf16[192,256]{1,0:T(8,128)(2,1)S(1)}, bf16[192,256]{1,0:T(8,128)(2,1)S(1)}, u32[]{:S(2)}, u32[]{:S(2)}) collective-permute-start(bf16[192,256]{1,0:T(8,128)(2,1)S(1)} %get-tuple-element.53), channel_id=1, source_target_pairs={{0,16},{2,18},{4,20},{6,22},{8,24},{10,26},{12,28},{14,30},{16,0},... | collective-permute-start | bytes 294920 | tf_op jit(solution)/shard_map/ppermute | solution.py:371
  35.5 3.4 %collective-permute-done.11.across_most = bf16[192,256]{1,0:T(8,128)(2,1)S(1)} collective-permute-done((bf16[192,256]{1,0:T(8,128)(2,1)S(1)}, bf16[192,256]{1,0:T(8,128)(2,1)S(1)}, u32[]{:S(2)}, u32[]{:S(2)}) %collective-permute-start.11) | collective-permute-done | bytes 98336 | tf_op jit(solution)/shard_map/ppermute | solution.py:371
  38.9 3.5 %collective-permute-start.17 = (bf16[192,256]{1,0:T(8,128)(2,1)S(1)}, bf16[192,256]{1,0:T(8,128)(2,1)S(1)}, u32[]{:S(2)}, u32[]{:S(2)}) collective-permute-start(bf16[192,256]{1,0:T(8,128)(2,1)S(1)} %collective-permute-done.11.across_most), channel_id=1, source_target_pairs={{0,8},{2,10},{4,12},{6,14},{8,0},{10,2},{12,4},{14,6},{16,24},{18,... | collective-permute-start | bytes 294920 | tf_op jit(solution)/shard_map/ppermute | solution.py:371
  42.5 0.5 collective-permute-done.14.across_last
  43.2 0.7 %shard_map.87.partial = f32[192,768]{1,0:T(8,128)S(1)} custom-call(bf16[192,384]{1,0:T(8,128)(2,1)S(1)} %get-tuple-element.52.full, bf16[192,384]{1,0:T(8,128)(2,1)S(1)} %collective-permute-done.10.beside, bf16[192,256]{1,0:T(8,128)(2,1)S(1)} %collective-permute-done.11.across_most, bf16[192,128]{1,0:T(8,128)(2,1)S(1)} %collective-permute-done.14.across_last, ...), custom_call_target="tpu_custom_call" | custom-call | flops 452984832 | bytes 589824 | tf_op jit(solution)/shard_map/pallas_call | solution.py:277
  44.0 1.6 %collective-permute-done.17.most = bf16[192,256]{1,0:T(8,128)(2,1)S(1)} collective-permute-done((bf16[192,256]{1,0:T(8,128)(2,1)S(1)}, bf16[192,256]{1,0:T(8,128)(2,1)S(1)}, u32[]{:S(2)}, u32[]{:S(2)}) %collective-permute-start.17) | collective-permute-done | bytes 98336 | tf_op jit(solution)/shard_map/ppermute | solution.py:371
  45.6 1.5 %collective-permute-done.18.last = bf16[192,128]{1,0:T(8,128)(2,1)S(1)} collective-permute-done((bf16[192,128]{1,0:T(8,128)(2,1)S(1)}, bf16[192,128]{1,0:T(8,128)(2,1)S(1)}, u32[]{:S(2)}, u32[]{:S(2)}) %collective-permute-start.18) | collective-permute-done | bytes 49184 | tf_op jit(solution)/shard_map/ppermute | solution.py:371
  47.5 2.8 %collective-permute-start.19 = (bf16[48,768]{1,0:T(8,128)(2,1)S(1)}, bf16[48,768]{1,0:T(8,128)(2,1)S(1)}, u32[]{:S(2)}, u32[]{:S(2)}) collective-permute-start(bf16[48,768]{1,0:T(8,128)(2,1)S(1)} %get-tuple-element.60), channel_id=1, source_target_pairs={{0,24},{2,26},{4,28},{6,30},{8,16},{10,18},{12,20},{14,22},{16,8},... | collective-permute-start | bytes 221192 | tf_op jit(solution)/shard_map/ppermute | solution.py:371
  50.3 1.7 %collective-permute-start.21 = (bf16[48,768]{1,0:T(8,128)(2,1)S(1)}, bf16[48,768]{1,0:T(8,128)(2,1)S(1)}, u32[]{:S(2)}, u32[]{:S(2)}) collective-permute-start(bf16[48,768]{1,0:T(8,128)(2,1)S(1)} %get-tuple-element.62), channel_id=1, source_target_pairs={{0,8},{2,10},{4,12},{6,14},{8,0},{10,2},{12,4},{14,6},{16,24},{18,... | collective-permute-start | bytes 221192 | tf_op jit(solution)/shard_map/ppermute | solution.py:371
  51.9 1.9 %collective-permute-done.19.refs_1_ = bf16[48,768]{1,0:T(8,128)(2,1)S(1)} collective-permute-done((bf16[48,768]{1,0:T(8,128)(2,1)S(1)}, bf16[48,768]{1,0:T(8,128)(2,1)S(1)}, u32[]{:S(2)}, u32[]{:S(2)}) %collective-permute-start.19) | collective-permute-done | bytes 73760 | tf_op jit(solution)/shard_map/ppermute | solution.py:371
  53.8 2.1 %collective-permute-done.20.refs_2_ = bf16[48,768]{1,0:T(8,128)(2,1)S(1)} collective-permute-done((bf16[48,768]{1,0:T(8,128)(2,1)S(1)}, bf16[48,768]{1,0:T(8,128)(2,1)S(1)}, u32[]{:S(2)}, u32[]{:S(2)}) %collective-permute-start.20) | collective-permute-done | bytes 73760 | tf_op jit(solution)/shard_map/ppermute | solution.py:371
  56.0 1.6 %collective-permute-start.22 = (bf16[2,48,768]{2,1,0:T(8,128)(2,1)S(1)}, bf16[2,48,768]{2,1,0:T(8,128)(2,1)S(1)}, u32[]{:S(2)}, u32[]{:S(2)}) collective-permute-start(bf16[2,48,768]{2,1,0:T(8,128)(2,1)S(1)} %get-tuple-element.64), channel_id=1, source_target_pairs={{0,1},{1,0},{2,3},{3,2},{4,5},{5,4},{6,7},{7,6},{8,9},{9,8},{10,11... | collective-permute-start | bytes 442376 | tf_op jit(solution)/shard_map/ppermute | solution.py:404
  57.6 3.6 %collective-permute-done.22.arrived = bf16[2,48,768]{2,1,0:T(8,128)(2,1)S(1)} collective-permute-done((bf16[2,48,768]{2,1,0:T(8,128)(2,1)S(1)}, bf16[2,48,768]{2,1,0:T(8,128)(2,1)S(1)}, u32[]{:S(2)}, u32[]{:S(2)}) %collective-permute-start.22) | collective-permute-done | bytes 147488 | tf_op jit(solution)/shard_map/ppermute | solution.py:404
  61.2 0.7 %shard_map.90 = bf16[48,1536]{1,0:T(8,128)(2,1)} custom-call(bf16[2,48,768]{2,1,0:T(8,128)(2,1)S(1)} %get-tuple-element.63.kept, bf16[2,48,768]{2,1,0:T(8,128)(2,1)S(1)} %collective-permute-done.22.arrived, f32[1,1536]{1,0:T(1,128)S(1)} %reshape.6.bias, f32[1,1536]{1,0:T(1,128)S(1)} %reshape.7.gate), custom_call_target="tpu_custom_call" | custom-call | flops 221184 | bytes 294912 | tf_op jit(solution)/shard_map/pallas_call | solution.py:352
  (42 shorter events, 1.4 us)
Async XLA Ops:
  2.5 12.9 %collective-permute-start.3 = (bf16[128,1536]{1,0:T(8,128)(2,1)}, bf16[128,1536]{1,0:T(8,128)(2,1)S(1)}, u32[]{:S(2)}, u32[]{:S(2)}) collective-permute-start(bf16[128,1536]{1,0:T(8,128)(2,1)} %get-tuple-element.41), channel_id=1, source_target_pairs={{0,4},{2,6},{4,0},{6,2},{8,12},{10,14},{12,8},{14,10},{16,20},{18,... | collective-permute-start | bytes 1179656 | tf_op jit(solution)/shard_map/ppermute | solution.py:371
  5.5 7.2 %collective-permute-start = (bf16[2,48,384]{2,1,0:T(8,128)(2,1)}, bf16[2,48,384]{2,1,0:T(8,128)(2,1)S(1)}, u32[]{:S(2)}, u32[]{:S(2)}) collective-permute-start(bf16[2,48,384]{2,1,0:T(8,128)(2,1)} %get-tuple-element.36), channel_id=1, source_target_pairs={{0,24},{2,26},{4,28},{6,30},{8,16},{10,18},{12,20},{14,22},{16,8},... | collective-permute-start | bytes 221192 | tf_op jit(solution)/shard_map/ppermute | solution.py:371
  9.1 6.2 %collective-permute-start.1 = (bf16[2,48,384]{2,1,0:T(8,128)(2,1)}, bf16[2,48,384]{2,1,0:T(8,128)(2,1)S(1)}, u32[]{:S(2)}, u32[]{:S(2)}) collective-permute-start(bf16[2,48,384]{2,1,0:T(8,128)(2,1)} %get-tuple-element.37), channel_id=1, source_target_pairs={{0,16},{2,18},{4,20},{6,22},{8,24},{10,26},{12,28},{14,30},{16,0},... | collective-permute-start | bytes 221192 | tf_op jit(solution)/shard_map/ppermute | solution.py:371
  9.1 6.3 %copy-start.1 = (bf16[2,48,384]{2,1,0:T(8,128)(2,1)S(1)}, bf16[2,48,384]{2,1,0:T(8,128)(2,1)}, u32[]{:S(2)}) copy-start(bf16[2,48,384]{2,1,0:T(8,128)(2,1)} %get-tuple-element.35.refs_0_) | copy-start | bytes 221188
  9.1 7.5 %copy-start.7 = (bf16[48,384]{1,0:T(8,128)(2,1)S(1)}, bf16[48,384]{1,0:T(8,128)(2,1)}, u32[]{:S(2)}) copy-start(bf16[48,384]{1,0:T(8,128)(2,1)} %get-tuple-element.48) | copy-start | bytes 110596
  9.1 11.1 %copy-start.6 = (bf16[48,384]{1,0:T(8,128)(2,1)S(1)}, bf16[48,384]{1,0:T(8,128)(2,1)}, u32[]{:S(2)}) copy-start(bf16[48,384]{1,0:T(8,128)(2,1)} %get-tuple-element.49) | copy-start | bytes 110596
  9.1 11.1 %copy-start.5 = (bf16[48,384]{1,0:T(8,128)(2,1)S(1)}, bf16[48,384]{1,0:T(8,128)(2,1)}, u32[]{:S(2)}) copy-start(bf16[48,384]{1,0:T(8,128)(2,1)} %get-tuple-element.50) | copy-start | bytes 110596
  9.1 18.1 %copy-start = (bf16[1536,192]{0,1:T(8,128)(2,1)S(1)}, bf16[1536,192]{0,1:T(8,128)(2,1)}, u32[]{:S(2)}) copy-start(bf16[1536,192]{0,1:T(8,128)(2,1)} %param.13) | copy-start | bytes 1769476
  9.1 20.1 %copy-start.2 = (bf16[48,384]{1,0:T(8,128)(2,1)S(1)}, bf16[48,384]{1,0:T(8,128)(2,1)}, u32[]{:S(2)}) copy-start(bf16[48,384]{1,0:T(8,128)(2,1)} %get-tuple-element.47.refs_4_) | copy-start | bytes 110596
  9.1 6.2 %collective-permute-start.2 = (bf16[2,48,384]{2,1,0:T(8,128)(2,1)}, bf16[2,48,384]{2,1,0:T(8,128)(2,1)S(1)}, u32[]{:S(2)}, u32[]{:S(2)}) collective-permute-start(bf16[2,48,384]{2,1,0:T(8,128)(2,1)} %get-tuple-element.38), channel_id=1, source_target_pairs={{0,8},{2,10},{4,12},{6,14},{8,0},{10,2},{12,4},{14,6},{16,24},{18,... | collective-permute-start | bytes 221192 | tf_op jit(solution)/shard_map/ppermute | solution.py:371
  15.4 9.6 %collective-permute-start.4 = (bf16[4,2,48,384]{3,2,1,0:T(8,128)(2,1)S(1)}, bf16[4,2,48,384]{3,2,1,0:T(8,128)(2,1)S(1)}, u32[]{:S(2)}, u32[]{:S(2)}) collective-permute-start(bf16[4,2,48,384]{3,2,1,0:T(8,128)(2,1)S(1)} %shard_map.83.refs_0_), channel_id=1, source_target_pairs={{0,2},{2,0},{4,6},{6,4},{8,10},{10,8},{12,14},{14,12},{16,18},{18,... | collective-permute-start | bytes 884744 | tf_op jit(solution)/shard_map/ppermute | solution.py:371
  15.5 9.6 %collective-permute-start.5 = (bf16[4,2,48,384]{3,2,1,0:T(8,128)(2,1)S(1)}, bf16[4,2,48,384]{3,2,1,0:T(8,128)(2,1)S(1)}, u32[]{:S(2)}, u32[]{:S(2)}) collective-permute-start(bf16[4,2,48,384]{3,2,1,0:T(8,128)(2,1)S(1)} %shard_map.83.refs_0_), channel_id=1, source_target_pairs={{0,4},{2,6},{4,0},{6,2},{8,12},{10,14},{12,8},{14,10},{16,20},{18,... | collective-permute-start | bytes 884744 | tf_op jit(solution)/shard_map/ppermute | solution.py:371
  16.6 5.8 %collective-permute-start.6 = (bf16[48,384]{1,0:T(8,128)(2,1)S(1)}, bf16[48,384]{1,0:T(8,128)(2,1)S(1)}, u32[]{:S(2)}, u32[]{:S(2)}) collective-permute-start(bf16[48,384]{1,0:T(8,128)(2,1)S(1)} %copy-done.7), channel_id=1, source_target_pairs={{0,24},{2,26},{4,28},{6,30},{8,16},{10,18},{12,20},{14,22},{16,8},... | collective-permute-start | bytes 110600 | tf_op jit(solution)/shard_map/ppermute | solution.py:371
  20.2 4.9 %collective-permute-start.7 = (bf16[48,384]{1,0:T(8,128)(2,1)S(1)}, bf16[48,384]{1,0:T(8,128)(2,1)S(1)}, u32[]{:S(2)}, u32[]{:S(2)}) collective-permute-start(bf16[48,384]{1,0:T(8,128)(2,1)S(1)} %copy-done.6), channel_id=1, source_target_pairs={{0,16},{2,18},{4,20},{6,22},{8,24},{10,26},{12,28},{14,30},{16,0},... | collective-permute-start | bytes 110600 | tf_op jit(solution)/shard_map/ppermute | solution.py:371
  20.2 4.9 %collective-permute-start.8 = (bf16[48,384]{1,0:T(8,128)(2,1)S(1)}, bf16[48,384]{1,0:T(8,128)(2,1)S(1)}, u32[]{:S(2)}, u32[]{:S(2)}) collective-permute-start(bf16[48,384]{1,0:T(8,128)(2,1)S(1)} %copy-done.5), channel_id=1, source_target_pairs={{0,8},{2,10},{4,12},{6,14},{8,0},{10,2},{12,4},{14,6},{16,24},{18,... | collective-permute-start | bytes 110600 | tf_op jit(solution)/shard_map/ppermute | solution.py:371
  25.0 2.2 %collective-permute-start.12 = (bf16[128,1536]{1,0:T(8,128)(2,1)S(1)}, bf16[128,1536]{1,0:T(8,128)(2,1)S(1)}, u32[]{:S(2)}, u32[]{:S(2)}) collective-permute-start(bf16[128,1536]{1,0:T(8,128)(2,1)S(1)} %collective-permute-done.3.early), channel_id=1, source_target_pairs={{0,2},{2,0},{4,6},{6,4},{8,10},{10,8},{12,14},{14,12},{16,18},{18,... | collective-permute-start | bytes 1179656 | tf_op jit(solution)/shard_map/ppermute | solution.py:371
  25.1 2.1 %collective-permute-start.9 = (bf16[4,2,48,384]{3,2,1,0:T(8,128)(2,1)S(1)}, bf16[4,2,48,384]{3,2,1,0:T(8,128)(2,1)S(1)}, u32[]{:S(2)}, u32[]{:S(2)}) collective-permute-start(bf16[4,2,48,384]{3,2,1,0:T(8,128)(2,1)S(1)} %collective-permute-done.5.refs_2_), channel_id=1, source_target_pairs={{0,2},{2,0},{4,6},{6,4},{8,10},{10,8},{12,14},{14,12},{16,18},{18,... | collective-permute-start | bytes 884744 | tf_op jit(solution)/shard_map/ppermute | solution.py:371
  27.3 7.9 %collective-permute-start.13 = (bf16[192,1536]{1,0:T(8,128)(2,1)S(1)}, bf16[192,1536]{1,0:T(8,128)(2,1)S(1)}, u32[]{:S(2)}, u32[]{:S(2)}) collective-permute-start(bf16[192,1536]{1,0:T(8,128)(2,1)S(1)} %bitcast.3), channel_id=1, source_target_pairs={{0,2},{2,0},{4,6},{6,4},{8,10},{10,8},{12,14},{14,12},{16,18},{18,... | collective-permute-start | bytes 1769480 | tf_op jit(solution)/shard_map/ppermute | solution.py:371
  27.4 15.0 %collective-permute-start.15 = (bf16[64,1536]{1,0:T(8,128)(2,1)S(1)}, bf16[64,1536]{1,0:T(8,128)(2,1)S(1)}, u32[]{:S(2)}, u32[]{:S(2)}) collective-permute-start(bf16[64,1536]{1,0:T(8,128)(2,1)S(1)} %slice.4), channel_id=1, source_target_pairs={{0,4},{2,6},{4,0},{6,2},{8,12},{10,14},{12,8},{14,10},{16,20},{18,... | collective-permute-start | bytes 589832 | tf_op jit(solution)/shard_map/ppermute | solution.py:371
  28.4 14.1 %collective-permute-start.16 = (bf16[64,1536]{1,0:T(8,128)(2,1)S(1)}, bf16[64,1536]{1,0:T(8,128)(2,1)S(1)}, u32[]{:S(2)}, u32[]{:S(2)}) collective-permute-start(bf16[64,1536]{1,0:T(8,128)(2,1)S(1)} %slice.4), channel_id=1, source_target_pairs={{0,6},{2,4},{4,2},{6,0},{8,14},{10,12},{12,10},{14,8},{16,22},{18,... | collective-permute-start | bytes 589832 | tf_op jit(solution)/shard_map/ppermute | solution.py:371
  31.6 10.9 %collective-permute-start.10 = (bf16[192,384]{1,0:T(8,128)(2,1)S(1)}, bf16[192,384]{1,0:T(8,128)(2,1)S(1)}, u32[]{:S(2)}, u32[]{:S(2)}) collective-permute-start(bf16[192,384]{1,0:T(8,128)(2,1)S(1)} %get-tuple-element.52.full), channel_id=1, source_target_pairs={{0,8},{2,10},{4,12},{6,14},{8,0},{10,2},{12,4},{14,6},{16,24},{18,... | collective-permute-start | bytes 442376 | tf_op jit(solution)/shard_map/ppermute | solution.py:371
  32.6 6.3 %collective-permute-start.11 = (bf16[192,256]{1,0:T(8,128)(2,1)S(1)}, bf16[192,256]{1,0:T(8,128)(2,1)S(1)}, u32[]{:S(2)}, u32[]{:S(2)}) collective-permute-start(bf16[192,256]{1,0:T(8,128)(2,1)S(1)} %get-tuple-element.53), channel_id=1, source_target_pairs={{0,16},{2,18},{4,20},{6,22},{8,24},{10,26},{12,28},{14,30},{16,0},... | collective-permute-start | bytes 294920 | tf_op jit(solution)/shard_map/ppermute | solution.py:371
  35.2 7.8 %collective-permute-start.14 = (bf16[192,128]{1,0:T(8,128)(2,1)S(1)}, bf16[192,128]{1,0:T(8,128)(2,1)S(1)}, u32[]{:S(2)}, u32[]{:S(2)}) collective-permute-start(bf16[192,128]{1,0:T(8,128)(2,1)S(1)} %get-tuple-element.57), channel_id=1, source_target_pairs={{0,16},{2,18},{4,20},{6,22},{8,24},{10,26},{12,28},{14,30},{16,0},... | collective-permute-start | bytes 147464 | tf_op jit(solution)/shard_map/ppermute | solution.py:371
  38.9 6.7 %collective-permute-start.17 = (bf16[192,256]{1,0:T(8,128)(2,1)S(1)}, bf16[192,256]{1,0:T(8,128)(2,1)S(1)}, u32[]{:S(2)}, u32[]{:S(2)}) collective-permute-start(bf16[192,256]{1,0:T(8,128)(2,1)S(1)} %collective-permute-done.11.across_most), channel_id=1, source_target_pairs={{0,8},{2,10},{4,12},{6,14},{8,0},{10,2},{12,4},{14,6},{16,24},{18,... | collective-permute-start | bytes 294920 | tf_op jit(solution)/shard_map/ppermute | solution.py:371
  43.0 4.1 %collective-permute-start.18 = (bf16[192,128]{1,0:T(8,128)(2,1)S(1)}, bf16[192,128]{1,0:T(8,128)(2,1)S(1)}, u32[]{:S(2)}, u32[]{:S(2)}) collective-permute-start(bf16[192,128]{1,0:T(8,128)(2,1)S(1)} %collective-permute-done.14.across_last), channel_id=1, source_target_pairs={{0,8},{2,10},{4,12},{6,14},{8,0},{10,2},{12,4},{14,6},{16,24},{18,... | collective-permute-start | bytes 147464 | tf_op jit(solution)/shard_map/ppermute | solution.py:371
  43.2 14.3 %copy-start.3 = (f32[1536]{0:T(1024)S(1)}, f32[1536]{0:T(1024)}, u32[]{:S(2)}) copy-start(f32[1536]{0:T(1024)} %param.14) | copy-start | bytes 18436
  43.2 14.3 %copy-start.4 = (f32[1536]{0:T(1024)S(1)}, f32[1536]{0:T(1024)}, u32[]{:S(2)}) copy-start(f32[1536]{0:T(1024)} %param.15) | copy-start | bytes 18436
  47.5 6.3 %collective-permute-start.19 = (bf16[48,768]{1,0:T(8,128)(2,1)S(1)}, bf16[48,768]{1,0:T(8,128)(2,1)S(1)}, u32[]{:S(2)}, u32[]{:S(2)}) collective-permute-start(bf16[48,768]{1,0:T(8,128)(2,1)S(1)} %get-tuple-element.60), channel_id=1, source_target_pairs={{0,24},{2,26},{4,28},{6,30},{8,16},{10,18},{12,20},{14,22},{16,8},... | collective-permute-start | bytes 221192 | tf_op jit(solution)/shard_map/ppermute | solution.py:371
  50.3 5.6 %collective-permute-start.20 = (bf16[48,768]{1,0:T(8,128)(2,1)S(1)}, bf16[48,768]{1,0:T(8,128)(2,1)S(1)}, u32[]{:S(2)}, u32[]{:S(2)}) collective-permute-start(bf16[48,768]{1,0:T(8,128)(2,1)S(1)} %get-tuple-element.61), channel_id=1, source_target_pairs={{0,16},{2,18},{4,20},{6,22},{8,24},{10,26},{12,28},{14,30},{16,0},... | collective-permute-start | bytes 221192 | tf_op jit(solution)/shard_map/ppermute | solution.py:371
  50.3 5.6 %collective-permute-start.21 = (bf16[48,768]{1,0:T(8,128)(2,1)S(1)}, bf16[48,768]{1,0:T(8,128)(2,1)S(1)}, u32[]{:S(2)}, u32[]{:S(2)}) collective-permute-start(bf16[48,768]{1,0:T(8,128)(2,1)S(1)} %get-tuple-element.62), channel_id=1, source_target_pairs={{0,8},{2,10},{4,12},{6,14},{8,0},{10,2},{12,4},{14,6},{16,24},{18,... | collective-permute-start | bytes 221192 | tf_op jit(solution)/shard_map/ppermute | solution.py:371
  56.0 5.2 %collective-permute-start.22 = (bf16[2,48,768]{2,1,0:T(8,128)(2,1)S(1)}, bf16[2,48,768]{2,1,0:T(8,128)(2,1)S(1)}, u32[]{:S(2)}, u32[]{:S(2)}) collective-permute-start(bf16[2,48,768]{2,1,0:T(8,128)(2,1)S(1)} %get-tuple-element.64), channel_id=1, source_target_pairs={{0,1},{1,0},{2,3},{3,2},{4,5},{5,4},{6,7},{7,6},{8,9},{9,8},{10,11... | collective-permute-start | bytes 442376 | tf_op jit(solution)/shard_map/ppermute | solution.py:404

commit v8 on v7

--- a/solution.py
+++ b/solution.py
@@ -97,8 +97,11 @@
         held[target, kinds - 1] = queries[:, target * width : (target + 1) * width]
     for turn in range(groups):
         target = jnp.bitwise_xor(group, turn)
-        outs[turn][...] = held[target, 0 : kinds - 1]
-        outs[groups + turn][...] = held[target, kinds - 1]
+        if turn == 1:
+            outs[turn][...] = held[target]
+        else:
+            outs[turn][...] = held[target, 0 : kinds - 1]
+            outs[groups + max(turn - 1, 0)][...] = held[target, kinds - 1]
     copies[3].wait()
 
 
@@ -108,13 +111,13 @@
     share = width // groups
     bf16 = jnp.bfloat16
     exponents = exponents.transpose(2, 0, 1)
+    residual, query = (kinds, rows, share), (rows, share)
+    shapes = [residual, (kinds + 1, rows, share)] + [residual] * (groups - 2) + [query] * (groups - 1) + [(cut, weight.shape[1])]
     outs = pl.pallas_call(
         pack_kernel,
-        out_shape=[jax.ShapeDtypeStruct((kinds, rows, share), bf16)] * groups
-        + [jax.ShapeDtypeStruct((rows, share), bf16)] * groups
-        + [jax.ShapeDtypeStruct((cut, weight.shape[1]), bf16)],
+        out_shape=[jax.ShapeDtypeStruct(shape, bf16) for shape in shapes],
         in_specs=[HBM] * 4,
-        out_specs=[VMEM] * (2 * groups + 1),
+        out_specs=[VMEM] * len(shapes),
         scratch_shapes=[
             pltpu.VMEM(codes.shape, jnp.int32),
             pltpu.VMEM(queries.shape, bf16),
@@ -125,7 +128,7 @@
         compiler_params=pltpu.CompilerParams(vmem_limit_bytes=PACK_LIMIT),
         cost_estimate=pl.CostEstimate(flops=2 * codes.size, bytes_accessed=6 * codes.size, transcendentals=0),
     )(queries, codes, exponents, weight)
-    return outs[:groups], outs[groups : 2 * groups], outs[-1]
+    return outs[:groups], outs[groups:-1], outs[-1]
 
 
 def pick_kernel(text_hbm, stale_hbm, text, stale, sems):
@@ -154,16 +157,23 @@
 
 
 def merge_kernel(*refs):
-    for index, ref in enumerate(refs[:-1]):
-        refs[-1][index] = ref[...]
+    parts, (out, query) = refs[:-2], refs[-2:]
+    kinds = out.shape[1]
+    for index, part in enumerate(parts):
+        out[index] = part[0:kinds]
+    query[...] = parts[-1][kinds]
 
 
 def merge(parts):
+    kinds, *block = parts[0].shape
     return pl.pallas_call(
         merge_kernel,
-        out_shape=jax.ShapeDtypeStruct((len(parts), *parts[0].shape), parts[0].dtype),
+        out_shape=[
+            jax.ShapeDtypeStruct((len(parts), kinds, *block), parts[0].dtype),
+            jax.ShapeDtypeStruct(tuple(block), parts[0].dtype),
+        ],
         in_specs=[VMEM] * len(parts),
-        out_specs=VMEM,
+        out_specs=[VMEM] * 2,
         compiler_params=pltpu.CompilerParams(vmem_limit_bytes=SMALL),
         cost_estimate=pl.CostEstimate(flops=0, bytes_accessed=4 * len(parts) * parts[0].size, transcendentals=0),
     )(*parts)
@@ -374,25 +384,25 @@
         return [swap(values[turn], turn * SPREAD) for turn in reversed(range(1, groups))]
 
     weight = out_weight.T
-    cut = weight.shape[0] // 48 * 32
-    residuals, queries, early = pack(groups, queries, codes, exponents, weight, cut)
+    cut = weight.shape[0] // 2
+    residuals, (asked_own, *asked_far), early = pack(groups, queries, codes, exponents, weight, cut)
     text, stale = pick(groups, text_kv, stale_kv)
-
-    own = merge([residuals[0], *along(residuals)])
-    early = swap(early, 2)
-
-    own = after(own, text, stale, early)
-    queries = lax.optimization_barrier((*queries, own))[:groups]
-    far, near = swap(own, 2), swap(own, 1)
-    asked = [queries[0], *along(queries)]
-
-    far, early = lax.optimization_barrier((far, early, near, *asked))[:2]
-    corner, early_corner = swap(far, 1), swap(early, 1)
-    weight = after(weight, corner, early_corner)
-    weight_near, late, late_corner = swap(weight, 1), swap(weight[cut:], 2), swap(weight[cut:], 3)
+    weight = after(weight, residuals[0])
+
+    own, asked_near = merge([residuals[0], *along(residuals)])
+    early, weight_near = swap(early, 2), swap(weight, 1)
+
+    own, early = lax.optimization_barrier((own, early, weight_near, text, stale))[:2]
+    asked_far = lax.optimization_barrier((*asked_far, own))[:-1]
+    far, near, early_corner = swap(own, 2), swap(own, 1), swap(early, 1)
+    asked_far = [swap(value, turn * SPREAD) for turn, value in reversed(list(enumerate(asked_far, 2)))]
+
+    far, weight = lax.optimization_barrier((far, weight, near, early_corner, *asked_far))[:2]
+    corner, late, late_corner = swap(far, 1), swap(weight[cut:], 2), swap(weight[cut:], 3)
+    asked = [asked_own, *asked_far, asked_near]
     full, most, last = attend([own, near, far, corner], asked, text, stale)
 
-    across_most, across_last = swap(most, 2 * SPREAD), swap(after(last, weight_near), 2 * SPREAD)
+    across_most, across_last = swap(most, 2 * SPREAD), swap(last, 2 * SPREAD)
     beside = swap(full, SPREAD)
     final_most = swap(across_most, SPREAD)
     final_last = swap(after(across_last, beside, late, late_corner), SPREAD)

time: 62.1 us -> 62.5 us (level)
  waiting for transfers between devices: 24.1 us -> 28.3 us
  starting transfers between devices: 29.1 us -> 25.3 us
    ppermute x22 -> x21, starting transfers between devices: 27.5 us -> 23.7 us  [swap(): return lax.ppermute(value, 'patch', [(p, p ^ twist) for p in range(size)])]
    ppermute x22 -> x21, waiting for transfers between devices: 20.5 us -> 24.2 us  [swap(): return lax.ppermute(value, 'patch', [(p, p ^ twist) for p in range(size)])]
  transfers between devices with their start and end apart: 23 -> 22, of which waited for: 12 -> 11; matrix products, arithmetic and copies ran while one was open for 0% -> 0% of each run, Pallas kernels for 8% -> 8%
where the time goes in v8:
time: 62.5 us; the launch traced here: 62.3 us
  waiting for transfers between devices  28.3 us (45%)
  starting transfers between devices  25.3 us (40%)
  Pallas kernels  8.45 us (14%)
    ppermute x21, waiting for transfers between devices, swap(): return lax.ppermute(value, 'patch', [(p, p ^ twist) for p in range(size)])  24.2 us
    ppermute x21, starting transfers between devices, swap(): return lax.ppermute(value, 'patch', [(p, p ^ twist) for p in range(size)])  23.7 us
    ppermute x1, waiting for transfers between devices, grouped_body(): received = lax.ppermute(sent, 'head', [(0, 1), (1, 0)])  4.07 us
    pallas_call x1, Pallas kernels, pack(): pl.pallas_call(pack_kernel, out_shape=[jax.ShapeDtypeStruct(shape, bf16)...  2.44 us
    pallas_call x1, Pallas kernels, attend(): pl.pallas_call(functools.partial(attend_kernel, groups), out_shape=[jax.S...  2.34 us
    ppermute x1, starting transfers between devices, grouped_body(): received = lax.ppermute(sent, 'head', [(0, 1), (1, 0)])  1.58 us
    pallas_call x1, Pallas kernels, pick(): pl.pallas_call(pick_kernel, out_shape=[jax.ShapeDtypeStruct(shape, jnp.bf...  1.58 us
  transfers between devices with their start and end apart: 22, of which 11 were waited for; matrix products, arithmetic and copies ran while one was open for 0% of the time, Pallas kernels for 8%

profile of v8, /device:TPU:0, one launch (start us, length us, event | category | flops | bytes accessed | tf_op | source)
XLA Modules:
  0.0 62.3 jit_solution(14890066929005082559)
XLA Ops:
  0.0 2.4 %shard_map.82 = (bf16[2,48,384]{2,1,0:T(8,128)(2,1)}, bf16[3,48,384]{2,1,0:T(8,128)(2,1)}, bf16[2,48,384]{2,1,0:T(8,128)(2,1)}, bf16[2,48,384]{2,1,0:T(8,128)(2,...) custom-call(bf16[48,1536]{1,0:T(8,128)(2,1)} %queries_hbm.1, ...), custom_call_target="tpu_custom_call" | custom-call | flops 294912 | bytes 884736 | tf_op jit(solution)/shard_map/pallas_call | solution.py:116
  2.4 0.5 collective-permute-start.4
  3.0 2.6 %collective-permute-start.3 = (bf16[96,1536]{1,0:T(8,128)(2,1)}, bf16[96,1536]{1,0:T(8,128)(2,1)S(1)}, u32[]{:S(2)}, u32[]{:S(2)}) collective-permute-start(bf16[96,1536]{1,0:T(8,128)(2,1)} %get-tuple-element.39), channel_id=1, source_target_pairs={{0,4},{2,6},{4,0},{6,2},{8,12},{10,14},{12,8},{14,10},{16,20},{18,... | collective-permute-start | bytes 884744 | tf_op jit(solution)/shard_map/ppermute | solution.py:381
  5.5 1.6 %collective-permute-start.2 = (bf16[3,48,384]{2,1,0:T(8,128)(2,1)}, bf16[3,48,384]{2,1,0:T(8,128)(2,1)S(1)}, u32[]{:S(2)}, u32[]{:S(2)}) collective-permute-start(bf16[3,48,384]{2,1,0:T(8,128)(2,1)} %get-tuple-element.37), channel_id=1, source_target_pairs={{0,8},{2,10},{4,12},{6,14},{8,0},{10,2},{12,4},{14,6},{16,24},{18,... | collective-permute-start | bytes 331784 | tf_op jit(solution)/shard_map/ppermute | solution.py:381
  7.1 2.5 %collective-permute-start = (bf16[2,48,384]{2,1,0:T(8,128)(2,1)}, bf16[2,48,384]{2,1,0:T(8,128)(2,1)S(1)}, u32[]{:S(2)}, u32[]{:S(2)}) collective-permute-start(bf16[2,48,384]{2,1,0:T(8,128)(2,1)} %get-tuple-element.35), channel_id=1, source_target_pairs={{0,24},{2,26},{4,28},{6,30},{8,16},{10,18},{12,20},{14,22},{16,8},... | collective-permute-start | bytes 221192 | tf_op jit(solution)/shard_map/ppermute | solution.py:381
  9.6 0.2 collective-permute-start.1
  9.8 1.6 %shard_map.84 = (bf16[2,512,384]{2,1,0:T(8,128)(2,1)S(1)}, bf16[2,768,384]{2,1,0:T(8,128)(2,1)S(1)}) custom-call(bf16[2,512,1536]{2,1,0:T(8,128)(2,1)} %text_hbm.1, bf16[2,768,1536]{2,1,0:T(8,128)(2,1)} %stale_hbm.1), custom_call_target="tpu_custom_call" | custom-call | bytes 8388608 | tf_op jit(solution)/shard_map/pallas_call | solution.py:148
  11.4 4.0 %collective-permute-done.refs_1_ = bf16[2,48,384]{2,1,0:T(8,128)(2,1)S(1)} collective-permute-done((bf16[2,48,384]{2,1,0:T(8,128)(2,1)}, bf16[2,48,384]{2,1,0:T(8,128)(2,1)S(1)}, u32[]{:S(2)}, u32[]{:S(2)}) %collective-permute-start) | collective-permute-done | bytes 73760 | tf_op jit(solution)/shard_map/ppermute | solution.py:381
  15.4 1.9 %collective-permute-done.1.refs_2_ = bf16[2,48,384]{2,1,0:T(8,128)(2,1)S(1)} collective-permute-done((bf16[2,48,384]{2,1,0:T(8,128)(2,1)}, bf16[2,48,384]{2,1,0:T(8,128)(2,1)S(1)}, u32[]{:S(2)}, u32[]{:S(2)}) %collective-permute-start.1) | collective-permute-done | bytes 73760 | tf_op jit(solution)/shard_map/ppermute | solution.py:381
  17.4 0.6 collective-permute-start.6
  18.2 2.5 %collective-permute-start.8 = (bf16[48,384]{1,0:T(8,128)(2,1)S(1)}, bf16[48,384]{1,0:T(8,128)(2,1)S(1)}, u32[]{:S(2)}, u32[]{:S(2)}) collective-permute-start(bf16[48,384]{1,0:T(8,128)(2,1)S(1)} %copy-done.6), channel_id=1, source_target_pairs={{0,24},{2,26},{4,28},{6,30},{8,16},{10,18},{12,20},{14,22},{16,8},... | collective-permute-start | bytes 110600 | tf_op jit(solution)/shard_map/ppermute | solution.py:381
  20.7 3.4 %collective-permute-done.8.refs_5_ = bf16[48,384]{1,0:T(8,128)(2,1)S(1)} collective-permute-done((bf16[48,384]{1,0:T(8,128)(2,1)S(1)}, bf16[48,384]{1,0:T(8,128)(2,1)S(1)}, u32[]{:S(2)}, u32[]{:S(2)}) %collective-permute-start.8) | collective-permute-done | bytes 36896 | tf_op jit(solution)/shard_map/ppermute | solution.py:381
  24.1 1.4 %collective-permute-done.9.refs_6_ = bf16[48,384]{1,0:T(8,128)(2,1)S(1)} collective-permute-done((bf16[48,384]{1,0:T(8,128)(2,1)S(1)}, bf16[48,384]{1,0:T(8,128)(2,1)S(1)}, u32[]{:S(2)}, u32[]{:S(2)}) %collective-permute-start.9) | collective-permute-done | bytes 36896 | tf_op jit(solution)/shard_map/ppermute | solution.py:381
  25.5 1.3 %collective-permute-done.6.refs_2_ = bf16[4,2,48,384]{3,2,1,0:T(8,128)(2,1)S(1)} collective-permute-done((bf16[4,2,48,384]{3,2,1,0:T(8,128)(2,1)S(1)}, bf16[4,2,48,384]{3,2,1,0:T(8,128)(2,1)S(1)}, u32[]{:S(2)}, u32[]{:S(2)}) %collective-permute-start.6) | collective-permute-done | bytes 294944 | tf_op jit(solution)/shard_map/ppermute | solution.py:381
  26.9 0.6 collective-permute-start.14
  27.5 1.3 %collective-permute-start.15 = (bf16[96,1536]{1,0:T(8,128)(2,1)S(1)}, bf16[96,1536]{1,0:T(8,128)(2,1)S(1)}, u32[]{:S(2)}, u32[]{:S(2)}) collective-permute-start(bf16[96,1536]{1,0:T(8,128)(2,1)S(1)} %slice.4), channel_id=1, source_target_pairs={{0,6},{2,4},{4,2},{6,0},{8,14},{10,12},{12,10},{14,8},{16,22},{18,... | collective-permute-start | bytes 884744 | tf_op jit(solution)/shard_map/ppermute | solution.py:381
  28.8 2.3 %shard_map.85 = (bf16[192,384]{1,0:T(8,128)(2,1)S(1)}, bf16[192,256]{1,0:T(8,128)(2,1)S(1)}, bf16[192,128]{1,0:T(8,128)(2,1)S(1)}) custom-call(bf16[4,2,48,384]{3,2,1,0:T(8,128)(2,1)S(1)} %get-tuple-element.43.refs_0_, bf16[4,2,48,384]{3,2,1,0:T(8,128)(2,1)S(1)} %collective-permute-done.5.refs_1_, ...), custom_call_target="tpu_custom_call" | custom-call | flops 603979776 | bytes 3145728 | tf_op jit(solution)/shard_map/pallas_call | solution.py:237
  31.2 3.0 %collective-permute-start.12 = (bf16[192,256]{1,0:T(8,128)(2,1)S(1)}, bf16[192,256]{1,0:T(8,128)(2,1)S(1)}, u32[]{:S(2)}, u32[]{:S(2)}) collective-permute-start(bf16[192,256]{1,0:T(8,128)(2,1)S(1)} %get-tuple-element.53), channel_id=1, source_target_pairs={{0,16},{2,18},{4,20},{6,22},{8,24},{10,26},{12,28},{14,30},{16,0},... | collective-permute-start | bytes 294920 | tf_op jit(solution)/shard_map/ppermute | solution.py:381
  34.3 3.2 %collective-permute-done.12.across_most = bf16[192,256]{1,0:T(8,128)(2,1)S(1)} collective-permute-done((bf16[192,256]{1,0:T(8,128)(2,1)S(1)}, bf16[192,256]{1,0:T(8,128)(2,1)S(1)}, u32[]{:S(2)}, u32[]{:S(2)}) %collective-permute-start.12) | collective-permute-done | bytes 98336 | tf_op jit(solution)/shard_map/ppermute | solution.py:381
  37.5 3.5 %collective-permute-start.16 = (bf16[192,256]{1,0:T(8,128)(2,1)S(1)}, bf16[192,256]{1,0:T(8,128)(2,1)S(1)}, u32[]{:S(2)}, u32[]{:S(2)}) collective-permute-start(bf16[192,256]{1,0:T(8,128)(2,1)S(1)} %collective-permute-done.12.across_most), channel_id=1, source_target_pairs={{0,8},{2,10},{4,12},{6,14},{8,0},{10,2},{12,4},{14,6},{16,24},{18,... | collective-permute-start | bytes 294920 | tf_op jit(solution)/shard_map/ppermute | solution.py:381
  41.1 1.2 %collective-permute-done.15.late_corner = bf16[96,1536]{1,0:T(8,128)(2,1)S(1)} collective-permute-done((bf16[96,1536]{1,0:T(8,128)(2,1)S(1)}, bf16[96,1536]{1,0:T(8,128)(2,1)S(1)}, u32[]{:S(2)}, u32[]{:S(2)}) %collective-permute-start.15) | collective-permute-done | bytes 294944 | tf_op jit(solution)/shard_map/ppermute | solution.py:381
  42.3 0.2 shard_map.86.weight
  42.5 0.7 %shard_map.87.partial = f32[192,768]{1,0:T(8,128)S(1)} custom-call(bf16[192,384]{1,0:T(8,128)(2,1)S(1)} %get-tuple-element.52.full, bf16[192,384]{1,0:T(8,128)(2,1)S(1)} %collective-permute-done.11.beside, bf16[192,256]{1,0:T(8,128)(2,1)S(1)} %collective-permute-done.12.across_most, bf16[192,128]{1,0:T(8,128)(2,1)S(1)} %collective-permute-done.13.across_last, ...), custom_call_target="tpu_custom_call" | custom-call | flops 452984832 | bytes 589824 | tf_op jit(solution)/shard_map/pallas_call | solution.py:287
  43.3 3.2 %collective-permute-done.17.last = bf16[192,128]{1,0:T(8,128)(2,1)S(1)} collective-permute-done((bf16[192,128]{1,0:T(8,128)(2,1)S(1)}, bf16[192,128]{1,0:T(8,128)(2,1)S(1)}, u32[]{:S(2)}, u32[]{:S(2)}) %collective-permute-start.17) | collective-permute-done | bytes 49184 | tf_op jit(solution)/shard_map/ppermute | solution.py:381
  46.5 0.4 shard_map.88
  46.9 2.7 %collective-permute-start.18 = (bf16[48,768]{1,0:T(8,128)(2,1)S(1)}, bf16[48,768]{1,0:T(8,128)(2,1)S(1)}, u32[]{:S(2)}, u32[]{:S(2)}) collective-permute-start(bf16[48,768]{1,0:T(8,128)(2,1)S(1)} %get-tuple-element.58), channel_id=1, source_target_pairs={{0,24},{2,26},{4,28},{6,30},{8,16},{10,18},{12,20},{14,22},{16,8},... | collective-permute-start | bytes 221192 | tf_op jit(solution)/shard_map/ppermute | solution.py:381
  49.6 1.7 %collective-permute-start.20 = (bf16[48,768]{1,0:T(8,128)(2,1)S(1)}, bf16[48,768]{1,0:T(8,128)(2,1)S(1)}, u32[]{:S(2)}, u32[]{:S(2)}) collective-permute-start(bf16[48,768]{1,0:T(8,128)(2,1)S(1)} %get-tuple-element.60), channel_id=1, source_target_pairs={{0,8},{2,10},{4,12},{6,14},{8,0},{10,2},{12,4},{14,6},{16,24},{18,... | collective-permute-start | bytes 221192 | tf_op jit(solution)/shard_map/ppermute | solution.py:381
  51.3 2.2 %collective-permute-done.18.refs_1_ = bf16[48,768]{1,0:T(8,128)(2,1)S(1)} collective-permute-done((bf16[48,768]{1,0:T(8,128)(2,1)S(1)}, bf16[48,768]{1,0:T(8,128)(2,1)S(1)}, u32[]{:S(2)}, u32[]{:S(2)}) %collective-permute-start.18) | collective-permute-done | bytes 73760 | tf_op jit(solution)/shard_map/ppermute | solution.py:381
  53.6 2.2 %collective-permute-done.19.refs_2_ = bf16[48,768]{1,0:T(8,128)(2,1)S(1)} collective-permute-done((bf16[48,768]{1,0:T(8,128)(2,1)S(1)}, bf16[48,768]{1,0:T(8,128)(2,1)S(1)}, u32[]{:S(2)}, u32[]{:S(2)}) %collective-permute-start.19) | collective-permute-done | bytes 73760 | tf_op jit(solution)/shard_map/ppermute | solution.py:381
  55.9 1.6 %collective-permute-start.21 = (bf16[2,48,768]{2,1,0:T(8,128)(2,1)S(1)}, bf16[2,48,768]{2,1,0:T(8,128)(2,1)S(1)}, u32[]{:S(2)}, u32[]{:S(2)}) collective-permute-start(bf16[2,48,768]{2,1,0:T(8,128)(2,1)S(1)} %get-tuple-element.62), channel_id=1, source_target_pairs={{0,1},{1,0},{2,3},{3,2},{4,5},{5,4},{6,7},{7,6},{8,9},{9,8},{10,11... | collective-permute-start | bytes 442376 | tf_op jit(solution)/shard_map/ppermute | solution.py:414
  57.5 4.1 %collective-permute-done.21.arrived = bf16[2,48,768]{2,1,0:T(8,128)(2,1)S(1)} collective-permute-done((bf16[2,48,768]{2,1,0:T(8,128)(2,1)S(1)}, bf16[2,48,768]{2,1,0:T(8,128)(2,1)S(1)}, u32[]{:S(2)}, u32[]{:S(2)}) %collective-permute-start.21) | collective-permute-done | bytes 147488 | tf_op jit(solution)/shard_map/ppermute | solution.py:414
  61.6 0.7 %shard_map.90 = bf16[48,1536]{1,0:T(8,128)(2,1)} custom-call(bf16[2,48,768]{2,1,0:T(8,128)(2,1)S(1)} %get-tuple-element.61.kept, bf16[2,48,768]{2,1,0:T(8,128)(2,1)S(1)} %collective-permute-done.21.arrived, f32[1,1536]{1,0:T(1,128)S(1)} %reshape.6.bias, f32[1,1536]{1,0:T(1,128)S(1)} %reshape.7.gate), custom_call_target="tpu_custom_call" | custom-call | flops 221184 | bytes 294912 | tf_op jit(solution)/shard_map/pallas_call | solution.py:362
  (38 shorter events, 0.5 us)
Async XLA Ops:
  2.4 14.9 %collective-permute-start.4 = (bf16[192,1536]{1,0:T(8,128)(2,1)}, bf16[192,1536]{1,0:T(8,128)(2,1)S(1)}, u32[]{:S(2)}, u32[]{:S(2)}) collective-permute-start(bf16[192,1536]{1,0:T(8,128)(2,1)} %bitcast.3), channel_id=1, source_target_pairs={{0,2},{2,0},{4,6},{6,4},{8,10},{10,8},{12,14},{14,12},{16,18},{18,... | collective-permute-start | bytes 1769480 | tf_op jit(solution)/shard_map/ppermute | solution.py:381
  3.0 14.4 %collective-permute-start.3 = (bf16[96,1536]{1,0:T(8,128)(2,1)}, bf16[96,1536]{1,0:T(8,128)(2,1)S(1)}, u32[]{:S(2)}, u32[]{:S(2)}) collective-permute-start(bf16[96,1536]{1,0:T(8,128)(2,1)} %get-tuple-element.39), channel_id=1, source_target_pairs={{0,4},{2,6},{4,0},{6,2},{8,12},{10,14},{12,8},{14,10},{16,20},{18,... | collective-permute-start | bytes 884744 | tf_op jit(solution)/shard_map/ppermute | solution.py:381
  5.5 11.8 %collective-permute-start.2 = (bf16[3,48,384]{2,1,0:T(8,128)(2,1)}, bf16[3,48,384]{2,1,0:T(8,128)(2,1)S(1)}, u32[]{:S(2)}, u32[]{:S(2)}) collective-permute-start(bf16[3,48,384]{2,1,0:T(8,128)(2,1)} %get-tuple-element.37), channel_id=1, source_target_pairs={{0,8},{2,10},{4,12},{6,14},{8,0},{10,2},{12,4},{14,6},{16,24},{18,... | collective-permute-start | bytes 331784 | tf_op jit(solution)/shard_map/ppermute | solution.py:381
  7.1 8.2 %collective-permute-start = (bf16[2,48,384]{2,1,0:T(8,128)(2,1)}, bf16[2,48,384]{2,1,0:T(8,128)(2,1)S(1)}, u32[]{:S(2)}, u32[]{:S(2)}) collective-permute-start(bf16[2,48,384]{2,1,0:T(8,128)(2,1)} %get-tuple-element.35), channel_id=1, source_target_pairs={{0,24},{2,26},{4,28},{6,30},{8,16},{10,18},{12,20},{14,22},{16,8},... | collective-permute-start | bytes 221192 | tf_op jit(solution)/shard_map/ppermute | solution.py:381
  9.6 7.7 %copy-start.1 = (bf16[2,48,384]{2,1,0:T(8,128)(2,1)S(1)}, bf16[2,48,384]{2,1,0:T(8,128)(2,1)}, u32[]{:S(2)}) copy-start(bf16[2,48,384]{2,1,0:T(8,128)(2,1)} %get-tuple-element.34.refs_0_) | copy-start | bytes 221188
  9.6 8.6 %copy-start.6 = (bf16[48,384]{1,0:T(8,128)(2,1)S(1)}, bf16[48,384]{1,0:T(8,128)(2,1)}, u32[]{:S(2)}) copy-start(bf16[48,384]{1,0:T(8,128)(2,1)} %get-tuple-element.47) | copy-start | bytes 110596
  9.6 11.1 %copy-start.5 = (bf16[48,384]{1,0:T(8,128)(2,1)S(1)}, bf16[48,384]{1,0:T(8,128)(2,1)}, u32[]{:S(2)}) copy-start(bf16[48,384]{1,0:T(8,128)(2,1)} %get-tuple-element.48) | copy-start | bytes 110596
  9.6 17.3 %copy-start = (bf16[1536,192]{0,1:T(8,128)(2,1)S(1)}, bf16[1536,192]{0,1:T(8,128)(2,1)}, u32[]{:S(2)}) copy-start(bf16[1536,192]{0,1:T(8,128)(2,1)} %param.13) | copy-start | bytes 1769476
  9.6 19.2 %copy-start.2 = (bf16[48,384]{1,0:T(8,128)(2,1)S(1)}, bf16[48,384]{1,0:T(8,128)(2,1)}, u32[]{:S(2)}) copy-start(bf16[48,384]{1,0:T(8,128)(2,1)} %get-tuple-element.50.refs_4_) | copy-start | bytes 110596
  9.6 7.7 %collective-permute-start.1 = (bf16[2,48,384]{2,1,0:T(8,128)(2,1)}, bf16[2,48,384]{2,1,0:T(8,128)(2,1)S(1)}, u32[]{:S(2)}, u32[]{:S(2)}) collective-permute-start(bf16[2,48,384]{2,1,0:T(8,128)(2,1)} %get-tuple-element.36), channel_id=1, source_target_pairs={{0,16},{2,18},{4,20},{6,22},{8,24},{10,26},{12,28},{14,30},{16,0},... | collective-permute-start | bytes 221192 | tf_op jit(solution)/shard_map/ppermute | solution.py:381
  17.4 8.2 %collective-permute-start.5 = (bf16[4,2,48,384]{3,2,1,0:T(8,128)(2,1)S(1)}, bf16[4,2,48,384]{3,2,1,0:T(8,128)(2,1)S(1)}, u32[]{:S(2)}, u32[]{:S(2)}) collective-permute-start(bf16[4,2,48,384]{3,2,1,0:T(8,128)(2,1)S(1)} %get-tuple-element.43.refs_0_), channel_id=1, source_target_pairs={{0,2},{2,0},{4,6},{6,4},{8,10},{10,8},{12,14},{14,12},{16,18},{18,... | collective-permute-start | bytes 884744 | tf_op jit(solution)/shard_map/ppermute | solution.py:381
  17.4 9.4 %collective-permute-start.6 = (bf16[4,2,48,384]{3,2,1,0:T(8,128)(2,1)S(1)}, bf16[4,2,48,384]{3,2,1,0:T(8,128)(2,1)S(1)}, u32[]{:S(2)}, u32[]{:S(2)}) collective-permute-start(bf16[4,2,48,384]{3,2,1,0:T(8,128)(2,1)S(1)} %get-tuple-element.43.refs_0_), channel_id=1, source_target_pairs={{0,4},{2,6},{4,0},{6,2},{8,12},{10,14},{12,8},{14,10},{16,20},{18,... | collective-permute-start | bytes 884744 | tf_op jit(solution)/shard_map/ppermute | solution.py:381
  18.0 8.8 %collective-permute-start.7 = (bf16[96,1536]{1,0:T(8,128)(2,1)S(1)}, bf16[96,1536]{1,0:T(8,128)(2,1)S(1)}, u32[]{:S(2)}, u32[]{:S(2)}) collective-permute-start(bf16[96,1536]{1,0:T(8,128)(2,1)S(1)} %collective-permute-done.3.early), channel_id=1, source_target_pairs={{0,2},{2,0},{4,6},{6,4},{8,10},{10,8},{12,14},{14,12},{16,18},{18,... | collective-permute-start | bytes 884744 | tf_op jit(solution)/shard_map/ppermute | solution.py:381
  18.2 5.9 %collective-permute-start.8 = (bf16[48,384]{1,0:T(8,128)(2,1)S(1)}, bf16[48,384]{1,0:T(8,128)(2,1)S(1)}, u32[]{:S(2)}, u32[]{:S(2)}) collective-permute-start(bf16[48,384]{1,0:T(8,128)(2,1)S(1)} %copy-done.6), channel_id=1, source_target_pairs={{0,24},{2,26},{4,28},{6,30},{8,16},{10,18},{12,20},{14,22},{16,8},... | collective-permute-start | bytes 110600 | tf_op jit(solution)/shard_map/ppermute | solution.py:381
  20.7 4.9 %collective-permute-start.9 = (bf16[48,384]{1,0:T(8,128)(2,1)S(1)}, bf16[48,384]{1,0:T(8,128)(2,1)S(1)}, u32[]{:S(2)}, u32[]{:S(2)}) collective-permute-start(bf16[48,384]{1,0:T(8,128)(2,1)S(1)} %copy-done.5), channel_id=1, source_target_pairs={{0,16},{2,18},{4,20},{6,22},{8,24},{10,26},{12,28},{14,30},{16,0},... | collective-permute-start | bytes 110600 | tf_op jit(solution)/shard_map/ppermute | solution.py:381
  26.9 2.0 %collective-permute-start.10 = (bf16[4,2,48,384]{3,2,1,0:T(8,128)(2,1)S(1)}, bf16[4,2,48,384]{3,2,1,0:T(8,128)(2,1)S(1)}, u32[]{:S(2)}, u32[]{:S(2)}) collective-permute-start(bf16[4,2,48,384]{3,2,1,0:T(8,128)(2,1)S(1)} %collective-permute-done.6.refs_2_), channel_id=1, source_target_pairs={{0,2},{2,0},{4,6},{6,4},{8,10},{10,8},{12,14},{14,12},{16,18},{18,... | collective-permute-start | bytes 884744 | tf_op jit(solution)/shard_map/ppermute | solution.py:381
  26.9 14.2 %collective-permute-start.14 = (bf16[96,1536]{1,0:T(8,128)(2,1)S(1)}, bf16[96,1536]{1,0:T(8,128)(2,1)S(1)}, u32[]{:S(2)}, u32[]{:S(2)}) collective-permute-start(bf16[96,1536]{1,0:T(8,128)(2,1)S(1)} %slice.4), channel_id=1, source_target_pairs={{0,4},{2,6},{4,0},{6,2},{8,12},{10,14},{12,8},{14,10},{16,20},{18,... | collective-permute-start | bytes 884744 | tf_op jit(solution)/shard_map/ppermute | solution.py:381
  27.5 14.8 %collective-permute-start.15 = (bf16[96,1536]{1,0:T(8,128)(2,1)S(1)}, bf16[96,1536]{1,0:T(8,128)(2,1)S(1)}, u32[]{:S(2)}, u32[]{:S(2)}) collective-permute-start(bf16[96,1536]{1,0:T(8,128)(2,1)S(1)} %slice.4), channel_id=1, source_target_pairs={{0,6},{2,4},{4,2},{6,0},{8,14},{10,12},{12,10},{14,8},{16,22},{18,... | collective-permute-start | bytes 884744 | tf_op jit(solution)/shard_map/ppermute | solution.py:381
  31.2 11.1 %collective-permute-start.11 = (bf16[192,384]{1,0:T(8,128)(2,1)S(1)}, bf16[192,384]{1,0:T(8,128)(2,1)S(1)}, u32[]{:S(2)}, u32[]{:S(2)}) collective-permute-start(bf16[192,384]{1,0:T(8,128)(2,1)S(1)} %get-tuple-element.52.full), channel_id=1, source_target_pairs={{0,8},{2,10},{4,12},{6,14},{8,0},{10,2},{12,4},{14,6},{16,24},{18,... | collective-permute-start | bytes 442376 | tf_op jit(solution)/shard_map/ppermute | solution.py:381
  31.2 6.3 %collective-permute-start.12 = (bf16[192,256]{1,0:T(8,128)(2,1)S(1)}, bf16[192,256]{1,0:T(8,128)(2,1)S(1)}, u32[]{:S(2)}, u32[]{:S(2)}) collective-permute-start(bf16[192,256]{1,0:T(8,128)(2,1)S(1)} %get-tuple-element.53), channel_id=1, source_target_pairs={{0,16},{2,18},{4,20},{6,22},{8,24},{10,26},{12,28},{14,30},{16,0},... | collective-permute-start | bytes 294920 | tf_op jit(solution)/shard_map/ppermute | solution.py:381
  34.3 8.0 %collective-permute-start.13 = (bf16[192,128]{1,0:T(8,128)(2,1)S(1)}, bf16[192,128]{1,0:T(8,128)(2,1)S(1)}, u32[]{:S(2)}, u32[]{:S(2)}) collective-permute-start(bf16[192,128]{1,0:T(8,128)(2,1)S(1)} %get-tuple-element.54), channel_id=1, source_target_pairs={{0,16},{2,18},{4,20},{6,22},{8,24},{10,26},{12,28},{14,30},{16,0},... | collective-permute-start | bytes 147464 | tf_op jit(solution)/shard_map/ppermute | solution.py:381
  37.5 8.9 %collective-permute-start.16 = (bf16[192,256]{1,0:T(8,128)(2,1)S(1)}, bf16[192,256]{1,0:T(8,128)(2,1)S(1)}, u32[]{:S(2)}, u32[]{:S(2)}) collective-permute-start(bf16[192,256]{1,0:T(8,128)(2,1)S(1)} %collective-permute-done.12.across_most), channel_id=1, source_target_pairs={{0,8},{2,10},{4,12},{6,14},{8,0},{10,2},{12,4},{14,6},{16,24},{18,... | collective-permute-start | bytes 294920 | tf_op jit(solution)/shard_map/ppermute | solution.py:381
  42.3 4.2 %collective-permute-start.17 = (bf16[192,128]{1,0:T(8,128)(2,1)S(1)}, bf16[192,128]{1,0:T(8,128)(2,1)S(1)}, u32[]{:S(2)}, u32[]{:S(2)}) collective-permute-start(bf16[192,128]{1,0:T(8,128)(2,1)S(1)} %collective-permute-done.13.across_last), channel_id=1, source_target_pairs={{0,8},{2,10},{4,12},{6,14},{8,0},{10,2},{12,4},{14,6},{16,24},{18,... | collective-permute-start | bytes 147464 | tf_op jit(solution)/shard_map/ppermute | solution.py:381
  42.5 14.9 %copy-start.3 = (f32[1536]{0:T(1024)S(1)}, f32[1536]{0:T(1024)}, u32[]{:S(2)}) copy-start(f32[1536]{0:T(1024)} %param.14) | copy-start | bytes 18436
  42.5 14.9 %copy-start.4 = (f32[1536]{0:T(1024)S(1)}, f32[1536]{0:T(1024)}, u32[]{:S(2)}) copy-start(f32[1536]{0:T(1024)} %param.15) | copy-start | bytes 18436
  46.9 6.7 %collective-permute-start.18 = (bf16[48,768]{1,0:T(8,128)(2,1)S(1)}, bf16[48,768]{1,0:T(8,128)(2,1)S(1)}, u32[]{:S(2)}, u32[]{:S(2)}) collective-permute-start(bf16[48,768]{1,0:T(8,128)(2,1)S(1)} %get-tuple-element.58), channel_id=1, source_target_pairs={{0,24},{2,26},{4,28},{6,30},{8,16},{10,18},{12,20},{14,22},{16,8},... | collective-permute-start | bytes 221192 | tf_op jit(solution)/shard_map/ppermute | solution.py:381
  49.6 6.2 %collective-permute-start.19 = (bf16[48,768]{1,0:T(8,128)(2,1)S(1)}, bf16[48,768]{1,0:T(8,128)(2,1)S(1)}, u32[]{:S(2)}, u32[]{:S(2)}) collective-permute-start(bf16[48,768]{1,0:T(8,128)(2,1)S(1)} %get-tuple-element.59), channel_id=1, source_target_pairs={{0,16},{2,18},{4,20},{6,22},{8,24},{10,26},{12,28},{14,30},{16,0},... | collective-permute-start | bytes 221192 | tf_op jit(solution)/shard_map/ppermute | solution.py:381
  49.6 6.2 %collective-permute-start.20 = (bf16[48,768]{1,0:T(8,128)(2,1)S(1)}, bf16[48,768]{1,0:T(8,128)(2,1)S(1)}, u32[]{:S(2)}, u32[]{:S(2)}) collective-permute-start(bf16[48,768]{1,0:T(8,128)(2,1)S(1)} %get-tuple-element.60), channel_id=1, source_target_pairs={{0,8},{2,10},{4,12},{6,14},{8,0},{10,2},{12,4},{14,6},{16,24},{18,... | collective-permute-start | bytes 221192 | tf_op jit(solution)/shard_map/ppermute | solution.py:381
  55.9 5.7 %collective-permute-start.21 = (bf16[2,48,768]{2,1,0:T(8,128)(2,1)S(1)}, bf16[2,48,768]{2,1,0:T(8,128)(2,1)S(1)}, u32[]{:S(2)}, u32[]{:S(2)}) collective-permute-start(bf16[2,48,768]{2,1,0:T(8,128)(2,1)S(1)} %get-tuple-element.62), channel_id=1, source_target_pairs={{0,1},{1,0},{2,3},{3,2},{4,5},{5,4},{6,7},{7,6},{8,9},{9,8},{10,11... | collective-permute-start | bytes 442376 | tf_op jit(solution)/shard_map/ppermute | solution.py:414

commit v9 on v7

--- a/solution.py
+++ b/solution.py
@@ -96,9 +96,8 @@
     for target in range(groups):
         held[target, kinds - 1] = queries[:, target * width : (target + 1) * width]
     for turn in range(groups):
-        target = jnp.bitwise_xor(group, turn)
-        outs[turn][...] = held[target, 0 : kinds - 1]
-        outs[groups + turn][...] = held[target, kinds - 1]
+        outs[turn][...] = held[jnp.bitwise_xor(group, turn)]
+    outs[groups][...] = held[group, 0 : kinds - 1]
     copies[3].wait()
 
 
@@ -108,13 +107,12 @@
     share = width // groups
     bf16 = jnp.bfloat16
     exponents = exponents.transpose(2, 0, 1)
+    shapes = [(kinds + 1, rows, share)] * groups + [(kinds, rows, share), (cut, weight.shape[1])]
     outs = pl.pallas_call(
         pack_kernel,
-        out_shape=[jax.ShapeDtypeStruct((kinds, rows, share), bf16)] * groups
-        + [jax.ShapeDtypeStruct((rows, share), bf16)] * groups
-        + [jax.ShapeDtypeStruct((cut, weight.shape[1]), bf16)],
+        out_shape=[jax.ShapeDtypeStruct(shape, bf16) for shape in shapes],
         in_specs=[HBM] * 4,
-        out_specs=[VMEM] * (2 * groups + 1),
+        out_specs=[VMEM] * len(shapes),
         scratch_shapes=[
             pltpu.VMEM(codes.shape, jnp.int32),
             pltpu.VMEM(queries.shape, bf16),
@@ -125,114 +123,168 @@
         compiler_params=pltpu.CompilerParams(vmem_limit_bytes=PACK_LIMIT),
         cost_estimate=pl.CostEstimate(flops=2 * codes.size, bytes_accessed=6 * codes.size, transcendentals=0),
     )(queries, codes, exponents, weight)
-    return outs[:groups], outs[groups : 2 * groups], outs[-1]
+    return outs
 
 
 def pick_kernel(text_hbm, stale_hbm, text, stale, sems):
-    group, _ = place()
+    group, spot = place()
     width = text.shape[2]
+    groups = text_hbm.shape[2] // width
+    rows = stale.shape[2] // groups
     columns = pl.ds(aligned(group, width), width)
-    text_copy = pltpu.make_async_copy(text_hbm.at[:, :, columns], text, sems.at[0])
-    stale_copy = pltpu.make_async_copy(stale_hbm.at[:, :, columns], stale, sems.at[1])
-    text_copy.start()
-    stale_copy.start()
-    text_copy.wait()
-    stale_copy.wait()
+    copies = [pltpu.make_async_copy(text_hbm.at[:, :, columns], text, sems.at[0])]
+    for twist in range(SPREAD):
+        for position in range(groups):
+            origin = jnp.bitwise_xor(group, (groups - position) % groups)
+            token = origin * SPREAD + jnp.bitwise_xor(spot, twist)
+            copies.append(
+                pltpu.make_async_copy(
+                    stale_hbm.at[:, pl.ds(aligned(token, rows), rows), columns],
+                    stale.at[twist, :, pl.ds(position * rows, rows), :],
+                    sems.at[len(copies)],
+                )
+            )
+    for copy in copies:
+        copy.start()
+    for copy in copies:
+        copy.wait()
 
 
 def pick(groups, text_kv, stale_kv):
-    shapes = [(2, value.shape[1], value.shape[2] // groups) for value in (text_kv, stale_kv)]
+    kinds, texts, heads_width = text_kv.shape
+    width = heads_width // groups
     return pl.pallas_call(
         pick_kernel,
-        out_shape=[jax.ShapeDtypeStruct(shape, jnp.bfloat16) for shape in shapes],
+        out_shape=[
+            jax.ShapeDtypeStruct((kinds, texts, width), jnp.bfloat16),
+            jax.ShapeDtypeStruct((SPREAD, kinds, stale_kv.shape[1] // SPREAD, width), jnp.bfloat16),
+        ],
         in_specs=[HBM] * 2,
         out_specs=[VMEM] * 2,
-        scratch_shapes=[pltpu.SemaphoreType.DMA((2,))],
+        scratch_shapes=[pltpu.SemaphoreType.DMA((1 + SPREAD * groups,))],
         compiler_params=pltpu.CompilerParams(vmem_limit_bytes=PICK_LIMIT),
         cost_estimate=pl.CostEstimate(flops=0, bytes_accessed=8 << 20, transcendentals=0),
     )(text_kv, stale_kv)
 
 
 def merge_kernel(*refs):
-    for index, ref in enumerate(refs[:-1]):
-        refs[-1][index] = ref[...]
+    parts, (every, some, query) = refs[:-3], refs[-3:]
+    groups, kinds, rows, _ = every.shape
+    group, _ = place()
+    for position, part in enumerate(parts):
+        every[position] = part[0:kinds]
+        if position:
+            some[position - 1] = part[0:kinds]
+        origin = jnp.bitwise_xor(group, (groups - position) % groups)
+        query[pl.ds(aligned(origin, rows), rows), :] = part[kinds]
 
 
 def merge(parts):
+    kinds, rows, width = parts[0].shape
+    shapes = [(len(parts), kinds - 1, rows, width), (len(parts) - 1, kinds - 1, rows, width), (len(parts) * rows, width)]
     return pl.pallas_call(
         merge_kernel,
-        out_shape=jax.ShapeDtypeStruct((len(parts), *parts[0].shape), parts[0].dtype),
+        out_shape=[jax.ShapeDtypeStruct(shape, jnp.bfloat16) for shape in shapes],
         in_specs=[VMEM] * len(parts),
-        out_specs=VMEM,
+        out_specs=[VMEM] * 3,
         compiler_params=pltpu.CompilerParams(vmem_limit_bytes=SMALL),
         cost_estimate=pl.CostEstimate(flops=0, bytes_accessed=4 * len(parts) * parts[0].size, transcendentals=0),
     )(*parts)
 
 
-def head_output(query, text, stale, residual, cols):
-    text_scores = lax.dot_general(query, text[0, :, cols], NT, preferred_element_type=jnp.float32)
-    image_scores = lax.dot_general(query, stale[0, :, cols], NT, preferred_element_type=jnp.float32)
-    image_scores += lax.dot_general(query, residual[0, :, cols], NT, preferred_element_type=jnp.float32)
-    text_scores *= HD**-0.5
-    image_scores *= HD**-0.5
-    peak = jnp.maximum(jnp.max(text_scores, axis=1, keepdims=True), jnp.max(image_scores, axis=1, keepdims=True))
-    text_weights = jnp.exp(text_scores - peak).astype(jnp.bfloat16)
-    image_weights = jnp.exp(image_scores - peak).astype(jnp.bfloat16)
-    total = jnp.sum(text_weights.astype(jnp.float32), axis=1, keepdims=True)
-    total += jnp.sum(image_weights.astype(jnp.float32), axis=1, keepdims=True)
-    mixed = jnp.dot(text_weights, text[1, :, cols], preferred_element_type=jnp.float32)
-    mixed += jnp.dot(image_weights, stale[1, :, cols], preferred_element_type=jnp.float32)
-    mixed += jnp.dot(image_weights, residual[1, :, cols], preferred_element_type=jnp.float32)
-    return (mixed / total).astype(jnp.bfloat16)
-
-
-def attend_kernel(groups, *refs):
-    pieces, refs = refs[:SPREAD], refs[SPREAD:]
-    asked, (text, stale, out, most, last, query, residual) = refs[:groups], refs[groups:]
-    group, spot = place()
-    rows, width = asked[0].shape
-    for turn in range(groups):
-        origin = jnp.bitwise_xor(group, turn)
-        position = (groups - turn) % groups
-        query[pl.ds(aligned(origin, rows), rows), :] = asked[position][...]
-        for twist in range(SPREAD):
-            token = origin * SPREAD + jnp.bitwise_xor(spot, twist)
-            residual[:, pl.ds(aligned(token, rows), rows), :] = pieces[twist][position]
-    for head in range(width // HD):
+def absorb(query, segments, state):
+    scores = []
+    for keys, _ in segments:
+        score = sum(lax.dot_general(query, key, NT, preferred_element_type=jnp.float32) for key in keys)
+        scores.append(score * HD**-0.5)
+    peaks = [jnp.max(score, axis=1, keepdims=True) for score in scores]
+    if state is not None:
+        peaks.append(state[0])
+    peak = functools.reduce(jnp.maximum, peaks)
+    total = mixed = 0.0
+    if state is not None:
+        fade = jnp.exp(state[0] - peak)
+        total, mixed = state[1] * fade, state[2] * fade
+    for score, (_, values) in zip(scores, segments):
+        weights = jnp.exp(score - peak).astype(jnp.bfloat16)
+        total += jnp.sum(weights.astype(jnp.float32), axis=1, keepdims=True)
+        for value in values:
+            mixed += jnp.dot(weights, value, preferred_element_type=jnp.float32)
+    return peak, total, mixed
+
+
+def image_segment(stale, twist, residual, cols):
+    both = [(stale[twist, kind, :, cols], residual(kind)) for kind in range(2)]
+    return both[0], both[1]
+
+
+def whole_part(part, cols):
+    return lambda kind: part[:, kind, :, cols].reshape(-1, HD)
+
+
+def split_part(own, some, cols):
+    return lambda kind: jnp.concatenate([own[kind, :, cols], some[:, kind, :, cols].reshape(-1, HD)], axis=0)
+
+
+def near_kernel(query, every, text, stale, peak, total, mixed):
+    for head in range(mixed.shape[0]):
         cols = slice(head * HD, (head + 1) * HD)
-        value = head_output(query[:, cols], text, stale, residual, cols)
-        out[:, cols] = value
-        if head < width // HD - 1:
+        segments = [
+            ((text[0, :, cols],), (text[1, :, cols],)),
+            image_segment(stale, 0, whole_part(every, cols), cols),
+        ]
+        peak[head], total[head], mixed[head] = absorb(query[:, cols], segments, None)
+
+
+def middle_kernel(query, near, own_far, some_far, stale, peak_in, total_in, mixed_in, peak, total, mixed):
+    for head in range(mixed.shape[0]):
+        cols = slice(head * HD, (head + 1) * HD)
+        segments = [
+            image_segment(stale, 1, whole_part(near, cols), cols),
+            image_segment(stale, 2, split_part(own_far, some_far, cols), cols),
+        ]
+        state = peak_in[head], total_in[head], mixed_in[head]
+        peak[head], total[head], mixed[head] = absorb(query[:, cols], segments, state)
+
+
+def last_kernel(query, own_corner, some_corner, stale, peak, total, mixed, full, most, last):
+    heads = mixed.shape[0]
+    for head in range(heads):
+        cols = slice(head * HD, (head + 1) * HD)
+        segments = [image_segment(stale, 3, split_part(own_corner, some_corner, cols), cols)]
+        state = peak[head], total[head], mixed[head]
+        _, sums, mix = absorb(query[:, cols], segments, state)
+        value = (mix / sums).astype(jnp.bfloat16)
+        full[:, cols] = value
+        if head < heads - 1:
             most[:, cols] = value
         else:
             last[...] = value
 
 
-def attend_cost(heads, tokens, texts, keys):
-    return pl.CostEstimate(
-        flops=4 * heads * tokens * HD * (texts + 2 * keys),
-        bytes_accessed=4 * heads * HD * (texts + 2 * keys),
-        transcendentals=heads * tokens * (texts + keys),
-    )
-
-
-def attend(pieces, query_parts, text, stale):
-    groups = len(query_parts)
-    rows, width = query_parts[0].shape
-    tokens = groups * rows
-    keys = stale.shape[1]
-    texts = text.shape[1]
+def attend_call(kernel, operands, shapes, keys):
+    tokens, width = operands[0].shape
+    return pl.pallas_call(
+        kernel,
+        out_shape=shapes,
+        in_specs=[VMEM] * len(operands),
+        out_specs=[VMEM] * len(shapes),
+        compiler_params=pltpu.CompilerParams(vmem_limit_bytes=SMALL),
+        cost_estimate=pl.CostEstimate(
+            flops=8 * tokens * width * keys, bytes_accessed=8 * width * keys, transcendentals=tokens * keys * width // HD
+        ),
+    )(*operands)
+
+
+def state_shapes(query):
+    tokens, width = query.shape
     heads = width // HD
-
-    return pl.pallas_call(
-        functools.partial(attend_kernel, groups),
-        out_shape=[jax.ShapeDtypeStruct((tokens, size), jnp.bfloat16) for size in (width, width - HD, HD)],
-        in_specs=[VMEM] * (len(pieces) + groups + 2),
-        out_specs=[VMEM] * 3,
-        scratch_shapes=[pltpu.VMEM((tokens, width), jnp.bfloat16), pltpu.VMEM((2, keys, width), jnp.bfloat16)],
-        compiler_params=pltpu.CompilerParams(vmem_limit_bytes=SMALL),
-        cost_estimate=attend_cost(heads, tokens, texts, keys),
-    )(*pieces, *query_parts, text, stale)
+    return [jax.ShapeDtypeStruct((heads, tokens, size), jnp.float32) for size in (1, 1, HD)]
+
+
+def result_shapes(query):
+    tokens, width = query.shape
+    return [jax.ShapeDtypeStruct((tokens, size), jnp.bfloat16) for size in (width, width - HD, HD)]
 
 
 def order_kernel(weight, near, early, late, early_corner, late_corner, out):
@@ -375,24 +427,28 @@
 
     weight = out_weight.T
     cut = weight.shape[0] // 48 * 32
-    residuals, queries, early = pack(groups, queries, codes, exponents, weight, cut)
+    *packed, own, early = pack(groups, queries, codes, exponents, weight, cut)
     text, stale = pick(groups, text_kv, stale_kv)
 
-    own = merge([residuals[0], *along(residuals)])
-    early = swap(early, 2)
-
-    own = after(own, text, stale, early)
-    queries = lax.optimization_barrier((*queries, own))[:groups]
-    far, near = swap(own, 2), swap(own, 1)
-    asked = [queries[0], *along(queries)]
-
-    far, early = lax.optimization_barrier((far, early, near, *asked))[:2]
-    corner, early_corner = swap(far, 1), swap(early, 1)
-    weight = after(weight, corner, early_corner)
-    weight_near, late, late_corner = swap(weight, 1), swap(weight[cut:], 2), swap(weight[cut:], 3)
-    full, most, last = attend([own, near, far, corner], asked, text, stale)
-
-    across_most, across_last = swap(most, 2 * SPREAD), swap(after(last, weight_near), 2 * SPREAD)
+    every, some, query = merge([packed[0], *along(packed)])
+    own_far, early = swap(own, 2), swap(early, 2)
+
+    every, some, early, query = lax.optimization_barrier((every, some, early, query, own_far, text, stale))[:4]
+    some_far, near = swap(some, 2), swap(every, 1)
+    weight, early = lax.optimization_barrier((weight, early, near))[:2]
+    early_corner, weight_near = swap(early, 1), swap(weight, 1)
+    share = stale.shape[2]
+    state = attend_call(near_kernel, [query, every, text, stale], state_shapes(query), share + text.shape[1])
+
+    ready = (own_far, some_far, weight, near, early_corner, weight_near, *state)
+    own_far, some_far, weight, near = lax.optimization_barrier(ready)[:4]
+    own_corner, some_corner = swap(own_far, 1), swap(some_far, 1)
+    late, late_corner = swap(weight[cut:], 2), swap(weight[cut:], 3)
+    state = attend_call(middle_kernel, [query, near, own_far, some_far, stale, *state], state_shapes(query), 2 * share)
+    operands = [query, own_corner, some_corner, stale, *state]
+    full, most, last = attend_call(last_kernel, operands, result_shapes(query), share)
+
+    across_most, across_last = swap(most, 2 * SPREAD), swap(last, 2 * SPREAD)
     beside = swap(full, SPREAD)
     final_most = swap(across_most, SPREAD)
     final_last = swap(after(across_last, beside, late, late_corner), SPREAD)

time: 62.1 us -> 63.3 us (1.019)
  starting transfers between devices: 29.1 us -> 23.4 us
  waiting for transfers between devices: 24.1 us -> 28.8 us
  Pallas kernels: 8.44 us -> 10.6 us
    ppermute x22 -> x21, starting transfers between devices: 27.5 us -> 21.9 us  [swap(): return lax.ppermute(value, 'patch', [(p, p ^ twist) for p in range(size)])]
    ppermute x22 -> x21, waiting for transfers between devices: 20.5 us -> 25.2 us  [swap(): return lax.ppermute(value, 'patch', [(p, p ^ twist) for p in range(size)])]
    pallas_call x4 -> x6, Pallas kernels: 6.39 us -> 8.54 us  [the longest x3 4.32 us: attend_call(): pl.pallas_call(kernel, out_shape=shapes, in_specs=[VMEM] * len(operands),...]
  transfers between devices with their start and end apart: 23 -> 22, of which waited for: 12 -> 10; matrix products, arithmetic and copies ran while one was open for 0% -> 0% of each run, Pallas kernels for 8% -> 11%
where the time goes in v9:
time: 63.3 us; the launch traced here: 63.1 us
  waiting for transfers between devices  28.8 us (45%)
  starting transfers between devices  23.4 us (37%)
  Pallas kernels  10.6 us (17%)
    ppermute x21, waiting for transfers between devices, swap(): return lax.ppermute(value, 'patch', [(p, p ^ twist) for p in range(size)])  25.2 us
    ppermute x21, starting transfers between devices, swap(): return lax.ppermute(value, 'patch', [(p, p ^ twist) for p in range(size)])  21.9 us
    pallas_call x3, Pallas kernels, attend_call(): pl.pallas_call(kernel, out_shape=shapes, in_specs=[VMEM] * len(operands),...  4.32 us
    ppermute x1, waiting for transfers between devices, grouped_body(): received = lax.ppermute(sent, 'head', [(0, 1), (1, 0)])  3.61 us
    pallas_call x1, Pallas kernels, pack(): pl.pallas_call(pack_kernel, out_shape=[jax.ShapeDtypeStruct(shape, bf16)...  2.51 us
    pallas_call x1, Pallas kernels, pick(): pl.pallas_call(pick_kernel, out_shape=[jax.ShapeDtypeStruct((kinds, texts...  1.65 us
    ppermute x1, starting transfers between devices, grouped_body(): received = lax.ppermute(sent, 'head', [(0, 1), (1, 0)])  1.57 us
  transfers between devices with their start and end apart: 22, of which 10 were waited for; matrix products, arithmetic and copies ran while one was open for 0% of the time, Pallas kernels for 11%

profile of v9, /device:TPU:0, one launch (start us, length us, event | category | flops | bytes accessed | tf_op | source)
XLA Modules:
  0.0 63.1 jit_solution(8100298649926228365)
XLA Ops:
  0.0 2.5 %shard_map.82 = (bf16[3,48,384]{2,1,0:T(8,128)(2,1)}, bf16[3,48,384]{2,1,0:T(8,128)(2,1)}, bf16[3,48,384]{2,1,0:T(8,128)(2,1)}, bf16[3,48,384]{2,1,0:T(8,128)(2,...) custom-call(bf16[48,1536]{1,0:T(8,128)(2,1)} %queries_hbm.1, s32[2,48,1536]{2,1,0:T(8,128)} %codes_hbm.1, ...), custom_call_target="tpu_custom_call" | custom-call | flops 294912 | bytes 884736 | tf_op jit(solution)/shard_map/pallas_call | solution.py:111
  2.5 3.0 %collective-permute-start.3 = (bf16[128,1536]{1,0:T(8,128)(2,1)}, bf16[128,1536]{1,0:T(8,128)(2,1)S(1)}, u32[]{:S(2)}, u32[]{:S(2)}) collective-permute-start(bf16[128,1536]{1,0:T(8,128)(2,1)} %get-tuple-element.48), channel_id=1, source_target_pairs={{0,4},{2,6},{4,0},{6,2},{8,12},{10,14},{12,8},{14,10},{16,20},{18,... | collective-permute-start | bytes 1179656 | tf_op jit(solution)/shard_map/ppermute | solution.py:423
  5.5 3.6 %collective-permute-start = (bf16[3,48,384]{2,1,0:T(8,128)(2,1)}, bf16[3,48,384]{2,1,0:T(8,128)(2,1)S(1)}, u32[]{:S(2)}, u32[]{:S(2)}) collective-permute-start(bf16[3,48,384]{2,1,0:T(8,128)(2,1)} %get-tuple-element.43), channel_id=1, source_target_pairs={{0,24},{2,26},{4,28},{6,30},{8,16},{10,18},{12,20},{14,22},{16,8},... | collective-permute-start | bytes 331784 | tf_op jit(solution)/shard_map/ppermute | solution.py:423
  9.1 0.8 %collective-permute-start.2 = (bf16[3,48,384]{2,1,0:T(8,128)(2,1)}, bf16[3,48,384]{2,1,0:T(8,128)(2,1)S(1)}, u32[]{:S(2)}, u32[]{:S(2)}) collective-permute-start(bf16[3,48,384]{2,1,0:T(8,128)(2,1)} %get-tuple-element.45), channel_id=1, source_target_pairs={{0,8},{2,10},{4,12},{6,14},{8,0},{10,2},{12,4},{14,6},{16,24},{18,... | collective-permute-start | bytes 331784 | tf_op jit(solution)/shard_map/ppermute | solution.py:423
  10.2 1.7 %shard_map.84 = (bf16[2,512,384]{2,1,0:T(8,128)(2,1)S(1)}, bf16[4,2,192,384]{3,2,1,0:T(8,128)(2,1)S(1)}) custom-call(bf16[2,512,1536]{2,1,0:T(8,128)(2,1)} %text_hbm.1, bf16[2,768,1536]{2,1,0:T(8,128)(2,1)} %stale_hbm.1), custom_call_target="tpu_custom_call" | custom-call | bytes 8388608 | tf_op jit(solution)/shard_map/pallas_call | solution.py:156
  11.9 1.6 %collective-permute-done.refs_1_ = bf16[3,48,384]{2,1,0:T(8,128)(2,1)S(1)} collective-permute-done((bf16[3,48,384]{2,1,0:T(8,128)(2,1)}, bf16[3,48,384]{2,1,0:T(8,128)(2,1)S(1)}, u32[]{:S(2)}, u32[]{:S(2)}) %collective-permute-start) | collective-permute-done | bytes 110624 | tf_op jit(solution)/shard_map/ppermute | solution.py:423
  13.5 4.9 %collective-permute-done.1.refs_2_ = bf16[3,48,384]{2,1,0:T(8,128)(2,1)S(1)} collective-permute-done((bf16[3,48,384]{2,1,0:T(8,128)(2,1)}, bf16[3,48,384]{2,1,0:T(8,128)(2,1)S(1)}, u32[]{:S(2)}, u32[]{:S(2)}) %collective-permute-start.1) | collective-permute-done | bytes 110624 | tf_op jit(solution)/shard_map/ppermute | solution.py:423
  18.5 1.6 %collective-permute-done.6.near = bf16[4,2,48,384]{3,2,1,0:T(8,128)(2,1)S(1)} collective-permute-done((bf16[4,2,48,384]{3,2,1,0:T(8,128)(2,1)S(1)}, bf16[4,2,48,384]{3,2,1,0:T(8,128)(2,1)S(1)}, u32[]{:S(2)}, u32[]{:S(2)}) %collective-permute-start.6) | collective-permute-done | bytes 294944 | tf_op jit(solution)/shard_map/ppermute | solution.py:423
  20.3 0.4 collective-permute-start.7
  20.6 0.5 collective-permute-start.5
  21.2 1.5 %shard_map.85 = (f32[3,192,1]{2,1,0:T(8,128)S(1)}, f32[3,192,1]{2,1,0:T(8,128)S(1)}, f32[3,192,128]{2,1,0:T(8,128)S(1)}) custom-call(bf16[192,384]{1,0:T(8,128)(2,1)S(1)} %get-tuple-element.53.query, bf16[4,2,48,384]{3,2,1,0:T(8,128)(2,1)S(1)} %get-tuple-element.56.every, bf16[2,512,384]{2,1,0:T(8,128)(2,1)S(1)} %get-tuple-element.51.text, ...), custom_call_target="tpu_custom_call" | custom-call | flops 415236096 | bytes 2162688 | tf_op jit(solution)/shard_map/pallas_call | solution.py:267
  22.6 5.5 %collective-permute-done.5.some_far = bf16[3,2,48,384]{3,2,1,0:T(8,128)(2,1)S(1)} collective-permute-done((bf16[3,2,48,384]{3,2,1,0:T(8,128)(2,1)S(1)}, bf16[3,2,48,384]{3,2,1,0:T(8,128)(2,1)S(1)}, u32[]{:S(2)}, u32[]{:S(2)}) %collective-permute-start.5) | collective-permute-done | bytes 221216 | tf_op jit(solution)/shard_map/ppermute | solution.py:423
  28.1 0.5 collective-permute-start.9
  28.6 0.6 collective-permute-start.14
  29.2 0.9 %collective-permute-start.15 = (bf16[64,1536]{1,0:T(8,128)(2,1)S(1)}, bf16[64,1536]{1,0:T(8,128)(2,1)S(1)}, u32[]{:S(2)}, u32[]{:S(2)}) collective-permute-start(bf16[64,1536]{1,0:T(8,128)(2,1)S(1)} %slice.4), channel_id=1, source_target_pairs={{0,6},{2,4},{4,2},{6,0},{8,14},{10,12},{12,10},{14,8},{16,22},{18,... | collective-permute-start | bytes 589832 | tf_op jit(solution)/shard_map/ppermute | solution.py:423
  30.1 1.3 %shard_map.86 = (f32[3,192,1]{2,1,0:T(8,128)S(1)}, f32[3,192,1]{2,1,0:T(8,128)S(1)}, f32[3,192,128]{2,1,0:T(8,128)S(1)}) custom-call(bf16[192,384]{1,0:T(8,128)(2,1)S(1)} %get-tuple-element.53.query, bf16[4,2,48,384]{3,2,1,0:T(8,128)(2,1)S(1)} %collective-permute-done.6.near, bf16[2,48,384]{2,1,0:T(8,128)(2,1)S(1)} %collective-permute-done.4.own_far, ...), custom_call_target="tpu_custom_call" | custom-call | flops 226492416 | bytes 1179648 | tf_op jit(solution)/shard_map/pallas_call | solution.py:267
  31.4 1.6 %shard_map.87 = (bf16[192,384]{1,0:T(8,128)(2,1)S(1)}, bf16[192,256]{1,0:T(8,128)(2,1)S(1)}, bf16[192,128]{1,0:T(8,128)(2,1)S(1)}) custom-call(bf16[192,384]{1,0:T(8,128)(2,1)S(1)} %get-tuple-element.53.query, bf16[2,48,384]{2,1,0:T(8,128)(2,1)S(1)} %collective-permute-done.9.own_corner, bf16[3,2,48,384]{3,2,1,0:T(8,128)(2,1)S(1)} %collective-permute-done.10.some_corner, ...), custom_call_target="tpu_custom_call" | custom-call | flops 113246208 | bytes 589824 | tf_op jit(solution)/shard_map/pallas_call | solution.py:267
  33.0 0.3 collective-permute-start.11
  33.3 2.8 %collective-permute-start.12 = (bf16[192,256]{1,0:T(8,128)(2,1)S(1)}, bf16[192,256]{1,0:T(8,128)(2,1)S(1)}, u32[]{:S(2)}, u32[]{:S(2)}) collective-permute-start(bf16[192,256]{1,0:T(8,128)(2,1)S(1)} %get-tuple-element.69), channel_id=1, source_target_pairs={{0,16},{2,18},{4,20},{6,22},{8,24},{10,26},{12,28},{14,30},{16,0},... | collective-permute-start | bytes 294920 | tf_op jit(solution)/shard_map/ppermute | solution.py:423
  36.3 3.5 %collective-permute-done.12.across_most = bf16[192,256]{1,0:T(8,128)(2,1)S(1)} collective-permute-done((bf16[192,256]{1,0:T(8,128)(2,1)S(1)}, bf16[192,256]{1,0:T(8,128)(2,1)S(1)}, u32[]{:S(2)}, u32[]{:S(2)}) %collective-permute-start.12) | collective-permute-done | bytes 98336 | tf_op jit(solution)/shard_map/ppermute | solution.py:423
  39.7 3.3 %collective-permute-start.16 = (bf16[192,256]{1,0:T(8,128)(2,1)S(1)}, bf16[192,256]{1,0:T(8,128)(2,1)S(1)}, u32[]{:S(2)}, u32[]{:S(2)}) collective-permute-start(bf16[192,256]{1,0:T(8,128)(2,1)S(1)} %collective-permute-done.12.across_most), channel_id=1, source_target_pairs={{0,8},{2,10},{4,12},{6,14},{8,0},{10,2},{12,4},{14,6},{16,24},{18,... | collective-permute-start | bytes 294920 | tf_op jit(solution)/shard_map/ppermute | solution.py:423
  43.0 1.0 %collective-permute-done.13.across_last = bf16[192,128]{1,0:T(8,128)(2,1)S(1)} collective-permute-done((bf16[192,128]{1,0:T(8,128)(2,1)S(1)}, bf16[192,128]{1,0:T(8,128)(2,1)S(1)}, u32[]{:S(2)}, u32[]{:S(2)}) %collective-permute-start.13) | collective-permute-done | bytes 49184 | tf_op jit(solution)/shard_map/ppermute | solution.py:423
  44.3 0.7 %shard_map.89.partial = f32[192,768]{1,0:T(8,128)S(1)} custom-call(bf16[192,384]{1,0:T(8,128)(2,1)S(1)} %get-tuple-element.68.full, bf16[192,384]{1,0:T(8,128)(2,1)S(1)} %collective-permute-done.11.beside, bf16[192,256]{1,0:T(8,128)(2,1)S(1)} %collective-permute-done.12.across_most, bf16[192,128]{1,0:T(8,128)(2,1)S(1)} %collective-permute-done.13.across_last, ...), custom_call_target="tpu_custom_call" | custom-call | flops 452984832 | bytes 589824 | tf_op jit(solution)/shard_map/pallas_call | solution.py:329
  45.0 3.1 %collective-permute-done.17.last = bf16[192,128]{1,0:T(8,128)(2,1)S(1)} collective-permute-done((bf16[192,128]{1,0:T(8,128)(2,1)S(1)}, bf16[192,128]{1,0:T(8,128)(2,1)S(1)}, u32[]{:S(2)}, u32[]{:S(2)}) %collective-permute-start.17) | collective-permute-done | bytes 49184 | tf_op jit(solution)/shard_map/ppermute | solution.py:423
  48.1 0.4 shard_map.90
  48.5 2.8 %collective-permute-start.18 = (bf16[48,768]{1,0:T(8,128)(2,1)S(1)}, bf16[48,768]{1,0:T(8,128)(2,1)S(1)}, u32[]{:S(2)}, u32[]{:S(2)}) collective-permute-start(bf16[48,768]{1,0:T(8,128)(2,1)S(1)} %get-tuple-element.74), channel_id=1, source_target_pairs={{0,24},{2,26},{4,28},{6,30},{8,16},{10,18},{12,20},{14,22},{16,8},... | collective-permute-start | bytes 221192 | tf_op jit(solution)/shard_map/ppermute | solution.py:423
  51.2 1.7 %collective-permute-start.20 = (bf16[48,768]{1,0:T(8,128)(2,1)S(1)}, bf16[48,768]{1,0:T(8,128)(2,1)S(1)}, u32[]{:S(2)}, u32[]{:S(2)}) collective-permute-start(bf16[48,768]{1,0:T(8,128)(2,1)S(1)} %get-tuple-element.76), channel_id=1, source_target_pairs={{0,8},{2,10},{4,12},{6,14},{8,0},{10,2},{12,4},{14,6},{16,24},{18,... | collective-permute-start | bytes 221192 | tf_op jit(solution)/shard_map/ppermute | solution.py:423
  52.9 2.2 %collective-permute-done.18.refs_1_ = bf16[48,768]{1,0:T(8,128)(2,1)S(1)} collective-permute-done((bf16[48,768]{1,0:T(8,128)(2,1)S(1)}, bf16[48,768]{1,0:T(8,128)(2,1)S(1)}, u32[]{:S(2)}, u32[]{:S(2)}) %collective-permute-start.18) | collective-permute-done | bytes 73760 | tf_op jit(solution)/shard_map/ppermute | solution.py:423
  55.1 2.0 %collective-permute-done.19.refs_2_ = bf16[48,768]{1,0:T(8,128)(2,1)S(1)} collective-permute-done((bf16[48,768]{1,0:T(8,128)(2,1)S(1)}, bf16[48,768]{1,0:T(8,128)(2,1)S(1)}, u32[]{:S(2)}, u32[]{:S(2)}) %collective-permute-start.19) | collective-permute-done | bytes 73760 | tf_op jit(solution)/shard_map/ppermute | solution.py:423
  57.2 1.6 %collective-permute-start.21 = (bf16[2,48,768]{2,1,0:T(8,128)(2,1)S(1)}, bf16[2,48,768]{2,1,0:T(8,128)(2,1)S(1)}, u32[]{:S(2)}, u32[]{:S(2)}) collective-permute-start(bf16[2,48,768]{2,1,0:T(8,128)(2,1)S(1)} %get-tuple-element.78), channel_id=1, source_target_pairs={{0,1},{1,0},{2,3},{3,2},{4,5},{5,4},{6,7},{7,6},{8,9},{9,8},{10,11... | collective-permute-start | bytes 442376 | tf_op jit(solution)/shard_map/ppermute | solution.py:460
  58.8 3.6 %collective-permute-done.21.arrived = bf16[2,48,768]{2,1,0:T(8,128)(2,1)S(1)} collective-permute-done((bf16[2,48,768]{2,1,0:T(8,128)(2,1)S(1)}, bf16[2,48,768]{2,1,0:T(8,128)(2,1)S(1)}, u32[]{:S(2)}, u32[]{:S(2)}) %collective-permute-start.21) | collective-permute-done | bytes 147488 | tf_op jit(solution)/shard_map/ppermute | solution.py:460
  62.4 0.7 %shard_map.92 = bf16[48,1536]{1,0:T(8,128)(2,1)} custom-call(bf16[2,48,768]{2,1,0:T(8,128)(2,1)S(1)} %get-tuple-element.77.kept, bf16[2,48,768]{2,1,0:T(8,128)(2,1)S(1)} %collective-permute-done.21.arrived, f32[1,1536]{1,0:T(1,128)S(1)} %reshape.6.bias, f32[1,1536]{1,0:T(1,128)S(1)} %reshape.7.gate), custom_call_target="tpu_custom_call" | custom-call | flops 221184 | bytes 294912 | tf_op jit(solution)/shard_map/pallas_call | solution.py:404
  (34 shorter events, 1.1 us)
Async XLA Ops:
  2.5 15.9 %collective-permute-start.3 = (bf16[128,1536]{1,0:T(8,128)(2,1)}, bf16[128,1536]{1,0:T(8,128)(2,1)S(1)}, u32[]{:S(2)}, u32[]{:S(2)}) collective-permute-start(bf16[128,1536]{1,0:T(8,128)(2,1)} %get-tuple-element.48), channel_id=1, source_target_pairs={{0,4},{2,6},{4,0},{6,2},{8,12},{10,14},{12,8},{14,10},{16,20},{18,... | collective-permute-start | bytes 1179656 | tf_op jit(solution)/shard_map/ppermute | solution.py:423
  5.5 8.0 %collective-permute-start = (bf16[3,48,384]{2,1,0:T(8,128)(2,1)}, bf16[3,48,384]{2,1,0:T(8,128)(2,1)S(1)}, u32[]{:S(2)}, u32[]{:S(2)}) collective-permute-start(bf16[3,48,384]{2,1,0:T(8,128)(2,1)} %get-tuple-element.43), channel_id=1, source_target_pairs={{0,24},{2,26},{4,28},{6,30},{8,16},{10,18},{12,20},{14,22},{16,8},... | collective-permute-start | bytes 331784 | tf_op jit(solution)/shard_map/ppermute | solution.py:423
  9.1 9.2 %collective-permute-start.1 = (bf16[3,48,384]{2,1,0:T(8,128)(2,1)}, bf16[3,48,384]{2,1,0:T(8,128)(2,1)S(1)}, u32[]{:S(2)}, u32[]{:S(2)}) collective-permute-start(bf16[3,48,384]{2,1,0:T(8,128)(2,1)} %get-tuple-element.44), channel_id=1, source_target_pairs={{0,16},{2,18},{4,20},{6,22},{8,24},{10,26},{12,28},{14,30},{16,0},... | collective-permute-start | bytes 331784 | tf_op jit(solution)/shard_map/ppermute | solution.py:423
  9.1 9.2 %collective-permute-start.2 = (bf16[3,48,384]{2,1,0:T(8,128)(2,1)}, bf16[3,48,384]{2,1,0:T(8,128)(2,1)S(1)}, u32[]{:S(2)}, u32[]{:S(2)}) collective-permute-start(bf16[3,48,384]{2,1,0:T(8,128)(2,1)} %get-tuple-element.45), channel_id=1, source_target_pairs={{0,8},{2,10},{4,12},{6,14},{8,0},{10,2},{12,4},{14,6},{16,24},{18,... | collective-permute-start | bytes 331784 | tf_op jit(solution)/shard_map/ppermute | solution.py:423
  9.9 8.5 %copy-start.1 = (bf16[3,48,384]{2,1,0:T(8,128)(2,1)S(1)}, bf16[3,48,384]{2,1,0:T(8,128)(2,1)}, u32[]{:S(2)}) copy-start(bf16[3,48,384]{2,1,0:T(8,128)(2,1)} %get-tuple-element.42.refs_0_) | copy-start | bytes 331780
  9.9 10.2 %copy-start = (bf16[1536,192]{0,1:T(8,128)(2,1)S(1)}, bf16[1536,192]{0,1:T(8,128)(2,1)}, u32[]{:S(2)}) copy-start(bf16[1536,192]{0,1:T(8,128)(2,1)} %param.13) | copy-start | bytes 1769476
  9.9 8.5 %collective-permute-start.4 = (bf16[2,48,384]{2,1,0:T(8,128)(2,1)}, bf16[2,48,384]{2,1,0:T(8,128)(2,1)S(1)}, u32[]{:S(2)}, u32[]{:S(2)}) collective-permute-start(bf16[2,48,384]{2,1,0:T(8,128)(2,1)} %get-tuple-element.50), channel_id=1, source_target_pairs={{0,4},{2,6},{4,0},{6,2},{8,12},{10,14},{12,8},{14,10},{16,20},{18,... | collective-permute-start | bytes 221192 | tf_op jit(solution)/shard_map/ppermute | solution.py:423
  18.5 1.6 %collective-permute-start.6 = (bf16[4,2,48,384]{3,2,1,0:T(8,128)(2,1)S(1)}, bf16[4,2,48,384]{3,2,1,0:T(8,128)(2,1)S(1)}, u32[]{:S(2)}, u32[]{:S(2)}) collective-permute-start(bf16[4,2,48,384]{3,2,1,0:T(8,128)(2,1)S(1)} %get-tuple-element.56.every), channel_id=1, source_target_pairs={{0,2},{2,0},{4,6},{6,4},{8,10},{10,8},{12,14},{14,12},{16,18},{18,... | collective-permute-start | bytes 884744 | tf_op jit(solution)/shard_map/ppermute | solution.py:423
  20.1 8.0 %collective-permute-start.8 = (bf16[192,1536]{1,0:T(8,128)(2,1)S(1)}, bf16[192,1536]{1,0:T(8,128)(2,1)S(1)}, u32[]{:S(2)}, u32[]{:S(2)}) collective-permute-start(bf16[192,1536]{1,0:T(8,128)(2,1)S(1)} %bitcast.3), channel_id=1, source_target_pairs={{0,2},{2,0},{4,6},{6,4},{8,10},{10,8},{12,14},{14,12},{16,18},{18,... | collective-permute-start | bytes 1769480 | tf_op jit(solution)/shard_map/ppermute | solution.py:423
  20.3 7.8 %collective-permute-start.7 = (bf16[128,1536]{1,0:T(8,128)(2,1)S(1)}, bf16[128,1536]{1,0:T(8,128)(2,1)S(1)}, u32[]{:S(2)}, u32[]{:S(2)}) collective-permute-start(bf16[128,1536]{1,0:T(8,128)(2,1)S(1)} %collective-permute-done.3.early), channel_id=1, source_target_pairs={{0,2},{2,0},{4,6},{6,4},{8,10},{10,8},{12,14},{14,12},{16,18},{18,... | collective-permute-start | bytes 1179656 | tf_op jit(solution)/shard_map/ppermute | solution.py:423
  20.6 7.5 %collective-permute-start.5 = (bf16[3,2,48,384]{3,2,1,0:T(8,128)(2,1)S(1)}, bf16[3,2,48,384]{3,2,1,0:T(8,128)(2,1)S(1)}, u32[]{:S(2)}, u32[]{:S(2)}) collective-permute-start(bf16[3,2,48,384]{3,2,1,0:T(8,128)(2,1)S(1)} %get-tuple-element.54), channel_id=1, source_target_pairs={{0,4},{2,6},{4,0},{6,2},{8,12},{10,14},{12,8},{14,10},{16,20},{18,... | collective-permute-start | bytes 663560 | tf_op jit(solution)/shard_map/ppermute | solution.py:423
  28.1 3.3 %collective-permute-start.10 = (bf16[3,2,48,384]{3,2,1,0:T(8,128)(2,1)S(1)}, bf16[3,2,48,384]{3,2,1,0:T(8,128)(2,1)S(1)}, u32[]{:S(2)}, u32[]{:S(2)}) collective-permute-start(bf16[3,2,48,384]{3,2,1,0:T(8,128)(2,1)S(1)} %collective-permute-done.5.some_far), channel_id=1, source_target_pairs={{0,2},{2,0},{4,6},{6,4},{8,10},{10,8},{12,14},{14,12},{16,18},{18,... | collective-permute-start | bytes 663560 | tf_op jit(solution)/shard_map/ppermute | solution.py:423
  28.1 3.3 %collective-permute-start.9 = (bf16[2,48,384]{2,1,0:T(8,128)(2,1)S(1)}, bf16[2,48,384]{2,1,0:T(8,128)(2,1)S(1)}, u32[]{:S(2)}, u32[]{:S(2)}) collective-permute-start(bf16[2,48,384]{2,1,0:T(8,128)(2,1)S(1)} %collective-permute-done.4.own_far), channel_id=1, source_target_pairs={{0,2},{2,0},{4,6},{6,4},{8,10},{10,8},{12,14},{14,12},{16,18},{18,... | collective-permute-start | bytes 221192 | tf_op jit(solution)/shard_map/ppermute | solution.py:423
  28.6 14.4 %collective-permute-start.14 = (bf16[64,1536]{1,0:T(8,128)(2,1)S(1)}, bf16[64,1536]{1,0:T(8,128)(2,1)S(1)}, u32[]{:S(2)}, u32[]{:S(2)}) collective-permute-start(bf16[64,1536]{1,0:T(8,128)(2,1)S(1)} %slice.4), channel_id=1, source_target_pairs={{0,4},{2,6},{4,0},{6,2},{8,12},{10,14},{12,8},{14,10},{16,20},{18,... | collective-permute-start | bytes 589832 | tf_op jit(solution)/shard_map/ppermute | solution.py:423
  29.2 13.8 %collective-permute-start.15 = (bf16[64,1536]{1,0:T(8,128)(2,1)S(1)}, bf16[64,1536]{1,0:T(8,128)(2,1)S(1)}, u32[]{:S(2)}, u32[]{:S(2)}) collective-permute-start(bf16[64,1536]{1,0:T(8,128)(2,1)S(1)} %slice.4), channel_id=1, source_target_pairs={{0,6},{2,4},{4,2},{6,0},{8,14},{10,12},{12,10},{14,8},{16,22},{18,... | collective-permute-start | bytes 589832 | tf_op jit(solution)/shard_map/ppermute | solution.py:423
  33.0 11.0 %collective-permute-start.11 = (bf16[192,384]{1,0:T(8,128)(2,1)S(1)}, bf16[192,384]{1,0:T(8,128)(2,1)S(1)}, u32[]{:S(2)}, u32[]{:S(2)}) collective-permute-start(bf16[192,384]{1,0:T(8,128)(2,1)S(1)} %get-tuple-element.68.full), channel_id=1, source_target_pairs={{0,8},{2,10},{4,12},{6,14},{8,0},{10,2},{12,4},{14,6},{16,24},{18,... | collective-permute-start | bytes 442376 | tf_op jit(solution)/shard_map/ppermute | solution.py:423
  33.3 6.4 %collective-permute-start.12 = (bf16[192,256]{1,0:T(8,128)(2,1)S(1)}, bf16[192,256]{1,0:T(8,128)(2,1)S(1)}, u32[]{:S(2)}, u32[]{:S(2)}) collective-permute-start(bf16[192,256]{1,0:T(8,128)(2,1)S(1)} %get-tuple-element.69), channel_id=1, source_target_pairs={{0,16},{2,18},{4,20},{6,22},{8,24},{10,26},{12,28},{14,30},{16,0},... | collective-permute-start | bytes 294920 | tf_op jit(solution)/shard_map/ppermute | solution.py:423
  36.1 7.9 %collective-permute-start.13 = (bf16[192,128]{1,0:T(8,128)(2,1)S(1)}, bf16[192,128]{1,0:T(8,128)(2,1)S(1)}, u32[]{:S(2)}, u32[]{:S(2)}) collective-permute-start(bf16[192,128]{1,0:T(8,128)(2,1)S(1)} %get-tuple-element.70), channel_id=1, source_target_pairs={{0,16},{2,18},{4,20},{6,22},{8,24},{10,26},{12,28},{14,30},{16,0},... | collective-permute-start | bytes 147464 | tf_op jit(solution)/shard_map/ppermute | solution.py:423
  39.7 8.4 %collective-permute-start.16 = (bf16[192,256]{1,0:T(8,128)(2,1)S(1)}, bf16[192,256]{1,0:T(8,128)(2,1)S(1)}, u32[]{:S(2)}, u32[]{:S(2)}) collective-permute-start(bf16[192,256]{1,0:T(8,128)(2,1)S(1)} %collective-permute-done.12.across_most), channel_id=1, source_target_pairs={{0,8},{2,10},{4,12},{6,14},{8,0},{10,2},{12,4},{14,6},{16,24},{18,... | collective-permute-start | bytes 294920 | tf_op jit(solution)/shard_map/ppermute | solution.py:423
  44.0 4.1 %collective-permute-start.17 = (bf16[192,128]{1,0:T(8,128)(2,1)S(1)}, bf16[192,128]{1,0:T(8,128)(2,1)S(1)}, u32[]{:S(2)}, u32[]{:S(2)}) collective-permute-start(bf16[192,128]{1,0:T(8,128)(2,1)S(1)} %collective-permute-done.13.across_last), channel_id=1, source_target_pairs={{0,8},{2,10},{4,12},{6,14},{8,0},{10,2},{12,4},{14,6},{16,24},{18,... | collective-permute-start | bytes 147464 | tf_op jit(solution)/shard_map/ppermute | solution.py:423
  44.2 14.5 %copy-start.2 = (f32[1536]{0:T(1024)S(1)}, f32[1536]{0:T(1024)}, u32[]{:S(2)}) copy-start(f32[1536]{0:T(1024)} %param.14) | copy-start | bytes 18436
  44.3 14.5 %copy-start.3 = (f32[1536]{0:T(1024)S(1)}, f32[1536]{0:T(1024)}, u32[]{:S(2)}) copy-start(f32[1536]{0:T(1024)} %param.15) | copy-start | bytes 18436
  48.5 6.6 %collective-permute-start.18 = (bf16[48,768]{1,0:T(8,128)(2,1)S(1)}, bf16[48,768]{1,0:T(8,128)(2,1)S(1)}, u32[]{:S(2)}, u32[]{:S(2)}) collective-permute-start(bf16[48,768]{1,0:T(8,128)(2,1)S(1)} %get-tuple-element.74), channel_id=1, source_target_pairs={{0,24},{2,26},{4,28},{6,30},{8,16},{10,18},{12,20},{14,22},{16,8},... | collective-permute-start | bytes 221192 | tf_op jit(solution)/shard_map/ppermute | solution.py:423
  51.2 5.8 %collective-permute-start.19 = (bf16[48,768]{1,0:T(8,128)(2,1)S(1)}, bf16[48,768]{1,0:T(8,128)(2,1)S(1)}, u32[]{:S(2)}, u32[]{:S(2)}) collective-permute-start(bf16[48,768]{1,0:T(8,128)(2,1)S(1)} %get-tuple-element.75), channel_id=1, source_target_pairs={{0,16},{2,18},{4,20},{6,22},{8,24},{10,26},{12,28},{14,30},{16,0},... | collective-permute-start | bytes 221192 | tf_op jit(solution)/shard_map/ppermute | solution.py:423
  51.2 5.8 %collective-permute-start.20 = (bf16[48,768]{1,0:T(8,128)(2,1)S(1)}, bf16[48,768]{1,0:T(8,128)(2,1)S(1)}, u32[]{:S(2)}, u32[]{:S(2)}) collective-permute-start(bf16[48,768]{1,0:T(8,128)(2,1)S(1)} %get-tuple-element.76), channel_id=1, source_target_pairs={{0,8},{2,10},{4,12},{6,14},{8,0},{10,2},{12,4},{14,6},{16,24},{18,... | collective-permute-start | bytes 221192 | tf_op jit(solution)/shard_map/ppermute | solution.py:423
  57.2 5.2 %collective-permute-start.21 = (bf16[2,48,768]{2,1,0:T(8,128)(2,1)S(1)}, bf16[2,48,768]{2,1,0:T(8,128)(2,1)S(1)}, u32[]{:S(2)}, u32[]{:S(2)}) collective-permute-start(bf16[2,48,768]{2,1,0:T(8,128)(2,1)S(1)} %get-tuple-element.78), channel_id=1, source_target_pairs={{0,1},{1,0},{2,3},{3,2},{4,5},{5,4},{6,7},{7,6},{8,9},{9,8},{10,11... | collective-permute-start | bytes 442376 | tf_op jit(solution)/shard_map/ppermute | solution.py:460

commit v10 on v9

--- a/solution.py
+++ b/solution.py
@@ -67,8 +67,8 @@
     return me // SPREAD, lax.rem(me, SPREAD)
 
 
-def pack_kernel(queries_hbm, codes_hbm, exponents_hbm, weight_hbm, *rest):
-    outs, early, (codes, queries, exponents, held, sems) = rest[:-6], rest[-6], rest[-5:]
+def pack_kernel(queries_hbm, codes_hbm, exponents_hbm, *rest):
+    outs, (codes, queries, exponents, held, sems) = rest[:-5], rest[-5:]
     groups, kinds, rows, width = held.shape
     group, _ = place()
     per = width // HD
@@ -76,7 +76,6 @@
         pltpu.make_async_copy(exponents_hbm, exponents, sems.at[0]),
         pltpu.make_async_copy(codes_hbm, codes, sems.at[1]),
         pltpu.make_async_copy(queries_hbm, queries, sems.at[2]),
-        pltpu.make_async_copy(weight_hbm.at[0 : early.shape[0]], early, sems.at[3]),
     ]
     for copy in copies:
         copy.start()
@@ -98,31 +97,30 @@
     for turn in range(groups):
         outs[turn][...] = held[jnp.bitwise_xor(group, turn)]
     outs[groups][...] = held[group, 0 : kinds - 1]
-    copies[3].wait()
-
-
-def pack(groups, queries, codes, exponents, weight, cut):
+
+
+def pack(groups, queries, codes, exponents):
     rows, width = queries.shape
     kinds = codes.shape[0]
     share = width // groups
     bf16 = jnp.bfloat16
     exponents = exponents.transpose(2, 0, 1)
-    shapes = [(kinds + 1, rows, share)] * groups + [(kinds, rows, share), (cut, weight.shape[1])]
+    shapes = [(kinds + 1, rows, share)] * groups + [(kinds, rows, share)]
     outs = pl.pallas_call(
         pack_kernel,
         out_shape=[jax.ShapeDtypeStruct(shape, bf16) for shape in shapes],
-        in_specs=[HBM] * 4,
+        in_specs=[HBM] * 3,
         out_specs=[VMEM] * len(shapes),
         scratch_shapes=[
             pltpu.VMEM(codes.shape, jnp.int32),
             pltpu.VMEM(queries.shape, bf16),
             pltpu.VMEM(exponents.shape, jnp.int32),
             pltpu.VMEM((groups, kinds + 1, rows, share), bf16),
-            pltpu.SemaphoreType.DMA((4,)),
+            pltpu.SemaphoreType.DMA((3,)),
         ],
         compiler_params=pltpu.CompilerParams(vmem_limit_bytes=PACK_LIMIT),
         cost_estimate=pl.CostEstimate(flops=2 * codes.size, bytes_accessed=6 * codes.size, transcendentals=0),
-    )(queries, codes, exponents, weight)
+    )(queries, codes, exponents)
     return outs
 
 
@@ -192,71 +190,88 @@
     )(*parts)
 
 
-def absorb(query, segments, state):
-    scores = []
-    for keys, _ in segments:
-        score = sum(lax.dot_general(query, key, NT, preferred_element_type=jnp.float32) for key in keys)
-        scores.append(score * HD**-0.5)
-    peaks = [jnp.max(score, axis=1, keepdims=True) for score in scores]
-    if state is not None:
-        peaks.append(state[0])
-    peak = functools.reduce(jnp.maximum, peaks)
-    total = mixed = 0.0
-    if state is not None:
-        fade = jnp.exp(state[0] - peak)
-        total, mixed = state[1] * fade, state[2] * fade
-    for score, (_, values) in zip(scores, segments):
-        weights = jnp.exp(score - peak).astype(jnp.bfloat16)
-        total += jnp.sum(weights.astype(jnp.float32), axis=1, keepdims=True)
-        for value in values:
-            mixed += jnp.dot(weights, value, preferred_element_type=jnp.float32)
-    return peak, total, mixed
-
-
-def image_segment(stale, twist, residual, cols):
-    both = [(stale[twist, kind, :, cols], residual(kind)) for kind in range(2)]
-    return both[0], both[1]
-
-
-def whole_part(part, cols):
-    return lambda kind: part[:, kind, :, cols].reshape(-1, HD)
-
-
-def split_part(own, some, cols):
-    return lambda kind: jnp.concatenate([own[kind, :, cols], some[:, kind, :, cols].reshape(-1, HD)], axis=0)
+def absorb(queries, segments, states):
+    scores = [
+        [
+            sum(lax.dot_general(query, key, NT, preferred_element_type=jnp.float32) for key in keys) * HD**-0.5
+            for keys, _ in parts
+        ]
+        for query, parts in zip(queries, segments)
+    ]
+    peaks = [[jnp.max(score, axis=1, keepdims=True) for score in row] for row in scores]
+    if states is not None:
+        peaks = [row + [state[0]] for row, state in zip(peaks, states)]
+    peaks = [functools.reduce(jnp.maximum, row) for row in peaks]
+    weights = [
+        [jnp.exp(score - peak).astype(jnp.bfloat16) for score in row] for row, peak in zip(scores, peaks)
+    ]
+    totals = [sum(jnp.sum(w.astype(jnp.float32), axis=1, keepdims=True) for w in row) for row in weights]
+    mixes = [
+        sum(
+            jnp.dot(w, value, preferred_element_type=jnp.float32)
+            for w, (_, values) in zip(row, parts)
+            for value in values
+        )
+        for row, parts in zip(weights, segments)
+    ]
+    if states is not None:
+        fades = [jnp.exp(state[0] - peak) for state, peak in zip(states, peaks)]
+        totals = [total + state[1] * fade for total, state, fade in zip(totals, states, fades)]
+        mixes = [mix + state[2] * fade for mix, state, fade in zip(mixes, states, fades)]
+    return list(zip(peaks, totals, mixes))
+
+
+def columns_of(width):
+    return [slice(start, start + HD) for start in range(0, width, HD)]
+
+
+def image_segment(stale, twist, residual):
+    def of(cols):
+        both = [(stale[twist, kind, :, cols], residual(kind, cols)) for kind in range(2)]
+        return both[0], both[1]
+
+    return of
+
+
+def whole_part(part):
+    return lambda kind, cols: part[:, kind, :, cols].reshape(-1, HD)
+
+
+def split_part(own, some):
+    return lambda kind, cols: jnp.concatenate([own[kind, :, cols], some[:, kind, :, cols].reshape(-1, HD)], axis=0)
 
 
 def near_kernel(query, every, text, stale, peak, total, mixed):
-    for head in range(mixed.shape[0]):
-        cols = slice(head * HD, (head + 1) * HD)
-        segments = [
-            ((text[0, :, cols],), (text[1, :, cols],)),
-            image_segment(stale, 0, whole_part(every, cols), cols),
-        ]
-        peak[head], total[head], mixed[head] = absorb(query[:, cols], segments, None)
+    heads = columns_of(query.shape[1])
+    image = image_segment(stale, 0, whole_part(every))
+    segments = [[((text[0, :, cols],), (text[1, :, cols],)), image(cols)] for cols in heads]
+    states = absorb([query[:, cols] for cols in heads], segments, None)
+    for head, state in enumerate(states):
+        peak[head], total[head], mixed[head] = state
 
 
 def middle_kernel(query, near, own_far, some_far, stale, peak_in, total_in, mixed_in, peak, total, mixed):
-    for head in range(mixed.shape[0]):
-        cols = slice(head * HD, (head + 1) * HD)
-        segments = [
-            image_segment(stale, 1, whole_part(near, cols), cols),
-            image_segment(stale, 2, split_part(own_far, some_far, cols), cols),
-        ]
-        state = peak_in[head], total_in[head], mixed_in[head]
-        peak[head], total[head], mixed[head] = absorb(query[:, cols], segments, state)
+    heads = columns_of(query.shape[1])
+    images = [
+        image_segment(stale, 1, whole_part(near)),
+        image_segment(stale, 2, split_part(own_far, some_far)),
+    ]
+    segments = [[image(cols) for image in images] for cols in heads]
+    states = [(peak_in[head], total_in[head], mixed_in[head]) for head in range(len(heads))]
+    states = absorb([query[:, cols] for cols in heads], segments, states)
+    for head, state in enumerate(states):
+        peak[head], total[head], mixed[head] = state
 
 
 def last_kernel(query, own_corner, some_corner, stale, peak, total, mixed, full, most, last):
-    heads = mixed.shape[0]
-    for head in range(heads):
-        cols = slice(head * HD, (head + 1) * HD)
-        segments = [image_segment(stale, 3, split_part(own_corner, some_corner, cols), cols)]
-        state = peak[head], total[head], mixed[head]
-        _, sums, mix = absorb(query[:, cols], segments, state)
+    heads = columns_of(query.shape[1])
+    image = image_segment(stale, 3, split_part(own_corner, some_corner))
+    states = [(peak[head], total[head], mixed[head]) for head in range(len(heads))]
+    states = absorb([query[:, cols] for cols in heads], [[image(cols)] for cols in heads], states)
+    for cols, (_, sums, mix) in zip(heads, states):
         value = (mix / sums).astype(jnp.bfloat16)
         full[:, cols] = value
-        if head < heads - 1:
+        if cols is not heads[-1]:
             most[:, cols] = value
         else:
             last[...] = value
@@ -287,16 +302,15 @@
     return [jax.ShapeDtypeStruct((tokens, size), jnp.bfloat16) for size in (width, width - HD, HD)]
 
 
-def order_kernel(weight, near, early, late, early_corner, late_corner, out):
+def order_kernel(*refs):
+    pieces, out = refs[:-1], refs[-1]
     _, spot = place()
-    span, cut = weight.shape[0], early.shape[0]
-    pieces = [(0, 0, weight), (1, 0, near), (2, 0, early), (2, cut, late), (3, 0, early_corner), (3, cut, late_corner)]
-    for twist, skip, piece in pieces:
-        start = jnp.bitwise_xor(spot, twist) * span + skip
-        out[pl.ds(pl.multiple_of(start, 16), piece.shape[0]), :] = piece[...]
-
-
-def order(*pieces):
+    span = out.shape[0] // SPREAD
+    for twist, piece in enumerate(pieces):
+        out[pl.ds(aligned(jnp.bitwise_xor(spot, twist), span), span), :] = piece[...]
+
+
+def order(pieces):
     span, depth = pieces[0].shape
     shape = (SPREAD * span, depth)
     return pl.pallas_call(
@@ -426,33 +440,32 @@
         return [swap(values[turn], turn * SPREAD) for turn in reversed(range(1, groups))]
 
     weight = out_weight.T
-    cut = weight.shape[0] // 48 * 32
-    *packed, own, early = pack(groups, queries, codes, exponents, weight, cut)
+    weight_far = swap(weight, 2)
+    *packed, own = pack(groups, queries, codes, exponents)
     text, stale = pick(groups, text_kv, stale_kv)
 
     every, some, query = merge([packed[0], *along(packed)])
-    own_far, early = swap(own, 2), swap(early, 2)
-
-    every, some, early, query = lax.optimization_barrier((every, some, early, query, own_far, text, stale))[:4]
-    some_far, near = swap(some, 2), swap(every, 1)
-    weight, early = lax.optimization_barrier((weight, early, near))[:2]
-    early_corner, weight_near = swap(early, 1), swap(weight, 1)
+    own_far = swap(own, 2)
+
+    ready = (every, some, query, weight, weight_far, own_far, text, stale)
+    every, some, query, weight, weight_far = lax.optimization_barrier(ready)[:5]
+    near, some_far = swap(every, 1), swap(some, 2)
     share = stale.shape[2]
     state = attend_call(near_kernel, [query, every, text, stale], state_shapes(query), share + text.shape[1])
 
-    ready = (own_far, some_far, weight, near, early_corner, weight_near, *state)
-    own_far, some_far, weight, near = lax.optimization_barrier(ready)[:4]
+    near, some_far, own_far = lax.optimization_barrier((near, some_far, own_far, *state))[:3]
     own_corner, some_corner = swap(own_far, 1), swap(some_far, 1)
-    late, late_corner = swap(weight[cut:], 2), swap(weight[cut:], 3)
     state = attend_call(middle_kernel, [query, near, own_far, some_far, stale, *state], state_shapes(query), 2 * share)
+    weight, weight_far = lax.optimization_barrier((weight, weight_far, *state))[:2]
+    weight_near, weight_corner = swap(weight, 1), swap(weight_far, 1)
     operands = [query, own_corner, some_corner, stale, *state]
     full, most, last = attend_call(last_kernel, operands, result_shapes(query), share)
 
     across_most, across_last = swap(most, 2 * SPREAD), swap(last, 2 * SPREAD)
     beside = swap(full, SPREAD)
     final_most = swap(across_most, SPREAD)
-    final_last = swap(after(across_last, beside, late, late_corner), SPREAD)
-    weight = order(weight, weight_near, early, late, early_corner, late_corner)
+    final_last = swap(after(across_last, beside, weight_near, weight_corner), SPREAD)
+    weight = order([weight, weight_near, weight_far, weight_corner])
     partial = begin([full, beside, across_most, across_last], weight)
     terms = close(groups, partial, [final_most, final_last], weight)
 

time: 63.3 us -> 63.3 us (level)
  starting transfers between devices: 23.4 us -> 24.6 us
    ppermute x21 -> x19, starting transfers between devices: 21.9 us -> 23 us  [swap(): return lax.ppermute(value, 'patch', [(p, p ^ twist) for p in range(size)])]
    ppermute x21 -> x19, waiting for transfers between devices: 25.2 us -> 24.6 us  [swap(): return lax.ppermute(value, 'patch', [(p, p ^ twist) for p in range(size)])]
  transfers between devices with their start and end apart: 22 -> 20, of which waited for: 10 -> 11; matrix products, arithmetic and copies ran while one was open for 0% -> 0% of each run, Pallas kernels for 11% -> 12%
where the time goes in v10:
time: 63.3 us; the launch traced here: 63.1 us
  waiting for transfers between devices  28.2 us (45%)
  starting transfers between devices  24.6 us (39%)
  Pallas kernels  10 us (16%)
    ppermute x19, waiting for transfers between devices, swap(): return lax.ppermute(value, 'patch', [(p, p ^ twist) for p in range(size)])  24.6 us
    ppermute x19, starting transfers between devices, swap(): return lax.ppermute(value, 'patch', [(p, p ^ twist) for p in range(size)])  23 us
    pallas_call x3, Pallas kernels, attend_call(): pl.pallas_call(kernel, out_shape=shapes, in_specs=[VMEM] * len(operands),...  3.93 us
    ppermute x1, waiting for transfers between devices, grouped_body(): received = lax.ppermute(sent, 'head', [(0, 1), (1, 0)])  3.59 us
    pallas_call x1, Pallas kernels, pack(): pl.pallas_call(pack_kernel, out_shape=[jax.ShapeDtypeStruct(shape, bf16)...  2.33 us
    pallas_call x1, Pallas kernels, pick(): pl.pallas_call(pick_kernel, out_shape=[jax.ShapeDtypeStruct((kinds, texts...  1.65 us
    ppermute x1, starting transfers between devices, grouped_body(): received = lax.ppermute(sent, 'head', [(0, 1), (1, 0)])  1.58 us
  transfers between devices with their start and end apart: 20, of which 11 were waited for; matrix products, arithmetic and copies ran while one was open for 0% of the time, Pallas kernels for 12%

profile of v10, /device:TPU:0, one launch (start us, length us, event | category | flops | bytes accessed | tf_op | source)
XLA Modules:
  0.0 63.1 jit_solution(14275687393910489644)
XLA Ops:
  0.0 2.9 %collective-permute-start.3 = (bf16[192,1536]{1,0:T(8,128)(2,1)}, bf16[192,1536]{1,0:T(8,128)(2,1)S(1)}, u32[]{:S(2)}, u32[]{:S(2)}) collective-permute-start(bf16[192,1536]{1,0:T(8,128)(2,1)} %bitcast.2), channel_id=1, source_target_pairs={{0,4},{2,6},{4,0},{6,2},{8,12},{10,14},{12,8},{14,10},{16,20},{18,... | collective-permute-start | bytes 1769480 | tf_op jit(solution)/shard_map/ppermute | solution.py:437
  2.9 2.3 %shard_map.82 = (bf16[3,48,384]{2,1,0:T(8,128)(2,1)}, bf16[3,48,384]{2,1,0:T(8,128)(2,1)}, bf16[3,48,384]{2,1,0:T(8,128)(2,1)}, bf16[3,48,384]{2,1,0:T(8,128)(2,1)}, bf16[2,48,384]{2,1,0:T(8,128)(2,1)}) custom-call(bf16[48,1536]{1,0:T(8,128)(2,1)} %queries_hbm.1, s32[2,48,1536]{2,1,0:T(8,128)} %codes_hbm.1, s32[12,2,48]{2,1,0:T(2,128)} %bitcast.5), custom_call_target="tpu_custom_call" | custom-call | flops 294912 | bytes 884736 | tf_op jit(solution)/shard_map/pallas_call | solution.py:109
  5.3 3.7 %collective-permute-start = (bf16[3,48,384]{2,1,0:T(8,128)(2,1)}, bf16[3,48,384]{2,1,0:T(8,128)(2,1)S(1)}, u32[]{:S(2)}, u32[]{:S(2)}) collective-permute-start(bf16[3,48,384]{2,1,0:T(8,128)(2,1)} %get-tuple-element.42), channel_id=1, source_target_pairs={{0,24},{2,26},{4,28},{6,30},{8,16},{10,18},{12,20},{14,22},{16,8},... | collective-permute-start | bytes 331784 | tf_op jit(solution)/shard_map/ppermute | solution.py:437
  8.9 0.8 %collective-permute-start.2 = (bf16[3,48,384]{2,1,0:T(8,128)(2,1)}, bf16[3,48,384]{2,1,0:T(8,128)(2,1)S(1)}, u32[]{:S(2)}, u32[]{:S(2)}) collective-permute-start(bf16[3,48,384]{2,1,0:T(8,128)(2,1)} %get-tuple-element.44), channel_id=1, source_target_pairs={{0,8},{2,10},{4,12},{6,14},{8,0},{10,2},{12,4},{14,6},{16,24},{18,... | collective-permute-start | bytes 331784 | tf_op jit(solution)/shard_map/ppermute | solution.py:437
  9.7 0.4 collective-permute-start.4
  10.1 1.7 %shard_map.84 = (bf16[2,512,384]{2,1,0:T(8,128)(2,1)S(1)}, bf16[4,2,192,384]{3,2,1,0:T(8,128)(2,1)S(1)}) custom-call(bf16[2,512,1536]{2,1,0:T(8,128)(2,1)} %text_hbm.1, bf16[2,768,1536]{2,1,0:T(8,128)(2,1)} %stale_hbm.1), custom_call_target="tpu_custom_call" | custom-call | bytes 8388608 | tf_op jit(solution)/shard_map/pallas_call | solution.py:154
  11.8 1.5 %collective-permute-done.refs_1_ = bf16[3,48,384]{2,1,0:T(8,128)(2,1)S(1)} collective-permute-done((bf16[3,48,384]{2,1,0:T(8,128)(2,1)}, bf16[3,48,384]{2,1,0:T(8,128)(2,1)S(1)}, u32[]{:S(2)}, u32[]{:S(2)}) %collective-permute-start) | collective-permute-done | bytes 110624 | tf_op jit(solution)/shard_map/ppermute | solution.py:437
  13.3 4.9 %collective-permute-done.1.refs_2_ = bf16[3,48,384]{2,1,0:T(8,128)(2,1)S(1)} collective-permute-done((bf16[3,48,384]{2,1,0:T(8,128)(2,1)}, bf16[3,48,384]{2,1,0:T(8,128)(2,1)S(1)}, u32[]{:S(2)}, u32[]{:S(2)}) %collective-permute-start.1) | collective-permute-done | bytes 110624 | tf_op jit(solution)/shard_map/ppermute | solution.py:437
  18.4 1.4 %collective-permute-start.6 = (bf16[3,2,48,384]{3,2,1,0:T(8,128)(2,1)S(1)}, bf16[3,2,48,384]{3,2,1,0:T(8,128)(2,1)S(1)}, u32[]{:S(2)}, u32[]{:S(2)}) collective-permute-start(bf16[3,2,48,384]{3,2,1,0:T(8,128)(2,1)S(1)} %get-tuple-element.53), channel_id=1, source_target_pairs={{0,4},{2,6},{4,0},{6,2},{8,12},{10,14},{12,8},{14,10},{16,20},{18,... | collective-permute-start | bytes 663560 | tf_op jit(solution)/shard_map/ppermute | solution.py:437
  19.8 1.0 %shard_map.85 = (f32[3,192,1]{2,1,0:T(8,128)S(1)}, f32[3,192,1]{2,1,0:T(8,128)S(1)}, f32[3,192,128]{2,1,0:T(8,128)S(1)}) custom-call(bf16[192,384]{1,0:T(8,128)(2,1)S(1)} %get-tuple-element.51.query, bf16[4,2,48,384]{3,2,1,0:T(8,128)(2,1)S(1)} %get-tuple-element.52.every, bf16[2,512,384]{2,1,0:T(8,128)(2,1)S(1)} %get-tuple-element.49.text, ...), custom_call_target="tpu_custom_call" | custom-call | flops 415236096 | bytes 2162688 | tf_op jit(solution)/shard_map/pallas_call | solution.py:282
  20.8 5.4 %collective-permute-done.6.some_far = bf16[3,2,48,384]{3,2,1,0:T(8,128)(2,1)S(1)} collective-permute-done((bf16[3,2,48,384]{3,2,1,0:T(8,128)(2,1)S(1)}, bf16[3,2,48,384]{3,2,1,0:T(8,128)(2,1)S(1)}, u32[]{:S(2)}, u32[]{:S(2)}) %collective-permute-start.6) | collective-permute-done | bytes 221216 | tf_op jit(solution)/shard_map/ppermute | solution.py:437
  26.2 1.6 %shard_map.86 = (f32[3,192,1]{2,1,0:T(8,128)S(1)}, f32[3,192,1]{2,1,0:T(8,128)S(1)}, f32[3,192,128]{2,1,0:T(8,128)S(1)}) custom-call(bf16[192,384]{1,0:T(8,128)(2,1)S(1)} %get-tuple-element.51.query, bf16[4,2,48,384]{3,2,1,0:T(8,128)(2,1)S(1)} %collective-permute-done.5.near, bf16[2,48,384]{2,1,0:T(8,128)(2,1)S(1)} %collective-permute-done.4.own_far, ...), custom_call_target="tpu_custom_call" | custom-call | flops 226492416 | bytes 1179648 | tf_op jit(solution)/shard_map/pallas_call | solution.py:282
  27.9 0.5 collective-permute-start.13
  28.5 0.4 collective-permute-start.7
  28.9 2.2 %collective-permute-done.7.own_corner = bf16[2,48,384]{2,1,0:T(8,128)(2,1)S(1)} collective-permute-done((bf16[2,48,384]{2,1,0:T(8,128)(2,1)S(1)}, bf16[2,48,384]{2,1,0:T(8,128)(2,1)S(1)}, u32[]{:S(2)}, u32[]{:S(2)}) %collective-permute-start.7) | collective-permute-done | bytes 73760 | tf_op jit(solution)/shard_map/ppermute | solution.py:437
  31.2 1.3 %shard_map.87 = (bf16[192,384]{1,0:T(8,128)(2,1)S(1)}, bf16[192,256]{1,0:T(8,128)(2,1)S(1)}, bf16[192,128]{1,0:T(8,128)(2,1)S(1)}) custom-call(bf16[192,384]{1,0:T(8,128)(2,1)S(1)} %get-tuple-element.51.query, bf16[2,48,384]{2,1,0:T(8,128)(2,1)S(1)} %collective-permute-done.7.own_corner, bf16[3,2,48,384]{3,2,1,0:T(8,128)(2,1)S(1)} %collective-permute-done.8.some_corner, ...), custom_call_target="tpu_custom_call" | custom-call | flops 113246208 | bytes 589824 | tf_op jit(solution)/shard_map/pallas_call | solution.py:282
  32.5 1.6 %collective-permute-start.9 = (bf16[192,384]{1,0:T(8,128)(2,1)S(1)}, bf16[192,384]{1,0:T(8,128)(2,1)S(1)}, u32[]{:S(2)}, u32[]{:S(2)}) collective-permute-start(bf16[192,384]{1,0:T(8,128)(2,1)S(1)} %get-tuple-element.63.full), channel_id=1, source_target_pairs={{0,8},{2,10},{4,12},{6,14},{8,0},{10,2},{12,4},{14,6},{16,24},{18,... | collective-permute-start | bytes 442376 | tf_op jit(solution)/shard_map/ppermute | solution.py:437
  34.1 2.6 %collective-permute-start.10 = (bf16[192,256]{1,0:T(8,128)(2,1)S(1)}, bf16[192,256]{1,0:T(8,128)(2,1)S(1)}, u32[]{:S(2)}, u32[]{:S(2)}) collective-permute-start(bf16[192,256]{1,0:T(8,128)(2,1)S(1)} %get-tuple-element.64), channel_id=1, source_target_pairs={{0,16},{2,18},{4,20},{6,22},{8,24},{10,26},{12,28},{14,30},{16,0},... | collective-permute-start | bytes 294920 | tf_op jit(solution)/shard_map/ppermute | solution.py:437
  37.0 3.2 %collective-permute-done.10.across_most = bf16[192,256]{1,0:T(8,128)(2,1)S(1)} collective-permute-done((bf16[192,256]{1,0:T(8,128)(2,1)S(1)}, bf16[192,256]{1,0:T(8,128)(2,1)S(1)}, u32[]{:S(2)}, u32[]{:S(2)}) %collective-permute-start.10) | collective-permute-done | bytes 98336 | tf_op jit(solution)/shard_map/ppermute | solution.py:437
  40.2 3.5 %collective-permute-start.14 = (bf16[192,256]{1,0:T(8,128)(2,1)S(1)}, bf16[192,256]{1,0:T(8,128)(2,1)S(1)}, u32[]{:S(2)}, u32[]{:S(2)}) collective-permute-start(bf16[192,256]{1,0:T(8,128)(2,1)S(1)} %collective-permute-done.10.across_most), channel_id=1, source_target_pairs={{0,8},{2,10},{4,12},{6,14},{8,0},{10,2},{12,4},{14,6},{16,24},{18,... | collective-permute-start | bytes 294920 | tf_op jit(solution)/shard_map/ppermute | solution.py:437
  43.7 0.4 collective-permute-done.11.across_last
  44.5 0.7 %shard_map.89.partial = f32[192,768]{1,0:T(8,128)S(1)} custom-call(bf16[192,384]{1,0:T(8,128)(2,1)S(1)} %get-tuple-element.63.full, bf16[192,384]{1,0:T(8,128)(2,1)S(1)} %collective-permute-done.9.beside, bf16[192,256]{1,0:T(8,128)(2,1)S(1)} %collective-permute-done.10.across_most, bf16[192,128]{1,0:T(8,128)(2,1)S(1)} %collective-permute-done.11.across_last, ...), custom_call_target="tpu_custom_call" | custom-call | flops 452984832 | bytes 589824 | tf_op jit(solution)/shard_map/pallas_call | solution.py:343
  45.2 1.1 %collective-permute-done.14.most = bf16[192,256]{1,0:T(8,128)(2,1)S(1)} collective-permute-done((bf16[192,256]{1,0:T(8,128)(2,1)S(1)}, bf16[192,256]{1,0:T(8,128)(2,1)S(1)}, u32[]{:S(2)}, u32[]{:S(2)}) %collective-permute-start.14) | collective-permute-done | bytes 98336 | tf_op jit(solution)/shard_map/ppermute | solution.py:437
  46.4 2.0 %collective-permute-done.15.last = bf16[192,128]{1,0:T(8,128)(2,1)S(1)} collective-permute-done((bf16[192,128]{1,0:T(8,128)(2,1)S(1)}, bf16[192,128]{1,0:T(8,128)(2,1)S(1)}, u32[]{:S(2)}, u32[]{:S(2)}) %collective-permute-start.15) | collective-permute-done | bytes 49184 | tf_op jit(solution)/shard_map/ppermute | solution.py:437
  48.3 0.4 shard_map.90
  48.7 2.7 %collective-permute-start.16 = (bf16[48,768]{1,0:T(8,128)(2,1)S(1)}, bf16[48,768]{1,0:T(8,128)(2,1)S(1)}, u32[]{:S(2)}, u32[]{:S(2)}) collective-permute-start(bf16[48,768]{1,0:T(8,128)(2,1)S(1)} %get-tuple-element.72), channel_id=1, source_target_pairs={{0,24},{2,26},{4,28},{6,30},{8,16},{10,18},{12,20},{14,22},{16,8},... | collective-permute-start | bytes 221192 | tf_op jit(solution)/shard_map/ppermute | solution.py:437
  51.4 1.7 %collective-permute-start.18 = (bf16[48,768]{1,0:T(8,128)(2,1)S(1)}, bf16[48,768]{1,0:T(8,128)(2,1)S(1)}, u32[]{:S(2)}, u32[]{:S(2)}) collective-permute-start(bf16[48,768]{1,0:T(8,128)(2,1)S(1)} %get-tuple-element.74), channel_id=1, source_target_pairs={{0,8},{2,10},{4,12},{6,14},{8,0},{10,2},{12,4},{14,6},{16,24},{18,... | collective-permute-start | bytes 221192 | tf_op jit(solution)/shard_map/ppermute | solution.py:437
  53.2 1.8 %collective-permute-done.16.refs_1_ = bf16[48,768]{1,0:T(8,128)(2,1)S(1)} collective-permute-done((bf16[48,768]{1,0:T(8,128)(2,1)S(1)}, bf16[48,768]{1,0:T(8,128)(2,1)S(1)}, u32[]{:S(2)}, u32[]{:S(2)}) %collective-permute-start.16) | collective-permute-done | bytes 73760 | tf_op jit(solution)/shard_map/ppermute | solution.py:437
  54.9 2.1 %collective-permute-done.17.refs_2_ = bf16[48,768]{1,0:T(8,128)(2,1)S(1)} collective-permute-done((bf16[48,768]{1,0:T(8,128)(2,1)S(1)}, bf16[48,768]{1,0:T(8,128)(2,1)S(1)}, u32[]{:S(2)}, u32[]{:S(2)}) %collective-permute-start.17) | collective-permute-done | bytes 73760 | tf_op jit(solution)/shard_map/ppermute | solution.py:437
  57.1 1.6 %collective-permute-start.19 = (bf16[2,48,768]{2,1,0:T(8,128)(2,1)S(1)}, bf16[2,48,768]{2,1,0:T(8,128)(2,1)S(1)}, u32[]{:S(2)}, u32[]{:S(2)}) collective-permute-start(bf16[2,48,768]{2,1,0:T(8,128)(2,1)S(1)} %get-tuple-element.76), channel_id=1, source_target_pairs={{0,1},{1,0},{2,3},{3,2},{4,5},{5,4},{6,7},{7,6},{8,9},{9,8},{10,11... | collective-permute-start | bytes 442376 | tf_op jit(solution)/shard_map/ppermute | solution.py:473
  58.8 3.6 %collective-permute-done.19.arrived = bf16[2,48,768]{2,1,0:T(8,128)(2,1)S(1)} collective-permute-done((bf16[2,48,768]{2,1,0:T(8,128)(2,1)S(1)}, bf16[2,48,768]{2,1,0:T(8,128)(2,1)S(1)}, u32[]{:S(2)}, u32[]{:S(2)}) %collective-permute-start.19) | collective-permute-done | bytes 147488 | tf_op jit(solution)/shard_map/ppermute | solution.py:473
  62.4 0.7 %shard_map.92 = bf16[48,1536]{1,0:T(8,128)(2,1)} custom-call(bf16[2,48,768]{2,1,0:T(8,128)(2,1)S(1)} %get-tuple-element.75.kept, bf16[2,48,768]{2,1,0:T(8,128)(2,1)S(1)} %collective-permute-done.19.arrived, f32[1,1536]{1,0:T(1,128)S(1)} %reshape.6.bias, f32[1,1536]{1,0:T(1,128)S(1)} %reshape.7.gate), custom_call_target="tpu_custom_call" | custom-call | flops 221184 | bytes 294912 | tf_op jit(solution)/shard_map/pallas_call | solution.py:418
  (29 shorter events, 1.0 us)
Async XLA Ops:
  0.0 18.3 %collective-permute-start.3 = (bf16[192,1536]{1,0:T(8,128)(2,1)}, bf16[192,1536]{1,0:T(8,128)(2,1)S(1)}, u32[]{:S(2)}, u32[]{:S(2)}) collective-permute-start(bf16[192,1536]{1,0:T(8,128)(2,1)} %bitcast.2), channel_id=1, source_target_pairs={{0,4},{2,6},{4,0},{6,2},{8,12},{10,14},{12,8},{14,10},{16,20},{18,... | collective-permute-start | bytes 1769480 | tf_op jit(solution)/shard_map/ppermute | solution.py:437
  5.3 8.1 %collective-permute-start = (bf16[3,48,384]{2,1,0:T(8,128)(2,1)}, bf16[3,48,384]{2,1,0:T(8,128)(2,1)S(1)}, u32[]{:S(2)}, u32[]{:S(2)}) collective-permute-start(bf16[3,48,384]{2,1,0:T(8,128)(2,1)} %get-tuple-element.42), channel_id=1, source_target_pairs={{0,24},{2,26},{4,28},{6,30},{8,16},{10,18},{12,20},{14,22},{16,8},... | collective-permute-start | bytes 331784 | tf_op jit(solution)/shard_map/ppermute | solution.py:437
  8.9 9.3 %collective-permute-start.1 = (bf16[3,48,384]{2,1,0:T(8,128)(2,1)}, bf16[3,48,384]{2,1,0:T(8,128)(2,1)S(1)}, u32[]{:S(2)}, u32[]{:S(2)}) collective-permute-start(bf16[3,48,384]{2,1,0:T(8,128)(2,1)} %get-tuple-element.43), channel_id=1, source_target_pairs={{0,16},{2,18},{4,20},{6,22},{8,24},{10,26},{12,28},{14,30},{16,0},... | collective-permute-start | bytes 331784 | tf_op jit(solution)/shard_map/ppermute | solution.py:437
  8.9 9.3 %collective-permute-start.2 = (bf16[3,48,384]{2,1,0:T(8,128)(2,1)}, bf16[3,48,384]{2,1,0:T(8,128)(2,1)S(1)}, u32[]{:S(2)}, u32[]{:S(2)}) collective-permute-start(bf16[3,48,384]{2,1,0:T(8,128)(2,1)} %get-tuple-element.44), channel_id=1, source_target_pairs={{0,8},{2,10},{4,12},{6,14},{8,0},{10,2},{12,4},{14,6},{16,24},{18,... | collective-permute-start | bytes 331784 | tf_op jit(solution)/shard_map/ppermute | solution.py:437
  9.7 8.5 %copy-start.1 = (bf16[3,48,384]{2,1,0:T(8,128)(2,1)S(1)}, bf16[3,48,384]{2,1,0:T(8,128)(2,1)}, u32[]{:S(2)}) copy-start(bf16[3,48,384]{2,1,0:T(8,128)(2,1)} %get-tuple-element.41.refs_0_) | copy-start | bytes 331780
  9.7 8.5 %collective-permute-start.4 = (bf16[2,48,384]{2,1,0:T(8,128)(2,1)}, bf16[2,48,384]{2,1,0:T(8,128)(2,1)S(1)}, u32[]{:S(2)}, u32[]{:S(2)}) collective-permute-start(bf16[2,48,384]{2,1,0:T(8,128)(2,1)} %get-tuple-element.48), channel_id=1, source_target_pairs={{0,4},{2,6},{4,0},{6,2},{8,12},{10,14},{12,8},{14,10},{16,20},{18,... | collective-permute-start | bytes 221192 | tf_op jit(solution)/shard_map/ppermute | solution.py:437
  11.8 16.0 %copy-start = (bf16[1536,192]{0,1:T(8,128)(2,1)S(1)}, bf16[1536,192]{0,1:T(8,128)(2,1)}, u32[]{:S(2)}) copy-start(bf16[1536,192]{0,1:T(8,128)(2,1)} %param.13) | copy-start | bytes 1769476
  18.3 7.9 %collective-permute-start.5 = (bf16[4,2,48,384]{3,2,1,0:T(8,128)(2,1)S(1)}, bf16[4,2,48,384]{3,2,1,0:T(8,128)(2,1)S(1)}, u32[]{:S(2)}, u32[]{:S(2)}) collective-permute-start(bf16[4,2,48,384]{3,2,1,0:T(8,128)(2,1)S(1)} %get-tuple-element.52.every), channel_id=1, source_target_pairs={{0,2},{2,0},{4,6},{6,4},{8,10},{10,8},{12,14},{14,12},{16,18},{18,... | collective-permute-start | bytes 884744 | tf_op jit(solution)/shard_map/ppermute | solution.py:437
  18.4 7.8 %collective-permute-start.6 = (bf16[3,2,48,384]{3,2,1,0:T(8,128)(2,1)S(1)}, bf16[3,2,48,384]{3,2,1,0:T(8,128)(2,1)S(1)}, u32[]{:S(2)}, u32[]{:S(2)}) collective-permute-start(bf16[3,2,48,384]{3,2,1,0:T(8,128)(2,1)S(1)} %get-tuple-element.53), channel_id=1, source_target_pairs={{0,4},{2,6},{4,0},{6,2},{8,12},{10,14},{12,8},{14,10},{16,20},{18,... | collective-permute-start | bytes 663560 | tf_op jit(solution)/shard_map/ppermute | solution.py:437
  27.8 16.3 %collective-permute-start.12 = (bf16[192,1536]{1,0:T(8,128)(2,1)S(1)}, bf16[192,1536]{1,0:T(8,128)(2,1)S(1)}, u32[]{:S(2)}, u32[]{:S(2)}) collective-permute-start(bf16[192,1536]{1,0:T(8,128)(2,1)S(1)} %bitcast.3), channel_id=1, source_target_pairs={{0,2},{2,0},{4,6},{6,4},{8,10},{10,8},{12,14},{14,12},{16,18},{18,... | collective-permute-start | bytes 1769480 | tf_op jit(solution)/shard_map/ppermute | solution.py:437
  27.9 16.3 %collective-permute-start.13 = (bf16[192,1536]{1,0:T(8,128)(2,1)S(1)}, bf16[192,1536]{1,0:T(8,128)(2,1)S(1)}, u32[]{:S(2)}, u32[]{:S(2)}) collective-permute-start(bf16[192,1536]{1,0:T(8,128)(2,1)S(1)} %collective-permute-done.3.refs_2_), channel_id=1, source_target_pairs={{0,2},{2,0},{4,6},{6,4},{8,10},{10,8},{12,14},{14,12},{16,18},{18,... | collective-permute-start | bytes 1769480 | tf_op jit(solution)/shard_map/ppermute | solution.py:437
  28.4 2.8 %collective-permute-start.8 = (bf16[3,2,48,384]{3,2,1,0:T(8,128)(2,1)S(1)}, bf16[3,2,48,384]{3,2,1,0:T(8,128)(2,1)S(1)}, u32[]{:S(2)}, u32[]{:S(2)}) collective-permute-start(bf16[3,2,48,384]{3,2,1,0:T(8,128)(2,1)S(1)} %collective-permute-done.6.some_far), channel_id=1, source_target_pairs={{0,2},{2,0},{4,6},{6,4},{8,10},{10,8},{12,14},{14,12},{16,18},{18,... | collective-permute-start | bytes 663560 | tf_op jit(solution)/shard_map/ppermute | solution.py:437
  28.5 2.7 %collective-permute-start.7 = (bf16[2,48,384]{2,1,0:T(8,128)(2,1)S(1)}, bf16[2,48,384]{2,1,0:T(8,128)(2,1)S(1)}, u32[]{:S(2)}, u32[]{:S(2)}) collective-permute-start(bf16[2,48,384]{2,1,0:T(8,128)(2,1)S(1)} %collective-permute-done.4.own_far), channel_id=1, source_target_pairs={{0,2},{2,0},{4,6},{6,4},{8,10},{10,8},{12,14},{14,12},{16,18},{18,... | collective-permute-start | bytes 221192 | tf_op jit(solution)/shard_map/ppermute | solution.py:437
  32.5 11.7 %collective-permute-start.9 = (bf16[192,384]{1,0:T(8,128)(2,1)S(1)}, bf16[192,384]{1,0:T(8,128)(2,1)S(1)}, u32[]{:S(2)}, u32[]{:S(2)}) collective-permute-start(bf16[192,384]{1,0:T(8,128)(2,1)S(1)} %get-tuple-element.63.full), channel_id=1, source_target_pairs={{0,8},{2,10},{4,12},{6,14},{8,0},{10,2},{12,4},{14,6},{16,24},{18,... | collective-permute-start | bytes 442376 | tf_op jit(solution)/shard_map/ppermute | solution.py:437
  34.1 6.1 %collective-permute-start.10 = (bf16[192,256]{1,0:T(8,128)(2,1)S(1)}, bf16[192,256]{1,0:T(8,128)(2,1)S(1)}, u32[]{:S(2)}, u32[]{:S(2)}) collective-permute-start(bf16[192,256]{1,0:T(8,128)(2,1)S(1)} %get-tuple-element.64), channel_id=1, source_target_pairs={{0,16},{2,18},{4,20},{6,22},{8,24},{10,26},{12,28},{14,30},{16,0},... | collective-permute-start | bytes 294920 | tf_op jit(solution)/shard_map/ppermute | solution.py:437
  36.7 7.5 %collective-permute-start.11 = (bf16[192,128]{1,0:T(8,128)(2,1)S(1)}, bf16[192,128]{1,0:T(8,128)(2,1)S(1)}, u32[]{:S(2)}, u32[]{:S(2)}) collective-permute-start(bf16[192,128]{1,0:T(8,128)(2,1)S(1)} %get-tuple-element.65), channel_id=1, source_target_pairs={{0,16},{2,18},{4,20},{6,22},{8,24},{10,26},{12,28},{14,30},{16,0},... | collective-permute-start | bytes 147464 | tf_op jit(solution)/shard_map/ppermute | solution.py:437
  40.2 6.2 %collective-permute-start.14 = (bf16[192,256]{1,0:T(8,128)(2,1)S(1)}, bf16[192,256]{1,0:T(8,128)(2,1)S(1)}, u32[]{:S(2)}, u32[]{:S(2)}) collective-permute-start(bf16[192,256]{1,0:T(8,128)(2,1)S(1)} %collective-permute-done.10.across_most), channel_id=1, source_target_pairs={{0,8},{2,10},{4,12},{6,14},{8,0},{10,2},{12,4},{14,6},{16,24},{18,... | collective-permute-start | bytes 294920 | tf_op jit(solution)/shard_map/ppermute | solution.py:437
  44.2 4.2 %collective-permute-start.15 = (bf16[192,128]{1,0:T(8,128)(2,1)S(1)}, bf16[192,128]{1,0:T(8,128)(2,1)S(1)}, u32[]{:S(2)}, u32[]{:S(2)}) collective-permute-start(bf16[192,128]{1,0:T(8,128)(2,1)S(1)} %collective-permute-done.11.across_last), channel_id=1, source_target_pairs={{0,8},{2,10},{4,12},{6,14},{8,0},{10,2},{12,4},{14,6},{16,24},{18,... | collective-permute-start | bytes 147464 | tf_op jit(solution)/shard_map/ppermute | solution.py:437
  44.5 14.2 %copy-start.2 = (f32[1536]{0:T(1024)S(1)}, f32[1536]{0:T(1024)}, u32[]{:S(2)}) copy-start(f32[1536]{0:T(1024)} %param.14) | copy-start | bytes 18436
  44.5 14.2 %copy-start.3 = (f32[1536]{0:T(1024)S(1)}, f32[1536]{0:T(1024)}, u32[]{:S(2)}) copy-start(f32[1536]{0:T(1024)} %param.15) | copy-start | bytes 18436
  48.7 6.2 %collective-permute-start.16 = (bf16[48,768]{1,0:T(8,128)(2,1)S(1)}, bf16[48,768]{1,0:T(8,128)(2,1)S(1)}, u32[]{:S(2)}, u32[]{:S(2)}) collective-permute-start(bf16[48,768]{1,0:T(8,128)(2,1)S(1)} %get-tuple-element.72), channel_id=1, source_target_pairs={{0,24},{2,26},{4,28},{6,30},{8,16},{10,18},{12,20},{14,22},{16,8},... | collective-permute-start | bytes 221192 | tf_op jit(solution)/shard_map/ppermute | solution.py:437
  51.4 5.6 %collective-permute-start.17 = (bf16[48,768]{1,0:T(8,128)(2,1)S(1)}, bf16[48,768]{1,0:T(8,128)(2,1)S(1)}, u32[]{:S(2)}, u32[]{:S(2)}) collective-permute-start(bf16[48,768]{1,0:T(8,128)(2,1)S(1)} %get-tuple-element.73), channel_id=1, source_target_pairs={{0,16},{2,18},{4,20},{6,22},{8,24},{10,26},{12,28},{14,30},{16,0},... | collective-permute-start | bytes 221192 | tf_op jit(solution)/shard_map/ppermute | solution.py:437
  51.4 5.6 %collective-permute-start.18 = (bf16[48,768]{1,0:T(8,128)(2,1)S(1)}, bf16[48,768]{1,0:T(8,128)(2,1)S(1)}, u32[]{:S(2)}, u32[]{:S(2)}) collective-permute-start(bf16[48,768]{1,0:T(8,128)(2,1)S(1)} %get-tuple-element.74), channel_id=1, source_target_pairs={{0,8},{2,10},{4,12},{6,14},{8,0},{10,2},{12,4},{14,6},{16,24},{18,... | collective-permute-start | bytes 221192 | tf_op jit(solution)/shard_map/ppermute | solution.py:437
  57.1 5.2 %collective-permute-start.19 = (bf16[2,48,768]{2,1,0:T(8,128)(2,1)S(1)}, bf16[2,48,768]{2,1,0:T(8,128)(2,1)S(1)}, u32[]{:S(2)}, u32[]{:S(2)}) collective-permute-start(bf16[2,48,768]{2,1,0:T(8,128)(2,1)S(1)} %get-tuple-element.76), channel_id=1, source_target_pairs={{0,1},{1,0},{2,3},{3,2},{4,5},{5,4},{6,7},{7,6},{8,9},{9,8},{10,11... | collective-permute-start | bytes 442376 | tf_op jit(solution)/shard_map/ppermute | solution.py:473

commit v11 on v10

--- a/solution.py
+++ b/solution.py
@@ -456,7 +456,7 @@
     near, some_far, own_far = lax.optimization_barrier((near, some_far, own_far, *state))[:3]
     own_corner, some_corner = swap(own_far, 1), swap(some_far, 1)
     state = attend_call(middle_kernel, [query, near, own_far, some_far, stale, *state], state_shapes(query), 2 * share)
-    weight, weight_far = lax.optimization_barrier((weight, weight_far, *state))[:2]
+    weight, weight_far = lax.optimization_barrier((weight, weight_far, own_corner, some_corner, *state))[:2]
     weight_near, weight_corner = swap(weight, 1), swap(weight_far, 1)
     operands = [query, own_corner, some_corner, stale, *state]
     full, most, last = attend_call(last_kernel, operands, result_shapes(query), share)

time: 63.3 us -> 61.2 us (0.967)
  waiting for transfers between devices: 28.2 us -> 26.1 us
    ppermute x19, waiting for transfers between devices: 24.6 us -> 22.5 us  [swap(): return lax.ppermute(value, 'patch', [(p, p ^ twist) for p in range(size)])]
  transfers between devices with their start and end apart: 20 -> 20, of which waited for: 11 -> 10; matrix products, arithmetic and copies ran while one was open for 0% -> 0% of each run, Pallas kernels for 12% -> 15%
where the time goes in v11:
time: 61.2 us; the launch traced here: 61 us
  waiting for transfers between devices  26.1 us (43%)
  starting transfers between devices  24.6 us (40%)
  Pallas kernels  10 us (16%)
    ppermute x19, starting transfers between devices, swap(): return lax.ppermute(value, 'patch', [(p, p ^ twist) for p in range(size)])  23 us
    ppermute x19, waiting for transfers between devices, swap(): return lax.ppermute(value, 'patch', [(p, p ^ twist) for p in range(size)])  22.5 us
    pallas_call x3, Pallas kernels, attend_call(): pl.pallas_call(kernel, out_shape=shapes, in_specs=[VMEM] * len(operands),...  3.93 us
    ppermute x1, waiting for transfers between devices, grouped_body(): received = lax.ppermute(sent, 'head', [(0, 1), (1, 0)])  3.58 us
    pallas_call x1, Pallas kernels, pack(): pl.pallas_call(pack_kernel, out_shape=[jax.ShapeDtypeStruct(shape, bf16)...  2.33 us
    pallas_call x1, Pallas kernels, pick(): pl.pallas_call(pick_kernel, out_shape=[jax.ShapeDtypeStruct((kinds, texts...  1.65 us
    ppermute x1, starting transfers between devices, grouped_body(): received = lax.ppermute(sent, 'head', [(0, 1), (1, 0)])  1.59 us
  transfers between devices with their start and end apart: 20, of which 10 were waited for; matrix products, arithmetic and copies ran while one was open for 0% of the time, Pallas kernels for 15%

profile of v11, /device:TPU:0, one launch (start us, length us, event | category | flops | bytes accessed | tf_op | source)
XLA Modules:
  0.0 61.0 jit_solution(5213681802996704416)
XLA Ops:
  0.0 2.9 %collective-permute-start.3 = (bf16[192,1536]{1,0:T(8,128)(2,1)}, bf16[192,1536]{1,0:T(8,128)(2,1)S(1)}, u32[]{:S(2)}, u32[]{:S(2)}) collective-permute-start(bf16[192,1536]{1,0:T(8,128)(2,1)} %bitcast.2), channel_id=1, source_target_pairs={{0,4},{2,6},{4,0},{6,2},{8,12},{10,14},{12,8},{14,10},{16,20},{18,... | collective-permute-start | bytes 1769480 | tf_op jit(solution)/shard_map/ppermute | solution.py:437
  2.9 2.3 %shard_map.82 = (bf16[3,48,384]{2,1,0:T(8,128)(2,1)}, bf16[3,48,384]{2,1,0:T(8,128)(2,1)}, bf16[3,48,384]{2,1,0:T(8,128)(2,1)}, bf16[3,48,384]{2,1,0:T(8,128)(2,1)}, bf16[2,48,384]{2,1,0:T(8,128)(2,1)}) custom-call(bf16[48,1536]{1,0:T(8,128)(2,1)} %queries_hbm.1, s32[2,48,1536]{2,1,0:T(8,128)} %codes_hbm.1, s32[12,2,48]{2,1,0:T(2,128)} %bitcast.5), custom_call_target="tpu_custom_call" | custom-call | flops 294912 | bytes 884736 | tf_op jit(solution)/shard_map/pallas_call | solution.py:109
  5.3 3.7 %collective-permute-start = (bf16[3,48,384]{2,1,0:T(8,128)(2,1)}, bf16[3,48,384]{2,1,0:T(8,128)(2,1)S(1)}, u32[]{:S(2)}, u32[]{:S(2)}) collective-permute-start(bf16[3,48,384]{2,1,0:T(8,128)(2,1)} %get-tuple-element.42), channel_id=1, source_target_pairs={{0,24},{2,26},{4,28},{6,30},{8,16},{10,18},{12,20},{14,22},{16,8},... | collective-permute-start | bytes 331784 | tf_op jit(solution)/shard_map/ppermute | solution.py:437
  8.9 0.8 %collective-permute-start.2 = (bf16[3,48,384]{2,1,0:T(8,128)(2,1)}, bf16[3,48,384]{2,1,0:T(8,128)(2,1)S(1)}, u32[]{:S(2)}, u32[]{:S(2)}) collective-permute-start(bf16[3,48,384]{2,1,0:T(8,128)(2,1)} %get-tuple-element.44), channel_id=1, source_target_pairs={{0,8},{2,10},{4,12},{6,14},{8,0},{10,2},{12,4},{14,6},{16,24},{18,... | collective-permute-start | bytes 331784 | tf_op jit(solution)/shard_map/ppermute | solution.py:437
  9.7 0.4 collective-permute-start.4
  10.1 1.7 %shard_map.84 = (bf16[2,512,384]{2,1,0:T(8,128)(2,1)S(1)}, bf16[4,2,192,384]{3,2,1,0:T(8,128)(2,1)S(1)}) custom-call(bf16[2,512,1536]{2,1,0:T(8,128)(2,1)} %text_hbm.1, bf16[2,768,1536]{2,1,0:T(8,128)(2,1)} %stale_hbm.1), custom_call_target="tpu_custom_call" | custom-call | bytes 8388608 | tf_op jit(solution)/shard_map/pallas_call | solution.py:154
  11.8 1.5 %collective-permute-done.refs_1_ = bf16[3,48,384]{2,1,0:T(8,128)(2,1)S(1)} collective-permute-done((bf16[3,48,384]{2,1,0:T(8,128)(2,1)}, bf16[3,48,384]{2,1,0:T(8,128)(2,1)S(1)}, u32[]{:S(2)}, u32[]{:S(2)}) %collective-permute-start) | collective-permute-done | bytes 110624 | tf_op jit(solution)/shard_map/ppermute | solution.py:437
  13.3 4.9 %collective-permute-done.1.refs_2_ = bf16[3,48,384]{2,1,0:T(8,128)(2,1)S(1)} collective-permute-done((bf16[3,48,384]{2,1,0:T(8,128)(2,1)}, bf16[3,48,384]{2,1,0:T(8,128)(2,1)S(1)}, u32[]{:S(2)}, u32[]{:S(2)}) %collective-permute-start.1) | collective-permute-done | bytes 110624 | tf_op jit(solution)/shard_map/ppermute | solution.py:437
  18.4 1.4 %collective-permute-start.6 = (bf16[3,2,48,384]{3,2,1,0:T(8,128)(2,1)S(1)}, bf16[3,2,48,384]{3,2,1,0:T(8,128)(2,1)S(1)}, u32[]{:S(2)}, u32[]{:S(2)}) collective-permute-start(bf16[3,2,48,384]{3,2,1,0:T(8,128)(2,1)S(1)} %get-tuple-element.53), channel_id=1, source_target_pairs={{0,4},{2,6},{4,0},{6,2},{8,12},{10,14},{12,8},{14,10},{16,20},{18,... | collective-permute-start | bytes 663560 | tf_op jit(solution)/shard_map/ppermute | solution.py:437
  19.8 1.0 %shard_map.85 = (f32[3,192,1]{2,1,0:T(8,128)S(1)}, f32[3,192,1]{2,1,0:T(8,128)S(1)}, f32[3,192,128]{2,1,0:T(8,128)S(1)}) custom-call(bf16[192,384]{1,0:T(8,128)(2,1)S(1)} %get-tuple-element.51.query, bf16[4,2,48,384]{3,2,1,0:T(8,128)(2,1)S(1)} %get-tuple-element.52.every, bf16[2,512,384]{2,1,0:T(8,128)(2,1)S(1)} %get-tuple-element.49.text, ...), custom_call_target="tpu_custom_call" | custom-call | flops 415236096 | bytes 2162688 | tf_op jit(solution)/shard_map/pallas_call | solution.py:282
  20.8 5.4 %collective-permute-done.6.some_far = bf16[3,2,48,384]{3,2,1,0:T(8,128)(2,1)S(1)} collective-permute-done((bf16[3,2,48,384]{3,2,1,0:T(8,128)(2,1)S(1)}, bf16[3,2,48,384]{3,2,1,0:T(8,128)(2,1)S(1)}, u32[]{:S(2)}, u32[]{:S(2)}) %collective-permute-start.6) | collective-permute-done | bytes 221216 | tf_op jit(solution)/shard_map/ppermute | solution.py:437
  26.2 0.5 collective-permute-start.7
  26.7 1.6 %shard_map.86 = (f32[3,192,1]{2,1,0:T(8,128)S(1)}, f32[3,192,1]{2,1,0:T(8,128)S(1)}, f32[3,192,128]{2,1,0:T(8,128)S(1)}) custom-call(bf16[192,384]{1,0:T(8,128)(2,1)S(1)} %get-tuple-element.51.query, bf16[4,2,48,384]{3,2,1,0:T(8,128)(2,1)S(1)} %collective-permute-done.5.near, bf16[2,48,384]{2,1,0:T(8,128)(2,1)S(1)} %collective-permute-done.4.own_far, ...), custom_call_target="tpu_custom_call" | custom-call | flops 226492416 | bytes 1179648 | tf_op jit(solution)/shard_map/pallas_call | solution.py:282
  28.4 0.5 collective-permute-start.13
  28.9 1.3 %shard_map.87 = (bf16[192,384]{1,0:T(8,128)(2,1)S(1)}, bf16[192,256]{1,0:T(8,128)(2,1)S(1)}, bf16[192,128]{1,0:T(8,128)(2,1)S(1)}) custom-call(bf16[192,384]{1,0:T(8,128)(2,1)S(1)} %get-tuple-element.51.query, bf16[2,48,384]{2,1,0:T(8,128)(2,1)S(1)} %collective-permute-done.7.own_corner, bf16[3,2,48,384]{3,2,1,0:T(8,128)(2,1)S(1)} %collective-permute-done.8.some_corner, ...), custom_call_target="tpu_custom_call" | custom-call | flops 113246208 | bytes 589824 | tf_op jit(solution)/shard_map/pallas_call | solution.py:282
  30.3 1.6 %collective-permute-start.9 = (bf16[192,384]{1,0:T(8,128)(2,1)S(1)}, bf16[192,384]{1,0:T(8,128)(2,1)S(1)}, u32[]{:S(2)}, u32[]{:S(2)}) collective-permute-start(bf16[192,384]{1,0:T(8,128)(2,1)S(1)} %get-tuple-element.63.full), channel_id=1, source_target_pairs={{0,8},{2,10},{4,12},{6,14},{8,0},{10,2},{12,4},{14,6},{16,24},{18,... | collective-permute-start | bytes 442376 | tf_op jit(solution)/shard_map/ppermute | solution.py:437
  31.8 2.6 %collective-permute-start.10 = (bf16[192,256]{1,0:T(8,128)(2,1)S(1)}, bf16[192,256]{1,0:T(8,128)(2,1)S(1)}, u32[]{:S(2)}, u32[]{:S(2)}) collective-permute-start(bf16[192,256]{1,0:T(8,128)(2,1)S(1)} %get-tuple-element.64), channel_id=1, source_target_pairs={{0,16},{2,18},{4,20},{6,22},{8,24},{10,26},{12,28},{14,30},{16,0},... | collective-permute-start | bytes 294920 | tf_op jit(solution)/shard_map/ppermute | solution.py:437
  34.4 0.3 collective-permute-start.11
  34.8 3.1 %collective-permute-done.10.across_most = bf16[192,256]{1,0:T(8,128)(2,1)S(1)} collective-permute-done((bf16[192,256]{1,0:T(8,128)(2,1)S(1)}, bf16[192,256]{1,0:T(8,128)(2,1)S(1)}, u32[]{:S(2)}, u32[]{:S(2)}) %collective-permute-start.10) | collective-permute-done | bytes 98336 | tf_op jit(solution)/shard_map/ppermute | solution.py:437
  37.9 3.5 %collective-permute-start.14 = (bf16[192,256]{1,0:T(8,128)(2,1)S(1)}, bf16[192,256]{1,0:T(8,128)(2,1)S(1)}, u32[]{:S(2)}, u32[]{:S(2)}) collective-permute-start(bf16[192,256]{1,0:T(8,128)(2,1)S(1)} %collective-permute-done.10.across_most), channel_id=1, source_target_pairs={{0,8},{2,10},{4,12},{6,14},{8,0},{10,2},{12,4},{14,6},{16,24},{18,... | collective-permute-start | bytes 294920 | tf_op jit(solution)/shard_map/ppermute | solution.py:437
  41.4 0.4 collective-permute-done.11.across_last
  42.2 0.7 %shard_map.89.partial = f32[192,768]{1,0:T(8,128)S(1)} custom-call(bf16[192,384]{1,0:T(8,128)(2,1)S(1)} %get-tuple-element.63.full, bf16[192,384]{1,0:T(8,128)(2,1)S(1)} %collective-permute-done.9.beside, bf16[192,256]{1,0:T(8,128)(2,1)S(1)} %collective-permute-done.10.across_most, bf16[192,128]{1,0:T(8,128)(2,1)S(1)} %collective-permute-done.11.across_last, ...), custom_call_target="tpu_custom_call" | custom-call | flops 452984832 | bytes 589824 | tf_op jit(solution)/shard_map/pallas_call | solution.py:343
  43.0 1.1 %collective-permute-done.14.most = bf16[192,256]{1,0:T(8,128)(2,1)S(1)} collective-permute-done((bf16[192,256]{1,0:T(8,128)(2,1)S(1)}, bf16[192,256]{1,0:T(8,128)(2,1)S(1)}, u32[]{:S(2)}, u32[]{:S(2)}) %collective-permute-start.14) | collective-permute-done | bytes 98336 | tf_op jit(solution)/shard_map/ppermute | solution.py:437
  44.0 2.0 %collective-permute-done.15.last = bf16[192,128]{1,0:T(8,128)(2,1)S(1)} collective-permute-done((bf16[192,128]{1,0:T(8,128)(2,1)S(1)}, bf16[192,128]{1,0:T(8,128)(2,1)S(1)}, u32[]{:S(2)}, u32[]{:S(2)}) %collective-permute-start.15) | collective-permute-done | bytes 49184 | tf_op jit(solution)/shard_map/ppermute | solution.py:437
  46.0 0.4 shard_map.90
  46.4 2.7 %collective-permute-start.16 = (bf16[48,768]{1,0:T(8,128)(2,1)S(1)}, bf16[48,768]{1,0:T(8,128)(2,1)S(1)}, u32[]{:S(2)}, u32[]{:S(2)}) collective-permute-start(bf16[48,768]{1,0:T(8,128)(2,1)S(1)} %get-tuple-element.72), channel_id=1, source_target_pairs={{0,24},{2,26},{4,28},{6,30},{8,16},{10,18},{12,20},{14,22},{16,8},... | collective-permute-start | bytes 221192 | tf_op jit(solution)/shard_map/ppermute | solution.py:437
  49.2 1.7 %collective-permute-start.18 = (bf16[48,768]{1,0:T(8,128)(2,1)S(1)}, bf16[48,768]{1,0:T(8,128)(2,1)S(1)}, u32[]{:S(2)}, u32[]{:S(2)}) collective-permute-start(bf16[48,768]{1,0:T(8,128)(2,1)S(1)} %get-tuple-element.74), channel_id=1, source_target_pairs={{0,8},{2,10},{4,12},{6,14},{8,0},{10,2},{12,4},{14,6},{16,24},{18,... | collective-permute-start | bytes 221192 | tf_op jit(solution)/shard_map/ppermute | solution.py:437
  50.9 1.8 %collective-permute-done.16.refs_1_ = bf16[48,768]{1,0:T(8,128)(2,1)S(1)} collective-permute-done((bf16[48,768]{1,0:T(8,128)(2,1)S(1)}, bf16[48,768]{1,0:T(8,128)(2,1)S(1)}, u32[]{:S(2)}, u32[]{:S(2)}) %collective-permute-start.16) | collective-permute-done | bytes 73760 | tf_op jit(solution)/shard_map/ppermute | solution.py:437
  52.6 2.3 %collective-permute-done.17.refs_2_ = bf16[48,768]{1,0:T(8,128)(2,1)S(1)} collective-permute-done((bf16[48,768]{1,0:T(8,128)(2,1)S(1)}, bf16[48,768]{1,0:T(8,128)(2,1)S(1)}, u32[]{:S(2)}, u32[]{:S(2)}) %collective-permute-start.17) | collective-permute-done | bytes 73760 | tf_op jit(solution)/shard_map/ppermute | solution.py:437
  55.0 1.6 %collective-permute-start.19 = (bf16[2,48,768]{2,1,0:T(8,128)(2,1)S(1)}, bf16[2,48,768]{2,1,0:T(8,128)(2,1)S(1)}, u32[]{:S(2)}, u32[]{:S(2)}) collective-permute-start(bf16[2,48,768]{2,1,0:T(8,128)(2,1)S(1)} %get-tuple-element.76), channel_id=1, source_target_pairs={{0,1},{1,0},{2,3},{3,2},{4,5},{5,4},{6,7},{7,6},{8,9},{9,8},{10,11... | collective-permute-start | bytes 442376 | tf_op jit(solution)/shard_map/ppermute | solution.py:473
  56.7 3.6 %collective-permute-done.19.arrived = bf16[2,48,768]{2,1,0:T(8,128)(2,1)S(1)} collective-permute-done((bf16[2,48,768]{2,1,0:T(8,128)(2,1)S(1)}, bf16[2,48,768]{2,1,0:T(8,128)(2,1)S(1)}, u32[]{:S(2)}, u32[]{:S(2)}) %collective-permute-start.19) | collective-permute-done | bytes 147488 | tf_op jit(solution)/shard_map/ppermute | solution.py:473
  60.2 0.7 %shard_map.92 = bf16[48,1536]{1,0:T(8,128)(2,1)} custom-call(bf16[2,48,768]{2,1,0:T(8,128)(2,1)S(1)} %get-tuple-element.75.kept, bf16[2,48,768]{2,1,0:T(8,128)(2,1)S(1)} %collective-permute-done.19.arrived, f32[1,1536]{1,0:T(1,128)S(1)} %reshape.6.bias, f32[1,1536]{1,0:T(1,128)S(1)} %reshape.7.gate), custom_call_target="tpu_custom_call" | custom-call | flops 221184 | bytes 294912 | tf_op jit(solution)/shard_map/pallas_call | solution.py:418
  (29 shorter events, 0.6 us)
Async XLA Ops:
  0.0 18.3 %collective-permute-start.3 = (bf16[192,1536]{1,0:T(8,128)(2,1)}, bf16[192,1536]{1,0:T(8,128)(2,1)S(1)}, u32[]{:S(2)}, u32[]{:S(2)}) collective-permute-start(bf16[192,1536]{1,0:T(8,128)(2,1)} %bitcast.2), channel_id=1, source_target_pairs={{0,4},{2,6},{4,0},{6,2},{8,12},{10,14},{12,8},{14,10},{16,20},{18,... | collective-permute-start | bytes 1769480 | tf_op jit(solution)/shard_map/ppermute | solution.py:437
  5.3 8.1 %collective-permute-start = (bf16[3,48,384]{2,1,0:T(8,128)(2,1)}, bf16[3,48,384]{2,1,0:T(8,128)(2,1)S(1)}, u32[]{:S(2)}, u32[]{:S(2)}) collective-permute-start(bf16[3,48,384]{2,1,0:T(8,128)(2,1)} %get-tuple-element.42), channel_id=1, source_target_pairs={{0,24},{2,26},{4,28},{6,30},{8,16},{10,18},{12,20},{14,22},{16,8},... | collective-permute-start | bytes 331784 | tf_op jit(solution)/shard_map/ppermute | solution.py:437
  8.9 9.3 %collective-permute-start.1 = (bf16[3,48,384]{2,1,0:T(8,128)(2,1)}, bf16[3,48,384]{2,1,0:T(8,128)(2,1)S(1)}, u32[]{:S(2)}, u32[]{:S(2)}) collective-permute-start(bf16[3,48,384]{2,1,0:T(8,128)(2,1)} %get-tuple-element.43), channel_id=1, source_target_pairs={{0,16},{2,18},{4,20},{6,22},{8,24},{10,26},{12,28},{14,30},{16,0},... | collective-permute-start | bytes 331784 | tf_op jit(solution)/shard_map/ppermute | solution.py:437
  8.9 9.3 %collective-permute-start.2 = (bf16[3,48,384]{2,1,0:T(8,128)(2,1)}, bf16[3,48,384]{2,1,0:T(8,128)(2,1)S(1)}, u32[]{:S(2)}, u32[]{:S(2)}) collective-permute-start(bf16[3,48,384]{2,1,0:T(8,128)(2,1)} %get-tuple-element.44), channel_id=1, source_target_pairs={{0,8},{2,10},{4,12},{6,14},{8,0},{10,2},{12,4},{14,6},{16,24},{18,... | collective-permute-start | bytes 331784 | tf_op jit(solution)/shard_map/ppermute | solution.py:437
  9.7 8.5 %copy-start.1 = (bf16[3,48,384]{2,1,0:T(8,128)(2,1)S(1)}, bf16[3,48,384]{2,1,0:T(8,128)(2,1)}, u32[]{:S(2)}) copy-start(bf16[3,48,384]{2,1,0:T(8,128)(2,1)} %get-tuple-element.41.refs_0_) | copy-start | bytes 331780
  9.7 8.5 %collective-permute-start.4 = (bf16[2,48,384]{2,1,0:T(8,128)(2,1)}, bf16[2,48,384]{2,1,0:T(8,128)(2,1)S(1)}, u32[]{:S(2)}, u32[]{:S(2)}) collective-permute-start(bf16[2,48,384]{2,1,0:T(8,128)(2,1)} %get-tuple-element.48), channel_id=1, source_target_pairs={{0,4},{2,6},{4,0},{6,2},{8,12},{10,14},{12,8},{14,10},{16,20},{18,... | collective-permute-start | bytes 221192 | tf_op jit(solution)/shard_map/ppermute | solution.py:437
  11.8 16.6 %copy-start = (bf16[1536,192]{0,1:T(8,128)(2,1)S(1)}, bf16[1536,192]{0,1:T(8,128)(2,1)}, u32[]{:S(2)}) copy-start(bf16[1536,192]{0,1:T(8,128)(2,1)} %param.13) | copy-start | bytes 1769476
  18.3 7.9 %collective-permute-start.5 = (bf16[4,2,48,384]{3,2,1,0:T(8,128)(2,1)S(1)}, bf16[4,2,48,384]{3,2,1,0:T(8,128)(2,1)S(1)}, u32[]{:S(2)}, u32[]{:S(2)}) collective-permute-start(bf16[4,2,48,384]{3,2,1,0:T(8,128)(2,1)S(1)} %get-tuple-element.52.every), channel_id=1, source_target_pairs={{0,2},{2,0},{4,6},{6,4},{8,10},{10,8},{12,14},{14,12},{16,18},{18,... | collective-permute-start | bytes 884744 | tf_op jit(solution)/shard_map/ppermute | solution.py:437
  18.4 7.8 %collective-permute-start.6 = (bf16[3,2,48,384]{3,2,1,0:T(8,128)(2,1)S(1)}, bf16[3,2,48,384]{3,2,1,0:T(8,128)(2,1)S(1)}, u32[]{:S(2)}, u32[]{:S(2)}) collective-permute-start(bf16[3,2,48,384]{3,2,1,0:T(8,128)(2,1)S(1)} %get-tuple-element.53), channel_id=1, source_target_pairs={{0,4},{2,6},{4,0},{6,2},{8,12},{10,14},{12,8},{14,10},{16,20},{18,... | collective-permute-start | bytes 663560 | tf_op jit(solution)/shard_map/ppermute | solution.py:437
  26.2 2.1 %collective-permute-start.8 = (bf16[3,2,48,384]{3,2,1,0:T(8,128)(2,1)S(1)}, bf16[3,2,48,384]{3,2,1,0:T(8,128)(2,1)S(1)}, u32[]{:S(2)}, u32[]{:S(2)}) collective-permute-start(bf16[3,2,48,384]{3,2,1,0:T(8,128)(2,1)S(1)} %collective-permute-done.6.some_far), channel_id=1, source_target_pairs={{0,2},{2,0},{4,6},{6,4},{8,10},{10,8},{12,14},{14,12},{16,18},{18,... | collective-permute-start | bytes 663560 | tf_op jit(solution)/shard_map/ppermute | solution.py:437
  26.2 2.1 %collective-permute-start.7 = (bf16[2,48,384]{2,1,0:T(8,128)(2,1)S(1)}, bf16[2,48,384]{2,1,0:T(8,128)(2,1)S(1)}, u32[]{:S(2)}, u32[]{:S(2)}) collective-permute-start(bf16[2,48,384]{2,1,0:T(8,128)(2,1)S(1)} %collective-permute-done.4.own_far), channel_id=1, source_target_pairs={{0,2},{2,0},{4,6},{6,4},{8,10},{10,8},{12,14},{14,12},{16,18},{18,... | collective-permute-start | bytes 221192 | tf_op jit(solution)/shard_map/ppermute | solution.py:437
  28.3 13.5 %collective-permute-start.12 = (bf16[192,1536]{1,0:T(8,128)(2,1)S(1)}, bf16[192,1536]{1,0:T(8,128)(2,1)S(1)}, u32[]{:S(2)}, u32[]{:S(2)}) collective-permute-start(bf16[192,1536]{1,0:T(8,128)(2,1)S(1)} %bitcast.3), channel_id=1, source_target_pairs={{0,2},{2,0},{4,6},{6,4},{8,10},{10,8},{12,14},{14,12},{16,18},{18,... | collective-permute-start | bytes 1769480 | tf_op jit(solution)/shard_map/ppermute | solution.py:437
  28.4 13.4 %collective-permute-start.13 = (bf16[192,1536]{1,0:T(8,128)(2,1)S(1)}, bf16[192,1536]{1,0:T(8,128)(2,1)S(1)}, u32[]{:S(2)}, u32[]{:S(2)}) collective-permute-start(bf16[192,1536]{1,0:T(8,128)(2,1)S(1)} %collective-permute-done.3.refs_2_), channel_id=1, source_target_pairs={{0,2},{2,0},{4,6},{6,4},{8,10},{10,8},{12,14},{14,12},{16,18},{18,... | collective-permute-start | bytes 1769480 | tf_op jit(solution)/shard_map/ppermute | solution.py:437
  30.3 11.6 %collective-permute-start.9 = (bf16[192,384]{1,0:T(8,128)(2,1)S(1)}, bf16[192,384]{1,0:T(8,128)(2,1)S(1)}, u32[]{:S(2)}, u32[]{:S(2)}) collective-permute-start(bf16[192,384]{1,0:T(8,128)(2,1)S(1)} %get-tuple-element.63.full), channel_id=1, source_target_pairs={{0,8},{2,10},{4,12},{6,14},{8,0},{10,2},{12,4},{14,6},{16,24},{18,... | collective-permute-start | bytes 442376 | tf_op jit(solution)/shard_map/ppermute | solution.py:437
  31.8 6.0 %collective-permute-start.10 = (bf16[192,256]{1,0:T(8,128)(2,1)S(1)}, bf16[192,256]{1,0:T(8,128)(2,1)S(1)}, u32[]{:S(2)}, u32[]{:S(2)}) collective-permute-start(bf16[192,256]{1,0:T(8,128)(2,1)S(1)} %get-tuple-element.64), channel_id=1, source_target_pairs={{0,16},{2,18},{4,20},{6,22},{8,24},{10,26},{12,28},{14,30},{16,0},... | collective-permute-start | bytes 294920 | tf_op jit(solution)/shard_map/ppermute | solution.py:437
  34.4 7.4 %collective-permute-start.11 = (bf16[192,128]{1,0:T(8,128)(2,1)S(1)}, bf16[192,128]{1,0:T(8,128)(2,1)S(1)}, u32[]{:S(2)}, u32[]{:S(2)}) collective-permute-start(bf16[192,128]{1,0:T(8,128)(2,1)S(1)} %get-tuple-element.65), channel_id=1, source_target_pairs={{0,16},{2,18},{4,20},{6,22},{8,24},{10,26},{12,28},{14,30},{16,0},... | collective-permute-start | bytes 147464 | tf_op jit(solution)/shard_map/ppermute | solution.py:437
  37.9 6.1 %collective-permute-start.14 = (bf16[192,256]{1,0:T(8,128)(2,1)S(1)}, bf16[192,256]{1,0:T(8,128)(2,1)S(1)}, u32[]{:S(2)}, u32[]{:S(2)}) collective-permute-start(bf16[192,256]{1,0:T(8,128)(2,1)S(1)} %collective-permute-done.10.across_most), channel_id=1, source_target_pairs={{0,8},{2,10},{4,12},{6,14},{8,0},{10,2},{12,4},{14,6},{16,24},{18,... | collective-permute-start | bytes 294920 | tf_op jit(solution)/shard_map/ppermute | solution.py:437
  41.9 4.2 %collective-permute-start.15 = (bf16[192,128]{1,0:T(8,128)(2,1)S(1)}, bf16[192,128]{1,0:T(8,128)(2,1)S(1)}, u32[]{:S(2)}, u32[]{:S(2)}) collective-permute-start(bf16[192,128]{1,0:T(8,128)(2,1)S(1)} %collective-permute-done.11.across_last), channel_id=1, source_target_pairs={{0,8},{2,10},{4,12},{6,14},{8,0},{10,2},{12,4},{14,6},{16,24},{18,... | collective-permute-start | bytes 147464 | tf_op jit(solution)/shard_map/ppermute | solution.py:437
  42.2 14.4 %copy-start.2 = (f32[1536]{0:T(1024)S(1)}, f32[1536]{0:T(1024)}, u32[]{:S(2)}) copy-start(f32[1536]{0:T(1024)} %param.14) | copy-start | bytes 18436
  42.2 14.4 %copy-start.3 = (f32[1536]{0:T(1024)S(1)}, f32[1536]{0:T(1024)}, u32[]{:S(2)}) copy-start(f32[1536]{0:T(1024)} %param.15) | copy-start | bytes 18436
  46.4 6.2 %collective-permute-start.16 = (bf16[48,768]{1,0:T(8,128)(2,1)S(1)}, bf16[48,768]{1,0:T(8,128)(2,1)S(1)}, u32[]{:S(2)}, u32[]{:S(2)}) collective-permute-start(bf16[48,768]{1,0:T(8,128)(2,1)S(1)} %get-tuple-element.72), channel_id=1, source_target_pairs={{0,24},{2,26},{4,28},{6,30},{8,16},{10,18},{12,20},{14,22},{16,8},... | collective-permute-start | bytes 221192 | tf_op jit(solution)/shard_map/ppermute | solution.py:437
  49.1 5.8 %collective-permute-start.17 = (bf16[48,768]{1,0:T(8,128)(2,1)S(1)}, bf16[48,768]{1,0:T(8,128)(2,1)S(1)}, u32[]{:S(2)}, u32[]{:S(2)}) collective-permute-start(bf16[48,768]{1,0:T(8,128)(2,1)S(1)} %get-tuple-element.73), channel_id=1, source_target_pairs={{0,16},{2,18},{4,20},{6,22},{8,24},{10,26},{12,28},{14,30},{16,0},... | collective-permute-start | bytes 221192 | tf_op jit(solution)/shard_map/ppermute | solution.py:437
  49.2 5.8 %collective-permute-start.18 = (bf16[48,768]{1,0:T(8,128)(2,1)S(1)}, bf16[48,768]{1,0:T(8,128)(2,1)S(1)}, u32[]{:S(2)}, u32[]{:S(2)}) collective-permute-start(bf16[48,768]{1,0:T(8,128)(2,1)S(1)} %get-tuple-element.74), channel_id=1, source_target_pairs={{0,8},{2,10},{4,12},{6,14},{8,0},{10,2},{12,4},{14,6},{16,24},{18,... | collective-permute-start | bytes 221192 | tf_op jit(solution)/shard_map/ppermute | solution.py:437
  55.0 5.2 %collective-permute-start.19 = (bf16[2,48,768]{2,1,0:T(8,128)(2,1)S(1)}, bf16[2,48,768]{2,1,0:T(8,128)(2,1)S(1)}, u32[]{:S(2)}, u32[]{:S(2)}) collective-permute-start(bf16[2,48,768]{2,1,0:T(8,128)(2,1)S(1)} %get-tuple-element.76), channel_id=1, source_target_pairs={{0,1},{1,0},{2,3},{3,2},{4,5},{5,4},{6,7},{7,6},{8,9},{9,8},{10,11... | collective-permute-start | bytes 442376 | tf_op jit(solution)/shard_map/ppermute | solution.py:473

commit v12 on v11

--- a/solution.py
+++ b/solution.py
@@ -193,8 +193,14 @@
 def absorb(queries, segments, states):
     scores = [
         [
-            sum(lax.dot_general(query, key, NT, preferred_element_type=jnp.float32) for key in keys) * HD**-0.5
-            for keys, _ in parts
+            lax.dot_general(
+                query if key.shape[1] == HD else jnp.concatenate([query, query], axis=1),
+                key,
+                NT,
+                preferred_element_type=jnp.float32,
+            )
+            * HD**-0.5
+            for key, _ in parts
         ]
         for query, parts in zip(queries, segments)
     ]
@@ -207,11 +213,7 @@
     ]
     totals = [sum(jnp.sum(w.astype(jnp.float32), axis=1, keepdims=True) for w in row) for row in weights]
     mixes = [
-        sum(
-            jnp.dot(w, value, preferred_element_type=jnp.float32)
-            for w, (_, values) in zip(row, parts)
-            for value in values
-        )
+        sum(jnp.dot(w, value, preferred_element_type=jnp.float32) for w, (_, value) in zip(row, parts))
         for row, parts in zip(weights, segments)
     ]
     if states is not None:
@@ -227,8 +229,9 @@
 
 def image_segment(stale, twist, residual):
     def of(cols):
-        both = [(stale[twist, kind, :, cols], residual(kind, cols)) for kind in range(2)]
-        return both[0], both[1]
+        key = jnp.concatenate([stale[twist, 0, :, cols], residual(0, cols)], axis=1)
+        value = stale[twist, 1, :, cols].astype(jnp.float32) + residual(1, cols).astype(jnp.float32)
+        return key, value.astype(jnp.bfloat16)
 
     return of
 
@@ -244,7 +247,7 @@
 def near_kernel(query, every, text, stale, peak, total, mixed):
     heads = columns_of(query.shape[1])
     image = image_segment(stale, 0, whole_part(every))
-    segments = [[((text[0, :, cols],), (text[1, :, cols],)), image(cols)] for cols in heads]
+    segments = [[(text[0, :, cols], text[1, :, cols]), image(cols)] for cols in heads]
     states = absorb([query[:, cols] for cols in heads], segments, None)
     for head, state in enumerate(states):
         peak[head], total[head], mixed[head] = state
@@ -330,11 +333,12 @@
     return lax.dot_general(part[...], weight[:, columns], NT, preferred_element_type=jnp.float32)
 
 
-def begin_kernel(full, beside, across_most, across_last, weight, out):
+def begin_kernel(full, across_most, beside_most, across_last, beside_last, weight, out):
     width = full.shape[1]
-    total = term_of(full, weight, 0, 0, width) + term_of(beside, weight, 1, 0, width)
-    total += term_of(across_most, weight, 2, 0, width)
-    out[...] = total + term_of(across_last, weight, 2, width - HD, width)
+    total = term_of(full, weight, 0, 0, width) + term_of(across_most, weight, 2, 0, width)
+    total += term_of(beside_most, weight, 1, 0, width)
+    total += term_of(across_last, weight, 2, width - HD, width)
+    out[...] = total + term_of(beside_last, weight, 1, width - HD, width)
 
 
 def begin(parts, weight):
@@ -462,11 +466,11 @@
     full, most, last = attend_call(last_kernel, operands, result_shapes(query), share)
 
     across_most, across_last = swap(most, 2 * SPREAD), swap(last, 2 * SPREAD)
-    beside = swap(full, SPREAD)
+    beside_most, beside_last = swap(most, SPREAD), swap(last, SPREAD)
     final_most = swap(across_most, SPREAD)
-    final_last = swap(after(across_last, beside, weight_near, weight_corner), SPREAD)
+    final_last = swap(across_last, SPREAD)
     weight = order([weight, weight_near, weight_far, weight_corner])
-    partial = begin([full, beside, across_most, across_last], weight)
+    partial = begin([full, across_most, beside_most, across_last, beside_last], weight)
     terms = close(groups, partial, [final_most, final_last], weight)
 
     kept, sent = divide([terms[0], *along(terms)])

time: 61.2 us -> 61.7 us (level)
  waiting for transfers between devices: 26.1 us -> 28.3 us
  starting transfers between devices: 24.6 us -> 23.2 us
    ppermute x19 -> x20, waiting for transfers between devices: 22.5 us -> 24.7 us  [swap(): return lax.ppermute(value, 'patch', [(p, p ^ twist) for p in range(size)])]
    ppermute x19 -> x20, starting transfers between devices: 23 us -> 21.6 us  [swap(): return lax.ppermute(value, 'patch', [(p, p ^ twist) for p in range(size)])]
  transfers between devices with their start and end apart: 20 -> 21, of which waited for: 10 -> 9; matrix products, arithmetic and copies ran while one was open for 0% -> 0% of each run, Pallas kernels for 15% -> 14%
where the time goes in v12:
time: 61.7 us; the launch traced here: 61.4 us
  waiting for transfers between devices  28.3 us (46%)
  starting transfers between devices  23.2 us (38%)
  Pallas kernels  9.77 us (16%)
    ppermute x20, waiting for transfers between devices, swap(): return lax.ppermute(value, 'patch', [(p, p ^ twist) for p in range(size)])  24.7 us
    ppermute x20, starting transfers between devices, swap(): return lax.ppermute(value, 'patch', [(p, p ^ twist) for p in range(size)])  21.6 us
    pallas_call x3, Pallas kernels, attend_call(): pl.pallas_call(kernel, out_shape=shapes, in_specs=[VMEM] * len(operands),...  3.64 us
    ppermute x1, waiting for transfers between devices, grouped_body(): received = lax.ppermute(sent, 'head', [(0, 1), (1, 0)])  3.59 us
    pallas_call x1, Pallas kernels, pack(): pl.pallas_call(pack_kernel, out_shape=[jax.ShapeDtypeStruct(shape, bf16)...  2.32 us
    pallas_call x1, Pallas kernels, pick(): pl.pallas_call(pick_kernel, out_shape=[jax.ShapeDtypeStruct((kinds, texts...  1.65 us
    ppermute x1, starting transfers between devices, grouped_body(): received = lax.ppermute(sent, 'head', [(0, 1), (1, 0)])  1.59 us
  transfers between devices with their start and end apart: 21, of which 9 were waited for; matrix products, arithmetic and copies ran while one was open for 0% of the time, Pallas kernels for 14%

profile of v12, /device:TPU:0, one launch (start us, length us, event | category | flops | bytes accessed | tf_op | source)
XLA Modules:
  0.0 61.4 jit_solution(1387700212686743107)
XLA Ops:
  0.0 2.9 %collective-permute-start.3 = (bf16[192,1536]{1,0:T(8,128)(2,1)}, bf16[192,1536]{1,0:T(8,128)(2,1)S(1)}, u32[]{:S(2)}, u32[]{:S(2)}) collective-permute-start(bf16[192,1536]{1,0:T(8,128)(2,1)} %bitcast.2), channel_id=1, source_target_pairs={{0,4},{2,6},{4,0},{6,2},{8,12},{10,14},{12,8},{14,10},{16,20},{18,... | collective-permute-start | bytes 1769480 | tf_op jit(solution)/shard_map/ppermute | solution.py:441
  2.9 2.3 %shard_map.82 = (bf16[3,48,384]{2,1,0:T(8,128)(2,1)}, bf16[3,48,384]{2,1,0:T(8,128)(2,1)}, bf16[3,48,384]{2,1,0:T(8,128)(2,1)}, bf16[3,48,384]{2,1,0:T(8,128)(2,1)}, bf16[2,48,384]{2,1,0:T(8,128)(2,1)}) custom-call(bf16[48,1536]{1,0:T(8,128)(2,1)} %queries_hbm.1, s32[2,48,1536]{2,1,0:T(8,128)} %codes_hbm.1, s32[12,2,48]{2,1,0:T(2,128)} %bitcast.5), custom_call_target="tpu_custom_call" | custom-call | flops 294912 | bytes 884736 | tf_op jit(solution)/shard_map/pallas_call | solution.py:109
  5.3 3.7 %collective-permute-start = (bf16[3,48,384]{2,1,0:T(8,128)(2,1)}, bf16[3,48,384]{2,1,0:T(8,128)(2,1)S(1)}, u32[]{:S(2)}, u32[]{:S(2)}) collective-permute-start(bf16[3,48,384]{2,1,0:T(8,128)(2,1)} %get-tuple-element.41), channel_id=1, source_target_pairs={{0,24},{2,26},{4,28},{6,30},{8,16},{10,18},{12,20},{14,22},{16,8},... | collective-permute-start | bytes 331784 | tf_op jit(solution)/shard_map/ppermute | solution.py:441
  8.9 0.8 %collective-permute-start.2 = (bf16[3,48,384]{2,1,0:T(8,128)(2,1)}, bf16[3,48,384]{2,1,0:T(8,128)(2,1)S(1)}, u32[]{:S(2)}, u32[]{:S(2)}) collective-permute-start(bf16[3,48,384]{2,1,0:T(8,128)(2,1)} %get-tuple-element.43), channel_id=1, source_target_pairs={{0,8},{2,10},{4,12},{6,14},{8,0},{10,2},{12,4},{14,6},{16,24},{18,... | collective-permute-start | bytes 331784 | tf_op jit(solution)/shard_map/ppermute | solution.py:441
  9.7 0.4 collective-permute-start.4
  10.1 1.7 %shard_map.84 = (bf16[2,512,384]{2,1,0:T(8,128)(2,1)S(1)}, bf16[4,2,192,384]{3,2,1,0:T(8,128)(2,1)S(1)}) custom-call(bf16[2,512,1536]{2,1,0:T(8,128)(2,1)} %text_hbm.1, bf16[2,768,1536]{2,1,0:T(8,128)(2,1)} %stale_hbm.1), custom_call_target="tpu_custom_call" | custom-call | bytes 8388608 | tf_op jit(solution)/shard_map/pallas_call | solution.py:154
  11.8 1.5 %collective-permute-done.refs_1_ = bf16[3,48,384]{2,1,0:T(8,128)(2,1)S(1)} collective-permute-done((bf16[3,48,384]{2,1,0:T(8,128)(2,1)}, bf16[3,48,384]{2,1,0:T(8,128)(2,1)S(1)}, u32[]{:S(2)}, u32[]{:S(2)}) %collective-permute-start) | collective-permute-done | bytes 110624 | tf_op jit(solution)/shard_map/ppermute | solution.py:441
  13.3 4.9 %collective-permute-done.1.refs_2_ = bf16[3,48,384]{2,1,0:T(8,128)(2,1)S(1)} collective-permute-done((bf16[3,48,384]{2,1,0:T(8,128)(2,1)}, bf16[3,48,384]{2,1,0:T(8,128)(2,1)S(1)}, u32[]{:S(2)}, u32[]{:S(2)}) %collective-permute-start.1) | collective-permute-done | bytes 110624 | tf_op jit(solution)/shard_map/ppermute | solution.py:441
  18.4 1.4 %collective-permute-start.6 = (bf16[3,2,48,384]{3,2,1,0:T(8,128)(2,1)S(1)}, bf16[3,2,48,384]{3,2,1,0:T(8,128)(2,1)S(1)}, u32[]{:S(2)}, u32[]{:S(2)}) collective-permute-start(bf16[3,2,48,384]{3,2,1,0:T(8,128)(2,1)S(1)} %get-tuple-element.52), channel_id=1, source_target_pairs={{0,4},{2,6},{4,0},{6,2},{8,12},{10,14},{12,8},{14,10},{16,20},{18,... | collective-permute-start | bytes 663560 | tf_op jit(solution)/shard_map/ppermute | solution.py:441
  19.8 0.9 %shard_map.85 = (f32[3,192,1]{2,1,0:T(8,128)S(1)}, f32[3,192,1]{2,1,0:T(8,128)S(1)}, f32[3,192,128]{2,1,0:T(8,128)S(1)}) custom-call(bf16[192,384]{1,0:T(8,128)(2,1)S(1)} %get-tuple-element.50.query, bf16[4,2,48,384]{3,2,1,0:T(8,128)(2,1)S(1)} %get-tuple-element.51.every, bf16[2,512,384]{2,1,0:T(8,128)(2,1)S(1)} %get-tuple-element.48.text, ...), custom_call_target="tpu_custom_call" | custom-call | flops 415236096 | bytes 2162688 | tf_op jit(solution)/shard_map/pallas_call | solution.py:285
  20.7 5.5 %collective-permute-done.6.some_far = bf16[3,2,48,384]{3,2,1,0:T(8,128)(2,1)S(1)} collective-permute-done((bf16[3,2,48,384]{3,2,1,0:T(8,128)(2,1)S(1)}, bf16[3,2,48,384]{3,2,1,0:T(8,128)(2,1)S(1)}, u32[]{:S(2)}, u32[]{:S(2)}) %collective-permute-start.6) | collective-permute-done | bytes 221216 | tf_op jit(solution)/shard_map/ppermute | solution.py:441
  26.2 0.5 collective-permute-start.7
  26.7 1.6 %shard_map.86 = (f32[3,192,1]{2,1,0:T(8,128)S(1)}, f32[3,192,1]{2,1,0:T(8,128)S(1)}, f32[3,192,128]{2,1,0:T(8,128)S(1)}) custom-call(bf16[192,384]{1,0:T(8,128)(2,1)S(1)} %get-tuple-element.50.query, bf16[4,2,48,384]{3,2,1,0:T(8,128)(2,1)S(1)} %collective-permute-done.5.near, bf16[2,48,384]{2,1,0:T(8,128)(2,1)S(1)} %collective-permute-done.4.own_far, ...), custom_call_target="tpu_custom_call" | custom-call | flops 226492416 | bytes 1179648 | tf_op jit(solution)/shard_map/pallas_call | solution.py:285
  28.4 0.5 collective-permute-start.14
  28.9 1.1 %shard_map.87 = (bf16[192,384]{1,0:T(8,128)(2,1)S(1)}, bf16[192,256]{1,0:T(8,128)(2,1)S(1)}, bf16[192,128]{1,0:T(8,128)(2,1)S(1)}) custom-call(bf16[192,384]{1,0:T(8,128)(2,1)S(1)} %get-tuple-element.50.query, bf16[2,48,384]{2,1,0:T(8,128)(2,1)S(1)} %collective-permute-done.7.own_corner, bf16[3,2,48,384]{3,2,1,0:T(8,128)(2,1)S(1)} %collective-permute-done.8.some_corner, ...), custom_call_target="tpu_custom_call" | custom-call | flops 113246208 | bytes 589824 | tf_op jit(solution)/shard_map/pallas_call | solution.py:285
  30.0 2.6 %collective-permute-start.9 = (bf16[192,256]{1,0:T(8,128)(2,1)S(1)}, bf16[192,256]{1,0:T(8,128)(2,1)S(1)}, u32[]{:S(2)}, u32[]{:S(2)}) collective-permute-start(bf16[192,256]{1,0:T(8,128)(2,1)S(1)} %get-tuple-element.63), channel_id=1, source_target_pairs={{0,16},{2,18},{4,20},{6,22},{8,24},{10,26},{12,28},{14,30},{16,0},... | collective-permute-start | bytes 294920 | tf_op jit(solution)/shard_map/ppermute | solution.py:441
  32.6 0.4 collective-permute-start.11
  33.0 1.5 %collective-permute-start.10 = (bf16[192,256]{1,0:T(8,128)(2,1)S(1)}, bf16[192,256]{1,0:T(8,128)(2,1)S(1)}, u32[]{:S(2)}, u32[]{:S(2)}) collective-permute-start(bf16[192,256]{1,0:T(8,128)(2,1)S(1)} %get-tuple-element.63), channel_id=1, source_target_pairs={{0,8},{2,10},{4,12},{6,14},{8,0},{10,2},{12,4},{14,6},{16,24},{18,... | collective-permute-start | bytes 294920 | tf_op jit(solution)/shard_map/ppermute | solution.py:441
  34.6 4.9 %collective-permute-done.9.across_most = bf16[192,256]{1,0:T(8,128)(2,1)S(1)} collective-permute-done((bf16[192,256]{1,0:T(8,128)(2,1)S(1)}, bf16[192,256]{1,0:T(8,128)(2,1)S(1)}, u32[]{:S(2)}, u32[]{:S(2)}) %collective-permute-start.9) | collective-permute-done | bytes 98336 | tf_op jit(solution)/shard_map/ppermute | solution.py:441
  39.7 0.3 collective-permute-done.11.across_last
  40.0 1.5 %collective-permute-start.12 = (bf16[192,128]{1,0:T(8,128)(2,1)S(1)}, bf16[192,128]{1,0:T(8,128)(2,1)S(1)}, u32[]{:S(2)}, u32[]{:S(2)}) collective-permute-start(bf16[192,128]{1,0:T(8,128)(2,1)S(1)} %get-tuple-element.64), channel_id=1, source_target_pairs={{0,8},{2,10},{4,12},{6,14},{8,0},{10,2},{12,4},{14,6},{16,24},{18,... | collective-permute-start | bytes 147464 | tf_op jit(solution)/shard_map/ppermute | solution.py:441
  41.5 0.5 collective-permute-start.16
  42.2 2.9 %collective-permute-done.12.beside_last = bf16[192,128]{1,0:T(8,128)(2,1)S(1)} collective-permute-done((bf16[192,128]{1,0:T(8,128)(2,1)S(1)}, bf16[192,128]{1,0:T(8,128)(2,1)S(1)}, u32[]{:S(2)}, u32[]{:S(2)}) %collective-permute-start.12) | collective-permute-done | bytes 49184 | tf_op jit(solution)/shard_map/ppermute | solution.py:441
  45.1 0.7 %shard_map.89.partial = f32[192,768]{1,0:T(8,128)S(1)} custom-call(bf16[192,384]{1,0:T(8,128)(2,1)S(1)} %get-tuple-element.62.full, bf16[192,256]{1,0:T(8,128)(2,1)S(1)} %collective-permute-done.9.across_most, bf16[192,256]{1,0:T(8,128)(2,1)S(1)} %collective-permute-done.10.beside_most, bf16[192,128]{1,0:T(8,128)(2,1)S(1)} %collective-permute-done.11.across_last, ...), custom_call_target="tpu_custom_call" | custom-call | flops 452984832 | bytes 589824 | tf_op jit(solution)/shard_map/pallas_call | solution.py:347
  45.9 0.4 shard_map.90
  46.3 3.7 %collective-permute-start.17 = (bf16[48,768]{1,0:T(8,128)(2,1)S(1)}, bf16[48,768]{1,0:T(8,128)(2,1)S(1)}, u32[]{:S(2)}, u32[]{:S(2)}) collective-permute-start(bf16[48,768]{1,0:T(8,128)(2,1)S(1)} %get-tuple-element.70), channel_id=1, source_target_pairs={{0,24},{2,26},{4,28},{6,30},{8,16},{10,18},{12,20},{14,22},{16,8},... | collective-permute-start | bytes 221192 | tf_op jit(solution)/shard_map/ppermute | solution.py:441
  50.0 0.8 %collective-permute-start.19 = (bf16[48,768]{1,0:T(8,128)(2,1)S(1)}, bf16[48,768]{1,0:T(8,128)(2,1)S(1)}, u32[]{:S(2)}, u32[]{:S(2)}) collective-permute-start(bf16[48,768]{1,0:T(8,128)(2,1)S(1)} %get-tuple-element.72), channel_id=1, source_target_pairs={{0,8},{2,10},{4,12},{6,14},{8,0},{10,2},{12,4},{14,6},{16,24},{18,... | collective-permute-start | bytes 221192 | tf_op jit(solution)/shard_map/ppermute | solution.py:441
  50.8 2.1 %collective-permute-done.17.refs_1_ = bf16[48,768]{1,0:T(8,128)(2,1)S(1)} collective-permute-done((bf16[48,768]{1,0:T(8,128)(2,1)S(1)}, bf16[48,768]{1,0:T(8,128)(2,1)S(1)}, u32[]{:S(2)}, u32[]{:S(2)}) %collective-permute-start.17) | collective-permute-done | bytes 73760 | tf_op jit(solution)/shard_map/ppermute | solution.py:441
  52.8 2.6 %collective-permute-done.18.refs_2_ = bf16[48,768]{1,0:T(8,128)(2,1)S(1)} collective-permute-done((bf16[48,768]{1,0:T(8,128)(2,1)S(1)}, bf16[48,768]{1,0:T(8,128)(2,1)S(1)}, u32[]{:S(2)}, u32[]{:S(2)}) %collective-permute-start.18) | collective-permute-done | bytes 73760 | tf_op jit(solution)/shard_map/ppermute | solution.py:441
  55.5 1.6 %collective-permute-start.20 = (bf16[2,48,768]{2,1,0:T(8,128)(2,1)S(1)}, bf16[2,48,768]{2,1,0:T(8,128)(2,1)S(1)}, u32[]{:S(2)}, u32[]{:S(2)}) collective-permute-start(bf16[2,48,768]{2,1,0:T(8,128)(2,1)S(1)} %get-tuple-element.74), channel_id=1, source_target_pairs={{0,1},{1,0},{2,3},{3,2},{4,5},{5,4},{6,7},{7,6},{8,9},{9,8},{10,11... | collective-permute-start | bytes 442376 | tf_op jit(solution)/shard_map/ppermute | solution.py:477
  57.1 3.6 %collective-permute-done.20.arrived = bf16[2,48,768]{2,1,0:T(8,128)(2,1)S(1)} collective-permute-done((bf16[2,48,768]{2,1,0:T(8,128)(2,1)S(1)}, bf16[2,48,768]{2,1,0:T(8,128)(2,1)S(1)}, u32[]{:S(2)}, u32[]{:S(2)}) %collective-permute-start.20) | collective-permute-done | bytes 147488 | tf_op jit(solution)/shard_map/ppermute | solution.py:477
  60.7 0.7 %shard_map.92 = bf16[48,1536]{1,0:T(8,128)(2,1)} custom-call(bf16[2,48,768]{2,1,0:T(8,128)(2,1)S(1)} %get-tuple-element.73.kept, bf16[2,48,768]{2,1,0:T(8,128)(2,1)S(1)} %collective-permute-done.20.arrived, f32[1,1536]{1,0:T(1,128)S(1)} %reshape.6.bias, f32[1,1536]{1,0:T(1,128)S(1)} %reshape.7.gate), custom_call_target="tpu_custom_call" | custom-call | flops 221184 | bytes 294912 | tf_op jit(solution)/shard_map/pallas_call | solution.py:422
  (31 shorter events, 0.7 us)
Async XLA Ops:
  0.0 18.3 %collective-permute-start.3 = (bf16[192,1536]{1,0:T(8,128)(2,1)}, bf16[192,1536]{1,0:T(8,128)(2,1)S(1)}, u32[]{:S(2)}, u32[]{:S(2)}) collective-permute-start(bf16[192,1536]{1,0:T(8,128)(2,1)} %bitcast.2), channel_id=1, source_target_pairs={{0,4},{2,6},{4,0},{6,2},{8,12},{10,14},{12,8},{14,10},{16,20},{18,... | collective-permute-start | bytes 1769480 | tf_op jit(solution)/shard_map/ppermute | solution.py:441
  5.3 8.1 %collective-permute-start = (bf16[3,48,384]{2,1,0:T(8,128)(2,1)}, bf16[3,48,384]{2,1,0:T(8,128)(2,1)S(1)}, u32[]{:S(2)}, u32[]{:S(2)}) collective-permute-start(bf16[3,48,384]{2,1,0:T(8,128)(2,1)} %get-tuple-element.41), channel_id=1, source_target_pairs={{0,24},{2,26},{4,28},{6,30},{8,16},{10,18},{12,20},{14,22},{16,8},... | collective-permute-start | bytes 331784 | tf_op jit(solution)/shard_map/ppermute | solution.py:441
  8.9 9.3 %collective-permute-start.1 = (bf16[3,48,384]{2,1,0:T(8,128)(2,1)}, bf16[3,48,384]{2,1,0:T(8,128)(2,1)S(1)}, u32[]{:S(2)}, u32[]{:S(2)}) collective-permute-start(bf16[3,48,384]{2,1,0:T(8,128)(2,1)} %get-tuple-element.42), channel_id=1, source_target_pairs={{0,16},{2,18},{4,20},{6,22},{8,24},{10,26},{12,28},{14,30},{16,0},... | collective-permute-start | bytes 331784 | tf_op jit(solution)/shard_map/ppermute | solution.py:441
  8.9 9.3 %collective-permute-start.2 = (bf16[3,48,384]{2,1,0:T(8,128)(2,1)}, bf16[3,48,384]{2,1,0:T(8,128)(2,1)S(1)}, u32[]{:S(2)}, u32[]{:S(2)}) collective-permute-start(bf16[3,48,384]{2,1,0:T(8,128)(2,1)} %get-tuple-element.43), channel_id=1, source_target_pairs={{0,8},{2,10},{4,12},{6,14},{8,0},{10,2},{12,4},{14,6},{16,24},{18,... | collective-permute-start | bytes 331784 | tf_op jit(solution)/shard_map/ppermute | solution.py:441
  9.7 8.5 %copy-start.1 = (bf16[3,48,384]{2,1,0:T(8,128)(2,1)S(1)}, bf16[3,48,384]{2,1,0:T(8,128)(2,1)}, u32[]{:S(2)}) copy-start(bf16[3,48,384]{2,1,0:T(8,128)(2,1)} %get-tuple-element.40.refs_0_) | copy-start | bytes 331780
  9.7 8.5 %collective-permute-start.4 = (bf16[2,48,384]{2,1,0:T(8,128)(2,1)}, bf16[2,48,384]{2,1,0:T(8,128)(2,1)S(1)}, u32[]{:S(2)}, u32[]{:S(2)}) collective-permute-start(bf16[2,48,384]{2,1,0:T(8,128)(2,1)} %get-tuple-element.47), channel_id=1, source_target_pairs={{0,4},{2,6},{4,0},{6,2},{8,12},{10,14},{12,8},{14,10},{16,20},{18,... | collective-permute-start | bytes 221192 | tf_op jit(solution)/shard_map/ppermute | solution.py:441
  11.8 16.6 %copy-start = (bf16[1536,192]{0,1:T(8,128)(2,1)S(1)}, bf16[1536,192]{0,1:T(8,128)(2,1)}, u32[]{:S(2)}) copy-start(bf16[1536,192]{0,1:T(8,128)(2,1)} %param.13) | copy-start | bytes 1769476
  18.3 7.9 %collective-permute-start.5 = (bf16[4,2,48,384]{3,2,1,0:T(8,128)(2,1)S(1)}, bf16[4,2,48,384]{3,2,1,0:T(8,128)(2,1)S(1)}, u32[]{:S(2)}, u32[]{:S(2)}) collective-permute-start(bf16[4,2,48,384]{3,2,1,0:T(8,128)(2,1)S(1)} %get-tuple-element.51.every), channel_id=1, source_target_pairs={{0,2},{2,0},{4,6},{6,4},{8,10},{10,8},{12,14},{14,12},{16,18},{18,... | collective-permute-start | bytes 884744 | tf_op jit(solution)/shard_map/ppermute | solution.py:441
  18.4 7.8 %collective-permute-start.6 = (bf16[3,2,48,384]{3,2,1,0:T(8,128)(2,1)S(1)}, bf16[3,2,48,384]{3,2,1,0:T(8,128)(2,1)S(1)}, u32[]{:S(2)}, u32[]{:S(2)}) collective-permute-start(bf16[3,2,48,384]{3,2,1,0:T(8,128)(2,1)S(1)} %get-tuple-element.52), channel_id=1, source_target_pairs={{0,4},{2,6},{4,0},{6,2},{8,12},{10,14},{12,8},{14,10},{16,20},{18,... | collective-permute-start | bytes 663560 | tf_op jit(solution)/shard_map/ppermute | solution.py:441
  26.2 2.1 %collective-permute-start.8 = (bf16[3,2,48,384]{3,2,1,0:T(8,128)(2,1)S(1)}, bf16[3,2,48,384]{3,2,1,0:T(8,128)(2,1)S(1)}, u32[]{:S(2)}, u32[]{:S(2)}) collective-permute-start(bf16[3,2,48,384]{3,2,1,0:T(8,128)(2,1)S(1)} %collective-permute-done.6.some_far), channel_id=1, source_target_pairs={{0,2},{2,0},{4,6},{6,4},{8,10},{10,8},{12,14},{14,12},{16,18},{18,... | collective-permute-start | bytes 663560 | tf_op jit(solution)/shard_map/ppermute | solution.py:441
  26.2 2.1 %collective-permute-start.7 = (bf16[2,48,384]{2,1,0:T(8,128)(2,1)S(1)}, bf16[2,48,384]{2,1,0:T(8,128)(2,1)S(1)}, u32[]{:S(2)}, u32[]{:S(2)}) collective-permute-start(bf16[2,48,384]{2,1,0:T(8,128)(2,1)S(1)} %collective-permute-done.4.own_far), channel_id=1, source_target_pairs={{0,2},{2,0},{4,6},{6,4},{8,10},{10,8},{12,14},{14,12},{16,18},{18,... | collective-permute-start | bytes 221192 | tf_op jit(solution)/shard_map/ppermute | solution.py:441
  28.3 13.2 %collective-permute-start.13 = (bf16[192,1536]{1,0:T(8,128)(2,1)S(1)}, bf16[192,1536]{1,0:T(8,128)(2,1)S(1)}, u32[]{:S(2)}, u32[]{:S(2)}) collective-permute-start(bf16[192,1536]{1,0:T(8,128)(2,1)S(1)} %bitcast.3), channel_id=1, source_target_pairs={{0,2},{2,0},{4,6},{6,4},{8,10},{10,8},{12,14},{14,12},{16,18},{18,... | collective-permute-start | bytes 1769480 | tf_op jit(solution)/shard_map/ppermute | solution.py:441
  28.4 13.6 %collective-permute-start.14 = (bf16[192,1536]{1,0:T(8,128)(2,1)S(1)}, bf16[192,1536]{1,0:T(8,128)(2,1)S(1)}, u32[]{:S(2)}, u32[]{:S(2)}) collective-permute-start(bf16[192,1536]{1,0:T(8,128)(2,1)S(1)} %collective-permute-done.3.refs_2_), channel_id=1, source_target_pairs={{0,2},{2,0},{4,6},{6,4},{8,10},{10,8},{12,14},{14,12},{16,18},{18,... | collective-permute-start | bytes 1769480 | tf_op jit(solution)/shard_map/ppermute | solution.py:441
  30.0 9.4 %collective-permute-start.9 = (bf16[192,256]{1,0:T(8,128)(2,1)S(1)}, bf16[192,256]{1,0:T(8,128)(2,1)S(1)}, u32[]{:S(2)}, u32[]{:S(2)}) collective-permute-start(bf16[192,256]{1,0:T(8,128)(2,1)S(1)} %get-tuple-element.63), channel_id=1, source_target_pairs={{0,16},{2,18},{4,20},{6,22},{8,24},{10,26},{12,28},{14,30},{16,0},... | collective-permute-start | bytes 294920 | tf_op jit(solution)/shard_map/ppermute | solution.py:441
  32.6 7.3 %collective-permute-start.11 = (bf16[192,128]{1,0:T(8,128)(2,1)S(1)}, bf16[192,128]{1,0:T(8,128)(2,1)S(1)}, u32[]{:S(2)}, u32[]{:S(2)}) collective-permute-start(bf16[192,128]{1,0:T(8,128)(2,1)S(1)} %get-tuple-element.64), channel_id=1, source_target_pairs={{0,16},{2,18},{4,20},{6,22},{8,24},{10,26},{12,28},{14,30},{16,0},... | collective-permute-start | bytes 147464 | tf_op jit(solution)/shard_map/ppermute | solution.py:441
  33.0 12.1 %collective-permute-start.10 = (bf16[192,256]{1,0:T(8,128)(2,1)S(1)}, bf16[192,256]{1,0:T(8,128)(2,1)S(1)}, u32[]{:S(2)}, u32[]{:S(2)}) collective-permute-start(bf16[192,256]{1,0:T(8,128)(2,1)S(1)} %get-tuple-element.63), channel_id=1, source_target_pairs={{0,8},{2,10},{4,12},{6,14},{8,0},{10,2},{12,4},{14,6},{16,24},{18,... | collective-permute-start | bytes 294920 | tf_op jit(solution)/shard_map/ppermute | solution.py:441
  39.5 6.4 %collective-permute-start.15 = (bf16[192,256]{1,0:T(8,128)(2,1)S(1)}, bf16[192,256]{1,0:T(8,128)(2,1)S(1)}, u32[]{:S(2)}, u32[]{:S(2)}) collective-permute-start(bf16[192,256]{1,0:T(8,128)(2,1)S(1)} %collective-permute-done.9.across_most), channel_id=1, source_target_pairs={{0,8},{2,10},{4,12},{6,14},{8,0},{10,2},{12,4},{14,6},{16,24},{18,... | collective-permute-start | bytes 294920 | tf_op jit(solution)/shard_map/ppermute | solution.py:441
  40.0 5.1 %collective-permute-start.12 = (bf16[192,128]{1,0:T(8,128)(2,1)S(1)}, bf16[192,128]{1,0:T(8,128)(2,1)S(1)}, u32[]{:S(2)}, u32[]{:S(2)}) collective-permute-start(bf16[192,128]{1,0:T(8,128)(2,1)S(1)} %get-tuple-element.64), channel_id=1, source_target_pairs={{0,8},{2,10},{4,12},{6,14},{8,0},{10,2},{12,4},{14,6},{16,24},{18,... | collective-permute-start | bytes 147464 | tf_op jit(solution)/shard_map/ppermute | solution.py:441
  41.5 4.4 %collective-permute-start.16 = (bf16[192,128]{1,0:T(8,128)(2,1)S(1)}, bf16[192,128]{1,0:T(8,128)(2,1)S(1)}, u32[]{:S(2)}, u32[]{:S(2)}) collective-permute-start(bf16[192,128]{1,0:T(8,128)(2,1)S(1)} %collective-permute-done.11.across_last), channel_id=1, source_target_pairs={{0,8},{2,10},{4,12},{6,14},{8,0},{10,2},{12,4},{14,6},{16,24},{18,... | collective-permute-start | bytes 147464 | tf_op jit(solution)/shard_map/ppermute | solution.py:441
  45.1 12.0 %copy-start.2 = (f32[1536]{0:T(1024)S(1)}, f32[1536]{0:T(1024)}, u32[]{:S(2)}) copy-start(f32[1536]{0:T(1024)} %param.14) | copy-start | bytes 18436
  45.1 12.0 %copy-start.3 = (f32[1536]{0:T(1024)S(1)}, f32[1536]{0:T(1024)}, u32[]{:S(2)}) copy-start(f32[1536]{0:T(1024)} %param.15) | copy-start | bytes 18436
  46.3 6.5 %collective-permute-start.17 = (bf16[48,768]{1,0:T(8,128)(2,1)S(1)}, bf16[48,768]{1,0:T(8,128)(2,1)S(1)}, u32[]{:S(2)}, u32[]{:S(2)}) collective-permute-start(bf16[48,768]{1,0:T(8,128)(2,1)S(1)} %get-tuple-element.70), channel_id=1, source_target_pairs={{0,24},{2,26},{4,28},{6,30},{8,16},{10,18},{12,20},{14,22},{16,8},... | collective-permute-start | bytes 221192 | tf_op jit(solution)/shard_map/ppermute | solution.py:441
  50.0 5.5 %collective-permute-start.18 = (bf16[48,768]{1,0:T(8,128)(2,1)S(1)}, bf16[48,768]{1,0:T(8,128)(2,1)S(1)}, u32[]{:S(2)}, u32[]{:S(2)}) collective-permute-start(bf16[48,768]{1,0:T(8,128)(2,1)S(1)} %get-tuple-element.71), channel_id=1, source_target_pairs={{0,16},{2,18},{4,20},{6,22},{8,24},{10,26},{12,28},{14,30},{16,0},... | collective-permute-start | bytes 221192 | tf_op jit(solution)/shard_map/ppermute | solution.py:441
  50.0 5.5 %collective-permute-start.19 = (bf16[48,768]{1,0:T(8,128)(2,1)S(1)}, bf16[48,768]{1,0:T(8,128)(2,1)S(1)}, u32[]{:S(2)}, u32[]{:S(2)}) collective-permute-start(bf16[48,768]{1,0:T(8,128)(2,1)S(1)} %get-tuple-element.72), channel_id=1, source_target_pairs={{0,8},{2,10},{4,12},{6,14},{8,0},{10,2},{12,4},{14,6},{16,24},{18,... | collective-permute-start | bytes 221192 | tf_op jit(solution)/shard_map/ppermute | solution.py:441
  55.5 5.2 %collective-permute-start.20 = (bf16[2,48,768]{2,1,0:T(8,128)(2,1)S(1)}, bf16[2,48,768]{2,1,0:T(8,128)(2,1)S(1)}, u32[]{:S(2)}, u32[]{:S(2)}) collective-permute-start(bf16[2,48,768]{2,1,0:T(8,128)(2,1)S(1)} %get-tuple-element.74), channel_id=1, source_target_pairs={{0,1},{1,0},{2,3},{3,2},{4,5},{5,4},{6,7},{7,6},{8,9},{9,8},{10,11... | collective-permute-start | bytes 442376 | tf_op jit(solution)/shard_map/ppermute | solution.py:477

commit v13 on v12

--- a/solution.py
+++ b/solution.py
@@ -67,6 +67,11 @@
     return me // SPREAD, lax.rem(me, SPREAD)
 
 
+def pieces_of(rows):
+    first = rows // 48 * 32
+    return [(0, first), (first, rows - first)]
+
+
 def pack_kernel(queries_hbm, codes_hbm, exponents_hbm, *rest):
     outs, (codes, queries, exponents, held, sems) = rest[:-5], rest[-5:]
     groups, kinds, rows, width = held.shape
@@ -174,7 +179,9 @@
         if position:
             some[position - 1] = part[0:kinds]
         origin = jnp.bitwise_xor(group, (groups - position) % groups)
-        query[pl.ds(aligned(origin, rows), rows), :] = part[kinds]
+        for skip, height in pieces_of(rows):
+            start = groups * skip + origin * height
+            query[pl.ds(pl.multiple_of(start, 16), height), :] = part[kinds, skip : skip + height, :]
 
 
 def merge(parts):
@@ -266,18 +273,15 @@
         peak[head], total[head], mixed[head] = state
 
 
-def last_kernel(query, own_corner, some_corner, stale, peak, total, mixed, full, most, last):
+def last_kernel(query, own_corner, some_corner, stale, peak, total, mixed, most, last):
     heads = columns_of(query.shape[1])
     image = image_segment(stale, 3, split_part(own_corner, some_corner))
     states = [(peak[head], total[head], mixed[head]) for head in range(len(heads))]
     states = absorb([query[:, cols] for cols in heads], [[image(cols)] for cols in heads], states)
     for cols, (_, sums, mix) in zip(heads, states):
         value = (mix / sums).astype(jnp.bfloat16)
-        full[:, cols] = value
-        if cols is not heads[-1]:
-            most[:, cols] = value
-        else:
-            last[...] = value
+        most[:, cols] = value[0 : most.shape[0]]
+        last[:, cols] = value[most.shape[0] :]
 
 
 def attend_call(kernel, operands, shapes, keys):
@@ -300,9 +304,9 @@
     return [jax.ShapeDtypeStruct((heads, tokens, size), jnp.float32) for size in (1, 1, HD)]
 
 
-def result_shapes(query):
+def result_shapes(query, rows):
     tokens, width = query.shape
-    return [jax.ShapeDtypeStruct((tokens, size), jnp.bfloat16) for size in (width, width - HD, HD)]
+    return [jax.ShapeDtypeStruct((tokens // rows * height, width), jnp.bfloat16) for _, height in pieces_of(rows)]
 
 
 def order_kernel(*refs):
@@ -326,19 +330,15 @@
     )(*pieces)
 
 
-def term_of(part, weight, turn, skip, width):
+def term_of(part, weight, turn):
     group, _ = place()
-    start = jnp.bitwise_xor(group, turn) * width + skip
-    columns = pl.ds(pl.multiple_of(start, HD), part.shape[1])
+    width = part.shape[1]
+    columns = pl.ds(aligned(jnp.bitwise_xor(group, turn), width), width)
     return lax.dot_general(part[...], weight[:, columns], NT, preferred_element_type=jnp.float32)
 
 
-def begin_kernel(full, across_most, beside_most, across_last, beside_last, weight, out):
-    width = full.shape[1]
-    total = term_of(full, weight, 0, 0, width) + term_of(across_most, weight, 2, 0, width)
-    total += term_of(beside_most, weight, 1, 0, width)
-    total += term_of(across_last, weight, 2, width - HD, width)
-    out[...] = total + term_of(beside_last, weight, 1, width - HD, width)
+def begin_kernel(own, across, beside, weight, out):
+    out[...] = term_of(own, weight, 0) + term_of(across, weight, 2) + term_of(beside, weight, 1)
 
 
 def begin(parts, weight):
@@ -356,30 +356,28 @@
     )(*parts, weight)
 
 
-def close_kernel(partial, most, last, weight, *rest):
+def close_kernel(partial, final, weight, *rest):
     outs, total = rest[:-1], rest[-1]
     group, _ = place()
     rows = outs[0].shape[0]
-    width = most.shape[1] + last.shape[1]
-    added = partial[...] + term_of(most, weight, 3, 0, width) + term_of(last, weight, 3, width - HD, width)
-    total[...] = added.astype(jnp.bfloat16)
+    total[...] = (partial[...] + term_of(final, weight, 3)).astype(jnp.bfloat16)
     for turn, out in enumerate(outs):
         out[...] = total[pl.ds(aligned(jnp.bitwise_xor(group, turn), rows), rows), :]
 
 
-def close(groups, partial, parts, weight):
+def close(groups, partial, final, weight):
     tokens, columns = partial.shape
     return pl.pallas_call(
         close_kernel,
         out_shape=[jax.ShapeDtypeStruct((tokens // groups, columns), jnp.bfloat16)] * groups,
-        in_specs=[VMEM] * 4,
+        in_specs=[VMEM] * 3,
         out_specs=[VMEM] * groups,
         scratch_shapes=[pltpu.VMEM((tokens, columns), jnp.bfloat16)],
         compiler_params=pltpu.CompilerParams(vmem_limit_bytes=SMALL),
         cost_estimate=pl.CostEstimate(
             flops=tokens * weight.size, bytes_accessed=8 * tokens * columns, transcendentals=0
         ),
-    )(partial, *parts, weight)
+    )(partial, final, weight)
 
 
 def divide_kernel(*refs):
@@ -408,25 +406,30 @@
     )(*parts)
 
 
-def finish_kernel(kept, arrived, bias, gate, out):
-    blocks, _, columns = kept.shape
-    for block in range(blocks):
-        cols = slice(block * columns, (block + 1) * columns)
-        total = kept[block].astype(jnp.float32) + arrived[block].astype(jnp.float32)
-        out[:, cols] = (gate[:, cols] * (total + bias[:, cols])).astype(jnp.bfloat16)
-
-
-def finish(kept, arrived, bias, gate):
-    blocks, rows, columns = kept.shape
+def finish_kernel(*refs):
+    pairs, (bias, gate, out) = refs[:-3], refs[-3:]
+    start = 0
+    for kept, arrived in zip(pairs[0::2], pairs[1::2]):
+        blocks, rows, columns = kept.shape
+        for block in range(blocks):
+            cols = slice(block * columns, (block + 1) * columns)
+            total = kept[block].astype(jnp.float32) + arrived[block].astype(jnp.float32)
+            out[start : start + rows, cols] = (gate[:, cols] * (total + bias[:, cols])).astype(jnp.bfloat16)
+        start += rows
+
+
+def finish(pairs, bias, gate):
+    blocks, _, columns = pairs[0].shape
     width = blocks * columns
+    rows = sum(kept.shape[1] for kept in pairs[0::2])
     return pl.pallas_call(
         finish_kernel,
         out_shape=jax.ShapeDtypeStruct((rows, width), jnp.bfloat16),
-        in_specs=[VMEM] * 4,
+        in_specs=[VMEM] * (len(pairs) + 2),
         out_specs=VMEM,
         compiler_params=pltpu.CompilerParams(vmem_limit_bytes=SMALL),
         cost_estimate=pl.CostEstimate(flops=3 * rows * width, bytes_accessed=4 * rows * width, transcendentals=0),
-    )(kept, arrived, bias.reshape(1, width), gate.reshape(1, width))
+    )(*pairs, bias.reshape(1, width), gate.reshape(1, width))
 
 
 def after(value, *others):
@@ -463,19 +466,17 @@
     weight, weight_far = lax.optimization_barrier((weight, weight_far, own_corner, some_corner, *state))[:2]
     weight_near, weight_corner = swap(weight, 1), swap(weight_far, 1)
     operands = [query, own_corner, some_corner, stale, *state]
-    full, most, last = attend_call(last_kernel, operands, result_shapes(query), share)
-
-    across_most, across_last = swap(most, 2 * SPREAD), swap(last, 2 * SPREAD)
-    beside_most, beside_last = swap(most, SPREAD), swap(last, SPREAD)
-    final_most = swap(across_most, SPREAD)
-    final_last = swap(across_last, SPREAD)
+    parts = attend_call(last_kernel, operands, result_shapes(query, every.shape[2]), share)
+
     weight = order([weight, weight_near, weight_far, weight_corner])
-    partial = begin([full, across_most, beside_most, across_last, beside_last], weight)
-    terms = close(groups, partial, [final_most, final_last], weight)
-
-    kept, sent = divide([terms[0], *along(terms)])
-    received = lax.ppermute(sent, "head", [(0, 1), (1, 0)])
-    return finish(kept, received, out_bias, out_gate)
+    pairs = []
+    for part in parts:
+        across, beside = swap(part, 2 * SPREAD), swap(part, SPREAD)
+        final = swap(across, SPREAD)
+        terms = close(groups, begin([part, across, beside], weight), final, weight)
+        kept, sent = divide([terms[0], *along(terms)])
+        pairs += [kept, lax.ppermute(sent, "head", [(0, 1), (1, 0)])]
+    return finish(pairs, out_bias, out_gate)
 
 
 def solution(mesh):

time: 61.7 us -> 67.4 us (1.092)
  starting transfers between devices: 23.2 us -> 32.6 us
  waiting for transfers between devices: 28.3 us -> 23.7 us
  Pallas kernels: 9.77 us -> 10.6 us
    ppermute x20 -> x23, starting transfers between devices: 21.6 us -> 29.6 us  [swap(): return lax.ppermute(value, 'patch', [(p, p ^ twist) for p in range(size)])]
    ppermute x20 -> x23, waiting for transfers between devices: 24.7 us -> 21 us  [swap(): return lax.ppermute(value, 'patch', [(p, p ^ twist) for p in range(size)])]
    ppermute x1 -> x2, starting transfers between devices: 1.59 us -> 2.99 us  [grouped_body(): pairs += [kept, lax.ppermute(sent, 'head', [(0, 1), (1, 0)])]]
    ppermute x1 -> x2, waiting for transfers between devices: 3.59 us -> 2.71 us  [grouped_body(): pairs += [kept, lax.ppermute(sent, 'head', [(0, 1), (1, 0)])]]
  transfers between devices with their start and end apart: 21 -> 25, of which waited for: 9 -> 9; matrix products, arithmetic and copies ran while one was open for 0% -> 0% of each run, Pallas kernels for 14% -> 15%
where the time goes in v13:
time: 67.4 us; the launch traced here: 67.2 us
  starting transfers between devices  32.6 us (48%)
  waiting for transfers between devices  23.7 us (35%)
  Pallas kernels  10.6 us (16%)
    ppermute x23, starting transfers between devices, swap(): return lax.ppermute(value, 'patch', [(p, p ^ twist) for p in range(size)])  29.6 us
    ppermute x23, waiting for transfers between devices, swap(): return lax.ppermute(value, 'patch', [(p, p ^ twist) for p in range(size)])  21 us
    pallas_call x3, Pallas kernels, attend_call(): pl.pallas_call(kernel, out_shape=shapes, in_specs=[VMEM] * len(operands),...  3.65 us
    ppermute x2, starting transfers between devices, grouped_body(): pairs += [kept, lax.ppermute(sent, 'head', [(0, 1), (1, 0)])]  2.99 us
    ppermute x2, waiting for transfers between devices, grouped_body(): pairs += [kept, lax.ppermute(sent, 'head', [(0, 1), (1, 0)])]  2.71 us
    pallas_call x1, Pallas kernels, pack(): pl.pallas_call(pack_kernel, out_shape=[jax.ShapeDtypeStruct(shape, bf16)...  2.33 us
    pallas_call x1, Pallas kernels, pick(): pl.pallas_call(pick_kernel, out_shape=[jax.ShapeDtypeStruct((kinds, texts...  1.65 us
  transfers between devices with their start and end apart: 25, of which 9 were waited for; matrix products, arithmetic and copies ran while one was open for 0% of the time, Pallas kernels for 15%

profile of v13, /device:TPU:0, one launch (start us, length us, event | category | flops | bytes accessed | tf_op | source)
XLA Modules:
  0.0 67.2 jit_solution(9700447168798576328)
XLA Ops:
  0.0 2.9 %collective-permute-start.3 = (bf16[192,1536]{1,0:T(8,128)(2,1)}, bf16[192,1536]{1,0:T(8,128)(2,1)S(1)}, u32[]{:S(2)}, u32[]{:S(2)}) collective-permute-start(bf16[192,1536]{1,0:T(8,128)(2,1)} %bitcast.2), channel_id=1, source_target_pairs={{0,4},{2,6},{4,0},{6,2},{8,12},{10,14},{12,8},{14,10},{16,20},{18,... | collective-permute-start | bytes 1769480 | tf_op jit(solution)/shard_map/ppermute | solution.py:444
  2.9 2.3 %shard_map.82 = (bf16[3,48,384]{2,1,0:T(8,128)(2,1)}, bf16[3,48,384]{2,1,0:T(8,128)(2,1)}, bf16[3,48,384]{2,1,0:T(8,128)(2,1)}, bf16[3,48,384]{2,1,0:T(8,128)(2,1)}, bf16[2,48,384]{2,1,0:T(8,128)(2,1)}) custom-call(bf16[48,1536]{1,0:T(8,128)(2,1)} %queries_hbm.1, s32[2,48,1536]{2,1,0:T(8,128)} %codes_hbm.1, s32[12,2,48]{2,1,0:T(2,128)} %bitcast.5), custom_call_target="tpu_custom_call" | custom-call | flops 294912 | bytes 884736 | tf_op jit(solution)/shard_map/pallas_call | solution.py:114
  5.3 3.7 %collective-permute-start = (bf16[3,48,384]{2,1,0:T(8,128)(2,1)}, bf16[3,48,384]{2,1,0:T(8,128)(2,1)S(1)}, u32[]{:S(2)}, u32[]{:S(2)}) collective-permute-start(bf16[3,48,384]{2,1,0:T(8,128)(2,1)} %get-tuple-element.46), channel_id=1, source_target_pairs={{0,24},{2,26},{4,28},{6,30},{8,16},{10,18},{12,20},{14,22},{16,8},... | collective-permute-start | bytes 331784 | tf_op jit(solution)/shard_map/ppermute | solution.py:444
  8.9 0.8 %collective-permute-start.2 = (bf16[3,48,384]{2,1,0:T(8,128)(2,1)}, bf16[3,48,384]{2,1,0:T(8,128)(2,1)S(1)}, u32[]{:S(2)}, u32[]{:S(2)}) collective-permute-start(bf16[3,48,384]{2,1,0:T(8,128)(2,1)} %get-tuple-element.48), channel_id=1, source_target_pairs={{0,8},{2,10},{4,12},{6,14},{8,0},{10,2},{12,4},{14,6},{16,24},{18,... | collective-permute-start | bytes 331784 | tf_op jit(solution)/shard_map/ppermute | solution.py:444
  10.1 1.7 %shard_map.84 = (bf16[2,512,384]{2,1,0:T(8,128)(2,1)S(1)}, bf16[4,2,192,384]{3,2,1,0:T(8,128)(2,1)S(1)}) custom-call(bf16[2,512,1536]{2,1,0:T(8,128)(2,1)} %text_hbm.1, bf16[2,768,1536]{2,1,0:T(8,128)(2,1)} %stale_hbm.1), custom_call_target="tpu_custom_call" | custom-call | bytes 8388608 | tf_op jit(solution)/shard_map/pallas_call | solution.py:159
  11.8 1.5 %collective-permute-done.refs_1_ = bf16[3,48,384]{2,1,0:T(8,128)(2,1)S(1)} collective-permute-done((bf16[3,48,384]{2,1,0:T(8,128)(2,1)}, bf16[3,48,384]{2,1,0:T(8,128)(2,1)S(1)}, u32[]{:S(2)}, u32[]{:S(2)}) %collective-permute-start) | collective-permute-done | bytes 110624 | tf_op jit(solution)/shard_map/ppermute | solution.py:444
  13.3 4.9 %collective-permute-done.1.refs_2_ = bf16[3,48,384]{2,1,0:T(8,128)(2,1)S(1)} collective-permute-done((bf16[3,48,384]{2,1,0:T(8,128)(2,1)}, bf16[3,48,384]{2,1,0:T(8,128)(2,1)S(1)}, u32[]{:S(2)}, u32[]{:S(2)}) %collective-permute-start.1) | collective-permute-done | bytes 110624 | tf_op jit(solution)/shard_map/ppermute | solution.py:444
  18.4 1.4 %collective-permute-start.6 = (bf16[3,2,48,384]{3,2,1,0:T(8,128)(2,1)S(1)}, bf16[3,2,48,384]{3,2,1,0:T(8,128)(2,1)S(1)}, u32[]{:S(2)}, u32[]{:S(2)}) collective-permute-start(bf16[3,2,48,384]{3,2,1,0:T(8,128)(2,1)S(1)} %get-tuple-element.57), channel_id=1, source_target_pairs={{0,4},{2,6},{4,0},{6,2},{8,12},{10,14},{12,8},{14,10},{16,20},{18,... | collective-permute-start | bytes 663560 | tf_op jit(solution)/shard_map/ppermute | solution.py:444
  19.8 0.9 %shard_map.85 = (f32[3,192,1]{2,1,0:T(8,128)S(1)}, f32[3,192,1]{2,1,0:T(8,128)S(1)}, f32[3,192,128]{2,1,0:T(8,128)S(1)}) custom-call(bf16[192,384]{1,0:T(8,128)(2,1)S(1)} %get-tuple-element.55.query, bf16[4,2,48,384]{3,2,1,0:T(8,128)(2,1)S(1)} %get-tuple-element.56.every, bf16[2,512,384]{2,1,0:T(8,128)(2,1)S(1)} %get-tuple-element.53.text, ...), custom_call_target="tpu_custom_call" | custom-call | flops 415236096 | bytes 2162688 | tf_op jit(solution)/shard_map/pallas_call | solution.py:289
  20.7 5.5 %collective-permute-done.6.some_far = bf16[3,2,48,384]{3,2,1,0:T(8,128)(2,1)S(1)} collective-permute-done((bf16[3,2,48,384]{3,2,1,0:T(8,128)(2,1)S(1)}, bf16[3,2,48,384]{3,2,1,0:T(8,128)(2,1)S(1)}, u32[]{:S(2)}, u32[]{:S(2)}) %collective-permute-start.6) | collective-permute-done | bytes 221216 | tf_op jit(solution)/shard_map/ppermute | solution.py:444
  26.7 1.6 %shard_map.86 = (f32[3,192,1]{2,1,0:T(8,128)S(1)}, f32[3,192,1]{2,1,0:T(8,128)S(1)}, f32[3,192,128]{2,1,0:T(8,128)S(1)}) custom-call(bf16[192,384]{1,0:T(8,128)(2,1)S(1)} %get-tuple-element.55.query, bf16[4,2,48,384]{3,2,1,0:T(8,128)(2,1)S(1)} %collective-permute-done.5.near, bf16[2,48,384]{2,1,0:T(8,128)(2,1)S(1)} %collective-permute-done.4.own_far, ...), custom_call_target="tpu_custom_call" | custom-call | flops 226492416 | bytes 1179648 | tf_op jit(solution)/shard_map/pallas_call | solution.py:289
  28.9 1.1 %shard_map.87 = (bf16[128,384]{1,0:T(8,128)(2,1)S(1)}, bf16[64,384]{1,0:T(8,128)(2,1)S(1)}) custom-call(bf16[192,384]{1,0:T(8,128)(2,1)S(1)} %get-tuple-element.55.query, bf16[2,48,384]{2,1,0:T(8,128)(2,1)S(1)} %collective-permute-done.7.own_corner, bf16[3,2,48,384]{3,2,1,0:T(8,128)(2,1)S(1)} %collective-permute-done.8.some_corner, ...), custom_call_target="tpu_custom_call" | custom-call | flops 113246208 | bytes 589824 | tf_op jit(solution)/shard_map/pallas_call | solution.py:289
  30.1 2.6 %collective-permute-start.9 = (bf16[128,384]{1,0:T(8,128)(2,1)S(1)}, bf16[128,384]{1,0:T(8,128)(2,1)S(1)}, u32[]{:S(2)}, u32[]{:S(2)}) collective-permute-start(bf16[128,384]{1,0:T(8,128)(2,1)S(1)} %get-tuple-element.67.own), channel_id=1, source_target_pairs={{0,16},{2,18},{4,20},{6,22},{8,24},{10,26},{12,28},{14,30},{16,0},... | collective-permute-start | bytes 294920 | tf_op jit(solution)/shard_map/ppermute | solution.py:444
  32.6 1.6 %collective-permute-start.10 = (bf16[128,384]{1,0:T(8,128)(2,1)S(1)}, bf16[128,384]{1,0:T(8,128)(2,1)S(1)}, u32[]{:S(2)}, u32[]{:S(2)}) collective-permute-start(bf16[128,384]{1,0:T(8,128)(2,1)S(1)} %get-tuple-element.67.own), channel_id=1, source_target_pairs={{0,8},{2,10},{4,12},{6,14},{8,0},{10,2},{12,4},{14,6},{16,24},{18,... | collective-permute-start | bytes 294920 | tf_op jit(solution)/shard_map/ppermute | solution.py:444
  34.2 3.8 %collective-permute-done.9.across = bf16[128,384]{1,0:T(8,128)(2,1)S(1)} collective-permute-done((bf16[128,384]{1,0:T(8,128)(2,1)S(1)}, bf16[128,384]{1,0:T(8,128)(2,1)S(1)}, u32[]{:S(2)}, u32[]{:S(2)}) %collective-permute-start.9) | collective-permute-done | bytes 98336 | tf_op jit(solution)/shard_map/ppermute | solution.py:444
  38.0 0.5 collective-permute-start.13
  38.5 3.4 %collective-permute-start.18 = (bf16[64,384]{1,0:T(8,128)(2,1)S(1)}, bf16[64,384]{1,0:T(8,128)(2,1)S(1)}, u32[]{:S(2)}, u32[]{:S(2)}) collective-permute-start(bf16[64,384]{1,0:T(8,128)(2,1)S(1)} %get-tuple-element.78.own), channel_id=1, source_target_pairs={{0,16},{2,18},{4,20},{6,22},{8,24},{10,26},{12,28},{14,30},{16,0},... | collective-permute-start | bytes 147464 | tf_op jit(solution)/shard_map/ppermute | solution.py:444
  42.1 0.7 shard_map.89.partial
  43.5 4.0 %collective-permute-start.14 = (bf16[32,768]{1,0:T(8,128)(2,1)S(1)}, bf16[32,768]{1,0:T(8,128)(2,1)S(1)}, u32[]{:S(2)}, u32[]{:S(2)}) collective-permute-start(bf16[32,768]{1,0:T(8,128)(2,1)S(1)} %get-tuple-element.73), channel_id=1, source_target_pairs={{0,24},{2,26},{4,28},{6,30},{8,16},{10,18},{12,20},{14,22},{16,8},... | collective-permute-start | bytes 147464 | tf_op jit(solution)/shard_map/ppermute | solution.py:444
  47.6 0.6 collective-permute-start.16
  48.2 1.4 %collective-permute-start.19 = (bf16[64,384]{1,0:T(8,128)(2,1)S(1)}, bf16[64,384]{1,0:T(8,128)(2,1)S(1)}, u32[]{:S(2)}, u32[]{:S(2)}) collective-permute-start(bf16[64,384]{1,0:T(8,128)(2,1)S(1)} %get-tuple-element.78.own), channel_id=1, source_target_pairs={{0,8},{2,10},{4,12},{6,14},{8,0},{10,2},{12,4},{14,6},{16,24},{18,... | collective-permute-start | bytes 147464 | tf_op jit(solution)/shard_map/ppermute | solution.py:444
  49.6 0.6 collective-permute-start.20
  50.2 2.4 %collective-permute-done.15.refs_2_ = bf16[32,768]{1,0:T(8,128)(2,1)S(1)} collective-permute-done((bf16[32,768]{1,0:T(8,128)(2,1)S(1)}, bf16[32,768]{1,0:T(8,128)(2,1)S(1)}, u32[]{:S(2)}, u32[]{:S(2)}) %collective-permute-start.15) | collective-permute-done | bytes 49184 | tf_op jit(solution)/shard_map/ppermute | solution.py:444
  52.7 1.6 %collective-permute-start.17 = (bf16[2,32,768]{2,1,0:T(8,128)(2,1)S(1)}, bf16[2,32,768]{2,1,0:T(8,128)(2,1)S(1)}, u32[]{:S(2)}, u32[]{:S(2)}) collective-permute-start(bf16[2,32,768]{2,1,0:T(8,128)(2,1)S(1)} %get-tuple-element.77), channel_id=1, source_target_pairs={{0,1},{1,0},{2,3},{3,2},{4,5},{5,4},{6,7},{7,6},{8,9},{9,8},{10,11... | collective-permute-start | bytes 294920 | tf_op jit(solution)/shard_map/ppermute | solution.py:478
  54.3 0.7 shard_map.92.partial
  55.3 2.1 %collective-permute-start.21 = (bf16[16,768]{1,0:T(8,128)(2,1)S(1)}, bf16[16,768]{1,0:T(8,128)(2,1)S(1)}, u32[]{:S(2)}, u32[]{:S(2)}) collective-permute-start(bf16[16,768]{1,0:T(8,128)(2,1)S(1)} %get-tuple-element.80), channel_id=1, source_target_pairs={{0,24},{2,26},{4,28},{6,30},{8,16},{10,18},{12,20},{14,22},{16,8},... | collective-permute-start | bytes 73736 | tf_op jit(solution)/shard_map/ppermute | solution.py:444
  57.4 2.3 %collective-permute-start.23 = (bf16[16,768]{1,0:T(8,128)(2,1)S(1)}, bf16[16,768]{1,0:T(8,128)(2,1)S(1)}, u32[]{:S(2)}, u32[]{:S(2)}) collective-permute-start(bf16[16,768]{1,0:T(8,128)(2,1)S(1)} %get-tuple-element.82), channel_id=1, source_target_pairs={{0,8},{2,10},{4,12},{6,14},{8,0},{10,2},{12,4},{14,6},{16,24},{18,... | collective-permute-start | bytes 73736 | tf_op jit(solution)/shard_map/ppermute | solution.py:444
  59.8 1.2 %collective-permute-done.21.refs_1_ = bf16[16,768]{1,0:T(8,128)(2,1)S(1)} collective-permute-done((bf16[16,768]{1,0:T(8,128)(2,1)S(1)}, bf16[16,768]{1,0:T(8,128)(2,1)S(1)}, u32[]{:S(2)}, u32[]{:S(2)}) %collective-permute-start.21) | collective-permute-done | bytes 24608 | tf_op jit(solution)/shard_map/ppermute | solution.py:444
  61.0 1.3 %collective-permute-done.22.refs_2_ = bf16[16,768]{1,0:T(8,128)(2,1)S(1)} collective-permute-done((bf16[16,768]{1,0:T(8,128)(2,1)S(1)}, bf16[16,768]{1,0:T(8,128)(2,1)S(1)}, u32[]{:S(2)}, u32[]{:S(2)}) %collective-permute-start.22) | collective-permute-done | bytes 24608 | tf_op jit(solution)/shard_map/ppermute | solution.py:444
  62.3 1.4 %collective-permute-start.24 = (bf16[2,16,768]{2,1,0:T(8,128)(2,1)S(1)}, bf16[2,16,768]{2,1,0:T(8,128)(2,1)S(1)}, u32[]{:S(2)}, u32[]{:S(2)}) collective-permute-start(bf16[2,16,768]{2,1,0:T(8,128)(2,1)S(1)} %get-tuple-element.84), channel_id=1, source_target_pairs={{0,1},{1,0},{2,3},{3,2},{4,5},{5,4},{6,7},{7,6},{8,9},{9,8},{10,11... | collective-permute-start | bytes 147464 | tf_op jit(solution)/shard_map/ppermute | solution.py:478
  63.8 2.7 %collective-permute-done.24.refs_3_ = bf16[2,16,768]{2,1,0:T(8,128)(2,1)S(1)} collective-permute-done((bf16[2,16,768]{2,1,0:T(8,128)(2,1)S(1)}, bf16[2,16,768]{2,1,0:T(8,128)(2,1)S(1)}, u32[]{:S(2)}, u32[]{:S(2)}) %collective-permute-start.24) | collective-permute-done | bytes 49184 | tf_op jit(solution)/shard_map/ppermute | solution.py:478
  66.5 0.7 %shard_map.95 = bf16[48,1536]{1,0:T(8,128)(2,1)} custom-call(bf16[2,32,768]{2,1,0:T(8,128)(2,1)S(1)} %get-tuple-element.76.refs_0_, bf16[2,32,768]{2,1,0:T(8,128)(2,1)S(1)} %collective-permute-done.17.refs_1_, bf16[2,16,768]{2,1,0:T(8,128)(2,1)S(1)} %get-tuple-element.83.refs_2_, bf16[2,16,768]{2,1,0:T(8,128)(2,1)S(1)} %collective-permute-done.24.refs_3_, ...), custom_call_target="tpu_custom_call" | custom-call | flops 221184 | bytes 294912 | tf_op jit(solution)/shard_map/pallas_call | solution.py:425
  (42 shorter events, 3.0 us)
Async XLA Ops:
  0.0 18.3 %collective-permute-start.3 = (bf16[192,1536]{1,0:T(8,128)(2,1)}, bf16[192,1536]{1,0:T(8,128)(2,1)S(1)}, u32[]{:S(2)}, u32[]{:S(2)}) collective-permute-start(bf16[192,1536]{1,0:T(8,128)(2,1)} %bitcast.2), channel_id=1, source_target_pairs={{0,4},{2,6},{4,0},{6,2},{8,12},{10,14},{12,8},{14,10},{16,20},{18,... | collective-permute-start | bytes 1769480 | tf_op jit(solution)/shard_map/ppermute | solution.py:444
  5.3 8.1 %collective-permute-start = (bf16[3,48,384]{2,1,0:T(8,128)(2,1)}, bf16[3,48,384]{2,1,0:T(8,128)(2,1)S(1)}, u32[]{:S(2)}, u32[]{:S(2)}) collective-permute-start(bf16[3,48,384]{2,1,0:T(8,128)(2,1)} %get-tuple-element.46), channel_id=1, source_target_pairs={{0,24},{2,26},{4,28},{6,30},{8,16},{10,18},{12,20},{14,22},{16,8},... | collective-permute-start | bytes 331784 | tf_op jit(solution)/shard_map/ppermute | solution.py:444
  8.9 9.3 %collective-permute-start.1 = (bf16[3,48,384]{2,1,0:T(8,128)(2,1)}, bf16[3,48,384]{2,1,0:T(8,128)(2,1)S(1)}, u32[]{:S(2)}, u32[]{:S(2)}) collective-permute-start(bf16[3,48,384]{2,1,0:T(8,128)(2,1)} %get-tuple-element.47), channel_id=1, source_target_pairs={{0,16},{2,18},{4,20},{6,22},{8,24},{10,26},{12,28},{14,30},{16,0},... | collective-permute-start | bytes 331784 | tf_op jit(solution)/shard_map/ppermute | solution.py:444
  8.9 9.3 %collective-permute-start.2 = (bf16[3,48,384]{2,1,0:T(8,128)(2,1)}, bf16[3,48,384]{2,1,0:T(8,128)(2,1)S(1)}, u32[]{:S(2)}, u32[]{:S(2)}) collective-permute-start(bf16[3,48,384]{2,1,0:T(8,128)(2,1)} %get-tuple-element.48), channel_id=1, source_target_pairs={{0,8},{2,10},{4,12},{6,14},{8,0},{10,2},{12,4},{14,6},{16,24},{18,... | collective-permute-start | bytes 331784 | tf_op jit(solution)/shard_map/ppermute | solution.py:444
  9.7 8.5 %copy-start.1 = (bf16[3,48,384]{2,1,0:T(8,128)(2,1)S(1)}, bf16[3,48,384]{2,1,0:T(8,128)(2,1)}, u32[]{:S(2)}) copy-start(bf16[3,48,384]{2,1,0:T(8,128)(2,1)} %get-tuple-element.45.refs_0_) | copy-start | bytes 331780
  9.7 8.5 %collective-permute-start.4 = (bf16[2,48,384]{2,1,0:T(8,128)(2,1)}, bf16[2,48,384]{2,1,0:T(8,128)(2,1)S(1)}, u32[]{:S(2)}, u32[]{:S(2)}) collective-permute-start(bf16[2,48,384]{2,1,0:T(8,128)(2,1)} %get-tuple-element.52), channel_id=1, source_target_pairs={{0,4},{2,6},{4,0},{6,2},{8,12},{10,14},{12,8},{14,10},{16,20},{18,... | collective-permute-start | bytes 221192 | tf_op jit(solution)/shard_map/ppermute | solution.py:444
  11.8 16.6 %copy-start = (bf16[1536,192]{0,1:T(8,128)(2,1)S(1)}, bf16[1536,192]{0,1:T(8,128)(2,1)}, u32[]{:S(2)}) copy-start(bf16[1536,192]{0,1:T(8,128)(2,1)} %param.13) | copy-start | bytes 1769476
  18.3 7.9 %collective-permute-start.5 = (bf16[4,2,48,384]{3,2,1,0:T(8,128)(2,1)S(1)}, bf16[4,2,48,384]{3,2,1,0:T(8,128)(2,1)S(1)}, u32[]{:S(2)}, u32[]{:S(2)}) collective-permute-start(bf16[4,2,48,384]{3,2,1,0:T(8,128)(2,1)S(1)} %get-tuple-element.56.every), channel_id=1, source_target_pairs={{0,2},{2,0},{4,6},{6,4},{8,10},{10,8},{12,14},{14,12},{16,18},{18,... | collective-permute-start | bytes 884744 | tf_op jit(solution)/shard_map/ppermute | solution.py:444
  18.4 7.8 %collective-permute-start.6 = (bf16[3,2,48,384]{3,2,1,0:T(8,128)(2,1)S(1)}, bf16[3,2,48,384]{3,2,1,0:T(8,128)(2,1)S(1)}, u32[]{:S(2)}, u32[]{:S(2)}) collective-permute-start(bf16[3,2,48,384]{3,2,1,0:T(8,128)(2,1)S(1)} %get-tuple-element.57), channel_id=1, source_target_pairs={{0,4},{2,6},{4,0},{6,2},{8,12},{10,14},{12,8},{14,10},{16,20},{18,... | collective-permute-start | bytes 663560 | tf_op jit(solution)/shard_map/ppermute | solution.py:444
  26.2 2.1 %collective-permute-start.8 = (bf16[3,2,48,384]{3,2,1,0:T(8,128)(2,1)S(1)}, bf16[3,2,48,384]{3,2,1,0:T(8,128)(2,1)S(1)}, u32[]{:S(2)}, u32[]{:S(2)}) collective-permute-start(bf16[3,2,48,384]{3,2,1,0:T(8,128)(2,1)S(1)} %collective-permute-done.6.some_far), channel_id=1, source_target_pairs={{0,2},{2,0},{4,6},{6,4},{8,10},{10,8},{12,14},{14,12},{16,18},{18,... | collective-permute-start | bytes 663560 | tf_op jit(solution)/shard_map/ppermute | solution.py:444
  26.2 2.1 %collective-permute-start.7 = (bf16[2,48,384]{2,1,0:T(8,128)(2,1)S(1)}, bf16[2,48,384]{2,1,0:T(8,128)(2,1)S(1)}, u32[]{:S(2)}, u32[]{:S(2)}) collective-permute-start(bf16[2,48,384]{2,1,0:T(8,128)(2,1)S(1)} %collective-permute-done.4.own_far), channel_id=1, source_target_pairs={{0,2},{2,0},{4,6},{6,4},{8,10},{10,8},{12,14},{14,12},{16,18},{18,... | collective-permute-start | bytes 221192 | tf_op jit(solution)/shard_map/ppermute | solution.py:444
  28.4 13.5 %collective-permute-start.11 = (bf16[192,1536]{1,0:T(8,128)(2,1)S(1)}, bf16[192,1536]{1,0:T(8,128)(2,1)S(1)}, u32[]{:S(2)}, u32[]{:S(2)}) collective-permute-start(bf16[192,1536]{1,0:T(8,128)(2,1)S(1)} %bitcast.3), channel_id=1, source_target_pairs={{0,2},{2,0},{4,6},{6,4},{8,10},{10,8},{12,14},{14,12},{16,18},{18,... | collective-permute-start | bytes 1769480 | tf_op jit(solution)/shard_map/ppermute | solution.py:444
  28.4 13.5 %collective-permute-start.12 = (bf16[192,1536]{1,0:T(8,128)(2,1)S(1)}, bf16[192,1536]{1,0:T(8,128)(2,1)S(1)}, u32[]{:S(2)}, u32[]{:S(2)}) collective-permute-start(bf16[192,1536]{1,0:T(8,128)(2,1)S(1)} %collective-permute-done.3.refs_2_), channel_id=1, source_target_pairs={{0,2},{2,0},{4,6},{6,4},{8,10},{10,8},{12,14},{14,12},{16,18},{18,... | collective-permute-start | bytes 1769480 | tf_op jit(solution)/shard_map/ppermute | solution.py:444
  30.1 8.0 %collective-permute-start.9 = (bf16[128,384]{1,0:T(8,128)(2,1)S(1)}, bf16[128,384]{1,0:T(8,128)(2,1)S(1)}, u32[]{:S(2)}, u32[]{:S(2)}) collective-permute-start(bf16[128,384]{1,0:T(8,128)(2,1)S(1)} %get-tuple-element.67.own), channel_id=1, source_target_pairs={{0,16},{2,18},{4,20},{6,22},{8,24},{10,26},{12,28},{14,30},{16,0},... | collective-permute-start | bytes 294920 | tf_op jit(solution)/shard_map/ppermute | solution.py:444
  32.6 9.4 %collective-permute-start.10 = (bf16[128,384]{1,0:T(8,128)(2,1)S(1)}, bf16[128,384]{1,0:T(8,128)(2,1)S(1)}, u32[]{:S(2)}, u32[]{:S(2)}) collective-permute-start(bf16[128,384]{1,0:T(8,128)(2,1)S(1)} %get-tuple-element.67.own), channel_id=1, source_target_pairs={{0,8},{2,10},{4,12},{6,14},{8,0},{10,2},{12,4},{14,6},{16,24},{18,... | collective-permute-start | bytes 294920 | tf_op jit(solution)/shard_map/ppermute | solution.py:444
  38.0 5.1 %collective-permute-start.13 = (bf16[128,384]{1,0:T(8,128)(2,1)S(1)}, bf16[128,384]{1,0:T(8,128)(2,1)S(1)}, u32[]{:S(2)}, u32[]{:S(2)}) collective-permute-start(bf16[128,384]{1,0:T(8,128)(2,1)S(1)} %collective-permute-done.9.across), channel_id=1, source_target_pairs={{0,8},{2,10},{4,12},{6,14},{8,0},{10,2},{12,4},{14,6},{16,24},{18,... | collective-permute-start | bytes 294920 | tf_op jit(solution)/shard_map/ppermute | solution.py:444
  38.5 11.1 %collective-permute-start.18 = (bf16[64,384]{1,0:T(8,128)(2,1)S(1)}, bf16[64,384]{1,0:T(8,128)(2,1)S(1)}, u32[]{:S(2)}, u32[]{:S(2)}) collective-permute-start(bf16[64,384]{1,0:T(8,128)(2,1)S(1)} %get-tuple-element.78.own), channel_id=1, source_target_pairs={{0,16},{2,18},{4,20},{6,22},{8,24},{10,26},{12,28},{14,30},{16,0},... | collective-permute-start | bytes 147464 | tf_op jit(solution)/shard_map/ppermute | solution.py:444
  43.5 20.2 %copy-start.2 = (f32[1536]{0:T(1024)S(1)}, f32[1536]{0:T(1024)}, u32[]{:S(2)}) copy-start(f32[1536]{0:T(1024)} %param.14) | copy-start | bytes 18436
  43.5 20.2 %copy-start.3 = (f32[1536]{0:T(1024)S(1)}, f32[1536]{0:T(1024)}, u32[]{:S(2)}) copy-start(f32[1536]{0:T(1024)} %param.15) | copy-start | bytes 18436
  43.5 6.7 %collective-permute-start.14 = (bf16[32,768]{1,0:T(8,128)(2,1)S(1)}, bf16[32,768]{1,0:T(8,128)(2,1)S(1)}, u32[]{:S(2)}, u32[]{:S(2)}) collective-permute-start(bf16[32,768]{1,0:T(8,128)(2,1)S(1)} %get-tuple-element.73), channel_id=1, source_target_pairs={{0,24},{2,26},{4,28},{6,30},{8,16},{10,18},{12,20},{14,22},{16,8},... | collective-permute-start | bytes 147464 | tf_op jit(solution)/shard_map/ppermute | solution.py:444
  47.5 5.1 %collective-permute-start.15 = (bf16[32,768]{1,0:T(8,128)(2,1)S(1)}, bf16[32,768]{1,0:T(8,128)(2,1)S(1)}, u32[]{:S(2)}, u32[]{:S(2)}) collective-permute-start(bf16[32,768]{1,0:T(8,128)(2,1)S(1)} %get-tuple-element.74), channel_id=1, source_target_pairs={{0,16},{2,18},{4,20},{6,22},{8,24},{10,26},{12,28},{14,30},{16,0},... | collective-permute-start | bytes 147464 | tf_op jit(solution)/shard_map/ppermute | solution.py:444
  47.6 5.1 %collective-permute-start.16 = (bf16[32,768]{1,0:T(8,128)(2,1)S(1)}, bf16[32,768]{1,0:T(8,128)(2,1)S(1)}, u32[]{:S(2)}, u32[]{:S(2)}) collective-permute-start(bf16[32,768]{1,0:T(8,128)(2,1)S(1)} %get-tuple-element.75), channel_id=1, source_target_pairs={{0,8},{2,10},{4,12},{6,14},{8,0},{10,2},{12,4},{14,6},{16,24},{18,... | collective-permute-start | bytes 147464 | tf_op jit(solution)/shard_map/ppermute | solution.py:444
  48.2 6.1 %collective-permute-start.19 = (bf16[64,384]{1,0:T(8,128)(2,1)S(1)}, bf16[64,384]{1,0:T(8,128)(2,1)S(1)}, u32[]{:S(2)}, u32[]{:S(2)}) collective-permute-start(bf16[64,384]{1,0:T(8,128)(2,1)S(1)} %get-tuple-element.78.own), channel_id=1, source_target_pairs={{0,8},{2,10},{4,12},{6,14},{8,0},{10,2},{12,4},{14,6},{16,24},{18,... | collective-permute-start | bytes 147464 | tf_op jit(solution)/shard_map/ppermute | solution.py:444
  49.6 5.4 %collective-permute-start.20 = (bf16[64,384]{1,0:T(8,128)(2,1)S(1)}, bf16[64,384]{1,0:T(8,128)(2,1)S(1)}, u32[]{:S(2)}, u32[]{:S(2)}) collective-permute-start(bf16[64,384]{1,0:T(8,128)(2,1)S(1)} %collective-permute-done.18.across), channel_id=1, source_target_pairs={{0,8},{2,10},{4,12},{6,14},{8,0},{10,2},{12,4},{14,6},{16,24},{18,... | collective-permute-start | bytes 147464 | tf_op jit(solution)/shard_map/ppermute | solution.py:444
  52.7 13.8 %collective-permute-start.17 = (bf16[2,32,768]{2,1,0:T(8,128)(2,1)S(1)}, bf16[2,32,768]{2,1,0:T(8,128)(2,1)S(1)}, u32[]{:S(2)}, u32[]{:S(2)}) collective-permute-start(bf16[2,32,768]{2,1,0:T(8,128)(2,1)S(1)} %get-tuple-element.77), channel_id=1, source_target_pairs={{0,1},{1,0},{2,3},{3,2},{4,5},{5,4},{6,7},{7,6},{8,9},{9,8},{10,11... | collective-permute-start | bytes 294920 | tf_op jit(solution)/shard_map/ppermute | solution.py:478
  55.3 5.7 %collective-permute-start.21 = (bf16[16,768]{1,0:T(8,128)(2,1)S(1)}, bf16[16,768]{1,0:T(8,128)(2,1)S(1)}, u32[]{:S(2)}, u32[]{:S(2)}) collective-permute-start(bf16[16,768]{1,0:T(8,128)(2,1)S(1)} %get-tuple-element.80), channel_id=1, source_target_pairs={{0,24},{2,26},{4,28},{6,30},{8,16},{10,18},{12,20},{14,22},{16,8},... | collective-permute-start | bytes 73736 | tf_op jit(solution)/shard_map/ppermute | solution.py:444
  57.4 4.8 %collective-permute-start.22 = (bf16[16,768]{1,0:T(8,128)(2,1)S(1)}, bf16[16,768]{1,0:T(8,128)(2,1)S(1)}, u32[]{:S(2)}, u32[]{:S(2)}) collective-permute-start(bf16[16,768]{1,0:T(8,128)(2,1)S(1)} %get-tuple-element.81), channel_id=1, source_target_pairs={{0,16},{2,18},{4,20},{6,22},{8,24},{10,26},{12,28},{14,30},{16,0},... | collective-permute-start | bytes 73736 | tf_op jit(solution)/shard_map/ppermute | solution.py:444
  57.4 4.8 %collective-permute-start.23 = (bf16[16,768]{1,0:T(8,128)(2,1)S(1)}, bf16[16,768]{1,0:T(8,128)(2,1)S(1)}, u32[]{:S(2)}, u32[]{:S(2)}) collective-permute-start(bf16[16,768]{1,0:T(8,128)(2,1)S(1)} %get-tuple-element.82), channel_id=1, source_target_pairs={{0,8},{2,10},{4,12},{6,14},{8,0},{10,2},{12,4},{14,6},{16,24},{18,... | collective-permute-start | bytes 73736 | tf_op jit(solution)/shard_map/ppermute | solution.py:444
  62.3 4.2 %collective-permute-start.24 = (bf16[2,16,768]{2,1,0:T(8,128)(2,1)S(1)}, bf16[2,16,768]{2,1,0:T(8,128)(2,1)S(1)}, u32[]{:S(2)}, u32[]{:S(2)}) collective-permute-start(bf16[2,16,768]{2,1,0:T(8,128)(2,1)S(1)} %get-tuple-element.84), channel_id=1, source_target_pairs={{0,1},{1,0},{2,3},{3,2},{4,5},{5,4},{6,7},{7,6},{8,9},{9,8},{10,11... | collective-permute-start | bytes 147464 | tf_op jit(solution)/shard_map/ppermute | solution.py:478

commit v14 on v12

--- a/solution.py
+++ b/solution.py
@@ -244,40 +244,32 @@
     return lambda kind, cols: jnp.concatenate([own[kind, :, cols], some[:, kind, :, cols].reshape(-1, HD)], axis=0)
 
 
-def near_kernel(query, every, text, stale, peak, total, mixed):
+def near_kernel(query, every, near, text, stale, peak, total, mixed):
     heads = columns_of(query.shape[1])
-    image = image_segment(stale, 0, whole_part(every))
-    segments = [[(text[0, :, cols], text[1, :, cols]), image(cols)] for cols in heads]
+    images = [image_segment(stale, 0, whole_part(every)), image_segment(stale, 1, whole_part(near))]
+    segments = [[(text[0, :, cols], text[1, :, cols])] + [image(cols) for image in images] for cols in heads]
     states = absorb([query[:, cols] for cols in heads], segments, None)
     for head, state in enumerate(states):
         peak[head], total[head], mixed[head] = state
 
 
-def middle_kernel(query, near, own_far, some_far, stale, peak_in, total_in, mixed_in, peak, total, mixed):
+def middle_kernel(query, own_far, some_far, stale, peak_in, total_in, mixed_in, peak, total, mixed):
     heads = columns_of(query.shape[1])
-    images = [
-        image_segment(stale, 1, whole_part(near)),
-        image_segment(stale, 2, split_part(own_far, some_far)),
-    ]
-    segments = [[image(cols) for image in images] for cols in heads]
+    image = image_segment(stale, 2, split_part(own_far, some_far))
+    segments = [[image(cols)] for cols in heads]
     states = [(peak_in[head], total_in[head], mixed_in[head]) for head in range(len(heads))]
     states = absorb([query[:, cols] for cols in heads], segments, states)
     for head, state in enumerate(states):
         peak[head], total[head], mixed[head] = state
 
 
-def last_kernel(query, own_corner, some_corner, stale, peak, total, mixed, full, most, last):
+def last_kernel(query, own_corner, some_corner, stale, peak, total, mixed, out):
     heads = columns_of(query.shape[1])
     image = image_segment(stale, 3, split_part(own_corner, some_corner))
     states = [(peak[head], total[head], mixed[head]) for head in range(len(heads))]
     states = absorb([query[:, cols] for cols in heads], [[image(cols)] for cols in heads], states)
     for cols, (_, sums, mix) in zip(heads, states):
-        value = (mix / sums).astype(jnp.bfloat16)
-        full[:, cols] = value
-        if cols is not heads[-1]:
-            most[:, cols] = value
-        else:
-            last[...] = value
+        out[:, cols] = (mix / sums).astype(jnp.bfloat16)
 
 
 def attend_call(kernel, operands, shapes, keys):
@@ -298,11 +290,6 @@
     tokens, width = query.shape
     heads = width // HD
     return [jax.ShapeDtypeStruct((heads, tokens, size), jnp.float32) for size in (1, 1, HD)]
-
-
-def result_shapes(query):
-    tokens, width = query.shape
-    return [jax.ShapeDtypeStruct((tokens, size), jnp.bfloat16) for size in (width, width - HD, HD)]
 
 
 def order_kernel(*refs):
@@ -326,19 +313,15 @@
     )(*pieces)
 
 
-def term_of(part, weight, turn, skip, width):
+def term_of(part, weight, turn):
     group, _ = place()
-    start = jnp.bitwise_xor(group, turn) * width + skip
-    columns = pl.ds(pl.multiple_of(start, HD), part.shape[1])
+    width = part.shape[1]
+    columns = pl.ds(aligned(jnp.bitwise_xor(group, turn), width), width)
     return lax.dot_general(part[...], weight[:, columns], NT, preferred_element_type=jnp.float32)
 
 
-def begin_kernel(full, across_most, beside_most, across_last, beside_last, weight, out):
-    width = full.shape[1]
-    total = term_of(full, weight, 0, 0, width) + term_of(across_most, weight, 2, 0, width)
-    total += term_of(beside_most, weight, 1, 0, width)
-    total += term_of(across_last, weight, 2, width - HD, width)
-    out[...] = total + term_of(beside_last, weight, 1, width - HD, width)
+def begin_kernel(own, third, weight, out):
+    out[...] = term_of(own, weight, 0) + term_of(third, weight, 3)
 
 
 def begin(parts, weight):
@@ -356,18 +339,16 @@
     )(*parts, weight)
 
 
-def close_kernel(partial, most, last, weight, *rest):
+def close_kernel(partial, second, first, weight, *rest):
     outs, total = rest[:-1], rest[-1]
     group, _ = place()
     rows = outs[0].shape[0]
-    width = most.shape[1] + last.shape[1]
-    added = partial[...] + term_of(most, weight, 3, 0, width) + term_of(last, weight, 3, width - HD, width)
-    total[...] = added.astype(jnp.bfloat16)
+    total[...] = (partial[...] + term_of(second, weight, 2) + term_of(first, weight, 1)).astype(jnp.bfloat16)
     for turn, out in enumerate(outs):
         out[...] = total[pl.ds(aligned(jnp.bitwise_xor(group, turn), rows), rows), :]
 
 
-def close(groups, partial, parts, weight):
+def close(groups, partial, second, first, weight):
     tokens, columns = partial.shape
     return pl.pallas_call(
         close_kernel,
@@ -379,7 +360,7 @@
         cost_estimate=pl.CostEstimate(
             flops=tokens * weight.size, bytes_accessed=8 * tokens * columns, transcendentals=0
         ),
-    )(partial, *parts, weight)
+    )(partial, second, first, weight)
 
 
 def divide_kernel(*refs):
@@ -455,24 +436,21 @@
     every, some, query, weight, weight_far = lax.optimization_barrier(ready)[:5]
     near, some_far = swap(every, 1), swap(some, 2)
     share = stale.shape[2]
-    state = attend_call(near_kernel, [query, every, text, stale], state_shapes(query), share + text.shape[1])
-
-    near, some_far, own_far = lax.optimization_barrier((near, some_far, own_far, *state))[:3]
+    operands = [query, every, near, text, stale]
+    state = attend_call(near_kernel, operands, state_shapes(query), 2 * share + text.shape[1])
+
+    some_far, own_far = lax.optimization_barrier((some_far, own_far, *state))[:2]
     own_corner, some_corner = swap(own_far, 1), swap(some_far, 1)
-    state = attend_call(middle_kernel, [query, near, own_far, some_far, stale, *state], state_shapes(query), 2 * share)
+    state = attend_call(middle_kernel, [query, own_far, some_far, stale, *state], state_shapes(query), share)
     weight, weight_far = lax.optimization_barrier((weight, weight_far, own_corner, some_corner, *state))[:2]
     weight_near, weight_corner = swap(weight, 1), swap(weight_far, 1)
     operands = [query, own_corner, some_corner, stale, *state]
-    full, most, last = attend_call(last_kernel, operands, result_shapes(query), share)
-
-    across_most, across_last = swap(most, 2 * SPREAD), swap(last, 2 * SPREAD)
-    beside_most, beside_last = swap(most, SPREAD), swap(last, SPREAD)
-    final_most = swap(across_most, SPREAD)
-    final_last = swap(across_last, SPREAD)
+    shape = jax.ShapeDtypeStruct(query.shape, jnp.bfloat16)
+    (attended,) = attend_call(last_kernel, operands, [shape], share)
+
+    third, second, first = along([attended] * groups)
     weight = order([weight, weight_near, weight_far, weight_corner])
-    partial = begin([full, across_most, beside_most, across_last, beside_last], weight)
-    terms = close(groups, partial, [final_most, final_last], weight)
-
+    terms = close(groups, begin([attended, third], weight), second, first, weight)
     kept, sent = divide([terms[0], *along(terms)])
     received = lax.ppermute(sent, "head", [(0, 1), (1, 0)])
     return finish(kept, received, out_bias, out_gate)

time: 61.7 us -> 61.5 us (level)
  waiting for transfers between devices: 28.3 us -> 31 us
  starting transfers between devices: 23.2 us -> 20.8 us
    ppermute x20 -> x17, waiting for transfers between devices: 24.7 us -> 27.2 us  [swap(): return lax.ppermute(value, 'patch', [(p, p ^ twist) for p in range(size)])]
    ppermute x20 -> x17, starting transfers between devices: 21.6 us -> 19.2 us  [swap(): return lax.ppermute(value, 'patch', [(p, p ^ twist) for p in range(size)])]
  transfers between devices with their start and end apart: 21 -> 18, of which waited for: 9 -> 10; matrix products, arithmetic and copies ran while one was open for 0% -> 0% of each run, Pallas kernels for 14% -> 13%
where the time goes in v14:
time: 61.5 us; the launch traced here: 61.3 us
  waiting for transfers between devices  31 us (50%)
  starting transfers between devices  20.8 us (34%)
  Pallas kernels  9.27 us (15%)
    ppermute x17, waiting for transfers between devices, swap(): return lax.ppermute(value, 'patch', [(p, p ^ twist) for p in range(size)])  27.2 us
    ppermute x17, starting transfers between devices, swap(): return lax.ppermute(value, 'patch', [(p, p ^ twist) for p in range(size)])  19.2 us
    ppermute x1, waiting for transfers between devices, grouped_body(): received = lax.ppermute(sent, 'head', [(0, 1), (1, 0)])  3.86 us
    pallas_call x3, Pallas kernels, attend_call(): pl.pallas_call(kernel, out_shape=shapes, in_specs=[VMEM] * len(operands),...  3.2 us
    pallas_call x1, Pallas kernels, pack(): pl.pallas_call(pack_kernel, out_shape=[jax.ShapeDtypeStruct(shape, bf16)...  2.32 us
    pallas_call x1, Pallas kernels, pick(): pl.pallas_call(pick_kernel, out_shape=[jax.ShapeDtypeStruct((kinds, texts...  1.65 us
    ppermute x1, starting transfers between devices, grouped_body(): received = lax.ppermute(sent, 'head', [(0, 1), (1, 0)])  1.58 us
  transfers between devices with their start and end apart: 18, of which 10 were waited for; matrix products, arithmetic and copies ran while one was open for 0% of the time, Pallas kernels for 13%

profile of v14, /device:TPU:0, one launch (start us, length us, event | category | flops | bytes accessed | tf_op | source)
XLA Modules:
  0.0 61.3 jit_solution(9828503044337404529)
XLA Ops:
  0.0 2.9 %collective-permute-start.3 = (bf16[192,1536]{1,0:T(8,128)(2,1)}, bf16[192,1536]{1,0:T(8,128)(2,1)S(1)}, u32[]{:S(2)}, u32[]{:S(2)}) collective-permute-start(bf16[192,1536]{1,0:T(8,128)(2,1)} %bitcast.2), channel_id=1, source_target_pairs={{0,4},{2,6},{4,0},{6,2},{8,12},{10,14},{12,8},{14,10},{16,20},{18,... | collective-permute-start | bytes 1769480 | tf_op jit(solution)/shard_map/ppermute | solution.py:422
  2.9 2.3 %shard_map.82 = (bf16[3,48,384]{2,1,0:T(8,128)(2,1)}, bf16[3,48,384]{2,1,0:T(8,128)(2,1)}, bf16[3,48,384]{2,1,0:T(8,128)(2,1)}, bf16[3,48,384]{2,1,0:T(8,128)(2,1)}, bf16[2,48,384]{2,1,0:T(8,128)(2,1)}) custom-call(bf16[48,1536]{1,0:T(8,128)(2,1)} %queries_hbm.1, s32[2,48,1536]{2,1,0:T(8,128)} %codes_hbm.1, s32[12,2,48]{2,1,0:T(2,128)} %bitcast.5), custom_call_target="tpu_custom_call" | custom-call | flops 294912 | bytes 884736 | tf_op jit(solution)/shard_map/pallas_call | solution.py:109
  5.3 3.7 %collective-permute-start = (bf16[3,48,384]{2,1,0:T(8,128)(2,1)}, bf16[3,48,384]{2,1,0:T(8,128)(2,1)S(1)}, u32[]{:S(2)}, u32[]{:S(2)}) collective-permute-start(bf16[3,48,384]{2,1,0:T(8,128)(2,1)} %get-tuple-element.37), channel_id=1, source_target_pairs={{0,24},{2,26},{4,28},{6,30},{8,16},{10,18},{12,20},{14,22},{16,8},... | collective-permute-start | bytes 331784 | tf_op jit(solution)/shard_map/ppermute | solution.py:422
  8.9 0.8 %collective-permute-start.2 = (bf16[3,48,384]{2,1,0:T(8,128)(2,1)}, bf16[3,48,384]{2,1,0:T(8,128)(2,1)S(1)}, u32[]{:S(2)}, u32[]{:S(2)}) collective-permute-start(bf16[3,48,384]{2,1,0:T(8,128)(2,1)} %get-tuple-element.39), channel_id=1, source_target_pairs={{0,8},{2,10},{4,12},{6,14},{8,0},{10,2},{12,4},{14,6},{16,24},{18,... | collective-permute-start | bytes 331784 | tf_op jit(solution)/shard_map/ppermute | solution.py:422
  9.7 0.4 collective-permute-start.4
  10.1 1.7 %shard_map.84 = (bf16[2,512,384]{2,1,0:T(8,128)(2,1)S(1)}, bf16[4,2,192,384]{3,2,1,0:T(8,128)(2,1)S(1)}) custom-call(bf16[2,512,1536]{2,1,0:T(8,128)(2,1)} %text_hbm.1, bf16[2,768,1536]{2,1,0:T(8,128)(2,1)} %stale_hbm.1), custom_call_target="tpu_custom_call" | custom-call | bytes 8388608 | tf_op jit(solution)/shard_map/pallas_call | solution.py:154
  11.8 1.5 %collective-permute-done.refs_1_ = bf16[3,48,384]{2,1,0:T(8,128)(2,1)S(1)} collective-permute-done((bf16[3,48,384]{2,1,0:T(8,128)(2,1)}, bf16[3,48,384]{2,1,0:T(8,128)(2,1)S(1)}, u32[]{:S(2)}, u32[]{:S(2)}) %collective-permute-start) | collective-permute-done | bytes 110624 | tf_op jit(solution)/shard_map/ppermute | solution.py:422
  13.3 4.9 %collective-permute-done.1.refs_2_ = bf16[3,48,384]{2,1,0:T(8,128)(2,1)S(1)} collective-permute-done((bf16[3,48,384]{2,1,0:T(8,128)(2,1)}, bf16[3,48,384]{2,1,0:T(8,128)(2,1)S(1)}, u32[]{:S(2)}, u32[]{:S(2)}) %collective-permute-start.1) | collective-permute-done | bytes 110624 | tf_op jit(solution)/shard_map/ppermute | solution.py:422
  18.4 1.4 %collective-permute-start.5 = (bf16[3,2,48,384]{3,2,1,0:T(8,128)(2,1)S(1)}, bf16[3,2,48,384]{3,2,1,0:T(8,128)(2,1)S(1)}, u32[]{:S(2)}, u32[]{:S(2)}) collective-permute-start(bf16[3,2,48,384]{3,2,1,0:T(8,128)(2,1)S(1)} %get-tuple-element.47), channel_id=1, source_target_pairs={{0,4},{2,6},{4,0},{6,2},{8,12},{10,14},{12,8},{14,10},{16,20},{18,... | collective-permute-start | bytes 663560 | tf_op jit(solution)/shard_map/ppermute | solution.py:422
  19.8 0.1 collective-permute-done.6.near
  19.9 1.2 %shard_map.85 = (f32[3,192,1]{2,1,0:T(8,128)S(1)}, f32[3,192,1]{2,1,0:T(8,128)S(1)}, f32[3,192,128]{2,1,0:T(8,128)S(1)}) custom-call(bf16[192,384]{1,0:T(8,128)(2,1)S(1)} %get-tuple-element.46.query, bf16[4,2,48,384]{3,2,1,0:T(8,128)(2,1)S(1)} %get-tuple-element.48.every, bf16[4,2,48,384]{3,2,1,0:T(8,128)(2,1)S(1)} %collective-permute-done.6.near, ...), custom_call_target="tpu_custom_call" | custom-call | flops 528482304 | bytes 2752512 | tf_op jit(solution)/shard_map/pallas_call | solution.py:277
  21.1 5.1 %collective-permute-done.5.some_far = bf16[3,2,48,384]{3,2,1,0:T(8,128)(2,1)S(1)} collective-permute-done((bf16[3,2,48,384]{3,2,1,0:T(8,128)(2,1)S(1)}, bf16[3,2,48,384]{3,2,1,0:T(8,128)(2,1)S(1)}, u32[]{:S(2)}, u32[]{:S(2)}) %collective-permute-start.5) | collective-permute-done | bytes 221216 | tf_op jit(solution)/shard_map/ppermute | solution.py:422
  26.2 0.5 collective-permute-start.7
  26.7 0.9 %shard_map.86 = (f32[3,192,1]{2,1,0:T(8,128)S(1)}, f32[3,192,1]{2,1,0:T(8,128)S(1)}, f32[3,192,128]{2,1,0:T(8,128)S(1)}) custom-call(bf16[192,384]{1,0:T(8,128)(2,1)S(1)} %get-tuple-element.46.query, bf16[2,48,384]{2,1,0:T(8,128)(2,1)S(1)} %collective-permute-done.4.own_far, bf16[3,2,48,384]{3,2,1,0:T(8,128)(2,1)S(1)} %collective-permute-done.5.some_far, ...), custom_call_target="tpu_custom_call" | custom-call | flops 113246208 | bytes 589824 | tf_op jit(solution)/shard_map/pallas_call | solution.py:277
  27.6 0.2 collective-permute-done.7.own_corner
  27.8 0.2 collective-permute-start.10
  28.0 0.3 collective-permute-start.11
  28.3 1.1 %shard_map.87.own = bf16[192,384]{1,0:T(8,128)(2,1)S(1)} custom-call(bf16[192,384]{1,0:T(8,128)(2,1)S(1)} %get-tuple-element.46.query, bf16[2,48,384]{2,1,0:T(8,128)(2,1)S(1)} %collective-permute-done.7.own_corner, bf16[3,2,48,384]{3,2,1,0:T(8,128)(2,1)S(1)} %collective-permute-done.8.some_corner, bf16[4,2,192,384]{3,2,1,0:T(8,128)(2,1)S(1)} %get-tuple-element.45.stale, ...), custom_call_target="tpu_custom_call" | custom-call | flops 113246208 | bytes 589824 | tf_op jit(solution)/shard_map/pallas_call | solution.py:277
  29.4 3.6 %collective-permute-start.9 = (bf16[192,384]{1,0:T(8,128)(2,1)S(1)}, bf16[192,384]{1,0:T(8,128)(2,1)S(1)}, u32[]{:S(2)}, u32[]{:S(2)}) collective-permute-start(bf16[192,384]{1,0:T(8,128)(2,1)S(1)} %shard_map.87.own), channel_id=1, source_target_pairs={{0,24},{2,26},{4,28},{6,30},{8,16},{10,18},{12,20},{14,22},{16,8},... | collective-permute-start | bytes 442376 | tf_op jit(solution)/shard_map/ppermute | solution.py:422
  33.1 0.8 %collective-permute-start.13 = (bf16[192,384]{1,0:T(8,128)(2,1)S(1)}, bf16[192,384]{1,0:T(8,128)(2,1)S(1)}, u32[]{:S(2)}, u32[]{:S(2)}) collective-permute-start(bf16[192,384]{1,0:T(8,128)(2,1)S(1)} %shard_map.87.own), channel_id=1, source_target_pairs={{0,8},{2,10},{4,12},{6,14},{8,0},{10,2},{12,4},{14,6},{16,24},{18,... | collective-permute-start | bytes 442376 | tf_op jit(solution)/shard_map/ppermute | solution.py:422
  33.9 0.2 shard_map.88.weight
  34.1 4.0 %collective-permute-done.9.third = bf16[192,384]{1,0:T(8,128)(2,1)S(1)} collective-permute-done((bf16[192,384]{1,0:T(8,128)(2,1)S(1)}, bf16[192,384]{1,0:T(8,128)(2,1)S(1)}, u32[]{:S(2)}, u32[]{:S(2)}) %collective-permute-start.9) | collective-permute-done | bytes 147488 | tf_op jit(solution)/shard_map/ppermute | solution.py:422
  38.1 0.5 shard_map.89.partial
  38.6 7.3 %collective-permute-done.12.second = bf16[192,384]{1,0:T(8,128)(2,1)S(1)} collective-permute-done((bf16[192,384]{1,0:T(8,128)(2,1)S(1)}, bf16[192,384]{1,0:T(8,128)(2,1)S(1)}, u32[]{:S(2)}, u32[]{:S(2)}) %collective-permute-start.12) | collective-permute-done | bytes 147488 | tf_op jit(solution)/shard_map/ppermute | solution.py:422
  45.9 0.6 shard_map.90
  46.5 2.5 %collective-permute-start.14 = (bf16[48,768]{1,0:T(8,128)(2,1)S(1)}, bf16[48,768]{1,0:T(8,128)(2,1)S(1)}, u32[]{:S(2)}, u32[]{:S(2)}) collective-permute-start(bf16[48,768]{1,0:T(8,128)(2,1)S(1)} %get-tuple-element.62), channel_id=1, source_target_pairs={{0,24},{2,26},{4,28},{6,30},{8,16},{10,18},{12,20},{14,22},{16,8},... | collective-permute-start | bytes 221192 | tf_op jit(solution)/shard_map/ppermute | solution.py:422
  49.0 1.9 %collective-permute-start.16 = (bf16[48,768]{1,0:T(8,128)(2,1)S(1)}, bf16[48,768]{1,0:T(8,128)(2,1)S(1)}, u32[]{:S(2)}, u32[]{:S(2)}) collective-permute-start(bf16[48,768]{1,0:T(8,128)(2,1)S(1)} %get-tuple-element.64), channel_id=1, source_target_pairs={{0,8},{2,10},{4,12},{6,14},{8,0},{10,2},{12,4},{14,6},{16,24},{18,... | collective-permute-start | bytes 221192 | tf_op jit(solution)/shard_map/ppermute | solution.py:422
  50.9 1.9 %collective-permute-done.14.refs_1_ = bf16[48,768]{1,0:T(8,128)(2,1)S(1)} collective-permute-done((bf16[48,768]{1,0:T(8,128)(2,1)S(1)}, bf16[48,768]{1,0:T(8,128)(2,1)S(1)}, u32[]{:S(2)}, u32[]{:S(2)}) %collective-permute-start.14) | collective-permute-done | bytes 73760 | tf_op jit(solution)/shard_map/ppermute | solution.py:422
  52.8 2.3 %collective-permute-done.15.refs_2_ = bf16[48,768]{1,0:T(8,128)(2,1)S(1)} collective-permute-done((bf16[48,768]{1,0:T(8,128)(2,1)S(1)}, bf16[48,768]{1,0:T(8,128)(2,1)S(1)}, u32[]{:S(2)}, u32[]{:S(2)}) %collective-permute-start.15) | collective-permute-done | bytes 73760 | tf_op jit(solution)/shard_map/ppermute | solution.py:422
  55.1 1.6 %collective-permute-start.17 = (bf16[2,48,768]{2,1,0:T(8,128)(2,1)S(1)}, bf16[2,48,768]{2,1,0:T(8,128)(2,1)S(1)}, u32[]{:S(2)}, u32[]{:S(2)}) collective-permute-start(bf16[2,48,768]{2,1,0:T(8,128)(2,1)S(1)} %get-tuple-element.66), channel_id=1, source_target_pairs={{0,1},{1,0},{2,3},{3,2},{4,5},{5,4},{6,7},{7,6},{8,9},{9,8},{10,11... | collective-permute-start | bytes 442376 | tf_op jit(solution)/shard_map/ppermute | solution.py:455
  56.7 3.9 %collective-permute-done.17.arrived = bf16[2,48,768]{2,1,0:T(8,128)(2,1)S(1)} collective-permute-done((bf16[2,48,768]{2,1,0:T(8,128)(2,1)S(1)}, bf16[2,48,768]{2,1,0:T(8,128)(2,1)S(1)}, u32[]{:S(2)}, u32[]{:S(2)}) %collective-permute-start.17) | collective-permute-done | bytes 147488 | tf_op jit(solution)/shard_map/ppermute | solution.py:455
  60.6 0.7 %shard_map.92 = bf16[48,1536]{1,0:T(8,128)(2,1)} custom-call(bf16[2,48,768]{2,1,0:T(8,128)(2,1)S(1)} %get-tuple-element.65.kept, bf16[2,48,768]{2,1,0:T(8,128)(2,1)S(1)} %collective-permute-done.17.arrived, f32[1,1536]{1,0:T(1,128)S(1)} %reshape.6.bias, f32[1,1536]{1,0:T(1,128)S(1)} %reshape.7.gate), custom_call_target="tpu_custom_call" | custom-call | flops 221184 | bytes 294912 | tf_op jit(solution)/shard_map/pallas_call | solution.py:403
  (25 shorter events, 0.3 us)
Async XLA Ops:
  0.0 18.3 %collective-permute-start.3 = (bf16[192,1536]{1,0:T(8,128)(2,1)}, bf16[192,1536]{1,0:T(8,128)(2,1)S(1)}, u32[]{:S(2)}, u32[]{:S(2)}) collective-permute-start(bf16[192,1536]{1,0:T(8,128)(2,1)} %bitcast.2), channel_id=1, source_target_pairs={{0,4},{2,6},{4,0},{6,2},{8,12},{10,14},{12,8},{14,10},{16,20},{18,... | collective-permute-start | bytes 1769480 | tf_op jit(solution)/shard_map/ppermute | solution.py:422
  5.3 8.1 %collective-permute-start = (bf16[3,48,384]{2,1,0:T(8,128)(2,1)}, bf16[3,48,384]{2,1,0:T(8,128)(2,1)S(1)}, u32[]{:S(2)}, u32[]{:S(2)}) collective-permute-start(bf16[3,48,384]{2,1,0:T(8,128)(2,1)} %get-tuple-element.37), channel_id=1, source_target_pairs={{0,24},{2,26},{4,28},{6,30},{8,16},{10,18},{12,20},{14,22},{16,8},... | collective-permute-start | bytes 331784 | tf_op jit(solution)/shard_map/ppermute | solution.py:422
  8.9 9.3 %collective-permute-start.1 = (bf16[3,48,384]{2,1,0:T(8,128)(2,1)}, bf16[3,48,384]{2,1,0:T(8,128)(2,1)S(1)}, u32[]{:S(2)}, u32[]{:S(2)}) collective-permute-start(bf16[3,48,384]{2,1,0:T(8,128)(2,1)} %get-tuple-element.38), channel_id=1, source_target_pairs={{0,16},{2,18},{4,20},{6,22},{8,24},{10,26},{12,28},{14,30},{16,0},... | collective-permute-start | bytes 331784 | tf_op jit(solution)/shard_map/ppermute | solution.py:422
  8.9 9.3 %collective-permute-start.2 = (bf16[3,48,384]{2,1,0:T(8,128)(2,1)}, bf16[3,48,384]{2,1,0:T(8,128)(2,1)S(1)}, u32[]{:S(2)}, u32[]{:S(2)}) collective-permute-start(bf16[3,48,384]{2,1,0:T(8,128)(2,1)} %get-tuple-element.39), channel_id=1, source_target_pairs={{0,8},{2,10},{4,12},{6,14},{8,0},{10,2},{12,4},{14,6},{16,24},{18,... | collective-permute-start | bytes 331784 | tf_op jit(solution)/shard_map/ppermute | solution.py:422
  9.7 8.5 %copy-start.1 = (bf16[3,48,384]{2,1,0:T(8,128)(2,1)S(1)}, bf16[3,48,384]{2,1,0:T(8,128)(2,1)}, u32[]{:S(2)}) copy-start(bf16[3,48,384]{2,1,0:T(8,128)(2,1)} %get-tuple-element.36.refs_0_) | copy-start | bytes 331780
  9.7 8.5 %collective-permute-start.4 = (bf16[2,48,384]{2,1,0:T(8,128)(2,1)}, bf16[2,48,384]{2,1,0:T(8,128)(2,1)S(1)}, u32[]{:S(2)}, u32[]{:S(2)}) collective-permute-start(bf16[2,48,384]{2,1,0:T(8,128)(2,1)} %get-tuple-element.43), channel_id=1, source_target_pairs={{0,4},{2,6},{4,0},{6,2},{8,12},{10,14},{12,8},{14,10},{16,20},{18,... | collective-permute-start | bytes 221192 | tf_op jit(solution)/shard_map/ppermute | solution.py:422
  11.8 16.0 %copy-start = (bf16[1536,192]{0,1:T(8,128)(2,1)S(1)}, bf16[1536,192]{0,1:T(8,128)(2,1)}, u32[]{:S(2)}) copy-start(bf16[1536,192]{0,1:T(8,128)(2,1)} %param.13) | copy-start | bytes 1769476
  18.3 1.6 %collective-permute-start.6 = (bf16[4,2,48,384]{3,2,1,0:T(8,128)(2,1)S(1)}, bf16[4,2,48,384]{3,2,1,0:T(8,128)(2,1)S(1)}, u32[]{:S(2)}, u32[]{:S(2)}) collective-permute-start(bf16[4,2,48,384]{3,2,1,0:T(8,128)(2,1)S(1)} %get-tuple-element.48.every), channel_id=1, source_target_pairs={{0,2},{2,0},{4,6},{6,4},{8,10},{10,8},{12,14},{14,12},{16,18},{18,... | collective-permute-start | bytes 884744 | tf_op jit(solution)/shard_map/ppermute | solution.py:422
  18.4 7.8 %collective-permute-start.5 = (bf16[3,2,48,384]{3,2,1,0:T(8,128)(2,1)S(1)}, bf16[3,2,48,384]{3,2,1,0:T(8,128)(2,1)S(1)}, u32[]{:S(2)}, u32[]{:S(2)}) collective-permute-start(bf16[3,2,48,384]{3,2,1,0:T(8,128)(2,1)S(1)} %get-tuple-element.47), channel_id=1, source_target_pairs={{0,4},{2,6},{4,0},{6,2},{8,12},{10,14},{12,8},{14,10},{16,20},{18,... | collective-permute-start | bytes 663560 | tf_op jit(solution)/shard_map/ppermute | solution.py:422
  26.2 1.6 %collective-permute-start.8 = (bf16[3,2,48,384]{3,2,1,0:T(8,128)(2,1)S(1)}, bf16[3,2,48,384]{3,2,1,0:T(8,128)(2,1)S(1)}, u32[]{:S(2)}, u32[]{:S(2)}) collective-permute-start(bf16[3,2,48,384]{3,2,1,0:T(8,128)(2,1)S(1)} %collective-permute-done.5.some_far), channel_id=1, source_target_pairs={{0,2},{2,0},{4,6},{6,4},{8,10},{10,8},{12,14},{14,12},{16,18},{18,... | collective-permute-start | bytes 663560 | tf_op jit(solution)/shard_map/ppermute | solution.py:422
  26.2 1.6 %collective-permute-start.7 = (bf16[2,48,384]{2,1,0:T(8,128)(2,1)S(1)}, bf16[2,48,384]{2,1,0:T(8,128)(2,1)S(1)}, u32[]{:S(2)}, u32[]{:S(2)}) collective-permute-start(bf16[2,48,384]{2,1,0:T(8,128)(2,1)S(1)} %collective-permute-done.4.own_far), channel_id=1, source_target_pairs={{0,2},{2,0},{4,6},{6,4},{8,10},{10,8},{12,14},{14,12},{16,18},{18,... | collective-permute-start | bytes 221192 | tf_op jit(solution)/shard_map/ppermute | solution.py:422
  27.8 6.1 %collective-permute-start.10 = (bf16[192,1536]{1,0:T(8,128)(2,1)S(1)}, bf16[192,1536]{1,0:T(8,128)(2,1)S(1)}, u32[]{:S(2)}, u32[]{:S(2)}) collective-permute-start(bf16[192,1536]{1,0:T(8,128)(2,1)S(1)} %bitcast.3), channel_id=1, source_target_pairs={{0,2},{2,0},{4,6},{6,4},{8,10},{10,8},{12,14},{14,12},{16,18},{18,... | collective-permute-start | bytes 1769480 | tf_op jit(solution)/shard_map/ppermute | solution.py:422
  28.0 5.9 %collective-permute-start.11 = (bf16[192,1536]{1,0:T(8,128)(2,1)S(1)}, bf16[192,1536]{1,0:T(8,128)(2,1)S(1)}, u32[]{:S(2)}, u32[]{:S(2)}) collective-permute-start(bf16[192,1536]{1,0:T(8,128)(2,1)S(1)} %collective-permute-done.3.refs_2_), channel_id=1, source_target_pairs={{0,2},{2,0},{4,6},{6,4},{8,10},{10,8},{12,14},{14,12},{16,18},{18,... | collective-permute-start | bytes 1769480 | tf_op jit(solution)/shard_map/ppermute | solution.py:422
  29.4 8.6 %collective-permute-start.9 = (bf16[192,384]{1,0:T(8,128)(2,1)S(1)}, bf16[192,384]{1,0:T(8,128)(2,1)S(1)}, u32[]{:S(2)}, u32[]{:S(2)}) collective-permute-start(bf16[192,384]{1,0:T(8,128)(2,1)S(1)} %shard_map.87.own), channel_id=1, source_target_pairs={{0,24},{2,26},{4,28},{6,30},{8,16},{10,18},{12,20},{14,22},{16,8},... | collective-permute-start | bytes 442376 | tf_op jit(solution)/shard_map/ppermute | solution.py:422
  33.0 12.8 %collective-permute-start.12 = (bf16[192,384]{1,0:T(8,128)(2,1)S(1)}, bf16[192,384]{1,0:T(8,128)(2,1)S(1)}, u32[]{:S(2)}, u32[]{:S(2)}) collective-permute-start(bf16[192,384]{1,0:T(8,128)(2,1)S(1)} %shard_map.87.own), channel_id=1, source_target_pairs={{0,16},{2,18},{4,20},{6,22},{8,24},{10,26},{12,28},{14,30},{16,0},... | collective-permute-start | bytes 442376 | tf_op jit(solution)/shard_map/ppermute | solution.py:422
  33.1 12.8 %collective-permute-start.13 = (bf16[192,384]{1,0:T(8,128)(2,1)S(1)}, bf16[192,384]{1,0:T(8,128)(2,1)S(1)}, u32[]{:S(2)}, u32[]{:S(2)}) collective-permute-start(bf16[192,384]{1,0:T(8,128)(2,1)S(1)} %shard_map.87.own), channel_id=1, source_target_pairs={{0,8},{2,10},{4,12},{6,14},{8,0},{10,2},{12,4},{14,6},{16,24},{18,... | collective-permute-start | bytes 442376 | tf_op jit(solution)/shard_map/ppermute | solution.py:422
  34.1 22.6 %copy-start.2 = (f32[1536]{0:T(1024)S(1)}, f32[1536]{0:T(1024)}, u32[]{:S(2)}) copy-start(f32[1536]{0:T(1024)} %param.14) | copy-start | bytes 18436
  34.1 22.6 %copy-start.3 = (f32[1536]{0:T(1024)S(1)}, f32[1536]{0:T(1024)}, u32[]{:S(2)}) copy-start(f32[1536]{0:T(1024)} %param.15) | copy-start | bytes 18436
  46.5 6.3 %collective-permute-start.14 = (bf16[48,768]{1,0:T(8,128)(2,1)S(1)}, bf16[48,768]{1,0:T(8,128)(2,1)S(1)}, u32[]{:S(2)}, u32[]{:S(2)}) collective-permute-start(bf16[48,768]{1,0:T(8,128)(2,1)S(1)} %get-tuple-element.62), channel_id=1, source_target_pairs={{0,24},{2,26},{4,28},{6,30},{8,16},{10,18},{12,20},{14,22},{16,8},... | collective-permute-start | bytes 221192 | tf_op jit(solution)/shard_map/ppermute | solution.py:422
  49.0 6.0 %collective-permute-start.15 = (bf16[48,768]{1,0:T(8,128)(2,1)S(1)}, bf16[48,768]{1,0:T(8,128)(2,1)S(1)}, u32[]{:S(2)}, u32[]{:S(2)}) collective-permute-start(bf16[48,768]{1,0:T(8,128)(2,1)S(1)} %get-tuple-element.63), channel_id=1, source_target_pairs={{0,16},{2,18},{4,20},{6,22},{8,24},{10,26},{12,28},{14,30},{16,0},... | collective-permute-start | bytes 221192 | tf_op jit(solution)/shard_map/ppermute | solution.py:422
  49.0 6.0 %collective-permute-start.16 = (bf16[48,768]{1,0:T(8,128)(2,1)S(1)}, bf16[48,768]{1,0:T(8,128)(2,1)S(1)}, u32[]{:S(2)}, u32[]{:S(2)}) collective-permute-start(bf16[48,768]{1,0:T(8,128)(2,1)S(1)} %get-tuple-element.64), channel_id=1, source_target_pairs={{0,8},{2,10},{4,12},{6,14},{8,0},{10,2},{12,4},{14,6},{16,24},{18,... | collective-permute-start | bytes 221192 | tf_op jit(solution)/shard_map/ppermute | solution.py:422
  55.1 5.5 %collective-permute-start.17 = (bf16[2,48,768]{2,1,0:T(8,128)(2,1)S(1)}, bf16[2,48,768]{2,1,0:T(8,128)(2,1)S(1)}, u32[]{:S(2)}, u32[]{:S(2)}) collective-permute-start(bf16[2,48,768]{2,1,0:T(8,128)(2,1)S(1)} %get-tuple-element.66), channel_id=1, source_target_pairs={{0,1},{1,0},{2,3},{3,2},{4,5},{5,4},{6,7},{7,6},{8,9},{9,8},{10,11... | collective-permute-start | bytes 442376 | tf_op jit(solution)/shard_map/ppermute | solution.py:455

commit v15 on v14

--- a/solution.py
+++ b/solution.py
@@ -9,6 +9,7 @@
 
 HD = 128
 SPREAD = 4
+TURNS = (0, 2, 3, 1)
 PACK_LIMIT = 56 << 20
 SMALL = 16 << 20
 PICK_LIMIT = 50 << 20
@@ -133,7 +134,7 @@
     copies = [pltpu.make_async_copy(text_hbm.at[:, :, columns], text, sems.at[0])]
     for twist in range(SPREAD):
         for position in range(groups):
-            origin = jnp.bitwise_xor(group, (groups - position) % groups)
+            origin = jnp.bitwise_xor(group, TURNS[position])
             token = origin * SPREAD + jnp.bitwise_xor(spot, twist)
             copies.append(
                 pltpu.make_async_copy(
@@ -173,7 +174,7 @@
         every[position] = part[0:kinds]
         if position:
             some[position - 1] = part[0:kinds]
-        origin = jnp.bitwise_xor(group, (groups - position) % groups)
+        origin = jnp.bitwise_xor(group, TURNS[position])
         query[pl.ds(aligned(origin, rows), rows), :] = part[kinds]
 
 
@@ -263,13 +264,16 @@
         peak[head], total[head], mixed[head] = state
 
 
-def last_kernel(query, own_corner, some_corner, stale, peak, total, mixed, out):
+def last_kernel(query, own_corner, some_corner, stale, peak, total, mixed, out, most):
     heads = columns_of(query.shape[1])
     image = image_segment(stale, 3, split_part(own_corner, some_corner))
     states = [(peak[head], total[head], mixed[head]) for head in range(len(heads))]
     states = absorb([query[:, cols] for cols in heads], [[image(cols)] for cols in heads], states)
     for cols, (_, sums, mix) in zip(heads, states):
-        out[:, cols] = (mix / sums).astype(jnp.bfloat16)
+        value = (mix / sums).astype(jnp.bfloat16)
+        out[:, cols] = value
+        if cols is not heads[-1]:
+            most[:, cols] = value
 
 
 def attend_call(kernel, operands, shapes, keys):
@@ -313,15 +317,16 @@
     )(*pieces)
 
 
-def term_of(part, weight, turn):
+def term_of(part, weight, turn, width, skip=0):
     group, _ = place()
-    width = part.shape[1]
-    columns = pl.ds(aligned(jnp.bitwise_xor(group, turn), width), width)
+    start = jnp.bitwise_xor(group, turn) * width + skip
+    columns = pl.ds(pl.multiple_of(start, HD), part.shape[1])
     return lax.dot_general(part[...], weight[:, columns], NT, preferred_element_type=jnp.float32)
 
 
-def begin_kernel(own, third, weight, out):
-    out[...] = term_of(own, weight, 0) + term_of(third, weight, 3)
+def begin_kernel(own, second, first, weight, out):
+    width = own.shape[1]
+    out[...] = term_of(own, weight, 0, width) + term_of(second, weight, 2, width) + term_of(first, weight, 1, width)
 
 
 def begin(parts, weight):
@@ -339,16 +344,18 @@
     )(*parts, weight)
 
 
-def close_kernel(partial, second, first, weight, *rest):
+def close_kernel(partial, most, last, weight, *rest):
     outs, total = rest[:-1], rest[-1]
     group, _ = place()
     rows = outs[0].shape[0]
-    total[...] = (partial[...] + term_of(second, weight, 2) + term_of(first, weight, 1)).astype(jnp.bfloat16)
+    width = most.shape[1] + last.shape[1]
+    added = partial[...] + term_of(most, weight, 3, width) + term_of(last, weight, 3, width, width - HD)
+    total[...] = added.astype(jnp.bfloat16)
     for turn, out in enumerate(outs):
         out[...] = total[pl.ds(aligned(jnp.bitwise_xor(group, turn), rows), rows), :]
 
 
-def close(groups, partial, second, first, weight):
+def close(groups, partial, most, last, weight):
     tokens, columns = partial.shape
     return pl.pallas_call(
         close_kernel,
@@ -360,7 +367,7 @@
         cost_estimate=pl.CostEstimate(
             flops=tokens * weight.size, bytes_accessed=8 * tokens * columns, transcendentals=0
         ),
-    )(partial, second, first, weight)
+    )(partial, most, last, weight)
 
 
 def divide_kernel(*refs):
@@ -369,7 +376,7 @@
     half = lax.axis_index("head")
     blocks = keep.shape[0]
     for position, part in enumerate(parts):
-        held[jnp.bitwise_xor(group, (len(parts) - position) % len(parts))] = part[...]
+        held[jnp.bitwise_xor(group, TURNS[position])] = part[...]
     for block in range(blocks):
         keep[block] = held[half * blocks + block]
         send[block] = held[(1 - half) * blocks + block]
@@ -422,7 +429,7 @@
         return lax.ppermute(value, "patch", [(p, p ^ twist) for p in range(size)])
 
     def along(values):
-        return [swap(values[turn], turn * SPREAD) for turn in reversed(range(1, groups))]
+        return [swap(values[turn], turn * SPREAD) for turn in TURNS[1:]]
 
     weight = out_weight.T
     weight_far = swap(weight, 2)
@@ -445,12 +452,14 @@
     weight, weight_far = lax.optimization_barrier((weight, weight_far, own_corner, some_corner, *state))[:2]
     weight_near, weight_corner = swap(weight, 1), swap(weight_far, 1)
     operands = [query, own_corner, some_corner, stale, *state]
-    shape = jax.ShapeDtypeStruct(query.shape, jnp.bfloat16)
-    (attended,) = attend_call(last_kernel, operands, [shape], share)
-
-    third, second, first = along([attended] * groups)
+    tokens, width = query.shape
+    shapes = [jax.ShapeDtypeStruct((tokens, size), jnp.bfloat16) for size in (width, width - HD)]
+    attended, most = attend_call(last_kernel, operands, shapes, share)
+
+    second, first, third = (swap(value, turn * SPREAD) for turn, value in ((2, attended), (1, attended), (3, most)))
+    passed = swap(second[:, width - HD :], SPREAD)
     weight = order([weight, weight_near, weight_far, weight_corner])
-    terms = close(groups, begin([attended, third], weight), second, first, weight)
+    terms = close(groups, begin([attended, second, first], weight), third, passed, weight)
     kept, sent = divide([terms[0], *along(terms)])
     received = lax.ppermute(sent, "head", [(0, 1), (1, 0)])
     return finish(kept, received, out_bias, out_gate)

time: 61.5 us -> 59.9 us (0.974)
  waiting for transfers between devices: 31 us -> 28.4 us
  starting transfers between devices: 20.8 us -> 21.8 us
    ppermute x17 -> x18, waiting for transfers between devices: 27.2 us -> 25.1 us  [swap(): return lax.ppermute(value, 'patch', [(p, p ^ twist) for p in range(size)])]
    ppermute x17 -> x18, starting transfers between devices: 19.2 us -> 19.9 us  [swap(): return lax.ppermute(value, 'patch', [(p, p ^ twist) for p in range(size)])]
  transfers between devices with their start and end apart: 18 -> 19, of which waited for: 10 -> 12; matrix products, arithmetic and copies ran while one was open for 0% -> 0% of each run, Pallas kernels for 13% -> 14%
where the time goes in v15:
time: 59.9 us; the launch traced here: 59.7 us
  waiting for transfers between devices  28.4 us (47%)
  starting transfers between devices  21.8 us (36%)
  Pallas kernels  9.29 us (16%)
    ppermute x18, waiting for transfers between devices, swap(): return lax.ppermute(value, 'patch', [(p, p ^ twist) for p in range(size)])  25.1 us
    ppermute x18, starting transfers between devices, swap(): return lax.ppermute(value, 'patch', [(p, p ^ twist) for p in range(size)])  19.9 us
    ppermute x1, waiting for transfers between devices, grouped_body(): received = lax.ppermute(sent, 'head', [(0, 1), (1, 0)])  3.3 us
    pallas_call x3, Pallas kernels, attend_call(): pl.pallas_call(kernel, out_shape=shapes, in_specs=[VMEM] * len(operands),...  3.19 us
    pallas_call x1, Pallas kernels, pack(): pl.pallas_call(pack_kernel, out_shape=[jax.ShapeDtypeStruct(shape, bf16)...  2.32 us
    ppermute x1, starting transfers between devices, grouped_body(): received = lax.ppermute(sent, 'head', [(0, 1), (1, 0)])  1.87 us
    pallas_call x1, Pallas kernels, pick(): pl.pallas_call(pick_kernel, out_shape=[jax.ShapeDtypeStruct((kinds, texts...  1.65 us
  transfers between devices with their start and end apart: 19, of which 12 were waited for; matrix products, arithmetic and copies ran while one was open for 0% of the time, Pallas kernels for 14%

profile of v15, /device:TPU:0, one launch (start us, length us, event | category | flops | bytes accessed | tf_op | source)
XLA Modules:
  0.0 59.7 jit_solution(17129822992341534544)
XLA Ops:
  0.0 2.9 %collective-permute-start.3 = (bf16[192,1536]{1,0:T(8,128)(2,1)}, bf16[192,1536]{1,0:T(8,128)(2,1)S(1)}, u32[]{:S(2)}, u32[]{:S(2)}) collective-permute-start(bf16[192,1536]{1,0:T(8,128)(2,1)} %bitcast.2), channel_id=1, source_target_pairs={{0,4},{2,6},{4,0},{6,2},{8,12},{10,14},{12,8},{14,10},{16,20},{18,... | collective-permute-start | bytes 1769480 | tf_op jit(solution)/shard_map/ppermute | solution.py:429
  2.9 2.3 %shard_map.82 = (bf16[3,48,384]{2,1,0:T(8,128)(2,1)}, bf16[3,48,384]{2,1,0:T(8,128)(2,1)}, bf16[3,48,384]{2,1,0:T(8,128)(2,1)}, bf16[3,48,384]{2,1,0:T(8,128)(2,1)}, bf16[2,48,384]{2,1,0:T(8,128)(2,1)}) custom-call(bf16[48,1536]{1,0:T(8,128)(2,1)} %queries_hbm.1, s32[2,48,1536]{2,1,0:T(8,128)} %codes_hbm.1, s32[12,2,48]{2,1,0:T(2,128)} %bitcast.5), custom_call_target="tpu_custom_call" | custom-call | flops 294912 | bytes 884736 | tf_op jit(solution)/shard_map/pallas_call | solution.py:110
  5.3 2.7 %collective-permute-start = (bf16[3,48,384]{2,1,0:T(8,128)(2,1)}, bf16[3,48,384]{2,1,0:T(8,128)(2,1)S(1)}, u32[]{:S(2)}, u32[]{:S(2)}) collective-permute-start(bf16[3,48,384]{2,1,0:T(8,128)(2,1)} %get-tuple-element.39), channel_id=1, source_target_pairs={{0,16},{2,18},{4,20},{6,22},{8,24},{10,26},{12,28},{14,30},{16,0},... | collective-permute-start | bytes 331784 | tf_op jit(solution)/shard_map/ppermute | solution.py:429
  7.9 1.3 %collective-permute-start.1 = (bf16[3,48,384]{2,1,0:T(8,128)(2,1)}, bf16[3,48,384]{2,1,0:T(8,128)(2,1)S(1)}, u32[]{:S(2)}, u32[]{:S(2)}) collective-permute-start(bf16[3,48,384]{2,1,0:T(8,128)(2,1)} %get-tuple-element.40), channel_id=1, source_target_pairs={{0,24},{2,26},{4,28},{6,30},{8,16},{10,18},{12,20},{14,22},{16,8},... | collective-permute-start | bytes 331784 | tf_op jit(solution)/shard_map/ppermute | solution.py:429
  9.5 0.5 collective-permute-start.4
  10.0 1.7 %shard_map.84 = (bf16[2,512,384]{2,1,0:T(8,128)(2,1)S(1)}, bf16[4,2,192,384]{3,2,1,0:T(8,128)(2,1)S(1)}) custom-call(bf16[2,512,1536]{2,1,0:T(8,128)(2,1)} %text_hbm.1, bf16[2,768,1536]{2,1,0:T(8,128)(2,1)} %stale_hbm.1), custom_call_target="tpu_custom_call" | custom-call | bytes 8388608 | tf_op jit(solution)/shard_map/pallas_call | solution.py:155
  11.7 5.1 %collective-permute-done.refs_1_ = bf16[3,48,384]{2,1,0:T(8,128)(2,1)S(1)} collective-permute-done((bf16[3,48,384]{2,1,0:T(8,128)(2,1)}, bf16[3,48,384]{2,1,0:T(8,128)(2,1)S(1)}, u32[]{:S(2)}, u32[]{:S(2)}) %collective-permute-start) | collective-permute-done | bytes 110624 | tf_op jit(solution)/shard_map/ppermute | solution.py:429
  17.0 1.0 %collective-permute-done.4.own_far = bf16[2,48,384]{2,1,0:T(8,128)(2,1)S(1)} collective-permute-done((bf16[2,48,384]{2,1,0:T(8,128)(2,1)}, bf16[2,48,384]{2,1,0:T(8,128)(2,1)S(1)}, u32[]{:S(2)}, u32[]{:S(2)}) %collective-permute-start.4) | collective-permute-done | bytes 73760 | tf_op jit(solution)/shard_map/ppermute | solution.py:429
  18.1 1.7 %collective-permute-start.5 = (bf16[3,2,48,384]{3,2,1,0:T(8,128)(2,1)S(1)}, bf16[3,2,48,384]{3,2,1,0:T(8,128)(2,1)S(1)}, u32[]{:S(2)}, u32[]{:S(2)}) collective-permute-start(bf16[3,2,48,384]{3,2,1,0:T(8,128)(2,1)S(1)} %get-tuple-element.49), channel_id=1, source_target_pairs={{0,4},{2,6},{4,0},{6,2},{8,12},{10,14},{12,8},{14,10},{16,20},{18,... | collective-permute-start | bytes 663560 | tf_op jit(solution)/shard_map/ppermute | solution.py:429
  19.8 1.2 %shard_map.85 = (f32[3,192,1]{2,1,0:T(8,128)S(1)}, f32[3,192,1]{2,1,0:T(8,128)S(1)}, f32[3,192,128]{2,1,0:T(8,128)S(1)}) custom-call(bf16[192,384]{1,0:T(8,128)(2,1)S(1)} %get-tuple-element.48.query, bf16[4,2,48,384]{3,2,1,0:T(8,128)(2,1)S(1)} %get-tuple-element.50.every, bf16[4,2,48,384]{3,2,1,0:T(8,128)(2,1)S(1)} %collective-permute-done.6.near, ...), custom_call_target="tpu_custom_call" | custom-call | flops 528482304 | bytes 2752512 | tf_op jit(solution)/shard_map/pallas_call | solution.py:281
  21.0 4.9 %collective-permute-done.5.some_far = bf16[3,2,48,384]{3,2,1,0:T(8,128)(2,1)S(1)} collective-permute-done((bf16[3,2,48,384]{3,2,1,0:T(8,128)(2,1)S(1)}, bf16[3,2,48,384]{3,2,1,0:T(8,128)(2,1)S(1)}, u32[]{:S(2)}, u32[]{:S(2)}) %collective-permute-start.5) | collective-permute-done | bytes 221216 | tf_op jit(solution)/shard_map/ppermute | solution.py:429
  25.9 0.5 collective-permute-start.7
  26.4 0.9 %shard_map.86 = (f32[3,192,1]{2,1,0:T(8,128)S(1)}, f32[3,192,1]{2,1,0:T(8,128)S(1)}, f32[3,192,128]{2,1,0:T(8,128)S(1)}) custom-call(bf16[192,384]{1,0:T(8,128)(2,1)S(1)} %get-tuple-element.48.query, bf16[2,48,384]{2,1,0:T(8,128)(2,1)S(1)} %collective-permute-done.4.own_far, bf16[3,2,48,384]{3,2,1,0:T(8,128)(2,1)S(1)} %collective-permute-done.5.some_far, ...), custom_call_target="tpu_custom_call" | custom-call | flops 113246208 | bytes 589824 | tf_op jit(solution)/shard_map/pallas_call | solution.py:281
  27.7 0.3 collective-permute-start.12
  28.0 1.1 %shard_map.87 = (bf16[192,384]{1,0:T(8,128)(2,1)S(1)}, bf16[192,256]{1,0:T(8,128)(2,1)S(1)}) custom-call(bf16[192,384]{1,0:T(8,128)(2,1)S(1)} %get-tuple-element.48.query, bf16[2,48,384]{2,1,0:T(8,128)(2,1)S(1)} %collective-permute-done.7.own_corner, bf16[3,2,48,384]{3,2,1,0:T(8,128)(2,1)S(1)} %collective-permute-done.8.some_corner, ...), custom_call_target="tpu_custom_call" | custom-call | flops 113246208 | bytes 589824 | tf_op jit(solution)/shard_map/pallas_call | solution.py:281
  29.1 2.9 %collective-permute-start.9 = (bf16[192,384]{1,0:T(8,128)(2,1)S(1)}, bf16[192,384]{1,0:T(8,128)(2,1)S(1)}, u32[]{:S(2)}, u32[]{:S(2)}) collective-permute-start(bf16[192,384]{1,0:T(8,128)(2,1)S(1)} %get-tuple-element.59.own), channel_id=1, source_target_pairs={{0,16},{2,18},{4,20},{6,22},{8,24},{10,26},{12,28},{14,30},{16,0},... | collective-permute-start | bytes 442376 | tf_op jit(solution)/shard_map/ppermute | solution.py:429
  32.0 1.6 %collective-permute-start.10 = (bf16[192,384]{1,0:T(8,128)(2,1)S(1)}, bf16[192,384]{1,0:T(8,128)(2,1)S(1)}, u32[]{:S(2)}, u32[]{:S(2)}) collective-permute-start(bf16[192,384]{1,0:T(8,128)(2,1)S(1)} %get-tuple-element.59.own), channel_id=1, source_target_pairs={{0,8},{2,10},{4,12},{6,14},{8,0},{10,2},{12,4},{14,6},{16,24},{18,... | collective-permute-start | bytes 442376 | tf_op jit(solution)/shard_map/ppermute | solution.py:429
  33.6 6.4 %collective-permute-done.9.second = bf16[192,384]{1,0:T(8,128)(2,1)S(1)} collective-permute-done((bf16[192,384]{1,0:T(8,128)(2,1)S(1)}, bf16[192,384]{1,0:T(8,128)(2,1)S(1)}, u32[]{:S(2)}, u32[]{:S(2)}) %collective-permute-start.9) | collective-permute-done | bytes 147488 | tf_op jit(solution)/shard_map/ppermute | solution.py:429
  40.1 0.6 %collective-permute-start.14 = (bf16[192,128]{1,0:T(8,128)(2,1)S(1)}, bf16[192,128]{1,0:T(8,128)(2,1)S(1)}, u32[]{:S(2)}, u32[]{:S(2)}) collective-permute-start(bf16[192,128]{1,0:T(8,128)(2,1)S(1)} %slice.4), channel_id=1, source_target_pairs={{0,8},{2,10},{4,12},{6,14},{8,0},{10,2},{12,4},{14,6},{16,24},{18,... | collective-permute-start | bytes 147464 | tf_op jit(solution)/shard_map/ppermute | solution.py:429
  40.9 0.7 %shard_map.89.partial = f32[192,768]{1,0:T(8,128)S(1)} custom-call(bf16[192,384]{1,0:T(8,128)(2,1)S(1)} %get-tuple-element.59.own, bf16[192,384]{1,0:T(8,128)(2,1)S(1)} %collective-permute-done.9.second, bf16[192,384]{1,0:T(8,128)(2,1)S(1)} %collective-permute-done.10.first, bf16[768,1536]{1,0:T(8,128)(2,1)S(1)} %shard_map.88.weight), custom_call_target="tpu_custom_call" | custom-call | flops 452984832 | bytes 589824 | tf_op jit(solution)/shard_map/pallas_call | solution.py:335
  41.6 1.1 %collective-permute-done.13.most = bf16[192,256]{1,0:T(8,128)(2,1)S(1)} collective-permute-done((bf16[192,256]{1,0:T(8,128)(2,1)S(1)}, bf16[192,256]{1,0:T(8,128)(2,1)S(1)}, u32[]{:S(2)}, u32[]{:S(2)}) %collective-permute-start.13) | collective-permute-done | bytes 98336 | tf_op jit(solution)/shard_map/ppermute | solution.py:429
  42.8 1.4 %collective-permute-done.14.last = bf16[192,128]{1,0:T(8,128)(2,1)S(1)} collective-permute-done((bf16[192,128]{1,0:T(8,128)(2,1)S(1)}, bf16[192,128]{1,0:T(8,128)(2,1)S(1)}, u32[]{:S(2)}, u32[]{:S(2)}) %collective-permute-start.14) | collective-permute-done | bytes 49184 | tf_op jit(solution)/shard_map/ppermute | solution.py:429
  44.1 0.4 shard_map.90
  44.5 2.3 %collective-permute-start.15 = (bf16[48,768]{1,0:T(8,128)(2,1)S(1)}, bf16[48,768]{1,0:T(8,128)(2,1)S(1)}, u32[]{:S(2)}, u32[]{:S(2)}) collective-permute-start(bf16[48,768]{1,0:T(8,128)(2,1)S(1)} %get-tuple-element.66), channel_id=1, source_target_pairs={{0,16},{2,18},{4,20},{6,22},{8,24},{10,26},{12,28},{14,30},{16,0},... | collective-permute-start | bytes 221192 | tf_op jit(solution)/shard_map/ppermute | solution.py:429
  46.9 1.5 %collective-permute-start.16 = (bf16[48,768]{1,0:T(8,128)(2,1)S(1)}, bf16[48,768]{1,0:T(8,128)(2,1)S(1)}, u32[]{:S(2)}, u32[]{:S(2)}) collective-permute-start(bf16[48,768]{1,0:T(8,128)(2,1)S(1)} %get-tuple-element.67), channel_id=1, source_target_pairs={{0,24},{2,26},{4,28},{6,30},{8,16},{10,18},{12,20},{14,22},{16,8},... | collective-permute-start | bytes 221192 | tf_op jit(solution)/shard_map/ppermute | solution.py:429
  48.4 0.5 collective-permute-start.17
  48.9 3.3 %collective-permute-done.15.refs_1_ = bf16[48,768]{1,0:T(8,128)(2,1)S(1)} collective-permute-done((bf16[48,768]{1,0:T(8,128)(2,1)S(1)}, bf16[48,768]{1,0:T(8,128)(2,1)S(1)}, u32[]{:S(2)}, u32[]{:S(2)}) %collective-permute-start.15) | collective-permute-done | bytes 73760 | tf_op jit(solution)/shard_map/ppermute | solution.py:429
  52.2 1.2 %collective-permute-done.16.refs_2_ = bf16[48,768]{1,0:T(8,128)(2,1)S(1)} collective-permute-done((bf16[48,768]{1,0:T(8,128)(2,1)S(1)}, bf16[48,768]{1,0:T(8,128)(2,1)S(1)}, u32[]{:S(2)}, u32[]{:S(2)}) %collective-permute-start.16) | collective-permute-done | bytes 73760 | tf_op jit(solution)/shard_map/ppermute | solution.py:429
  53.4 0.3 collective-permute-done.17.refs_3_
  53.7 1.9 %collective-permute-start.18 = (bf16[2,48,768]{2,1,0:T(8,128)(2,1)S(1)}, bf16[2,48,768]{2,1,0:T(8,128)(2,1)S(1)}, u32[]{:S(2)}, u32[]{:S(2)}) collective-permute-start(bf16[2,48,768]{2,1,0:T(8,128)(2,1)S(1)} %get-tuple-element.70), channel_id=1, source_target_pairs={{0,1},{1,0},{2,3},{3,2},{4,5},{5,4},{6,7},{7,6},{8,9},{9,8},{10,11... | collective-permute-start | bytes 442376 | tf_op jit(solution)/shard_map/ppermute | solution.py:464
  55.6 3.3 %collective-permute-done.18.arrived = bf16[2,48,768]{2,1,0:T(8,128)(2,1)S(1)} collective-permute-done((bf16[2,48,768]{2,1,0:T(8,128)(2,1)S(1)}, bf16[2,48,768]{2,1,0:T(8,128)(2,1)S(1)}, u32[]{:S(2)}, u32[]{:S(2)}) %collective-permute-start.18) | collective-permute-done | bytes 147488 | tf_op jit(solution)/shard_map/ppermute | solution.py:464
  58.9 0.7 %shard_map.92 = bf16[48,1536]{1,0:T(8,128)(2,1)} custom-call(bf16[2,48,768]{2,1,0:T(8,128)(2,1)S(1)} %get-tuple-element.69.kept, bf16[2,48,768]{2,1,0:T(8,128)(2,1)S(1)} %collective-permute-done.18.arrived, f32[1,1536]{1,0:T(1,128)S(1)} %reshape.6.bias, f32[1,1536]{1,0:T(1,128)S(1)} %reshape.7.gate), custom_call_target="tpu_custom_call" | custom-call | flops 221184 | bytes 294912 | tf_op jit(solution)/shard_map/pallas_call | solution.py:410
  (28 shorter events, 1.1 us)
Async XLA Ops:
  0.0 18.1 %collective-permute-start.3 = (bf16[192,1536]{1,0:T(8,128)(2,1)}, bf16[192,1536]{1,0:T(8,128)(2,1)S(1)}, u32[]{:S(2)}, u32[]{:S(2)}) collective-permute-start(bf16[192,1536]{1,0:T(8,128)(2,1)} %bitcast.2), channel_id=1, source_target_pairs={{0,4},{2,6},{4,0},{6,2},{8,12},{10,14},{12,8},{14,10},{16,20},{18,... | collective-permute-start | bytes 1769480 | tf_op jit(solution)/shard_map/ppermute | solution.py:429
  5.3 11.6 %collective-permute-start = (bf16[3,48,384]{2,1,0:T(8,128)(2,1)}, bf16[3,48,384]{2,1,0:T(8,128)(2,1)S(1)}, u32[]{:S(2)}, u32[]{:S(2)}) collective-permute-start(bf16[3,48,384]{2,1,0:T(8,128)(2,1)} %get-tuple-element.39), channel_id=1, source_target_pairs={{0,16},{2,18},{4,20},{6,22},{8,24},{10,26},{12,28},{14,30},{16,0},... | collective-permute-start | bytes 331784 | tf_op jit(solution)/shard_map/ppermute | solution.py:429
  7.9 8.9 %collective-permute-start.1 = (bf16[3,48,384]{2,1,0:T(8,128)(2,1)}, bf16[3,48,384]{2,1,0:T(8,128)(2,1)S(1)}, u32[]{:S(2)}, u32[]{:S(2)}) collective-permute-start(bf16[3,48,384]{2,1,0:T(8,128)(2,1)} %get-tuple-element.40), channel_id=1, source_target_pairs={{0,24},{2,26},{4,28},{6,30},{8,16},{10,18},{12,20},{14,22},{16,8},... | collective-permute-start | bytes 331784 | tf_op jit(solution)/shard_map/ppermute | solution.py:429
  9.3 7.7 %collective-permute-start.2 = (bf16[3,48,384]{2,1,0:T(8,128)(2,1)}, bf16[3,48,384]{2,1,0:T(8,128)(2,1)S(1)}, u32[]{:S(2)}, u32[]{:S(2)}) collective-permute-start(bf16[3,48,384]{2,1,0:T(8,128)(2,1)} %get-tuple-element.41), channel_id=1, source_target_pairs={{0,8},{2,10},{4,12},{6,14},{8,0},{10,2},{12,4},{14,6},{16,24},{18,... | collective-permute-start | bytes 331784 | tf_op jit(solution)/shard_map/ppermute | solution.py:429
  9.5 7.5 %copy-start.1 = (bf16[3,48,384]{2,1,0:T(8,128)(2,1)S(1)}, bf16[3,48,384]{2,1,0:T(8,128)(2,1)}, u32[]{:S(2)}) copy-start(bf16[3,48,384]{2,1,0:T(8,128)(2,1)} %get-tuple-element.38.refs_0_) | copy-start | bytes 331780
  9.5 8.6 %collective-permute-start.4 = (bf16[2,48,384]{2,1,0:T(8,128)(2,1)}, bf16[2,48,384]{2,1,0:T(8,128)(2,1)S(1)}, u32[]{:S(2)}, u32[]{:S(2)}) collective-permute-start(bf16[2,48,384]{2,1,0:T(8,128)(2,1)} %get-tuple-element.45), channel_id=1, source_target_pairs={{0,4},{2,6},{4,0},{6,2},{8,12},{10,14},{12,8},{14,10},{16,20},{18,... | collective-permute-start | bytes 221192 | tf_op jit(solution)/shard_map/ppermute | solution.py:429
  11.7 15.8 %copy-start = (bf16[1536,192]{0,1:T(8,128)(2,1)S(1)}, bf16[1536,192]{0,1:T(8,128)(2,1)}, u32[]{:S(2)}) copy-start(bf16[1536,192]{0,1:T(8,128)(2,1)} %param.13) | copy-start | bytes 1769476
  18.1 1.8 %collective-permute-start.6 = (bf16[4,2,48,384]{3,2,1,0:T(8,128)(2,1)S(1)}, bf16[4,2,48,384]{3,2,1,0:T(8,128)(2,1)S(1)}, u32[]{:S(2)}, u32[]{:S(2)}) collective-permute-start(bf16[4,2,48,384]{3,2,1,0:T(8,128)(2,1)S(1)} %get-tuple-element.50.every), channel_id=1, source_target_pairs={{0,2},{2,0},{4,6},{6,4},{8,10},{10,8},{12,14},{14,12},{16,18},{18,... | collective-permute-start | bytes 884744 | tf_op jit(solution)/shard_map/ppermute | solution.py:429
  18.1 7.8 %collective-permute-start.5 = (bf16[3,2,48,384]{3,2,1,0:T(8,128)(2,1)S(1)}, bf16[3,2,48,384]{3,2,1,0:T(8,128)(2,1)S(1)}, u32[]{:S(2)}, u32[]{:S(2)}) collective-permute-start(bf16[3,2,48,384]{3,2,1,0:T(8,128)(2,1)S(1)} %get-tuple-element.49), channel_id=1, source_target_pairs={{0,4},{2,6},{4,0},{6,2},{8,12},{10,14},{12,8},{14,10},{16,20},{18,... | collective-permute-start | bytes 663560 | tf_op jit(solution)/shard_map/ppermute | solution.py:429
  25.9 1.6 %collective-permute-start.8 = (bf16[3,2,48,384]{3,2,1,0:T(8,128)(2,1)S(1)}, bf16[3,2,48,384]{3,2,1,0:T(8,128)(2,1)S(1)}, u32[]{:S(2)}, u32[]{:S(2)}) collective-permute-start(bf16[3,2,48,384]{3,2,1,0:T(8,128)(2,1)S(1)} %collective-permute-done.5.some_far), channel_id=1, source_target_pairs={{0,2},{2,0},{4,6},{6,4},{8,10},{10,8},{12,14},{14,12},{16,18},{18,... | collective-permute-start | bytes 663560 | tf_op jit(solution)/shard_map/ppermute | solution.py:429
  25.9 1.6 %collective-permute-start.7 = (bf16[2,48,384]{2,1,0:T(8,128)(2,1)S(1)}, bf16[2,48,384]{2,1,0:T(8,128)(2,1)S(1)}, u32[]{:S(2)}, u32[]{:S(2)}) collective-permute-start(bf16[2,48,384]{2,1,0:T(8,128)(2,1)S(1)} %collective-permute-done.4.own_far), channel_id=1, source_target_pairs={{0,2},{2,0},{4,6},{6,4},{8,10},{10,8},{12,14},{14,12},{16,18},{18,... | collective-permute-start | bytes 221192 | tf_op jit(solution)/shard_map/ppermute | solution.py:429
  27.5 13.2 %collective-permute-start.11 = (bf16[192,1536]{1,0:T(8,128)(2,1)S(1)}, bf16[192,1536]{1,0:T(8,128)(2,1)S(1)}, u32[]{:S(2)}, u32[]{:S(2)}) collective-permute-start(bf16[192,1536]{1,0:T(8,128)(2,1)S(1)} %bitcast.3), channel_id=1, source_target_pairs={{0,2},{2,0},{4,6},{6,4},{8,10},{10,8},{12,14},{14,12},{16,18},{18,... | collective-permute-start | bytes 1769480 | tf_op jit(solution)/shard_map/ppermute | solution.py:429
  27.7 13.0 %collective-permute-start.12 = (bf16[192,1536]{1,0:T(8,128)(2,1)S(1)}, bf16[192,1536]{1,0:T(8,128)(2,1)S(1)}, u32[]{:S(2)}, u32[]{:S(2)}) collective-permute-start(bf16[192,1536]{1,0:T(8,128)(2,1)S(1)} %collective-permute-done.3.refs_2_), channel_id=1, source_target_pairs={{0,2},{2,0},{4,6},{6,4},{8,10},{10,8},{12,14},{14,12},{16,18},{18,... | collective-permute-start | bytes 1769480 | tf_op jit(solution)/shard_map/ppermute | solution.py:429
  29.1 10.9 %collective-permute-start.9 = (bf16[192,384]{1,0:T(8,128)(2,1)S(1)}, bf16[192,384]{1,0:T(8,128)(2,1)S(1)}, u32[]{:S(2)}, u32[]{:S(2)}) collective-permute-start(bf16[192,384]{1,0:T(8,128)(2,1)S(1)} %get-tuple-element.59.own), channel_id=1, source_target_pairs={{0,16},{2,18},{4,20},{6,22},{8,24},{10,26},{12,28},{14,30},{16,0},... | collective-permute-start | bytes 442376 | tf_op jit(solution)/shard_map/ppermute | solution.py:429
  32.0 8.9 %collective-permute-start.10 = (bf16[192,384]{1,0:T(8,128)(2,1)S(1)}, bf16[192,384]{1,0:T(8,128)(2,1)S(1)}, u32[]{:S(2)}, u32[]{:S(2)}) collective-permute-start(bf16[192,384]{1,0:T(8,128)(2,1)S(1)} %get-tuple-element.59.own), channel_id=1, source_target_pairs={{0,8},{2,10},{4,12},{6,14},{8,0},{10,2},{12,4},{14,6},{16,24},{18,... | collective-permute-start | bytes 442376 | tf_op jit(solution)/shard_map/ppermute | solution.py:429
  33.6 9.2 %collective-permute-start.13 = (bf16[192,256]{1,0:T(8,128)(2,1)S(1)}, bf16[192,256]{1,0:T(8,128)(2,1)S(1)}, u32[]{:S(2)}, u32[]{:S(2)}) collective-permute-start(bf16[192,256]{1,0:T(8,128)(2,1)S(1)} %get-tuple-element.64), channel_id=1, source_target_pairs={{0,24},{2,26},{4,28},{6,30},{8,16},{10,18},{12,20},{14,22},{16,8},... | collective-permute-start | bytes 294920 | tf_op jit(solution)/shard_map/ppermute | solution.py:429
  40.1 4.1 %collective-permute-start.14 = (bf16[192,128]{1,0:T(8,128)(2,1)S(1)}, bf16[192,128]{1,0:T(8,128)(2,1)S(1)}, u32[]{:S(2)}, u32[]{:S(2)}) collective-permute-start(bf16[192,128]{1,0:T(8,128)(2,1)S(1)} %slice.4), channel_id=1, source_target_pairs={{0,8},{2,10},{4,12},{6,14},{8,0},{10,2},{12,4},{14,6},{16,24},{18,... | collective-permute-start | bytes 147464 | tf_op jit(solution)/shard_map/ppermute | solution.py:429
  40.9 14.7 %copy-start.2 = (f32[1536]{0:T(1024)S(1)}, f32[1536]{0:T(1024)}, u32[]{:S(2)}) copy-start(f32[1536]{0:T(1024)} %param.14) | copy-start | bytes 18436
  40.9 14.7 %copy-start.3 = (f32[1536]{0:T(1024)S(1)}, f32[1536]{0:T(1024)}, u32[]{:S(2)}) copy-start(f32[1536]{0:T(1024)} %param.15) | copy-start | bytes 18436
  44.5 7.7 %collective-permute-start.15 = (bf16[48,768]{1,0:T(8,128)(2,1)S(1)}, bf16[48,768]{1,0:T(8,128)(2,1)S(1)}, u32[]{:S(2)}, u32[]{:S(2)}) collective-permute-start(bf16[48,768]{1,0:T(8,128)(2,1)S(1)} %get-tuple-element.66), channel_id=1, source_target_pairs={{0,16},{2,18},{4,20},{6,22},{8,24},{10,26},{12,28},{14,30},{16,0},... | collective-permute-start | bytes 221192 | tf_op jit(solution)/shard_map/ppermute | solution.py:429
  46.9 6.5 %collective-permute-start.16 = (bf16[48,768]{1,0:T(8,128)(2,1)S(1)}, bf16[48,768]{1,0:T(8,128)(2,1)S(1)}, u32[]{:S(2)}, u32[]{:S(2)}) collective-permute-start(bf16[48,768]{1,0:T(8,128)(2,1)S(1)} %get-tuple-element.67), channel_id=1, source_target_pairs={{0,24},{2,26},{4,28},{6,30},{8,16},{10,18},{12,20},{14,22},{16,8},... | collective-permute-start | bytes 221192 | tf_op jit(solution)/shard_map/ppermute | solution.py:429
  48.4 5.3 %collective-permute-start.17 = (bf16[48,768]{1,0:T(8,128)(2,1)S(1)}, bf16[48,768]{1,0:T(8,128)(2,1)S(1)}, u32[]{:S(2)}, u32[]{:S(2)}) collective-permute-start(bf16[48,768]{1,0:T(8,128)(2,1)S(1)} %get-tuple-element.68), channel_id=1, source_target_pairs={{0,8},{2,10},{4,12},{6,14},{8,0},{10,2},{12,4},{14,6},{16,24},{18,... | collective-permute-start | bytes 221192 | tf_op jit(solution)/shard_map/ppermute | solution.py:429
  53.7 5.2 %collective-permute-start.18 = (bf16[2,48,768]{2,1,0:T(8,128)(2,1)S(1)}, bf16[2,48,768]{2,1,0:T(8,128)(2,1)S(1)}, u32[]{:S(2)}, u32[]{:S(2)}) collective-permute-start(bf16[2,48,768]{2,1,0:T(8,128)(2,1)S(1)} %get-tuple-element.70), channel_id=1, source_target_pairs={{0,1},{1,0},{2,3},{3,2},{4,5},{5,4},{6,7},{7,6},{8,9},{9,8},{10,11... | collective-permute-start | bytes 442376 | tf_op jit(solution)/shard_map/ppermute | solution.py:464

commit v16 on v15

--- a/solution.py
+++ b/solution.py
@@ -370,51 +370,58 @@
     )(partial, most, last, weight)
 
 
-def divide_kernel(*refs):
-    parts, (keep, send, held) = refs[:-3], refs[-3:]
-    group, _ = place()
-    half = lax.axis_index("head")
-    blocks = keep.shape[0]
-    for position, part in enumerate(parts):
-        held[jnp.bitwise_xor(group, TURNS[position])] = part[...]
-    for block in range(blocks):
-        keep[block] = held[half * blocks + block]
-        send[block] = held[(1 - half) * blocks + block]
-
-
-def divide(parts):
-    groups = len(parts)
-    shape = jax.ShapeDtypeStruct((groups // 2, *parts[0].shape), jnp.bfloat16)
+def at_home(group):
+    return group // TURNS[1] == lax.axis_index("head")
+
+
+def divide_kernel(far, near, keep, send):
+    group, _ = place()
+
+    @pl.when(at_home(group))
+    def _():
+        keep[...] = near[...]
+        send[...] = far[...]
+
+    @pl.when(jnp.logical_not(at_home(group)))
+    def _():
+        keep[...] = far[...]
+        send[...] = near[...]
+
+
+def divide(far, near):
     return pl.pallas_call(
         divide_kernel,
-        out_shape=[shape] * 2,
-        in_specs=[VMEM] * groups,
+        out_shape=[jax.ShapeDtypeStruct(near.shape, near.dtype)] * 2,
+        in_specs=[VMEM] * 2,
         out_specs=[VMEM] * 2,
-        scratch_shapes=[pltpu.VMEM((groups, *parts[0].shape), jnp.bfloat16)],
-        compiler_params=pltpu.CompilerParams(vmem_limit_bytes=SMALL),
-        cost_estimate=pl.CostEstimate(flops=0, bytes_accessed=4 * groups * parts[0].size, transcendentals=0),
-    )(*parts)
-
-
-def finish_kernel(kept, arrived, bias, gate, out):
-    blocks, _, columns = kept.shape
-    for block in range(blocks):
+        compiler_params=pltpu.CompilerParams(vmem_limit_bytes=SMALL),
+        cost_estimate=pl.CostEstimate(flops=0, bytes_accessed=8 * near.size, transcendentals=0),
+    )(far, near)
+
+
+def finish_kernel(kept_even, arrived_even, kept_odd, arrived_odd, bias, gate, out, held):
+    group, _ = place()
+    columns = kept_even.shape[1]
+    side = lax.rem(group, 2)
+    held[side] = kept_even[...].astype(jnp.float32) + arrived_even[...].astype(jnp.float32)
+    held[1 - side] = kept_odd[...].astype(jnp.float32) + arrived_odd[...].astype(jnp.float32)
+    for block in range(2):
         cols = slice(block * columns, (block + 1) * columns)
-        total = kept[block].astype(jnp.float32) + arrived[block].astype(jnp.float32)
-        out[:, cols] = (gate[:, cols] * (total + bias[:, cols])).astype(jnp.bfloat16)
-
-
-def finish(kept, arrived, bias, gate):
-    blocks, rows, columns = kept.shape
-    width = blocks * columns
+        out[:, cols] = (gate[:, cols] * (held[block] + bias[:, cols])).astype(jnp.bfloat16)
+
+
+def finish(pieces, bias, gate):
+    rows, columns = pieces[0].shape
+    width = 2 * columns
     return pl.pallas_call(
         finish_kernel,
         out_shape=jax.ShapeDtypeStruct((rows, width), jnp.bfloat16),
-        in_specs=[VMEM] * 4,
+        in_specs=[VMEM] * (len(pieces) + 2),
         out_specs=VMEM,
+        scratch_shapes=[pltpu.VMEM((2, rows, columns), jnp.float32)],
         compiler_params=pltpu.CompilerParams(vmem_limit_bytes=SMALL),
         cost_estimate=pl.CostEstimate(flops=3 * rows * width, bytes_accessed=4 * rows * width, transcendentals=0),
-    )(kept, arrived, bias.reshape(1, width), gate.reshape(1, width))
+    )(*pieces, bias.reshape(1, width), gate.reshape(1, width))
 
 
 def after(value, *others):
@@ -460,9 +467,12 @@
     passed = swap(second[:, width - HD :], SPREAD)
     weight = order([weight, weight_near, weight_far, weight_corner])
     terms = close(groups, begin([attended, second, first], weight), third, passed, weight)
-    kept, sent = divide([terms[0], *along(terms)])
-    received = lax.ppermute(sent, "head", [(0, 1), (1, 0)])
-    return finish(kept, received, out_bias, out_gate)
+    second, third, first = along(terms)
+    pieces = []
+    for near, far in ((terms[0], second), (first, third)):
+        kept, sent = divide(far, near)
+        pieces += [kept, lax.ppermute(sent, "head", [(0, 1), (1, 0)])]
+    return finish(pieces, out_bias, out_gate)
 
 
 def solution(mesh):

time: 59.9 us -> 59.8 us (level)
  waiting for transfers between devices: 28.4 us -> 26.9 us
  starting transfers between devices: 21.8 us -> 23.2 us
    ppermute x18, waiting for transfers between devices: 25.1 us -> 23.6 us  [swap(): return lax.ppermute(value, 'patch', [(p, p ^ twist) for p in range(size)])]
    ppermute x1 -> x2, starting transfers between devices: 1.87 us -> 3.29 us  [grouped_body(): pieces += [kept, lax.ppermute(sent, 'head', [(0, 1), (1, 0)])]]
    ppermute x1 -> x2, waiting for transfers between devices: 3.3 us -> 3.22 us  [grouped_body(): pieces += [kept, lax.ppermute(sent, 'head', [(0, 1), (1, 0)])]]
  transfers between devices with their start and end apart: 19 -> 20, of which waited for: 12 -> 11; matrix products, arithmetic and copies ran while one was open for 0% -> 0% of each run, Pallas kernels for 14% -> 14%
where the time goes in v16:
time: 59.8 us; the launch traced here: 59.5 us
  waiting for transfers between devices  26.9 us (45%)
  starting transfers between devices  23.2 us (39%)
  Pallas kernels  9.27 us (16%)
    ppermute x18, waiting for transfers between devices, swap(): return lax.ppermute(value, 'patch', [(p, p ^ twist) for p in range(size)])  23.6 us
    ppermute x18, starting transfers between devices, swap(): return lax.ppermute(value, 'patch', [(p, p ^ twist) for p in range(size)])  19.9 us
    ppermute x2, starting transfers between devices, grouped_body(): pieces += [kept, lax.ppermute(sent, 'head', [(0, 1), (1, 0)])]  3.29 us
    ppermute x2, waiting for transfers between devices, grouped_body(): pieces += [kept, lax.ppermute(sent, 'head', [(0, 1), (1, 0)])]  3.22 us
    pallas_call x3, Pallas kernels, attend_call(): pl.pallas_call(kernel, out_shape=shapes, in_specs=[VMEM] * len(operands),...  3.19 us
    pallas_call x1, Pallas kernels, pack(): pl.pallas_call(pack_kernel, out_shape=[jax.ShapeDtypeStruct(shape, bf16)...  2.32 us
    pallas_call x1, Pallas kernels, pick(): pl.pallas_call(pick_kernel, out_shape=[jax.ShapeDtypeStruct((kinds, texts...  1.65 us
  transfers between devices with their start and end apart: 20, of which 11 were waited for; matrix products, arithmetic and copies ran while one was open for 0% of the time, Pallas kernels for 14%

profile of v16, /device:TPU:0, one launch (start us, length us, event | category | flops | bytes accessed | tf_op | source)
XLA Modules:
  0.0 59.5 jit_solution(17681222378253397720)
XLA Ops:
  0.0 2.9 %collective-permute-start.3 = (bf16[192,1536]{1,0:T(8,128)(2,1)}, bf16[192,1536]{1,0:T(8,128)(2,1)S(1)}, u32[]{:S(2)}, u32[]{:S(2)}) collective-permute-start(bf16[192,1536]{1,0:T(8,128)(2,1)} %bitcast.2), channel_id=1, source_target_pairs={{0,4},{2,6},{4,0},{6,2},{8,12},{10,14},{12,8},{14,10},{16,20},{18,... | collective-permute-start | bytes 1769480 | tf_op jit(solution)/shard_map/ppermute | solution.py:436
  2.9 2.3 %shard_map.82 = (bf16[3,48,384]{2,1,0:T(8,128)(2,1)}, bf16[3,48,384]{2,1,0:T(8,128)(2,1)}, bf16[3,48,384]{2,1,0:T(8,128)(2,1)}, bf16[3,48,384]{2,1,0:T(8,128)(2,1)}, bf16[2,48,384]{2,1,0:T(8,128)(2,1)}) custom-call(bf16[48,1536]{1,0:T(8,128)(2,1)} %queries_hbm.1, s32[2,48,1536]{2,1,0:T(8,128)} %codes_hbm.1, s32[12,2,48]{2,1,0:T(2,128)} %bitcast.5), custom_call_target="tpu_custom_call" | custom-call | flops 294912 | bytes 884736 | tf_op jit(solution)/shard_map/pallas_call | solution.py:110
  5.3 2.7 %collective-permute-start = (bf16[3,48,384]{2,1,0:T(8,128)(2,1)}, bf16[3,48,384]{2,1,0:T(8,128)(2,1)S(1)}, u32[]{:S(2)}, u32[]{:S(2)}) collective-permute-start(bf16[3,48,384]{2,1,0:T(8,128)(2,1)} %get-tuple-element.41), channel_id=1, source_target_pairs={{0,16},{2,18},{4,20},{6,22},{8,24},{10,26},{12,28},{14,30},{16,0},... | collective-permute-start | bytes 331784 | tf_op jit(solution)/shard_map/ppermute | solution.py:436
  7.9 1.3 %collective-permute-start.1 = (bf16[3,48,384]{2,1,0:T(8,128)(2,1)}, bf16[3,48,384]{2,1,0:T(8,128)(2,1)S(1)}, u32[]{:S(2)}, u32[]{:S(2)}) collective-permute-start(bf16[3,48,384]{2,1,0:T(8,128)(2,1)} %get-tuple-element.42), channel_id=1, source_target_pairs={{0,24},{2,26},{4,28},{6,30},{8,16},{10,18},{12,20},{14,22},{16,8},... | collective-permute-start | bytes 331784 | tf_op jit(solution)/shard_map/ppermute | solution.py:436
  9.5 0.5 collective-permute-start.4
  10.0 1.7 %shard_map.84 = (bf16[2,512,384]{2,1,0:T(8,128)(2,1)S(1)}, bf16[4,2,192,384]{3,2,1,0:T(8,128)(2,1)S(1)}) custom-call(bf16[2,512,1536]{2,1,0:T(8,128)(2,1)} %text_hbm.1, bf16[2,768,1536]{2,1,0:T(8,128)(2,1)} %stale_hbm.1), custom_call_target="tpu_custom_call" | custom-call | bytes 8388608 | tf_op jit(solution)/shard_map/pallas_call | solution.py:155
  11.7 5.1 %collective-permute-done.refs_1_ = bf16[3,48,384]{2,1,0:T(8,128)(2,1)S(1)} collective-permute-done((bf16[3,48,384]{2,1,0:T(8,128)(2,1)}, bf16[3,48,384]{2,1,0:T(8,128)(2,1)S(1)}, u32[]{:S(2)}, u32[]{:S(2)}) %collective-permute-start) | collective-permute-done | bytes 110624 | tf_op jit(solution)/shard_map/ppermute | solution.py:436
  17.0 1.0 %collective-permute-done.4.own_far = bf16[2,48,384]{2,1,0:T(8,128)(2,1)S(1)} collective-permute-done((bf16[2,48,384]{2,1,0:T(8,128)(2,1)}, bf16[2,48,384]{2,1,0:T(8,128)(2,1)S(1)}, u32[]{:S(2)}, u32[]{:S(2)}) %collective-permute-start.4) | collective-permute-done | bytes 73760 | tf_op jit(solution)/shard_map/ppermute | solution.py:436
  18.1 1.7 %collective-permute-start.5 = (bf16[3,2,48,384]{3,2,1,0:T(8,128)(2,1)S(1)}, bf16[3,2,48,384]{3,2,1,0:T(8,128)(2,1)S(1)}, u32[]{:S(2)}, u32[]{:S(2)}) collective-permute-start(bf16[3,2,48,384]{3,2,1,0:T(8,128)(2,1)S(1)} %get-tuple-element.51), channel_id=1, source_target_pairs={{0,4},{2,6},{4,0},{6,2},{8,12},{10,14},{12,8},{14,10},{16,20},{18,... | collective-permute-start | bytes 663560 | tf_op jit(solution)/shard_map/ppermute | solution.py:436
  19.8 1.2 %shard_map.85 = (f32[3,192,1]{2,1,0:T(8,128)S(1)}, f32[3,192,1]{2,1,0:T(8,128)S(1)}, f32[3,192,128]{2,1,0:T(8,128)S(1)}) custom-call(bf16[192,384]{1,0:T(8,128)(2,1)S(1)} %get-tuple-element.50.query, bf16[4,2,48,384]{3,2,1,0:T(8,128)(2,1)S(1)} %get-tuple-element.52.every, bf16[4,2,48,384]{3,2,1,0:T(8,128)(2,1)S(1)} %collective-permute-done.6.near, ...), custom_call_target="tpu_custom_call" | custom-call | flops 528482304 | bytes 2752512 | tf_op jit(solution)/shard_map/pallas_call | solution.py:281
  21.0 4.9 %collective-permute-done.5.some_far = bf16[3,2,48,384]{3,2,1,0:T(8,128)(2,1)S(1)} collective-permute-done((bf16[3,2,48,384]{3,2,1,0:T(8,128)(2,1)S(1)}, bf16[3,2,48,384]{3,2,1,0:T(8,128)(2,1)S(1)}, u32[]{:S(2)}, u32[]{:S(2)}) %collective-permute-start.5) | collective-permute-done | bytes 221216 | tf_op jit(solution)/shard_map/ppermute | solution.py:436
  25.9 0.5 collective-permute-start.7
  26.4 0.9 %shard_map.86 = (f32[3,192,1]{2,1,0:T(8,128)S(1)}, f32[3,192,1]{2,1,0:T(8,128)S(1)}, f32[3,192,128]{2,1,0:T(8,128)S(1)}) custom-call(bf16[192,384]{1,0:T(8,128)(2,1)S(1)} %get-tuple-element.50.query, bf16[2,48,384]{2,1,0:T(8,128)(2,1)S(1)} %collective-permute-done.4.own_far, bf16[3,2,48,384]{3,2,1,0:T(8,128)(2,1)S(1)} %collective-permute-done.5.some_far, ...), custom_call_target="tpu_custom_call" | custom-call | flops 113246208 | bytes 589824 | tf_op jit(solution)/shard_map/pallas_call | solution.py:281
  27.7 0.3 collective-permute-start.12
  28.0 1.1 %shard_map.87 = (bf16[192,384]{1,0:T(8,128)(2,1)S(1)}, bf16[192,256]{1,0:T(8,128)(2,1)S(1)}) custom-call(bf16[192,384]{1,0:T(8,128)(2,1)S(1)} %get-tuple-element.50.query, bf16[2,48,384]{2,1,0:T(8,128)(2,1)S(1)} %collective-permute-done.7.own_corner, bf16[3,2,48,384]{3,2,1,0:T(8,128)(2,1)S(1)} %collective-permute-done.8.some_corner, ...), custom_call_target="tpu_custom_call" | custom-call | flops 113246208 | bytes 589824 | tf_op jit(solution)/shard_map/pallas_call | solution.py:281
  29.1 2.9 %collective-permute-start.9 = (bf16[192,384]{1,0:T(8,128)(2,1)S(1)}, bf16[192,384]{1,0:T(8,128)(2,1)S(1)}, u32[]{:S(2)}, u32[]{:S(2)}) collective-permute-start(bf16[192,384]{1,0:T(8,128)(2,1)S(1)} %get-tuple-element.61.own), channel_id=1, source_target_pairs={{0,16},{2,18},{4,20},{6,22},{8,24},{10,26},{12,28},{14,30},{16,0},... | collective-permute-start | bytes 442376 | tf_op jit(solution)/shard_map/ppermute | solution.py:436
  32.0 1.6 %collective-permute-start.10 = (bf16[192,384]{1,0:T(8,128)(2,1)S(1)}, bf16[192,384]{1,0:T(8,128)(2,1)S(1)}, u32[]{:S(2)}, u32[]{:S(2)}) collective-permute-start(bf16[192,384]{1,0:T(8,128)(2,1)S(1)} %get-tuple-element.61.own), channel_id=1, source_target_pairs={{0,8},{2,10},{4,12},{6,14},{8,0},{10,2},{12,4},{14,6},{16,24},{18,... | collective-permute-start | bytes 442376 | tf_op jit(solution)/shard_map/ppermute | solution.py:436
  33.6 6.4 %collective-permute-done.9.second = bf16[192,384]{1,0:T(8,128)(2,1)S(1)} collective-permute-done((bf16[192,384]{1,0:T(8,128)(2,1)S(1)}, bf16[192,384]{1,0:T(8,128)(2,1)S(1)}, u32[]{:S(2)}, u32[]{:S(2)}) %collective-permute-start.9) | collective-permute-done | bytes 147488 | tf_op jit(solution)/shard_map/ppermute | solution.py:436
  40.1 0.6 %collective-permute-start.14 = (bf16[192,128]{1,0:T(8,128)(2,1)S(1)}, bf16[192,128]{1,0:T(8,128)(2,1)S(1)}, u32[]{:S(2)}, u32[]{:S(2)}) collective-permute-start(bf16[192,128]{1,0:T(8,128)(2,1)S(1)} %slice.4), channel_id=1, source_target_pairs={{0,8},{2,10},{4,12},{6,14},{8,0},{10,2},{12,4},{14,6},{16,24},{18,... | collective-permute-start | bytes 147464 | tf_op jit(solution)/shard_map/ppermute | solution.py:436
  40.9 0.7 %shard_map.89.partial = f32[192,768]{1,0:T(8,128)S(1)} custom-call(bf16[192,384]{1,0:T(8,128)(2,1)S(1)} %get-tuple-element.61.own, bf16[192,384]{1,0:T(8,128)(2,1)S(1)} %collective-permute-done.9.second, bf16[192,384]{1,0:T(8,128)(2,1)S(1)} %collective-permute-done.10.first, bf16[768,1536]{1,0:T(8,128)(2,1)S(1)} %shard_map.88.weight), custom_call_target="tpu_custom_call" | custom-call | flops 452984832 | bytes 589824 | tf_op jit(solution)/shard_map/pallas_call | solution.py:335
  41.6 1.1 %collective-permute-done.13.most = bf16[192,256]{1,0:T(8,128)(2,1)S(1)} collective-permute-done((bf16[192,256]{1,0:T(8,128)(2,1)S(1)}, bf16[192,256]{1,0:T(8,128)(2,1)S(1)}, u32[]{:S(2)}, u32[]{:S(2)}) %collective-permute-start.13) | collective-permute-done | bytes 98336 | tf_op jit(solution)/shard_map/ppermute | solution.py:436
  42.8 1.4 %collective-permute-done.14.last = bf16[192,128]{1,0:T(8,128)(2,1)S(1)} collective-permute-done((bf16[192,128]{1,0:T(8,128)(2,1)S(1)}, bf16[192,128]{1,0:T(8,128)(2,1)S(1)}, u32[]{:S(2)}, u32[]{:S(2)}) %collective-permute-start.14) | collective-permute-done | bytes 49184 | tf_op jit(solution)/shard_map/ppermute | solution.py:436
  44.1 0.4 shard_map.90
  44.5 2.3 %collective-permute-start.15 = (bf16[48,768]{1,0:T(8,128)(2,1)S(1)}, bf16[48,768]{1,0:T(8,128)(2,1)S(1)}, u32[]{:S(2)}, u32[]{:S(2)}) collective-permute-start(bf16[48,768]{1,0:T(8,128)(2,1)S(1)} %get-tuple-element.67), channel_id=1, source_target_pairs={{0,16},{2,18},{4,20},{6,22},{8,24},{10,26},{12,28},{14,30},{16,0},... | collective-permute-start | bytes 221192 | tf_op jit(solution)/shard_map/ppermute | solution.py:436
  46.9 1.5 %collective-permute-start.17 = (bf16[48,768]{1,0:T(8,128)(2,1)S(1)}, bf16[48,768]{1,0:T(8,128)(2,1)S(1)}, u32[]{:S(2)}, u32[]{:S(2)}) collective-permute-start(bf16[48,768]{1,0:T(8,128)(2,1)S(1)} %get-tuple-element.71), channel_id=1, source_target_pairs={{0,24},{2,26},{4,28},{6,30},{8,16},{10,18},{12,20},{14,22},{16,8},... | collective-permute-start | bytes 221192 | tf_op jit(solution)/shard_map/ppermute | solution.py:436
  48.4 0.5 collective-permute-start.18
  48.9 3.3 %collective-permute-done.15.far = bf16[48,768]{1,0:T(8,128)(2,1)S(1)} collective-permute-done((bf16[48,768]{1,0:T(8,128)(2,1)S(1)}, bf16[48,768]{1,0:T(8,128)(2,1)S(1)}, u32[]{:S(2)}, u32[]{:S(2)}) %collective-permute-start.15) | collective-permute-done | bytes 73760 | tf_op jit(solution)/shard_map/ppermute | solution.py:436
  52.2 2.1 %collective-permute-start.16 = (bf16[48,768]{1,0:T(8,128)(2,1)S(1)}, bf16[48,768]{1,0:T(8,128)(2,1)S(1)}, u32[]{:S(2)}, u32[]{:S(2)}) collective-permute-start(bf16[48,768]{1,0:T(8,128)(2,1)S(1)} %get-tuple-element.70), channel_id=1, source_target_pairs={{0,1},{1,0},{2,3},{3,2},{4,5},{5,4},{6,7},{7,6},{8,9},{9,8},{10,11... | collective-permute-start | bytes 221192 | tf_op jit(solution)/shard_map/ppermute | solution.py:474
  54.4 1.2 %collective-permute-start.19 = (bf16[48,768]{1,0:T(8,128)(2,1)S(1)}, bf16[48,768]{1,0:T(8,128)(2,1)S(1)}, u32[]{:S(2)}, u32[]{:S(2)}) collective-permute-start(bf16[48,768]{1,0:T(8,128)(2,1)S(1)} %get-tuple-element.74), channel_id=1, source_target_pairs={{0,1},{1,0},{2,3},{3,2},{4,5},{5,4},{6,7},{7,6},{8,9},{9,8},{10,11... | collective-permute-start | bytes 221192 | tf_op jit(solution)/shard_map/ppermute | solution.py:474
  55.6 1.1 %collective-permute-done.16.arrived_even = bf16[48,768]{1,0:T(8,128)(2,1)S(1)} collective-permute-done((bf16[48,768]{1,0:T(8,128)(2,1)S(1)}, bf16[48,768]{1,0:T(8,128)(2,1)S(1)}, u32[]{:S(2)}, u32[]{:S(2)}) %collective-permute-start.16) | collective-permute-done | bytes 73760 | tf_op jit(solution)/shard_map/ppermute | solution.py:474
  56.7 2.1 %collective-permute-done.19.arrived_odd = bf16[48,768]{1,0:T(8,128)(2,1)S(1)} collective-permute-done((bf16[48,768]{1,0:T(8,128)(2,1)S(1)}, bf16[48,768]{1,0:T(8,128)(2,1)S(1)}, u32[]{:S(2)}, u32[]{:S(2)}) %collective-permute-start.19) | collective-permute-done | bytes 73760 | tf_op jit(solution)/shard_map/ppermute | solution.py:474
  58.8 0.7 %shard_map.93 = bf16[48,1536]{1,0:T(8,128)(2,1)} custom-call(bf16[48,768]{1,0:T(8,128)(2,1)S(1)} %get-tuple-element.69.kept_even, bf16[48,768]{1,0:T(8,128)(2,1)S(1)} %collective-permute-done.16.arrived_even, bf16[48,768]{1,0:T(8,128)(2,1)S(1)} %get-tuple-element.73.kept_odd, bf16[48,768]{1,0:T(8,128)(2,1)S(1)} %collective-permute-done.19.arrived_odd, ...), custom_call_target="tpu_custom_call" | custom-call | flops 221184 | bytes 294912 | tf_op jit(solution)/shard_map/pallas_call | solution.py:416
  (31 shorter events, 1.1 us)
Async XLA Ops:
  0.0 18.1 %collective-permute-start.3 = (bf16[192,1536]{1,0:T(8,128)(2,1)}, bf16[192,1536]{1,0:T(8,128)(2,1)S(1)}, u32[]{:S(2)}, u32[]{:S(2)}) collective-permute-start(bf16[192,1536]{1,0:T(8,128)(2,1)} %bitcast.2), channel_id=1, source_target_pairs={{0,4},{2,6},{4,0},{6,2},{8,12},{10,14},{12,8},{14,10},{16,20},{18,... | collective-permute-start | bytes 1769480 | tf_op jit(solution)/shard_map/ppermute | solution.py:436
  5.3 11.6 %collective-permute-start = (bf16[3,48,384]{2,1,0:T(8,128)(2,1)}, bf16[3,48,384]{2,1,0:T(8,128)(2,1)S(1)}, u32[]{:S(2)}, u32[]{:S(2)}) collective-permute-start(bf16[3,48,384]{2,1,0:T(8,128)(2,1)} %get-tuple-element.41), channel_id=1, source_target_pairs={{0,16},{2,18},{4,20},{6,22},{8,24},{10,26},{12,28},{14,30},{16,0},... | collective-permute-start | bytes 331784 | tf_op jit(solution)/shard_map/ppermute | solution.py:436
  7.9 8.9 %collective-permute-start.1 = (bf16[3,48,384]{2,1,0:T(8,128)(2,1)}, bf16[3,48,384]{2,1,0:T(8,128)(2,1)S(1)}, u32[]{:S(2)}, u32[]{:S(2)}) collective-permute-start(bf16[3,48,384]{2,1,0:T(8,128)(2,1)} %get-tuple-element.42), channel_id=1, source_target_pairs={{0,24},{2,26},{4,28},{6,30},{8,16},{10,18},{12,20},{14,22},{16,8},... | collective-permute-start | bytes 331784 | tf_op jit(solution)/shard_map/ppermute | solution.py:436
  9.3 7.7 %collective-permute-start.2 = (bf16[3,48,384]{2,1,0:T(8,128)(2,1)}, bf16[3,48,384]{2,1,0:T(8,128)(2,1)S(1)}, u32[]{:S(2)}, u32[]{:S(2)}) collective-permute-start(bf16[3,48,384]{2,1,0:T(8,128)(2,1)} %get-tuple-element.43), channel_id=1, source_target_pairs={{0,8},{2,10},{4,12},{6,14},{8,0},{10,2},{12,4},{14,6},{16,24},{18,... | collective-permute-start | bytes 331784 | tf_op jit(solution)/shard_map/ppermute | solution.py:436
  9.5 7.5 %copy-start.1 = (bf16[3,48,384]{2,1,0:T(8,128)(2,1)S(1)}, bf16[3,48,384]{2,1,0:T(8,128)(2,1)}, u32[]{:S(2)}) copy-start(bf16[3,48,384]{2,1,0:T(8,128)(2,1)} %get-tuple-element.40.refs_0_) | copy-start | bytes 331780
  9.5 8.6 %collective-permute-start.4 = (bf16[2,48,384]{2,1,0:T(8,128)(2,1)}, bf16[2,48,384]{2,1,0:T(8,128)(2,1)S(1)}, u32[]{:S(2)}, u32[]{:S(2)}) collective-permute-start(bf16[2,48,384]{2,1,0:T(8,128)(2,1)} %get-tuple-element.47), channel_id=1, source_target_pairs={{0,4},{2,6},{4,0},{6,2},{8,12},{10,14},{12,8},{14,10},{16,20},{18,... | collective-permute-start | bytes 221192 | tf_op jit(solution)/shard_map/ppermute | solution.py:436
  11.7 15.8 %copy-start = (bf16[1536,192]{0,1:T(8,128)(2,1)S(1)}, bf16[1536,192]{0,1:T(8,128)(2,1)}, u32[]{:S(2)}) copy-start(bf16[1536,192]{0,1:T(8,128)(2,1)} %param.13) | copy-start | bytes 1769476
  18.1 1.8 %collective-permute-start.6 = (bf16[4,2,48,384]{3,2,1,0:T(8,128)(2,1)S(1)}, bf16[4,2,48,384]{3,2,1,0:T(8,128)(2,1)S(1)}, u32[]{:S(2)}, u32[]{:S(2)}) collective-permute-start(bf16[4,2,48,384]{3,2,1,0:T(8,128)(2,1)S(1)} %get-tuple-element.52.every), channel_id=1, source_target_pairs={{0,2},{2,0},{4,6},{6,4},{8,10},{10,8},{12,14},{14,12},{16,18},{18,... | collective-permute-start | bytes 884744 | tf_op jit(solution)/shard_map/ppermute | solution.py:436
  18.1 7.8 %collective-permute-start.5 = (bf16[3,2,48,384]{3,2,1,0:T(8,128)(2,1)S(1)}, bf16[3,2,48,384]{3,2,1,0:T(8,128)(2,1)S(1)}, u32[]{:S(2)}, u32[]{:S(2)}) collective-permute-start(bf16[3,2,48,384]{3,2,1,0:T(8,128)(2,1)S(1)} %get-tuple-element.51), channel_id=1, source_target_pairs={{0,4},{2,6},{4,0},{6,2},{8,12},{10,14},{12,8},{14,10},{16,20},{18,... | collective-permute-start | bytes 663560 | tf_op jit(solution)/shard_map/ppermute | solution.py:436
  25.9 1.6 %collective-permute-start.8 = (bf16[3,2,48,384]{3,2,1,0:T(8,128)(2,1)S(1)}, bf16[3,2,48,384]{3,2,1,0:T(8,128)(2,1)S(1)}, u32[]{:S(2)}, u32[]{:S(2)}) collective-permute-start(bf16[3,2,48,384]{3,2,1,0:T(8,128)(2,1)S(1)} %collective-permute-done.5.some_far), channel_id=1, source_target_pairs={{0,2},{2,0},{4,6},{6,4},{8,10},{10,8},{12,14},{14,12},{16,18},{18,... | collective-permute-start | bytes 663560 | tf_op jit(solution)/shard_map/ppermute | solution.py:436
  25.9 1.6 %collective-permute-start.7 = (bf16[2,48,384]{2,1,0:T(8,128)(2,1)S(1)}, bf16[2,48,384]{2,1,0:T(8,128)(2,1)S(1)}, u32[]{:S(2)}, u32[]{:S(2)}) collective-permute-start(bf16[2,48,384]{2,1,0:T(8,128)(2,1)S(1)} %collective-permute-done.4.own_far), channel_id=1, source_target_pairs={{0,2},{2,0},{4,6},{6,4},{8,10},{10,8},{12,14},{14,12},{16,18},{18,... | collective-permute-start | bytes 221192 | tf_op jit(solution)/shard_map/ppermute | solution.py:436
  27.5 13.2 %collective-permute-start.11 = (bf16[192,1536]{1,0:T(8,128)(2,1)S(1)}, bf16[192,1536]{1,0:T(8,128)(2,1)S(1)}, u32[]{:S(2)}, u32[]{:S(2)}) collective-permute-start(bf16[192,1536]{1,0:T(8,128)(2,1)S(1)} %bitcast.3), channel_id=1, source_target_pairs={{0,2},{2,0},{4,6},{6,4},{8,10},{10,8},{12,14},{14,12},{16,18},{18,... | collective-permute-start | bytes 1769480 | tf_op jit(solution)/shard_map/ppermute | solution.py:436
  27.7 13.0 %collective-permute-start.12 = (bf16[192,1536]{1,0:T(8,128)(2,1)S(1)}, bf16[192,1536]{1,0:T(8,128)(2,1)S(1)}, u32[]{:S(2)}, u32[]{:S(2)}) collective-permute-start(bf16[192,1536]{1,0:T(8,128)(2,1)S(1)} %collective-permute-done.3.refs_2_), channel_id=1, source_target_pairs={{0,2},{2,0},{4,6},{6,4},{8,10},{10,8},{12,14},{14,12},{16,18},{18,... | collective-permute-start | bytes 1769480 | tf_op jit(solution)/shard_map/ppermute | solution.py:436
  29.1 10.9 %collective-permute-start.9 = (bf16[192,384]{1,0:T(8,128)(2,1)S(1)}, bf16[192,384]{1,0:T(8,128)(2,1)S(1)}, u32[]{:S(2)}, u32[]{:S(2)}) collective-permute-start(bf16[192,384]{1,0:T(8,128)(2,1)S(1)} %get-tuple-element.61.own), channel_id=1, source_target_pairs={{0,16},{2,18},{4,20},{6,22},{8,24},{10,26},{12,28},{14,30},{16,0},... | collective-permute-start | bytes 442376 | tf_op jit(solution)/shard_map/ppermute | solution.py:436
  32.0 8.9 %collective-permute-start.10 = (bf16[192,384]{1,0:T(8,128)(2,1)S(1)}, bf16[192,384]{1,0:T(8,128)(2,1)S(1)}, u32[]{:S(2)}, u32[]{:S(2)}) collective-permute-start(bf16[192,384]{1,0:T(8,128)(2,1)S(1)} %get-tuple-element.61.own), channel_id=1, source_target_pairs={{0,8},{2,10},{4,12},{6,14},{8,0},{10,2},{12,4},{14,6},{16,24},{18,... | collective-permute-start | bytes 442376 | tf_op jit(solution)/shard_map/ppermute | solution.py:436
  33.6 9.2 %collective-permute-start.13 = (bf16[192,256]{1,0:T(8,128)(2,1)S(1)}, bf16[192,256]{1,0:T(8,128)(2,1)S(1)}, u32[]{:S(2)}, u32[]{:S(2)}) collective-permute-start(bf16[192,256]{1,0:T(8,128)(2,1)S(1)} %get-tuple-element.66), channel_id=1, source_target_pairs={{0,24},{2,26},{4,28},{6,30},{8,16},{10,18},{12,20},{14,22},{16,8},... | collective-permute-start | bytes 294920 | tf_op jit(solution)/shard_map/ppermute | solution.py:436
  40.1 4.1 %collective-permute-start.14 = (bf16[192,128]{1,0:T(8,128)(2,1)S(1)}, bf16[192,128]{1,0:T(8,128)(2,1)S(1)}, u32[]{:S(2)}, u32[]{:S(2)}) collective-permute-start(bf16[192,128]{1,0:T(8,128)(2,1)S(1)} %slice.4), channel_id=1, source_target_pairs={{0,8},{2,10},{4,12},{6,14},{8,0},{10,2},{12,4},{14,6},{16,24},{18,... | collective-permute-start | bytes 147464 | tf_op jit(solution)/shard_map/ppermute | solution.py:436
  40.9 14.7 %copy-start.2 = (f32[1536]{0:T(1024)S(1)}, f32[1536]{0:T(1024)}, u32[]{:S(2)}) copy-start(f32[1536]{0:T(1024)} %param.14) | copy-start | bytes 18436
  40.9 14.7 %copy-start.3 = (f32[1536]{0:T(1024)S(1)}, f32[1536]{0:T(1024)}, u32[]{:S(2)}) copy-start(f32[1536]{0:T(1024)} %param.15) | copy-start | bytes 18436
  44.5 7.7 %collective-permute-start.15 = (bf16[48,768]{1,0:T(8,128)(2,1)S(1)}, bf16[48,768]{1,0:T(8,128)(2,1)S(1)}, u32[]{:S(2)}, u32[]{:S(2)}) collective-permute-start(bf16[48,768]{1,0:T(8,128)(2,1)S(1)} %get-tuple-element.67), channel_id=1, source_target_pairs={{0,16},{2,18},{4,20},{6,22},{8,24},{10,26},{12,28},{14,30},{16,0},... | collective-permute-start | bytes 221192 | tf_op jit(solution)/shard_map/ppermute | solution.py:436
  46.9 7.5 %collective-permute-start.17 = (bf16[48,768]{1,0:T(8,128)(2,1)S(1)}, bf16[48,768]{1,0:T(8,128)(2,1)S(1)}, u32[]{:S(2)}, u32[]{:S(2)}) collective-permute-start(bf16[48,768]{1,0:T(8,128)(2,1)S(1)} %get-tuple-element.71), channel_id=1, source_target_pairs={{0,24},{2,26},{4,28},{6,30},{8,16},{10,18},{12,20},{14,22},{16,8},... | collective-permute-start | bytes 221192 | tf_op jit(solution)/shard_map/ppermute | solution.py:436
  48.4 6.0 %collective-permute-start.18 = (bf16[48,768]{1,0:T(8,128)(2,1)S(1)}, bf16[48,768]{1,0:T(8,128)(2,1)S(1)}, u32[]{:S(2)}, u32[]{:S(2)}) collective-permute-start(bf16[48,768]{1,0:T(8,128)(2,1)S(1)} %get-tuple-element.72), channel_id=1, source_target_pairs={{0,8},{2,10},{4,12},{6,14},{8,0},{10,2},{12,4},{14,6},{16,24},{18,... | collective-permute-start | bytes 221192 | tf_op jit(solution)/shard_map/ppermute | solution.py:436
  52.2 4.5 %collective-permute-start.16 = (bf16[48,768]{1,0:T(8,128)(2,1)S(1)}, bf16[48,768]{1,0:T(8,128)(2,1)S(1)}, u32[]{:S(2)}, u32[]{:S(2)}) collective-permute-start(bf16[48,768]{1,0:T(8,128)(2,1)S(1)} %get-tuple-element.70), channel_id=1, source_target_pairs={{0,1},{1,0},{2,3},{3,2},{4,5},{5,4},{6,7},{7,6},{8,9},{9,8},{10,11... | collective-permute-start | bytes 221192 | tf_op jit(solution)/shard_map/ppermute | solution.py:474
  54.4 4.4 %collective-permute-start.19 = (bf16[48,768]{1,0:T(8,128)(2,1)S(1)}, bf16[48,768]{1,0:T(8,128)(2,1)S(1)}, u32[]{:S(2)}, u32[]{:S(2)}) collective-permute-start(bf16[48,768]{1,0:T(8,128)(2,1)S(1)} %get-tuple-element.74), channel_id=1, source_target_pairs={{0,1},{1,0},{2,3},{3,2},{4,5},{5,4},{6,7},{7,6},{8,9},{9,8},{10,11... | collective-permute-start | bytes 221192 | tf_op jit(solution)/shard_map/ppermute | solution.py:474

commit v17 on v16

--- a/solution.py
+++ b/solution.py
@@ -95,9 +95,14 @@
     copies[2].wait()
     for target in range(groups):
         held[target, kinds - 1] = queries[:, target * width : (target + 1) * width]
-    for turn in range(groups):
-        outs[turn][...] = held[jnp.bitwise_xor(group, turn)]
-    outs[groups][...] = held[group, 0 : kinds - 1]
+    writes = [
+        pltpu.make_async_copy(held.at[jnp.bitwise_xor(group, turn)], outs[turn], sems.at[3 + turn])
+        for turn in range(groups)
+    ]
+    for write in writes:
+        write.start()
+    for write in writes:
+        write.wait()
 
 
 def pack(groups, queries, codes, exponents):
@@ -106,18 +111,18 @@
     share = width // groups
     bf16 = jnp.bfloat16
     exponents = exponents.transpose(2, 0, 1)
-    shapes = [(kinds + 1, rows, share)] * groups + [(kinds, rows, share)]
+    shapes = [(kinds + 1, rows, share)] * groups
     outs = pl.pallas_call(
         pack_kernel,
         out_shape=[jax.ShapeDtypeStruct(shape, bf16) for shape in shapes],
         in_specs=[HBM] * 3,
-        out_specs=[VMEM] * len(shapes),
+        out_specs=[HBM] * len(shapes),
         scratch_shapes=[
             pltpu.VMEM(codes.shape, jnp.int32),
             pltpu.VMEM(queries.shape, bf16),
             pltpu.VMEM(exponents.shape, jnp.int32),
             pltpu.VMEM((groups, kinds + 1, rows, share), bf16),
-            pltpu.SemaphoreType.DMA((3,)),
+            pltpu.SemaphoreType.DMA((3 + groups,)),
         ],
         compiler_params=pltpu.CompilerParams(vmem_limit_bytes=PACK_LIMIT),
         cost_estimate=pl.CostEstimate(flops=2 * codes.size, bytes_accessed=6 * codes.size, transcendentals=0),
@@ -167,25 +172,23 @@
 
 
 def merge_kernel(*refs):
-    parts, (every, some, query) = refs[:-3], refs[-3:]
+    parts, (every, query) = refs[:-2], refs[-2:]
     groups, kinds, rows, _ = every.shape
     group, _ = place()
     for position, part in enumerate(parts):
         every[position] = part[0:kinds]
-        if position:
-            some[position - 1] = part[0:kinds]
         origin = jnp.bitwise_xor(group, TURNS[position])
         query[pl.ds(aligned(origin, rows), rows), :] = part[kinds]
 
 
 def merge(parts):
     kinds, rows, width = parts[0].shape
-    shapes = [(len(parts), kinds - 1, rows, width), (len(parts) - 1, kinds - 1, rows, width), (len(parts) * rows, width)]
+    shapes = [(len(parts), kinds - 1, rows, width), (len(parts) * rows, width)]
     return pl.pallas_call(
         merge_kernel,
         out_shape=[jax.ShapeDtypeStruct(shape, jnp.bfloat16) for shape in shapes],
         in_specs=[VMEM] * len(parts),
-        out_specs=[VMEM] * 3,
+        out_specs=[VMEM] * 2,
         compiler_params=pltpu.CompilerParams(vmem_limit_bytes=SMALL),
         cost_estimate=pl.CostEstimate(flops=0, bytes_accessed=4 * len(parts) * parts[0].size, transcendentals=0),
     )(*parts)
@@ -241,10 +244,6 @@
     return lambda kind, cols: part[:, kind, :, cols].reshape(-1, HD)
 
 
-def split_part(own, some):
-    return lambda kind, cols: jnp.concatenate([own[kind, :, cols], some[:, kind, :, cols].reshape(-1, HD)], axis=0)
-
-
 def near_kernel(query, every, near, text, stale, peak, total, mixed):
     heads = columns_of(query.shape[1])
     images = [image_segment(stale, 0, whole_part(every)), image_segment(stale, 1, whole_part(near))]
@@ -254,9 +253,9 @@
         peak[head], total[head], mixed[head] = state
 
 
-def middle_kernel(query, own_far, some_far, stale, peak_in, total_in, mixed_in, peak, total, mixed):
+def middle_kernel(query, far, stale, peak_in, total_in, mixed_in, peak, total, mixed):
     heads = columns_of(query.shape[1])
-    image = image_segment(stale, 2, split_part(own_far, some_far))
+    image = image_segment(stale, 2, whole_part(far))
     segments = [[image(cols)] for cols in heads]
     states = [(peak_in[head], total_in[head], mixed_in[head]) for head in range(len(heads))]
     states = absorb([query[:, cols] for cols in heads], segments, states)
@@ -264,9 +263,9 @@
         peak[head], total[head], mixed[head] = state
 
 
-def last_kernel(query, own_corner, some_corner, stale, peak, total, mixed, out, most):
+def last_kernel(query, corner, stale, peak, total, mixed, out, most):
     heads = columns_of(query.shape[1])
-    image = image_segment(stale, 3, split_part(own_corner, some_corner))
+    image = image_segment(stale, 3, whole_part(corner))
     states = [(peak[head], total[head], mixed[head]) for head in range(len(heads))]
     states = absorb([query[:, cols] for cols in heads], [[image(cols)] for cols in heads], states)
     for cols, (_, sums, mix) in zip(heads, states):
@@ -296,25 +295,41 @@
     return [jax.ShapeDtypeStruct((heads, tokens, size), jnp.float32) for size in (1, 1, HD)]
 
 
-def order_kernel(*refs):
-    pieces, out = refs[:-1], refs[-1]
+def stack_kernel(first, second, out):
+    out[0] = first[...]
+    out[1] = second[...]
+
+
+def stack(first, second):
+    return pl.pallas_call(
+        stack_kernel,
+        out_shape=jax.ShapeDtypeStruct((2, *first.shape), first.dtype),
+        in_specs=[VMEM] * 2,
+        out_specs=VMEM,
+        compiler_params=pltpu.CompilerParams(vmem_limit_bytes=SMALL),
+        cost_estimate=pl.CostEstimate(flops=0, bytes_accessed=8 * first.size, transcendentals=0),
+    )(first, second)
+
+
+def order_kernel(own, across, out):
     _, spot = place()
-    span = out.shape[0] // SPREAD
-    for twist, piece in enumerate(pieces):
-        out[pl.ds(aligned(jnp.bitwise_xor(spot, twist), span), span), :] = piece[...]
-
-
-def order(pieces):
-    span, depth = pieces[0].shape
-    shape = (SPREAD * span, depth)
+    span = own.shape[1]
+    for twist in range(SPREAD):
+        piece = (own, across)[twist % 2][twist // 2]
+        out[pl.ds(aligned(jnp.bitwise_xor(spot, twist), span), span), :] = piece
+
+
+def order(own, across):
+    count, span, depth = own.shape
+    shape = (2 * count * span, depth)
     return pl.pallas_call(
         order_kernel,
         out_shape=jax.ShapeDtypeStruct(shape, jnp.bfloat16),
-        in_specs=[VMEM] * len(pieces),
+        in_specs=[VMEM] * 2,
         out_specs=VMEM,
         compiler_params=pltpu.CompilerParams(vmem_limit_bytes=SMALL),
         cost_estimate=pl.CostEstimate(flops=0, bytes_accessed=4 * shape[0] * depth, transcendentals=0),
-    )(*pieces)
+    )(own, across)
 
 
 def term_of(part, weight, turn, width, skip=0):
@@ -440,32 +455,31 @@
 
     weight = out_weight.T
     weight_far = swap(weight, 2)
-    *packed, own = pack(groups, queries, codes, exponents)
+    packed = pack(groups, queries, codes, exponents)
     text, stale = pick(groups, text_kv, stale_kv)
 
-    every, some, query = merge([packed[0], *along(packed)])
-    own_far = swap(own, 2)
-
-    ready = (every, some, query, weight, weight_far, own_far, text, stale)
-    every, some, query, weight, weight_far = lax.optimization_barrier(ready)[:5]
-    near, some_far = swap(every, 1), swap(some, 2)
+    every, query = merge([packed[0], *along(packed)])
+
+    ready = (every, query, weight, weight_far, text, stale)
+    every, query, weight, weight_far = lax.optimization_barrier(ready)[:4]
+    far, near = swap(every, 2), swap(every, 1)
     share = stale.shape[2]
     operands = [query, every, near, text, stale]
     state = attend_call(near_kernel, operands, state_shapes(query), 2 * share + text.shape[1])
 
-    some_far, own_far = lax.optimization_barrier((some_far, own_far, *state))[:2]
-    own_corner, some_corner = swap(own_far, 1), swap(some_far, 1)
-    state = attend_call(middle_kernel, [query, own_far, some_far, stale, *state], state_shapes(query), share)
-    weight, weight_far = lax.optimization_barrier((weight, weight_far, own_corner, some_corner, *state))[:2]
-    weight_near, weight_corner = swap(weight, 1), swap(weight_far, 1)
-    operands = [query, own_corner, some_corner, stale, *state]
+    far, weight = lax.optimization_barrier((far, stack(weight, weight_far), *state))[:2]
+    corner = swap(far, 1)
+    state = attend_call(middle_kernel, [query, far, stale, *state], state_shapes(query), share)
+    weight = after(weight, corner, *state)
+    weight_across = swap(weight, 1)
+    operands = [query, corner, stale, *state]
     tokens, width = query.shape
     shapes = [jax.ShapeDtypeStruct((tokens, size), jnp.bfloat16) for size in (width, width - HD)]
     attended, most = attend_call(last_kernel, operands, shapes, share)
 
     second, first, third = (swap(value, turn * SPREAD) for turn, value in ((2, attended), (1, attended), (3, most)))
     passed = swap(second[:, width - HD :], SPREAD)
-    weight = order([weight, weight_near, weight_far, weight_corner])
+    weight = order(weight, weight_across)
     terms = close(groups, begin([attended, second, first], weight), third, passed, weight)
     second, third, first = along(terms)
     pieces = []

time: 59.8 us -> 61 us (1.020)
  waiting for transfers between devices: 26.9 us -> 31.7 us
  starting transfers between devices: 23.2 us -> 19.5 us
    ppermute x18 -> x15, waiting for transfers between devices: 23.6 us -> 27.9 us  [swap(): return lax.ppermute(value, 'patch', [(p, p ^ twist) for p in range(size)])]
    ppermute x18 -> x15, starting transfers between devices: 19.9 us -> 17.4 us  [swap(): return lax.ppermute(value, 'patch', [(p, p ^ twist) for p in range(size)])]
    ppermute x2, starting transfers between devices: 3.29 us -> 2.15 us  [grouped_body(): pieces += [kept, lax.ppermute(sent, 'head', [(0, 1), (1, 0)])]]
  transfers between devices with their start and end apart: 20 -> 17, of which waited for: 11 -> 11; matrix products, arithmetic and copies ran while one was open for 0% -> 0% of each run, Pallas kernels for 14% -> 13%
where the time goes in v17:
time: 61 us; the launch traced here: 60.8 us
  waiting for transfers between devices  31.7 us (52%)
  starting transfers between devices  19.5 us (32%)
  Pallas kernels  9.31 us (15%)
    ppermute x15, waiting for transfers between devices, swap(): return lax.ppermute(value, 'patch', [(p, p ^ twist) for p in range(size)])  27.9 us
    ppermute x15, starting transfers between devices, swap(): return lax.ppermute(value, 'patch', [(p, p ^ twist) for p in range(size)])  17.4 us
    ppermute x2, waiting for transfers between devices, grouped_body(): pieces += [kept, lax.ppermute(sent, 'head', [(0, 1), (1, 0)])]  3.81 us
    pallas_call x3, Pallas kernels, attend_call(): pl.pallas_call(kernel, out_shape=shapes, in_specs=[VMEM] * len(operands),...  3.19 us
    pallas_call x1, Pallas kernels, pack(): pl.pallas_call(pack_kernel, out_shape=[jax.ShapeDtypeStruct(shape, bf16)...  2.32 us
    ppermute x2, starting transfers between devices, grouped_body(): pieces += [kept, lax.ppermute(sent, 'head', [(0, 1), (1, 0)])]  2.15 us
    pallas_call x1, Pallas kernels, pick(): pl.pallas_call(pick_kernel, out_shape=[jax.ShapeDtypeStruct((kinds, texts...  1.65 us
  transfers between devices with their start and end apart: 17, of which 11 were waited for; matrix products, arithmetic and copies ran while one was open for 0% of the time, Pallas kernels for 13%

profile of v17, /device:TPU:0, one launch (start us, length us, event | category | flops | bytes accessed | tf_op | source)
XLA Modules:
  0.0 60.8 jit_solution(14707359680963946080)
XLA Ops:
  0.0 2.9 %collective-permute-start.3 = (bf16[192,1536]{1,0:T(8,128)(2,1)}, bf16[192,1536]{1,0:T(8,128)(2,1)S(1)}, u32[]{:S(2)}, u32[]{:S(2)}) collective-permute-start(bf16[192,1536]{1,0:T(8,128)(2,1)} %bitcast.2), channel_id=1, source_target_pairs={{0,4},{2,6},{4,0},{6,2},{8,12},{10,14},{12,8},{14,10},{16,20},{18,... | collective-permute-start | bytes 1769480 | tf_op jit(solution)/shard_map/ppermute | solution.py:451
  2.9 2.3 %shard_map.82 = (bf16[3,48,384]{2,1,0:T(8,128)(2,1)}, bf16[3,48,384]{2,1,0:T(8,128)(2,1)}, bf16[3,48,384]{2,1,0:T(8,128)(2,1)}, bf16[3,48,384]{2,1,0:T(8,128)(2,1)}) custom-call(bf16[48,1536]{1,0:T(8,128)(2,1)} %queries_hbm.1, s32[2,48,1536]{2,1,0:T(8,128)} %codes_hbm.1, s32[12,2,48]{2,1,0:T(2,128)} %bitcast.4), custom_call_target="tpu_custom_call" | custom-call | flops 294912 | bytes 884736 | tf_op jit(solution)/shard_map/pallas_call | solution.py:115
  5.3 2.7 %collective-permute-start = (bf16[3,48,384]{2,1,0:T(8,128)(2,1)}, bf16[3,48,384]{2,1,0:T(8,128)(2,1)S(1)}, u32[]{:S(2)}, u32[]{:S(2)}) collective-permute-start(bf16[3,48,384]{2,1,0:T(8,128)(2,1)} %get-tuple-element.37), channel_id=1, source_target_pairs={{0,16},{2,18},{4,20},{6,22},{8,24},{10,26},{12,28},{14,30},{16,0},... | collective-permute-start | bytes 331784 | tf_op jit(solution)/shard_map/ppermute | solution.py:451
  7.9 1.3 %collective-permute-start.1 = (bf16[3,48,384]{2,1,0:T(8,128)(2,1)}, bf16[3,48,384]{2,1,0:T(8,128)(2,1)S(1)}, u32[]{:S(2)}, u32[]{:S(2)}) collective-permute-start(bf16[3,48,384]{2,1,0:T(8,128)(2,1)} %get-tuple-element.38), channel_id=1, source_target_pairs={{0,24},{2,26},{4,28},{6,30},{8,16},{10,18},{12,20},{14,22},{16,8},... | collective-permute-start | bytes 331784 | tf_op jit(solution)/shard_map/ppermute | solution.py:451
  9.3 0.2 collective-permute-start.2
  9.5 1.7 %shard_map.84 = (bf16[2,512,384]{2,1,0:T(8,128)(2,1)S(1)}, bf16[4,2,192,384]{3,2,1,0:T(8,128)(2,1)S(1)}) custom-call(bf16[2,512,1536]{2,1,0:T(8,128)(2,1)} %text_hbm.1, bf16[2,768,1536]{2,1,0:T(8,128)(2,1)} %stale_hbm.1), custom_call_target="tpu_custom_call" | custom-call | bytes 8388608 | tf_op jit(solution)/shard_map/pallas_call | solution.py:160
  11.2 5.7 %collective-permute-done.refs_1_ = bf16[3,48,384]{2,1,0:T(8,128)(2,1)S(1)} collective-permute-done((bf16[3,48,384]{2,1,0:T(8,128)(2,1)}, bf16[3,48,384]{2,1,0:T(8,128)(2,1)S(1)}, u32[]{:S(2)}, u32[]{:S(2)}) %collective-permute-start) | collective-permute-done | bytes 110624 | tf_op jit(solution)/shard_map/ppermute | solution.py:451
  17.1 1.1 %collective-permute-start.4 = (bf16[4,2,48,384]{3,2,1,0:T(8,128)(2,1)S(1)}, bf16[4,2,48,384]{3,2,1,0:T(8,128)(2,1)S(1)}, u32[]{:S(2)}, u32[]{:S(2)}) collective-permute-start(bf16[4,2,48,384]{3,2,1,0:T(8,128)(2,1)S(1)} %get-tuple-element.45.every), channel_id=1, source_target_pairs={{0,4},{2,6},{4,0},{6,2},{8,12},{10,14},{12,8},{14,10},{16,20},{18,... | collective-permute-start | bytes 884744 | tf_op jit(solution)/shard_map/ppermute | solution.py:451
  18.3 0.4 collective-permute-done.5.near
  18.7 1.2 %shard_map.86 = (f32[3,192,1]{2,1,0:T(8,128)S(1)}, f32[3,192,1]{2,1,0:T(8,128)S(1)}, f32[3,192,128]{2,1,0:T(8,128)S(1)}) custom-call(bf16[192,384]{1,0:T(8,128)(2,1)S(1)} %get-tuple-element.44.query, bf16[4,2,48,384]{3,2,1,0:T(8,128)(2,1)S(1)} %get-tuple-element.45.every, bf16[4,2,48,384]{3,2,1,0:T(8,128)(2,1)S(1)} %collective-permute-done.5.near, ...), custom_call_target="tpu_custom_call" | custom-call | flops 528482304 | bytes 2752512 | tf_op jit(solution)/shard_map/pallas_call | solution.py:280
  19.9 6.7 %collective-permute-done.4.far = bf16[4,2,48,384]{3,2,1,0:T(8,128)(2,1)S(1)} collective-permute-done((bf16[4,2,48,384]{3,2,1,0:T(8,128)(2,1)S(1)}, bf16[4,2,48,384]{3,2,1,0:T(8,128)(2,1)S(1)}, u32[]{:S(2)}, u32[]{:S(2)}) %collective-permute-start.4) | collective-permute-done | bytes 294944 | tf_op jit(solution)/shard_map/ppermute | solution.py:451
  26.5 0.9 %shard_map.87 = (f32[3,192,1]{2,1,0:T(8,128)S(1)}, f32[3,192,1]{2,1,0:T(8,128)S(1)}, f32[3,192,128]{2,1,0:T(8,128)S(1)}) custom-call(bf16[192,384]{1,0:T(8,128)(2,1)S(1)} %get-tuple-element.44.query, bf16[4,2,48,384]{3,2,1,0:T(8,128)(2,1)S(1)} %collective-permute-done.4.far, bf16[4,2,192,384]{3,2,1,0:T(8,128)(2,1)S(1)} %get-tuple-element.43.stale, ...), custom_call_target="tpu_custom_call" | custom-call | flops 113246208 | bytes 589824 | tf_op jit(solution)/shard_map/pallas_call | solution.py:280
  27.4 0.7 %collective-permute-done.6.corner = bf16[4,2,48,384]{3,2,1,0:T(8,128)(2,1)S(1)} collective-permute-done((bf16[4,2,48,384]{3,2,1,0:T(8,128)(2,1)S(1)}, bf16[4,2,48,384]{3,2,1,0:T(8,128)(2,1)S(1)}, u32[]{:S(2)}, u32[]{:S(2)}) %collective-permute-start.6) | collective-permute-done | bytes 294944 | tf_op jit(solution)/shard_map/ppermute | solution.py:451
  28.3 1.1 %shard_map.88 = (bf16[192,384]{1,0:T(8,128)(2,1)S(1)}, bf16[192,256]{1,0:T(8,128)(2,1)S(1)}) custom-call(bf16[192,384]{1,0:T(8,128)(2,1)S(1)} %get-tuple-element.44.query, bf16[4,2,48,384]{3,2,1,0:T(8,128)(2,1)S(1)} %collective-permute-done.6.corner, bf16[4,2,192,384]{3,2,1,0:T(8,128)(2,1)S(1)} %get-tuple-element.43.stale, ...), custom_call_target="tpu_custom_call" | custom-call | flops 113246208 | bytes 589824 | tf_op jit(solution)/shard_map/pallas_call | solution.py:280
  29.4 3.8 %collective-permute-start.7 = (bf16[192,384]{1,0:T(8,128)(2,1)S(1)}, bf16[192,384]{1,0:T(8,128)(2,1)S(1)}, u32[]{:S(2)}, u32[]{:S(2)}) collective-permute-start(bf16[192,384]{1,0:T(8,128)(2,1)S(1)} %get-tuple-element.55.own), channel_id=1, source_target_pairs={{0,16},{2,18},{4,20},{6,22},{8,24},{10,26},{12,28},{14,30},{16,0},... | collective-permute-start | bytes 442376 | tf_op jit(solution)/shard_map/ppermute | solution.py:451
  33.1 0.3 collective-permute-start.8
  33.4 1.3 %collective-permute-start.10 = (bf16[192,256]{1,0:T(8,128)(2,1)S(1)}, bf16[192,256]{1,0:T(8,128)(2,1)S(1)}, u32[]{:S(2)}, u32[]{:S(2)}) collective-permute-start(bf16[192,256]{1,0:T(8,128)(2,1)S(1)} %get-tuple-element.58), channel_id=1, source_target_pairs={{0,24},{2,26},{4,28},{6,30},{8,16},{10,18},{12,20},{14,22},{16,8},... | collective-permute-start | bytes 294920 | tf_op jit(solution)/shard_map/ppermute | solution.py:451
  34.7 6.9 %collective-permute-done.7.second = bf16[192,384]{1,0:T(8,128)(2,1)S(1)} collective-permute-done((bf16[192,384]{1,0:T(8,128)(2,1)S(1)}, bf16[192,384]{1,0:T(8,128)(2,1)S(1)}, u32[]{:S(2)}, u32[]{:S(2)}) %collective-permute-start.7) | collective-permute-done | bytes 147488 | tf_op jit(solution)/shard_map/ppermute | solution.py:451
  41.6 0.2 shard_map.89.weight
  41.8 2.6 %collective-permute-done.8.first = bf16[192,384]{1,0:T(8,128)(2,1)S(1)} collective-permute-done((bf16[192,384]{1,0:T(8,128)(2,1)S(1)}, bf16[192,384]{1,0:T(8,128)(2,1)S(1)}, u32[]{:S(2)}, u32[]{:S(2)}) %collective-permute-start.8) | collective-permute-done | bytes 147488 | tf_op jit(solution)/shard_map/ppermute | solution.py:451
  44.4 0.7 %shard_map.90.partial = f32[192,768]{1,0:T(8,128)S(1)} custom-call(bf16[192,384]{1,0:T(8,128)(2,1)S(1)} %get-tuple-element.55.own, bf16[192,384]{1,0:T(8,128)(2,1)S(1)} %collective-permute-done.7.second, bf16[192,384]{1,0:T(8,128)(2,1)S(1)} %collective-permute-done.8.first, bf16[768,1536]{1,0:T(8,128)(2,1)S(1)} %shard_map.89.weight), custom_call_target="tpu_custom_call" | custom-call | flops 452984832 | bytes 589824 | tf_op jit(solution)/shard_map/pallas_call | solution.py:350
  45.2 0.5 collective-permute-done.11.last
  45.7 0.4 shard_map.91
  46.1 0.8 %collective-permute-start.12 = (bf16[48,768]{1,0:T(8,128)(2,1)S(1)}, bf16[48,768]{1,0:T(8,128)(2,1)S(1)}, u32[]{:S(2)}, u32[]{:S(2)}) collective-permute-start(bf16[48,768]{1,0:T(8,128)(2,1)S(1)} %get-tuple-element.59), channel_id=1, source_target_pairs={{0,16},{2,18},{4,20},{6,22},{8,24},{10,26},{12,28},{14,30},{16,0},... | collective-permute-start | bytes 221192 | tf_op jit(solution)/shard_map/ppermute | solution.py:451
  46.9 1.7 %collective-permute-start.14 = (bf16[48,768]{1,0:T(8,128)(2,1)S(1)}, bf16[48,768]{1,0:T(8,128)(2,1)S(1)}, u32[]{:S(2)}, u32[]{:S(2)}) collective-permute-start(bf16[48,768]{1,0:T(8,128)(2,1)S(1)} %get-tuple-element.63), channel_id=1, source_target_pairs={{0,24},{2,26},{4,28},{6,30},{8,16},{10,18},{12,20},{14,22},{16,8},... | collective-permute-start | bytes 221192 | tf_op jit(solution)/shard_map/ppermute | solution.py:451
  48.5 1.1 %collective-permute-start.15 = (bf16[48,768]{1,0:T(8,128)(2,1)S(1)}, bf16[48,768]{1,0:T(8,128)(2,1)S(1)}, u32[]{:S(2)}, u32[]{:S(2)}) collective-permute-start(bf16[48,768]{1,0:T(8,128)(2,1)S(1)} %get-tuple-element.64), channel_id=1, source_target_pairs={{0,8},{2,10},{4,12},{6,14},{8,0},{10,2},{12,4},{14,6},{16,24},{18,... | collective-permute-start | bytes 221192 | tf_op jit(solution)/shard_map/ppermute | solution.py:451
  49.6 4.3 %collective-permute-done.12.far = bf16[48,768]{1,0:T(8,128)(2,1)S(1)} collective-permute-done((bf16[48,768]{1,0:T(8,128)(2,1)S(1)}, bf16[48,768]{1,0:T(8,128)(2,1)S(1)}, u32[]{:S(2)}, u32[]{:S(2)}) %collective-permute-start.12) | collective-permute-done | bytes 73760 | tf_op jit(solution)/shard_map/ppermute | solution.py:451
  54.0 1.6 %collective-permute-start.13 = (bf16[48,768]{1,0:T(8,128)(2,1)S(1)}, bf16[48,768]{1,0:T(8,128)(2,1)S(1)}, u32[]{:S(2)}, u32[]{:S(2)}) collective-permute-start(bf16[48,768]{1,0:T(8,128)(2,1)S(1)} %get-tuple-element.62), channel_id=1, source_target_pairs={{0,1},{1,0},{2,3},{3,2},{4,5},{5,4},{6,7},{7,6},{8,9},{9,8},{10,11... | collective-permute-start | bytes 221192 | tf_op jit(solution)/shard_map/ppermute | solution.py:488
  55.6 0.6 collective-permute-start.16
  56.2 2.2 %collective-permute-done.13.arrived_even = bf16[48,768]{1,0:T(8,128)(2,1)S(1)} collective-permute-done((bf16[48,768]{1,0:T(8,128)(2,1)S(1)}, bf16[48,768]{1,0:T(8,128)(2,1)S(1)}, u32[]{:S(2)}, u32[]{:S(2)}) %collective-permute-start.13) | collective-permute-done | bytes 73760 | tf_op jit(solution)/shard_map/ppermute | solution.py:488
  58.4 1.6 %collective-permute-done.16.arrived_odd = bf16[48,768]{1,0:T(8,128)(2,1)S(1)} collective-permute-done((bf16[48,768]{1,0:T(8,128)(2,1)S(1)}, bf16[48,768]{1,0:T(8,128)(2,1)S(1)}, u32[]{:S(2)}, u32[]{:S(2)}) %collective-permute-start.16) | collective-permute-done | bytes 73760 | tf_op jit(solution)/shard_map/ppermute | solution.py:488
  60.0 0.7 %shard_map.94 = bf16[48,1536]{1,0:T(8,128)(2,1)} custom-call(bf16[48,768]{1,0:T(8,128)(2,1)S(1)} %get-tuple-element.61.kept_even, bf16[48,768]{1,0:T(8,128)(2,1)S(1)} %collective-permute-done.13.arrived_even, bf16[48,768]{1,0:T(8,128)(2,1)S(1)} %get-tuple-element.65.kept_odd, bf16[48,768]{1,0:T(8,128)(2,1)S(1)} %collective-permute-done.16.arrived_odd, ...), custom_call_target="tpu_custom_call" | custom-call | flops 221184 | bytes 294912 | tf_op jit(solution)/shard_map/pallas_call | solution.py:431
  (26 shorter events, 0.5 us)
Async XLA Ops:
  0.0 17.0 %collective-permute-start.3 = (bf16[192,1536]{1,0:T(8,128)(2,1)}, bf16[192,1536]{1,0:T(8,128)(2,1)S(1)}, u32[]{:S(2)}, u32[]{:S(2)}) collective-permute-start(bf16[192,1536]{1,0:T(8,128)(2,1)} %bitcast.2), channel_id=1, source_target_pairs={{0,4},{2,6},{4,0},{6,2},{8,12},{10,14},{12,8},{14,10},{16,20},{18,... | collective-permute-start | bytes 1769480 | tf_op jit(solution)/shard_map/ppermute | solution.py:451
  5.3 11.6 %collective-permute-start = (bf16[3,48,384]{2,1,0:T(8,128)(2,1)}, bf16[3,48,384]{2,1,0:T(8,128)(2,1)S(1)}, u32[]{:S(2)}, u32[]{:S(2)}) collective-permute-start(bf16[3,48,384]{2,1,0:T(8,128)(2,1)} %get-tuple-element.37), channel_id=1, source_target_pairs={{0,16},{2,18},{4,20},{6,22},{8,24},{10,26},{12,28},{14,30},{16,0},... | collective-permute-start | bytes 331784 | tf_op jit(solution)/shard_map/ppermute | solution.py:451
  7.9 8.9 %collective-permute-start.1 = (bf16[3,48,384]{2,1,0:T(8,128)(2,1)}, bf16[3,48,384]{2,1,0:T(8,128)(2,1)S(1)}, u32[]{:S(2)}, u32[]{:S(2)}) collective-permute-start(bf16[3,48,384]{2,1,0:T(8,128)(2,1)} %get-tuple-element.38), channel_id=1, source_target_pairs={{0,24},{2,26},{4,28},{6,30},{8,16},{10,18},{12,20},{14,22},{16,8},... | collective-permute-start | bytes 331784 | tf_op jit(solution)/shard_map/ppermute | solution.py:451
  9.3 7.7 %copy-start.1 = (bf16[3,48,384]{2,1,0:T(8,128)(2,1)S(1)}, bf16[3,48,384]{2,1,0:T(8,128)(2,1)}, u32[]{:S(2)}) copy-start(bf16[3,48,384]{2,1,0:T(8,128)(2,1)} %get-tuple-element.36.refs_0_) | copy-start | bytes 331780
  9.3 9.0 %copy-start = (bf16[1536,192]{0,1:T(8,128)(2,1)S(1)}, bf16[1536,192]{0,1:T(8,128)(2,1)}, u32[]{:S(2)}) copy-start(bf16[1536,192]{0,1:T(8,128)(2,1)} %param.13) | copy-start | bytes 1769476
  9.3 7.7 %collective-permute-start.2 = (bf16[3,48,384]{2,1,0:T(8,128)(2,1)}, bf16[3,48,384]{2,1,0:T(8,128)(2,1)S(1)}, u32[]{:S(2)}, u32[]{:S(2)}) collective-permute-start(bf16[3,48,384]{2,1,0:T(8,128)(2,1)} %get-tuple-element.39), channel_id=1, source_target_pairs={{0,8},{2,10},{4,12},{6,14},{8,0},{10,2},{12,4},{14,6},{16,24},{18,... | collective-permute-start | bytes 331784 | tf_op jit(solution)/shard_map/ppermute | solution.py:451
  17.0 1.6 %collective-permute-start.5 = (bf16[4,2,48,384]{3,2,1,0:T(8,128)(2,1)S(1)}, bf16[4,2,48,384]{3,2,1,0:T(8,128)(2,1)S(1)}, u32[]{:S(2)}, u32[]{:S(2)}) collective-permute-start(bf16[4,2,48,384]{3,2,1,0:T(8,128)(2,1)S(1)} %get-tuple-element.45.every), channel_id=1, source_target_pairs={{0,2},{2,0},{4,6},{6,4},{8,10},{10,8},{12,14},{14,12},{16,18},{18,... | collective-permute-start | bytes 884744 | tf_op jit(solution)/shard_map/ppermute | solution.py:451
  17.1 9.4 %collective-permute-start.4 = (bf16[4,2,48,384]{3,2,1,0:T(8,128)(2,1)S(1)}, bf16[4,2,48,384]{3,2,1,0:T(8,128)(2,1)S(1)}, u32[]{:S(2)}, u32[]{:S(2)}) collective-permute-start(bf16[4,2,48,384]{3,2,1,0:T(8,128)(2,1)S(1)} %get-tuple-element.45.every), channel_id=1, source_target_pairs={{0,4},{2,6},{4,0},{6,2},{8,12},{10,14},{12,8},{14,10},{16,20},{18,... | collective-permute-start | bytes 884744 | tf_op jit(solution)/shard_map/ppermute | solution.py:451
  26.5 1.6 %collective-permute-start.6 = (bf16[4,2,48,384]{3,2,1,0:T(8,128)(2,1)S(1)}, bf16[4,2,48,384]{3,2,1,0:T(8,128)(2,1)S(1)}, u32[]{:S(2)}, u32[]{:S(2)}) collective-permute-start(bf16[4,2,48,384]{3,2,1,0:T(8,128)(2,1)S(1)} %collective-permute-done.4.far), channel_id=1, source_target_pairs={{0,2},{2,0},{4,6},{6,4},{8,10},{10,8},{12,14},{14,12},{16,18},{18,... | collective-permute-start | bytes 884744 | tf_op jit(solution)/shard_map/ppermute | solution.py:451
  28.1 13.5 %collective-permute-start.9 = (bf16[2,192,1536]{2,1,0:T(8,128)(2,1)S(1)}, bf16[2,192,1536]{2,1,0:T(8,128)(2,1)S(1)}, u32[]{:S(2)}, u32[]{:S(2)}) collective-permute-start(bf16[2,192,1536]{2,1,0:T(8,128)(2,1)S(1)} %shard_map.85.own), channel_id=1, source_target_pairs={{0,2},{2,0},{4,6},{6,4},{8,10},{10,8},{12,14},{14,12},{16,18},{18,... | collective-permute-start | bytes 3538952 | tf_op jit(solution)/shard_map/ppermute | solution.py:451
  29.4 12.2 %collective-permute-start.7 = (bf16[192,384]{1,0:T(8,128)(2,1)S(1)}, bf16[192,384]{1,0:T(8,128)(2,1)S(1)}, u32[]{:S(2)}, u32[]{:S(2)}) collective-permute-start(bf16[192,384]{1,0:T(8,128)(2,1)S(1)} %get-tuple-element.55.own), channel_id=1, source_target_pairs={{0,16},{2,18},{4,20},{6,22},{8,24},{10,26},{12,28},{14,30},{16,0},... | collective-permute-start | bytes 442376 | tf_op jit(solution)/shard_map/ppermute | solution.py:451
  33.1 11.3 %collective-permute-start.8 = (bf16[192,384]{1,0:T(8,128)(2,1)S(1)}, bf16[192,384]{1,0:T(8,128)(2,1)S(1)}, u32[]{:S(2)}, u32[]{:S(2)}) collective-permute-start(bf16[192,384]{1,0:T(8,128)(2,1)S(1)} %get-tuple-element.55.own), channel_id=1, source_target_pairs={{0,8},{2,10},{4,12},{6,14},{8,0},{10,2},{12,4},{14,6},{16,24},{18,... | collective-permute-start | bytes 442376 | tf_op jit(solution)/shard_map/ppermute | solution.py:451
  33.4 11.7 %collective-permute-start.10 = (bf16[192,256]{1,0:T(8,128)(2,1)S(1)}, bf16[192,256]{1,0:T(8,128)(2,1)S(1)}, u32[]{:S(2)}, u32[]{:S(2)}) collective-permute-start(bf16[192,256]{1,0:T(8,128)(2,1)S(1)} %get-tuple-element.58), channel_id=1, source_target_pairs={{0,24},{2,26},{4,28},{6,30},{8,16},{10,18},{12,20},{14,22},{16,8},... | collective-permute-start | bytes 294920 | tf_op jit(solution)/shard_map/ppermute | solution.py:451
  41.6 4.1 %collective-permute-start.11 = (bf16[192,128]{1,0:T(8,128)(2,1)S(1)}, bf16[192,128]{1,0:T(8,128)(2,1)S(1)}, u32[]{:S(2)}, u32[]{:S(2)}) collective-permute-start(bf16[192,128]{1,0:T(8,128)(2,1)S(1)} %slice.4), channel_id=1, source_target_pairs={{0,8},{2,10},{4,12},{6,14},{8,0},{10,2},{12,4},{14,6},{16,24},{18,... | collective-permute-start | bytes 147464 | tf_op jit(solution)/shard_map/ppermute | solution.py:451
  45.1 11.0 %copy-start.2 = (f32[1536]{0:T(1024)S(1)}, f32[1536]{0:T(1024)}, u32[]{:S(2)}) copy-start(f32[1536]{0:T(1024)} %param.14) | copy-start | bytes 18436
  45.1 11.0 %copy-start.3 = (f32[1536]{0:T(1024)S(1)}, f32[1536]{0:T(1024)}, u32[]{:S(2)}) copy-start(f32[1536]{0:T(1024)} %param.15) | copy-start | bytes 18436
  46.1 7.9 %collective-permute-start.12 = (bf16[48,768]{1,0:T(8,128)(2,1)S(1)}, bf16[48,768]{1,0:T(8,128)(2,1)S(1)}, u32[]{:S(2)}, u32[]{:S(2)}) collective-permute-start(bf16[48,768]{1,0:T(8,128)(2,1)S(1)} %get-tuple-element.59), channel_id=1, source_target_pairs={{0,16},{2,18},{4,20},{6,22},{8,24},{10,26},{12,28},{14,30},{16,0},... | collective-permute-start | bytes 221192 | tf_op jit(solution)/shard_map/ppermute | solution.py:451
  46.9 8.7 %collective-permute-start.14 = (bf16[48,768]{1,0:T(8,128)(2,1)S(1)}, bf16[48,768]{1,0:T(8,128)(2,1)S(1)}, u32[]{:S(2)}, u32[]{:S(2)}) collective-permute-start(bf16[48,768]{1,0:T(8,128)(2,1)S(1)} %get-tuple-element.63), channel_id=1, source_target_pairs={{0,24},{2,26},{4,28},{6,30},{8,16},{10,18},{12,20},{14,22},{16,8},... | collective-permute-start | bytes 221192 | tf_op jit(solution)/shard_map/ppermute | solution.py:451
  48.5 7.1 %collective-permute-start.15 = (bf16[48,768]{1,0:T(8,128)(2,1)S(1)}, bf16[48,768]{1,0:T(8,128)(2,1)S(1)}, u32[]{:S(2)}, u32[]{:S(2)}) collective-permute-start(bf16[48,768]{1,0:T(8,128)(2,1)S(1)} %get-tuple-element.64), channel_id=1, source_target_pairs={{0,8},{2,10},{4,12},{6,14},{8,0},{10,2},{12,4},{14,6},{16,24},{18,... | collective-permute-start | bytes 221192 | tf_op jit(solution)/shard_map/ppermute | solution.py:451
  54.0 4.4 %collective-permute-start.13 = (bf16[48,768]{1,0:T(8,128)(2,1)S(1)}, bf16[48,768]{1,0:T(8,128)(2,1)S(1)}, u32[]{:S(2)}, u32[]{:S(2)}) collective-permute-start(bf16[48,768]{1,0:T(8,128)(2,1)S(1)} %get-tuple-element.62), channel_id=1, source_target_pairs={{0,1},{1,0},{2,3},{3,2},{4,5},{5,4},{6,7},{7,6},{8,9},{9,8},{10,11... | collective-permute-start | bytes 221192 | tf_op jit(solution)/shard_map/ppermute | solution.py:488
  55.6 4.4 %collective-permute-start.16 = (bf16[48,768]{1,0:T(8,128)(2,1)S(1)}, bf16[48,768]{1,0:T(8,128)(2,1)S(1)}, u32[]{:S(2)}, u32[]{:S(2)}) collective-permute-start(bf16[48,768]{1,0:T(8,128)(2,1)S(1)} %get-tuple-element.66), channel_id=1, source_target_pairs={{0,1},{1,0},{2,3},{3,2},{4,5},{5,4},{6,7},{7,6},{8,9},{9,8},{10,11... | collective-permute-start | bytes 221192 | tf_op jit(solution)/shard_map/ppermute | solution.py:488

commit v18 on v16

--- a/solution.py
+++ b/solution.py
@@ -68,8 +68,8 @@
     return me // SPREAD, lax.rem(me, SPREAD)
 
 
-def pack_kernel(queries_hbm, codes_hbm, exponents_hbm, *rest):
-    outs, (codes, queries, exponents, held, sems) = rest[:-5], rest[-5:]
+def pack_kernel(queries_hbm, codes_hbm, exponents_hbm, weight_hbm, *rest):
+    outs, early, (codes, queries, exponents, held, sems) = rest[:-6], rest[-6], rest[-5:]
     groups, kinds, rows, width = held.shape
     group, _ = place()
     per = width // HD
@@ -77,6 +77,7 @@
         pltpu.make_async_copy(exponents_hbm, exponents, sems.at[0]),
         pltpu.make_async_copy(codes_hbm, codes, sems.at[1]),
         pltpu.make_async_copy(queries_hbm, queries, sems.at[2]),
+        pltpu.make_async_copy(weight_hbm.at[0 : early.shape[0]], early, sems.at[3]),
     ]
     for copy in copies:
         copy.start()
@@ -98,30 +99,31 @@
     for turn in range(groups):
         outs[turn][...] = held[jnp.bitwise_xor(group, turn)]
     outs[groups][...] = held[group, 0 : kinds - 1]
-
-
-def pack(groups, queries, codes, exponents):
+    copies[3].wait()
+
+
+def pack(groups, queries, codes, exponents, weight, cut):
     rows, width = queries.shape
     kinds = codes.shape[0]
     share = width // groups
     bf16 = jnp.bfloat16
     exponents = exponents.transpose(2, 0, 1)
-    shapes = [(kinds + 1, rows, share)] * groups + [(kinds, rows, share)]
+    shapes = [(kinds + 1, rows, share)] * groups + [(kinds, rows, share), (cut, weight.shape[1])]
     outs = pl.pallas_call(
         pack_kernel,
         out_shape=[jax.ShapeDtypeStruct(shape, bf16) for shape in shapes],
-        in_specs=[HBM] * 3,
+        in_specs=[HBM] * 4,
         out_specs=[VMEM] * len(shapes),
         scratch_shapes=[
             pltpu.VMEM(codes.shape, jnp.int32),
             pltpu.VMEM(queries.shape, bf16),
             pltpu.VMEM(exponents.shape, jnp.int32),
             pltpu.VMEM((groups, kinds + 1, rows, share), bf16),
-            pltpu.SemaphoreType.DMA((3,)),
+            pltpu.SemaphoreType.DMA((4,)),
         ],
         compiler_params=pltpu.CompilerParams(vmem_limit_bytes=PACK_LIMIT),
         cost_estimate=pl.CostEstimate(flops=2 * codes.size, bytes_accessed=6 * codes.size, transcendentals=0),
-    )(queries, codes, exponents)
+    )(queries, codes, exponents, weight)
     return outs
 
 
@@ -296,15 +298,16 @@
     return [jax.ShapeDtypeStruct((heads, tokens, size), jnp.float32) for size in (1, 1, HD)]
 
 
-def order_kernel(*refs):
-    pieces, out = refs[:-1], refs[-1]
+def order_kernel(weight, near, early, late, early_corner, late_corner, out):
     _, spot = place()
-    span = out.shape[0] // SPREAD
-    for twist, piece in enumerate(pieces):
-        out[pl.ds(aligned(jnp.bitwise_xor(spot, twist), span), span), :] = piece[...]
-
-
-def order(pieces):
+    span, cut = weight.shape[0], early.shape[0]
+    pieces = [(0, 0, weight), (1, 0, near), (2, 0, early), (2, cut, late), (3, 0, early_corner), (3, cut, late_corner)]
+    for twist, skip, piece in pieces:
+        start = jnp.bitwise_xor(spot, twist) * span + skip
+        out[pl.ds(pl.multiple_of(start, 16), piece.shape[0]), :] = piece[...]
+
+
+def order(*pieces):
     span, depth = pieces[0].shape
     shape = (SPREAD * span, depth)
     return pl.pallas_call(
@@ -439,33 +442,36 @@
         return [swap(values[turn], turn * SPREAD) for turn in TURNS[1:]]
 
     weight = out_weight.T
-    weight_far = swap(weight, 2)
-    *packed, own = pack(groups, queries, codes, exponents)
+    cut = weight.shape[0] - 16
+    *packed, own, early = pack(groups, queries, codes, exponents, weight, cut)
     text, stale = pick(groups, text_kv, stale_kv)
 
     every, some, query = merge([packed[0], *along(packed)])
-    own_far = swap(own, 2)
-
-    ready = (every, some, query, weight, weight_far, own_far, text, stale)
-    every, some, query, weight, weight_far = lax.optimization_barrier(ready)[:5]
+    own_far, early = swap(own, 2), swap(early, 2)
+
+    ready = (every, some, query, weight, early, own_far, text, stale)
+    every, some, query, weight, early = lax.optimization_barrier(ready)[:5]
     near, some_far = swap(every, 1), swap(some, 2)
     share = stale.shape[2]
     operands = [query, every, near, text, stale]
     state = attend_call(near_kernel, operands, state_shapes(query), 2 * share + text.shape[1])
 
-    some_far, own_far = lax.optimization_barrier((some_far, own_far, *state))[:2]
+    some_far, own_far, weight = lax.optimization_barrier((some_far, own_far, weight, *state))[:3]
+    late, late_corner = swap(weight[cut:], 2), swap(weight[cut:], 3)
     own_corner, some_corner = swap(own_far, 1), swap(some_far, 1)
     state = attend_call(middle_kernel, [query, own_far, some_far, stale, *state], state_shapes(query), share)
-    weight, weight_far = lax.optimization_barrier((weight, weight_far, own_corner, some_corner, *state))[:2]
-    weight_near, weight_corner = swap(weight, 1), swap(weight_far, 1)
+    weight, early = lax.optimization_barrier((weight, early, own_corner, some_corner, *state))[:2]
+    weight_near, early_corner = swap(weight, 1), swap(early, 1)
     operands = [query, own_corner, some_corner, stale, *state]
     tokens, width = query.shape
     shapes = [jax.ShapeDtypeStruct((tokens, size), jnp.bfloat16) for size in (width, width - HD)]
     attended, most = attend_call(last_kernel, operands, shapes, share)
 
-    second, first, third = (swap(value, turn * SPREAD) for turn, value in ((2, attended), (1, attended), (3, most)))
+    second, third = swap(attended, 2 * SPREAD), swap(most, 3 * SPREAD)
+    attended, late, late_corner = lax.optimization_barrier((attended, late, late_corner))
+    first = swap(attended, SPREAD)
     passed = swap(second[:, width - HD :], SPREAD)
-    weight = order([weight, weight_near, weight_far, weight_corner])
+    weight = order(weight, weight_near, early, late, early_corner, late_corner)
     terms = close(groups, begin([attended, second, first], weight), third, passed, weight)
     second, third, first = along(terms)
     pieces = []

time: 59.8 us -> 63.3 us (1.059)
  starting transfers between devices: 23.2 us -> 26.2 us
    ppermute x18 -> x20, starting transfers between devices: 19.9 us -> 23.8 us  [swap(): return lax.ppermute(value, 'patch', [(p, p ^ twist) for p in range(size)])]
    ppermute x2, starting transfers between devices: 3.29 us -> 2.39 us  [grouped_body(): pieces += [kept, lax.ppermute(sent, 'head', [(0, 1), (1, 0)])]]
    ppermute x18 -> x20, waiting for transfers between devices: 23.6 us -> 23.6 us  [swap(): return lax.ppermute(value, 'patch', [(p, p ^ twist) for p in range(size)])]
  transfers between devices with their start and end apart: 20 -> 22, of which waited for: 11 -> 12; matrix products, arithmetic and copies ran while one was open for 0% -> 0% of each run, Pallas kernels for 14% -> 9%
where the time goes in v18:
time: 63.3 us; the launch traced here: 63.1 us
  waiting for transfers between devices  27.2 us (43%)
  starting transfers between devices  26.2 us (41%)
  Pallas kernels  9.52 us (15%)
    ppermute x20, starting transfers between devices, swap(): return lax.ppermute(value, 'patch', [(p, p ^ twist) for p in range(size)])  23.8 us
    ppermute x20, waiting for transfers between devices, swap(): return lax.ppermute(value, 'patch', [(p, p ^ twist) for p in range(size)])  23.6 us
    ppermute x2, waiting for transfers between devices, grouped_body(): pieces += [kept, lax.ppermute(sent, 'head', [(0, 1), (1, 0)])]  3.58 us
    pallas_call x3, Pallas kernels, attend_call(): pl.pallas_call(kernel, out_shape=shapes, in_specs=[VMEM] * len(operands),...  3.2 us
    pallas_call x1, Pallas kernels, pack(): pl.pallas_call(pack_kernel, out_shape=[jax.ShapeDtypeStruct(shape, bf16)...  2.56 us
    ppermute x2, starting transfers between devices, grouped_body(): pieces += [kept, lax.ppermute(sent, 'head', [(0, 1), (1, 0)])]  2.39 us
    pallas_call x1, Pallas kernels, pick(): pl.pallas_call(pick_kernel, out_shape=[jax.ShapeDtypeStruct((kinds, texts...  1.65 us
  transfers between devices with their start and end apart: 22, of which 12 were waited for; matrix products, arithmetic and copies ran while one was open for 0% of the time, Pallas kernels for 9%

profile of v18, /device:TPU:0, one launch (start us, length us, event | category | flops | bytes accessed | tf_op | source)
XLA Modules:
  0.0 63.1 jit_solution(14974318504760108200)
XLA Ops:
  0.0 2.6 %shard_map.82 = (bf16[3,48,384]{2,1,0:T(8,128)(2,1)}, bf16[3,48,384]{2,1,0:T(8,128)(2,1)}, bf16[3,48,384]{2,1,0:T(8,128)(2,1)}, bf16[3,48,384]{2,1,0:T(8,128)(2,...) custom-call(bf16[48,1536]{1,0:T(8,128)(2,1)} %queries_hbm.1, s32[2,48,1536]{2,1,0:T(8,128)} %codes_hbm.1, ...), custom_call_target="tpu_custom_call" | custom-call | flops 294912 | bytes 884736 | tf_op jit(solution)/shard_map/pallas_call | solution.py:112
  2.6 3.0 %collective-permute-start.3 = (bf16[176,1536]{1,0:T(8,128)(2,1)}, bf16[176,1536]{1,0:T(8,128)(2,1)S(1)}, u32[]{:S(2)}, u32[]{:S(2)}) collective-permute-start(bf16[176,1536]{1,0:T(8,128)(2,1)} %get-tuple-element.52), channel_id=1, source_target_pairs={{0,4},{2,6},{4,0},{6,2},{8,12},{10,14},{12,8},{14,10},{16,20},{18,... | collective-permute-start | bytes 1622024 | tf_op jit(solution)/shard_map/ppermute | solution.py:439
  5.6 2.6 %collective-permute-start = (bf16[3,48,384]{2,1,0:T(8,128)(2,1)}, bf16[3,48,384]{2,1,0:T(8,128)(2,1)S(1)}, u32[]{:S(2)}, u32[]{:S(2)}) collective-permute-start(bf16[3,48,384]{2,1,0:T(8,128)(2,1)} %get-tuple-element.46), channel_id=1, source_target_pairs={{0,16},{2,18},{4,20},{6,22},{8,24},{10,26},{12,28},{14,30},{16,0},... | collective-permute-start | bytes 331784 | tf_op jit(solution)/shard_map/ppermute | solution.py:439
  8.2 1.3 %collective-permute-start.1 = (bf16[3,48,384]{2,1,0:T(8,128)(2,1)}, bf16[3,48,384]{2,1,0:T(8,128)(2,1)S(1)}, u32[]{:S(2)}, u32[]{:S(2)}) collective-permute-start(bf16[3,48,384]{2,1,0:T(8,128)(2,1)} %get-tuple-element.47), channel_id=1, source_target_pairs={{0,24},{2,26},{4,28},{6,30},{8,16},{10,18},{12,20},{14,22},{16,8},... | collective-permute-start | bytes 331784 | tf_op jit(solution)/shard_map/ppermute | solution.py:439
  9.7 0.5 collective-permute-start.4
  10.3 1.7 %shard_map.84 = (bf16[2,512,384]{2,1,0:T(8,128)(2,1)S(1)}, bf16[4,2,192,384]{3,2,1,0:T(8,128)(2,1)S(1)}) custom-call(bf16[2,512,1536]{2,1,0:T(8,128)(2,1)} %text_hbm.1, bf16[2,768,1536]{2,1,0:T(8,128)(2,1)} %stale_hbm.1), custom_call_target="tpu_custom_call" | custom-call | bytes 8388608 | tf_op jit(solution)/shard_map/pallas_call | solution.py:157
  11.9 5.1 %collective-permute-done.refs_1_ = bf16[3,48,384]{2,1,0:T(8,128)(2,1)S(1)} collective-permute-done((bf16[3,48,384]{2,1,0:T(8,128)(2,1)}, bf16[3,48,384]{2,1,0:T(8,128)(2,1)S(1)}, u32[]{:S(2)}, u32[]{:S(2)}) %collective-permute-start) | collective-permute-done | bytes 110624 | tf_op jit(solution)/shard_map/ppermute | solution.py:439
  17.2 2.4 %collective-permute-done.4.own_far = bf16[2,48,384]{2,1,0:T(8,128)(2,1)S(1)} collective-permute-done((bf16[2,48,384]{2,1,0:T(8,128)(2,1)}, bf16[2,48,384]{2,1,0:T(8,128)(2,1)S(1)}, u32[]{:S(2)}, u32[]{:S(2)}) %collective-permute-start.4) | collective-permute-done | bytes 73760 | tf_op jit(solution)/shard_map/ppermute | solution.py:439
  19.6 1.7 %collective-permute-start.5 = (bf16[3,2,48,384]{3,2,1,0:T(8,128)(2,1)S(1)}, bf16[3,2,48,384]{3,2,1,0:T(8,128)(2,1)S(1)}, u32[]{:S(2)}, u32[]{:S(2)}) collective-permute-start(bf16[3,2,48,384]{3,2,1,0:T(8,128)(2,1)S(1)} %get-tuple-element.57), channel_id=1, source_target_pairs={{0,4},{2,6},{4,0},{6,2},{8,12},{10,14},{12,8},{14,10},{16,20},{18,... | collective-permute-start | bytes 663560 | tf_op jit(solution)/shard_map/ppermute | solution.py:439
  21.4 1.2 %shard_map.85 = (f32[3,192,1]{2,1,0:T(8,128)S(1)}, f32[3,192,1]{2,1,0:T(8,128)S(1)}, f32[3,192,128]{2,1,0:T(8,128)S(1)}) custom-call(bf16[192,384]{1,0:T(8,128)(2,1)S(1)} %get-tuple-element.56.query, bf16[4,2,48,384]{3,2,1,0:T(8,128)(2,1)S(1)} %get-tuple-element.59.every, bf16[4,2,48,384]{3,2,1,0:T(8,128)(2,1)S(1)} %collective-permute-done.6.near, ...), custom_call_target="tpu_custom_call" | custom-call | flops 528482304 | bytes 2752512 | tf_op jit(solution)/shard_map/pallas_call | solution.py:283
  22.6 4.9 %collective-permute-done.5.some_far = bf16[3,2,48,384]{3,2,1,0:T(8,128)(2,1)S(1)} collective-permute-done((bf16[3,2,48,384]{3,2,1,0:T(8,128)(2,1)S(1)}, bf16[3,2,48,384]{3,2,1,0:T(8,128)(2,1)S(1)}, u32[]{:S(2)}, u32[]{:S(2)}) %collective-permute-start.5) | collective-permute-done | bytes 221216 | tf_op jit(solution)/shard_map/ppermute | solution.py:439
  27.5 0.5 collective-permute-start.7
  28.0 0.9 %shard_map.86 = (f32[3,192,1]{2,1,0:T(8,128)S(1)}, f32[3,192,1]{2,1,0:T(8,128)S(1)}, f32[3,192,128]{2,1,0:T(8,128)S(1)}) custom-call(bf16[192,384]{1,0:T(8,128)(2,1)S(1)} %get-tuple-element.56.query, bf16[2,48,384]{2,1,0:T(8,128)(2,1)S(1)} %collective-permute-done.4.own_far, bf16[3,2,48,384]{3,2,1,0:T(8,128)(2,1)S(1)} %collective-permute-done.5.some_far, ...), custom_call_target="tpu_custom_call" | custom-call | flops 113246208 | bytes 589824 | tf_op jit(solution)/shard_map/pallas_call | solution.py:283
  29.6 1.5 %collective-permute-start.10 = (bf16[16,1536]{1,0:T(8,128)(2,1)S(1)}, bf16[16,1536]{1,0:T(8,128)(2,1)S(1)}, u32[]{:S(2)}, u32[]{:S(2)}) collective-permute-start(bf16[16,1536]{1,0:T(8,128)(2,1)S(1)} %slice.7), channel_id=1, source_target_pairs={{0,6},{2,4},{4,2},{6,0},{8,14},{10,12},{12,10},{14,8},{16,22},{18,... | collective-permute-start | bytes 147464 | tf_op jit(solution)/shard_map/ppermute | solution.py:439
  31.4 1.1 %shard_map.87 = (bf16[192,384]{1,0:T(8,128)(2,1)S(1)}, bf16[192,256]{1,0:T(8,128)(2,1)S(1)}) custom-call(bf16[192,384]{1,0:T(8,128)(2,1)S(1)} %get-tuple-element.56.query, bf16[2,48,384]{2,1,0:T(8,128)(2,1)S(1)} %collective-permute-done.7.own_corner, bf16[3,2,48,384]{3,2,1,0:T(8,128)(2,1)S(1)} %collective-permute-done.8.some_corner, ...), custom_call_target="tpu_custom_call" | custom-call | flops 113246208 | bytes 589824 | tf_op jit(solution)/shard_map/pallas_call | solution.py:283
  32.5 2.9 %collective-permute-start.11 = (bf16[192,384]{1,0:T(8,128)(2,1)S(1)}, bf16[192,384]{1,0:T(8,128)(2,1)S(1)}, u32[]{:S(2)}, u32[]{:S(2)}) collective-permute-start(bf16[192,384]{1,0:T(8,128)(2,1)S(1)} %get-tuple-element.70.own), channel_id=1, source_target_pairs={{0,16},{2,18},{4,20},{6,22},{8,24},{10,26},{12,28},{14,30},{16,0},... | collective-permute-start | bytes 442376 | tf_op jit(solution)/shard_map/ppermute | solution.py:439
  35.4 1.6 %collective-permute-start.12 = (bf16[192,384]{1,0:T(8,128)(2,1)S(1)}, bf16[192,384]{1,0:T(8,128)(2,1)S(1)}, u32[]{:S(2)}, u32[]{:S(2)}) collective-permute-start(bf16[192,384]{1,0:T(8,128)(2,1)S(1)} %get-tuple-element.70.own), channel_id=1, source_target_pairs={{0,8},{2,10},{4,12},{6,14},{8,0},{10,2},{12,4},{14,6},{16,24},{18,... | collective-permute-start | bytes 442376 | tf_op jit(solution)/shard_map/ppermute | solution.py:439
  37.0 2.2 %collective-permute-start.15 = (bf16[192,256]{1,0:T(8,128)(2,1)S(1)}, bf16[192,256]{1,0:T(8,128)(2,1)S(1)}, u32[]{:S(2)}, u32[]{:S(2)}) collective-permute-start(bf16[192,256]{1,0:T(8,128)(2,1)S(1)} %get-tuple-element.76), channel_id=1, source_target_pairs={{0,24},{2,26},{4,28},{6,30},{8,16},{10,18},{12,20},{14,22},{16,8},... | collective-permute-start | bytes 294920 | tf_op jit(solution)/shard_map/ppermute | solution.py:439
  39.3 4.6 %collective-permute-done.11.second = bf16[192,384]{1,0:T(8,128)(2,1)S(1)} collective-permute-done((bf16[192,384]{1,0:T(8,128)(2,1)S(1)}, bf16[192,384]{1,0:T(8,128)(2,1)S(1)}, u32[]{:S(2)}, u32[]{:S(2)}) %collective-permute-start.11) | collective-permute-done | bytes 147488 | tf_op jit(solution)/shard_map/ppermute | solution.py:439
  44.4 0.7 %shard_map.89.partial = f32[192,768]{1,0:T(8,128)S(1)} custom-call(bf16[192,384]{1,0:T(8,128)(2,1)S(1)} %get-tuple-element.70.own, bf16[192,384]{1,0:T(8,128)(2,1)S(1)} %collective-permute-done.11.second, bf16[192,384]{1,0:T(8,128)(2,1)S(1)} %collective-permute-done.12.first, bf16[768,1536]{1,0:T(8,128)(2,1)S(1)} %shard_map.88.weight), custom_call_target="tpu_custom_call" | custom-call | flops 452984832 | bytes 589824 | tf_op jit(solution)/shard_map/pallas_call | solution.py:338
  45.2 0.9 %collective-permute-done.15.most = bf16[192,256]{1,0:T(8,128)(2,1)S(1)} collective-permute-done((bf16[192,256]{1,0:T(8,128)(2,1)S(1)}, bf16[192,256]{1,0:T(8,128)(2,1)S(1)}, u32[]{:S(2)}, u32[]{:S(2)}) %collective-permute-start.15) | collective-permute-done | bytes 98336 | tf_op jit(solution)/shard_map/ppermute | solution.py:439
  46.0 1.9 %collective-permute-done.16.last = bf16[192,128]{1,0:T(8,128)(2,1)S(1)} collective-permute-done((bf16[192,128]{1,0:T(8,128)(2,1)S(1)}, bf16[192,128]{1,0:T(8,128)(2,1)S(1)}, u32[]{:S(2)}, u32[]{:S(2)}) %collective-permute-start.16) | collective-permute-done | bytes 49184 | tf_op jit(solution)/shard_map/ppermute | solution.py:439
  48.0 0.4 shard_map.90
  48.3 3.5 %collective-permute-start.19 = (bf16[48,768]{1,0:T(8,128)(2,1)S(1)}, bf16[48,768]{1,0:T(8,128)(2,1)S(1)}, u32[]{:S(2)}, u32[]{:S(2)}) collective-permute-start(bf16[48,768]{1,0:T(8,128)(2,1)S(1)} %get-tuple-element.81), channel_id=1, source_target_pairs={{0,24},{2,26},{4,28},{6,30},{8,16},{10,18},{12,20},{14,22},{16,8},... | collective-permute-start | bytes 221192 | tf_op jit(solution)/shard_map/ppermute | solution.py:439
  51.8 1.0 %collective-permute-start.17 = (bf16[48,768]{1,0:T(8,128)(2,1)S(1)}, bf16[48,768]{1,0:T(8,128)(2,1)S(1)}, u32[]{:S(2)}, u32[]{:S(2)}) collective-permute-start(bf16[48,768]{1,0:T(8,128)(2,1)S(1)} %get-tuple-element.77), channel_id=1, source_target_pairs={{0,16},{2,18},{4,20},{6,22},{8,24},{10,26},{12,28},{14,30},{16,0},... | collective-permute-start | bytes 221192 | tf_op jit(solution)/shard_map/ppermute | solution.py:439
  52.8 1.9 %collective-permute-done.19.far = bf16[48,768]{1,0:T(8,128)(2,1)S(1)} collective-permute-done((bf16[48,768]{1,0:T(8,128)(2,1)S(1)}, bf16[48,768]{1,0:T(8,128)(2,1)S(1)}, u32[]{:S(2)}, u32[]{:S(2)}) %collective-permute-start.19) | collective-permute-done | bytes 73760 | tf_op jit(solution)/shard_map/ppermute | solution.py:439
  54.7 1.7 %collective-permute-done.20.near = bf16[48,768]{1,0:T(8,128)(2,1)S(1)} collective-permute-done((bf16[48,768]{1,0:T(8,128)(2,1)S(1)}, bf16[48,768]{1,0:T(8,128)(2,1)S(1)}, u32[]{:S(2)}, u32[]{:S(2)}) %collective-permute-start.20) | collective-permute-done | bytes 73760 | tf_op jit(solution)/shard_map/ppermute | solution.py:439
  56.3 1.6 %collective-permute-start.21 = (bf16[48,768]{1,0:T(8,128)(2,1)S(1)}, bf16[48,768]{1,0:T(8,128)(2,1)S(1)}, u32[]{:S(2)}, u32[]{:S(2)}) collective-permute-start(bf16[48,768]{1,0:T(8,128)(2,1)S(1)} %get-tuple-element.84), channel_id=1, source_target_pairs={{0,1},{1,0},{2,3},{3,2},{4,5},{5,4},{6,7},{7,6},{8,9},{9,8},{10,11... | collective-permute-start | bytes 221192 | tf_op jit(solution)/shard_map/ppermute | solution.py:480
  57.9 0.8 %collective-permute-start.18 = (bf16[48,768]{1,0:T(8,128)(2,1)S(1)}, bf16[48,768]{1,0:T(8,128)(2,1)S(1)}, u32[]{:S(2)}, u32[]{:S(2)}) collective-permute-start(bf16[48,768]{1,0:T(8,128)(2,1)S(1)} %get-tuple-element.80), channel_id=1, source_target_pairs={{0,1},{1,0},{2,3},{3,2},{4,5},{5,4},{6,7},{7,6},{8,9},{9,8},{10,11... | collective-permute-start | bytes 221192 | tf_op jit(solution)/shard_map/ppermute | solution.py:480
  58.8 2.0 %collective-permute-done.21.arrived_odd = bf16[48,768]{1,0:T(8,128)(2,1)S(1)} collective-permute-done((bf16[48,768]{1,0:T(8,128)(2,1)S(1)}, bf16[48,768]{1,0:T(8,128)(2,1)S(1)}, u32[]{:S(2)}, u32[]{:S(2)}) %collective-permute-start.21) | collective-permute-done | bytes 73760 | tf_op jit(solution)/shard_map/ppermute | solution.py:480
  60.8 1.6 %collective-permute-done.18.arrived_even = bf16[48,768]{1,0:T(8,128)(2,1)S(1)} collective-permute-done((bf16[48,768]{1,0:T(8,128)(2,1)S(1)}, bf16[48,768]{1,0:T(8,128)(2,1)S(1)}, u32[]{:S(2)}, u32[]{:S(2)}) %collective-permute-start.18) | collective-permute-done | bytes 73760 | tf_op jit(solution)/shard_map/ppermute | solution.py:480
  62.4 0.7 %shard_map.93 = bf16[48,1536]{1,0:T(8,128)(2,1)} custom-call(bf16[48,768]{1,0:T(8,128)(2,1)S(1)} %get-tuple-element.79.kept_even, bf16[48,768]{1,0:T(8,128)(2,1)S(1)} %collective-permute-done.18.arrived_even, bf16[48,768]{1,0:T(8,128)(2,1)S(1)} %get-tuple-element.83.kept_odd, bf16[48,768]{1,0:T(8,128)(2,1)S(1)} %collective-permute-done.21.arrived_odd, ...), custom_call_target="tpu_custom_call" | custom-call | flops 221184 | bytes 294912 | tf_op jit(solution)/shard_map/pallas_call | solution.py:419
  (36 shorter events, 2.0 us)
Async XLA Ops:
  2.6 17.1 %collective-permute-start.3 = (bf16[176,1536]{1,0:T(8,128)(2,1)}, bf16[176,1536]{1,0:T(8,128)(2,1)S(1)}, u32[]{:S(2)}, u32[]{:S(2)}) collective-permute-start(bf16[176,1536]{1,0:T(8,128)(2,1)} %get-tuple-element.52), channel_id=1, source_target_pairs={{0,4},{2,6},{4,0},{6,2},{8,12},{10,14},{12,8},{14,10},{16,20},{18,... | collective-permute-start | bytes 1622024 | tf_op jit(solution)/shard_map/ppermute | solution.py:439
  5.6 11.5 %collective-permute-start = (bf16[3,48,384]{2,1,0:T(8,128)(2,1)}, bf16[3,48,384]{2,1,0:T(8,128)(2,1)S(1)}, u32[]{:S(2)}, u32[]{:S(2)}) collective-permute-start(bf16[3,48,384]{2,1,0:T(8,128)(2,1)} %get-tuple-element.46), channel_id=1, source_target_pairs={{0,16},{2,18},{4,20},{6,22},{8,24},{10,26},{12,28},{14,30},{16,0},... | collective-permute-start | bytes 331784 | tf_op jit(solution)/shard_map/ppermute | solution.py:439
  8.2 8.9 %collective-permute-start.1 = (bf16[3,48,384]{2,1,0:T(8,128)(2,1)}, bf16[3,48,384]{2,1,0:T(8,128)(2,1)S(1)}, u32[]{:S(2)}, u32[]{:S(2)}) collective-permute-start(bf16[3,48,384]{2,1,0:T(8,128)(2,1)} %get-tuple-element.47), channel_id=1, source_target_pairs={{0,24},{2,26},{4,28},{6,30},{8,16},{10,18},{12,20},{14,22},{16,8},... | collective-permute-start | bytes 331784 | tf_op jit(solution)/shard_map/ppermute | solution.py:439
  9.5 7.7 %collective-permute-start.2 = (bf16[3,48,384]{2,1,0:T(8,128)(2,1)}, bf16[3,48,384]{2,1,0:T(8,128)(2,1)S(1)}, u32[]{:S(2)}, u32[]{:S(2)}) collective-permute-start(bf16[3,48,384]{2,1,0:T(8,128)(2,1)} %get-tuple-element.48), channel_id=1, source_target_pairs={{0,8},{2,10},{4,12},{6,14},{8,0},{10,2},{12,4},{14,6},{16,24},{18,... | collective-permute-start | bytes 331784 | tf_op jit(solution)/shard_map/ppermute | solution.py:439
  9.7 7.4 %copy-start.1 = (bf16[3,48,384]{2,1,0:T(8,128)(2,1)S(1)}, bf16[3,48,384]{2,1,0:T(8,128)(2,1)}, u32[]{:S(2)}) copy-start(bf16[3,48,384]{2,1,0:T(8,128)(2,1)} %get-tuple-element.45.refs_0_) | copy-start | bytes 331780
  9.7 9.9 %collective-permute-start.4 = (bf16[2,48,384]{2,1,0:T(8,128)(2,1)}, bf16[2,48,384]{2,1,0:T(8,128)(2,1)S(1)}, u32[]{:S(2)}, u32[]{:S(2)}) collective-permute-start(bf16[2,48,384]{2,1,0:T(8,128)(2,1)} %get-tuple-element.53), channel_id=1, source_target_pairs={{0,4},{2,6},{4,0},{6,2},{8,12},{10,14},{12,8},{14,10},{16,20},{18,... | collective-permute-start | bytes 221192 | tf_op jit(solution)/shard_map/ppermute | solution.py:439
  11.9 17.1 %copy-start = (bf16[1536,192]{0,1:T(8,128)(2,1)S(1)}, bf16[1536,192]{0,1:T(8,128)(2,1)}, u32[]{:S(2)}) copy-start(bf16[1536,192]{0,1:T(8,128)(2,1)} %param.13) | copy-start | bytes 1769476
  19.6 1.7 %collective-permute-start.6 = (bf16[4,2,48,384]{3,2,1,0:T(8,128)(2,1)S(1)}, bf16[4,2,48,384]{3,2,1,0:T(8,128)(2,1)S(1)}, u32[]{:S(2)}, u32[]{:S(2)}) collective-permute-start(bf16[4,2,48,384]{3,2,1,0:T(8,128)(2,1)S(1)} %get-tuple-element.59.every), channel_id=1, source_target_pairs={{0,2},{2,0},{4,6},{6,4},{8,10},{10,8},{12,14},{14,12},{16,18},{18,... | collective-permute-start | bytes 884744 | tf_op jit(solution)/shard_map/ppermute | solution.py:439
  19.6 7.8 %collective-permute-start.5 = (bf16[3,2,48,384]{3,2,1,0:T(8,128)(2,1)S(1)}, bf16[3,2,48,384]{3,2,1,0:T(8,128)(2,1)S(1)}, u32[]{:S(2)}, u32[]{:S(2)}) collective-permute-start(bf16[3,2,48,384]{3,2,1,0:T(8,128)(2,1)S(1)} %get-tuple-element.57), channel_id=1, source_target_pairs={{0,4},{2,6},{4,0},{6,2},{8,12},{10,14},{12,8},{14,10},{16,20},{18,... | collective-permute-start | bytes 663560 | tf_op jit(solution)/shard_map/ppermute | solution.py:439
  27.5 1.6 %collective-permute-start.8 = (bf16[3,2,48,384]{3,2,1,0:T(8,128)(2,1)S(1)}, bf16[3,2,48,384]{3,2,1,0:T(8,128)(2,1)S(1)}, u32[]{:S(2)}, u32[]{:S(2)}) collective-permute-start(bf16[3,2,48,384]{3,2,1,0:T(8,128)(2,1)S(1)} %collective-permute-done.5.some_far), channel_id=1, source_target_pairs={{0,2},{2,0},{4,6},{6,4},{8,10},{10,8},{12,14},{14,12},{16,18},{18,... | collective-permute-start | bytes 663560 | tf_op jit(solution)/shard_map/ppermute | solution.py:439
  27.5 1.6 %collective-permute-start.7 = (bf16[2,48,384]{2,1,0:T(8,128)(2,1)S(1)}, bf16[2,48,384]{2,1,0:T(8,128)(2,1)S(1)}, u32[]{:S(2)}, u32[]{:S(2)}) collective-permute-start(bf16[2,48,384]{2,1,0:T(8,128)(2,1)S(1)} %collective-permute-done.4.own_far), channel_id=1, source_target_pairs={{0,2},{2,0},{4,6},{6,4},{8,10},{10,8},{12,14},{14,12},{16,18},{18,... | collective-permute-start | bytes 221192 | tf_op jit(solution)/shard_map/ppermute | solution.py:439
  29.1 15.1 %collective-permute-start.13 = (bf16[192,1536]{1,0:T(8,128)(2,1)S(1)}, bf16[192,1536]{1,0:T(8,128)(2,1)S(1)}, u32[]{:S(2)}, u32[]{:S(2)}) collective-permute-start(bf16[192,1536]{1,0:T(8,128)(2,1)S(1)} %bitcast.3), channel_id=1, source_target_pairs={{0,2},{2,0},{4,6},{6,4},{8,10},{10,8},{12,14},{14,12},{16,18},{18,... | collective-permute-start | bytes 1769480 | tf_op jit(solution)/shard_map/ppermute | solution.py:439
  29.3 14.9 %collective-permute-start.14 = (bf16[176,1536]{1,0:T(8,128)(2,1)S(1)}, bf16[176,1536]{1,0:T(8,128)(2,1)S(1)}, u32[]{:S(2)}, u32[]{:S(2)}) collective-permute-start(bf16[176,1536]{1,0:T(8,128)(2,1)S(1)} %collective-permute-done.3.early), channel_id=1, source_target_pairs={{0,2},{2,0},{4,6},{6,4},{8,10},{10,8},{12,14},{14,12},{16,18},{18,... | collective-permute-start | bytes 1622024 | tf_op jit(solution)/shard_map/ppermute | solution.py:439
  29.6 5.8 %collective-permute-start.10 = (bf16[16,1536]{1,0:T(8,128)(2,1)S(1)}, bf16[16,1536]{1,0:T(8,128)(2,1)S(1)}, u32[]{:S(2)}, u32[]{:S(2)}) collective-permute-start(bf16[16,1536]{1,0:T(8,128)(2,1)S(1)} %slice.7), channel_id=1, source_target_pairs={{0,6},{2,4},{4,2},{6,0},{8,14},{10,12},{12,10},{14,8},{16,22},{18,... | collective-permute-start | bytes 147464 | tf_op jit(solution)/shard_map/ppermute | solution.py:439
  31.1 4.3 %collective-permute-start.9 = (bf16[16,1536]{1,0:T(8,128)(2,1)S(1)}, bf16[16,1536]{1,0:T(8,128)(2,1)S(1)}, u32[]{:S(2)}, u32[]{:S(2)}) collective-permute-start(bf16[16,1536]{1,0:T(8,128)(2,1)S(1)} %slice.7), channel_id=1, source_target_pairs={{0,4},{2,6},{4,0},{6,2},{8,12},{10,14},{12,8},{14,10},{16,20},{18,... | collective-permute-start | bytes 147464 | tf_op jit(solution)/shard_map/ppermute | solution.py:439
  32.5 11.3 %collective-permute-start.11 = (bf16[192,384]{1,0:T(8,128)(2,1)S(1)}, bf16[192,384]{1,0:T(8,128)(2,1)S(1)}, u32[]{:S(2)}, u32[]{:S(2)}) collective-permute-start(bf16[192,384]{1,0:T(8,128)(2,1)S(1)} %get-tuple-element.70.own), channel_id=1, source_target_pairs={{0,16},{2,18},{4,20},{6,22},{8,24},{10,26},{12,28},{14,30},{16,0},... | collective-permute-start | bytes 442376 | tf_op jit(solution)/shard_map/ppermute | solution.py:439
  35.4 9.0 %collective-permute-start.12 = (bf16[192,384]{1,0:T(8,128)(2,1)S(1)}, bf16[192,384]{1,0:T(8,128)(2,1)S(1)}, u32[]{:S(2)}, u32[]{:S(2)}) collective-permute-start(bf16[192,384]{1,0:T(8,128)(2,1)S(1)} %get-tuple-element.70.own), channel_id=1, source_target_pairs={{0,8},{2,10},{4,12},{6,14},{8,0},{10,2},{12,4},{14,6},{16,24},{18,... | collective-permute-start | bytes 442376 | tf_op jit(solution)/shard_map/ppermute | solution.py:439
  37.0 9.0 %collective-permute-start.15 = (bf16[192,256]{1,0:T(8,128)(2,1)S(1)}, bf16[192,256]{1,0:T(8,128)(2,1)S(1)}, u32[]{:S(2)}, u32[]{:S(2)}) collective-permute-start(bf16[192,256]{1,0:T(8,128)(2,1)S(1)} %get-tuple-element.76), channel_id=1, source_target_pairs={{0,24},{2,26},{4,28},{6,30},{8,16},{10,18},{12,20},{14,22},{16,8},... | collective-permute-start | bytes 294920 | tf_op jit(solution)/shard_map/ppermute | solution.py:439
  43.9 4.1 %collective-permute-start.16 = (bf16[192,128]{1,0:T(8,128)(2,1)S(1)}, bf16[192,128]{1,0:T(8,128)(2,1)S(1)}, u32[]{:S(2)}, u32[]{:S(2)}) collective-permute-start(bf16[192,128]{1,0:T(8,128)(2,1)S(1)} %slice.9), channel_id=1, source_target_pairs={{0,8},{2,10},{4,12},{6,14},{8,0},{10,2},{12,4},{14,6},{16,24},{18,... | collective-permute-start | bytes 147464 | tf_op jit(solution)/shard_map/ppermute | solution.py:439
  44.4 14.4 %copy-start.2 = (f32[1536]{0:T(1024)S(1)}, f32[1536]{0:T(1024)}, u32[]{:S(2)}) copy-start(f32[1536]{0:T(1024)} %param.14) | copy-start | bytes 18436
  44.4 14.4 %copy-start.3 = (f32[1536]{0:T(1024)S(1)}, f32[1536]{0:T(1024)}, u32[]{:S(2)}) copy-start(f32[1536]{0:T(1024)} %param.15) | copy-start | bytes 18436
  48.3 6.3 %collective-permute-start.19 = (bf16[48,768]{1,0:T(8,128)(2,1)S(1)}, bf16[48,768]{1,0:T(8,128)(2,1)S(1)}, u32[]{:S(2)}, u32[]{:S(2)}) collective-permute-start(bf16[48,768]{1,0:T(8,128)(2,1)S(1)} %get-tuple-element.81), channel_id=1, source_target_pairs={{0,24},{2,26},{4,28},{6,30},{8,16},{10,18},{12,20},{14,22},{16,8},... | collective-permute-start | bytes 221192 | tf_op jit(solution)/shard_map/ppermute | solution.py:439
  51.8 4.5 %collective-permute-start.20 = (bf16[48,768]{1,0:T(8,128)(2,1)S(1)}, bf16[48,768]{1,0:T(8,128)(2,1)S(1)}, u32[]{:S(2)}, u32[]{:S(2)}) collective-permute-start(bf16[48,768]{1,0:T(8,128)(2,1)S(1)} %get-tuple-element.82), channel_id=1, source_target_pairs={{0,8},{2,10},{4,12},{6,14},{8,0},{10,2},{12,4},{14,6},{16,24},{18,... | collective-permute-start | bytes 221192 | tf_op jit(solution)/shard_map/ppermute | solution.py:439
  51.8 6.1 %collective-permute-start.17 = (bf16[48,768]{1,0:T(8,128)(2,1)S(1)}, bf16[48,768]{1,0:T(8,128)(2,1)S(1)}, u32[]{:S(2)}, u32[]{:S(2)}) collective-permute-start(bf16[48,768]{1,0:T(8,128)(2,1)S(1)} %get-tuple-element.77), channel_id=1, source_target_pairs={{0,16},{2,18},{4,20},{6,22},{8,24},{10,26},{12,28},{14,30},{16,0},... | collective-permute-start | bytes 221192 | tf_op jit(solution)/shard_map/ppermute | solution.py:439
  56.3 4.4 %collective-permute-start.21 = (bf16[48,768]{1,0:T(8,128)(2,1)S(1)}, bf16[48,768]{1,0:T(8,128)(2,1)S(1)}, u32[]{:S(2)}, u32[]{:S(2)}) collective-permute-start(bf16[48,768]{1,0:T(8,128)(2,1)S(1)} %get-tuple-element.84), channel_id=1, source_target_pairs={{0,1},{1,0},{2,3},{3,2},{4,5},{5,4},{6,7},{7,6},{8,9},{9,8},{10,11... | collective-permute-start | bytes 221192 | tf_op jit(solution)/shard_map/ppermute | solution.py:480
  57.9 4.4 %collective-permute-start.18 = (bf16[48,768]{1,0:T(8,128)(2,1)S(1)}, bf16[48,768]{1,0:T(8,128)(2,1)S(1)}, u32[]{:S(2)}, u32[]{:S(2)}) collective-permute-start(bf16[48,768]{1,0:T(8,128)(2,1)S(1)} %get-tuple-element.80), channel_id=1, source_target_pairs={{0,1},{1,0},{2,3},{3,2},{4,5},{5,4},{6,7},{7,6},{8,9},{9,8},{10,11... | collective-permute-start | bytes 221192 | tf_op jit(solution)/shard_map/ppermute | solution.py:480

commit v19 on v16

--- a/solution.py
+++ b/solution.py
@@ -264,16 +264,13 @@
         peak[head], total[head], mixed[head] = state
 
 
-def last_kernel(query, own_corner, some_corner, stale, peak, total, mixed, out, most):
+def last_kernel(query, own_corner, some_corner, stale, peak, total, mixed, out):
     heads = columns_of(query.shape[1])
     image = image_segment(stale, 3, split_part(own_corner, some_corner))
     states = [(peak[head], total[head], mixed[head]) for head in range(len(heads))]
     states = absorb([query[:, cols] for cols in heads], [[image(cols)] for cols in heads], states)
     for cols, (_, sums, mix) in zip(heads, states):
-        value = (mix / sums).astype(jnp.bfloat16)
-        out[:, cols] = value
-        if cols is not heads[-1]:
-            most[:, cols] = value
+        out[:, cols] = (mix / sums).astype(jnp.bfloat16)
 
 
 def attend_call(kernel, operands, shapes, keys):
@@ -296,25 +293,41 @@
     return [jax.ShapeDtypeStruct((heads, tokens, size), jnp.float32) for size in (1, 1, HD)]
 
 
-def order_kernel(*refs):
-    pieces, out = refs[:-1], refs[-1]
+def stack_kernel(first, second, out):
+    out[0] = first[...]
+    out[1] = second[...]
+
+
+def stack(first, second):
+    return pl.pallas_call(
+        stack_kernel,
+        out_shape=jax.ShapeDtypeStruct((2, *first.shape), first.dtype),
+        in_specs=[VMEM] * 2,
+        out_specs=VMEM,
+        compiler_params=pltpu.CompilerParams(vmem_limit_bytes=SMALL),
+        cost_estimate=pl.CostEstimate(flops=0, bytes_accessed=8 * first.size, transcendentals=0),
+    )(first, second)
+
+
+def order_kernel(own, across, out):
     _, spot = place()
-    span = out.shape[0] // SPREAD
-    for twist, piece in enumerate(pieces):
-        out[pl.ds(aligned(jnp.bitwise_xor(spot, twist), span), span), :] = piece[...]
-
-
-def order(pieces):
-    span, depth = pieces[0].shape
-    shape = (SPREAD * span, depth)
+    span = own.shape[1]
+    for twist in range(SPREAD):
+        piece = (own, across)[twist % 2][twist // 2]
+        out[pl.ds(aligned(jnp.bitwise_xor(spot, twist), span), span), :] = piece
+
+
+def order(own, across):
+    count, span, depth = own.shape
+    shape = (2 * count * span, depth)
     return pl.pallas_call(
         order_kernel,
         out_shape=jax.ShapeDtypeStruct(shape, jnp.bfloat16),
-        in_specs=[VMEM] * len(pieces),
+        in_specs=[VMEM] * 2,
         out_specs=VMEM,
         compiler_params=pltpu.CompilerParams(vmem_limit_bytes=SMALL),
         cost_estimate=pl.CostEstimate(flops=0, bytes_accessed=4 * shape[0] * depth, transcendentals=0),
-    )(*pieces)
+    )(own, across)
 
 
 def term_of(part, weight, turn, width, skip=0):
@@ -344,30 +357,28 @@
     )(*parts, weight)
 
 
-def close_kernel(partial, most, last, weight, *rest):
+def close_kernel(partial, third, weight, *rest):
     outs, total = rest[:-1], rest[-1]
     group, _ = place()
     rows = outs[0].shape[0]
-    width = most.shape[1] + last.shape[1]
-    added = partial[...] + term_of(most, weight, 3, width) + term_of(last, weight, 3, width, width - HD)
-    total[...] = added.astype(jnp.bfloat16)
+    total[...] = (partial[...] + term_of(third, weight, 3, third.shape[1])).astype(jnp.bfloat16)
     for turn, out in enumerate(outs):
         out[...] = total[pl.ds(aligned(jnp.bitwise_xor(group, turn), rows), rows), :]
 
 
-def close(groups, partial, most, last, weight):
+def close(groups, partial, third, weight):
     tokens, columns = partial.shape
     return pl.pallas_call(
         close_kernel,
         out_shape=[jax.ShapeDtypeStruct((tokens // groups, columns), jnp.bfloat16)] * groups,
-        in_specs=[VMEM] * 4,
+        in_specs=[VMEM] * 3,
         out_specs=[VMEM] * groups,
         scratch_shapes=[pltpu.VMEM((tokens, columns), jnp.bfloat16)],
         compiler_params=pltpu.CompilerParams(vmem_limit_bytes=SMALL),
         cost_estimate=pl.CostEstimate(
             flops=tokens * weight.size, bytes_accessed=8 * tokens * columns, transcendentals=0
         ),
-    )(partial, most, last, weight)
+    )(partial, third, weight)
 
 
 def at_home(group):
@@ -453,20 +464,20 @@
     operands = [query, every, near, text, stale]
     state = attend_call(near_kernel, operands, state_shapes(query), 2 * share + text.shape[1])
 
-    some_far, own_far = lax.optimization_barrier((some_far, own_far, *state))[:2]
+    ready = (some_far, own_far, stack(weight, weight_far), *state)
+    some_far, own_far, weight = lax.optimization_barrier(ready)[:3]
     own_corner, some_corner = swap(own_far, 1), swap(some_far, 1)
     state = attend_call(middle_kernel, [query, own_far, some_far, stale, *state], state_shapes(query), share)
-    weight, weight_far = lax.optimization_barrier((weight, weight_far, own_corner, some_corner, *state))[:2]
-    weight_near, weight_corner = swap(weight, 1), swap(weight_far, 1)
+    weight = after(weight, own_corner, some_corner, *state)
+    weight_across = swap(weight, 1)
     operands = [query, own_corner, some_corner, stale, *state]
-    tokens, width = query.shape
-    shapes = [jax.ShapeDtypeStruct((tokens, size), jnp.bfloat16) for size in (width, width - HD)]
-    attended, most = attend_call(last_kernel, operands, shapes, share)
-
-    second, first, third = (swap(value, turn * SPREAD) for turn, value in ((2, attended), (1, attended), (3, most)))
-    passed = swap(second[:, width - HD :], SPREAD)
-    weight = order([weight, weight_near, weight_far, weight_corner])
-    terms = close(groups, begin([attended, second, first], weight), third, passed, weight)
+    shape = jax.ShapeDtypeStruct(query.shape, jnp.bfloat16)
+    (attended,) = attend_call(last_kernel, operands, [shape], share)
+
+    second, first = swap(attended, 2 * SPREAD), swap(attended, SPREAD)
+    third = swap(second, SPREAD)
+    weight = order(weight, weight_across)
+    terms = close(groups, begin([attended, second, first], weight), third, weight)
     second, third, first = along(terms)
     pieces = []
     for near, far in ((terms[0], second), (first, third)):

time: 59.8 us -> 59.6 us (level)
    ppermute x18 -> x16, waiting for transfers between devices: 23.6 us -> 24.2 us  [swap(): return lax.ppermute(value, 'patch', [(p, p ^ twist) for p in range(size)])]
    ppermute x18 -> x16, starting transfers between devices: 19.9 us -> 19.7 us  [swap(): return lax.ppermute(value, 'patch', [(p, p ^ twist) for p in range(size)])]
  transfers between devices with their start and end apart: 20 -> 18, of which waited for: 11 -> 12; matrix products, arithmetic and copies ran while one was open for 0% -> 0% of each run, Pallas kernels for 14% -> 14%
where the time goes in v19:
time: 59.6 us; the launch traced here: 59.4 us
  waiting for transfers between devices  27 us (45%)
  starting transfers between devices  22.9 us (38%)
  Pallas kernels  9.35 us (16%)
    ppermute x16, waiting for transfers between devices, swap(): return lax.ppermute(value, 'patch', [(p, p ^ twist) for p in range(size)])  24.2 us
    ppermute x16, starting transfers between devices, swap(): return lax.ppermute(value, 'patch', [(p, p ^ twist) for p in range(size)])  19.7 us
    pallas_call x3, Pallas kernels, attend_call(): pl.pallas_call(kernel, out_shape=shapes, in_specs=[VMEM] * len(operands),...  3.2 us
    ppermute x2, starting transfers between devices, grouped_body(): pieces += [kept, lax.ppermute(sent, 'head', [(0, 1), (1, 0)])]  3.13 us
    ppermute x2, waiting for transfers between devices, grouped_body(): pieces += [kept, lax.ppermute(sent, 'head', [(0, 1), (1, 0)])]  2.8 us
    pallas_call x1, Pallas kernels, pack(): pl.pallas_call(pack_kernel, out_shape=[jax.ShapeDtypeStruct(shape, bf16)...  2.32 us
    pallas_call x1, Pallas kernels, pick(): pl.pallas_call(pick_kernel, out_shape=[jax.ShapeDtypeStruct((kinds, texts...  1.65 us
  transfers between devices with their start and end apart: 18, of which 12 were waited for; matrix products, arithmetic and copies ran while one was open for 0% of the time, Pallas kernels for 14%

profile of v19, /device:TPU:0, one launch (start us, length us, event | category | flops | bytes accessed | tf_op | source)
XLA Modules:
  0.0 59.4 jit_solution(15395098193226766447)
XLA Ops:
  0.0 2.9 %collective-permute-start.3 = (bf16[192,1536]{1,0:T(8,128)(2,1)}, bf16[192,1536]{1,0:T(8,128)(2,1)S(1)}, u32[]{:S(2)}, u32[]{:S(2)}) collective-permute-start(bf16[192,1536]{1,0:T(8,128)(2,1)} %bitcast.2), channel_id=1, source_target_pairs={{0,4},{2,6},{4,0},{6,2},{8,12},{10,14},{12,8},{14,10},{16,20},{18,... | collective-permute-start | bytes 1769480 | tf_op jit(solution)/shard_map/ppermute | solution.py:447
  2.9 2.3 %shard_map.82 = (bf16[3,48,384]{2,1,0:T(8,128)(2,1)}, bf16[3,48,384]{2,1,0:T(8,128)(2,1)}, bf16[3,48,384]{2,1,0:T(8,128)(2,1)}, bf16[3,48,384]{2,1,0:T(8,128)(2,1)}, bf16[2,48,384]{2,1,0:T(8,128)(2,1)}) custom-call(bf16[48,1536]{1,0:T(8,128)(2,1)} %queries_hbm.1, s32[2,48,1536]{2,1,0:T(8,128)} %codes_hbm.1, s32[12,2,48]{2,1,0:T(2,128)} %bitcast.4), custom_call_target="tpu_custom_call" | custom-call | flops 294912 | bytes 884736 | tf_op jit(solution)/shard_map/pallas_call | solution.py:110
  5.3 2.7 %collective-permute-start = (bf16[3,48,384]{2,1,0:T(8,128)(2,1)}, bf16[3,48,384]{2,1,0:T(8,128)(2,1)S(1)}, u32[]{:S(2)}, u32[]{:S(2)}) collective-permute-start(bf16[3,48,384]{2,1,0:T(8,128)(2,1)} %get-tuple-element.39), channel_id=1, source_target_pairs={{0,16},{2,18},{4,20},{6,22},{8,24},{10,26},{12,28},{14,30},{16,0},... | collective-permute-start | bytes 331784 | tf_op jit(solution)/shard_map/ppermute | solution.py:447
  7.9 1.3 %collective-permute-start.1 = (bf16[3,48,384]{2,1,0:T(8,128)(2,1)}, bf16[3,48,384]{2,1,0:T(8,128)(2,1)S(1)}, u32[]{:S(2)}, u32[]{:S(2)}) collective-permute-start(bf16[3,48,384]{2,1,0:T(8,128)(2,1)} %get-tuple-element.40), channel_id=1, source_target_pairs={{0,24},{2,26},{4,28},{6,30},{8,16},{10,18},{12,20},{14,22},{16,8},... | collective-permute-start | bytes 331784 | tf_op jit(solution)/shard_map/ppermute | solution.py:447
  9.3 0.2 collective-permute-start.2
  9.5 0.5 collective-permute-start.4
  10.0 1.7 %shard_map.84 = (bf16[2,512,384]{2,1,0:T(8,128)(2,1)S(1)}, bf16[4,2,192,384]{3,2,1,0:T(8,128)(2,1)S(1)}) custom-call(bf16[2,512,1536]{2,1,0:T(8,128)(2,1)} %text_hbm.1, bf16[2,768,1536]{2,1,0:T(8,128)(2,1)} %stale_hbm.1), custom_call_target="tpu_custom_call" | custom-call | bytes 8388608 | tf_op jit(solution)/shard_map/pallas_call | solution.py:155
  11.7 5.1 %collective-permute-done.refs_1_ = bf16[3,48,384]{2,1,0:T(8,128)(2,1)S(1)} collective-permute-done((bf16[3,48,384]{2,1,0:T(8,128)(2,1)}, bf16[3,48,384]{2,1,0:T(8,128)(2,1)S(1)}, u32[]{:S(2)}, u32[]{:S(2)}) %collective-permute-start) | collective-permute-done | bytes 110624 | tf_op jit(solution)/shard_map/ppermute | solution.py:447
  17.0 1.0 %collective-permute-done.4.own_far = bf16[2,48,384]{2,1,0:T(8,128)(2,1)S(1)} collective-permute-done((bf16[2,48,384]{2,1,0:T(8,128)(2,1)}, bf16[2,48,384]{2,1,0:T(8,128)(2,1)S(1)}, u32[]{:S(2)}, u32[]{:S(2)}) %collective-permute-start.4) | collective-permute-done | bytes 73760 | tf_op jit(solution)/shard_map/ppermute | solution.py:447
  18.1 1.7 %collective-permute-start.5 = (bf16[3,2,48,384]{3,2,1,0:T(8,128)(2,1)S(1)}, bf16[3,2,48,384]{3,2,1,0:T(8,128)(2,1)S(1)}, u32[]{:S(2)}, u32[]{:S(2)}) collective-permute-start(bf16[3,2,48,384]{3,2,1,0:T(8,128)(2,1)S(1)} %get-tuple-element.49), channel_id=1, source_target_pairs={{0,4},{2,6},{4,0},{6,2},{8,12},{10,14},{12,8},{14,10},{16,20},{18,... | collective-permute-start | bytes 663560 | tf_op jit(solution)/shard_map/ppermute | solution.py:447
  19.9 1.2 %shard_map.86 = (f32[3,192,1]{2,1,0:T(8,128)S(1)}, f32[3,192,1]{2,1,0:T(8,128)S(1)}, f32[3,192,128]{2,1,0:T(8,128)S(1)}) custom-call(bf16[192,384]{1,0:T(8,128)(2,1)S(1)} %get-tuple-element.48.query, bf16[4,2,48,384]{3,2,1,0:T(8,128)(2,1)S(1)} %get-tuple-element.52.every, bf16[4,2,48,384]{3,2,1,0:T(8,128)(2,1)S(1)} %collective-permute-done.6.near, ...), custom_call_target="tpu_custom_call" | custom-call | flops 528482304 | bytes 2752512 | tf_op jit(solution)/shard_map/pallas_call | solution.py:278
  21.1 4.8 %collective-permute-done.5.some_far = bf16[3,2,48,384]{3,2,1,0:T(8,128)(2,1)S(1)} collective-permute-done((bf16[3,2,48,384]{3,2,1,0:T(8,128)(2,1)S(1)}, bf16[3,2,48,384]{3,2,1,0:T(8,128)(2,1)S(1)}, u32[]{:S(2)}, u32[]{:S(2)}) %collective-permute-start.5) | collective-permute-done | bytes 221216 | tf_op jit(solution)/shard_map/ppermute | solution.py:447
  25.9 0.5 collective-permute-start.7
  26.4 0.9 %shard_map.87 = (f32[3,192,1]{2,1,0:T(8,128)S(1)}, f32[3,192,1]{2,1,0:T(8,128)S(1)}, f32[3,192,128]{2,1,0:T(8,128)S(1)}) custom-call(bf16[192,384]{1,0:T(8,128)(2,1)S(1)} %get-tuple-element.48.query, bf16[2,48,384]{2,1,0:T(8,128)(2,1)S(1)} %collective-permute-done.4.own_far, bf16[3,2,48,384]{3,2,1,0:T(8,128)(2,1)S(1)} %collective-permute-done.5.some_far, ...), custom_call_target="tpu_custom_call" | custom-call | flops 113246208 | bytes 589824 | tf_op jit(solution)/shard_map/pallas_call | solution.py:278
  27.7 1.1 %shard_map.88.own = bf16[192,384]{1,0:T(8,128)(2,1)S(1)} custom-call(bf16[192,384]{1,0:T(8,128)(2,1)S(1)} %get-tuple-element.48.query, bf16[2,48,384]{2,1,0:T(8,128)(2,1)S(1)} %collective-permute-done.7.own_corner, bf16[3,2,48,384]{3,2,1,0:T(8,128)(2,1)S(1)} %collective-permute-done.8.some_corner, bf16[4,2,192,384]{3,2,1,0:T(8,128)(2,1)S(1)} %get-tuple-element.47.stale, ...), custom_call_target="tpu_custom_call" | custom-call | flops 113246208 | bytes 589824 | tf_op jit(solution)/shard_map/pallas_call | solution.py:278
  28.8 2.9 %collective-permute-start.9 = (bf16[192,384]{1,0:T(8,128)(2,1)S(1)}, bf16[192,384]{1,0:T(8,128)(2,1)S(1)}, u32[]{:S(2)}, u32[]{:S(2)}) collective-permute-start(bf16[192,384]{1,0:T(8,128)(2,1)S(1)} %shard_map.88.own), channel_id=1, source_target_pairs={{0,16},{2,18},{4,20},{6,22},{8,24},{10,26},{12,28},{14,30},{16,0},... | collective-permute-start | bytes 442376 | tf_op jit(solution)/shard_map/ppermute | solution.py:447
  31.7 1.6 %collective-permute-start.10 = (bf16[192,384]{1,0:T(8,128)(2,1)S(1)}, bf16[192,384]{1,0:T(8,128)(2,1)S(1)}, u32[]{:S(2)}, u32[]{:S(2)}) collective-permute-start(bf16[192,384]{1,0:T(8,128)(2,1)S(1)} %shard_map.88.own), channel_id=1, source_target_pairs={{0,8},{2,10},{4,12},{6,14},{8,0},{10,2},{12,4},{14,6},{16,24},{18,... | collective-permute-start | bytes 442376 | tf_op jit(solution)/shard_map/ppermute | solution.py:447
  33.3 6.0 %collective-permute-done.9.second = bf16[192,384]{1,0:T(8,128)(2,1)S(1)} collective-permute-done((bf16[192,384]{1,0:T(8,128)(2,1)S(1)}, bf16[192,384]{1,0:T(8,128)(2,1)S(1)}, u32[]{:S(2)}, u32[]{:S(2)}) %collective-permute-start.9) | collective-permute-done | bytes 147488 | tf_op jit(solution)/shard_map/ppermute | solution.py:447
  39.3 0.6 %collective-permute-start.12 = (bf16[192,384]{1,0:T(8,128)(2,1)S(1)}, bf16[192,384]{1,0:T(8,128)(2,1)S(1)}, u32[]{:S(2)}, u32[]{:S(2)}) collective-permute-start(bf16[192,384]{1,0:T(8,128)(2,1)S(1)} %collective-permute-done.9.second), channel_id=1, source_target_pairs={{0,8},{2,10},{4,12},{6,14},{8,0},{10,2},{12,4},{14,6},{16,24},{18,... | collective-permute-start | bytes 442376 | tf_op jit(solution)/shard_map/ppermute | solution.py:447
  40.1 0.7 %shard_map.90.partial = f32[192,768]{1,0:T(8,128)S(1)} custom-call(bf16[192,384]{1,0:T(8,128)(2,1)S(1)} %shard_map.88.own, bf16[192,384]{1,0:T(8,128)(2,1)S(1)} %collective-permute-done.9.second, bf16[192,384]{1,0:T(8,128)(2,1)S(1)} %collective-permute-done.10.first, bf16[768,1536]{1,0:T(8,128)(2,1)S(1)} %shard_map.89.weight), custom_call_target="tpu_custom_call" | custom-call | flops 452984832 | bytes 589824 | tf_op jit(solution)/shard_map/pallas_call | solution.py:348
  40.9 3.8 %collective-permute-done.12.third = bf16[192,384]{1,0:T(8,128)(2,1)S(1)} collective-permute-done((bf16[192,384]{1,0:T(8,128)(2,1)S(1)}, bf16[192,384]{1,0:T(8,128)(2,1)S(1)}, u32[]{:S(2)}, u32[]{:S(2)}) %collective-permute-start.12) | collective-permute-done | bytes 147488 | tf_op jit(solution)/shard_map/ppermute | solution.py:447
  44.7 0.4 shard_map.91
  45.1 2.7 %collective-permute-start.13 = (bf16[48,768]{1,0:T(8,128)(2,1)S(1)}, bf16[48,768]{1,0:T(8,128)(2,1)S(1)}, u32[]{:S(2)}, u32[]{:S(2)}) collective-permute-start(bf16[48,768]{1,0:T(8,128)(2,1)S(1)} %get-tuple-element.63), channel_id=1, source_target_pairs={{0,16},{2,18},{4,20},{6,22},{8,24},{10,26},{12,28},{14,30},{16,0},... | collective-permute-start | bytes 221192 | tf_op jit(solution)/shard_map/ppermute | solution.py:447
  47.8 1.3 %collective-permute-start.15 = (bf16[48,768]{1,0:T(8,128)(2,1)S(1)}, bf16[48,768]{1,0:T(8,128)(2,1)S(1)}, u32[]{:S(2)}, u32[]{:S(2)}) collective-permute-start(bf16[48,768]{1,0:T(8,128)(2,1)S(1)} %get-tuple-element.67), channel_id=1, source_target_pairs={{0,24},{2,26},{4,28},{6,30},{8,16},{10,18},{12,20},{14,22},{16,8},... | collective-permute-start | bytes 221192 | tf_op jit(solution)/shard_map/ppermute | solution.py:447
  49.1 0.5 collective-permute-start.16
  49.6 2.8 %collective-permute-done.13.far = bf16[48,768]{1,0:T(8,128)(2,1)S(1)} collective-permute-done((bf16[48,768]{1,0:T(8,128)(2,1)S(1)}, bf16[48,768]{1,0:T(8,128)(2,1)S(1)}, u32[]{:S(2)}, u32[]{:S(2)}) %collective-permute-start.13) | collective-permute-done | bytes 73760 | tf_op jit(solution)/shard_map/ppermute | solution.py:447
  52.4 1.6 %collective-permute-start.14 = (bf16[48,768]{1,0:T(8,128)(2,1)S(1)}, bf16[48,768]{1,0:T(8,128)(2,1)S(1)}, u32[]{:S(2)}, u32[]{:S(2)}) collective-permute-start(bf16[48,768]{1,0:T(8,128)(2,1)S(1)} %get-tuple-element.66), channel_id=1, source_target_pairs={{0,1},{1,0},{2,3},{3,2},{4,5},{5,4},{6,7},{7,6},{8,9},{9,8},{10,11... | collective-permute-start | bytes 221192 | tf_op jit(solution)/shard_map/ppermute | solution.py:485
  53.9 0.2 collective-permute-done.15.far
  54.2 1.6 %collective-permute-start.17 = (bf16[48,768]{1,0:T(8,128)(2,1)S(1)}, bf16[48,768]{1,0:T(8,128)(2,1)S(1)}, u32[]{:S(2)}, u32[]{:S(2)}) collective-permute-start(bf16[48,768]{1,0:T(8,128)(2,1)S(1)} %get-tuple-element.70), channel_id=1, source_target_pairs={{0,1},{1,0},{2,3},{3,2},{4,5},{5,4},{6,7},{7,6},{8,9},{9,8},{10,11... | collective-permute-start | bytes 221192 | tf_op jit(solution)/shard_map/ppermute | solution.py:485
  55.9 0.9 %collective-permute-done.14.arrived_even = bf16[48,768]{1,0:T(8,128)(2,1)S(1)} collective-permute-done((bf16[48,768]{1,0:T(8,128)(2,1)S(1)}, bf16[48,768]{1,0:T(8,128)(2,1)S(1)}, u32[]{:S(2)}, u32[]{:S(2)}) %collective-permute-start.14) | collective-permute-done | bytes 73760 | tf_op jit(solution)/shard_map/ppermute | solution.py:485
  56.8 1.9 %collective-permute-done.17.arrived_odd = bf16[48,768]{1,0:T(8,128)(2,1)S(1)} collective-permute-done((bf16[48,768]{1,0:T(8,128)(2,1)S(1)}, bf16[48,768]{1,0:T(8,128)(2,1)S(1)}, u32[]{:S(2)}, u32[]{:S(2)}) %collective-permute-start.17) | collective-permute-done | bytes 73760 | tf_op jit(solution)/shard_map/ppermute | solution.py:485
  58.7 0.7 %shard_map.94 = bf16[48,1536]{1,0:T(8,128)(2,1)} custom-call(bf16[48,768]{1,0:T(8,128)(2,1)S(1)} %get-tuple-element.65.kept_even, bf16[48,768]{1,0:T(8,128)(2,1)S(1)} %collective-permute-done.14.arrived_even, bf16[48,768]{1,0:T(8,128)(2,1)S(1)} %get-tuple-element.69.kept_odd, bf16[48,768]{1,0:T(8,128)(2,1)S(1)} %collective-permute-done.17.arrived_odd, ...), custom_call_target="tpu_custom_call" | custom-call | flops 221184 | bytes 294912 | tf_op jit(solution)/shard_map/pallas_call | solution.py:427
  (27 shorter events, 1.0 us)
Async XLA Ops:
  0.0 18.1 %collective-permute-start.3 = (bf16[192,1536]{1,0:T(8,128)(2,1)}, bf16[192,1536]{1,0:T(8,128)(2,1)S(1)}, u32[]{:S(2)}, u32[]{:S(2)}) collective-permute-start(bf16[192,1536]{1,0:T(8,128)(2,1)} %bitcast.2), channel_id=1, source_target_pairs={{0,4},{2,6},{4,0},{6,2},{8,12},{10,14},{12,8},{14,10},{16,20},{18,... | collective-permute-start | bytes 1769480 | tf_op jit(solution)/shard_map/ppermute | solution.py:447
  5.3 11.6 %collective-permute-start = (bf16[3,48,384]{2,1,0:T(8,128)(2,1)}, bf16[3,48,384]{2,1,0:T(8,128)(2,1)S(1)}, u32[]{:S(2)}, u32[]{:S(2)}) collective-permute-start(bf16[3,48,384]{2,1,0:T(8,128)(2,1)} %get-tuple-element.39), channel_id=1, source_target_pairs={{0,16},{2,18},{4,20},{6,22},{8,24},{10,26},{12,28},{14,30},{16,0},... | collective-permute-start | bytes 331784 | tf_op jit(solution)/shard_map/ppermute | solution.py:447
  7.9 8.9 %collective-permute-start.1 = (bf16[3,48,384]{2,1,0:T(8,128)(2,1)}, bf16[3,48,384]{2,1,0:T(8,128)(2,1)S(1)}, u32[]{:S(2)}, u32[]{:S(2)}) collective-permute-start(bf16[3,48,384]{2,1,0:T(8,128)(2,1)} %get-tuple-element.40), channel_id=1, source_target_pairs={{0,24},{2,26},{4,28},{6,30},{8,16},{10,18},{12,20},{14,22},{16,8},... | collective-permute-start | bytes 331784 | tf_op jit(solution)/shard_map/ppermute | solution.py:447
  9.3 7.7 %collective-permute-start.2 = (bf16[3,48,384]{2,1,0:T(8,128)(2,1)}, bf16[3,48,384]{2,1,0:T(8,128)(2,1)S(1)}, u32[]{:S(2)}, u32[]{:S(2)}) collective-permute-start(bf16[3,48,384]{2,1,0:T(8,128)(2,1)} %get-tuple-element.41), channel_id=1, source_target_pairs={{0,8},{2,10},{4,12},{6,14},{8,0},{10,2},{12,4},{14,6},{16,24},{18,... | collective-permute-start | bytes 331784 | tf_op jit(solution)/shard_map/ppermute | solution.py:447
  9.5 7.5 %copy-start.1 = (bf16[3,48,384]{2,1,0:T(8,128)(2,1)S(1)}, bf16[3,48,384]{2,1,0:T(8,128)(2,1)}, u32[]{:S(2)}) copy-start(bf16[3,48,384]{2,1,0:T(8,128)(2,1)} %get-tuple-element.38.refs_0_) | copy-start | bytes 331780
  9.5 10.3 %copy-start = (bf16[1536,192]{0,1:T(8,128)(2,1)S(1)}, bf16[1536,192]{0,1:T(8,128)(2,1)}, u32[]{:S(2)}) copy-start(bf16[1536,192]{0,1:T(8,128)(2,1)} %param.13) | copy-start | bytes 1769476
  9.5 8.5 %collective-permute-start.4 = (bf16[2,48,384]{2,1,0:T(8,128)(2,1)}, bf16[2,48,384]{2,1,0:T(8,128)(2,1)S(1)}, u32[]{:S(2)}, u32[]{:S(2)}) collective-permute-start(bf16[2,48,384]{2,1,0:T(8,128)(2,1)} %get-tuple-element.45), channel_id=1, source_target_pairs={{0,4},{2,6},{4,0},{6,2},{8,12},{10,14},{12,8},{14,10},{16,20},{18,... | collective-permute-start | bytes 221192 | tf_op jit(solution)/shard_map/ppermute | solution.py:447
  18.1 1.8 %collective-permute-start.6 = (bf16[4,2,48,384]{3,2,1,0:T(8,128)(2,1)S(1)}, bf16[4,2,48,384]{3,2,1,0:T(8,128)(2,1)S(1)}, u32[]{:S(2)}, u32[]{:S(2)}) collective-permute-start(bf16[4,2,48,384]{3,2,1,0:T(8,128)(2,1)S(1)} %get-tuple-element.52.every), channel_id=1, source_target_pairs={{0,2},{2,0},{4,6},{6,4},{8,10},{10,8},{12,14},{14,12},{16,18},{18,... | collective-permute-start | bytes 884744 | tf_op jit(solution)/shard_map/ppermute | solution.py:447
  18.1 7.8 %collective-permute-start.5 = (bf16[3,2,48,384]{3,2,1,0:T(8,128)(2,1)S(1)}, bf16[3,2,48,384]{3,2,1,0:T(8,128)(2,1)S(1)}, u32[]{:S(2)}, u32[]{:S(2)}) collective-permute-start(bf16[3,2,48,384]{3,2,1,0:T(8,128)(2,1)S(1)} %get-tuple-element.49), channel_id=1, source_target_pairs={{0,4},{2,6},{4,0},{6,2},{8,12},{10,14},{12,8},{14,10},{16,20},{18,... | collective-permute-start | bytes 663560 | tf_op jit(solution)/shard_map/ppermute | solution.py:447
  25.9 1.6 %collective-permute-start.8 = (bf16[3,2,48,384]{3,2,1,0:T(8,128)(2,1)S(1)}, bf16[3,2,48,384]{3,2,1,0:T(8,128)(2,1)S(1)}, u32[]{:S(2)}, u32[]{:S(2)}) collective-permute-start(bf16[3,2,48,384]{3,2,1,0:T(8,128)(2,1)S(1)} %collective-permute-done.5.some_far), channel_id=1, source_target_pairs={{0,2},{2,0},{4,6},{6,4},{8,10},{10,8},{12,14},{14,12},{16,18},{18,... | collective-permute-start | bytes 663560 | tf_op jit(solution)/shard_map/ppermute | solution.py:447
  25.9 1.6 %collective-permute-start.7 = (bf16[2,48,384]{2,1,0:T(8,128)(2,1)S(1)}, bf16[2,48,384]{2,1,0:T(8,128)(2,1)S(1)}, u32[]{:S(2)}, u32[]{:S(2)}) collective-permute-start(bf16[2,48,384]{2,1,0:T(8,128)(2,1)S(1)} %collective-permute-done.4.own_far), channel_id=1, source_target_pairs={{0,2},{2,0},{4,6},{6,4},{8,10},{10,8},{12,14},{14,12},{16,18},{18,... | collective-permute-start | bytes 221192 | tf_op jit(solution)/shard_map/ppermute | solution.py:447
  27.5 12.5 %collective-permute-start.11 = (bf16[2,192,1536]{2,1,0:T(8,128)(2,1)S(1)}, bf16[2,192,1536]{2,1,0:T(8,128)(2,1)S(1)}, u32[]{:S(2)}, u32[]{:S(2)}) collective-permute-start(bf16[2,192,1536]{2,1,0:T(8,128)(2,1)S(1)} %shard_map.85.own), channel_id=1, source_target_pairs={{0,2},{2,0},{4,6},{6,4},{8,10},{10,8},{12,14},{14,12},{16,18},{18,... | collective-permute-start | bytes 3538952 | tf_op jit(solution)/shard_map/ppermute | solution.py:447
  28.8 10.5 %collective-permute-start.9 = (bf16[192,384]{1,0:T(8,128)(2,1)S(1)}, bf16[192,384]{1,0:T(8,128)(2,1)S(1)}, u32[]{:S(2)}, u32[]{:S(2)}) collective-permute-start(bf16[192,384]{1,0:T(8,128)(2,1)S(1)} %shard_map.88.own), channel_id=1, source_target_pairs={{0,16},{2,18},{4,20},{6,22},{8,24},{10,26},{12,28},{14,30},{16,0},... | collective-permute-start | bytes 442376 | tf_op jit(solution)/shard_map/ppermute | solution.py:447
  31.7 8.4 %collective-permute-start.10 = (bf16[192,384]{1,0:T(8,128)(2,1)S(1)}, bf16[192,384]{1,0:T(8,128)(2,1)S(1)}, u32[]{:S(2)}, u32[]{:S(2)}) collective-permute-start(bf16[192,384]{1,0:T(8,128)(2,1)S(1)} %shard_map.88.own), channel_id=1, source_target_pairs={{0,8},{2,10},{4,12},{6,14},{8,0},{10,2},{12,4},{14,6},{16,24},{18,... | collective-permute-start | bytes 442376 | tf_op jit(solution)/shard_map/ppermute | solution.py:447
  39.3 5.4 %collective-permute-start.12 = (bf16[192,384]{1,0:T(8,128)(2,1)S(1)}, bf16[192,384]{1,0:T(8,128)(2,1)S(1)}, u32[]{:S(2)}, u32[]{:S(2)}) collective-permute-start(bf16[192,384]{1,0:T(8,128)(2,1)S(1)} %collective-permute-done.9.second), channel_id=1, source_target_pairs={{0,8},{2,10},{4,12},{6,14},{8,0},{10,2},{12,4},{14,6},{16,24},{18,... | collective-permute-start | bytes 442376 | tf_op jit(solution)/shard_map/ppermute | solution.py:447
  40.9 15.0 %copy-start.2 = (f32[1536]{0:T(1024)S(1)}, f32[1536]{0:T(1024)}, u32[]{:S(2)}) copy-start(f32[1536]{0:T(1024)} %param.14) | copy-start | bytes 18436
  40.9 15.0 %copy-start.3 = (f32[1536]{0:T(1024)S(1)}, f32[1536]{0:T(1024)}, u32[]{:S(2)}) copy-start(f32[1536]{0:T(1024)} %param.15) | copy-start | bytes 18436
  45.1 7.2 %collective-permute-start.13 = (bf16[48,768]{1,0:T(8,128)(2,1)S(1)}, bf16[48,768]{1,0:T(8,128)(2,1)S(1)}, u32[]{:S(2)}, u32[]{:S(2)}) collective-permute-start(bf16[48,768]{1,0:T(8,128)(2,1)S(1)} %get-tuple-element.63), channel_id=1, source_target_pairs={{0,16},{2,18},{4,20},{6,22},{8,24},{10,26},{12,28},{14,30},{16,0},... | collective-permute-start | bytes 221192 | tf_op jit(solution)/shard_map/ppermute | solution.py:447
  47.8 6.3 %collective-permute-start.15 = (bf16[48,768]{1,0:T(8,128)(2,1)S(1)}, bf16[48,768]{1,0:T(8,128)(2,1)S(1)}, u32[]{:S(2)}, u32[]{:S(2)}) collective-permute-start(bf16[48,768]{1,0:T(8,128)(2,1)S(1)} %get-tuple-element.67), channel_id=1, source_target_pairs={{0,24},{2,26},{4,28},{6,30},{8,16},{10,18},{12,20},{14,22},{16,8},... | collective-permute-start | bytes 221192 | tf_op jit(solution)/shard_map/ppermute | solution.py:447
  49.1 5.1 %collective-permute-start.16 = (bf16[48,768]{1,0:T(8,128)(2,1)S(1)}, bf16[48,768]{1,0:T(8,128)(2,1)S(1)}, u32[]{:S(2)}, u32[]{:S(2)}) collective-permute-start(bf16[48,768]{1,0:T(8,128)(2,1)S(1)} %get-tuple-element.68), channel_id=1, source_target_pairs={{0,8},{2,10},{4,12},{6,14},{8,0},{10,2},{12,4},{14,6},{16,24},{18,... | collective-permute-start | bytes 221192 | tf_op jit(solution)/shard_map/ppermute | solution.py:447
  52.4 4.4 %collective-permute-start.14 = (bf16[48,768]{1,0:T(8,128)(2,1)S(1)}, bf16[48,768]{1,0:T(8,128)(2,1)S(1)}, u32[]{:S(2)}, u32[]{:S(2)}) collective-permute-start(bf16[48,768]{1,0:T(8,128)(2,1)S(1)} %get-tuple-element.66), channel_id=1, source_target_pairs={{0,1},{1,0},{2,3},{3,2},{4,5},{5,4},{6,7},{7,6},{8,9},{9,8},{10,11... | collective-permute-start | bytes 221192 | tf_op jit(solution)/shard_map/ppermute | solution.py:485
  54.2 4.4 %collective-permute-start.17 = (bf16[48,768]{1,0:T(8,128)(2,1)S(1)}, bf16[48,768]{1,0:T(8,128)(2,1)S(1)}, u32[]{:S(2)}, u32[]{:S(2)}) collective-permute-start(bf16[48,768]{1,0:T(8,128)(2,1)S(1)} %get-tuple-element.70), channel_id=1, source_target_pairs={{0,1},{1,0},{2,3},{3,2},{4,5},{5,4},{6,7},{7,6},{8,9},{9,8},{10,11... | collective-permute-start | bytes 221192 | tf_op jit(solution)/shard_map/ppermute | solution.py:485

commit v20 on v19

--- a/solution.py
+++ b/solution.py
@@ -167,25 +167,27 @@
 
 
 def merge_kernel(*refs):
-    parts, (every, some, query) = refs[:-3], refs[-3:]
+    parts, (every, some, left, right, query) = refs[:-5], refs[-5:]
     groups, kinds, rows, _ = every.shape
     group, _ = place()
     for position, part in enumerate(parts):
         every[position] = part[0:kinds]
         if position:
             some[position - 1] = part[0:kinds]
+        (left, right)[position // 2][position % 2] = part[0:kinds]
         origin = jnp.bitwise_xor(group, TURNS[position])
         query[pl.ds(aligned(origin, rows), rows), :] = part[kinds]
 
 
 def merge(parts):
     kinds, rows, width = parts[0].shape
-    shapes = [(len(parts), kinds - 1, rows, width), (len(parts) - 1, kinds - 1, rows, width), (len(parts) * rows, width)]
+    counts = (len(parts), len(parts) - 1, len(parts) // 2, len(parts) // 2)
+    shapes = [(count, kinds - 1, rows, width) for count in counts] + [(len(parts) * rows, width)]
     return pl.pallas_call(
         merge_kernel,
         out_shape=[jax.ShapeDtypeStruct(shape, jnp.bfloat16) for shape in shapes],
         in_specs=[VMEM] * len(parts),
-        out_specs=[VMEM] * 3,
+        out_specs=[VMEM] * 5,
         compiler_params=pltpu.CompilerParams(vmem_limit_bytes=SMALL),
         cost_estimate=pl.CostEstimate(flops=0, bytes_accessed=4 * len(parts) * parts[0].size, transcendentals=0),
     )(*parts)
@@ -241,13 +243,18 @@
     return lambda kind, cols: part[:, kind, :, cols].reshape(-1, HD)
 
 
+def halves_part(*parts):
+    wholes = [whole_part(part) for part in parts]
+    return lambda kind, cols: jnp.concatenate([whole(kind, cols) for whole in wholes], axis=0)
+
+
 def split_part(own, some):
     return lambda kind, cols: jnp.concatenate([own[kind, :, cols], some[:, kind, :, cols].reshape(-1, HD)], axis=0)
 
 
-def near_kernel(query, every, near, text, stale, peak, total, mixed):
+def near_kernel(query, every, left, right, text, stale, peak, total, mixed):
     heads = columns_of(query.shape[1])
-    images = [image_segment(stale, 0, whole_part(every)), image_segment(stale, 1, whole_part(near))]
+    images = [image_segment(stale, 0, whole_part(every)), image_segment(stale, 1, halves_part(left, right))]
     segments = [[(text[0, :, cols], text[1, :, cols])] + [image(cols) for image in images] for cols in heads]
     states = absorb([query[:, cols] for cols in heads], segments, None)
     for head, state in enumerate(states):
@@ -454,14 +461,14 @@
     *packed, own = pack(groups, queries, codes, exponents)
     text, stale = pick(groups, text_kv, stale_kv)
 
-    every, some, query = merge([packed[0], *along(packed)])
+    every, some, left, right, query = merge([packed[0], *along(packed)])
     own_far = swap(own, 2)
 
-    ready = (every, some, query, weight, weight_far, own_far, text, stale)
-    every, some, query, weight, weight_far = lax.optimization_barrier(ready)[:5]
-    near, some_far = swap(every, 1), swap(some, 2)
+    ready = (every, some, left, right, query, weight, weight_far, own_far, text, stale)
+    every, some, left, right, query, weight, weight_far = lax.optimization_barrier(ready)[:7]
+    left, right, some_far = swap(left, 1), swap(right, 1), swap(some, 2)
     share = stale.shape[2]
-    operands = [query, every, near, text, stale]
+    operands = [query, every, left, right, text, stale]
     state = attend_call(near_kernel, operands, state_shapes(query), 2 * share + text.shape[1])
 
     ready = (some_far, own_far, stack(weight, weight_far), *state)

time: 59.6 us -> 59.7 us (level)
  starting transfers between devices: 22.9 us -> 20.5 us
  waiting for transfers between devices: 27 us -> 29.4 us
    ppermute x16 -> x17, waiting for transfers between devices: 24.2 us -> 25.6 us  [swap(): return lax.ppermute(value, 'patch', [(p, p ^ twist) for p in range(size)])]
    ppermute x16 -> x17, starting transfers between devices: 19.7 us -> 18.4 us  [swap(): return lax.ppermute(value, 'patch', [(p, p ^ twist) for p in range(size)])]
    ppermute x2, waiting for transfers between devices: 2.8 us -> 3.81 us  [grouped_body(): pieces += [kept, lax.ppermute(sent, 'head', [(0, 1), (1, 0)])]]
    ppermute x2, starting transfers between devices: 3.13 us -> 2.15 us  [grouped_body(): pieces += [kept, lax.ppermute(sent, 'head', [(0, 1), (1, 0)])]]
  transfers between devices with their start and end apart: 18 -> 19, of which waited for: 12 -> 13; matrix products, arithmetic and copies ran while one was open for 0% -> 0% of each run, Pallas kernels for 14% -> 14%
where the time goes in v20:
time: 59.7 us; the launch traced here: 59.5 us
  waiting for transfers between devices  29.4 us (49%)
  starting transfers between devices  20.5 us (34%)
  Pallas kernels  9.34 us (16%)
    ppermute x17, waiting for transfers between devices, swap(): return lax.ppermute(value, 'patch', [(p, p ^ twist) for p in range(size)])  25.6 us
    ppermute x17, starting transfers between devices, swap(): return lax.ppermute(value, 'patch', [(p, p ^ twist) for p in range(size)])  18.4 us
    ppermute x2, waiting for transfers between devices, grouped_body(): pieces += [kept, lax.ppermute(sent, 'head', [(0, 1), (1, 0)])]  3.81 us
    pallas_call x3, Pallas kernels, attend_call(): pl.pallas_call(kernel, out_shape=shapes, in_specs=[VMEM] * len(operands),...  3.19 us
    pallas_call x1, Pallas kernels, pack(): pl.pallas_call(pack_kernel, out_shape=[jax.ShapeDtypeStruct(shape, bf16)...  2.32 us
    ppermute x2, starting transfers between devices, grouped_body(): pieces += [kept, lax.ppermute(sent, 'head', [(0, 1), (1, 0)])]  2.15 us
    pallas_call x1, Pallas kernels, pick(): pl.pallas_call(pick_kernel, out_shape=[jax.ShapeDtypeStruct((kinds, texts...  1.65 us
  transfers between devices with their start and end apart: 19, of which 13 were waited for; matrix products, arithmetic and copies ran while one was open for 0% of the time, Pallas kernels for 14%

profile of v20, /device:TPU:0, one launch (start us, length us, event | category | flops | bytes accessed | tf_op | source)
XLA Modules:
  0.0 59.5 jit_solution(6691375225038093633)
XLA Ops:
  0.0 2.9 %collective-permute-start.3 = (bf16[192,1536]{1,0:T(8,128)(2,1)}, bf16[192,1536]{1,0:T(8,128)(2,1)S(1)}, u32[]{:S(2)}, u32[]{:S(2)}) collective-permute-start(bf16[192,1536]{1,0:T(8,128)(2,1)} %bitcast.2), channel_id=1, source_target_pairs={{0,4},{2,6},{4,0},{6,2},{8,12},{10,14},{12,8},{14,10},{16,20},{18,... | collective-permute-start | bytes 1769480 | tf_op jit(solution)/shard_map/ppermute | solution.py:454
  2.9 2.3 %shard_map.82 = (bf16[3,48,384]{2,1,0:T(8,128)(2,1)}, bf16[3,48,384]{2,1,0:T(8,128)(2,1)}, bf16[3,48,384]{2,1,0:T(8,128)(2,1)}, bf16[3,48,384]{2,1,0:T(8,128)(2,1)}, bf16[2,48,384]{2,1,0:T(8,128)(2,1)}) custom-call(bf16[48,1536]{1,0:T(8,128)(2,1)} %queries_hbm.1, s32[2,48,1536]{2,1,0:T(8,128)} %codes_hbm.1, s32[12,2,48]{2,1,0:T(2,128)} %bitcast.4), custom_call_target="tpu_custom_call" | custom-call | flops 294912 | bytes 884736 | tf_op jit(solution)/shard_map/pallas_call | solution.py:110
  5.3 2.7 %collective-permute-start = (bf16[3,48,384]{2,1,0:T(8,128)(2,1)}, bf16[3,48,384]{2,1,0:T(8,128)(2,1)S(1)}, u32[]{:S(2)}, u32[]{:S(2)}) collective-permute-start(bf16[3,48,384]{2,1,0:T(8,128)(2,1)} %get-tuple-element.43), channel_id=1, source_target_pairs={{0,16},{2,18},{4,20},{6,22},{8,24},{10,26},{12,28},{14,30},{16,0},... | collective-permute-start | bytes 331784 | tf_op jit(solution)/shard_map/ppermute | solution.py:454
  7.9 1.3 %collective-permute-start.1 = (bf16[3,48,384]{2,1,0:T(8,128)(2,1)}, bf16[3,48,384]{2,1,0:T(8,128)(2,1)S(1)}, u32[]{:S(2)}, u32[]{:S(2)}) collective-permute-start(bf16[3,48,384]{2,1,0:T(8,128)(2,1)} %get-tuple-element.44), channel_id=1, source_target_pairs={{0,24},{2,26},{4,28},{6,30},{8,16},{10,18},{12,20},{14,22},{16,8},... | collective-permute-start | bytes 331784 | tf_op jit(solution)/shard_map/ppermute | solution.py:454
  9.5 0.5 collective-permute-start.4
  10.0 1.7 %shard_map.84 = (bf16[2,512,384]{2,1,0:T(8,128)(2,1)S(1)}, bf16[4,2,192,384]{3,2,1,0:T(8,128)(2,1)S(1)}) custom-call(bf16[2,512,1536]{2,1,0:T(8,128)(2,1)} %text_hbm.1, bf16[2,768,1536]{2,1,0:T(8,128)(2,1)} %stale_hbm.1), custom_call_target="tpu_custom_call" | custom-call | bytes 8388608 | tf_op jit(solution)/shard_map/pallas_call | solution.py:155
  11.7 5.1 %collective-permute-done.refs_1_ = bf16[3,48,384]{2,1,0:T(8,128)(2,1)S(1)} collective-permute-done((bf16[3,48,384]{2,1,0:T(8,128)(2,1)}, bf16[3,48,384]{2,1,0:T(8,128)(2,1)S(1)}, u32[]{:S(2)}, u32[]{:S(2)}) %collective-permute-start) | collective-permute-done | bytes 110624 | tf_op jit(solution)/shard_map/ppermute | solution.py:454
  17.0 1.0 %collective-permute-done.4.own_far = bf16[2,48,384]{2,1,0:T(8,128)(2,1)S(1)} collective-permute-done((bf16[2,48,384]{2,1,0:T(8,128)(2,1)}, bf16[2,48,384]{2,1,0:T(8,128)(2,1)S(1)}, u32[]{:S(2)}, u32[]{:S(2)}) %collective-permute-start.4) | collective-permute-done | bytes 73760 | tf_op jit(solution)/shard_map/ppermute | solution.py:454
  18.1 1.7 %collective-permute-start.5 = (bf16[3,2,48,384]{3,2,1,0:T(8,128)(2,1)S(1)}, bf16[3,2,48,384]{3,2,1,0:T(8,128)(2,1)S(1)}, u32[]{:S(2)}, u32[]{:S(2)}) collective-permute-start(bf16[3,2,48,384]{3,2,1,0:T(8,128)(2,1)S(1)} %get-tuple-element.55), channel_id=1, source_target_pairs={{0,4},{2,6},{4,0},{6,2},{8,12},{10,14},{12,8},{14,10},{16,20},{18,... | collective-permute-start | bytes 663560 | tf_op jit(solution)/shard_map/ppermute | solution.py:454
  19.8 0.5 collective-permute-start.7
  20.4 0.8 %collective-permute-done.6.left = bf16[2,2,48,384]{3,2,1,0:T(8,128)(2,1)S(1)} collective-permute-done((bf16[2,2,48,384]{3,2,1,0:T(8,128)(2,1)S(1)}, bf16[2,2,48,384]{3,2,1,0:T(8,128)(2,1)S(1)}, u32[]{:S(2)}, u32[]{:S(2)}) %collective-permute-start.6) | collective-permute-done | bytes 147488 | tf_op jit(solution)/shard_map/ppermute | solution.py:454
  21.4 1.2 %shard_map.86 = (f32[3,192,1]{2,1,0:T(8,128)S(1)}, f32[3,192,1]{2,1,0:T(8,128)S(1)}, f32[3,192,128]{2,1,0:T(8,128)S(1)}) custom-call(bf16[192,384]{1,0:T(8,128)(2,1)S(1)} %get-tuple-element.54.query, bf16[4,2,48,384]{3,2,1,0:T(8,128)(2,1)S(1)} %get-tuple-element.58.every, bf16[2,2,48,384]{3,2,1,0:T(8,128)(2,1)S(1)} %collective-permute-done.6.left, ...), custom_call_target="tpu_custom_call" | custom-call | flops 528482304 | bytes 2752512 | tf_op jit(solution)/shard_map/pallas_call | solution.py:285
  22.6 2.1 %collective-permute-done.5.some_far = bf16[3,2,48,384]{3,2,1,0:T(8,128)(2,1)S(1)} collective-permute-done((bf16[3,2,48,384]{3,2,1,0:T(8,128)(2,1)S(1)}, bf16[3,2,48,384]{3,2,1,0:T(8,128)(2,1)S(1)}, u32[]{:S(2)}, u32[]{:S(2)}) %collective-permute-start.5) | collective-permute-done | bytes 221216 | tf_op jit(solution)/shard_map/ppermute | solution.py:454
  24.7 0.5 collective-permute-start.8
  25.2 0.9 %shard_map.87 = (f32[3,192,1]{2,1,0:T(8,128)S(1)}, f32[3,192,1]{2,1,0:T(8,128)S(1)}, f32[3,192,128]{2,1,0:T(8,128)S(1)}) custom-call(bf16[192,384]{1,0:T(8,128)(2,1)S(1)} %get-tuple-element.54.query, bf16[2,48,384]{2,1,0:T(8,128)(2,1)S(1)} %collective-permute-done.4.own_far, bf16[3,2,48,384]{3,2,1,0:T(8,128)(2,1)S(1)} %collective-permute-done.5.some_far, ...), custom_call_target="tpu_custom_call" | custom-call | flops 113246208 | bytes 589824 | tf_op jit(solution)/shard_map/pallas_call | solution.py:285
  26.5 1.1 %shard_map.88.own = bf16[192,384]{1,0:T(8,128)(2,1)S(1)} custom-call(bf16[192,384]{1,0:T(8,128)(2,1)S(1)} %get-tuple-element.54.query, bf16[2,48,384]{2,1,0:T(8,128)(2,1)S(1)} %collective-permute-done.8.own_corner, bf16[3,2,48,384]{3,2,1,0:T(8,128)(2,1)S(1)} %collective-permute-done.9.some_corner, bf16[4,2,192,384]{3,2,1,0:T(8,128)(2,1)S(1)} %get-tuple-element.53.stale, ...), custom_call_target="tpu_custom_call" | custom-call | flops 113246208 | bytes 589824 | tf_op jit(solution)/shard_map/pallas_call | solution.py:285
  27.6 3.6 %collective-permute-start.10 = (bf16[192,384]{1,0:T(8,128)(2,1)S(1)}, bf16[192,384]{1,0:T(8,128)(2,1)S(1)}, u32[]{:S(2)}, u32[]{:S(2)}) collective-permute-start(bf16[192,384]{1,0:T(8,128)(2,1)S(1)} %shard_map.88.own), channel_id=1, source_target_pairs={{0,16},{2,18},{4,20},{6,22},{8,24},{10,26},{12,28},{14,30},{16,0},... | collective-permute-start | bytes 442376 | tf_op jit(solution)/shard_map/ppermute | solution.py:454
  31.2 0.6 collective-permute-start.11
  31.7 7.0 %collective-permute-done.10.second = bf16[192,384]{1,0:T(8,128)(2,1)S(1)} collective-permute-done((bf16[192,384]{1,0:T(8,128)(2,1)S(1)}, bf16[192,384]{1,0:T(8,128)(2,1)S(1)}, u32[]{:S(2)}, u32[]{:S(2)}) %collective-permute-start.10) | collective-permute-done | bytes 147488 | tf_op jit(solution)/shard_map/ppermute | solution.py:454
  38.9 0.8 %collective-permute-done.11.first = bf16[192,384]{1,0:T(8,128)(2,1)S(1)} collective-permute-done((bf16[192,384]{1,0:T(8,128)(2,1)S(1)}, bf16[192,384]{1,0:T(8,128)(2,1)S(1)}, u32[]{:S(2)}, u32[]{:S(2)}) %collective-permute-start.11) | collective-permute-done | bytes 147488 | tf_op jit(solution)/shard_map/ppermute | solution.py:454
  39.7 0.7 %shard_map.90.partial = f32[192,768]{1,0:T(8,128)S(1)} custom-call(bf16[192,384]{1,0:T(8,128)(2,1)S(1)} %shard_map.88.own, bf16[192,384]{1,0:T(8,128)(2,1)S(1)} %collective-permute-done.10.second, bf16[192,384]{1,0:T(8,128)(2,1)S(1)} %collective-permute-done.11.first, bf16[768,1536]{1,0:T(8,128)(2,1)S(1)} %shard_map.89.weight), custom_call_target="tpu_custom_call" | custom-call | flops 452984832 | bytes 589824 | tf_op jit(solution)/shard_map/pallas_call | solution.py:355
  40.5 3.8 %collective-permute-done.13.third = bf16[192,384]{1,0:T(8,128)(2,1)S(1)} collective-permute-done((bf16[192,384]{1,0:T(8,128)(2,1)S(1)}, bf16[192,384]{1,0:T(8,128)(2,1)S(1)}, u32[]{:S(2)}, u32[]{:S(2)}) %collective-permute-start.13) | collective-permute-done | bytes 147488 | tf_op jit(solution)/shard_map/ppermute | solution.py:454
  44.3 0.4 shard_map.91
  44.7 1.2 %collective-permute-start.14 = (bf16[48,768]{1,0:T(8,128)(2,1)S(1)}, bf16[48,768]{1,0:T(8,128)(2,1)S(1)}, u32[]{:S(2)}, u32[]{:S(2)}) collective-permute-start(bf16[48,768]{1,0:T(8,128)(2,1)S(1)} %get-tuple-element.71), channel_id=1, source_target_pairs={{0,16},{2,18},{4,20},{6,22},{8,24},{10,26},{12,28},{14,30},{16,0},... | collective-permute-start | bytes 221192 | tf_op jit(solution)/shard_map/ppermute | solution.py:454
  45.8 1.5 %collective-permute-start.16 = (bf16[48,768]{1,0:T(8,128)(2,1)S(1)}, bf16[48,768]{1,0:T(8,128)(2,1)S(1)}, u32[]{:S(2)}, u32[]{:S(2)}) collective-permute-start(bf16[48,768]{1,0:T(8,128)(2,1)S(1)} %get-tuple-element.75), channel_id=1, source_target_pairs={{0,24},{2,26},{4,28},{6,30},{8,16},{10,18},{12,20},{14,22},{16,8},... | collective-permute-start | bytes 221192 | tf_op jit(solution)/shard_map/ppermute | solution.py:454
  47.4 0.8 %collective-permute-start.17 = (bf16[48,768]{1,0:T(8,128)(2,1)S(1)}, bf16[48,768]{1,0:T(8,128)(2,1)S(1)}, u32[]{:S(2)}, u32[]{:S(2)}) collective-permute-start(bf16[48,768]{1,0:T(8,128)(2,1)S(1)} %get-tuple-element.76), channel_id=1, source_target_pairs={{0,8},{2,10},{4,12},{6,14},{8,0},{10,2},{12,4},{14,6},{16,24},{18,... | collective-permute-start | bytes 221192 | tf_op jit(solution)/shard_map/ppermute | solution.py:454
  48.2 4.5 %collective-permute-done.14.far = bf16[48,768]{1,0:T(8,128)(2,1)S(1)} collective-permute-done((bf16[48,768]{1,0:T(8,128)(2,1)S(1)}, bf16[48,768]{1,0:T(8,128)(2,1)S(1)}, u32[]{:S(2)}, u32[]{:S(2)}) %collective-permute-start.14) | collective-permute-done | bytes 73760 | tf_op jit(solution)/shard_map/ppermute | solution.py:454
  52.7 1.6 %collective-permute-start.15 = (bf16[48,768]{1,0:T(8,128)(2,1)S(1)}, bf16[48,768]{1,0:T(8,128)(2,1)S(1)}, u32[]{:S(2)}, u32[]{:S(2)}) collective-permute-start(bf16[48,768]{1,0:T(8,128)(2,1)S(1)} %get-tuple-element.74), channel_id=1, source_target_pairs={{0,1},{1,0},{2,3},{3,2},{4,5},{5,4},{6,7},{7,6},{8,9},{9,8},{10,11... | collective-permute-start | bytes 221192 | tf_op jit(solution)/shard_map/ppermute | solution.py:492
  54.3 0.6 collective-permute-start.18
  54.9 2.2 %collective-permute-done.15.arrived_even = bf16[48,768]{1,0:T(8,128)(2,1)S(1)} collective-permute-done((bf16[48,768]{1,0:T(8,128)(2,1)S(1)}, bf16[48,768]{1,0:T(8,128)(2,1)S(1)}, u32[]{:S(2)}, u32[]{:S(2)}) %collective-permute-start.15) | collective-permute-done | bytes 73760 | tf_op jit(solution)/shard_map/ppermute | solution.py:492
  57.1 1.6 %collective-permute-done.18.arrived_odd = bf16[48,768]{1,0:T(8,128)(2,1)S(1)} collective-permute-done((bf16[48,768]{1,0:T(8,128)(2,1)S(1)}, bf16[48,768]{1,0:T(8,128)(2,1)S(1)}, u32[]{:S(2)}, u32[]{:S(2)}) %collective-permute-start.18) | collective-permute-done | bytes 73760 | tf_op jit(solution)/shard_map/ppermute | solution.py:492
  58.7 0.7 %shard_map.94 = bf16[48,1536]{1,0:T(8,128)(2,1)} custom-call(bf16[48,768]{1,0:T(8,128)(2,1)S(1)} %get-tuple-element.73.kept_even, bf16[48,768]{1,0:T(8,128)(2,1)S(1)} %collective-permute-done.15.arrived_even, bf16[48,768]{1,0:T(8,128)(2,1)S(1)} %get-tuple-element.77.kept_odd, bf16[48,768]{1,0:T(8,128)(2,1)S(1)} %collective-permute-done.18.arrived_odd, ...), custom_call_target="tpu_custom_call" | custom-call | flops 221184 | bytes 294912 | tf_op jit(solution)/shard_map/pallas_call | solution.py:434
  (29 shorter events, 1.4 us)
Async XLA Ops:
  0.0 18.1 %collective-permute-start.3 = (bf16[192,1536]{1,0:T(8,128)(2,1)}, bf16[192,1536]{1,0:T(8,128)(2,1)S(1)}, u32[]{:S(2)}, u32[]{:S(2)}) collective-permute-start(bf16[192,1536]{1,0:T(8,128)(2,1)} %bitcast.2), channel_id=1, source_target_pairs={{0,4},{2,6},{4,0},{6,2},{8,12},{10,14},{12,8},{14,10},{16,20},{18,... | collective-permute-start | bytes 1769480 | tf_op jit(solution)/shard_map/ppermute | solution.py:454
  5.3 11.6 %collective-permute-start = (bf16[3,48,384]{2,1,0:T(8,128)(2,1)}, bf16[3,48,384]{2,1,0:T(8,128)(2,1)S(1)}, u32[]{:S(2)}, u32[]{:S(2)}) collective-permute-start(bf16[3,48,384]{2,1,0:T(8,128)(2,1)} %get-tuple-element.43), channel_id=1, source_target_pairs={{0,16},{2,18},{4,20},{6,22},{8,24},{10,26},{12,28},{14,30},{16,0},... | collective-permute-start | bytes 331784 | tf_op jit(solution)/shard_map/ppermute | solution.py:454
  7.9 8.9 %collective-permute-start.1 = (bf16[3,48,384]{2,1,0:T(8,128)(2,1)}, bf16[3,48,384]{2,1,0:T(8,128)(2,1)S(1)}, u32[]{:S(2)}, u32[]{:S(2)}) collective-permute-start(bf16[3,48,384]{2,1,0:T(8,128)(2,1)} %get-tuple-element.44), channel_id=1, source_target_pairs={{0,24},{2,26},{4,28},{6,30},{8,16},{10,18},{12,20},{14,22},{16,8},... | collective-permute-start | bytes 331784 | tf_op jit(solution)/shard_map/ppermute | solution.py:454
  9.3 7.7 %collective-permute-start.2 = (bf16[3,48,384]{2,1,0:T(8,128)(2,1)}, bf16[3,48,384]{2,1,0:T(8,128)(2,1)S(1)}, u32[]{:S(2)}, u32[]{:S(2)}) collective-permute-start(bf16[3,48,384]{2,1,0:T(8,128)(2,1)} %get-tuple-element.45), channel_id=1, source_target_pairs={{0,8},{2,10},{4,12},{6,14},{8,0},{10,2},{12,4},{14,6},{16,24},{18,... | collective-permute-start | bytes 331784 | tf_op jit(solution)/shard_map/ppermute | solution.py:454
  9.5 7.5 %copy-start.1 = (bf16[3,48,384]{2,1,0:T(8,128)(2,1)S(1)}, bf16[3,48,384]{2,1,0:T(8,128)(2,1)}, u32[]{:S(2)}) copy-start(bf16[3,48,384]{2,1,0:T(8,128)(2,1)} %get-tuple-element.42.refs_0_) | copy-start | bytes 331780
  9.5 10.8 %copy-start = (bf16[1536,192]{0,1:T(8,128)(2,1)S(1)}, bf16[1536,192]{0,1:T(8,128)(2,1)}, u32[]{:S(2)}) copy-start(bf16[1536,192]{0,1:T(8,128)(2,1)} %param.13) | copy-start | bytes 1769476
  9.5 8.6 %collective-permute-start.4 = (bf16[2,48,384]{2,1,0:T(8,128)(2,1)}, bf16[2,48,384]{2,1,0:T(8,128)(2,1)S(1)}, u32[]{:S(2)}, u32[]{:S(2)}) collective-permute-start(bf16[2,48,384]{2,1,0:T(8,128)(2,1)} %get-tuple-element.51), channel_id=1, source_target_pairs={{0,4},{2,6},{4,0},{6,2},{8,12},{10,14},{12,8},{14,10},{16,20},{18,... | collective-permute-start | bytes 221192 | tf_op jit(solution)/shard_map/ppermute | solution.py:454
  18.1 6.6 %collective-permute-start.5 = (bf16[3,2,48,384]{3,2,1,0:T(8,128)(2,1)S(1)}, bf16[3,2,48,384]{3,2,1,0:T(8,128)(2,1)S(1)}, u32[]{:S(2)}, u32[]{:S(2)}) collective-permute-start(bf16[3,2,48,384]{3,2,1,0:T(8,128)(2,1)S(1)} %get-tuple-element.55), channel_id=1, source_target_pairs={{0,4},{2,6},{4,0},{6,2},{8,12},{10,14},{12,8},{14,10},{16,20},{18,... | collective-permute-start | bytes 663560 | tf_op jit(solution)/shard_map/ppermute | solution.py:454
  19.8 1.4 %collective-permute-start.6 = (bf16[2,2,48,384]{3,2,1,0:T(8,128)(2,1)S(1)}, bf16[2,2,48,384]{3,2,1,0:T(8,128)(2,1)S(1)}, u32[]{:S(2)}, u32[]{:S(2)}) collective-permute-start(bf16[2,2,48,384]{3,2,1,0:T(8,128)(2,1)S(1)} %get-tuple-element.59), channel_id=1, source_target_pairs={{0,2},{2,0},{4,6},{6,4},{8,10},{10,8},{12,14},{14,12},{16,18},{18,... | collective-permute-start | bytes 442376 | tf_op jit(solution)/shard_map/ppermute | solution.py:454
  19.8 1.6 %collective-permute-start.7 = (bf16[2,2,48,384]{3,2,1,0:T(8,128)(2,1)S(1)}, bf16[2,2,48,384]{3,2,1,0:T(8,128)(2,1)S(1)}, u32[]{:S(2)}, u32[]{:S(2)}) collective-permute-start(bf16[2,2,48,384]{3,2,1,0:T(8,128)(2,1)S(1)} %get-tuple-element.60), channel_id=1, source_target_pairs={{0,2},{2,0},{4,6},{6,4},{8,10},{10,8},{12,14},{14,12},{16,18},{18,... | collective-permute-start | bytes 442376 | tf_op jit(solution)/shard_map/ppermute | solution.py:454
  24.7 1.6 %collective-permute-start.9 = (bf16[3,2,48,384]{3,2,1,0:T(8,128)(2,1)S(1)}, bf16[3,2,48,384]{3,2,1,0:T(8,128)(2,1)S(1)}, u32[]{:S(2)}, u32[]{:S(2)}) collective-permute-start(bf16[3,2,48,384]{3,2,1,0:T(8,128)(2,1)S(1)} %collective-permute-done.5.some_far), channel_id=1, source_target_pairs={{0,2},{2,0},{4,6},{6,4},{8,10},{10,8},{12,14},{14,12},{16,18},{18,... | collective-permute-start | bytes 663560 | tf_op jit(solution)/shard_map/ppermute | solution.py:454
  24.7 1.6 %collective-permute-start.8 = (bf16[2,48,384]{2,1,0:T(8,128)(2,1)S(1)}, bf16[2,48,384]{2,1,0:T(8,128)(2,1)S(1)}, u32[]{:S(2)}, u32[]{:S(2)}) collective-permute-start(bf16[2,48,384]{2,1,0:T(8,128)(2,1)S(1)} %collective-permute-done.4.own_far), channel_id=1, source_target_pairs={{0,2},{2,0},{4,6},{6,4},{8,10},{10,8},{12,14},{14,12},{16,18},{18,... | collective-permute-start | bytes 221192 | tf_op jit(solution)/shard_map/ppermute | solution.py:454
  26.3 12.5 %collective-permute-start.12 = (bf16[2,192,1536]{2,1,0:T(8,128)(2,1)S(1)}, bf16[2,192,1536]{2,1,0:T(8,128)(2,1)S(1)}, u32[]{:S(2)}, u32[]{:S(2)}) collective-permute-start(bf16[2,192,1536]{2,1,0:T(8,128)(2,1)S(1)} %shard_map.85.own), channel_id=1, source_target_pairs={{0,2},{2,0},{4,6},{6,4},{8,10},{10,8},{12,14},{14,12},{16,18},{18,... | collective-permute-start | bytes 3538952 | tf_op jit(solution)/shard_map/ppermute | solution.py:454
  27.6 11.2 %collective-permute-start.10 = (bf16[192,384]{1,0:T(8,128)(2,1)S(1)}, bf16[192,384]{1,0:T(8,128)(2,1)S(1)}, u32[]{:S(2)}, u32[]{:S(2)}) collective-permute-start(bf16[192,384]{1,0:T(8,128)(2,1)S(1)} %shard_map.88.own), channel_id=1, source_target_pairs={{0,16},{2,18},{4,20},{6,22},{8,24},{10,26},{12,28},{14,30},{16,0},... | collective-permute-start | bytes 442376 | tf_op jit(solution)/shard_map/ppermute | solution.py:454
  31.2 8.6 %collective-permute-start.11 = (bf16[192,384]{1,0:T(8,128)(2,1)S(1)}, bf16[192,384]{1,0:T(8,128)(2,1)S(1)}, u32[]{:S(2)}, u32[]{:S(2)}) collective-permute-start(bf16[192,384]{1,0:T(8,128)(2,1)S(1)} %shard_map.88.own), channel_id=1, source_target_pairs={{0,8},{2,10},{4,12},{6,14},{8,0},{10,2},{12,4},{14,6},{16,24},{18,... | collective-permute-start | bytes 442376 | tf_op jit(solution)/shard_map/ppermute | solution.py:454
  38.8 5.5 %collective-permute-start.13 = (bf16[192,384]{1,0:T(8,128)(2,1)S(1)}, bf16[192,384]{1,0:T(8,128)(2,1)S(1)}, u32[]{:S(2)}, u32[]{:S(2)}) collective-permute-start(bf16[192,384]{1,0:T(8,128)(2,1)S(1)} %collective-permute-done.10.second), channel_id=1, source_target_pairs={{0,8},{2,10},{4,12},{6,14},{8,0},{10,2},{12,4},{14,6},{16,24},{18,... | collective-permute-start | bytes 442376 | tf_op jit(solution)/shard_map/ppermute | solution.py:454
  40.5 14.4 %copy-start.2 = (f32[1536]{0:T(1024)S(1)}, f32[1536]{0:T(1024)}, u32[]{:S(2)}) copy-start(f32[1536]{0:T(1024)} %param.14) | copy-start | bytes 18436
  40.5 14.4 %copy-start.3 = (f32[1536]{0:T(1024)S(1)}, f32[1536]{0:T(1024)}, u32[]{:S(2)}) copy-start(f32[1536]{0:T(1024)} %param.15) | copy-start | bytes 18436
  44.7 8.0 %collective-permute-start.14 = (bf16[48,768]{1,0:T(8,128)(2,1)S(1)}, bf16[48,768]{1,0:T(8,128)(2,1)S(1)}, u32[]{:S(2)}, u32[]{:S(2)}) collective-permute-start(bf16[48,768]{1,0:T(8,128)(2,1)S(1)} %get-tuple-element.71), channel_id=1, source_target_pairs={{0,16},{2,18},{4,20},{6,22},{8,24},{10,26},{12,28},{14,30},{16,0},... | collective-permute-start | bytes 221192 | tf_op jit(solution)/shard_map/ppermute | solution.py:454
  45.8 8.4 %collective-permute-start.16 = (bf16[48,768]{1,0:T(8,128)(2,1)S(1)}, bf16[48,768]{1,0:T(8,128)(2,1)S(1)}, u32[]{:S(2)}, u32[]{:S(2)}) collective-permute-start(bf16[48,768]{1,0:T(8,128)(2,1)S(1)} %get-tuple-element.75), channel_id=1, source_target_pairs={{0,24},{2,26},{4,28},{6,30},{8,16},{10,18},{12,20},{14,22},{16,8},... | collective-permute-start | bytes 221192 | tf_op jit(solution)/shard_map/ppermute | solution.py:454
  47.4 6.9 %collective-permute-start.17 = (bf16[48,768]{1,0:T(8,128)(2,1)S(1)}, bf16[48,768]{1,0:T(8,128)(2,1)S(1)}, u32[]{:S(2)}, u32[]{:S(2)}) collective-permute-start(bf16[48,768]{1,0:T(8,128)(2,1)S(1)} %get-tuple-element.76), channel_id=1, source_target_pairs={{0,8},{2,10},{4,12},{6,14},{8,0},{10,2},{12,4},{14,6},{16,24},{18,... | collective-permute-start | bytes 221192 | tf_op jit(solution)/shard_map/ppermute | solution.py:454
  52.7 4.4 %collective-permute-start.15 = (bf16[48,768]{1,0:T(8,128)(2,1)S(1)}, bf16[48,768]{1,0:T(8,128)(2,1)S(1)}, u32[]{:S(2)}, u32[]{:S(2)}) collective-permute-start(bf16[48,768]{1,0:T(8,128)(2,1)S(1)} %get-tuple-element.74), channel_id=1, source_target_pairs={{0,1},{1,0},{2,3},{3,2},{4,5},{5,4},{6,7},{7,6},{8,9},{9,8},{10,11... | collective-permute-start | bytes 221192 | tf_op jit(solution)/shard_map/ppermute | solution.py:492
  54.3 4.4 %collective-permute-start.18 = (bf16[48,768]{1,0:T(8,128)(2,1)S(1)}, bf16[48,768]{1,0:T(8,128)(2,1)S(1)}, u32[]{:S(2)}, u32[]{:S(2)}) collective-permute-start(bf16[48,768]{1,0:T(8,128)(2,1)S(1)} %get-tuple-element.78), channel_id=1, source_target_pairs={{0,1},{1,0},{2,3},{3,2},{4,5},{5,4},{6,7},{7,6},{8,9},{9,8},{10,11... | collective-permute-start | bytes 221192 | tf_op jit(solution)/shard_map/ppermute | solution.py:492

commit v21 on v20

--- a/solution.py
+++ b/solution.py
@@ -388,58 +388,51 @@
     )(partial, third, weight)
 
 
-def at_home(group):
-    return group // TURNS[1] == lax.axis_index("head")
-
-
-def divide_kernel(far, near, keep, send):
+def divide_kernel(*refs):
+    parts, (keep, send, held) = refs[:-3], refs[-3:]
     group, _ = place()
-
-    @pl.when(at_home(group))
-    def _():
-        keep[...] = near[...]
-        send[...] = far[...]
-
-    @pl.when(jnp.logical_not(at_home(group)))
-    def _():
-        keep[...] = far[...]
-        send[...] = near[...]
-
-
-def divide(far, near):
+    half = lax.axis_index("head")
+    blocks = keep.shape[0]
+    for position, part in enumerate(parts):
+        held[jnp.bitwise_xor(group, TURNS[position])] = part[...]
+    for block in range(blocks):
+        keep[block] = held[half * blocks + block]
+        send[block] = held[(1 - half) * blocks + block]
+
+
+def divide(parts):
+    groups = len(parts)
+    shape = jax.ShapeDtypeStruct((groups // 2, *parts[0].shape), jnp.bfloat16)
     return pl.pallas_call(
         divide_kernel,
-        out_shape=[jax.ShapeDtypeStruct(near.shape, near.dtype)] * 2,
-        in_specs=[VMEM] * 2,
+        out_shape=[shape] * 2,
+        in_specs=[VMEM] * groups,
         out_specs=[VMEM] * 2,
-        compiler_params=pltpu.CompilerParams(vmem_limit_bytes=SMALL),
-        cost_estimate=pl.CostEstimate(flops=0, bytes_accessed=8 * near.size, transcendentals=0),
-    )(far, near)
-
-
-def finish_kernel(kept_even, arrived_even, kept_odd, arrived_odd, bias, gate, out, held):
-    group, _ = place()
-    columns = kept_even.shape[1]
-    side = lax.rem(group, 2)
-    held[side] = kept_even[...].astype(jnp.float32) + arrived_even[...].astype(jnp.float32)
-    held[1 - side] = kept_odd[...].astype(jnp.float32) + arrived_odd[...].astype(jnp.float32)
-    for block in range(2):
+        scratch_shapes=[pltpu.VMEM((groups, *parts[0].shape), jnp.bfloat16)],
+        compiler_params=pltpu.CompilerParams(vmem_limit_bytes=SMALL),
+        cost_estimate=pl.CostEstimate(flops=0, bytes_accessed=4 * groups * parts[0].size, transcendentals=0),
+    )(*parts)
+
+
+def finish_kernel(kept, arrived, bias, gate, out):
+    blocks, _, columns = kept.shape
+    for block in range(blocks):
         cols = slice(block * columns, (block + 1) * columns)
-        out[:, cols] = (gate[:, cols] * (held[block] + bias[:, cols])).astype(jnp.bfloat16)
-
-
-def finish(pieces, bias, gate):
-    rows, columns = pieces[0].shape
-    width = 2 * columns
+        total = kept[block].astype(jnp.float32) + arrived[block].astype(jnp.float32)
+        out[:, cols] = (gate[:, cols] * (total + bias[:, cols])).astype(jnp.bfloat16)
+
+
+def finish(kept, arrived, bias, gate):
+    blocks, rows, columns = kept.shape
+    width = blocks * columns
     return pl.pallas_call(
         finish_kernel,
         out_shape=jax.ShapeDtypeStruct((rows, width), jnp.bfloat16),
-        in_specs=[VMEM] * (len(pieces) + 2),
+        in_specs=[VMEM] * 4,
         out_specs=VMEM,
-        scratch_shapes=[pltpu.VMEM((2, rows, columns), jnp.float32)],
         compiler_params=pltpu.CompilerParams(vmem_limit_bytes=SMALL),
         cost_estimate=pl.CostEstimate(flops=3 * rows * width, bytes_accessed=4 * rows * width, transcendentals=0),
-    )(*pieces, bias.reshape(1, width), gate.reshape(1, width))
+    )(kept, arrived, bias.reshape(1, width), gate.reshape(1, width))
 
 
 def after(value, *others):
@@ -485,12 +478,9 @@
     third = swap(second, SPREAD)
     weight = order(weight, weight_across)
     terms = close(groups, begin([attended, second, first], weight), third, weight)
-    second, third, first = along(terms)
-    pieces = []
-    for near, far in ((terms[0], second), (first, third)):
-        kept, sent = divide(far, near)
-        pieces += [kept, lax.ppermute(sent, "head", [(0, 1), (1, 0)])]
-    return finish(pieces, out_bias, out_gate)
+    kept, sent = divide([terms[0], *along(terms)])
+    received = lax.ppermute(sent, "head", [(0, 1), (1, 0)])
+    return finish(kept, received, out_bias, out_gate)
 
 
 def solution(mesh):

time: 59.7 us -> 59.4 us (level)
    ppermute x2 -> x1, starting transfers between devices: 2.15 us -> 1.58 us  [grouped_body(): received = lax.ppermute(sent, 'head', [(0, 1), (1, 0)])]
    ppermute x2 -> x1, waiting for transfers between devices: 3.81 us -> 3.59 us  [grouped_body(): received = lax.ppermute(sent, 'head', [(0, 1), (1, 0)])]
  transfers between devices with their start and end apart: 19 -> 18, of which waited for: 13 -> 13; matrix products, arithmetic and copies ran while one was open for 0% -> 0% of each run, Pallas kernels for 14% -> 14%
where the time goes in v21:
time: 59.4 us; the launch traced here: 59.1 us
  waiting for transfers between devices  29.6 us (50%)
  starting transfers between devices  20 us (34%)
  Pallas kernels  9.36 us (16%)
    ppermute x17, waiting for transfers between devices, swap(): return lax.ppermute(value, 'patch', [(p, p ^ twist) for p in range(size)])  26.1 us
    ppermute x17, starting transfers between devices, swap(): return lax.ppermute(value, 'patch', [(p, p ^ twist) for p in range(size)])  18.4 us
    ppermute x1, waiting for transfers between devices, grouped_body(): received = lax.ppermute(sent, 'head', [(0, 1), (1, 0)])  3.59 us
    pallas_call x3, Pallas kernels, attend_call(): pl.pallas_call(kernel, out_shape=shapes, in_specs=[VMEM] * len(operands),...  3.19 us
    pallas_call x1, Pallas kernels, pack(): pl.pallas_call(pack_kernel, out_shape=[jax.ShapeDtypeStruct(shape, bf16)...  2.32 us
    pallas_call x1, Pallas kernels, pick(): pl.pallas_call(pick_kernel, out_shape=[jax.ShapeDtypeStruct((kinds, texts...  1.65 us
    ppermute x1, starting transfers between devices, grouped_body(): received = lax.ppermute(sent, 'head', [(0, 1), (1, 0)])  1.58 us
  transfers between devices with their start and end apart: 18, of which 13 were waited for; matrix products, arithmetic and copies ran while one was open for 0% of the time, Pallas kernels for 14%

profile of v21, /device:TPU:0, one launch (start us, length us, event | category | flops | bytes accessed | tf_op | source)
XLA Modules:
  0.0 59.1 jit_solution(17383253768510968001)
XLA Ops:
  0.0 2.9 %collective-permute-start.3 = (bf16[192,1536]{1,0:T(8,128)(2,1)}, bf16[192,1536]{1,0:T(8,128)(2,1)S(1)}, u32[]{:S(2)}, u32[]{:S(2)}) collective-permute-start(bf16[192,1536]{1,0:T(8,128)(2,1)} %bitcast.2), channel_id=1, source_target_pairs={{0,4},{2,6},{4,0},{6,2},{8,12},{10,14},{12,8},{14,10},{16,20},{18,... | collective-permute-start | bytes 1769480 | tf_op jit(solution)/shard_map/ppermute | solution.py:447
  2.9 2.3 %shard_map.82 = (bf16[3,48,384]{2,1,0:T(8,128)(2,1)}, bf16[3,48,384]{2,1,0:T(8,128)(2,1)}, bf16[3,48,384]{2,1,0:T(8,128)(2,1)}, bf16[3,48,384]{2,1,0:T(8,128)(2,1)}, bf16[2,48,384]{2,1,0:T(8,128)(2,1)}) custom-call(bf16[48,1536]{1,0:T(8,128)(2,1)} %queries_hbm.1, s32[2,48,1536]{2,1,0:T(8,128)} %codes_hbm.1, s32[12,2,48]{2,1,0:T(2,128)} %bitcast.4), custom_call_target="tpu_custom_call" | custom-call | flops 294912 | bytes 884736 | tf_op jit(solution)/shard_map/pallas_call | solution.py:110
  5.3 2.7 %collective-permute-start = (bf16[3,48,384]{2,1,0:T(8,128)(2,1)}, bf16[3,48,384]{2,1,0:T(8,128)(2,1)S(1)}, u32[]{:S(2)}, u32[]{:S(2)}) collective-permute-start(bf16[3,48,384]{2,1,0:T(8,128)(2,1)} %get-tuple-element.41), channel_id=1, source_target_pairs={{0,16},{2,18},{4,20},{6,22},{8,24},{10,26},{12,28},{14,30},{16,0},... | collective-permute-start | bytes 331784 | tf_op jit(solution)/shard_map/ppermute | solution.py:447
  7.9 1.3 %collective-permute-start.1 = (bf16[3,48,384]{2,1,0:T(8,128)(2,1)}, bf16[3,48,384]{2,1,0:T(8,128)(2,1)S(1)}, u32[]{:S(2)}, u32[]{:S(2)}) collective-permute-start(bf16[3,48,384]{2,1,0:T(8,128)(2,1)} %get-tuple-element.42), channel_id=1, source_target_pairs={{0,24},{2,26},{4,28},{6,30},{8,16},{10,18},{12,20},{14,22},{16,8},... | collective-permute-start | bytes 331784 | tf_op jit(solution)/shard_map/ppermute | solution.py:447
  9.3 0.2 collective-permute-start.2
  9.5 0.5 collective-permute-start.4
  10.0 1.7 %shard_map.84 = (bf16[2,512,384]{2,1,0:T(8,128)(2,1)S(1)}, bf16[4,2,192,384]{3,2,1,0:T(8,128)(2,1)S(1)}) custom-call(bf16[2,512,1536]{2,1,0:T(8,128)(2,1)} %text_hbm.1, bf16[2,768,1536]{2,1,0:T(8,128)(2,1)} %stale_hbm.1), custom_call_target="tpu_custom_call" | custom-call | bytes 8388608 | tf_op jit(solution)/shard_map/pallas_call | solution.py:155
  11.7 5.1 %collective-permute-done.refs_1_ = bf16[3,48,384]{2,1,0:T(8,128)(2,1)S(1)} collective-permute-done((bf16[3,48,384]{2,1,0:T(8,128)(2,1)}, bf16[3,48,384]{2,1,0:T(8,128)(2,1)S(1)}, u32[]{:S(2)}, u32[]{:S(2)}) %collective-permute-start) | collective-permute-done | bytes 110624 | tf_op jit(solution)/shard_map/ppermute | solution.py:447
  17.1 1.0 %collective-permute-done.4.own_far = bf16[2,48,384]{2,1,0:T(8,128)(2,1)S(1)} collective-permute-done((bf16[2,48,384]{2,1,0:T(8,128)(2,1)}, bf16[2,48,384]{2,1,0:T(8,128)(2,1)S(1)}, u32[]{:S(2)}, u32[]{:S(2)}) %collective-permute-start.4) | collective-permute-done | bytes 73760 | tf_op jit(solution)/shard_map/ppermute | solution.py:447
  18.1 1.7 %collective-permute-start.5 = (bf16[3,2,48,384]{3,2,1,0:T(8,128)(2,1)S(1)}, bf16[3,2,48,384]{3,2,1,0:T(8,128)(2,1)S(1)}, u32[]{:S(2)}, u32[]{:S(2)}) collective-permute-start(bf16[3,2,48,384]{3,2,1,0:T(8,128)(2,1)S(1)} %get-tuple-element.53), channel_id=1, source_target_pairs={{0,4},{2,6},{4,0},{6,2},{8,12},{10,14},{12,8},{14,10},{16,20},{18,... | collective-permute-start | bytes 663560 | tf_op jit(solution)/shard_map/ppermute | solution.py:447
  19.8 0.5 collective-permute-start.7
  20.4 0.8 %collective-permute-done.6.left = bf16[2,2,48,384]{3,2,1,0:T(8,128)(2,1)S(1)} collective-permute-done((bf16[2,2,48,384]{3,2,1,0:T(8,128)(2,1)S(1)}, bf16[2,2,48,384]{3,2,1,0:T(8,128)(2,1)S(1)}, u32[]{:S(2)}, u32[]{:S(2)}) %collective-permute-start.6) | collective-permute-done | bytes 147488 | tf_op jit(solution)/shard_map/ppermute | solution.py:447
  21.4 1.2 %shard_map.86 = (f32[3,192,1]{2,1,0:T(8,128)S(1)}, f32[3,192,1]{2,1,0:T(8,128)S(1)}, f32[3,192,128]{2,1,0:T(8,128)S(1)}) custom-call(bf16[192,384]{1,0:T(8,128)(2,1)S(1)} %get-tuple-element.52.query, bf16[4,2,48,384]{3,2,1,0:T(8,128)(2,1)S(1)} %get-tuple-element.56.every, bf16[2,2,48,384]{3,2,1,0:T(8,128)(2,1)S(1)} %collective-permute-done.6.left, ...), custom_call_target="tpu_custom_call" | custom-call | flops 528482304 | bytes 2752512 | tf_op jit(solution)/shard_map/pallas_call | solution.py:285
  22.6 2.1 %collective-permute-done.5.some_far = bf16[3,2,48,384]{3,2,1,0:T(8,128)(2,1)S(1)} collective-permute-done((bf16[3,2,48,384]{3,2,1,0:T(8,128)(2,1)S(1)}, bf16[3,2,48,384]{3,2,1,0:T(8,128)(2,1)S(1)}, u32[]{:S(2)}, u32[]{:S(2)}) %collective-permute-start.5) | collective-permute-done | bytes 221216 | tf_op jit(solution)/shard_map/ppermute | solution.py:447
  24.7 0.5 collective-permute-start.8
  25.2 0.9 %shard_map.87 = (f32[3,192,1]{2,1,0:T(8,128)S(1)}, f32[3,192,1]{2,1,0:T(8,128)S(1)}, f32[3,192,128]{2,1,0:T(8,128)S(1)}) custom-call(bf16[192,384]{1,0:T(8,128)(2,1)S(1)} %get-tuple-element.52.query, bf16[2,48,384]{2,1,0:T(8,128)(2,1)S(1)} %collective-permute-done.4.own_far, bf16[3,2,48,384]{3,2,1,0:T(8,128)(2,1)S(1)} %collective-permute-done.5.some_far, ...), custom_call_target="tpu_custom_call" | custom-call | flops 113246208 | bytes 589824 | tf_op jit(solution)/shard_map/pallas_call | solution.py:285
  26.5 1.1 %shard_map.88.own = bf16[192,384]{1,0:T(8,128)(2,1)S(1)} custom-call(bf16[192,384]{1,0:T(8,128)(2,1)S(1)} %get-tuple-element.52.query, bf16[2,48,384]{2,1,0:T(8,128)(2,1)S(1)} %collective-permute-done.8.own_corner, bf16[3,2,48,384]{3,2,1,0:T(8,128)(2,1)S(1)} %collective-permute-done.9.some_corner, bf16[4,2,192,384]{3,2,1,0:T(8,128)(2,1)S(1)} %get-tuple-element.51.stale, ...), custom_call_target="tpu_custom_call" | custom-call | flops 113246208 | bytes 589824 | tf_op jit(solution)/shard_map/pallas_call | solution.py:285
  27.6 3.6 %collective-permute-start.10 = (bf16[192,384]{1,0:T(8,128)(2,1)S(1)}, bf16[192,384]{1,0:T(8,128)(2,1)S(1)}, u32[]{:S(2)}, u32[]{:S(2)}) collective-permute-start(bf16[192,384]{1,0:T(8,128)(2,1)S(1)} %shard_map.88.own), channel_id=1, source_target_pairs={{0,16},{2,18},{4,20},{6,22},{8,24},{10,26},{12,28},{14,30},{16,0},... | collective-permute-start | bytes 442376 | tf_op jit(solution)/shard_map/ppermute | solution.py:447
  31.2 0.6 collective-permute-start.11
  31.7 7.0 %collective-permute-done.10.second = bf16[192,384]{1,0:T(8,128)(2,1)S(1)} collective-permute-done((bf16[192,384]{1,0:T(8,128)(2,1)S(1)}, bf16[192,384]{1,0:T(8,128)(2,1)S(1)}, u32[]{:S(2)}, u32[]{:S(2)}) %collective-permute-start.10) | collective-permute-done | bytes 147488 | tf_op jit(solution)/shard_map/ppermute | solution.py:447
  38.9 0.8 %collective-permute-done.11.first = bf16[192,384]{1,0:T(8,128)(2,1)S(1)} collective-permute-done((bf16[192,384]{1,0:T(8,128)(2,1)S(1)}, bf16[192,384]{1,0:T(8,128)(2,1)S(1)}, u32[]{:S(2)}, u32[]{:S(2)}) %collective-permute-start.11) | collective-permute-done | bytes 147488 | tf_op jit(solution)/shard_map/ppermute | solution.py:447
  39.7 0.7 %shard_map.90.partial = f32[192,768]{1,0:T(8,128)S(1)} custom-call(bf16[192,384]{1,0:T(8,128)(2,1)S(1)} %shard_map.88.own, bf16[192,384]{1,0:T(8,128)(2,1)S(1)} %collective-permute-done.10.second, bf16[192,384]{1,0:T(8,128)(2,1)S(1)} %collective-permute-done.11.first, bf16[768,1536]{1,0:T(8,128)(2,1)S(1)} %shard_map.89.weight), custom_call_target="tpu_custom_call" | custom-call | flops 452984832 | bytes 589824 | tf_op jit(solution)/shard_map/pallas_call | solution.py:355
  40.5 3.8 %collective-permute-done.13.third = bf16[192,384]{1,0:T(8,128)(2,1)S(1)} collective-permute-done((bf16[192,384]{1,0:T(8,128)(2,1)S(1)}, bf16[192,384]{1,0:T(8,128)(2,1)S(1)}, u32[]{:S(2)}, u32[]{:S(2)}) %collective-permute-start.13) | collective-permute-done | bytes 147488 | tf_op jit(solution)/shard_map/ppermute | solution.py:447
  44.3 0.4 shard_map.91
  44.7 1.2 %collective-permute-start.14 = (bf16[48,768]{1,0:T(8,128)(2,1)S(1)}, bf16[48,768]{1,0:T(8,128)(2,1)S(1)}, u32[]{:S(2)}, u32[]{:S(2)}) collective-permute-start(bf16[48,768]{1,0:T(8,128)(2,1)S(1)} %get-tuple-element.70), channel_id=1, source_target_pairs={{0,16},{2,18},{4,20},{6,22},{8,24},{10,26},{12,28},{14,30},{16,0},... | collective-permute-start | bytes 221192 | tf_op jit(solution)/shard_map/ppermute | solution.py:447
  45.8 1.5 %collective-permute-start.15 = (bf16[48,768]{1,0:T(8,128)(2,1)S(1)}, bf16[48,768]{1,0:T(8,128)(2,1)S(1)}, u32[]{:S(2)}, u32[]{:S(2)}) collective-permute-start(bf16[48,768]{1,0:T(8,128)(2,1)S(1)} %get-tuple-element.71), channel_id=1, source_target_pairs={{0,24},{2,26},{4,28},{6,30},{8,16},{10,18},{12,20},{14,22},{16,8},... | collective-permute-start | bytes 221192 | tf_op jit(solution)/shard_map/ppermute | solution.py:447
  47.4 0.8 %collective-permute-start.16 = (bf16[48,768]{1,0:T(8,128)(2,1)S(1)}, bf16[48,768]{1,0:T(8,128)(2,1)S(1)}, u32[]{:S(2)}, u32[]{:S(2)}) collective-permute-start(bf16[48,768]{1,0:T(8,128)(2,1)S(1)} %get-tuple-element.72), channel_id=1, source_target_pairs={{0,8},{2,10},{4,12},{6,14},{8,0},{10,2},{12,4},{14,6},{16,24},{18,... | collective-permute-start | bytes 221192 | tf_op jit(solution)/shard_map/ppermute | solution.py:447
  48.2 4.5 %collective-permute-done.14.refs_1_ = bf16[48,768]{1,0:T(8,128)(2,1)S(1)} collective-permute-done((bf16[48,768]{1,0:T(8,128)(2,1)S(1)}, bf16[48,768]{1,0:T(8,128)(2,1)S(1)}, u32[]{:S(2)}, u32[]{:S(2)}) %collective-permute-start.14) | collective-permute-done | bytes 73760 | tf_op jit(solution)/shard_map/ppermute | solution.py:447
  52.7 0.5 collective-permute-done.16.refs_3_
  53.2 1.6 %collective-permute-start.17 = (bf16[2,48,768]{2,1,0:T(8,128)(2,1)S(1)}, bf16[2,48,768]{2,1,0:T(8,128)(2,1)S(1)}, u32[]{:S(2)}, u32[]{:S(2)}) collective-permute-start(bf16[2,48,768]{2,1,0:T(8,128)(2,1)S(1)} %get-tuple-element.74), channel_id=1, source_target_pairs={{0,1},{1,0},{2,3},{3,2},{4,5},{5,4},{6,7},{7,6},{8,9},{9,8},{10,11... | collective-permute-start | bytes 442376 | tf_op jit(solution)/shard_map/ppermute | solution.py:482
  54.8 3.6 %collective-permute-done.17.arrived = bf16[2,48,768]{2,1,0:T(8,128)(2,1)S(1)} collective-permute-done((bf16[2,48,768]{2,1,0:T(8,128)(2,1)S(1)}, bf16[2,48,768]{2,1,0:T(8,128)(2,1)S(1)}, u32[]{:S(2)}, u32[]{:S(2)}) %collective-permute-start.17) | collective-permute-done | bytes 147488 | tf_op jit(solution)/shard_map/ppermute | solution.py:482
  58.4 0.7 %shard_map.93 = bf16[48,1536]{1,0:T(8,128)(2,1)} custom-call(bf16[2,48,768]{2,1,0:T(8,128)(2,1)S(1)} %get-tuple-element.73.kept, bf16[2,48,768]{2,1,0:T(8,128)(2,1)S(1)} %collective-permute-done.17.arrived, f32[1,1536]{1,0:T(1,128)S(1)} %reshape.6.bias, f32[1,1536]{1,0:T(1,128)S(1)} %reshape.7.gate), custom_call_target="tpu_custom_call" | custom-call | flops 221184 | bytes 294912 | tf_op jit(solution)/shard_map/pallas_call | solution.py:428
  (26 shorter events, 1.2 us)
Async XLA Ops:
  0.0 18.1 %collective-permute-start.3 = (bf16[192,1536]{1,0:T(8,128)(2,1)}, bf16[192,1536]{1,0:T(8,128)(2,1)S(1)}, u32[]{:S(2)}, u32[]{:S(2)}) collective-permute-start(bf16[192,1536]{1,0:T(8,128)(2,1)} %bitcast.2), channel_id=1, source_target_pairs={{0,4},{2,6},{4,0},{6,2},{8,12},{10,14},{12,8},{14,10},{16,20},{18,... | collective-permute-start | bytes 1769480 | tf_op jit(solution)/shard_map/ppermute | solution.py:447
  5.3 11.6 %collective-permute-start = (bf16[3,48,384]{2,1,0:T(8,128)(2,1)}, bf16[3,48,384]{2,1,0:T(8,128)(2,1)S(1)}, u32[]{:S(2)}, u32[]{:S(2)}) collective-permute-start(bf16[3,48,384]{2,1,0:T(8,128)(2,1)} %get-tuple-element.41), channel_id=1, source_target_pairs={{0,16},{2,18},{4,20},{6,22},{8,24},{10,26},{12,28},{14,30},{16,0},... | collective-permute-start | bytes 331784 | tf_op jit(solution)/shard_map/ppermute | solution.py:447
  7.9 8.9 %collective-permute-start.1 = (bf16[3,48,384]{2,1,0:T(8,128)(2,1)}, bf16[3,48,384]{2,1,0:T(8,128)(2,1)S(1)}, u32[]{:S(2)}, u32[]{:S(2)}) collective-permute-start(bf16[3,48,384]{2,1,0:T(8,128)(2,1)} %get-tuple-element.42), channel_id=1, source_target_pairs={{0,24},{2,26},{4,28},{6,30},{8,16},{10,18},{12,20},{14,22},{16,8},... | collective-permute-start | bytes 331784 | tf_op jit(solution)/shard_map/ppermute | solution.py:447
  9.3 7.7 %collective-permute-start.2 = (bf16[3,48,384]{2,1,0:T(8,128)(2,1)}, bf16[3,48,384]{2,1,0:T(8,128)(2,1)S(1)}, u32[]{:S(2)}, u32[]{:S(2)}) collective-permute-start(bf16[3,48,384]{2,1,0:T(8,128)(2,1)} %get-tuple-element.43), channel_id=1, source_target_pairs={{0,8},{2,10},{4,12},{6,14},{8,0},{10,2},{12,4},{14,6},{16,24},{18,... | collective-permute-start | bytes 331784 | tf_op jit(solution)/shard_map/ppermute | solution.py:447
  9.5 7.5 %copy-start.1 = (bf16[3,48,384]{2,1,0:T(8,128)(2,1)S(1)}, bf16[3,48,384]{2,1,0:T(8,128)(2,1)}, u32[]{:S(2)}) copy-start(bf16[3,48,384]{2,1,0:T(8,128)(2,1)} %get-tuple-element.40.refs_0_) | copy-start | bytes 331780
  9.5 10.8 %copy-start = (bf16[1536,192]{0,1:T(8,128)(2,1)S(1)}, bf16[1536,192]{0,1:T(8,128)(2,1)}, u32[]{:S(2)}) copy-start(bf16[1536,192]{0,1:T(8,128)(2,1)} %param.13) | copy-start | bytes 1769476
  9.5 8.5 %collective-permute-start.4 = (bf16[2,48,384]{2,1,0:T(8,128)(2,1)}, bf16[2,48,384]{2,1,0:T(8,128)(2,1)S(1)}, u32[]{:S(2)}, u32[]{:S(2)}) collective-permute-start(bf16[2,48,384]{2,1,0:T(8,128)(2,1)} %get-tuple-element.49), channel_id=1, source_target_pairs={{0,4},{2,6},{4,0},{6,2},{8,12},{10,14},{12,8},{14,10},{16,20},{18,... | collective-permute-start | bytes 221192 | tf_op jit(solution)/shard_map/ppermute | solution.py:447
  18.1 6.6 %collective-permute-start.5 = (bf16[3,2,48,384]{3,2,1,0:T(8,128)(2,1)S(1)}, bf16[3,2,48,384]{3,2,1,0:T(8,128)(2,1)S(1)}, u32[]{:S(2)}, u32[]{:S(2)}) collective-permute-start(bf16[3,2,48,384]{3,2,1,0:T(8,128)(2,1)S(1)} %get-tuple-element.53), channel_id=1, source_target_pairs={{0,4},{2,6},{4,0},{6,2},{8,12},{10,14},{12,8},{14,10},{16,20},{18,... | collective-permute-start | bytes 663560 | tf_op jit(solution)/shard_map/ppermute | solution.py:447
  19.8 1.4 %collective-permute-start.6 = (bf16[2,2,48,384]{3,2,1,0:T(8,128)(2,1)S(1)}, bf16[2,2,48,384]{3,2,1,0:T(8,128)(2,1)S(1)}, u32[]{:S(2)}, u32[]{:S(2)}) collective-permute-start(bf16[2,2,48,384]{3,2,1,0:T(8,128)(2,1)S(1)} %get-tuple-element.57), channel_id=1, source_target_pairs={{0,2},{2,0},{4,6},{6,4},{8,10},{10,8},{12,14},{14,12},{16,18},{18,... | collective-permute-start | bytes 442376 | tf_op jit(solution)/shard_map/ppermute | solution.py:447
  19.8 1.6 %collective-permute-start.7 = (bf16[2,2,48,384]{3,2,1,0:T(8,128)(2,1)S(1)}, bf16[2,2,48,384]{3,2,1,0:T(8,128)(2,1)S(1)}, u32[]{:S(2)}, u32[]{:S(2)}) collective-permute-start(bf16[2,2,48,384]{3,2,1,0:T(8,128)(2,1)S(1)} %get-tuple-element.58), channel_id=1, source_target_pairs={{0,2},{2,0},{4,6},{6,4},{8,10},{10,8},{12,14},{14,12},{16,18},{18,... | collective-permute-start | bytes 442376 | tf_op jit(solution)/shard_map/ppermute | solution.py:447
  24.7 1.6 %collective-permute-start.9 = (bf16[3,2,48,384]{3,2,1,0:T(8,128)(2,1)S(1)}, bf16[3,2,48,384]{3,2,1,0:T(8,128)(2,1)S(1)}, u32[]{:S(2)}, u32[]{:S(2)}) collective-permute-start(bf16[3,2,48,384]{3,2,1,0:T(8,128)(2,1)S(1)} %collective-permute-done.5.some_far), channel_id=1, source_target_pairs={{0,2},{2,0},{4,6},{6,4},{8,10},{10,8},{12,14},{14,12},{16,18},{18,... | collective-permute-start | bytes 663560 | tf_op jit(solution)/shard_map/ppermute | solution.py:447
  24.7 1.6 %collective-permute-start.8 = (bf16[2,48,384]{2,1,0:T(8,128)(2,1)S(1)}, bf16[2,48,384]{2,1,0:T(8,128)(2,1)S(1)}, u32[]{:S(2)}, u32[]{:S(2)}) collective-permute-start(bf16[2,48,384]{2,1,0:T(8,128)(2,1)S(1)} %collective-permute-done.4.own_far), channel_id=1, source_target_pairs={{0,2},{2,0},{4,6},{6,4},{8,10},{10,8},{12,14},{14,12},{16,18},{18,... | collective-permute-start | bytes 221192 | tf_op jit(solution)/shard_map/ppermute | solution.py:447
  26.3 12.5 %collective-permute-start.12 = (bf16[2,192,1536]{2,1,0:T(8,128)(2,1)S(1)}, bf16[2,192,1536]{2,1,0:T(8,128)(2,1)S(1)}, u32[]{:S(2)}, u32[]{:S(2)}) collective-permute-start(bf16[2,192,1536]{2,1,0:T(8,128)(2,1)S(1)} %shard_map.85.own), channel_id=1, source_target_pairs={{0,2},{2,0},{4,6},{6,4},{8,10},{10,8},{12,14},{14,12},{16,18},{18,... | collective-permute-start | bytes 3538952 | tf_op jit(solution)/shard_map/ppermute | solution.py:447
  27.6 11.2 %collective-permute-start.10 = (bf16[192,384]{1,0:T(8,128)(2,1)S(1)}, bf16[192,384]{1,0:T(8,128)(2,1)S(1)}, u32[]{:S(2)}, u32[]{:S(2)}) collective-permute-start(bf16[192,384]{1,0:T(8,128)(2,1)S(1)} %shard_map.88.own), channel_id=1, source_target_pairs={{0,16},{2,18},{4,20},{6,22},{8,24},{10,26},{12,28},{14,30},{16,0},... | collective-permute-start | bytes 442376 | tf_op jit(solution)/shard_map/ppermute | solution.py:447
  31.2 8.6 %collective-permute-start.11 = (bf16[192,384]{1,0:T(8,128)(2,1)S(1)}, bf16[192,384]{1,0:T(8,128)(2,1)S(1)}, u32[]{:S(2)}, u32[]{:S(2)}) collective-permute-start(bf16[192,384]{1,0:T(8,128)(2,1)S(1)} %shard_map.88.own), channel_id=1, source_target_pairs={{0,8},{2,10},{4,12},{6,14},{8,0},{10,2},{12,4},{14,6},{16,24},{18,... | collective-permute-start | bytes 442376 | tf_op jit(solution)/shard_map/ppermute | solution.py:447
  38.8 5.5 %collective-permute-start.13 = (bf16[192,384]{1,0:T(8,128)(2,1)S(1)}, bf16[192,384]{1,0:T(8,128)(2,1)S(1)}, u32[]{:S(2)}, u32[]{:S(2)}) collective-permute-start(bf16[192,384]{1,0:T(8,128)(2,1)S(1)} %collective-permute-done.10.second), channel_id=1, source_target_pairs={{0,8},{2,10},{4,12},{6,14},{8,0},{10,2},{12,4},{14,6},{16,24},{18,... | collective-permute-start | bytes 442376 | tf_op jit(solution)/shard_map/ppermute | solution.py:447
  40.5 14.3 %copy-start.2 = (f32[1536]{0:T(1024)S(1)}, f32[1536]{0:T(1024)}, u32[]{:S(2)}) copy-start(f32[1536]{0:T(1024)} %param.14) | copy-start | bytes 18436
  40.5 14.3 %copy-start.3 = (f32[1536]{0:T(1024)S(1)}, f32[1536]{0:T(1024)}, u32[]{:S(2)}) copy-start(f32[1536]{0:T(1024)} %param.15) | copy-start | bytes 18436
  44.7 8.0 %collective-permute-start.14 = (bf16[48,768]{1,0:T(8,128)(2,1)S(1)}, bf16[48,768]{1,0:T(8,128)(2,1)S(1)}, u32[]{:S(2)}, u32[]{:S(2)}) collective-permute-start(bf16[48,768]{1,0:T(8,128)(2,1)S(1)} %get-tuple-element.70), channel_id=1, source_target_pairs={{0,16},{2,18},{4,20},{6,22},{8,24},{10,26},{12,28},{14,30},{16,0},... | collective-permute-start | bytes 221192 | tf_op jit(solution)/shard_map/ppermute | solution.py:447
  45.8 6.9 %collective-permute-start.15 = (bf16[48,768]{1,0:T(8,128)(2,1)S(1)}, bf16[48,768]{1,0:T(8,128)(2,1)S(1)}, u32[]{:S(2)}, u32[]{:S(2)}) collective-permute-start(bf16[48,768]{1,0:T(8,128)(2,1)S(1)} %get-tuple-element.71), channel_id=1, source_target_pairs={{0,24},{2,26},{4,28},{6,30},{8,16},{10,18},{12,20},{14,22},{16,8},... | collective-permute-start | bytes 221192 | tf_op jit(solution)/shard_map/ppermute | solution.py:447
  47.4 5.8 %collective-permute-start.16 = (bf16[48,768]{1,0:T(8,128)(2,1)S(1)}, bf16[48,768]{1,0:T(8,128)(2,1)S(1)}, u32[]{:S(2)}, u32[]{:S(2)}) collective-permute-start(bf16[48,768]{1,0:T(8,128)(2,1)S(1)} %get-tuple-element.72), channel_id=1, source_target_pairs={{0,8},{2,10},{4,12},{6,14},{8,0},{10,2},{12,4},{14,6},{16,24},{18,... | collective-permute-start | bytes 221192 | tf_op jit(solution)/shard_map/ppermute | solution.py:447
  53.2 5.2 %collective-permute-start.17 = (bf16[2,48,768]{2,1,0:T(8,128)(2,1)S(1)}, bf16[2,48,768]{2,1,0:T(8,128)(2,1)S(1)}, u32[]{:S(2)}, u32[]{:S(2)}) collective-permute-start(bf16[2,48,768]{2,1,0:T(8,128)(2,1)S(1)} %get-tuple-element.74), channel_id=1, source_target_pairs={{0,1},{1,0},{2,3},{3,2},{4,5},{5,4},{6,7},{7,6},{8,9},{9,8},{10,11... | collective-permute-start | bytes 442376 | tf_op jit(solution)/shard_map/ppermute | solution.py:482

commit v22 on v21

--- a/solution.py
+++ b/solution.py
@@ -457,8 +457,8 @@
     every, some, left, right, query = merge([packed[0], *along(packed)])
     own_far = swap(own, 2)
 
-    ready = (every, some, left, right, query, weight, weight_far, own_far, text, stale)
-    every, some, left, right, query, weight, weight_far = lax.optimization_barrier(ready)[:7]
+    ready = (every, some, left, right, query, own_far, text, stale)
+    every, some, left, right, query = lax.optimization_barrier(ready)[:5]
     left, right, some_far = swap(left, 1), swap(right, 1), swap(some, 2)
     share = stale.shape[2]
     operands = [query, every, left, right, text, stale]

time: 59.4 us -> 59.4 us (level)
  no operation moved by 1% of the time
where the time goes in v22:
time: 59.4 us; the launch traced here: 59.1 us
  waiting for transfers between devices  29.6 us (50%)
  starting transfers between devices  20 us (34%)
  Pallas kernels  9.38 us (16%)
    ppermute x17, waiting for transfers between devices, swap(): return lax.ppermute(value, 'patch', [(p, p ^ twist) for p in range(size)])  26 us
    ppermute x17, starting transfers between devices, swap(): return lax.ppermute(value, 'patch', [(p, p ^ twist) for p in range(size)])  18.4 us
    ppermute x1, waiting for transfers between devices, grouped_body(): received = lax.ppermute(sent, 'head', [(0, 1), (1, 0)])  3.59 us
    pallas_call x3, Pallas kernels, attend_call(): pl.pallas_call(kernel, out_shape=shapes, in_specs=[VMEM] * len(operands),...  3.21 us
    pallas_call x1, Pallas kernels, pack(): pl.pallas_call(pack_kernel, out_shape=[jax.ShapeDtypeStruct(shape, bf16)...  2.32 us
    pallas_call x1, Pallas kernels, pick(): pl.pallas_call(pick_kernel, out_shape=[jax.ShapeDtypeStruct((kinds, texts...  1.65 us
    ppermute x1, starting transfers between devices, grouped_body(): received = lax.ppermute(sent, 'head', [(0, 1), (1, 0)])  1.59 us
  transfers between devices with their start and end apart: 18, of which 13 were waited for; matrix products, arithmetic and copies ran while one was open for 0% of the time, Pallas kernels for 14%

profile of v22, /device:TPU:0, one launch (start us, length us, event | category | flops | bytes accessed | tf_op | source)
XLA Modules:
  0.0 59.1 jit_solution(17784342752101482129)
XLA Ops:
  0.0 2.9 %collective-permute-start.5 = (bf16[192,1536]{1,0:T(8,128)(2,1)}, bf16[192,1536]{1,0:T(8,128)(2,1)S(1)}, u32[]{:S(2)}, u32[]{:S(2)}) collective-permute-start(bf16[192,1536]{1,0:T(8,128)(2,1)} %bitcast.2), channel_id=1, source_target_pairs={{0,4},{2,6},{4,0},{6,2},{8,12},{10,14},{12,8},{14,10},{16,20},{18,... | collective-permute-start | bytes 1769480 | tf_op jit(solution)/shard_map/ppermute | solution.py:447
  2.9 2.3 %shard_map.82 = (bf16[3,48,384]{2,1,0:T(8,128)(2,1)}, bf16[3,48,384]{2,1,0:T(8,128)(2,1)}, bf16[3,48,384]{2,1,0:T(8,128)(2,1)}, bf16[3,48,384]{2,1,0:T(8,128)(2,1)}, bf16[2,48,384]{2,1,0:T(8,128)(2,1)}) custom-call(bf16[48,1536]{1,0:T(8,128)(2,1)} %queries_hbm.1, s32[2,48,1536]{2,1,0:T(8,128)} %codes_hbm.1, s32[12,2,48]{2,1,0:T(2,128)} %bitcast.4), custom_call_target="tpu_custom_call" | custom-call | flops 294912 | bytes 884736 | tf_op jit(solution)/shard_map/pallas_call | solution.py:110
  5.3 2.7 %collective-permute-start = (bf16[3,48,384]{2,1,0:T(8,128)(2,1)}, bf16[3,48,384]{2,1,0:T(8,128)(2,1)S(1)}, u32[]{:S(2)}, u32[]{:S(2)}) collective-permute-start(bf16[3,48,384]{2,1,0:T(8,128)(2,1)} %get-tuple-element.39), channel_id=1, source_target_pairs={{0,16},{2,18},{4,20},{6,22},{8,24},{10,26},{12,28},{14,30},{16,0},... | collective-permute-start | bytes 331784 | tf_op jit(solution)/shard_map/ppermute | solution.py:447
  7.9 1.3 %collective-permute-start.1 = (bf16[3,48,384]{2,1,0:T(8,128)(2,1)}, bf16[3,48,384]{2,1,0:T(8,128)(2,1)S(1)}, u32[]{:S(2)}, u32[]{:S(2)}) collective-permute-start(bf16[3,48,384]{2,1,0:T(8,128)(2,1)} %get-tuple-element.40), channel_id=1, source_target_pairs={{0,24},{2,26},{4,28},{6,30},{8,16},{10,18},{12,20},{14,22},{16,8},... | collective-permute-start | bytes 331784 | tf_op jit(solution)/shard_map/ppermute | solution.py:447
  9.3 0.2 collective-permute-start.2
  9.5 0.5 collective-permute-start.3
  10.0 1.7 %shard_map.84 = (bf16[2,512,384]{2,1,0:T(8,128)(2,1)S(1)}, bf16[4,2,192,384]{3,2,1,0:T(8,128)(2,1)S(1)}) custom-call(bf16[2,512,1536]{2,1,0:T(8,128)(2,1)} %text_hbm.1, bf16[2,768,1536]{2,1,0:T(8,128)(2,1)} %stale_hbm.1), custom_call_target="tpu_custom_call" | custom-call | bytes 8388608 | tf_op jit(solution)/shard_map/pallas_call | solution.py:155
  11.7 5.1 %collective-permute-done.refs_1_ = bf16[3,48,384]{2,1,0:T(8,128)(2,1)S(1)} collective-permute-done((bf16[3,48,384]{2,1,0:T(8,128)(2,1)}, bf16[3,48,384]{2,1,0:T(8,128)(2,1)S(1)}, u32[]{:S(2)}, u32[]{:S(2)}) %collective-permute-start) | collective-permute-done | bytes 110624 | tf_op jit(solution)/shard_map/ppermute | solution.py:447
  17.1 1.0 %collective-permute-done.3.own_far = bf16[2,48,384]{2,1,0:T(8,128)(2,1)S(1)} collective-permute-done((bf16[2,48,384]{2,1,0:T(8,128)(2,1)}, bf16[2,48,384]{2,1,0:T(8,128)(2,1)S(1)}, u32[]{:S(2)}, u32[]{:S(2)}) %collective-permute-start.3) | collective-permute-done | bytes 73760 | tf_op jit(solution)/shard_map/ppermute | solution.py:447
  18.1 1.7 %collective-permute-start.4 = (bf16[3,2,48,384]{3,2,1,0:T(8,128)(2,1)S(1)}, bf16[3,2,48,384]{3,2,1,0:T(8,128)(2,1)S(1)}, u32[]{:S(2)}, u32[]{:S(2)}) collective-permute-start(bf16[3,2,48,384]{3,2,1,0:T(8,128)(2,1)S(1)} %get-tuple-element.51), channel_id=1, source_target_pairs={{0,4},{2,6},{4,0},{6,2},{8,12},{10,14},{12,8},{14,10},{16,20},{18,... | collective-permute-start | bytes 663560 | tf_op jit(solution)/shard_map/ppermute | solution.py:447
  19.8 0.5 collective-permute-start.7
  20.3 0.9 %collective-permute-done.6.left = bf16[2,2,48,384]{3,2,1,0:T(8,128)(2,1)S(1)} collective-permute-done((bf16[2,2,48,384]{3,2,1,0:T(8,128)(2,1)S(1)}, bf16[2,2,48,384]{3,2,1,0:T(8,128)(2,1)S(1)}, u32[]{:S(2)}, u32[]{:S(2)}) %collective-permute-start.6) | collective-permute-done | bytes 147488 | tf_op jit(solution)/shard_map/ppermute | solution.py:447
  21.4 1.2 %shard_map.86 = (f32[3,192,1]{2,1,0:T(8,128)S(1)}, f32[3,192,1]{2,1,0:T(8,128)S(1)}, f32[3,192,128]{2,1,0:T(8,128)S(1)}) custom-call(bf16[192,384]{1,0:T(8,128)(2,1)S(1)} %get-tuple-element.50.query, bf16[4,2,48,384]{3,2,1,0:T(8,128)(2,1)S(1)} %get-tuple-element.52.every, bf16[2,2,48,384]{3,2,1,0:T(8,128)(2,1)S(1)} %collective-permute-done.6.left, ...), custom_call_target="tpu_custom_call" | custom-call | flops 528482304 | bytes 2752512 | tf_op jit(solution)/shard_map/pallas_call | solution.py:285
  22.7 2.0 %collective-permute-done.4.some_far = bf16[3,2,48,384]{3,2,1,0:T(8,128)(2,1)S(1)} collective-permute-done((bf16[3,2,48,384]{3,2,1,0:T(8,128)(2,1)S(1)}, bf16[3,2,48,384]{3,2,1,0:T(8,128)(2,1)S(1)}, u32[]{:S(2)}, u32[]{:S(2)}) %collective-permute-start.4) | collective-permute-done | bytes 221216 | tf_op jit(solution)/shard_map/ppermute | solution.py:447
  24.7 0.5 collective-permute-start.8
  25.2 0.9 %shard_map.87 = (f32[3,192,1]{2,1,0:T(8,128)S(1)}, f32[3,192,1]{2,1,0:T(8,128)S(1)}, f32[3,192,128]{2,1,0:T(8,128)S(1)}) custom-call(bf16[192,384]{1,0:T(8,128)(2,1)S(1)} %get-tuple-element.50.query, bf16[2,48,384]{2,1,0:T(8,128)(2,1)S(1)} %collective-permute-done.3.own_far, bf16[3,2,48,384]{3,2,1,0:T(8,128)(2,1)S(1)} %collective-permute-done.4.some_far, ...), custom_call_target="tpu_custom_call" | custom-call | flops 113246208 | bytes 589824 | tf_op jit(solution)/shard_map/pallas_call | solution.py:285
  26.5 1.1 %shard_map.88.own = bf16[192,384]{1,0:T(8,128)(2,1)S(1)} custom-call(bf16[192,384]{1,0:T(8,128)(2,1)S(1)} %get-tuple-element.50.query, bf16[2,48,384]{2,1,0:T(8,128)(2,1)S(1)} %collective-permute-done.8.own_corner, bf16[3,2,48,384]{3,2,1,0:T(8,128)(2,1)S(1)} %collective-permute-done.9.some_corner, bf16[4,2,192,384]{3,2,1,0:T(8,128)(2,1)S(1)} %get-tuple-element.49.stale, ...), custom_call_target="tpu_custom_call" | custom-call | flops 113246208 | bytes 589824 | tf_op jit(solution)/shard_map/pallas_call | solution.py:285
  27.6 3.6 %collective-permute-start.10 = (bf16[192,384]{1,0:T(8,128)(2,1)S(1)}, bf16[192,384]{1,0:T(8,128)(2,1)S(1)}, u32[]{:S(2)}, u32[]{:S(2)}) collective-permute-start(bf16[192,384]{1,0:T(8,128)(2,1)S(1)} %shard_map.88.own), channel_id=1, source_target_pairs={{0,16},{2,18},{4,20},{6,22},{8,24},{10,26},{12,28},{14,30},{16,0},... | collective-permute-start | bytes 442376 | tf_op jit(solution)/shard_map/ppermute | solution.py:447
  31.2 0.6 collective-permute-start.11
  31.7 7.0 %collective-permute-done.10.second = bf16[192,384]{1,0:T(8,128)(2,1)S(1)} collective-permute-done((bf16[192,384]{1,0:T(8,128)(2,1)S(1)}, bf16[192,384]{1,0:T(8,128)(2,1)S(1)}, u32[]{:S(2)}, u32[]{:S(2)}) %collective-permute-start.10) | collective-permute-done | bytes 147488 | tf_op jit(solution)/shard_map/ppermute | solution.py:447
  38.9 0.8 %collective-permute-done.11.first = bf16[192,384]{1,0:T(8,128)(2,1)S(1)} collective-permute-done((bf16[192,384]{1,0:T(8,128)(2,1)S(1)}, bf16[192,384]{1,0:T(8,128)(2,1)S(1)}, u32[]{:S(2)}, u32[]{:S(2)}) %collective-permute-start.11) | collective-permute-done | bytes 147488 | tf_op jit(solution)/shard_map/ppermute | solution.py:447
  39.7 0.7 %shard_map.90.partial = f32[192,768]{1,0:T(8,128)S(1)} custom-call(bf16[192,384]{1,0:T(8,128)(2,1)S(1)} %shard_map.88.own, bf16[192,384]{1,0:T(8,128)(2,1)S(1)} %collective-permute-done.10.second, bf16[192,384]{1,0:T(8,128)(2,1)S(1)} %collective-permute-done.11.first, bf16[768,1536]{1,0:T(8,128)(2,1)S(1)} %shard_map.89.weight), custom_call_target="tpu_custom_call" | custom-call | flops 452984832 | bytes 589824 | tf_op jit(solution)/shard_map/pallas_call | solution.py:355
  40.5 3.8 %collective-permute-done.13.third = bf16[192,384]{1,0:T(8,128)(2,1)S(1)} collective-permute-done((bf16[192,384]{1,0:T(8,128)(2,1)S(1)}, bf16[192,384]{1,0:T(8,128)(2,1)S(1)}, u32[]{:S(2)}, u32[]{:S(2)}) %collective-permute-start.13) | collective-permute-done | bytes 147488 | tf_op jit(solution)/shard_map/ppermute | solution.py:447
  44.3 0.4 shard_map.91
  44.7 1.2 %collective-permute-start.14 = (bf16[48,768]{1,0:T(8,128)(2,1)S(1)}, bf16[48,768]{1,0:T(8,128)(2,1)S(1)}, u32[]{:S(2)}, u32[]{:S(2)}) collective-permute-start(bf16[48,768]{1,0:T(8,128)(2,1)S(1)} %get-tuple-element.66), channel_id=1, source_target_pairs={{0,16},{2,18},{4,20},{6,22},{8,24},{10,26},{12,28},{14,30},{16,0},... | collective-permute-start | bytes 221192 | tf_op jit(solution)/shard_map/ppermute | solution.py:447
  45.8 1.5 %collective-permute-start.15 = (bf16[48,768]{1,0:T(8,128)(2,1)S(1)}, bf16[48,768]{1,0:T(8,128)(2,1)S(1)}, u32[]{:S(2)}, u32[]{:S(2)}) collective-permute-start(bf16[48,768]{1,0:T(8,128)(2,1)S(1)} %get-tuple-element.67), channel_id=1, source_target_pairs={{0,24},{2,26},{4,28},{6,30},{8,16},{10,18},{12,20},{14,22},{16,8},... | collective-permute-start | bytes 221192 | tf_op jit(solution)/shard_map/ppermute | solution.py:447
  47.4 0.8 %collective-permute-start.16 = (bf16[48,768]{1,0:T(8,128)(2,1)S(1)}, bf16[48,768]{1,0:T(8,128)(2,1)S(1)}, u32[]{:S(2)}, u32[]{:S(2)}) collective-permute-start(bf16[48,768]{1,0:T(8,128)(2,1)S(1)} %get-tuple-element.68), channel_id=1, source_target_pairs={{0,8},{2,10},{4,12},{6,14},{8,0},{10,2},{12,4},{14,6},{16,24},{18,... | collective-permute-start | bytes 221192 | tf_op jit(solution)/shard_map/ppermute | solution.py:447
  48.2 4.5 %collective-permute-done.14.refs_1_ = bf16[48,768]{1,0:T(8,128)(2,1)S(1)} collective-permute-done((bf16[48,768]{1,0:T(8,128)(2,1)S(1)}, bf16[48,768]{1,0:T(8,128)(2,1)S(1)}, u32[]{:S(2)}, u32[]{:S(2)}) %collective-permute-start.14) | collective-permute-done | bytes 73760 | tf_op jit(solution)/shard_map/ppermute | solution.py:447
  52.7 0.5 collective-permute-done.16.refs_3_
  53.2 1.6 %collective-permute-start.17 = (bf16[2,48,768]{2,1,0:T(8,128)(2,1)S(1)}, bf16[2,48,768]{2,1,0:T(8,128)(2,1)S(1)}, u32[]{:S(2)}, u32[]{:S(2)}) collective-permute-start(bf16[2,48,768]{2,1,0:T(8,128)(2,1)S(1)} %get-tuple-element.70), channel_id=1, source_target_pairs={{0,1},{1,0},{2,3},{3,2},{4,5},{5,4},{6,7},{7,6},{8,9},{9,8},{10,11... | collective-permute-start | bytes 442376 | tf_op jit(solution)/shard_map/ppermute | solution.py:482
  54.8 3.6 %collective-permute-done.17.arrived = bf16[2,48,768]{2,1,0:T(8,128)(2,1)S(1)} collective-permute-done((bf16[2,48,768]{2,1,0:T(8,128)(2,1)S(1)}, bf16[2,48,768]{2,1,0:T(8,128)(2,1)S(1)}, u32[]{:S(2)}, u32[]{:S(2)}) %collective-permute-start.17) | collective-permute-done | bytes 147488 | tf_op jit(solution)/shard_map/ppermute | solution.py:482
  58.4 0.7 %shard_map.93 = bf16[48,1536]{1,0:T(8,128)(2,1)} custom-call(bf16[2,48,768]{2,1,0:T(8,128)(2,1)S(1)} %get-tuple-element.69.kept, bf16[2,48,768]{2,1,0:T(8,128)(2,1)S(1)} %collective-permute-done.17.arrived, f32[1,1536]{1,0:T(1,128)S(1)} %reshape.6.bias, f32[1,1536]{1,0:T(1,128)S(1)} %reshape.7.gate), custom_call_target="tpu_custom_call" | custom-call | flops 221184 | bytes 294912 | tf_op jit(solution)/shard_map/pallas_call | solution.py:428
  (26 shorter events, 1.2 us)
Async XLA Ops:
  0.0 22.6 %collective-permute-start.5 = (bf16[192,1536]{1,0:T(8,128)(2,1)}, bf16[192,1536]{1,0:T(8,128)(2,1)S(1)}, u32[]{:S(2)}, u32[]{:S(2)}) collective-permute-start(bf16[192,1536]{1,0:T(8,128)(2,1)} %bitcast.2), channel_id=1, source_target_pairs={{0,4},{2,6},{4,0},{6,2},{8,12},{10,14},{12,8},{14,10},{16,20},{18,... | collective-permute-start | bytes 1769480 | tf_op jit(solution)/shard_map/ppermute | solution.py:447
  5.3 11.6 %collective-permute-start = (bf16[3,48,384]{2,1,0:T(8,128)(2,1)}, bf16[3,48,384]{2,1,0:T(8,128)(2,1)S(1)}, u32[]{:S(2)}, u32[]{:S(2)}) collective-permute-start(bf16[3,48,384]{2,1,0:T(8,128)(2,1)} %get-tuple-element.39), channel_id=1, source_target_pairs={{0,16},{2,18},{4,20},{6,22},{8,24},{10,26},{12,28},{14,30},{16,0},... | collective-permute-start | bytes 331784 | tf_op jit(solution)/shard_map/ppermute | solution.py:447
  7.9 8.9 %collective-permute-start.1 = (bf16[3,48,384]{2,1,0:T(8,128)(2,1)}, bf16[3,48,384]{2,1,0:T(8,128)(2,1)S(1)}, u32[]{:S(2)}, u32[]{:S(2)}) collective-permute-start(bf16[3,48,384]{2,1,0:T(8,128)(2,1)} %get-tuple-element.40), channel_id=1, source_target_pairs={{0,24},{2,26},{4,28},{6,30},{8,16},{10,18},{12,20},{14,22},{16,8},... | collective-permute-start | bytes 331784 | tf_op jit(solution)/shard_map/ppermute | solution.py:447
  9.3 7.7 %collective-permute-start.2 = (bf16[3,48,384]{2,1,0:T(8,128)(2,1)}, bf16[3,48,384]{2,1,0:T(8,128)(2,1)S(1)}, u32[]{:S(2)}, u32[]{:S(2)}) collective-permute-start(bf16[3,48,384]{2,1,0:T(8,128)(2,1)} %get-tuple-element.41), channel_id=1, source_target_pairs={{0,8},{2,10},{4,12},{6,14},{8,0},{10,2},{12,4},{14,6},{16,24},{18,... | collective-permute-start | bytes 331784 | tf_op jit(solution)/shard_map/ppermute | solution.py:447
  9.5 7.5 %copy-start.1 = (bf16[3,48,384]{2,1,0:T(8,128)(2,1)S(1)}, bf16[3,48,384]{2,1,0:T(8,128)(2,1)}, u32[]{:S(2)}) copy-start(bf16[3,48,384]{2,1,0:T(8,128)(2,1)} %get-tuple-element.38.refs_0_) | copy-start | bytes 331780
  9.5 8.5 %collective-permute-start.3 = (bf16[2,48,384]{2,1,0:T(8,128)(2,1)}, bf16[2,48,384]{2,1,0:T(8,128)(2,1)S(1)}, u32[]{:S(2)}, u32[]{:S(2)}) collective-permute-start(bf16[2,48,384]{2,1,0:T(8,128)(2,1)} %get-tuple-element.47), channel_id=1, source_target_pairs={{0,4},{2,6},{4,0},{6,2},{8,12},{10,14},{12,8},{14,10},{16,20},{18,... | collective-permute-start | bytes 221192 | tf_op jit(solution)/shard_map/ppermute | solution.py:447
  11.7 10.9 %copy-start = (bf16[1536,192]{0,1:T(8,128)(2,1)S(1)}, bf16[1536,192]{0,1:T(8,128)(2,1)}, u32[]{:S(2)}) copy-start(bf16[1536,192]{0,1:T(8,128)(2,1)} %param.13) | copy-start | bytes 1769476
  18.1 6.6 %collective-permute-start.4 = (bf16[3,2,48,384]{3,2,1,0:T(8,128)(2,1)S(1)}, bf16[3,2,48,384]{3,2,1,0:T(8,128)(2,1)S(1)}, u32[]{:S(2)}, u32[]{:S(2)}) collective-permute-start(bf16[3,2,48,384]{3,2,1,0:T(8,128)(2,1)S(1)} %get-tuple-element.51), channel_id=1, source_target_pairs={{0,4},{2,6},{4,0},{6,2},{8,12},{10,14},{12,8},{14,10},{16,20},{18,... | collective-permute-start | bytes 663560 | tf_op jit(solution)/shard_map/ppermute | solution.py:447
  19.8 1.4 %collective-permute-start.6 = (bf16[2,2,48,384]{3,2,1,0:T(8,128)(2,1)S(1)}, bf16[2,2,48,384]{3,2,1,0:T(8,128)(2,1)S(1)}, u32[]{:S(2)}, u32[]{:S(2)}) collective-permute-start(bf16[2,2,48,384]{3,2,1,0:T(8,128)(2,1)S(1)} %get-tuple-element.53), channel_id=1, source_target_pairs={{0,2},{2,0},{4,6},{6,4},{8,10},{10,8},{12,14},{14,12},{16,18},{18,... | collective-permute-start | bytes 442376 | tf_op jit(solution)/shard_map/ppermute | solution.py:447
  19.8 1.6 %collective-permute-start.7 = (bf16[2,2,48,384]{3,2,1,0:T(8,128)(2,1)S(1)}, bf16[2,2,48,384]{3,2,1,0:T(8,128)(2,1)S(1)}, u32[]{:S(2)}, u32[]{:S(2)}) collective-permute-start(bf16[2,2,48,384]{3,2,1,0:T(8,128)(2,1)S(1)} %get-tuple-element.54), channel_id=1, source_target_pairs={{0,2},{2,0},{4,6},{6,4},{8,10},{10,8},{12,14},{14,12},{16,18},{18,... | collective-permute-start | bytes 442376 | tf_op jit(solution)/shard_map/ppermute | solution.py:447
  24.7 1.6 %collective-permute-start.9 = (bf16[3,2,48,384]{3,2,1,0:T(8,128)(2,1)S(1)}, bf16[3,2,48,384]{3,2,1,0:T(8,128)(2,1)S(1)}, u32[]{:S(2)}, u32[]{:S(2)}) collective-permute-start(bf16[3,2,48,384]{3,2,1,0:T(8,128)(2,1)S(1)} %collective-permute-done.4.some_far), channel_id=1, source_target_pairs={{0,2},{2,0},{4,6},{6,4},{8,10},{10,8},{12,14},{14,12},{16,18},{18,... | collective-permute-start | bytes 663560 | tf_op jit(solution)/shard_map/ppermute | solution.py:447
  24.7 1.6 %collective-permute-start.8 = (bf16[2,48,384]{2,1,0:T(8,128)(2,1)S(1)}, bf16[2,48,384]{2,1,0:T(8,128)(2,1)S(1)}, u32[]{:S(2)}, u32[]{:S(2)}) collective-permute-start(bf16[2,48,384]{2,1,0:T(8,128)(2,1)S(1)} %collective-permute-done.3.own_far), channel_id=1, source_target_pairs={{0,2},{2,0},{4,6},{6,4},{8,10},{10,8},{12,14},{14,12},{16,18},{18,... | collective-permute-start | bytes 221192 | tf_op jit(solution)/shard_map/ppermute | solution.py:447
  26.3 12.5 %collective-permute-start.12 = (bf16[2,192,1536]{2,1,0:T(8,128)(2,1)S(1)}, bf16[2,192,1536]{2,1,0:T(8,128)(2,1)S(1)}, u32[]{:S(2)}, u32[]{:S(2)}) collective-permute-start(bf16[2,192,1536]{2,1,0:T(8,128)(2,1)S(1)} %shard_map.85.own), channel_id=1, source_target_pairs={{0,2},{2,0},{4,6},{6,4},{8,10},{10,8},{12,14},{14,12},{16,18},{18,... | collective-permute-start | bytes 3538952 | tf_op jit(solution)/shard_map/ppermute | solution.py:447
  27.6 11.2 %collective-permute-start.10 = (bf16[192,384]{1,0:T(8,128)(2,1)S(1)}, bf16[192,384]{1,0:T(8,128)(2,1)S(1)}, u32[]{:S(2)}, u32[]{:S(2)}) collective-permute-start(bf16[192,384]{1,0:T(8,128)(2,1)S(1)} %shard_map.88.own), channel_id=1, source_target_pairs={{0,16},{2,18},{4,20},{6,22},{8,24},{10,26},{12,28},{14,30},{16,0},... | collective-permute-start | bytes 442376 | tf_op jit(solution)/shard_map/ppermute | solution.py:447
  31.2 8.6 %collective-permute-start.11 = (bf16[192,384]{1,0:T(8,128)(2,1)S(1)}, bf16[192,384]{1,0:T(8,128)(2,1)S(1)}, u32[]{:S(2)}, u32[]{:S(2)}) collective-permute-start(bf16[192,384]{1,0:T(8,128)(2,1)S(1)} %shard_map.88.own), channel_id=1, source_target_pairs={{0,8},{2,10},{4,12},{6,14},{8,0},{10,2},{12,4},{14,6},{16,24},{18,... | collective-permute-start | bytes 442376 | tf_op jit(solution)/shard_map/ppermute | solution.py:447
  38.7 5.5 %collective-permute-start.13 = (bf16[192,384]{1,0:T(8,128)(2,1)S(1)}, bf16[192,384]{1,0:T(8,128)(2,1)S(1)}, u32[]{:S(2)}, u32[]{:S(2)}) collective-permute-start(bf16[192,384]{1,0:T(8,128)(2,1)S(1)} %collective-permute-done.10.second), channel_id=1, source_target_pairs={{0,8},{2,10},{4,12},{6,14},{8,0},{10,2},{12,4},{14,6},{16,24},{18,... | collective-permute-start | bytes 442376 | tf_op jit(solution)/shard_map/ppermute | solution.py:447
  40.5 14.3 %copy-start.2 = (f32[1536]{0:T(1024)S(1)}, f32[1536]{0:T(1024)}, u32[]{:S(2)}) copy-start(f32[1536]{0:T(1024)} %param.14) | copy-start | bytes 18436
  40.5 14.3 %copy-start.3 = (f32[1536]{0:T(1024)S(1)}, f32[1536]{0:T(1024)}, u32[]{:S(2)}) copy-start(f32[1536]{0:T(1024)} %param.15) | copy-start | bytes 18436
  44.7 8.0 %collective-permute-start.14 = (bf16[48,768]{1,0:T(8,128)(2,1)S(1)}, bf16[48,768]{1,0:T(8,128)(2,1)S(1)}, u32[]{:S(2)}, u32[]{:S(2)}) collective-permute-start(bf16[48,768]{1,0:T(8,128)(2,1)S(1)} %get-tuple-element.66), channel_id=1, source_target_pairs={{0,16},{2,18},{4,20},{6,22},{8,24},{10,26},{12,28},{14,30},{16,0},... | collective-permute-start | bytes 221192 | tf_op jit(solution)/shard_map/ppermute | solution.py:447
  45.8 6.9 %collective-permute-start.15 = (bf16[48,768]{1,0:T(8,128)(2,1)S(1)}, bf16[48,768]{1,0:T(8,128)(2,1)S(1)}, u32[]{:S(2)}, u32[]{:S(2)}) collective-permute-start(bf16[48,768]{1,0:T(8,128)(2,1)S(1)} %get-tuple-element.67), channel_id=1, source_target_pairs={{0,24},{2,26},{4,28},{6,30},{8,16},{10,18},{12,20},{14,22},{16,8},... | collective-permute-start | bytes 221192 | tf_op jit(solution)/shard_map/ppermute | solution.py:447
  47.4 5.8 %collective-permute-start.16 = (bf16[48,768]{1,0:T(8,128)(2,1)S(1)}, bf16[48,768]{1,0:T(8,128)(2,1)S(1)}, u32[]{:S(2)}, u32[]{:S(2)}) collective-permute-start(bf16[48,768]{1,0:T(8,128)(2,1)S(1)} %get-tuple-element.68), channel_id=1, source_target_pairs={{0,8},{2,10},{4,12},{6,14},{8,0},{10,2},{12,4},{14,6},{16,24},{18,... | collective-permute-start | bytes 221192 | tf_op jit(solution)/shard_map/ppermute | solution.py:447
  53.2 5.2 %collective-permute-start.17 = (bf16[2,48,768]{2,1,0:T(8,128)(2,1)S(1)}, bf16[2,48,768]{2,1,0:T(8,128)(2,1)S(1)}, u32[]{:S(2)}, u32[]{:S(2)}) collective-permute-start(bf16[2,48,768]{2,1,0:T(8,128)(2,1)S(1)} %get-tuple-element.70), channel_id=1, source_target_pairs={{0,1},{1,0},{2,3},{3,2},{4,5},{5,4},{6,7},{7,6},{8,9},{9,8},{10,11... | collective-permute-start | bytes 442376 | tf_op jit(solution)/shard_map/ppermute | solution.py:482

commit v23 on v22

--- a/solution.py
+++ b/solution.py
@@ -457,7 +457,7 @@
     every, some, left, right, query = merge([packed[0], *along(packed)])
     own_far = swap(own, 2)
 
-    ready = (every, some, left, right, query, own_far, text, stale)
+    ready = (every, some, left, right, query, text, stale)
     every, some, left, right, query = lax.optimization_barrier(ready)[:5]
     left, right, some_far = swap(left, 1), swap(right, 1), swap(some, 2)
     share = stale.shape[2]

time: 59.4 us -> 60.4 us (1.017)
  starting transfers between devices: 20 us -> 20.8 us
    ppermute x17, starting transfers between devices: 18.4 us -> 19.2 us  [swap(): return lax.ppermute(value, 'patch', [(p, p ^ twist) for p in range(size)])]
  transfers between devices with their start and end apart: 18 -> 18, of which waited for: 13 -> 10; matrix products, arithmetic and copies ran while one was open for 0% -> 0% of each run, Pallas kernels for 14% -> 14%
where the time goes in v23:
time: 60.4 us; the launch traced here: 60.2 us
  waiting for transfers between devices  29.8 us (49%)
  starting transfers between devices  20.8 us (34%)
  Pallas kernels  9.38 us (16%)
    ppermute x17, waiting for transfers between devices, swap(): return lax.ppermute(value, 'patch', [(p, p ^ twist) for p in range(size)])  26.2 us
    ppermute x17, starting transfers between devices, swap(): return lax.ppermute(value, 'patch', [(p, p ^ twist) for p in range(size)])  19.2 us
    ppermute x1, waiting for transfers between devices, grouped_body(): received = lax.ppermute(sent, 'head', [(0, 1), (1, 0)])  3.59 us
    pallas_call x3, Pallas kernels, attend_call(): pl.pallas_call(kernel, out_shape=shapes, in_specs=[VMEM] * len(operands),...  3.21 us
    pallas_call x1, Pallas kernels, pack(): pl.pallas_call(pack_kernel, out_shape=[jax.ShapeDtypeStruct(shape, bf16)...  2.32 us
    pallas_call x1, Pallas kernels, pick(): pl.pallas_call(pick_kernel, out_shape=[jax.ShapeDtypeStruct((kinds, texts...  1.65 us
    ppermute x1, starting transfers between devices, grouped_body(): received = lax.ppermute(sent, 'head', [(0, 1), (1, 0)])  1.58 us
  transfers between devices with their start and end apart: 18, of which 10 were waited for; matrix products, arithmetic and copies ran while one was open for 0% of the time, Pallas kernels for 14%

profile of v23, /device:TPU:0, one launch (start us, length us, event | category | flops | bytes accessed | tf_op | source)
XLA Modules:
  0.0 60.2 jit_solution(17614718526718313367)
XLA Ops:
  0.0 2.9 %collective-permute-start.5 = (bf16[192,1536]{1,0:T(8,128)(2,1)}, bf16[192,1536]{1,0:T(8,128)(2,1)S(1)}, u32[]{:S(2)}, u32[]{:S(2)}) collective-permute-start(bf16[192,1536]{1,0:T(8,128)(2,1)} %bitcast.2), channel_id=1, source_target_pairs={{0,4},{2,6},{4,0},{6,2},{8,12},{10,14},{12,8},{14,10},{16,20},{18,... | collective-permute-start | bytes 1769480 | tf_op jit(solution)/shard_map/ppermute | solution.py:447
  2.9 2.3 %shard_map.82 = (bf16[3,48,384]{2,1,0:T(8,128)(2,1)}, bf16[3,48,384]{2,1,0:T(8,128)(2,1)}, bf16[3,48,384]{2,1,0:T(8,128)(2,1)}, bf16[3,48,384]{2,1,0:T(8,128)(2,1)}, bf16[2,48,384]{2,1,0:T(8,128)(2,1)}) custom-call(bf16[48,1536]{1,0:T(8,128)(2,1)} %queries_hbm.1, s32[2,48,1536]{2,1,0:T(8,128)} %codes_hbm.1, s32[12,2,48]{2,1,0:T(2,128)} %bitcast.4), custom_call_target="tpu_custom_call" | custom-call | flops 294912 | bytes 884736 | tf_op jit(solution)/shard_map/pallas_call | solution.py:110
  5.3 2.7 %collective-permute-start = (bf16[3,48,384]{2,1,0:T(8,128)(2,1)}, bf16[3,48,384]{2,1,0:T(8,128)(2,1)S(1)}, u32[]{:S(2)}, u32[]{:S(2)}) collective-permute-start(bf16[3,48,384]{2,1,0:T(8,128)(2,1)} %get-tuple-element.39), channel_id=1, source_target_pairs={{0,16},{2,18},{4,20},{6,22},{8,24},{10,26},{12,28},{14,30},{16,0},... | collective-permute-start | bytes 331784 | tf_op jit(solution)/shard_map/ppermute | solution.py:447
  7.9 1.3 %collective-permute-start.1 = (bf16[3,48,384]{2,1,0:T(8,128)(2,1)}, bf16[3,48,384]{2,1,0:T(8,128)(2,1)S(1)}, u32[]{:S(2)}, u32[]{:S(2)}) collective-permute-start(bf16[3,48,384]{2,1,0:T(8,128)(2,1)} %get-tuple-element.40), channel_id=1, source_target_pairs={{0,24},{2,26},{4,28},{6,30},{8,16},{10,18},{12,20},{14,22},{16,8},... | collective-permute-start | bytes 331784 | tf_op jit(solution)/shard_map/ppermute | solution.py:447
  9.3 0.2 collective-permute-start.2
  9.5 1.7 %shard_map.84 = (bf16[2,512,384]{2,1,0:T(8,128)(2,1)S(1)}, bf16[4,2,192,384]{3,2,1,0:T(8,128)(2,1)S(1)}) custom-call(bf16[2,512,1536]{2,1,0:T(8,128)(2,1)} %text_hbm.1, bf16[2,768,1536]{2,1,0:T(8,128)(2,1)} %stale_hbm.1), custom_call_target="tpu_custom_call" | custom-call | bytes 8388608 | tf_op jit(solution)/shard_map/pallas_call | solution.py:155
  11.2 5.6 %collective-permute-done.refs_1_ = bf16[3,48,384]{2,1,0:T(8,128)(2,1)S(1)} collective-permute-done((bf16[3,48,384]{2,1,0:T(8,128)(2,1)}, bf16[3,48,384]{2,1,0:T(8,128)(2,1)S(1)}, u32[]{:S(2)}, u32[]{:S(2)}) %collective-permute-start) | collective-permute-done | bytes 110624 | tf_op jit(solution)/shard_map/ppermute | solution.py:447
  16.8 0.1 collective-permute-done.2.refs_3_
  17.1 0.6 collective-permute-start.3
  17.6 0.5 collective-permute-start.7
  18.1 1.5 %collective-permute-start.4 = (bf16[2,48,384]{2,1,0:T(8,128)(2,1)S(1)}, bf16[2,48,384]{2,1,0:T(8,128)(2,1)S(1)}, u32[]{:S(2)}, u32[]{:S(2)}) collective-permute-start(bf16[2,48,384]{2,1,0:T(8,128)(2,1)S(1)} %copy-done.4), channel_id=1, source_target_pairs={{0,4},{2,6},{4,0},{6,2},{8,12},{10,14},{12,8},{14,10},{16,20},{18,... | collective-permute-start | bytes 221192 | tf_op jit(solution)/shard_map/ppermute | solution.py:447
  19.7 1.2 %shard_map.86 = (f32[3,192,1]{2,1,0:T(8,128)S(1)}, f32[3,192,1]{2,1,0:T(8,128)S(1)}, f32[3,192,128]{2,1,0:T(8,128)S(1)}) custom-call(bf16[192,384]{1,0:T(8,128)(2,1)S(1)} %get-tuple-element.49.query, bf16[4,2,48,384]{3,2,1,0:T(8,128)(2,1)S(1)} %get-tuple-element.52.every, bf16[2,2,48,384]{3,2,1,0:T(8,128)(2,1)S(1)} %collective-permute-done.6.left, ...), custom_call_target="tpu_custom_call" | custom-call | flops 528482304 | bytes 2752512 | tf_op jit(solution)/shard_map/pallas_call | solution.py:285
  21.0 3.6 %collective-permute-done.4.own_far = bf16[2,48,384]{2,1,0:T(8,128)(2,1)S(1)} collective-permute-done((bf16[2,48,384]{2,1,0:T(8,128)(2,1)S(1)}, bf16[2,48,384]{2,1,0:T(8,128)(2,1)S(1)}, u32[]{:S(2)}, u32[]{:S(2)}) %collective-permute-start.4) | collective-permute-done | bytes 73760 | tf_op jit(solution)/shard_map/ppermute | solution.py:447
  24.6 0.5 collective-permute-start.8
  25.1 0.9 %shard_map.87 = (f32[3,192,1]{2,1,0:T(8,128)S(1)}, f32[3,192,1]{2,1,0:T(8,128)S(1)}, f32[3,192,128]{2,1,0:T(8,128)S(1)}) custom-call(bf16[192,384]{1,0:T(8,128)(2,1)S(1)} %get-tuple-element.49.query, bf16[2,48,384]{2,1,0:T(8,128)(2,1)S(1)} %collective-permute-done.4.own_far, bf16[3,2,48,384]{3,2,1,0:T(8,128)(2,1)S(1)} %collective-permute-done.3.some_far, ...), custom_call_target="tpu_custom_call" | custom-call | flops 113246208 | bytes 589824 | tf_op jit(solution)/shard_map/pallas_call | solution.py:285
  26.0 0.2 collective-permute-done.8.own_corner
  26.2 0.2 collective-permute-start.12
  26.4 1.1 %shard_map.88.own = bf16[192,384]{1,0:T(8,128)(2,1)S(1)} custom-call(bf16[192,384]{1,0:T(8,128)(2,1)S(1)} %get-tuple-element.49.query, bf16[2,48,384]{2,1,0:T(8,128)(2,1)S(1)} %collective-permute-done.8.own_corner, bf16[3,2,48,384]{3,2,1,0:T(8,128)(2,1)S(1)} %collective-permute-done.9.some_corner, bf16[4,2,192,384]{3,2,1,0:T(8,128)(2,1)S(1)} %get-tuple-element.48.stale, ...), custom_call_target="tpu_custom_call" | custom-call | flops 113246208 | bytes 589824 | tf_op jit(solution)/shard_map/pallas_call | solution.py:285
  27.5 5.2 %collective-permute-start.10 = (bf16[192,384]{1,0:T(8,128)(2,1)S(1)}, bf16[192,384]{1,0:T(8,128)(2,1)S(1)}, u32[]{:S(2)}, u32[]{:S(2)}) collective-permute-start(bf16[192,384]{1,0:T(8,128)(2,1)S(1)} %shard_map.88.own), channel_id=1, source_target_pairs={{0,16},{2,18},{4,20},{6,22},{8,24},{10,26},{12,28},{14,30},{16,0},... | collective-permute-start | bytes 442376 | tf_op jit(solution)/shard_map/ppermute | solution.py:447
  32.7 7.6 %collective-permute-done.10.second = bf16[192,384]{1,0:T(8,128)(2,1)S(1)} collective-permute-done((bf16[192,384]{1,0:T(8,128)(2,1)S(1)}, bf16[192,384]{1,0:T(8,128)(2,1)S(1)}, u32[]{:S(2)}, u32[]{:S(2)}) %collective-permute-start.10) | collective-permute-done | bytes 147488 | tf_op jit(solution)/shard_map/ppermute | solution.py:447
  40.3 0.2 shard_map.89.weight
  40.5 0.8 %collective-permute-done.11.first = bf16[192,384]{1,0:T(8,128)(2,1)S(1)} collective-permute-done((bf16[192,384]{1,0:T(8,128)(2,1)S(1)}, bf16[192,384]{1,0:T(8,128)(2,1)S(1)}, u32[]{:S(2)}, u32[]{:S(2)}) %collective-permute-start.11) | collective-permute-done | bytes 147488 | tf_op jit(solution)/shard_map/ppermute | solution.py:447
  41.3 0.7 %shard_map.90.partial = f32[192,768]{1,0:T(8,128)S(1)} custom-call(bf16[192,384]{1,0:T(8,128)(2,1)S(1)} %shard_map.88.own, bf16[192,384]{1,0:T(8,128)(2,1)S(1)} %collective-permute-done.10.second, bf16[192,384]{1,0:T(8,128)(2,1)S(1)} %collective-permute-done.11.first, bf16[768,1536]{1,0:T(8,128)(2,1)S(1)} %shard_map.89.weight), custom_call_target="tpu_custom_call" | custom-call | flops 452984832 | bytes 589824 | tf_op jit(solution)/shard_map/pallas_call | solution.py:355
  42.0 3.8 %collective-permute-done.13.third = bf16[192,384]{1,0:T(8,128)(2,1)S(1)} collective-permute-done((bf16[192,384]{1,0:T(8,128)(2,1)S(1)}, bf16[192,384]{1,0:T(8,128)(2,1)S(1)}, u32[]{:S(2)}, u32[]{:S(2)}) %collective-permute-start.13) | collective-permute-done | bytes 147488 | tf_op jit(solution)/shard_map/ppermute | solution.py:447
  45.8 0.4 shard_map.91
  46.3 2.6 %collective-permute-start.15 = (bf16[48,768]{1,0:T(8,128)(2,1)S(1)}, bf16[48,768]{1,0:T(8,128)(2,1)S(1)}, u32[]{:S(2)}, u32[]{:S(2)}) collective-permute-start(bf16[48,768]{1,0:T(8,128)(2,1)S(1)} %get-tuple-element.67), channel_id=1, source_target_pairs={{0,24},{2,26},{4,28},{6,30},{8,16},{10,18},{12,20},{14,22},{16,8},... | collective-permute-start | bytes 221192 | tf_op jit(solution)/shard_map/ppermute | solution.py:447
  48.9 0.8 %collective-permute-start.16 = (bf16[48,768]{1,0:T(8,128)(2,1)S(1)}, bf16[48,768]{1,0:T(8,128)(2,1)S(1)}, u32[]{:S(2)}, u32[]{:S(2)}) collective-permute-start(bf16[48,768]{1,0:T(8,128)(2,1)S(1)} %get-tuple-element.68), channel_id=1, source_target_pairs={{0,8},{2,10},{4,12},{6,14},{8,0},{10,2},{12,4},{14,6},{16,24},{18,... | collective-permute-start | bytes 221192 | tf_op jit(solution)/shard_map/ppermute | solution.py:447
  49.8 4.0 %collective-permute-done.14.refs_1_ = bf16[48,768]{1,0:T(8,128)(2,1)S(1)} collective-permute-done((bf16[48,768]{1,0:T(8,128)(2,1)S(1)}, bf16[48,768]{1,0:T(8,128)(2,1)S(1)}, u32[]{:S(2)}, u32[]{:S(2)}) %collective-permute-start.14) | collective-permute-done | bytes 73760 | tf_op jit(solution)/shard_map/ppermute | solution.py:447
  53.8 0.4 collective-permute-done.16.refs_3_
  54.3 1.6 %collective-permute-start.17 = (bf16[2,48,768]{2,1,0:T(8,128)(2,1)S(1)}, bf16[2,48,768]{2,1,0:T(8,128)(2,1)S(1)}, u32[]{:S(2)}, u32[]{:S(2)}) collective-permute-start(bf16[2,48,768]{2,1,0:T(8,128)(2,1)S(1)} %get-tuple-element.70), channel_id=1, source_target_pairs={{0,1},{1,0},{2,3},{3,2},{4,5},{5,4},{6,7},{7,6},{8,9},{9,8},{10,11... | collective-permute-start | bytes 442376 | tf_op jit(solution)/shard_map/ppermute | solution.py:482
  55.9 3.6 %collective-permute-done.17.arrived = bf16[2,48,768]{2,1,0:T(8,128)(2,1)S(1)} collective-permute-done((bf16[2,48,768]{2,1,0:T(8,128)(2,1)S(1)}, bf16[2,48,768]{2,1,0:T(8,128)(2,1)S(1)}, u32[]{:S(2)}, u32[]{:S(2)}) %collective-permute-start.17) | collective-permute-done | bytes 147488 | tf_op jit(solution)/shard_map/ppermute | solution.py:482
  59.5 0.7 %shard_map.93 = bf16[48,1536]{1,0:T(8,128)(2,1)} custom-call(bf16[2,48,768]{2,1,0:T(8,128)(2,1)S(1)} %get-tuple-element.69.kept, bf16[2,48,768]{2,1,0:T(8,128)(2,1)S(1)} %collective-permute-done.17.arrived, f32[1,1536]{1,0:T(1,128)S(1)} %reshape.6.bias, f32[1,1536]{1,0:T(1,128)S(1)} %reshape.7.gate), custom_call_target="tpu_custom_call" | custom-call | flops 221184 | bytes 294912 | tf_op jit(solution)/shard_map/pallas_call | solution.py:428
  (28 shorter events, 0.4 us)
Async XLA Ops:
  0.0 20.9 %collective-permute-start.5 = (bf16[192,1536]{1,0:T(8,128)(2,1)}, bf16[192,1536]{1,0:T(8,128)(2,1)S(1)}, u32[]{:S(2)}, u32[]{:S(2)}) collective-permute-start(bf16[192,1536]{1,0:T(8,128)(2,1)} %bitcast.2), channel_id=1, source_target_pairs={{0,4},{2,6},{4,0},{6,2},{8,12},{10,14},{12,8},{14,10},{16,20},{18,... | collective-permute-start | bytes 1769480 | tf_op jit(solution)/shard_map/ppermute | solution.py:447
  5.3 11.6 %collective-permute-start = (bf16[3,48,384]{2,1,0:T(8,128)(2,1)}, bf16[3,48,384]{2,1,0:T(8,128)(2,1)S(1)}, u32[]{:S(2)}, u32[]{:S(2)}) collective-permute-start(bf16[3,48,384]{2,1,0:T(8,128)(2,1)} %get-tuple-element.39), channel_id=1, source_target_pairs={{0,16},{2,18},{4,20},{6,22},{8,24},{10,26},{12,28},{14,30},{16,0},... | collective-permute-start | bytes 331784 | tf_op jit(solution)/shard_map/ppermute | solution.py:447
  7.9 8.9 %collective-permute-start.1 = (bf16[3,48,384]{2,1,0:T(8,128)(2,1)}, bf16[3,48,384]{2,1,0:T(8,128)(2,1)S(1)}, u32[]{:S(2)}, u32[]{:S(2)}) collective-permute-start(bf16[3,48,384]{2,1,0:T(8,128)(2,1)} %get-tuple-element.40), channel_id=1, source_target_pairs={{0,24},{2,26},{4,28},{6,30},{8,16},{10,18},{12,20},{14,22},{16,8},... | collective-permute-start | bytes 331784 | tf_op jit(solution)/shard_map/ppermute | solution.py:447
  9.3 7.7 %copy-start.1 = (bf16[3,48,384]{2,1,0:T(8,128)(2,1)S(1)}, bf16[3,48,384]{2,1,0:T(8,128)(2,1)}, u32[]{:S(2)}) copy-start(bf16[3,48,384]{2,1,0:T(8,128)(2,1)} %get-tuple-element.38.refs_0_) | copy-start | bytes 331780
  9.3 8.8 %copy-start.4 = (bf16[2,48,384]{2,1,0:T(8,128)(2,1)S(1)}, bf16[2,48,384]{2,1,0:T(8,128)(2,1)}, u32[]{:S(2)}) copy-start(bf16[2,48,384]{2,1,0:T(8,128)(2,1)} %get-tuple-element.51) | copy-start | bytes 221188
  9.3 7.7 %collective-permute-start.2 = (bf16[3,48,384]{2,1,0:T(8,128)(2,1)}, bf16[3,48,384]{2,1,0:T(8,128)(2,1)S(1)}, u32[]{:S(2)}, u32[]{:S(2)}) collective-permute-start(bf16[3,48,384]{2,1,0:T(8,128)(2,1)} %get-tuple-element.41), channel_id=1, source_target_pairs={{0,8},{2,10},{4,12},{6,14},{8,0},{10,2},{12,4},{14,6},{16,24},{18,... | collective-permute-start | bytes 331784 | tf_op jit(solution)/shard_map/ppermute | solution.py:447
  11.2 9.7 %copy-start = (bf16[1536,192]{0,1:T(8,128)(2,1)S(1)}, bf16[1536,192]{0,1:T(8,128)(2,1)}, u32[]{:S(2)}) copy-start(bf16[1536,192]{0,1:T(8,128)(2,1)} %param.13) | copy-start | bytes 1769476
  17.1 7.6 %collective-permute-start.3 = (bf16[3,2,48,384]{3,2,1,0:T(8,128)(2,1)S(1)}, bf16[3,2,48,384]{3,2,1,0:T(8,128)(2,1)S(1)}, u32[]{:S(2)}, u32[]{:S(2)}) collective-permute-start(bf16[3,2,48,384]{3,2,1,0:T(8,128)(2,1)S(1)} %get-tuple-element.50), channel_id=1, source_target_pairs={{0,4},{2,6},{4,0},{6,2},{8,12},{10,14},{12,8},{14,10},{16,20},{18,... | collective-permute-start | bytes 663560 | tf_op jit(solution)/shard_map/ppermute | solution.py:447
  17.6 2.1 %collective-permute-start.6 = (bf16[2,2,48,384]{3,2,1,0:T(8,128)(2,1)S(1)}, bf16[2,2,48,384]{3,2,1,0:T(8,128)(2,1)S(1)}, u32[]{:S(2)}, u32[]{:S(2)}) collective-permute-start(bf16[2,2,48,384]{3,2,1,0:T(8,128)(2,1)S(1)} %get-tuple-element.53), channel_id=1, source_target_pairs={{0,2},{2,0},{4,6},{6,4},{8,10},{10,8},{12,14},{14,12},{16,18},{18,... | collective-permute-start | bytes 442376 | tf_op jit(solution)/shard_map/ppermute | solution.py:447
  17.6 2.1 %collective-permute-start.7 = (bf16[2,2,48,384]{3,2,1,0:T(8,128)(2,1)S(1)}, bf16[2,2,48,384]{3,2,1,0:T(8,128)(2,1)S(1)}, u32[]{:S(2)}, u32[]{:S(2)}) collective-permute-start(bf16[2,2,48,384]{3,2,1,0:T(8,128)(2,1)S(1)} %get-tuple-element.54), channel_id=1, source_target_pairs={{0,2},{2,0},{4,6},{6,4},{8,10},{10,8},{12,14},{14,12},{16,18},{18,... | collective-permute-start | bytes 442376 | tf_op jit(solution)/shard_map/ppermute | solution.py:447
  18.1 6.5 %collective-permute-start.4 = (bf16[2,48,384]{2,1,0:T(8,128)(2,1)S(1)}, bf16[2,48,384]{2,1,0:T(8,128)(2,1)S(1)}, u32[]{:S(2)}, u32[]{:S(2)}) collective-permute-start(bf16[2,48,384]{2,1,0:T(8,128)(2,1)S(1)} %copy-done.4), channel_id=1, source_target_pairs={{0,4},{2,6},{4,0},{6,2},{8,12},{10,14},{12,8},{14,10},{16,20},{18,... | collective-permute-start | bytes 221192 | tf_op jit(solution)/shard_map/ppermute | solution.py:447
  24.6 1.6 %collective-permute-start.9 = (bf16[3,2,48,384]{3,2,1,0:T(8,128)(2,1)S(1)}, bf16[3,2,48,384]{3,2,1,0:T(8,128)(2,1)S(1)}, u32[]{:S(2)}, u32[]{:S(2)}) collective-permute-start(bf16[3,2,48,384]{3,2,1,0:T(8,128)(2,1)S(1)} %collective-permute-done.3.some_far), channel_id=1, source_target_pairs={{0,2},{2,0},{4,6},{6,4},{8,10},{10,8},{12,14},{14,12},{16,18},{18,... | collective-permute-start | bytes 663560 | tf_op jit(solution)/shard_map/ppermute | solution.py:447
  24.6 1.6 %collective-permute-start.8 = (bf16[2,48,384]{2,1,0:T(8,128)(2,1)S(1)}, bf16[2,48,384]{2,1,0:T(8,128)(2,1)S(1)}, u32[]{:S(2)}, u32[]{:S(2)}) collective-permute-start(bf16[2,48,384]{2,1,0:T(8,128)(2,1)S(1)} %collective-permute-done.4.own_far), channel_id=1, source_target_pairs={{0,2},{2,0},{4,6},{6,4},{8,10},{10,8},{12,14},{14,12},{16,18},{18,... | collective-permute-start | bytes 221192 | tf_op jit(solution)/shard_map/ppermute | solution.py:447
  26.2 14.1 %collective-permute-start.12 = (bf16[2,192,1536]{2,1,0:T(8,128)(2,1)S(1)}, bf16[2,192,1536]{2,1,0:T(8,128)(2,1)S(1)}, u32[]{:S(2)}, u32[]{:S(2)}) collective-permute-start(bf16[2,192,1536]{2,1,0:T(8,128)(2,1)S(1)} %shard_map.85.own), channel_id=1, source_target_pairs={{0,2},{2,0},{4,6},{6,4},{8,10},{10,8},{12,14},{14,12},{16,18},{18,... | collective-permute-start | bytes 3538952 | tf_op jit(solution)/shard_map/ppermute | solution.py:447
  27.5 12.8 %collective-permute-start.10 = (bf16[192,384]{1,0:T(8,128)(2,1)S(1)}, bf16[192,384]{1,0:T(8,128)(2,1)S(1)}, u32[]{:S(2)}, u32[]{:S(2)}) collective-permute-start(bf16[192,384]{1,0:T(8,128)(2,1)S(1)} %shard_map.88.own), channel_id=1, source_target_pairs={{0,16},{2,18},{4,20},{6,22},{8,24},{10,26},{12,28},{14,30},{16,0},... | collective-permute-start | bytes 442376 | tf_op jit(solution)/shard_map/ppermute | solution.py:447
  32.7 8.6 %collective-permute-start.11 = (bf16[192,384]{1,0:T(8,128)(2,1)S(1)}, bf16[192,384]{1,0:T(8,128)(2,1)S(1)}, u32[]{:S(2)}, u32[]{:S(2)}) collective-permute-start(bf16[192,384]{1,0:T(8,128)(2,1)S(1)} %shard_map.88.own), channel_id=1, source_target_pairs={{0,8},{2,10},{4,12},{6,14},{8,0},{10,2},{12,4},{14,6},{16,24},{18,... | collective-permute-start | bytes 442376 | tf_op jit(solution)/shard_map/ppermute | solution.py:447
  40.3 5.5 %collective-permute-start.13 = (bf16[192,384]{1,0:T(8,128)(2,1)S(1)}, bf16[192,384]{1,0:T(8,128)(2,1)S(1)}, u32[]{:S(2)}, u32[]{:S(2)}) collective-permute-start(bf16[192,384]{1,0:T(8,128)(2,1)S(1)} %collective-permute-done.10.second), channel_id=1, source_target_pairs={{0,8},{2,10},{4,12},{6,14},{8,0},{10,2},{12,4},{14,6},{16,24},{18,... | collective-permute-start | bytes 442376 | tf_op jit(solution)/shard_map/ppermute | solution.py:447
  42.0 13.8 %copy-start.2 = (f32[1536]{0:T(1024)S(1)}, f32[1536]{0:T(1024)}, u32[]{:S(2)}) copy-start(f32[1536]{0:T(1024)} %param.14) | copy-start | bytes 18436
  42.0 13.8 %copy-start.3 = (f32[1536]{0:T(1024)S(1)}, f32[1536]{0:T(1024)}, u32[]{:S(2)}) copy-start(f32[1536]{0:T(1024)} %param.15) | copy-start | bytes 18436
  46.2 7.5 %collective-permute-start.14 = (bf16[48,768]{1,0:T(8,128)(2,1)S(1)}, bf16[48,768]{1,0:T(8,128)(2,1)S(1)}, u32[]{:S(2)}, u32[]{:S(2)}) collective-permute-start(bf16[48,768]{1,0:T(8,128)(2,1)S(1)} %get-tuple-element.66), channel_id=1, source_target_pairs={{0,16},{2,18},{4,20},{6,22},{8,24},{10,26},{12,28},{14,30},{16,0},... | collective-permute-start | bytes 221192 | tf_op jit(solution)/shard_map/ppermute | solution.py:447
  46.3 7.5 %collective-permute-start.15 = (bf16[48,768]{1,0:T(8,128)(2,1)S(1)}, bf16[48,768]{1,0:T(8,128)(2,1)S(1)}, u32[]{:S(2)}, u32[]{:S(2)}) collective-permute-start(bf16[48,768]{1,0:T(8,128)(2,1)S(1)} %get-tuple-element.67), channel_id=1, source_target_pairs={{0,24},{2,26},{4,28},{6,30},{8,16},{10,18},{12,20},{14,22},{16,8},... | collective-permute-start | bytes 221192 | tf_op jit(solution)/shard_map/ppermute | solution.py:447
  48.9 5.3 %collective-permute-start.16 = (bf16[48,768]{1,0:T(8,128)(2,1)S(1)}, bf16[48,768]{1,0:T(8,128)(2,1)S(1)}, u32[]{:S(2)}, u32[]{:S(2)}) collective-permute-start(bf16[48,768]{1,0:T(8,128)(2,1)S(1)} %get-tuple-element.68), channel_id=1, source_target_pairs={{0,8},{2,10},{4,12},{6,14},{8,0},{10,2},{12,4},{14,6},{16,24},{18,... | collective-permute-start | bytes 221192 | tf_op jit(solution)/shard_map/ppermute | solution.py:447
  54.3 5.2 %collective-permute-start.17 = (bf16[2,48,768]{2,1,0:T(8,128)(2,1)S(1)}, bf16[2,48,768]{2,1,0:T(8,128)(2,1)S(1)}, u32[]{:S(2)}, u32[]{:S(2)}) collective-permute-start(bf16[2,48,768]{2,1,0:T(8,128)(2,1)S(1)} %get-tuple-element.70), channel_id=1, source_target_pairs={{0,1},{1,0},{2,3},{3,2},{4,5},{5,4},{6,7},{7,6},{8,9},{9,8},{10,11... | collective-permute-start | bytes 442376 | tf_op jit(solution)/shard_map/ppermute | solution.py:482
